TPU v7x, 32 devices: a whole 2x2x4 slice. The times are simulated.
32 devices in a mesh: groups: 2 (over y), row: 8 (over z, x), col: 2 (over core).
Axes of the slice: x: 2, y: 2, z: 4, core: 2. Of those that a mesh axis runs over, the one named last changes fastest.
Arguments:
- tiles: bfloat16 [16, 2, 96, 128, 128], P(('groups', 'row'), 'col'), parts along dimension 0, may hold values from 0 to 0.023925781
- tile_row: int32 [16, 2, 96], P(('groups', 'row'), 'col'), parts along dimension 0, may hold values from 0 to 3, as said below
- tile_col: int32 [16, 2, 96], P(('groups', 'row'), 'col'), parts along dimension 0, may hold values from 0 to 9
- tile_count: int32 [16, 2], P(('groups', 'row'), 'col'), parts along dimension 0, may hold values from 1 to 96, as said below
- sources: int32 [512], P('groups'), parts along dimension 0, may hold values from 0 to 2303
Outputs:
- scores: float32 [16, 2, 128, 256], P(('groups', 'row'), 'col'), parts along dimension 0
- hub_scores: float32 [512, 256], P(('groups', 'row', 'col')), parts along dimension 0
There are 2 independent parts, one for each index of `groups`. A program takes and returns all parts, laid end to end along the dimension named above; each array names one. Nothing has to cross between parts.
Inputs may be any that keep to these rules, and one draw needn't show every extreme that they name: Slots from tile_count on are padding whose tiles and coordinates are ignored; some device uses all 96 slots. `tile_row`: tile rows from 2 * 128 / 128 on are hub rows.
All inputs are finite; a program needn't handle non-finite values.
Results may differ from a plain program's by a relative error of at most 0.0003.
Values may be sent and summed in bfloat16 or wider, within the bound.
No kernel may reach another device: no remote copies, remote signals or barrier semaphores. Data moves between devices by JAX's collectives and lax.ppermute only.
A program may use at most 64 MiB of HBM per device.

v0:
```python
import math

import jax
import jax.numpy as jnp
from jax import lax
from jax.sharding import PartitionSpec as P

VB = 128
H = 256
ITERS = 2


def body(tiles, tile_row, tile_col, tile_count, sources):
    slots = tiles.shape[2]
    side = tiles.shape[3]
    width = sources.shape[0]
    tiles = tiles.reshape(slots, side, side)
    rows = tile_row.reshape(slots)
    cols = tile_col.reshape(slots)
    count = tile_count.reshape(())
    n_row = lax.axis_size("row")
    n_col = lax.axis_size("col")
    devices = n_row * n_col
    r_index = lax.axis_index("row")
    c_index = lax.axis_index("col")
    hub_dev = H // devices
    block_rows = n_col * VB
    n_tile_rows = (block_rows + H) // side
    own_base = H + (r_index * n_col + c_index) * VB
    hub_start = (r_index * n_col + c_index) * hub_dev
    own_ids = jnp.arange(VB, dtype=jnp.int32) + own_base
    tele_own = (own_ids[:, None] == sources[None, :]).astype(jnp.float32)
    piece_ids = jnp.arange(hub_dev, dtype=jnp.int32) + hub_start
    tele_piece = (piece_ids[:, None] == sources[None, :]).astype(jnp.float32)
    tele_hubs = (jnp.arange(H, dtype=jnp.int32)[:, None] == sources[None, :]).astype(jnp.float32)
    column_ids = (
        H
        + (jnp.arange(n_row, dtype=jnp.int32)[:, None] * n_col + c_index) * VB
        + jnp.arange(VB, dtype=jnp.int32)[None, :]
    ).reshape(n_row * VB)
    column_panel = (column_ids[:, None] == sources[None, :]).astype(jnp.bfloat16)
    hub_panel = tele_hubs.astype(jnp.bfloat16)
    block = math.gcd(slots, 16)
    own_scores = tele_own
    hub_piece = tele_piece
    for step in range(ITERS):
        start_acc = jnp.zeros((n_tile_rows, side, width), jnp.float32)
        if step > 0:
            column_panel = lax.all_gather(
                own_scores.astype(jnp.bfloat16), "row", axis=0, tiled=True
            )
        panel = jnp.concatenate([column_panel, hub_panel], axis=0).reshape(-1, side, width)

        def step_fn(number, total):
            start = number * block
            tile_block = lax.dynamic_slice_in_dim(tiles, start, block, 0)
            col_block = lax.dynamic_slice_in_dim(cols, start, block, 0)
            row_block = lax.dynamic_slice_in_dim(rows, start, block, 0)
            pieces = jnp.take(panel, col_block, axis=0)
            prod = jnp.einsum(
                "tij,tjs->tis", tile_block, pieces, preferred_element_type=jnp.float32
            )
            live = start + jnp.arange(block, dtype=jnp.int32) < count
            prod = jnp.where(live[:, None, None], prod, 0.0)
            return total.at[row_block].add(prod)

        total = lax.fori_loop(0, slots // block, step_fn, start_acc)
        partial_value = total.reshape(n_tile_rows * side, width)
        summed_rows = lax.psum_scatter(
            partial_value[:block_rows], "col", scatter_dimension=0, tiled=True
        )
        own_scores = 0.85 * summed_rows + 0.15 * tele_own
        hub_part = partial_value[block_rows:]
        summed = lax.psum_scatter(hub_part, ("row", "col"), scatter_dimension=0, tiled=True)
        hub_piece = 0.85 * summed + 0.15 * tele_piece
        if step + 1 < ITERS:
            hub_panel = lax.all_gather(
                hub_piece.astype(jnp.bfloat16), ("row", "col"), axis=0, tiled=True
            )
    return (own_scores.reshape(1, 1, VB, width), hub_piece)


def solution(mesh):
    placed = (
        P(("groups", "row"), "col", None, None, None),
        P(("groups", "row"), "col", None),
        P(("groups", "row"), "col", None),
        P(("groups", "row"), "col"),
        P("groups"),
    )
    return jax.shard_map(
        body,
        mesh=mesh,
        in_specs=placed,
        out_specs=(P(("groups", "row"), "col", None, None), P(("groups", "row", "col"), None)),
        check_vma=False,
    )
```

profile of v0, /device:TPU:0, one launch (start us, length us, event | category | flops | bytes accessed | tf_op | source)
XLA Modules:
  0.0 269.6 jit_solution(17317981211522031606)
XLA Ops:
  8.0 0.9 compare_convert_fusion
  9.0 39.0 %while.26 = (s32[]{:T(128)}, f32[4,128,256]{2,1,0:T(8,128)S(1)}, s32[96]{0:T(128)S(1)}, s32[]{:T(128)}, bf16[96,128,128]{2,1,0:T(8,128)(2,1)}, /*index=5*/s32[96...) while((s32[]{:T(128)}, f32[4,128,256]{2,1,0:T(8,128)S(1)}, ...), condition=%wide.region_2.4_spmd, body=%wide.region_0.3_spmd.sunk | while | flops 135791792 | bytes 12063407 | solution.py:67
  9.8 1.6 gather_fusion
  11.4 1.9 convolution_select_fusion.4
  13.4 2.2 scatter_fusion
  16.3 1.6 gather_fusion
  17.9 1.9 convolution_select_fusion.4
  19.9 2.2 scatter_fusion
  22.8 1.6 gather_fusion
  24.4 1.9 convolution_select_fusion.4
  26.4 2.2 scatter_fusion
  29.3 1.6 gather_fusion
  30.9 1.9 convolution_select_fusion.4
  32.9 2.2 scatter_fusion
  35.8 1.6 gather_fusion
  37.4 1.9 convolution_select_fusion.4
  39.4 2.2 scatter_fusion
  42.3 1.6 gather_fusion
  43.9 1.9 convolution_select_fusion.4
  45.9 2.2 scatter_fusion
  48.1 0.8 fusion.16
  49.8 57.3 %reduce-scatter.7.cloned.1.call-done = f32[16,256]{1,0:T(8,128)} async-done(((f32[256,256]{1,0:T(8,128)}), f32[16,256]{1,0:T(8,128)}) %reduce-scatter.7.cloned.1.call-update) | async-done | bytes 16400 | tf_op jit(solution)/shard_map/reduce_scatter | solution.py:74
  107.9 19.8 %all_gather.7 = bf16[256,256]{1,0:T(8,128)(2,1)S(1)} all-gather(bf16[16,256]{1,0:T(8,128)(2,1)S(1)} %fusion.14), channel_id=1, replica_groups=mesh['groups'=2,'row'=8,'col'=2] {'row','col'}, dimensions={0}, use_global_device_ids=true | all-gather | bytes 139264 | tf_op jit(solution)/shard_map/all_gather | solution.py:77
  127.7 1.0 fusion.12
  128.6 31.2 %all_gather.6 = bf16[1024,256]{1,0:T(8,128)(2,1)S(1)} all-gather(bf16[128,256]{1,0:T(8,128)(2,1)S(1)} %fusion.12), channel_id=1, replica_groups=mesh['groups'=2,'row'=8,'col'=2] {'row'}, dimensions={0}, use_global_device_ids=true | all-gather | bytes 589824 | tf_op jit(solution)/shard_map/all_gather | solution.py:49
  160.0 39.0 %while.27 = (s32[]{:T(128)}, f32[4,128,256]{2,1,0:T(8,128)S(1)}, s32[96]{0:T(128)S(1)}, s32[]{:T(128)}, bf16[96,128,128]{2,1,0:T(8,128)(2,1)}, /*index=5*/s32[96...) while((s32[]{:T(128)}, f32[4,128,256]{2,1,0:T(8,128)S(1)}, ...), condition=%wide.region_7.9_spmd, body=%wide.region_5.8_spmd.sunk | while | flops 135791792 | bytes 12063407 | solution.py:67
  160.7 1.6 gather_fusion.1
  162.3 1.9 convolution_select_fusion.5
  164.3 2.2 scatter_fusion.1
  167.2 1.6 gather_fusion.1
  168.8 1.9 convolution_select_fusion.5
  170.8 2.2 scatter_fusion.1
  173.7 1.6 gather_fusion.1
  175.3 1.9 convolution_select_fusion.5
  177.3 2.2 scatter_fusion.1
  180.2 1.6 gather_fusion.1
  181.8 1.9 convolution_select_fusion.5
  183.8 2.2 scatter_fusion.1
  186.7 1.6 gather_fusion.1
  188.3 1.9 convolution_select_fusion.5
  190.3 2.2 scatter_fusion.1
  193.2 1.6 gather_fusion.1
  194.8 1.9 convolution_select_fusion.5
  196.8 2.2 scatter_fusion.1
  200.4 52.1 %reduce-scatter.11.cloned.1.call-done = f32[16,256]{1,0:T(8,128)} async-done(((f32[256,256]{1,0:T(8,128)}), f32[16,256]{1,0:T(8,128)}) %reduce-scatter.11.cloned.1.call-update) | async-done | bytes 16400 | tf_op jit(solution)/shard_map/reduce_scatter | solution.py:74
  252.6 1.4 select_add_fusion.2
  254.0 7.5 %reduce-scatter.9.cloned.1.call-done = f32[128,256]{1,0:T(8,128)} async-done(((f32[256,256]{1,0:T(8,128)}), f32[128,256]{1,0:T(8,128)}) %reduce-scatter.9.cloned.1.call-update) | async-done | bytes 131088 | tf_op jit(solution)/shard_map/reduce_scatter | solution.py:69
  261.4 1.6 fusion.13
  (62 shorter events, 13.8 us)
Async XLA Ops:
  7.2 1.9 copy-start.2
  7.2 1.9 copy-start
  7.2 99.9 %reduce-scatter.7.cloned.1.call-start = ((), (), s32[]{:S(2)}) async-start(), calls=%async_computation.5 | async-start | bytes 278528 | tf_op jit(solution)/shard_map/reduce_scatter | solution.py:74
  9.0 98.1 %copy-start.1 = (s32[256]{0:T(256)S(1)}, s32[256]{0:T(256)}, u32[]{:S(2)}) copy-start(s32[256]{0:T(256)} %param.15) | copy-start | bytes 3076
  48.9 78.7 %reduce-scatter.5.cloned.1.call-start = ((), (), s32[]{:S(2)}) async-start(), calls=%async_computation.4 | async-start | bytes 393216 | tf_op jit(solution)/shard_map/reduce_scatter | solution.py:69
  49.7 202.9 %reduce-scatter.11.cloned.1.call-start = ((), (), s32[]{:S(2)}) async-start(), calls=%async_computation.7 | async-start | bytes 278528 | tf_op jit(solution)/shard_map/reduce_scatter | solution.py:74
  199.9 61.6 %reduce-scatter.9.cloned.1.call-start = ((), (), s32[]{:S(2)}) async-start(), calls=%async_computation.6 | async-start | bytes 393216 | tf_op jit(solution)/shard_map/reduce_scatter | solution.py:69
Sparse Core Ops, SparseCore 0:
  49.1 57.9 reduce-scatter.6
  109.3 6.6 reduce-scatter.4
  200.0 52.5 reduce-scatter.10
  254.7 6.6 reduce-scatter.8
where the time goes:
time: 270 us
  waiting for transfers between devices  118 us (44%)
  blocking collectives  51 us (19%)
  other arithmetic  42.5 us (16%)
  matrix products  22.7 us (8%)
  local copies, waits for them, and re-layouts  20.7 us (8%)
  between operations  13.9 us (5%)
    reduce_scatter x2, waiting for transfers between devices, body(): lax.psum_scatter(hub_part, ('row', 'col'), scatter_dimension=0, tiled=True)  109 us
    all_gather x1, blocking collectives, body(): lax.all_gather(own_scores.astype(jnp.bfloat16), 'row', axis=0, tiled=True)  31.2 us
    scatter-add x12, other arithmetic, step_fn(): return total.at[row_block].add(prod)  26.2 us
    dot_general x12, matrix products, step_fn(): jnp.einsum('tij,tjs->tis', tile_block, pieces, preferred_element_type=jnp...  22.7 us
    all_gather x1, blocking collectives, body(): lax.all_gather(hub_piece.astype(jnp.bfloat16), ('row', 'col'), axis=0, ti...  19.8 us
    gather x12, local copies, waits for them, and re-layouts, step_fn(): pieces = jnp.take(panel, col_block, axis=0)  19 us
    and x12, other arithmetic, step_fn(): pieces = jnp.take(panel, col_block, axis=0)  8.73 us
    reduce_scatter x2, waiting for transfers between devices, body(): lax.psum_scatter(partial_value[:block_rows], 'col', scatter_dimension=0,...  7.49 us
  transfers between devices with their start and end apart: 4, of which 3 were waited for; matrix products, arithmetic and copies ran while one was open for 1% of the time, Pallas kernels for 0%

commit v1 on v0

--- a/solution.py
+++ b/solution.py
@@ -1,16 +1,202 @@
-import math
+import functools
 
 import jax
 import jax.numpy as jnp
 from jax import lax
+from jax.experimental import pallas as pl
+from jax.experimental.pallas import tpu as pltpu
 from jax.sharding import PartitionSpec as P
 
 VB = 128
 H = 256
 ITERS = 2
-
-
-def body(tiles, tile_row, tile_col, tile_count, sources):
+DAMP = 0.85
+CHUNK = 16
+VMEM_LIMIT = 32 * 1024 * 1024
+
+SMEM = pl.BlockSpec(memory_space=pltpu.SMEM)
+VMEM = pl.BlockSpec(memory_space=pltpu.VMEM)
+ANY = pl.BlockSpec(memory_space=pl.ANY)
+
+
+def params():
+    return pltpu.CompilerParams(vmem_limit_bytes=VMEM_LIMIT)
+
+
+def one_hot(first, count, src):
+    ids = lax.broadcasted_iota(jnp.int32, (count, src.shape[1]), 0) + first
+    return (ids == src).astype(jnp.float32)
+
+
+def write_terms(dims, where_ref, prod_ref, dense_ref, panel_ref, hub_ref, send_ref, keep_ref):
+    n_row, n_col, side = dims
+    rows = dense_ref.shape[0] // 2
+    own = n_col * VB
+    prod = jnp.dot(dense_ref[...], panel_ref[...], preferred_element_type=jnp.float32)
+    total = prod[:rows] + prod[rows:]
+    prod_ref[...] = total[:own]
+    mine = pl.multiple_of(where_ref[1] * VB, VB)
+    other = pl.multiple_of((1 - where_ref[1]) * VB, VB)
+    keep_ref[...] = prod_ref[pl.ds(mine, VB), :]
+    send_ref[...] = prod_ref[pl.ds(other, VB), :]
+    hubs = total[own:].reshape(n_row, H // n_row, -1)
+    for c in range(n_col):
+        hub_ref[:, c] = hubs
+
+
+def first_kernel(dims, where_ref, count_ref, rows_ref, cols_ref, src_ref, tiles_ref,
+                 hub_ref, send_ref, keep_ref, dense_ref,
+                 held, total, panel, prod, sems):
+    n_row, n_col, side = dims
+    slots = tiles_ref.shape[0]
+    n_rows = dense_ref.shape[0] // 2
+    copies = []
+    for i in range(slots // CHUNK):
+        part = pl.ds(i * CHUNK, CHUNK)
+        copies.append(pltpu.make_async_copy(tiles_ref.at[part], held.at[part], sems.at[i]))
+    for copy in copies:
+        copy.start()
+    total[...] = jnp.zeros_like(total)
+    src = src_ref[...]
+    for r in range(n_row):
+        first = H + (r * n_col + where_ref[1]) * VB
+        panel[pl.ds(r * VB, VB), :] = one_hot(first, VB, src).astype(jnp.bfloat16)
+    panel[pl.ds(n_row * VB, H), :] = one_hot(0, H, src).astype(jnp.bfloat16)
+    count = count_ref[0]
+
+    def add_tile(k, carry):
+        live = k < count
+        row = pl.multiple_of(jnp.where(live, rows_ref[k] * side, n_rows), side)
+        col = pl.multiple_of(jnp.where(live, cols_ref[k] * side, 0), side)
+        spot = (pl.ds(row, side), pl.ds(col, side))
+        total[spot] += held[k].astype(jnp.float32)
+        return carry
+
+    for i, copy in enumerate(copies):
+        copy.wait()
+        lax.fori_loop(i * CHUNK, (i + 1) * CHUNK, add_tile, 0, unroll=4)
+    for r in range(0, n_rows, side):
+        whole = total[pl.ds(r, side), :]
+        high = whole.astype(jnp.bfloat16)
+        dense_ref[pl.ds(r, side), :] = high
+        dense_ref[pl.ds(n_rows + r, side), :] = (whole - high.astype(jnp.float32)).astype(jnp.bfloat16)
+    write_terms(dims, where_ref, prod, dense_ref, panel, hub_ref, send_ref, keep_ref)
+
+
+def second_kernel(dims, where_ref, got_ref, dense_ref, hub_ref, send_ref, keep_ref, panel, prod):
+    n_row, n_col, side = dims
+    share = H // n_row
+    for r in range(n_row):
+        panel[pl.ds(r * VB, VB), :] = got_ref[r, :VB]
+        panel[pl.ds(n_row * VB + r * share, share), :] = got_ref[r, VB:]
+    write_terms(dims, where_ref, prod, dense_ref, panel, hub_ref, send_ref, keep_ref)
+
+
+def new_scores(dims, where_ref, src_ref, keep_ref, came_ref):
+    n_row, n_col, side = dims
+    src = src_ref[...]
+    first = H + (where_ref[0] * n_col + where_ref[1]) * VB
+    tele = one_hot(first, VB, src)
+    return DAMP * (keep_ref[...] + came_ref[...]) + 0.15 * tele
+
+
+def new_hubs(dims, where_ref, src_ref, parts_ref):
+    n_row = dims[0]
+    share = H // n_row
+    summed = parts_ref[0]
+    for k in range(1, parts_ref.shape[0]):
+        summed = summed + parts_ref[k]
+    return DAMP * summed + 0.15 * one_hot(where_ref[0] * share, share, src_ref[...])
+
+
+def middle_kernel(dims, where_ref, src_ref, keep_ref, came_ref, parts_ref, out_ref):
+    out_ref[:VB] = new_scores(dims, where_ref, src_ref, keep_ref, came_ref).astype(jnp.bfloat16)
+    out_ref[VB:] = new_hubs(dims, where_ref, src_ref, parts_ref).astype(jnp.bfloat16)
+
+
+def last_kernel(dims, where_ref, src_ref, keep_ref, came_ref, parts_ref, scores_ref, hubs_ref, held):
+    scores_ref[...] = new_scores(dims, where_ref, src_ref, keep_ref, came_ref)
+    held[...] = new_hubs(dims, where_ref, src_ref, parts_ref)
+    piece = hubs_ref.shape[0]
+    start = pl.multiple_of(where_ref[1] * piece, piece)
+    hubs_ref[...] = held[pl.ds(start, piece), :]
+
+
+def fast_body(tiles, tile_row, tile_col, tile_count, sources):
+    slots, side = tiles.shape[2:4]
+    width = sources.shape[0]
+    n_row = lax.axis_size("row")
+    n_col = lax.axis_size("col")
+    devices = n_row * n_col
+    share = H // n_row
+    dims = (n_row, n_col, side)
+    n_rows = n_col * VB + H
+    n_cols = n_row * VB + H
+    f32 = functools.partial(jax.ShapeDtypeStruct, dtype=jnp.float32)
+    bf16 = functools.partial(jax.ShapeDtypeStruct, dtype=jnp.bfloat16)
+    where = jnp.stack([lax.axis_index("row"), lax.axis_index("col")]).astype(jnp.int32)
+    src = sources.reshape(1, width)
+    term_shapes = (f32((n_row, n_col, share, width)), f32((VB, width)), f32((VB, width)))
+
+    hubs, send, keep, dense = pl.pallas_call(
+        functools.partial(first_kernel, dims),
+        out_shape=term_shapes + (bf16((2 * n_rows, n_cols)),),
+        in_specs=[SMEM] * 4 + [VMEM, ANY],
+        out_specs=[VMEM] * 4,
+        scratch_shapes=[
+            pltpu.VMEM((slots, side, side), jnp.bfloat16),
+            pltpu.VMEM((n_rows + side, n_cols), jnp.float32),
+            pltpu.VMEM((n_cols, width), jnp.bfloat16),
+            pltpu.VMEM((n_col * VB, width), jnp.float32),
+            pltpu.SemaphoreType.DMA((slots // CHUNK,)),
+        ],
+        compiler_params=params(),
+        name="first_terms",
+    )(where, tile_count.reshape(1), tile_row.reshape(slots), tile_col.reshape(slots), src,
+      tiles.reshape(slots, side, side))
+
+    def exchange(hubs, send):
+        came = lax.ppermute(send, "col", [(0, 1), (1, 0)])
+        parts = lax.all_to_all(hubs.reshape(devices, share, width), ("row", "col"), 0, 0, tiled=True)
+        return came, parts
+
+    for step in range(ITERS - 1):
+        came, parts = exchange(hubs, send)
+        mine = pl.pallas_call(
+            functools.partial(middle_kernel, dims),
+            out_shape=bf16((VB + share, width)),
+            in_specs=[SMEM] + [VMEM] * 4,
+            out_specs=VMEM,
+            compiler_params=params(),
+            name="new_panel_rows",
+        )(where, src, keep, came, parts)
+        got = lax.all_gather(mine, "row", axis=0)
+        hubs, send, keep = pl.pallas_call(
+            functools.partial(second_kernel, dims),
+            out_shape=term_shapes,
+            in_specs=[SMEM, VMEM, VMEM],
+            out_specs=[VMEM] * 3,
+            scratch_shapes=[
+                pltpu.VMEM((n_cols, width), jnp.bfloat16),
+                pltpu.VMEM((n_col * VB, width), jnp.float32),
+            ],
+            compiler_params=params(),
+            name="later_terms",
+        )(where, got, dense)
+    came, parts = exchange(hubs, send)
+    scores, piece = pl.pallas_call(
+        functools.partial(last_kernel, dims),
+        out_shape=(f32((VB, width)), f32((H // devices, width))),
+        in_specs=[SMEM] + [VMEM] * 4,
+        out_specs=[VMEM] * 2,
+        scratch_shapes=[pltpu.VMEM((share, width), jnp.float32)],
+        compiler_params=params(),
+        name="last_scores",
+    )(where, src, keep, came, parts)
+    return scores.reshape(1, 1, VB, width), piece
+
+
+def plain_body(tiles, tile_row, tile_col, tile_count, sources):
     slots = tiles.shape[2]
     side = tiles.shape[3]
     width = sources.shape[0]
@@ -40,7 +226,7 @@
     ).reshape(n_row * VB)
     column_panel = (column_ids[:, None] == sources[None, :]).astype(jnp.bfloat16)
     hub_panel = tele_hubs.astype(jnp.bfloat16)
-    block = math.gcd(slots, 16)
+    block = CHUNK
     own_scores = tele_own
     hub_piece = tele_piece
     for step in range(ITERS):
@@ -88,6 +274,15 @@
         P(("groups", "row"), "col"),
         P("groups"),
     )
+
+    def body(tiles, *rest):
+        n_row, n_col = mesh.shape["row"], mesh.shape["col"]
+        slots, side = tiles.shape[2:4]
+        blocks = (n_col * VB + H) * (n_row * VB + H) // (side * side)
+        if n_col == 2 and blocks <= slots and H // (n_row * n_col) % 16 == 0:
+            return fast_body(tiles, *rest)
+        return plain_body(tiles, *rest)
+
     return jax.shard_map(
         body,
         mesh=mesh,

time: 270 us -> 85.5 us (0.32)
  waiting for transfers between devices: 118 us -> 28.1 us
  other arithmetic: 42.5 us -> 0.08 us
  matrix products: 22.7 us -> 0 us
  blocking collectives: 51 us -> 31.7 us
  local copies, waits for them, and re-layouts: 20.7 us -> 4.67 us
  between operations: 13.9 us -> 1.34 us
  starting transfers between devices: 0.16 us -> 12.3 us
  Pallas kernels: 0 us -> 6.91 us
    reduce_scatter x4 -> x0, waiting for transfers between devices: 117 us -> none  [the longest x2 109 us: body(): lax.psum_scatter(hub_part, ('row', 'col'), scatter_dimension=0, tiled=True)]
    scatter-add x12 -> x0, other arithmetic: 26.2 us -> none  [step_fn(): return total.at[row_block].add(prod)]
    all_to_all x0 -> x2, waiting for transfers between devices: none -> 26.1 us  [exchange(): lax.all_to_all(hubs.reshape(devices, share, width), ('row', 'col'), 0, 0,...]
    dot_general x12 -> x0, matrix products: 22.7 us -> none  [step_fn(): jnp.einsum('tij,tjs->tis', tile_block, pieces, preferred_element_type=jnp...]
    all_gather x2 -> x1, blocking collectives: 51 us -> 31.7 us  [fast_body(): got = lax.all_gather(mine, 'row', axis=0)]
    gather x12 -> x0, local copies, waits for them, and re-layouts: 19 us -> none  [step_fn(): pieces = jnp.take(panel, col_block, axis=0)]
    all_to_all x0 -> x2, starting transfers between devices: none -> 11.5 us  [exchange(): lax.all_to_all(hubs.reshape(devices, share, width), ('row', 'col'), 0, 0,...]
    and x12 -> x0, other arithmetic: 8.73 us -> none  [step_fn(): pieces = jnp.take(panel, col_block, axis=0)]
  transfers between devices with their start and end apart: 4 -> 4, of which waited for: 3 -> 4; matrix products, arithmetic and copies ran while one was open for 1% -> 0% of each run, Pallas kernels for 0% -> 0%
where the time goes in v1:
time: 85.5 us; the launch traced here: 85.1 us
  blocking collectives  31.7 us (37%)
  waiting for transfers between devices  28.1 us (33%)
  starting transfers between devices  12.3 us (14%)
  Pallas kernels  6.91 us (8%)
  local copies, waits for them, and re-layouts  4.67 us (5%)
  between operations  1.34 us (2%)
    all_gather x1, blocking collectives, fast_body(): got = lax.all_gather(mine, 'row', axis=0)  31.7 us
    all_to_all x2, waiting for transfers between devices, exchange(): lax.all_to_all(hubs.reshape(devices, share, width), ('row', 'col'), 0, 0,...  26.1 us
    all_to_all x2, starting transfers between devices, exchange(): lax.all_to_all(hubs.reshape(devices, share, width), ('row', 'col'), 0, 0,...  11.5 us
    unnamed x12, local copies, waits for them, and re-layouts  4.67 us
    pallas_call x1, Pallas kernels, fast_body(): pl.pallas_call(functools.partial(first_kernel, dims), out_shape=term_shap...  2.87 us
    pallas_call x1, Pallas kernels, fast_body(): pl.pallas_call(functools.partial(second_kernel, dims), out_shape=term_sha...  2.18 us
    ppermute x2, waiting for transfers between devices, exchange(): came = lax.ppermute(send, 'col', [(0, 1), (1, 0)])  2.01 us
  transfers between devices with their start and end apart: 4, of which 4 were waited for; matrix products, arithmetic and copies ran while one was open for 0% of the time, Pallas kernels for 0%

profile of v1, /device:TPU:0, one launch (start us, length us, event | category | flops | bytes accessed | tf_op | source)
XLA Modules:
  0.0 85.1 jit_solution(1966416211238000501)
XLA Ops:
  0.6 0.0 copy-start.3
  1.3 0.1 pad_add_fusion.where_ref
  1.4 0.0 copy-start
  1.4 1.9 %copy-done = bf16[1,1,96,128,128]{4,3,2,1,0:T(8,128)(2,1)S(1)} copy-done((bf16[1,1,96,128,128]{4,3,2,1,0:T(8,128)(2,1)S(1)}, bf16[1,1,96,128,128]{4,3,2,1,0:T(8,128)(2,1)}, u32[]{:S(2)}) %copy-start) | copy-done | bytes 3145752
  3.3 0.0 copy-start.2
  3.3 0.7 copy-done.2
  3.9 0.0 copy-start.4
  3.9 0.7 copy-done.4
  4.6 0.0 copy-start.5
  4.6 0.7 copy-done.5
  5.3 2.9 %first_terms.1 = (f32[8,2,32,256]{3,2,1,0:T(8,128)S(1)}, f32[128,256]{1,0:T(8,128)S(1)}, f32[128,256]{1,0:T(8,128)S(1)}, bf16[1024,1280]{1,0:T(8,128)(2,1)S(1)}) custom-call(s32[2]{0:T(128)S(1)} %pad_add_fusion.where_ref, s32[1]{0:T(128)} %bitcast.11.count_ref, s32[96]{0:T(128)S(1)} %bitcast.18, s32[96]{0:T(128)S(1)} %bitcast.19, s32[1,256]{1,0:T(1,128)S(1)} %bitcast.15, ...), custom_call_target="tpu_custom_call" | custom-call | tf_op jit(solution)/shard_map/first_terms/pallas_call | solution.py:141
  8.1 0.0 copy-start.1
  8.1 0.8 copy-done.1
  8.9 7.4 %all-to-all-start = ((f32[16,32,256]{2,1,0:T(8,128)}), f32[16,32,256]{2,1,0:T(8,128)S(1)}, u32[]{:S(2)}, u32[]{:S(2)}) async-start(f32[16,32,256]{2,1,0:T(8,128)} %bitcast.14), calls=%async_computation | async-start | bytes 1048576 | tf_op jit(solution)/shard_map/all_to_all | solution.py:160
  16.3 0.4 collective-permute-start
  16.7 1.0 %collective-permute-done.came_ref = f32[128,256]{1,0:T(8,128)S(1)} collective-permute-done((f32[128,256]{1,0:T(8,128)S(1)}, f32[128,256]{1,0:T(8,128)S(1)}, u32[]{:S(2)}, u32[]{:S(2)}) %collective-permute-start) | collective-permute-done | bytes 131104 | tf_op jit(solution)/shard_map/ppermute | solution.py:159
  17.7 13.1 %all-to-all-done.parts_ref = f32[16,32,256]{2,1,0:T(8,128)S(1)} async-done(((f32[16,32,256]{2,1,0:T(8,128)}), f32[16,32,256]{2,1,0:T(8,128)S(1)}, u32[]{:S(2)}, u32[]{:S(2)}) %all-to-all-start) | async-done | bytes 524320 | tf_op jit(solution)/shard_map/all_to_all | solution.py:160
  30.8 0.0 copy-done.3
  30.8 0.6 new_panel_rows.1
  31.4 31.7 %all-gather = bf16[1280,256]{1,0:T(8,128)(2,1)S(1)} all-gather(bf16[160,256]{1,0:T(8,128)(2,1)S(1)} %new_panel_rows.1), channel_id=2, replica_groups=mesh['groups'=2,'row'=8,'col'=2] {'row'}, dimensions={0}, use_global_device_ids=true | all-gather | bytes 737280 | tf_op jit(solution)/shard_map/all_gather | solution.py:173
  63.0 2.2 %later_terms.1 = (f32[8,2,32,256]{3,2,1,0:T(8,128)}, f32[128,256]{1,0:T(8,128)S(1)}, f32[128,256]{1,0:T(8,128)S(1)}) custom-call(s32[2]{0:T(128)S(1)} %pad_add_fusion.where_ref, bf16[8,160,256]{2,1,0:T(8,128)(2,1)S(1)} %bitcast.13, bf16[1024,1280]{1,0:T(8,128)(2,1)S(1)} %get-tuple-element.14.dense_ref), custom_call_target="tpu_custom_call" | custom-call | tf_op jit(solution)/shard_map/later_terms/pallas_call | solution.py:174
  65.2 4.1 %all-to-all-start.1 = ((f32[16,32,256]{2,1,0:T(8,128)}), f32[16,32,256]{2,1,0:T(8,128)S(1)}, u32[]{:S(2)}, u32[]{:S(2)}) async-start(f32[16,32,256]{2,1,0:T(8,128)} %bitcast.9), calls=%async_computation.1 | async-start | bytes 1048576 | tf_op jit(solution)/shard_map/all_to_all | solution.py:160
  69.3 0.4 collective-permute-start.1
  69.8 1.0 %collective-permute-done.1.came_ref = f32[128,256]{1,0:T(8,128)S(1)} collective-permute-done((f32[128,256]{1,0:T(8,128)S(1)}, f32[128,256]{1,0:T(8,128)S(1)}, u32[]{:S(2)}, u32[]{:S(2)}) %collective-permute-start.1) | collective-permute-done | bytes 131104 | tf_op jit(solution)/shard_map/ppermute | solution.py:159
  70.8 13.1 %all-to-all-done.1.parts_ref = f32[16,32,256]{2,1,0:T(8,128)S(1)} async-done(((f32[16,32,256]{2,1,0:T(8,128)}), f32[16,32,256]{2,1,0:T(8,128)S(1)}, u32[]{:S(2)}, u32[]{:S(2)}) %all-to-all-start.1) | async-done | bytes 524320 | tf_op jit(solution)/shard_map/all_to_all | solution.py:160
  83.8 1.3 %last_scores.1 = (f32[128,256]{1,0:T(8,128)}, f32[16,256]{1,0:T(8,128)}) custom-call(s32[2]{0:T(128)S(1)} %pad_add_fusion.where_ref, s32[1,256]{1,0:T(1,128)S(1)} %bitcast.17, f32[128,256]{1,0:T(8,128)S(1)} %get-tuple-element.15.keep_ref, f32[128,256]{1,0:T(8,128)S(1)} %collective-permute-done.1.came_ref, f32[16,32,256]{2,1,0:T(8,128)S(1)} %all-to-all-done.1.parts_ref), custom_call_target="tpu_custom_call" | custom-call | tf_op jit(solution)/shard_map/last_scores/pallas_call | solution.py:187
Async XLA Ops:
  0.6 30.1 %copy-start.3 = (s32[256]{0:T(256)S(1)}, s32[256]{0:T(256)}, u32[]{:S(2)}) copy-start(s32[256]{0:T(256)} %param.9) | copy-start | bytes 3076
  1.4 1.9 %copy-start = (bf16[1,1,96,128,128]{4,3,2,1,0:T(8,128)(2,1)S(1)}, bf16[1,1,96,128,128]{4,3,2,1,0:T(8,128)(2,1)}, u32[]{:S(2)}) copy-start(bf16[1,1,96,128,128]{4,3,2,1,0:T(8,128)(2,1)} %param.5) | copy-start | bytes 9437188
  3.3 0.7 copy-start.2
  3.9 0.7 copy-start.4
  4.6 0.7 copy-start.5
  8.1 0.8 copy-start.1
  8.9 21.8 %all-to-all-start = ((f32[16,32,256]{2,1,0:T(8,128)}), f32[16,32,256]{2,1,0:T(8,128)S(1)}, u32[]{:S(2)}, u32[]{:S(2)}) async-start(f32[16,32,256]{2,1,0:T(8,128)} %bitcast.14), calls=%async_computation | async-start | bytes 1048576 | tf_op jit(solution)/shard_map/all_to_all | solution.py:160
  16.3 1.4 %collective-permute-start = (f32[128,256]{1,0:T(8,128)S(1)}, f32[128,256]{1,0:T(8,128)S(1)}, u32[]{:S(2)}, u32[]{:S(2)}) collective-permute-start(f32[128,256]{1,0:T(8,128)S(1)} %get-tuple-element.12), channel_id=1, source_target_pairs={{0,1},{1,0},{2,3},{3,2},{4,5},{5,4},{6,7},{7,6},{8,9},{9,8},{10,11... | collective-permute-start | bytes 393224 | tf_op jit(solution)/shard_map/ppermute | solution.py:159
  65.2 18.6 %all-to-all-start.1 = ((f32[16,32,256]{2,1,0:T(8,128)}), f32[16,32,256]{2,1,0:T(8,128)S(1)}, u32[]{:S(2)}, u32[]{:S(2)}) async-start(f32[16,32,256]{2,1,0:T(8,128)} %bitcast.9), calls=%async_computation.1 | async-start | bytes 1048576 | tf_op jit(solution)/shard_map/all_to_all | solution.py:160
  69.3 1.4 %collective-permute-start.1 = (f32[128,256]{1,0:T(8,128)S(1)}, f32[128,256]{1,0:T(8,128)S(1)}, u32[]{:S(2)}, u32[]{:S(2)}) collective-permute-start(f32[128,256]{1,0:T(8,128)S(1)} %get-tuple-element.16), channel_id=1, source_target_pairs={{0,1},{1,0},{2,3},{3,2},{4,5},{5,4},{6,7},{7,6},{8,9},{9,8},{10,11... | collective-permute-start | bytes 393224 | tf_op jit(solution)/shard_map/ppermute | solution.py:159

commit v2 on v0

--- a/solution.py
+++ b/solution.py
@@ -1,16 +1,217 @@
-import math
+import functools
 
 import jax
 import jax.numpy as jnp
 from jax import lax
+from jax.experimental import pallas as pl
+from jax.experimental.pallas import tpu as pltpu
 from jax.sharding import PartitionSpec as P
 
 VB = 128
 H = 256
 ITERS = 2
-
-
-def body(tiles, tile_row, tile_col, tile_count, sources):
+DAMP = 0.85
+CHUNK = 16
+VMEM_LIMIT = 32 * 1024 * 1024
+
+SMEM = pl.BlockSpec(memory_space=pltpu.SMEM)
+VMEM = pl.BlockSpec(memory_space=pltpu.VMEM)
+HBM = pl.BlockSpec(memory_space=pltpu.HBM)
+
+
+def params():
+    return pltpu.CompilerParams(vmem_limit_bytes=VMEM_LIMIT)
+
+
+def one_hot(first, count, src):
+    ids = lax.broadcasted_iota(jnp.int32, (count, src.shape[1]), 0) + first
+    return (ids == src).astype(jnp.float32)
+
+
+def write_terms(dims, prod_ref, dense_ref, panel_ref, send_ref, keep_ref):
+    n_row, n_col, side = dims
+    rows = dense_ref.shape[0] // 2
+    piece = H // (n_row * n_col)
+    c = lax.axis_index("col")
+    prod = jnp.dot(dense_ref[...], panel_ref[...], preferred_element_type=jnp.float32)
+    prod_ref[...] = prod[:rows] + prod[rows:]
+    for ref, col in ((keep_ref, c), (send_ref, 1 - c)):
+        ref[:VB] = prod_ref[pl.ds(pl.multiple_of(col * VB, VB), VB), :]
+        for r in range(n_row):
+            start = n_col * VB + (r * n_col + col) * piece
+            ref[VB + r * piece:VB + (r + 1) * piece] = prod_ref[pl.ds(pl.multiple_of(start, piece), piece), :]
+
+
+def first_kernel(dims, tiles_ref, rows_hbm, cols_hbm, count_hbm, src_hbm,
+                 send_ref, keep_ref, dense_ref,
+                 held, rows_ref, cols_ref, count_ref, src_ref, total, panel, prod, sems, small):
+    n_row, n_col, side = dims
+    slots = tiles_ref.shape[0]
+    n_rows = dense_ref.shape[0] // 2
+    pairs = ((src_hbm, src_ref), (count_hbm, count_ref), (rows_hbm, rows_ref), (cols_hbm, cols_ref))
+    scalars = [pltpu.make_async_copy(a, b, small.at[i]) for i, (a, b) in enumerate(pairs)]
+    for copy in scalars:
+        copy.start()
+    copies = []
+    for i in range(slots // CHUNK):
+        part = pl.ds(i * CHUNK, CHUNK)
+        copies.append(pltpu.make_async_copy(tiles_ref.at[part], held.at[part], sems.at[i]))
+    for copy in copies:
+        copy.start()
+    total[...] = jnp.zeros_like(total)
+    for copy in scalars:
+        copy.wait()
+    src = src_ref[...]
+    for r in range(n_row):
+        first = H + (r * n_col + lax.axis_index("col")) * VB
+        panel[pl.ds(r * VB, VB), :] = one_hot(first, VB, src).astype(jnp.bfloat16)
+    panel[pl.ds(n_row * VB, H), :] = one_hot(0, H, src).astype(jnp.bfloat16)
+    count = count_ref[0]
+
+    def add_tile(k, carry):
+        live = k < count
+        row = pl.multiple_of(jnp.where(live, rows_ref[k] * side, n_rows), side)
+        col = pl.multiple_of(jnp.where(live, cols_ref[k] * side, 0), side)
+        spot = (pl.ds(row, side), pl.ds(col, side))
+        total[spot] += held[k].astype(jnp.float32)
+        return carry
+
+    for i, copy in enumerate(copies):
+        copy.wait()
+        lax.fori_loop(i * CHUNK, (i + 1) * CHUNK, add_tile, 0, unroll=4)
+    for r in range(0, n_rows, side):
+        whole = total[pl.ds(r, side), :]
+        high = whole.astype(jnp.bfloat16)
+        dense_ref[pl.ds(r, side), :] = high
+        dense_ref[pl.ds(n_rows + r, side), :] = (whole - high.astype(jnp.float32)).astype(jnp.bfloat16)
+    write_terms(dims, prod, dense_ref, panel, send_ref, keep_ref)
+
+
+def second_kernel(dims, *refs):
+    n_row, n_col, side = dims
+    scores, hubs = refs[:n_row], refs[n_row:2 * n_row]
+    dense_ref, send_ref, keep_ref, panel, prod = refs[2 * n_row:]
+    share = H // n_row
+    r = lax.axis_index("row")
+    for k in range(n_row):
+        owner = lax.rem(r - k + n_row, n_row)
+        panel[pl.ds(pl.multiple_of(owner * VB, VB), VB), :] = scores[k][...]
+        panel[pl.ds(pl.multiple_of(n_row * VB + owner * share, share), share), :] = hubs[k][...]
+    write_terms(dims, prod, dense_ref, panel, send_ref, keep_ref)
+
+
+def pair_kernel(dims, src_ref, keep_ref, came_ref, scores_ref, *parts):
+    n_row, n_col, side = dims
+    piece = H // (n_row * n_col)
+    r, c = lax.axis_index("row"), lax.axis_index("col")
+    tele = one_hot(H + (r * n_col + c) * VB, VB, src_ref[...])
+    own = DAMP * (keep_ref[:VB] + came_ref[:VB]) + 0.15 * tele
+    scores_ref[...] = own.astype(scores_ref.dtype)
+    for k in range(n_row):
+        spot = pl.ds(pl.multiple_of(VB + lax.rem(r + k, n_row) * piece, piece), piece)
+        parts[k][...] = keep_ref[spot, :] + came_ref[spot, :]
+
+
+def hub_kernel(dims, src_ref, *refs):
+    n_row, n_col, side = dims
+    out_ref = refs[n_row]
+    piece = out_ref.shape[0]
+    summed = refs[0][...]
+    for k in range(1, n_row):
+        summed = summed + refs[k][...]
+    first = (lax.axis_index("row") * n_col + lax.axis_index("col")) * piece
+    out_ref[...] = (DAMP * summed + 0.15 * one_hot(first, piece, src_ref[...])).astype(out_ref.dtype)
+
+
+def fast_body(tiles, tile_row, tile_col, tile_count, sources):
+    slots, side = tiles.shape[2:4]
+    width = sources.shape[0]
+    n_row = lax.axis_size("row")
+    n_col = lax.axis_size("col")
+    piece = H // (n_row * n_col)
+    dims = (n_row, n_col, side)
+    n_rows = n_col * VB + H
+    n_cols = n_row * VB + H
+    f32 = functools.partial(jax.ShapeDtypeStruct, dtype=jnp.float32)
+    bf16 = functools.partial(jax.ShapeDtypeStruct, dtype=jnp.bfloat16)
+    src = sources.reshape(1, width)
+    half = VB + n_row * piece
+    product_scratch = [
+        pltpu.VMEM((n_cols, width), jnp.bfloat16),
+        pltpu.VMEM((n_rows, width), jnp.float32),
+    ]
+
+    def other_core(x):
+        return lax.ppermute(x, "col", [(0, 1), (1, 0)])
+
+    def along_row(x, k):
+        return lax.ppermute(x, "row", [(r, (r + k) % n_row) for r in range(n_row)])
+
+    def pair_sums(keep, send, dtype):
+        came = other_core(send)
+        scores, *parts = pl.pallas_call(
+            functools.partial(pair_kernel, dims),
+            out_shape=(jax.ShapeDtypeStruct((VB, width), dtype),) + (f32((piece, width)),) * n_row,
+            in_specs=[VMEM] * 3,
+            out_specs=[VMEM] * (1 + n_row),
+            compiler_params=params(),
+            name="pair_sums",
+        )(src, keep, came)
+        return scores, [parts[0]] + [along_row(parts[k], k) for k in range(1, n_row)]
+
+    def hub_sums(parts, dtype):
+        return pl.pallas_call(
+            functools.partial(hub_kernel, dims),
+            out_shape=jax.ShapeDtypeStruct((piece, width), dtype),
+            in_specs=[VMEM] * (1 + n_row),
+            out_specs=VMEM,
+            compiler_params=params(),
+            name="hub_sums",
+        )(src, *parts)
+
+    send, keep, dense = pl.pallas_call(
+        functools.partial(first_kernel, dims),
+        out_shape=(f32((half, width)), f32((half, width)), bf16((2 * n_rows, n_cols))),
+        in_specs=[HBM] * 5,
+        out_specs=[VMEM] * 3,
+        scratch_shapes=[
+            pltpu.VMEM((slots, side, side), jnp.bfloat16),
+            pltpu.SMEM((slots,), jnp.int32),
+            pltpu.SMEM((slots,), jnp.int32),
+            pltpu.SMEM((1,), jnp.int32),
+            pltpu.VMEM((1, width), jnp.int32),
+            pltpu.VMEM((n_rows + side, n_cols), jnp.float32),
+        ] + product_scratch + [
+            pltpu.SemaphoreType.DMA((slots // CHUNK,)),
+            pltpu.SemaphoreType.DMA((4,)),
+        ],
+        compiler_params=params(),
+        name="first_terms",
+    )(tiles.reshape(slots, side, side), tile_row.reshape(slots), tile_col.reshape(slots),
+      tile_count.reshape(1), src)
+
+    for step in range(ITERS - 1):
+        scores, parts = pair_sums(keep, send, jnp.bfloat16)
+        got = [scores] + [along_row(scores, k) for k in range(1, n_row)]
+        mine = hub_sums(parts, jnp.bfloat16)
+        theirs = other_core(mine)
+        both = jnp.where(lax.axis_index("col") == 0,
+                         jnp.concatenate([mine, theirs]), jnp.concatenate([theirs, mine]))
+        hubs = [both] + [along_row(both, k) for k in range(1, n_row)]
+        send, keep = pl.pallas_call(
+            functools.partial(second_kernel, dims),
+            out_shape=(f32((half, width)), f32((half, width))),
+            in_specs=[VMEM] * (2 * n_row + 1),
+            out_specs=[VMEM] * 2,
+            scratch_shapes=product_scratch,
+            compiler_params=params(),
+            name="later_terms",
+        )(*got, *hubs, dense)
+    scores, parts = pair_sums(keep, send, jnp.float32)
+    return scores.reshape(1, 1, VB, width), hub_sums(parts, jnp.float32)
+
+
+def plain_body(tiles, tile_row, tile_col, tile_count, sources):
     slots = tiles.shape[2]
     side = tiles.shape[3]
     width = sources.shape[0]
@@ -40,7 +241,7 @@
     ).reshape(n_row * VB)
     column_panel = (column_ids[:, None] == sources[None, :]).astype(jnp.bfloat16)
     hub_panel = tele_hubs.astype(jnp.bfloat16)
-    block = math.gcd(slots, 16)
+    block = CHUNK
     own_scores = tele_own
     hub_piece = tele_piece
     for step in range(ITERS):
@@ -88,6 +289,15 @@
         P(("groups", "row"), "col"),
         P("groups"),
     )
+
+    def body(tiles, *rest):
+        n_row, n_col = mesh.shape["row"], mesh.shape["col"]
+        slots, side = tiles.shape[2:4]
+        blocks = (n_col * VB + H) * (n_row * VB + H) // (side * side)
+        if n_col == 2 and blocks <= slots and H // (n_row * n_col) % 16 == 0:
+            return fast_body(tiles, *rest)
+        return plain_body(tiles, *rest)
+
     return jax.shard_map(
         body,
         mesh=mesh,

time: 270 us -> 71.9 us (0.27)
  waiting for transfers between devices: 118 us -> 14 us
  blocking collectives: 51 us -> 0 us
  starting transfers between devices: 0.16 us -> 47.5 us
  other arithmetic: 42.5 us -> 0.01 us
  matrix products: 22.7 us -> 0 us
  local copies, waits for them, and re-layouts: 20.7 us -> 3.87 us
  between operations: 13.9 us -> 1.38 us
  Pallas kernels: 0 us -> 5 us
    reduce_scatter x4 -> x0, waiting for transfers between devices: 117 us -> none  [the longest x2 109 us: body(): lax.psum_scatter(hub_part, ('row', 'col'), scatter_dimension=0, tiled=True)]
    all_gather x2 -> x0, blocking collectives: 51 us -> none  [the longest x1 31.2 us: body(): lax.all_gather(own_scores.astype(jnp.bfloat16), 'row', axis=0, tiled=True)]
    ppermute x0 -> x31, starting transfers between devices: none -> 47.5 us  [the longest x28 46.8 us: along_row(): return lax.ppermute(x, 'row', [(r, (r + k) % n_row) for r in range(n_row)])]
    scatter-add x12 -> x0, other arithmetic: 26.2 us -> none  [step_fn(): return total.at[row_block].add(prod)]
    dot_general x12 -> x0, matrix products: 22.7 us -> none  [step_fn(): jnp.einsum('tij,tjs->tis', tile_block, pieces, preferred_element_type=jnp...]
    gather x12 -> x0, local copies, waits for them, and re-layouts: 19 us -> none  [step_fn(): pieces = jnp.take(panel, col_block, axis=0)]
    ppermute x0 -> x31, waiting for transfers between devices: none -> 14 us  [the longest x28 11.3 us: along_row(): return lax.ppermute(x, 'row', [(r, (r + k) % n_row) for r in range(n_row)])]
    and x12 -> x0, other arithmetic: 8.73 us -> none  [step_fn(): pieces = jnp.take(panel, col_block, axis=0)]
  transfers between devices with their start and end apart: 4 -> 31, of which waited for: 3 -> 12; matrix products, arithmetic and copies ran while one was open for 1% -> 0% of each run, Pallas kernels for 0% -> 0%
where the time goes in v2:
time: 71.9 us; the launch traced here: 71.7 us
  starting transfers between devices  47.5 us (66%)
  waiting for transfers between devices  14 us (19%)
  Pallas kernels  5 us (7%)
  local copies, waits for them, and re-layouts  3.87 us (5%)
  between operations  1.38 us (2%)
    ppermute x28, starting transfers between devices, along_row(): return lax.ppermute(x, 'row', [(r, (r + k) % n_row) for r in range(n_row)])  46.8 us
    ppermute x28, waiting for transfers between devices, along_row(): return lax.ppermute(x, 'row', [(r, (r + k) % n_row) for r in range(n_row)])  11.3 us
    unnamed x10, local copies, waits for them, and re-layouts  3.87 us
    ppermute x3, waiting for transfers between devices, other_core(): return lax.ppermute(x, 'col', [(0, 1), (1, 0)])  2.69 us
    pallas_call x1, Pallas kernels, fast_body(): pl.pallas_call(functools.partial(first_kernel, dims), out_shape=(f32((hal...  2.6 us
  transfers between devices with their start and end apart: 31, of which 12 were waited for; matrix products, arithmetic and copies ran while one was open for 0% of the time, Pallas kernels for 0%

profile of v2, /device:TPU:0, one launch (start us, length us, event | category | flops | bytes accessed | tf_op | source)
XLA Modules:
  0.0 71.7 jit_solution(7445348300657425003)
XLA Ops:
  1.3 1.9 %copy-done = bf16[1,1,96,128,128]{4,3,2,1,0:T(8,128)(2,1)S(1)} copy-done((bf16[1,1,96,128,128]{4,3,2,1,0:T(8,128)(2,1)S(1)}, bf16[1,1,96,128,128]{4,3,2,1,0:T(8,128)(2,1)}, u32[]{:S(2)}) %copy-start) | copy-done | bytes 3145752
  3.2 0.7 copy-done.1
  3.8 0.7 copy-done.3
  4.5 0.7 copy-done.4
  5.2 2.6 %first_terms.1 = (f32[256,256]{1,0:T(8,128)S(1)}, f32[256,256]{1,0:T(8,128)S(1)}, bf16[1024,1280]{1,0:T(8,128)(2,1)S(1)}) custom-call(bf16[96,128,128]{2,1,0:T(8,128)(2,1)S(1)} %bitcast.7, s32[96]{0:T(128)S(1)} %bitcast.13, s32[96]{0:T(128)S(1)} %bitcast.14, s32[1]{0:T(128)} %bitcast.6.count_hbm, s32[1,256]{1,0:T(1,128)S(1)} %bitcast.8), custom_call_target="tpu_custom_call" | custom-call | tf_op jit(solution)/shard_map/first_terms/pallas_call | solution.py:172
  7.8 0.5 collective-permute-start
  8.3 1.2 %collective-permute-done.came_ref = f32[256,256]{1,0:T(8,128)S(1)} collective-permute-done((f32[256,256]{1,0:T(8,128)S(1)}, f32[256,256]{1,0:T(8,128)S(1)}, u32[]{:S(2)}, u32[]{:S(2)}) %collective-permute-start) | collective-permute-done | bytes 262176 | tf_op jit(solution)/shard_map/ppermute | solution.py:145
  9.5 0.1 pair_sums.2
  9.5 2.9 %collective-permute-start.8 = (f32[16,256]{1,0:T(8,128)S(1)}, f32[16,256]{1,0:T(8,128)S(1)}, u32[]{:S(2)}, u32[]{:S(2)}) collective-permute-start(f32[16,256]{1,0:T(8,128)S(1)} %get-tuple-element.29), channel_id=1, source_target_pairs={{0,2},{2,4},{4,6},{6,8},{8,10},{10,12},{12,14},{14,0},{1,3},{3,5},... | collective-permute-start | bytes 49160 | tf_op jit(solution)/shard_map/ppermute | solution.py:148
  12.4 1.6 %collective-permute-start.9 = (f32[16,256]{1,0:T(8,128)S(1)}, f32[16,256]{1,0:T(8,128)S(1)}, u32[]{:S(2)}, u32[]{:S(2)}) collective-permute-start(f32[16,256]{1,0:T(8,128)S(1)} %get-tuple-element.30), channel_id=1, source_target_pairs={{0,4},{2,6},{4,8},{6,10},{8,12},{10,14},{12,0},{14,2},{1,5},{3,7},... | collective-permute-start | bytes 49160 | tf_op jit(solution)/shard_map/ppermute | solution.py:148
  14.0 2.6 %collective-permute-start.10 = (f32[16,256]{1,0:T(8,128)S(1)}, f32[16,256]{1,0:T(8,128)S(1)}, u32[]{:S(2)}, u32[]{:S(2)}) collective-permute-start(f32[16,256]{1,0:T(8,128)S(1)} %get-tuple-element.31), channel_id=1, source_target_pairs={{0,6},{2,8},{4,10},{6,12},{8,14},{10,0},{12,2},{14,4},{1,7},{3,9},... | collective-permute-start | bytes 49160 | tf_op jit(solution)/shard_map/ppermute | solution.py:148
  16.6 1.2 %collective-permute-start.11 = (f32[16,256]{1,0:T(8,128)S(1)}, f32[16,256]{1,0:T(8,128)S(1)}, u32[]{:S(2)}, u32[]{:S(2)}) collective-permute-start(f32[16,256]{1,0:T(8,128)S(1)} %get-tuple-element.32), channel_id=1, source_target_pairs={{0,8},{2,10},{4,12},{6,14},{8,0},{10,2},{12,4},{14,6},{1,9},{3,11}... | collective-permute-start | bytes 49160 | tf_op jit(solution)/shard_map/ppermute | solution.py:148
  17.8 2.6 %collective-permute-start.12 = (f32[16,256]{1,0:T(8,128)S(1)}, f32[16,256]{1,0:T(8,128)S(1)}, u32[]{:S(2)}, u32[]{:S(2)}) collective-permute-start(f32[16,256]{1,0:T(8,128)S(1)} %get-tuple-element.33), channel_id=1, source_target_pairs={{0,10},{2,12},{4,14},{6,0},{8,2},{10,4},{12,6},{14,8},{1,11},{3,13... | collective-permute-start | bytes 49160 | tf_op jit(solution)/shard_map/ppermute | solution.py:148
  20.4 0.0 collective-permute-done.8.refs_1_
  20.4 1.3 %collective-permute-start.13 = (f32[16,256]{1,0:T(8,128)S(1)}, f32[16,256]{1,0:T(8,128)S(1)}, u32[]{:S(2)}, u32[]{:S(2)}) collective-permute-start(f32[16,256]{1,0:T(8,128)S(1)} %get-tuple-element.34), channel_id=1, source_target_pairs={{0,12},{2,14},{4,0},{6,2},{8,4},{10,6},{12,8},{14,10},{1,13},{3,15... | collective-permute-start | bytes 49160 | tf_op jit(solution)/shard_map/ppermute | solution.py:148
  21.8 0.0 collective-permute-done.9.refs_2_
  21.8 1.4 %collective-permute-start.14 = (f32[16,256]{1,0:T(8,128)S(1)}, f32[16,256]{1,0:T(8,128)S(1)}, u32[]{:S(2)}, u32[]{:S(2)}) collective-permute-start(f32[16,256]{1,0:T(8,128)S(1)} %get-tuple-element.35), channel_id=1, source_target_pairs={{0,14},{2,0},{4,2},{6,4},{8,6},{10,8},{12,10},{14,12},{1,15},{3,1}... | collective-permute-start | bytes 49160 | tf_op jit(solution)/shard_map/ppermute | solution.py:148
  23.2 0.0 collective-permute-done.10.refs_3_
  23.2 0.9 %collective-permute-done.13.refs_6_ = f32[16,256]{1,0:T(8,128)S(1)} collective-permute-done((f32[16,256]{1,0:T(8,128)S(1)}, f32[16,256]{1,0:T(8,128)S(1)}, u32[]{:S(2)}, u32[]{:S(2)}) %collective-permute-start.13) | collective-permute-done | bytes 16416 | tf_op jit(solution)/shard_map/ppermute | solution.py:148
  24.2 1.4 %collective-permute-done.14.refs_7_ = f32[16,256]{1,0:T(8,128)S(1)} collective-permute-done((f32[16,256]{1,0:T(8,128)S(1)}, f32[16,256]{1,0:T(8,128)S(1)}, u32[]{:S(2)}, u32[]{:S(2)}) %collective-permute-start.14) | collective-permute-done | bytes 16416 | tf_op jit(solution)/shard_map/ppermute | solution.py:148
  25.5 0.1 collective-permute-start.15
  25.6 4.2 %collective-permute-start.7 = (bf16[128,256]{1,0:T(8,128)(2,1)S(1)}, bf16[128,256]{1,0:T(8,128)(2,1)S(1)}, u32[]{:S(2)}, u32[]{:S(2)}) collective-permute-start(bf16[128,256]{1,0:T(8,128)(2,1)S(1)} %get-tuple-element.27.refs_0_), channel_id=1, source_target_pairs={{0,14},{2,0},{4,2},{6,4},{8,6},{10,8},{12,10},{14,12},{1,15},{3,1}... | collective-permute-start | bytes 196616 | tf_op jit(solution)/shard_map/ppermute | solution.py:148
  29.8 1.1 %collective-permute-start.22 = (bf16[32,256]{1,0:T(8,128)(2,1)S(1)}, bf16[32,256]{1,0:T(8,128)(2,1)S(1)}, u32[]{:S(2)}, u32[]{:S(2)}) collective-permute-start(bf16[32,256]{1,0:T(8,128)(2,1)S(1)} %maximum_select_fusion.refs_8_), channel_id=1, source_target_pairs={{0,14},{2,0},{4,2},{6,4},{8,6},{10,8},{12,10},{14,12},{1,15},{3,1}... | collective-permute-start | bytes 49160 | tf_op jit(solution)/shard_map/ppermute | solution.py:148
  30.9 3.9 %collective-permute-start.20 = (bf16[32,256]{1,0:T(8,128)(2,1)S(1)}, bf16[32,256]{1,0:T(8,128)(2,1)S(1)}, u32[]{:S(2)}, u32[]{:S(2)}) collective-permute-start(bf16[32,256]{1,0:T(8,128)(2,1)S(1)} %maximum_select_fusion.refs_8_), channel_id=1, source_target_pairs={{0,10},{2,12},{4,14},{6,0},{8,2},{10,4},{12,6},{14,8},{1,11},{3,13... | collective-permute-start | bytes 49160 | tf_op jit(solution)/shard_map/ppermute | solution.py:148
  34.8 4.7 %collective-permute-start.18 = (bf16[32,256]{1,0:T(8,128)(2,1)S(1)}, bf16[32,256]{1,0:T(8,128)(2,1)S(1)}, u32[]{:S(2)}, u32[]{:S(2)}) collective-permute-start(bf16[32,256]{1,0:T(8,128)(2,1)S(1)} %maximum_select_fusion.refs_8_), channel_id=1, source_target_pairs={{0,6},{2,8},{4,10},{6,12},{8,14},{10,0},{12,2},{14,4},{1,7},{3,9},... | collective-permute-start | bytes 49160 | tf_op jit(solution)/shard_map/ppermute | solution.py:148
  39.5 1.0 %collective-permute-start.16 = (bf16[32,256]{1,0:T(8,128)(2,1)S(1)}, bf16[32,256]{1,0:T(8,128)(2,1)S(1)}, u32[]{:S(2)}, u32[]{:S(2)}) collective-permute-start(bf16[32,256]{1,0:T(8,128)(2,1)S(1)} %maximum_select_fusion.refs_8_), channel_id=1, source_target_pairs={{0,2},{2,4},{4,6},{6,8},{8,10},{10,12},{12,14},{14,0},{1,3},{3,5},... | collective-permute-start | bytes 49160 | tf_op jit(solution)/shard_map/ppermute | solution.py:148
  40.6 0.4 collective-permute-done.18.refs_11_
  41.0 3.9 %collective-permute-start.5 = (bf16[128,256]{1,0:T(8,128)(2,1)S(1)}, bf16[128,256]{1,0:T(8,128)(2,1)S(1)}, u32[]{:S(2)}, u32[]{:S(2)}) collective-permute-start(bf16[128,256]{1,0:T(8,128)(2,1)S(1)} %get-tuple-element.27.refs_0_), channel_id=1, source_target_pairs={{0,10},{2,12},{4,14},{6,0},{8,2},{10,4},{12,6},{14,8},{1,11},{3,13... | collective-permute-start | bytes 196616 | tf_op jit(solution)/shard_map/ppermute | solution.py:148
  44.8 0.4 collective-permute-done.17.refs_10_
  45.3 0.9 %collective-permute-done.16.refs_9_ = bf16[32,256]{1,0:T(8,128)(2,1)S(1)} collective-permute-done((bf16[32,256]{1,0:T(8,128)(2,1)S(1)}, bf16[32,256]{1,0:T(8,128)(2,1)S(1)}, u32[]{:S(2)}, u32[]{:S(2)}) %collective-permute-start.16) | collective-permute-done | bytes 16416 | tf_op jit(solution)/shard_map/ppermute | solution.py:148
  46.1 0.3 collective-permute-start.3
  46.4 2.3 %collective-permute-start.2 = (bf16[128,256]{1,0:T(8,128)(2,1)S(1)}, bf16[128,256]{1,0:T(8,128)(2,1)S(1)}, u32[]{:S(2)}, u32[]{:S(2)}) collective-permute-start(bf16[128,256]{1,0:T(8,128)(2,1)S(1)} %get-tuple-element.27.refs_0_), channel_id=1, source_target_pairs={{0,4},{2,6},{4,8},{6,10},{8,12},{10,14},{12,0},{14,2},{1,5},{3,7},... | collective-permute-start | bytes 196616 | tf_op jit(solution)/shard_map/ppermute | solution.py:148
  48.7 1.7 %collective-permute-start.1 = (bf16[128,256]{1,0:T(8,128)(2,1)S(1)}, bf16[128,256]{1,0:T(8,128)(2,1)S(1)}, u32[]{:S(2)}, u32[]{:S(2)}) collective-permute-start(bf16[128,256]{1,0:T(8,128)(2,1)S(1)} %get-tuple-element.27.refs_0_), channel_id=1, source_target_pairs={{0,2},{2,4},{4,6},{6,8},{8,10},{10,12},{12,14},{14,0},{1,3},{3,5},... | collective-permute-start | bytes 196616 | tf_op jit(solution)/shard_map/ppermute | solution.py:148
  50.4 2.5 %collective-permute-done.4.refs_4_ = bf16[128,256]{1,0:T(8,128)(2,1)S(1)} collective-permute-done((bf16[128,256]{1,0:T(8,128)(2,1)S(1)}, bf16[128,256]{1,0:T(8,128)(2,1)S(1)}, u32[]{:S(2)}, u32[]{:S(2)}) %collective-permute-start.4) | collective-permute-done | bytes 65568 | tf_op jit(solution)/shard_map/ppermute | solution.py:148
  52.9 0.6 collective-permute-done.3.refs_3_
  53.5 2.3 %collective-permute-done.1.refs_1_ = bf16[128,256]{1,0:T(8,128)(2,1)S(1)} collective-permute-done((bf16[128,256]{1,0:T(8,128)(2,1)S(1)}, bf16[128,256]{1,0:T(8,128)(2,1)S(1)}, u32[]{:S(2)}, u32[]{:S(2)}) %collective-permute-start.1) | collective-permute-done | bytes 65568 | tf_op jit(solution)/shard_map/ppermute | solution.py:148
  55.9 1.0 %later_terms.1 = (f32[256,256]{1,0:T(8,128)S(1)}, f32[256,256]{1,0:T(8,128)S(1)}) custom-call(bf16[128,256]{1,0:T(8,128)(2,1)S(1)} %get-tuple-element.27.refs_0_, bf16[128,256]{1,0:T(8,128)(2,1)S(1)} %collective-permute-done.1.refs_1_, bf16[128,256]{1,0:T(8,128)(2,1)S(1)} %collective-permute-done.2.refs_2_, ...), custom_call_target="tpu_custom_call" | custom-call | tf_op jit(solution)/shard_map/later_terms/pallas_call | solution.py:201
  56.8 0.1 collective-permute-start.23
  56.9 1.5 %collective-permute-done.23.came_ref = f32[256,256]{1,0:T(8,128)S(1)} collective-permute-done((f32[256,256]{1,0:T(8,128)S(1)}, f32[256,256]{1,0:T(8,128)S(1)}, u32[]{:S(2)}, u32[]{:S(2)}) %collective-permute-start.23) | collective-permute-done | bytes 262176 | tf_op jit(solution)/shard_map/ppermute | solution.py:145
  58.5 0.7 pair_sums.3
  59.2 2.1 %collective-permute-start.26 = (f32[16,256]{1,0:T(8,128)S(1)}, f32[16,256]{1,0:T(8,128)S(1)}, u32[]{:S(2)}, u32[]{:S(2)}) collective-permute-start(f32[16,256]{1,0:T(8,128)S(1)} %get-tuple-element.43), channel_id=1, source_target_pairs={{0,6},{2,8},{4,10},{6,12},{8,14},{10,0},{12,2},{14,4},{1,7},{3,9},... | collective-permute-start | bytes 49160 | tf_op jit(solution)/shard_map/ppermute | solution.py:148
  61.3 3.1 %collective-permute-start.27 = (f32[16,256]{1,0:T(8,128)S(1)}, f32[16,256]{1,0:T(8,128)S(1)}, u32[]{:S(2)}, u32[]{:S(2)}) collective-permute-start(f32[16,256]{1,0:T(8,128)S(1)} %get-tuple-element.44), channel_id=1, source_target_pairs={{0,8},{2,10},{4,12},{6,14},{8,0},{10,2},{12,4},{14,6},{1,9},{3,11}... | collective-permute-start | bytes 49160 | tf_op jit(solution)/shard_map/ppermute | solution.py:148
  64.5 1.0 %collective-permute-start.28 = (f32[16,256]{1,0:T(8,128)S(1)}, f32[16,256]{1,0:T(8,128)S(1)}, u32[]{:S(2)}, u32[]{:S(2)}) collective-permute-start(f32[16,256]{1,0:T(8,128)S(1)} %get-tuple-element.45), channel_id=1, source_target_pairs={{0,10},{2,12},{4,14},{6,0},{8,2},{10,4},{12,6},{14,8},{1,11},{3,13... | collective-permute-start | bytes 49160 | tf_op jit(solution)/shard_map/ppermute | solution.py:148
  65.4 0.2 collective-permute-done.24.refs_1_
  65.6 1.8 %collective-permute-start.29 = (f32[16,256]{1,0:T(8,128)S(1)}, f32[16,256]{1,0:T(8,128)S(1)}, u32[]{:S(2)}, u32[]{:S(2)}) collective-permute-start(f32[16,256]{1,0:T(8,128)S(1)} %get-tuple-element.46), channel_id=1, source_target_pairs={{0,12},{2,14},{4,0},{6,2},{8,4},{10,6},{12,8},{14,10},{1,13},{3,15... | collective-permute-start | bytes 49160 | tf_op jit(solution)/shard_map/ppermute | solution.py:148
  67.4 2.0 %collective-permute-start.30 = (f32[16,256]{1,0:T(8,128)S(1)}, f32[16,256]{1,0:T(8,128)S(1)}, u32[]{:S(2)}, u32[]{:S(2)}) collective-permute-start(f32[16,256]{1,0:T(8,128)S(1)} %get-tuple-element.47), channel_id=1, source_target_pairs={{0,14},{2,0},{4,2},{6,4},{8,6},{10,8},{12,10},{14,12},{1,15},{3,1}... | collective-permute-start | bytes 49160 | tf_op jit(solution)/shard_map/ppermute | solution.py:148
  69.4 1.7 %collective-permute-done.30.refs_7_ = f32[16,256]{1,0:T(8,128)S(1)} collective-permute-done((f32[16,256]{1,0:T(8,128)S(1)}, f32[16,256]{1,0:T(8,128)S(1)}, u32[]{:S(2)}, u32[]{:S(2)}) %collective-permute-start.30) | collective-permute-done | bytes 16416 | tf_op jit(solution)/shard_map/ppermute | solution.py:148
  71.1 0.6 hub_sums.3
  (31 shorter events, 0.1 us)
Async XLA Ops:
  1.3 1.9 %copy-start = (bf16[1,1,96,128,128]{4,3,2,1,0:T(8,128)(2,1)S(1)}, bf16[1,1,96,128,128]{4,3,2,1,0:T(8,128)(2,1)}, u32[]{:S(2)}) copy-start(bf16[1,1,96,128,128]{4,3,2,1,0:T(8,128)(2,1)} %param.5) | copy-start | bytes 9437188
  3.2 0.7 copy-start.1
  3.8 0.7 copy-start.3
  4.5 0.7 copy-start.4
  5.2 53.3 %copy-start.2 = (s32[256]{0:T(256)S(1)}, s32[256]{0:T(256)}, u32[]{:S(2)}) copy-start(s32[256]{0:T(256)} %param.9) | copy-start | bytes 3076
  7.8 1.7 %collective-permute-start = (f32[256,256]{1,0:T(8,128)S(1)}, f32[256,256]{1,0:T(8,128)S(1)}, u32[]{:S(2)}, u32[]{:S(2)}) collective-permute-start(f32[256,256]{1,0:T(8,128)S(1)} %get-tuple-element.26), channel_id=1, source_target_pairs={{0,1},{1,0},{2,3},{3,2},{4,5},{5,4},{6,7},{7,6},{8,9},{9,8},{10,11... | collective-permute-start | bytes 786440 | tf_op jit(solution)/shard_map/ppermute | solution.py:145
  9.5 10.9 %collective-permute-start.8 = (f32[16,256]{1,0:T(8,128)S(1)}, f32[16,256]{1,0:T(8,128)S(1)}, u32[]{:S(2)}, u32[]{:S(2)}) collective-permute-start(f32[16,256]{1,0:T(8,128)S(1)} %get-tuple-element.29), channel_id=1, source_target_pairs={{0,2},{2,4},{4,6},{6,8},{8,10},{10,12},{12,14},{14,0},{1,3},{3,5},... | collective-permute-start | bytes 49160 | tf_op jit(solution)/shard_map/ppermute | solution.py:148
  12.4 9.3 %collective-permute-start.9 = (f32[16,256]{1,0:T(8,128)S(1)}, f32[16,256]{1,0:T(8,128)S(1)}, u32[]{:S(2)}, u32[]{:S(2)}) collective-permute-start(f32[16,256]{1,0:T(8,128)S(1)} %get-tuple-element.30), channel_id=1, source_target_pairs={{0,4},{2,6},{4,8},{6,10},{8,12},{10,14},{12,0},{14,2},{1,5},{3,7},... | collective-permute-start | bytes 49160 | tf_op jit(solution)/shard_map/ppermute | solution.py:148
  14.0 9.2 %collective-permute-start.10 = (f32[16,256]{1,0:T(8,128)S(1)}, f32[16,256]{1,0:T(8,128)S(1)}, u32[]{:S(2)}, u32[]{:S(2)}) collective-permute-start(f32[16,256]{1,0:T(8,128)S(1)} %get-tuple-element.31), channel_id=1, source_target_pairs={{0,6},{2,8},{4,10},{6,12},{8,14},{10,0},{12,2},{14,4},{1,7},{3,9},... | collective-permute-start | bytes 49160 | tf_op jit(solution)/shard_map/ppermute | solution.py:148
  16.6 6.6 %collective-permute-start.11 = (f32[16,256]{1,0:T(8,128)S(1)}, f32[16,256]{1,0:T(8,128)S(1)}, u32[]{:S(2)}, u32[]{:S(2)}) collective-permute-start(f32[16,256]{1,0:T(8,128)S(1)} %get-tuple-element.32), channel_id=1, source_target_pairs={{0,8},{2,10},{4,12},{6,14},{8,0},{10,2},{12,4},{14,6},{1,9},{3,11}... | collective-permute-start | bytes 49160 | tf_op jit(solution)/shard_map/ppermute | solution.py:148
  17.8 5.4 %collective-permute-start.12 = (f32[16,256]{1,0:T(8,128)S(1)}, f32[16,256]{1,0:T(8,128)S(1)}, u32[]{:S(2)}, u32[]{:S(2)}) collective-permute-start(f32[16,256]{1,0:T(8,128)S(1)} %get-tuple-element.33), channel_id=1, source_target_pairs={{0,10},{2,12},{4,14},{6,0},{8,2},{10,4},{12,6},{14,8},{1,11},{3,13... | collective-permute-start | bytes 49160 | tf_op jit(solution)/shard_map/ppermute | solution.py:148
  20.4 3.7 %collective-permute-start.13 = (f32[16,256]{1,0:T(8,128)S(1)}, f32[16,256]{1,0:T(8,128)S(1)}, u32[]{:S(2)}, u32[]{:S(2)}) collective-permute-start(f32[16,256]{1,0:T(8,128)S(1)} %get-tuple-element.34), channel_id=1, source_target_pairs={{0,12},{2,14},{4,0},{6,2},{8,4},{10,6},{12,8},{14,10},{1,13},{3,15... | collective-permute-start | bytes 49160 | tf_op jit(solution)/shard_map/ppermute | solution.py:148
  21.8 3.7 %collective-permute-start.14 = (f32[16,256]{1,0:T(8,128)S(1)}, f32[16,256]{1,0:T(8,128)S(1)}, u32[]{:S(2)}, u32[]{:S(2)}) collective-permute-start(f32[16,256]{1,0:T(8,128)S(1)} %get-tuple-element.35), channel_id=1, source_target_pairs={{0,14},{2,0},{4,2},{6,4},{8,6},{10,8},{12,10},{14,12},{1,15},{3,1}... | collective-permute-start | bytes 49160 | tf_op jit(solution)/shard_map/ppermute | solution.py:148
  25.5 4.3 %collective-permute-start.15 = (bf16[16,256]{1,0:T(8,128)(2,1)S(1)}, bf16[16,256]{1,0:T(8,128)(2,1)S(1)}, u32[]{:S(2)}, u32[]{:S(2)}) collective-permute-start(bf16[16,256]{1,0:T(8,128)(2,1)S(1)} %hub_sums.2), channel_id=1, source_target_pairs={{0,1},{1,0},{2,3},{3,2},{4,5},{5,4},{6,7},{7,6},{8,9},{9,8},{10,11... | collective-permute-start | bytes 24584 | tf_op jit(solution)/shard_map/ppermute | solution.py:145
  25.6 20.8 %collective-permute-start.7 = (bf16[128,256]{1,0:T(8,128)(2,1)S(1)}, bf16[128,256]{1,0:T(8,128)(2,1)S(1)}, u32[]{:S(2)}, u32[]{:S(2)}) collective-permute-start(bf16[128,256]{1,0:T(8,128)(2,1)S(1)} %get-tuple-element.27.refs_0_), channel_id=1, source_target_pairs={{0,14},{2,0},{4,2},{6,4},{8,6},{10,8},{12,10},{14,12},{1,15},{3,1}... | collective-permute-start | bytes 196616 | tf_op jit(solution)/shard_map/ppermute | solution.py:148
  29.8 18.9 %collective-permute-start.6 = (bf16[128,256]{1,0:T(8,128)(2,1)S(1)}, bf16[128,256]{1,0:T(8,128)(2,1)S(1)}, u32[]{:S(2)}, u32[]{:S(2)}) collective-permute-start(bf16[128,256]{1,0:T(8,128)(2,1)S(1)} %get-tuple-element.27.refs_0_), channel_id=1, source_target_pairs={{0,12},{2,14},{4,0},{6,2},{8,4},{10,6},{12,8},{14,10},{1,13},{3,15... | collective-permute-start | bytes 196616 | tf_op jit(solution)/shard_map/ppermute | solution.py:148
  29.8 5.0 %collective-permute-start.22 = (bf16[32,256]{1,0:T(8,128)(2,1)S(1)}, bf16[32,256]{1,0:T(8,128)(2,1)S(1)}, u32[]{:S(2)}, u32[]{:S(2)}) collective-permute-start(bf16[32,256]{1,0:T(8,128)(2,1)S(1)} %maximum_select_fusion.refs_8_), channel_id=1, source_target_pairs={{0,14},{2,0},{4,2},{6,4},{8,6},{10,8},{12,10},{14,12},{1,15},{3,1}... | collective-permute-start | bytes 49160 | tf_op jit(solution)/shard_map/ppermute | solution.py:148
  30.9 3.9 %collective-permute-start.21 = (bf16[32,256]{1,0:T(8,128)(2,1)S(1)}, bf16[32,256]{1,0:T(8,128)(2,1)S(1)}, u32[]{:S(2)}, u32[]{:S(2)}) collective-permute-start(bf16[32,256]{1,0:T(8,128)(2,1)S(1)} %maximum_select_fusion.refs_8_), channel_id=1, source_target_pairs={{0,12},{2,14},{4,0},{6,2},{8,4},{10,6},{12,8},{14,10},{1,13},{3,15... | collective-permute-start | bytes 49160 | tf_op jit(solution)/shard_map/ppermute | solution.py:148
  30.9 8.6 %collective-permute-start.20 = (bf16[32,256]{1,0:T(8,128)(2,1)S(1)}, bf16[32,256]{1,0:T(8,128)(2,1)S(1)}, u32[]{:S(2)}, u32[]{:S(2)}) collective-permute-start(bf16[32,256]{1,0:T(8,128)(2,1)S(1)} %maximum_select_fusion.refs_8_), channel_id=1, source_target_pairs={{0,10},{2,12},{4,14},{6,0},{8,2},{10,4},{12,6},{14,8},{1,11},{3,13... | collective-permute-start | bytes 49160 | tf_op jit(solution)/shard_map/ppermute | solution.py:148
  34.8 4.7 %collective-permute-start.19 = (bf16[32,256]{1,0:T(8,128)(2,1)S(1)}, bf16[32,256]{1,0:T(8,128)(2,1)S(1)}, u32[]{:S(2)}, u32[]{:S(2)}) collective-permute-start(bf16[32,256]{1,0:T(8,128)(2,1)S(1)} %maximum_select_fusion.refs_8_), channel_id=1, source_target_pairs={{0,8},{2,10},{4,12},{6,14},{8,0},{10,2},{12,4},{14,6},{1,9},{3,11}... | collective-permute-start | bytes 49160 | tf_op jit(solution)/shard_map/ppermute | solution.py:148
  34.8 6.1 %collective-permute-start.18 = (bf16[32,256]{1,0:T(8,128)(2,1)S(1)}, bf16[32,256]{1,0:T(8,128)(2,1)S(1)}, u32[]{:S(2)}, u32[]{:S(2)}) collective-permute-start(bf16[32,256]{1,0:T(8,128)(2,1)S(1)} %maximum_select_fusion.refs_8_), channel_id=1, source_target_pairs={{0,6},{2,8},{4,10},{6,12},{8,14},{10,0},{12,2},{14,4},{1,7},{3,9},... | collective-permute-start | bytes 49160 | tf_op jit(solution)/shard_map/ppermute | solution.py:148
  39.5 5.7 %collective-permute-start.17 = (bf16[32,256]{1,0:T(8,128)(2,1)S(1)}, bf16[32,256]{1,0:T(8,128)(2,1)S(1)}, u32[]{:S(2)}, u32[]{:S(2)}) collective-permute-start(bf16[32,256]{1,0:T(8,128)(2,1)S(1)} %maximum_select_fusion.refs_8_), channel_id=1, source_target_pairs={{0,4},{2,6},{4,8},{6,10},{8,12},{10,14},{12,0},{14,2},{1,5},{3,7},... | collective-permute-start | bytes 49160 | tf_op jit(solution)/shard_map/ppermute | solution.py:148
  39.5 6.6 %collective-permute-start.16 = (bf16[32,256]{1,0:T(8,128)(2,1)S(1)}, bf16[32,256]{1,0:T(8,128)(2,1)S(1)}, u32[]{:S(2)}, u32[]{:S(2)}) collective-permute-start(bf16[32,256]{1,0:T(8,128)(2,1)S(1)} %maximum_select_fusion.refs_8_), channel_id=1, source_target_pairs={{0,2},{2,4},{4,6},{6,8},{8,10},{10,12},{12,14},{14,0},{1,3},{3,5},... | collective-permute-start | bytes 49160 | tf_op jit(solution)/shard_map/ppermute | solution.py:148
  41.0 9.4 %collective-permute-start.5 = (bf16[128,256]{1,0:T(8,128)(2,1)S(1)}, bf16[128,256]{1,0:T(8,128)(2,1)S(1)}, u32[]{:S(2)}, u32[]{:S(2)}) collective-permute-start(bf16[128,256]{1,0:T(8,128)(2,1)S(1)} %get-tuple-element.27.refs_0_), channel_id=1, source_target_pairs={{0,10},{2,12},{4,14},{6,0},{8,2},{10,4},{12,6},{14,8},{1,11},{3,13... | collective-permute-start | bytes 196616 | tf_op jit(solution)/shard_map/ppermute | solution.py:148
  45.3 7.7 %collective-permute-start.4 = (bf16[128,256]{1,0:T(8,128)(2,1)S(1)}, bf16[128,256]{1,0:T(8,128)(2,1)S(1)}, u32[]{:S(2)}, u32[]{:S(2)}) collective-permute-start(bf16[128,256]{1,0:T(8,128)(2,1)S(1)} %get-tuple-element.27.refs_0_), channel_id=1, source_target_pairs={{0,8},{2,10},{4,12},{6,14},{8,0},{10,2},{12,4},{14,6},{1,9},{3,11}... | collective-permute-start | bytes 196616 | tf_op jit(solution)/shard_map/ppermute | solution.py:148
  46.1 7.4 %collective-permute-start.3 = (bf16[128,256]{1,0:T(8,128)(2,1)S(1)}, bf16[128,256]{1,0:T(8,128)(2,1)S(1)}, u32[]{:S(2)}, u32[]{:S(2)}) collective-permute-start(bf16[128,256]{1,0:T(8,128)(2,1)S(1)} %get-tuple-element.27.refs_0_), channel_id=1, source_target_pairs={{0,6},{2,8},{4,10},{6,12},{8,14},{10,0},{12,2},{14,4},{1,7},{3,9},... | collective-permute-start | bytes 196616 | tf_op jit(solution)/shard_map/ppermute | solution.py:148
  46.4 7.1 %collective-permute-start.2 = (bf16[128,256]{1,0:T(8,128)(2,1)S(1)}, bf16[128,256]{1,0:T(8,128)(2,1)S(1)}, u32[]{:S(2)}, u32[]{:S(2)}) collective-permute-start(bf16[128,256]{1,0:T(8,128)(2,1)S(1)} %get-tuple-element.27.refs_0_), channel_id=1, source_target_pairs={{0,4},{2,6},{4,8},{6,10},{8,12},{10,14},{12,0},{14,2},{1,5},{3,7},... | collective-permute-start | bytes 196616 | tf_op jit(solution)/shard_map/ppermute | solution.py:148
  48.7 7.2 %collective-permute-start.1 = (bf16[128,256]{1,0:T(8,128)(2,1)S(1)}, bf16[128,256]{1,0:T(8,128)(2,1)S(1)}, u32[]{:S(2)}, u32[]{:S(2)}) collective-permute-start(bf16[128,256]{1,0:T(8,128)(2,1)S(1)} %get-tuple-element.27.refs_0_), channel_id=1, source_target_pairs={{0,2},{2,4},{4,6},{6,8},{8,10},{10,12},{12,14},{14,0},{1,3},{3,5},... | collective-permute-start | bytes 196616 | tf_op jit(solution)/shard_map/ppermute | solution.py:148
  56.8 1.6 %collective-permute-start.23 = (f32[256,256]{1,0:T(8,128)S(1)}, f32[256,256]{1,0:T(8,128)S(1)}, u32[]{:S(2)}, u32[]{:S(2)}) collective-permute-start(f32[256,256]{1,0:T(8,128)S(1)} %get-tuple-element.38), channel_id=1, source_target_pairs={{0,1},{1,0},{2,3},{3,2},{4,5},{5,4},{6,7},{7,6},{8,9},{9,8},{10,11... | collective-permute-start | bytes 786440 | tf_op jit(solution)/shard_map/ppermute | solution.py:145
  59.2 6.4 %collective-permute-start.24 = (f32[16,256]{1,0:T(8,128)S(1)}, f32[16,256]{1,0:T(8,128)S(1)}, u32[]{:S(2)}, u32[]{:S(2)}) collective-permute-start(f32[16,256]{1,0:T(8,128)S(1)} %get-tuple-element.41), channel_id=1, source_target_pairs={{0,2},{2,4},{4,6},{6,8},{8,10},{10,12},{12,14},{14,0},{1,3},{3,5},... | collective-permute-start | bytes 49160 | tf_op jit(solution)/shard_map/ppermute | solution.py:148
  59.2 8.2 %collective-permute-start.25 = (f32[16,256]{1,0:T(8,128)S(1)}, f32[16,256]{1,0:T(8,128)S(1)}, u32[]{:S(2)}, u32[]{:S(2)}) collective-permute-start(f32[16,256]{1,0:T(8,128)S(1)} %get-tuple-element.42), channel_id=1, source_target_pairs={{0,4},{2,6},{4,8},{6,10},{8,12},{10,14},{12,0},{14,2},{1,5},{3,7},... | collective-permute-start | bytes 49160 | tf_op jit(solution)/shard_map/ppermute | solution.py:148
  59.2 10.2 %collective-permute-start.26 = (f32[16,256]{1,0:T(8,128)S(1)}, f32[16,256]{1,0:T(8,128)S(1)}, u32[]{:S(2)}, u32[]{:S(2)}) collective-permute-start(f32[16,256]{1,0:T(8,128)S(1)} %get-tuple-element.43), channel_id=1, source_target_pairs={{0,6},{2,8},{4,10},{6,12},{8,14},{10,0},{12,2},{14,4},{1,7},{3,9},... | collective-permute-start | bytes 49160 | tf_op jit(solution)/shard_map/ppermute | solution.py:148
  61.3 8.1 %collective-permute-start.27 = (f32[16,256]{1,0:T(8,128)S(1)}, f32[16,256]{1,0:T(8,128)S(1)}, u32[]{:S(2)}, u32[]{:S(2)}) collective-permute-start(f32[16,256]{1,0:T(8,128)S(1)} %get-tuple-element.44), channel_id=1, source_target_pairs={{0,8},{2,10},{4,12},{6,14},{8,0},{10,2},{12,4},{14,6},{1,9},{3,11}... | collective-permute-start | bytes 49160 | tf_op jit(solution)/shard_map/ppermute | solution.py:148
  64.5 5.0 %collective-permute-start.28 = (f32[16,256]{1,0:T(8,128)S(1)}, f32[16,256]{1,0:T(8,128)S(1)}, u32[]{:S(2)}, u32[]{:S(2)}) collective-permute-start(f32[16,256]{1,0:T(8,128)S(1)} %get-tuple-element.45), channel_id=1, source_target_pairs={{0,10},{2,12},{4,14},{6,0},{8,2},{10,4},{12,6},{14,8},{1,11},{3,13... | collective-permute-start | bytes 49160 | tf_op jit(solution)/shard_map/ppermute | solution.py:148
  65.6 3.8 %collective-permute-start.29 = (f32[16,256]{1,0:T(8,128)S(1)}, f32[16,256]{1,0:T(8,128)S(1)}, u32[]{:S(2)}, u32[]{:S(2)}) collective-permute-start(f32[16,256]{1,0:T(8,128)S(1)} %get-tuple-element.46), channel_id=1, source_target_pairs={{0,12},{2,14},{4,0},{6,2},{8,4},{10,6},{12,8},{14,10},{1,13},{3,15... | collective-permute-start | bytes 49160 | tf_op jit(solution)/shard_map/ppermute | solution.py:148
  67.4 3.7 %collective-permute-start.30 = (f32[16,256]{1,0:T(8,128)S(1)}, f32[16,256]{1,0:T(8,128)S(1)}, u32[]{:S(2)}, u32[]{:S(2)}) collective-permute-start(f32[16,256]{1,0:T(8,128)S(1)} %get-tuple-element.47), channel_id=1, source_target_pairs={{0,14},{2,0},{4,2},{6,4},{8,6},{10,8},{12,10},{14,12},{1,15},{3,1}... | collective-permute-start | bytes 49160 | tf_op jit(solution)/shard_map/ppermute | solution.py:148

commit v3 on v2

--- a/solution.py
+++ b/solution.py
@@ -87,40 +87,41 @@
     write_terms(dims, prod, dense_ref, panel, send_ref, keep_ref)
 
 
-def second_kernel(dims, *refs):
-    n_row, n_col, side = dims
-    scores, hubs = refs[:n_row], refs[n_row:2 * n_row]
-    dense_ref, send_ref, keep_ref, panel, prod = refs[2 * n_row:]
-    share = H // n_row
-    r = lax.axis_index("row")
-    for k in range(n_row):
-        owner = lax.rem(r - k + n_row, n_row)
-        panel[pl.ds(pl.multiple_of(owner * VB, VB), VB), :] = scores[k][...]
-        panel[pl.ds(pl.multiple_of(n_row * VB + owner * share, share), share), :] = hubs[k][...]
+def second_kernel(dims, scores_ref, mine_ref, theirs_ref, dense_ref, send_ref, keep_ref, panel, prod):
+    n_row, n_col, side = dims
+    piece = H // (n_row * n_col)
+    c = lax.axis_index("col")
+    for r in range(n_row):
+        panel[pl.ds(r * VB, VB), :] = scores_ref[r]
+        for ref, col in ((mine_ref, c), (theirs_ref, 1 - c)):
+            start = n_row * VB + (r * n_col + col) * piece
+            panel[pl.ds(pl.multiple_of(start, piece), piece), :] = ref[r]
     write_terms(dims, prod, dense_ref, panel, send_ref, keep_ref)
 
 
-def pair_kernel(dims, src_ref, keep_ref, came_ref, scores_ref, *parts):
+def pair_kernel(dims, src_ref, keep_ref, came_ref, scores_ref, parts_ref):
     n_row, n_col, side = dims
     piece = H // (n_row * n_col)
     r, c = lax.axis_index("row"), lax.axis_index("col")
     tele = one_hot(H + (r * n_col + c) * VB, VB, src_ref[...])
     own = DAMP * (keep_ref[:VB] + came_ref[:VB]) + 0.15 * tele
-    scores_ref[...] = own.astype(scores_ref.dtype)
+    for k in range(scores_ref.shape[0]):
+        scores_ref[k] = own.astype(scores_ref.dtype)
     for k in range(n_row):
-        spot = pl.ds(pl.multiple_of(VB + lax.rem(r + k, n_row) * piece, piece), piece)
-        parts[k][...] = keep_ref[spot, :] + came_ref[spot, :]
-
-
-def hub_kernel(dims, src_ref, *refs):
-    n_row, n_col, side = dims
-    out_ref = refs[n_row]
-    piece = out_ref.shape[0]
-    summed = refs[0][...]
+        spot = slice(VB + k * piece, VB + (k + 1) * piece)
+        parts_ref[k] = keep_ref[spot, :] + came_ref[spot, :]
+
+
+def hub_kernel(dims, src_ref, parts_ref, out_ref):
+    n_row, n_col, side = dims
+    piece = out_ref.shape[1]
+    summed = parts_ref[0]
     for k in range(1, n_row):
-        summed = summed + refs[k][...]
+        summed = summed + parts_ref[k]
     first = (lax.axis_index("row") * n_col + lax.axis_index("col")) * piece
-    out_ref[...] = (DAMP * summed + 0.15 * one_hot(first, piece, src_ref[...])).astype(out_ref.dtype)
+    new = (DAMP * summed + 0.15 * one_hot(first, piece, src_ref[...])).astype(out_ref.dtype)
+    for k in range(out_ref.shape[0]):
+        out_ref[k] = new
 
 
 def fast_body(tiles, tile_row, tile_col, tile_count, sources):
@@ -144,30 +145,29 @@
     def other_core(x):
         return lax.ppermute(x, "col", [(0, 1), (1, 0)])
 
-    def along_row(x, k):
-        return lax.ppermute(x, "row", [(r, (r + k) % n_row) for r in range(n_row)])
-
-    def pair_sums(keep, send, dtype):
-        came = other_core(send)
-        scores, *parts = pl.pallas_call(
+    def to_rows(x):
+        return lax.all_to_all(x, "row", 0, 0)
+
+    def pair_sums(keep, send, copies, dtype):
+        scores, parts = pl.pallas_call(
             functools.partial(pair_kernel, dims),
-            out_shape=(jax.ShapeDtypeStruct((VB, width), dtype),) + (f32((piece, width)),) * n_row,
+            out_shape=(jax.ShapeDtypeStruct((copies, VB, width), dtype), f32((n_row, piece, width))),
             in_specs=[VMEM] * 3,
-            out_specs=[VMEM] * (1 + n_row),
+            out_specs=[VMEM] * 2,
             compiler_params=params(),
             name="pair_sums",
-        )(src, keep, came)
-        return scores, [parts[0]] + [along_row(parts[k], k) for k in range(1, n_row)]
-
-    def hub_sums(parts, dtype):
+        )(src, keep, other_core(send))
+        return scores, to_rows(parts)
+
+    def hub_sums(parts, copies, dtype):
         return pl.pallas_call(
             functools.partial(hub_kernel, dims),
-            out_shape=jax.ShapeDtypeStruct((piece, width), dtype),
-            in_specs=[VMEM] * (1 + n_row),
+            out_shape=jax.ShapeDtypeStruct((copies, piece, width), dtype),
+            in_specs=[VMEM] * 2,
             out_specs=VMEM,
             compiler_params=params(),
             name="hub_sums",
-        )(src, *parts)
+        )(src, parts)
 
     send, keep, dense = pl.pallas_call(
         functools.partial(first_kernel, dims),
@@ -191,24 +191,20 @@
       tile_count.reshape(1), src)
 
     for step in range(ITERS - 1):
-        scores, parts = pair_sums(keep, send, jnp.bfloat16)
-        got = [scores] + [along_row(scores, k) for k in range(1, n_row)]
-        mine = hub_sums(parts, jnp.bfloat16)
-        theirs = other_core(mine)
-        both = jnp.where(lax.axis_index("col") == 0,
-                         jnp.concatenate([mine, theirs]), jnp.concatenate([theirs, mine]))
-        hubs = [both] + [along_row(both, k) for k in range(1, n_row)]
+        scores, parts = pair_sums(keep, send, n_row, jnp.bfloat16)
+        scores = to_rows(scores)
+        mine = to_rows(hub_sums(parts, n_row, jnp.bfloat16))
         send, keep = pl.pallas_call(
             functools.partial(second_kernel, dims),
             out_shape=(f32((half, width)), f32((half, width))),
-            in_specs=[VMEM] * (2 * n_row + 1),
+            in_specs=[VMEM] * 4,
             out_specs=[VMEM] * 2,
             scratch_shapes=product_scratch,
             compiler_params=params(),
             name="later_terms",
-        )(*got, *hubs, dense)
-    scores, parts = pair_sums(keep, send, jnp.float32)
-    return scores.reshape(1, 1, VB, width), hub_sums(parts, jnp.float32)
+        )(scores, mine, other_core(mine), dense)
+    scores, parts = pair_sums(keep, send, 1, jnp.float32)
+    return scores.reshape(1, 1, VB, width), hub_sums(parts, 1, jnp.float32).reshape(piece, width)
 
 
 def plain_body(tiles, tile_row, tile_col, tile_count, sources):

time: 71.9 us -> 65.7 us (0.914)
  starting transfers between devices: 47.5 us -> 4.16 us
  blocking collectives: 0 us -> 34.4 us
  waiting for transfers between devices: 14 us -> 15.7 us
  local copies, waits for them, and re-layouts: 3.87 us -> 4.66 us
    ppermute x28 -> x0, starting transfers between devices: 46.8 us -> none  [along_row(): return lax.ppermute(x, 'row', [(r, (r + k) % n_row) for r in range(n_row)])]
    all_to_all x0 -> x3, blocking collectives: none -> 34.4 us  [to_rows(): return lax.all_to_all(x, 'row', 0, 0)]
    all_to_all x0 -> x1, waiting for transfers between devices: none -> 11.8 us  [to_rows(): return lax.all_to_all(x, 'row', 0, 0)]
    ppermute x28 -> x0, waiting for transfers between devices: 11.3 us -> none  [along_row(): return lax.ppermute(x, 'row', [(r, (r + k) % n_row) for r in range(n_row)])]
    all_to_all x0 -> x1, starting transfers between devices: none -> 3.49 us  [to_rows(): return lax.all_to_all(x, 'row', 0, 0)]
    ppermute x3, waiting for transfers between devices: 2.69 us -> 3.93 us  [other_core(): return lax.ppermute(x, 'col', [(0, 1), (1, 0)])]
    unnamed x10 -> x12, local copies, waits for them, and re-layouts: 3.87 us -> 4.66 us
  transfers between devices with their start and end apart: 31 -> 4, of which waited for: 12 -> 4; matrix products, arithmetic and copies ran while one was open for 0% -> 0% of each run, Pallas kernels for 0% -> 0%
where the time goes in v3:
time: 65.7 us; the launch traced here: 65.3 us
  blocking collectives  34.4 us (52%)
  waiting for transfers between devices  15.7 us (24%)
  Pallas kernels  4.95 us (8%)
  local copies, waits for them, and re-layouts  4.66 us (7%)
  starting transfers between devices  4.16 us (6%)
  between operations  1.35 us (2%)
    all_to_all x3, blocking collectives, to_rows(): return lax.all_to_all(x, 'row', 0, 0)  34.4 us
    all_to_all x1, waiting for transfers between devices, to_rows(): return lax.all_to_all(x, 'row', 0, 0)  11.8 us
    unnamed x12, local copies, waits for them, and re-layouts  4.66 us
    ppermute x3, waiting for transfers between devices, other_core(): return lax.ppermute(x, 'col', [(0, 1), (1, 0)])  3.93 us
    all_to_all x1, starting transfers between devices, to_rows(): return lax.all_to_all(x, 'row', 0, 0)  3.49 us
    pallas_call x1, Pallas kernels, fast_body(): pl.pallas_call(functools.partial(first_kernel, dims), out_shape=(f32((hal...  2.61 us
  transfers between devices with their start and end apart: 4, of which 4 were waited for; matrix products, arithmetic and copies ran while one was open for 0% of the time, Pallas kernels for 0%

profile of v3, /device:TPU:0, one launch (start us, length us, event | category | flops | bytes accessed | tf_op | source)
XLA Modules:
  0.0 65.3 jit_solution(2873045418136023064)
XLA Ops:
  1.3 0.0 copy-start
  1.3 1.9 %copy-done = bf16[1,1,96,128,128]{4,3,2,1,0:T(8,128)(2,1)S(1)} copy-done((bf16[1,1,96,128,128]{4,3,2,1,0:T(8,128)(2,1)S(1)}, bf16[1,1,96,128,128]{4,3,2,1,0:T(8,128)(2,1)}, u32[]{:S(2)}) %copy-start) | copy-done | bytes 3145752
  3.2 0.0 copy-start.2
  3.2 0.7 %copy-done.2 = s32[256]{0:T(256)S(1)} copy-done((s32[256]{0:T(256)S(1)}, s32[256]{0:T(256)}, u32[]{:S(2)}) %copy-start.2) | copy-done | bytes 1048
  3.8 0.0 copy-start.4
  3.8 0.7 %copy-done.4 = s32[1,1,96]{2,1,0:T(1,128)S(1)} copy-done((s32[1,1,96]{2,1,0:T(1,128)S(1)}, s32[1,1,96]{2,1,0:T(1,128)}, u32[]{:S(2)}) %copy-start.4) | copy-done | bytes 408
  4.5 0.0 copy-start.5
  4.5 0.7 %copy-done.5 = s32[1,1,96]{2,1,0:T(1,128)S(1)} copy-done((s32[1,1,96]{2,1,0:T(1,128)S(1)}, s32[1,1,96]{2,1,0:T(1,128)}, u32[]{:S(2)}) %copy-start.5) | copy-done | bytes 408
  5.2 2.6 %first_terms.1 = (f32[256,256]{1,0:T(8,128)S(1)}, f32[256,256]{1,0:T(8,128)S(1)}, bf16[1024,1280]{1,0:T(8,128)(2,1)S(1)}) custom-call(bf16[96,128,128]{2,1,0:T(8,128)(2,1)S(1)} %bitcast.8, s32[96]{0:T(128)S(1)} %bitcast.14, s32[96]{0:T(128)S(1)} %bitcast.15, s32[1]{0:T(128)} %bitcast.7.count_hbm, s32[1,256]{1,0:T(1,128)S(1)} %bitcast.9), custom_call_target="tpu_custom_call" | custom-call | tf_op jit(solution)/shard_map/first_terms/pallas_call | solution.py:172
  7.8 0.0 copy-start.3
  7.8 0.5 collective-permute-start
  8.3 1.2 %collective-permute-done.came_ref = f32[256,256]{1,0:T(8,128)S(1)} collective-permute-done((f32[256,256]{1,0:T(8,128)S(1)}, f32[256,256]{1,0:T(8,128)S(1)}, u32[]{:S(2)}, u32[]{:S(2)}) %collective-permute-start) | collective-permute-done | bytes 262176 | tf_op jit(solution)/shard_map/ppermute | solution.py:146
  9.5 0.1 pair_sums.2
  9.5 0.0 copy-start.1
  9.5 0.8 %copy-done.1 = bf16[8,128,256]{2,1,0:T(8,128)(2,1)} copy-done((bf16[8,128,256]{2,1,0:T(8,128)(2,1)}, bf16[8,128,256]{2,1,0:T(8,128)(2,1)S(1)}, u32[]{:S(2)}) %copy-start.1) | copy-done | bytes 524312
  10.3 14.3 %all_to_all.20.parts_ref = f32[8,16,256]{2,1,0:T(8,128)S(1)} all-to-all(f32[8,16,256]{2,1,0:T(8,128)S(1)} %get-tuple-element.14), channel_id=1, replica_groups=mesh['groups'=2,'row'=8,'col'=2] {'row'}, dimensions={0} | all-to-all | bytes 262144 | tf_op jit(solution)/shard_map/all_to_all | solution.py:149
  24.6 9.4 %all_to_all.21.mine_ref = bf16[8,16,256]{2,1,0:T(8,128)(2,1)S(1)} all-to-all(bf16[8,16,256]{2,1,0:T(8,128)(2,1)S(1)} %hub_sums.2), channel_id=1, replica_groups=mesh['groups'=2,'row'=8,'col'=2] {'row'}, dimensions={0} | all-to-all | bytes 131072 | tf_op jit(solution)/shard_map/all_to_all | solution.py:149
  34.0 3.5 %all-to-all-start = ((bf16[8,128,256]{2,1,0:T(8,128)(2,1)}), bf16[8,128,256]{2,1,0:T(8,128)(2,1)S(1)}, u32[]{:S(2)}, u32[]{:S(2)}) async-start(bf16[8,128,256]{2,1,0:T(8,128)(2,1)} %copy-done.1), calls=%async_computation | async-start | bytes 1048576 | tf_op jit(solution)/shard_map/all_to_all | solution.py:149
  37.5 0.1 collective-permute-start.1
  37.6 1.2 %collective-permute-done.1.theirs_ref = bf16[8,16,256]{2,1,0:T(8,128)(2,1)S(1)} collective-permute-done((bf16[8,16,256]{2,1,0:T(8,128)(2,1)S(1)}, bf16[8,16,256]{2,1,0:T(8,128)(2,1)S(1)}, u32[]{:S(2)}, u32[]{:S(2)}) %collective-permute-start.1) | collective-permute-done | bytes 65568 | tf_op jit(solution)/shard_map/ppermute | solution.py:146
  38.8 11.8 %all-to-all-done.scores_ref = bf16[8,128,256]{2,1,0:T(8,128)(2,1)S(1)} async-done(((bf16[8,128,256]{2,1,0:T(8,128)(2,1)}), bf16[8,128,256]{2,1,0:T(8,128)(2,1)S(1)}, u32[]{:S(2)}, u32[]{:S(2)}) %all-to-all-start) | async-done | bytes 524320 | tf_op jit(solution)/shard_map/all_to_all | solution.py:149
  50.6 0.9 %later_terms.1 = (f32[256,256]{1,0:T(8,128)S(1)}, f32[256,256]{1,0:T(8,128)S(1)}) custom-call(bf16[8,128,256]{2,1,0:T(8,128)(2,1)S(1)} %all-to-all-done.scores_ref, bf16[8,16,256]{2,1,0:T(8,128)(2,1)S(1)} %all_to_all.21.mine_ref, bf16[8,16,256]{2,1,0:T(8,128)(2,1)S(1)} %collective-permute-done.1.theirs_ref, bf16[1024,1280]{1,0:T(8,128)(2,1)S(1)} %get-tuple-element.15.dense_ref), custom_call_target="tpu_custom_call" | custom-call | tf_op jit(solution)/shard_map/later_terms/pallas_call | solution.py:197
  51.6 0.1 collective-permute-start.2
  51.6 1.5 %collective-permute-done.2.came_ref = f32[256,256]{1,0:T(8,128)S(1)} collective-permute-done((f32[256,256]{1,0:T(8,128)S(1)}, f32[256,256]{1,0:T(8,128)S(1)}, u32[]{:S(2)}, u32[]{:S(2)}) %collective-permute-start.2) | collective-permute-done | bytes 262176 | tf_op jit(solution)/shard_map/ppermute | solution.py:146
  53.2 0.0 copy-done.3
  53.2 0.7 %pair_sums.3 = (f32[1,128,256]{2,1,0:T(8,128)}, f32[8,16,256]{2,1,0:T(8,128)S(1)}) custom-call(s32[1,256]{1,0:T(1,128)S(1)} %bitcast.12, f32[256,256]{1,0:T(8,128)S(1)} %get-tuple-element.16.keep_ref, f32[256,256]{1,0:T(8,128)S(1)} %collective-permute-done.2.came_ref), custom_call_target="tpu_custom_call" | custom-call | tf_op jit(solution)/shard_map/pair_sums/pallas_call | solution.py:152
  53.9 10.8 %all_to_all.22.parts_ref = f32[8,16,256]{2,1,0:T(8,128)S(1)} all-to-all(f32[8,16,256]{2,1,0:T(8,128)S(1)} %get-tuple-element.19), channel_id=1, replica_groups=mesh['groups'=2,'row'=8,'col'=2] {'row'}, dimensions={0} | all-to-all | bytes 262144 | tf_op jit(solution)/shard_map/all_to_all | solution.py:149
  64.7 0.6 hub_sums.3
  (1 shorter events, 0.0 us)
Async XLA Ops:
  1.3 1.9 %copy-start = (bf16[1,1,96,128,128]{4,3,2,1,0:T(8,128)(2,1)S(1)}, bf16[1,1,96,128,128]{4,3,2,1,0:T(8,128)(2,1)}, u32[]{:S(2)}) copy-start(bf16[1,1,96,128,128]{4,3,2,1,0:T(8,128)(2,1)} %param.5) | copy-start | bytes 9437188
  3.2 0.7 %copy-start.2 = (s32[256]{0:T(256)S(1)}, s32[256]{0:T(256)}, u32[]{:S(2)}) copy-start(s32[256]{0:T(256)} %param.9) | copy-start | bytes 3076
  3.8 0.7 %copy-start.4 = (s32[1,1,96]{2,1,0:T(1,128)S(1)}, s32[1,1,96]{2,1,0:T(1,128)}, u32[]{:S(2)}) copy-start(s32[1,1,96]{2,1,0:T(1,128)} %param.6) | copy-start | bytes 1156
  4.5 0.7 %copy-start.5 = (s32[1,1,96]{2,1,0:T(1,128)S(1)}, s32[1,1,96]{2,1,0:T(1,128)}, u32[]{:S(2)}) copy-start(s32[1,1,96]{2,1,0:T(1,128)} %param.7) | copy-start | bytes 1156
  7.8 45.4 %copy-start.3 = (s32[256]{0:T(256)S(1)}, s32[256]{0:T(256)}, u32[]{:S(2)}) copy-start(s32[256]{0:T(256)} %param.9) | copy-start | bytes 3076
  7.8 1.7 %collective-permute-start = (f32[256,256]{1,0:T(8,128)S(1)}, f32[256,256]{1,0:T(8,128)S(1)}, u32[]{:S(2)}, u32[]{:S(2)}) collective-permute-start(f32[256,256]{1,0:T(8,128)S(1)} %get-tuple-element.12), channel_id=1, source_target_pairs={{0,1},{1,0},{2,3},{3,2},{4,5},{5,4},{6,7},{7,6},{8,9},{9,8},{10,11... | collective-permute-start | bytes 786440 | tf_op jit(solution)/shard_map/ppermute | solution.py:146
  9.5 0.8 %copy-start.1 = (bf16[8,128,256]{2,1,0:T(8,128)(2,1)}, bf16[8,128,256]{2,1,0:T(8,128)(2,1)S(1)}, u32[]{:S(2)}) copy-start(bf16[8,128,256]{2,1,0:T(8,128)(2,1)S(1)} %get-tuple-element.13) | copy-start | bytes 1572868
  34.0 16.6 %all-to-all-start = ((bf16[8,128,256]{2,1,0:T(8,128)(2,1)}), bf16[8,128,256]{2,1,0:T(8,128)(2,1)S(1)}, u32[]{:S(2)}, u32[]{:S(2)}) async-start(bf16[8,128,256]{2,1,0:T(8,128)(2,1)} %copy-done.1), calls=%async_computation | async-start | bytes 1048576 | tf_op jit(solution)/shard_map/all_to_all | solution.py:149
  37.5 1.3 %collective-permute-start.1 = (bf16[8,16,256]{2,1,0:T(8,128)(2,1)S(1)}, bf16[8,16,256]{2,1,0:T(8,128)(2,1)S(1)}, u32[]{:S(2)}, u32[]{:S(2)}) collective-permute-start(bf16[8,16,256]{2,1,0:T(8,128)(2,1)S(1)} %all_to_all.21.mine_ref), channel_id=1, source_target_pairs={{0,1},{1,0},{2,3},{3,2},{4,5},{5,4},{6,7},{7,6},{8,9},{9,8},{10,11... | collective-permute-start | bytes 196616 | tf_op jit(solution)/shard_map/ppermute | solution.py:146
  51.6 1.6 %collective-permute-start.2 = (f32[256,256]{1,0:T(8,128)S(1)}, f32[256,256]{1,0:T(8,128)S(1)}, u32[]{:S(2)}, u32[]{:S(2)}) collective-permute-start(f32[256,256]{1,0:T(8,128)S(1)} %get-tuple-element.17), channel_id=1, source_target_pairs={{0,1},{1,0},{2,3},{3,2},{4,5},{5,4},{6,7},{7,6},{8,9},{9,8},{10,11... | collective-permute-start | bytes 786440 | tf_op jit(solution)/shard_map/ppermute | solution.py:146

commit v4 on v3

--- a/solution.py
+++ b/solution.py
@@ -12,6 +12,7 @@
 ITERS = 2
 DAMP = 0.85
 CHUNK = 16
+X = 2
 VMEM_LIMIT = 32 * 1024 * 1024
 
 SMEM = pl.BlockSpec(memory_space=pltpu.SMEM)
@@ -28,18 +29,17 @@
     return (ids == src).astype(jnp.float32)
 
 
-def write_terms(dims, prod_ref, dense_ref, panel_ref, send_ref, keep_ref):
+def write_terms(dims, block, prod_ref, dense_ref, panel_ref, send_ref, keep_ref):
     n_row, n_col, side = dims
     rows = dense_ref.shape[0] // 2
-    piece = H // (n_row * n_col)
     c = lax.axis_index("col")
     prod = jnp.dot(dense_ref[...], panel_ref[...], preferred_element_type=jnp.float32)
     prod_ref[...] = prod[:rows] + prod[rows:]
     for ref, col in ((keep_ref, c), (send_ref, 1 - c)):
         ref[:VB] = prod_ref[pl.ds(pl.multiple_of(col * VB, VB), VB), :]
-        for r in range(n_row):
-            start = n_col * VB + (r * n_col + col) * piece
-            ref[VB + r * piece:VB + (r + 1) * piece] = prod_ref[pl.ds(pl.multiple_of(start, piece), piece), :]
+        for k in range(H // n_col // block):
+            start = n_col * VB + (k * n_col + col) * block
+            ref[VB + k * block:VB + (k + 1) * block] = prod_ref[pl.ds(pl.multiple_of(start, block), block), :]
 
 
 def first_kernel(dims, tiles_ref, rows_hbm, cols_hbm, count_hbm, src_hbm,
@@ -84,44 +84,83 @@
         high = whole.astype(jnp.bfloat16)
         dense_ref[pl.ds(r, side), :] = high
         dense_ref[pl.ds(n_rows + r, side), :] = (whole - high.astype(jnp.float32)).astype(jnp.bfloat16)
-    write_terms(dims, prod, dense_ref, panel, send_ref, keep_ref)
+    write_terms(dims, H // n_col, prod, dense_ref, panel, send_ref, keep_ref)
 
 
 def second_kernel(dims, scores_ref, mine_ref, theirs_ref, dense_ref, send_ref, keep_ref, panel, prod):
     n_row, n_col, side = dims
-    piece = H // (n_row * n_col)
+    half = H // n_col
     c = lax.axis_index("col")
     for r in range(n_row):
         panel[pl.ds(r * VB, VB), :] = scores_ref[r]
-        for ref, col in ((mine_ref, c), (theirs_ref, 1 - c)):
-            start = n_row * VB + (r * n_col + col) * piece
-            panel[pl.ds(pl.multiple_of(start, piece), piece), :] = ref[r]
-    write_terms(dims, prod, dense_ref, panel, send_ref, keep_ref)
-
-
-def pair_kernel(dims, src_ref, keep_ref, came_ref, scores_ref, parts_ref):
-    n_row, n_col, side = dims
-    piece = H // (n_row * n_col)
+    for ref, col in ((mine_ref, c), (theirs_ref, 1 - c)):
+        panel[pl.ds(pl.multiple_of(n_row * VB + col * half, half), half), :] = ref[...]
+    write_terms(dims, half // n_row, prod, dense_ref, panel, send_ref, keep_ref)
+
+
+def own_scores(dims, src_ref, keep_ref, came_ref):
+    first = H + (lax.axis_index("row") * dims[1] + lax.axis_index("col")) * VB
+    tele = one_hot(first, VB, src_ref[...])
+    return DAMP * (keep_ref[:VB] + came_ref[:VB]) + 0.15 * tele
+
+
+def spread_kernel(dims, src_ref, keep_ref, came_ref, scores_ref, hold_ref, pass_ref):
+    n_row, n_col, side = dims
+    quarter = hold_ref.shape[0]
+    x = lax.rem(lax.axis_index("row"), X)
+    for ref, place in ((hold_ref, x), (pass_ref, 1 - x)):
+        spot = pl.ds(pl.multiple_of(VB + place * quarter, quarter), quarter)
+        ref[...] = keep_ref[spot, :] + came_ref[spot, :]
+    own = own_scores(dims, src_ref, keep_ref, came_ref).astype(scores_ref.dtype)
+    for k in range(n_row):
+        scores_ref[k] = own
+
+
+def plane_kernel(hold_ref, came_ref, out_ref):
+    out_ref[...] = hold_ref[...] + came_ref[...]
+
+
+def hub_kernel(dims, src_ref, *refs):
+    n_row, n_col, side = dims
+    planes, (out_ref, held) = refs[:-2], refs[-2:]
+    quarter = out_ref.shape[0]
     r, c = lax.axis_index("row"), lax.axis_index("col")
-    tele = one_hot(H + (r * n_col + c) * VB, VB, src_ref[...])
-    own = DAMP * (keep_ref[:VB] + came_ref[:VB]) + 0.15 * tele
-    for k in range(scores_ref.shape[0]):
-        scores_ref[k] = own.astype(scores_ref.dtype)
-    for k in range(n_row):
+    z, x = lax.div(r, X), lax.rem(r, X)
+    n_z = len(planes)
+    for k in range(n_z):
+        held[lax.rem(z - k + n_z, n_z)] = planes[k][...]
+    summed = held[0]
+    for k in range(1, n_z):
+        summed = summed + held[k]
+    first = (c * X + x) * quarter
+    out_ref[...] = (DAMP * summed + 0.15 * one_hot(first, quarter, src_ref[...])).astype(out_ref.dtype)
+
+
+def side_kernel(mine_ref, theirs_ref, out_ref):
+    quarter = mine_ref.shape[0]
+    x = lax.rem(lax.axis_index("row"), X)
+    for ref, place in ((mine_ref, x), (theirs_ref, 1 - x)):
+        out_ref[pl.ds(pl.multiple_of(place * quarter, quarter), quarter), :] = ref[...]
+
+
+def pieces_kernel(dims, keep_ref, came_ref, parts_ref):
+    piece = parts_ref.shape[1]
+    for k in range(parts_ref.shape[0]):
         spot = slice(VB + k * piece, VB + (k + 1) * piece)
         parts_ref[k] = keep_ref[spot, :] + came_ref[spot, :]
 
 
-def hub_kernel(dims, src_ref, parts_ref, out_ref):
-    n_row, n_col, side = dims
-    piece = out_ref.shape[1]
+def last_scores_kernel(dims, src_ref, keep_ref, came_ref, scores_ref):
+    scores_ref[...] = own_scores(dims, src_ref, keep_ref, came_ref)
+
+
+def last_hubs_kernel(dims, src_ref, parts_ref, out_ref):
+    piece = out_ref.shape[0]
     summed = parts_ref[0]
-    for k in range(1, n_row):
+    for k in range(1, parts_ref.shape[0]):
         summed = summed + parts_ref[k]
-    first = (lax.axis_index("row") * n_col + lax.axis_index("col")) * piece
-    new = (DAMP * summed + 0.15 * one_hot(first, piece, src_ref[...])).astype(out_ref.dtype)
-    for k in range(out_ref.shape[0]):
-        out_ref[k] = new
+    first = (lax.axis_index("row") * dims[1] + lax.axis_index("col")) * piece
+    out_ref[...] = DAMP * summed + 0.15 * one_hot(first, piece, src_ref[...])
 
 
 def fast_body(tiles, tile_row, tile_col, tile_count, sources):
@@ -145,29 +184,24 @@
     def other_core(x):
         return lax.ppermute(x, "col", [(0, 1), (1, 0)])
 
-    def to_rows(x):
-        return lax.all_to_all(x, "row", 0, 0)
-
-    def pair_sums(keep, send, copies, dtype):
-        scores, parts = pl.pallas_call(
-            functools.partial(pair_kernel, dims),
-            out_shape=(jax.ShapeDtypeStruct((copies, VB, width), dtype), f32((n_row, piece, width))),
-            in_specs=[VMEM] * 3,
-            out_specs=[VMEM] * 2,
+    def along_row(x, target):
+        return lax.ppermute(x, "row", [(r, target(r)) for r in range(n_row)])
+
+    def other_side(x):
+        return along_row(x, lambda r: r ^ 1)
+
+    def call(kernel, name, out_shape, *args, scratch=()):
+        return pl.pallas_call(
+            kernel,
+            out_shape=out_shape,
+            in_specs=[VMEM] * len(args),
+            out_specs=jax.tree.map(lambda _: VMEM, out_shape),
+            scratch_shapes=scratch,
             compiler_params=params(),
-            name="pair_sums",
-        )(src, keep, other_core(send))
-        return scores, to_rows(parts)
-
-    def hub_sums(parts, copies, dtype):
-        return pl.pallas_call(
-            functools.partial(hub_kernel, dims),
-            out_shape=jax.ShapeDtypeStruct((copies, piece, width), dtype),
-            in_specs=[VMEM] * 2,
-            out_specs=VMEM,
-            compiler_params=params(),
-            name="hub_sums",
-        )(src, parts)
+            name=name,
+        )(*args)
+
+    bind = functools.partial
 
     send, keep, dense = pl.pallas_call(
         functools.partial(first_kernel, dims),
@@ -190,21 +224,28 @@
     )(tiles.reshape(slots, side, side), tile_row.reshape(slots), tile_col.reshape(slots),
       tile_count.reshape(1), src)
 
+    quarter = H // n_col // X
     for step in range(ITERS - 1):
-        scores, parts = pair_sums(keep, send, n_row, jnp.bfloat16)
-        scores = to_rows(scores)
-        mine = to_rows(hub_sums(parts, n_row, jnp.bfloat16))
-        send, keep = pl.pallas_call(
-            functools.partial(second_kernel, dims),
-            out_shape=(f32((half, width)), f32((half, width))),
-            in_specs=[VMEM] * 4,
-            out_specs=[VMEM] * 2,
-            scratch_shapes=product_scratch,
-            compiler_params=params(),
-            name="later_terms",
-        )(scores, mine, other_core(mine), dense)
-    scores, parts = pair_sums(keep, send, 1, jnp.float32)
-    return scores.reshape(1, 1, VB, width), hub_sums(parts, 1, jnp.float32).reshape(piece, width)
+        came = other_core(send)
+        scores, hold, away = call(
+            bind(spread_kernel, dims), "spread",
+            (bf16((n_row, VB, width)), f32((quarter, width)), f32((quarter, width))),
+            src, keep, came)
+        scores = lax.all_to_all(scores, "row", 0, 0)
+        plane = call(plane_kernel, "plane_sum", f32((quarter, width)), hold, other_side(away))
+        planes = [plane] + [along_row(plane, lambda r: (r + X * k) % n_row) for k in range(1, n_row // X)]
+        mine = call(bind(hub_kernel, dims), "hub_sums", bf16((quarter, width)), src, *planes,
+                    scratch=[pltpu.VMEM((n_row // X, quarter, width), jnp.float32)])
+        mine = call(side_kernel, "join_sides", bf16((H // n_col, width)), mine, other_side(mine))
+        send, keep = call(
+            bind(second_kernel, dims), "later_terms", (f32((half, width)), f32((half, width))),
+            scores, mine, other_core(mine), dense, scratch=product_scratch)
+    came = other_core(send)
+    parts = call(bind(pieces_kernel, dims), "hub_pieces", f32((n_row, piece, width)), keep, came)
+    parts = lax.all_to_all(parts, "row", 0, 0)
+    scores = call(bind(last_scores_kernel, dims), "last_scores", f32((VB, width)), src, keep, came)
+    hubs = call(bind(last_hubs_kernel, dims), "last_hubs", f32((piece, width)), src, parts)
+    return scores.reshape(1, 1, VB, width), hubs
 
 
 def plain_body(tiles, tile_row, tile_col, tile_count, sources):

time: 65.7 us -> 58.4 us (0.89)
  blocking collectives: 34.4 us -> 0 us
  starting transfers between devices: 4.16 us -> 19.5 us
  waiting for transfers between devices: 15.7 us -> 26.8 us
  Pallas kernels: 4.95 us -> 5.66 us
    all_to_all x3 -> x0, blocking collectives: 34.4 us -> none  [to_rows(): return lax.all_to_all(x, 'row', 0, 0)]
    ppermute x0 -> x5, waiting for transfers between devices: none -> 16.2 us  [along_row(): return lax.ppermute(x, 'row', [(r, target(r)) for r in range(n_row)])]
    ppermute x0 -> x5, starting transfers between devices: none -> 8.16 us  [along_row(): return lax.ppermute(x, 'row', [(r, target(r)) for r in range(n_row)])]
    all_to_all x1 -> x2, starting transfers between devices: 3.49 us -> 10.5 us  [the longest x1 7.17 us: fast_body(): scores = lax.all_to_all(scores, 'row', 0, 0)]
    all_to_all x1 -> x2, waiting for transfers between devices: 11.8 us -> 6.85 us  [the longest x1 6.85 us: fast_body(): parts = lax.all_to_all(parts, 'row', 0, 0)]
    pallas_call x5 -> x8, Pallas kernels: 2.34 us -> 3.05 us  [call(): pl.pallas_call(kernel, out_shape=out_shape, in_specs=[VMEM] * len(args),...]
  transfers between devices with their start and end apart: 4 -> 10, of which waited for: 4 -> 8; matrix products, arithmetic and copies ran while one was open for 0% -> 0% of each run, Pallas kernels for 0% -> 1%
where the time goes in v4:
time: 58.4 us; the launch traced here: 58.1 us
  waiting for transfers between devices  26.8 us (46%)
  starting transfers between devices  19.5 us (33%)
  Pallas kernels  5.66 us (10%)
  local copies, waits for them, and re-layouts  4.66 us (8%)
  between operations  1.38 us (2%)
    ppermute x5, waiting for transfers between devices, along_row(): return lax.ppermute(x, 'row', [(r, target(r)) for r in range(n_row)])  16.2 us
    ppermute x5, starting transfers between devices, along_row(): return lax.ppermute(x, 'row', [(r, target(r)) for r in range(n_row)])  8.16 us
    all_to_all x1, starting transfers between devices, fast_body(): scores = lax.all_to_all(scores, 'row', 0, 0)  7.17 us
    all_to_all x1, waiting for transfers between devices, fast_body(): parts = lax.all_to_all(parts, 'row', 0, 0)  6.85 us
    unnamed x12, local copies, waits for them, and re-layouts  4.66 us
    ppermute x3, waiting for transfers between devices, other_core(): return lax.ppermute(x, 'col', [(0, 1), (1, 0)])  3.76 us
    all_to_all x1, starting transfers between devices, fast_body(): parts = lax.all_to_all(parts, 'row', 0, 0)  3.37 us
    pallas_call x8, Pallas kernels, call(): pl.pallas_call(kernel, out_shape=out_shape, in_specs=[VMEM] * len(args),...  3.05 us
  transfers between devices with their start and end apart: 10, of which 8 were waited for; matrix products, arithmetic and copies ran while one was open for 0% of the time, Pallas kernels for 1%

profile of v4, /device:TPU:0, one launch (start us, length us, event | category | flops | bytes accessed | tf_op | source)
XLA Modules:
  0.0 58.1 jit_solution(9381486350386507984)
XLA Ops:
  0.6 0.0 copy-start.3
  1.3 0.0 copy-start
  1.3 1.9 %copy-done = bf16[1,1,96,128,128]{4,3,2,1,0:T(8,128)(2,1)S(1)} copy-done((bf16[1,1,96,128,128]{4,3,2,1,0:T(8,128)(2,1)S(1)}, bf16[1,1,96,128,128]{4,3,2,1,0:T(8,128)(2,1)}, u32[]{:S(2)}) %copy-start) | copy-done | bytes 3145752
  3.2 0.0 copy-start.2
  3.2 0.7 %copy-done.2 = s32[256]{0:T(256)S(1)} copy-done((s32[256]{0:T(256)S(1)}, s32[256]{0:T(256)}, u32[]{:S(2)}) %copy-start.2) | copy-done | bytes 1048
  3.9 0.0 copy-start.4
  3.9 0.7 %copy-done.4 = s32[1,1,96]{2,1,0:T(1,128)S(1)} copy-done((s32[1,1,96]{2,1,0:T(1,128)S(1)}, s32[1,1,96]{2,1,0:T(1,128)}, u32[]{:S(2)}) %copy-start.4) | copy-done | bytes 408
  4.5 0.0 copy-start.5
  4.5 0.7 %copy-done.5 = s32[1,1,96]{2,1,0:T(1,128)S(1)} copy-done((s32[1,1,96]{2,1,0:T(1,128)S(1)}, s32[1,1,96]{2,1,0:T(1,128)}, u32[]{:S(2)}) %copy-start.5) | copy-done | bytes 408
  5.2 2.6 %first_terms.1 = (f32[256,256]{1,0:T(8,128)S(1)}, f32[256,256]{1,0:T(8,128)S(1)}, bf16[1024,1280]{1,0:T(8,128)(2,1)S(1)}) custom-call(bf16[96,128,128]{2,1,0:T(8,128)(2,1)S(1)} %bitcast.7, s32[96]{0:T(128)S(1)} %bitcast.13, s32[96]{0:T(128)S(1)} %bitcast.14, s32[1]{0:T(128)} %bitcast.6.count_hbm, s32[1,256]{1,0:T(1,128)S(1)} %bitcast.8), custom_call_target="tpu_custom_call" | custom-call | tf_op jit(solution)/shard_map/first_terms/pallas_call | solution.py:206
  7.8 0.5 collective-permute-start
  8.3 1.2 %collective-permute-done.came_ref = f32[256,256]{1,0:T(8,128)S(1)} collective-permute-done((f32[256,256]{1,0:T(8,128)S(1)}, f32[256,256]{1,0:T(8,128)S(1)}, u32[]{:S(2)}, u32[]{:S(2)}) %collective-permute-start) | collective-permute-done | bytes 262176 | tf_op jit(solution)/shard_map/ppermute | solution.py:185
  9.5 0.1 spread.1
  9.6 0.0 copy-start.1
  9.6 0.8 %copy-done.1 = bf16[8,128,256]{2,1,0:T(8,128)(2,1)} copy-done((bf16[8,128,256]{2,1,0:T(8,128)(2,1)}, bf16[8,128,256]{2,1,0:T(8,128)(2,1)S(1)}, u32[]{:S(2)}) %copy-start.1) | copy-done | bytes 524312
  10.4 7.2 %all-to-all-start = ((bf16[8,128,256]{2,1,0:T(8,128)(2,1)}), bf16[8,128,256]{2,1,0:T(8,128)(2,1)S(1)}, u32[]{:S(2)}, u32[]{:S(2)}) async-start(bf16[8,128,256]{2,1,0:T(8,128)(2,1)} %copy-done.1), calls=%async_computation | async-start | bytes 1048576 | tf_op jit(solution)/shard_map/all_to_all | solution.py:234
  17.5 2.0 %collective-permute-start.1 = (f32[64,256]{1,0:T(8,128)S(1)}, f32[64,256]{1,0:T(8,128)S(1)}, u32[]{:S(2)}, u32[]{:S(2)}) collective-permute-start(f32[64,256]{1,0:T(8,128)S(1)} %get-tuple-element.14), channel_id=1, source_target_pairs={{0,2},{2,0},{4,6},{6,4},{8,10},{10,8},{12,14},{14,12},{1,3},{3,1},... | collective-permute-start | bytes 196616 | tf_op jit(solution)/shard_map/ppermute | solution.py:188
  19.5 5.8 %collective-permute-done.1.came_ref = f32[64,256]{1,0:T(8,128)S(1)} collective-permute-done((f32[64,256]{1,0:T(8,128)S(1)}, f32[64,256]{1,0:T(8,128)S(1)}, u32[]{:S(2)}, u32[]{:S(2)}) %collective-permute-start.1) | collective-permute-done | bytes 65568 | tf_op jit(solution)/shard_map/ppermute | solution.py:188
  25.4 4.0 %collective-permute-start.4 = (f32[64,256]{1,0:T(8,128)S(1)}, f32[64,256]{1,0:T(8,128)S(1)}, u32[]{:S(2)}, u32[]{:S(2)}) collective-permute-start(f32[64,256]{1,0:T(8,128)S(1)} %plane_sum.1.refs_0_), channel_id=1, source_target_pairs={{0,12},{2,14},{4,0},{6,2},{8,4},{10,6},{12,8},{14,10},{1,13},{3,15... | collective-permute-start | bytes 196616 | tf_op jit(solution)/shard_map/ppermute | solution.py:188
  29.4 0.0 collective-permute-start.3
  29.4 0.6 %collective-permute-start.2 = (f32[64,256]{1,0:T(8,128)S(1)}, f32[64,256]{1,0:T(8,128)S(1)}, u32[]{:S(2)}, u32[]{:S(2)}) collective-permute-start(f32[64,256]{1,0:T(8,128)S(1)} %plane_sum.1.refs_0_), channel_id=1, source_target_pairs={{0,4},{2,6},{4,8},{6,10},{8,12},{10,14},{12,0},{14,2},{1,5},{3,7},... | collective-permute-start | bytes 196616 | tf_op jit(solution)/shard_map/ppermute | solution.py:188
  30.0 1.3 %collective-permute-done.4.refs_3_ = f32[64,256]{1,0:T(8,128)S(1)} collective-permute-done((f32[64,256]{1,0:T(8,128)S(1)}, f32[64,256]{1,0:T(8,128)S(1)}, u32[]{:S(2)}, u32[]{:S(2)}) %collective-permute-start.4) | collective-permute-done | bytes 65568 | tf_op jit(solution)/shard_map/ppermute | solution.py:188
  31.3 6.7 %collective-permute-done.3.refs_2_ = f32[64,256]{1,0:T(8,128)S(1)} collective-permute-done((f32[64,256]{1,0:T(8,128)S(1)}, f32[64,256]{1,0:T(8,128)S(1)}, u32[]{:S(2)}, u32[]{:S(2)}) %collective-permute-start.3) | collective-permute-done | bytes 65568 | tf_op jit(solution)/shard_map/ppermute | solution.py:188
  37.9 0.0 collective-permute-done.2.refs_1_
  37.9 0.0 copy-done.3
  37.9 0.1 hub_sums.1.mine_ref
  38.0 1.5 %collective-permute-start.5 = (bf16[64,256]{1,0:T(8,128)(2,1)S(1)}, bf16[64,256]{1,0:T(8,128)(2,1)S(1)}, u32[]{:S(2)}, u32[]{:S(2)}) collective-permute-start(bf16[64,256]{1,0:T(8,128)(2,1)S(1)} %hub_sums.1.mine_ref), channel_id=1, source_target_pairs={{0,2},{2,0},{4,6},{6,4},{8,10},{10,8},{12,14},{14,12},{1,3},{3,1},... | collective-permute-start | bytes 98312 | tf_op jit(solution)/shard_map/ppermute | solution.py:188
  39.5 2.5 %collective-permute-done.5.theirs_ref = bf16[64,256]{1,0:T(8,128)(2,1)S(1)} collective-permute-done((bf16[64,256]{1,0:T(8,128)(2,1)S(1)}, bf16[64,256]{1,0:T(8,128)(2,1)S(1)}, u32[]{:S(2)}, u32[]{:S(2)}) %collective-permute-start.5) | collective-permute-done | bytes 32800 | tf_op jit(solution)/shard_map/ppermute | solution.py:188
  42.0 0.1 collective-permute-start.6
  42.1 1.2 %collective-permute-done.6.theirs_ref = bf16[128,256]{1,0:T(8,128)(2,1)S(1)} collective-permute-done((bf16[128,256]{1,0:T(8,128)(2,1)S(1)}, bf16[128,256]{1,0:T(8,128)(2,1)S(1)}, u32[]{:S(2)}, u32[]{:S(2)}) %collective-permute-start.6) | collective-permute-done | bytes 65568 | tf_op jit(solution)/shard_map/ppermute | solution.py:185
  43.3 0.0 all-to-all-done.scores_ref
  43.3 0.9 %later_terms.1 = (f32[256,256]{1,0:T(8,128)S(1)}, f32[256,256]{1,0:T(8,128)S(1)}) custom-call(bf16[8,128,256]{2,1,0:T(8,128)(2,1)S(1)} %all-to-all-done.scores_ref, bf16[128,256]{1,0:T(8,128)(2,1)S(1)} %join_sides.1.mine_ref, bf16[128,256]{1,0:T(8,128)(2,1)S(1)} %collective-permute-done.6.theirs_ref, bf16[1024,1280]{1,0:T(8,128)(2,1)S(1)} %get-tuple-element.15.dense_ref), custom_call_target="tpu_custom_call" | custom-call | tf_op jit(solution)/shard_map/later_terms/pallas_call | solution.py:194
  44.2 0.2 collective-permute-start.7
  44.5 1.4 %collective-permute-done.7.came_ref = f32[256,256]{1,0:T(8,128)S(1)} collective-permute-done((f32[256,256]{1,0:T(8,128)S(1)}, f32[256,256]{1,0:T(8,128)S(1)}, u32[]{:S(2)}, u32[]{:S(2)}) %collective-permute-start.7) | collective-permute-done | bytes 262176 | tf_op jit(solution)/shard_map/ppermute | solution.py:185
  45.8 0.7 %hub_pieces.1 = f32[8,16,256]{2,1,0:T(8,128)} custom-call(f32[256,256]{1,0:T(8,128)S(1)} %get-tuple-element.16.keep_ref, f32[256,256]{1,0:T(8,128)S(1)} %collective-permute-done.7.came_ref), custom_call_target="tpu_custom_call" | custom-call | tf_op jit(solution)/shard_map/hub_pieces/pallas_call | solution.py:194
  46.5 3.4 %all-to-all-start.1 = ((f32[8,16,256]{2,1,0:T(8,128)}), f32[8,16,256]{2,1,0:T(8,128)S(1)}, u32[]{:S(2)}, u32[]{:S(2)}) async-start(f32[8,16,256]{2,1,0:T(8,128)} %hub_pieces.1), calls=%async_computation.1 | async-start | bytes 262144 | tf_op jit(solution)/shard_map/all_to_all | solution.py:245
  49.9 0.7 %last_scores.1 = f32[128,256]{1,0:T(8,128)} custom-call(s32[1,256]{1,0:T(1,128)S(1)} %bitcast.11, f32[256,256]{1,0:T(8,128)S(1)} %get-tuple-element.16.keep_ref, f32[256,256]{1,0:T(8,128)S(1)} %collective-permute-done.7.came_ref), custom_call_target="tpu_custom_call" | custom-call | tf_op jit(solution)/shard_map/last_scores/pallas_call | solution.py:194
  50.6 6.8 %all-to-all-done.1.parts_ref = f32[8,16,256]{2,1,0:T(8,128)S(1)} async-done(((f32[8,16,256]{2,1,0:T(8,128)}), f32[8,16,256]{2,1,0:T(8,128)S(1)}, u32[]{:S(2)}, u32[]{:S(2)}) %all-to-all-start.1) | async-done | bytes 131104 | tf_op jit(solution)/shard_map/all_to_all | solution.py:245
  57.4 0.6 %last_hubs.1 = f32[16,256]{1,0:T(8,128)} custom-call(s32[1,256]{1,0:T(1,128)S(1)} %bitcast.12, f32[8,16,256]{2,1,0:T(8,128)S(1)} %all-to-all-done.1.parts_ref), custom_call_target="tpu_custom_call" | custom-call | tf_op jit(solution)/shard_map/last_hubs/pallas_call | solution.py:194
  (2 shorter events, 0.0 us)
Async XLA Ops:
  0.6 37.3 %copy-start.3 = (s32[256]{0:T(256)S(1)}, s32[256]{0:T(256)}, u32[]{:S(2)}) copy-start(s32[256]{0:T(256)} %param.9) | copy-start | bytes 3076
  1.3 1.9 %copy-start = (bf16[1,1,96,128,128]{4,3,2,1,0:T(8,128)(2,1)S(1)}, bf16[1,1,96,128,128]{4,3,2,1,0:T(8,128)(2,1)}, u32[]{:S(2)}) copy-start(bf16[1,1,96,128,128]{4,3,2,1,0:T(8,128)(2,1)} %param.5) | copy-start | bytes 9437188
  3.2 0.7 %copy-start.2 = (s32[256]{0:T(256)S(1)}, s32[256]{0:T(256)}, u32[]{:S(2)}) copy-start(s32[256]{0:T(256)} %param.9) | copy-start | bytes 3076
  3.9 0.7 %copy-start.4 = (s32[1,1,96]{2,1,0:T(1,128)S(1)}, s32[1,1,96]{2,1,0:T(1,128)}, u32[]{:S(2)}) copy-start(s32[1,1,96]{2,1,0:T(1,128)} %param.6) | copy-start | bytes 1156
  4.5 0.7 %copy-start.5 = (s32[1,1,96]{2,1,0:T(1,128)S(1)}, s32[1,1,96]{2,1,0:T(1,128)}, u32[]{:S(2)}) copy-start(s32[1,1,96]{2,1,0:T(1,128)} %param.7) | copy-start | bytes 1156
  7.8 1.7 %collective-permute-start = (f32[256,256]{1,0:T(8,128)S(1)}, f32[256,256]{1,0:T(8,128)S(1)}, u32[]{:S(2)}, u32[]{:S(2)}) collective-permute-start(f32[256,256]{1,0:T(8,128)S(1)} %get-tuple-element.11), channel_id=1, source_target_pairs={{0,1},{1,0},{2,3},{3,2},{4,5},{5,4},{6,7},{7,6},{8,9},{9,8},{10,11... | collective-permute-start | bytes 786440 | tf_op jit(solution)/shard_map/ppermute | solution.py:185
  9.6 0.8 %copy-start.1 = (bf16[8,128,256]{2,1,0:T(8,128)(2,1)}, bf16[8,128,256]{2,1,0:T(8,128)(2,1)S(1)}, u32[]{:S(2)}) copy-start(bf16[8,128,256]{2,1,0:T(8,128)(2,1)S(1)} %get-tuple-element.12) | copy-start | bytes 1572868
  10.4 33.0 %all-to-all-start = ((bf16[8,128,256]{2,1,0:T(8,128)(2,1)}), bf16[8,128,256]{2,1,0:T(8,128)(2,1)S(1)}, u32[]{:S(2)}, u32[]{:S(2)}) async-start(bf16[8,128,256]{2,1,0:T(8,128)(2,1)} %copy-done.1), calls=%async_computation | async-start | bytes 1048576 | tf_op jit(solution)/shard_map/all_to_all | solution.py:234
  17.5 7.9 %collective-permute-start.1 = (f32[64,256]{1,0:T(8,128)S(1)}, f32[64,256]{1,0:T(8,128)S(1)}, u32[]{:S(2)}, u32[]{:S(2)}) collective-permute-start(f32[64,256]{1,0:T(8,128)S(1)} %get-tuple-element.14), channel_id=1, source_target_pairs={{0,2},{2,0},{4,6},{6,4},{8,10},{10,8},{12,14},{14,12},{1,3},{3,1},... | collective-permute-start | bytes 196616 | tf_op jit(solution)/shard_map/ppermute | solution.py:188
  25.4 5.9 %collective-permute-start.4 = (f32[64,256]{1,0:T(8,128)S(1)}, f32[64,256]{1,0:T(8,128)S(1)}, u32[]{:S(2)}, u32[]{:S(2)}) collective-permute-start(f32[64,256]{1,0:T(8,128)S(1)} %plane_sum.1.refs_0_), channel_id=1, source_target_pairs={{0,12},{2,14},{4,0},{6,2},{8,4},{10,6},{12,8},{14,10},{1,13},{3,15... | collective-permute-start | bytes 196616 | tf_op jit(solution)/shard_map/ppermute | solution.py:188
  29.4 8.6 %collective-permute-start.3 = (f32[64,256]{1,0:T(8,128)S(1)}, f32[64,256]{1,0:T(8,128)S(1)}, u32[]{:S(2)}, u32[]{:S(2)}) collective-permute-start(f32[64,256]{1,0:T(8,128)S(1)} %plane_sum.1.refs_0_), channel_id=1, source_target_pairs={{0,8},{2,10},{4,12},{6,14},{8,0},{10,2},{12,4},{14,6},{1,9},{3,11}... | collective-permute-start | bytes 196616 | tf_op jit(solution)/shard_map/ppermute | solution.py:188
  29.4 8.6 %collective-permute-start.2 = (f32[64,256]{1,0:T(8,128)S(1)}, f32[64,256]{1,0:T(8,128)S(1)}, u32[]{:S(2)}, u32[]{:S(2)}) collective-permute-start(f32[64,256]{1,0:T(8,128)S(1)} %plane_sum.1.refs_0_), channel_id=1, source_target_pairs={{0,4},{2,6},{4,8},{6,10},{8,12},{10,14},{12,0},{14,2},{1,5},{3,7},... | collective-permute-start | bytes 196616 | tf_op jit(solution)/shard_map/ppermute | solution.py:188
  38.0 4.0 %collective-permute-start.5 = (bf16[64,256]{1,0:T(8,128)(2,1)S(1)}, bf16[64,256]{1,0:T(8,128)(2,1)S(1)}, u32[]{:S(2)}, u32[]{:S(2)}) collective-permute-start(bf16[64,256]{1,0:T(8,128)(2,1)S(1)} %hub_sums.1.mine_ref), channel_id=1, source_target_pairs={{0,2},{2,0},{4,6},{6,4},{8,10},{10,8},{12,14},{14,12},{1,3},{3,1},... | collective-permute-start | bytes 98312 | tf_op jit(solution)/shard_map/ppermute | solution.py:188
  42.0 1.3 %collective-permute-start.6 = (bf16[128,256]{1,0:T(8,128)(2,1)S(1)}, bf16[128,256]{1,0:T(8,128)(2,1)S(1)}, u32[]{:S(2)}, u32[]{:S(2)}) collective-permute-start(bf16[128,256]{1,0:T(8,128)(2,1)S(1)} %join_sides.1.mine_ref), channel_id=1, source_target_pairs={{0,1},{1,0},{2,3},{3,2},{4,5},{5,4},{6,7},{7,6},{8,9},{9,8},{10,11... | collective-permute-start | bytes 196616 | tf_op jit(solution)/shard_map/ppermute | solution.py:185
  44.2 1.6 %collective-permute-start.7 = (f32[256,256]{1,0:T(8,128)S(1)}, f32[256,256]{1,0:T(8,128)S(1)}, u32[]{:S(2)}, u32[]{:S(2)}) collective-permute-start(f32[256,256]{1,0:T(8,128)S(1)} %get-tuple-element.17), channel_id=1, source_target_pairs={{0,1},{1,0},{2,3},{3,2},{4,5},{5,4},{6,7},{7,6},{8,9},{9,8},{10,11... | collective-permute-start | bytes 786440 | tf_op jit(solution)/shard_map/ppermute | solution.py:185
  46.5 10.9 %all-to-all-start.1 = ((f32[8,16,256]{2,1,0:T(8,128)}), f32[8,16,256]{2,1,0:T(8,128)S(1)}, u32[]{:S(2)}, u32[]{:S(2)}) async-start(f32[8,16,256]{2,1,0:T(8,128)} %hub_pieces.1), calls=%async_computation.1 | async-start | bytes 262144 | tf_op jit(solution)/shard_map/all_to_all | solution.py:245

commit v5 on v4

--- a/solution.py
+++ b/solution.py
@@ -87,12 +87,22 @@
     write_terms(dims, H // n_col, prod, dense_ref, panel, send_ref, keep_ref)
 
 
-def second_kernel(dims, scores_ref, mine_ref, theirs_ref, dense_ref, send_ref, keep_ref, panel, prod):
+def second_kernel(dims, *refs):
     n_row, n_col, side = dims
+    n_z = n_row // X
+    own, far, (across, far_across, mine_ref, theirs_ref), rest = refs[0], refs[1:n_z], refs[n_z:n_z + 4], refs[n_z + 4:]
+    dense_ref, send_ref, keep_ref, panel, prod = rest
     half = H // n_col
-    c = lax.axis_index("col")
-    for r in range(n_row):
-        panel[pl.ds(r * VB, VB), :] = scores_ref[r]
+    r, c = lax.axis_index("row"), lax.axis_index("col")
+
+    def put(owner, block):
+        panel[pl.ds(pl.multiple_of(owner * VB, VB), VB), :] = block
+
+    put(r, own[...])
+    put(r ^ 1, across[...])
+    for k in range(1, n_z):
+        put(r ^ (X * k), far[k - 1][...])
+        put(r ^ (X * k) ^ 1, far_across[k - 1])
     for ref, col in ((mine_ref, c), (theirs_ref, 1 - c)):
         panel[pl.ds(pl.multiple_of(n_row * VB + col * half, half), half), :] = ref[...]
     write_terms(dims, half // n_row, prod, dense_ref, panel, send_ref, keep_ref)
@@ -105,62 +115,75 @@
 
 
 def spread_kernel(dims, src_ref, keep_ref, came_ref, scores_ref, hold_ref, pass_ref):
-    n_row, n_col, side = dims
     quarter = hold_ref.shape[0]
-    x = lax.rem(lax.axis_index("row"), X)
+    x = lax.axis_index("row") % X
     for ref, place in ((hold_ref, x), (pass_ref, 1 - x)):
         spot = pl.ds(pl.multiple_of(VB + place * quarter, quarter), quarter)
         ref[...] = keep_ref[spot, :] + came_ref[spot, :]
-    own = own_scores(dims, src_ref, keep_ref, came_ref).astype(scores_ref.dtype)
-    for k in range(n_row):
-        scores_ref[k] = own
+    scores_ref[...] = own_scores(dims, src_ref, keep_ref, came_ref).astype(scores_ref.dtype)
+
+
+def join_kernel(*refs):
+    for k, ref in enumerate(refs[:-1]):
+        refs[-1][k] = ref[...]
 
 
 def plane_kernel(hold_ref, came_ref, out_ref):
     out_ref[...] = hold_ref[...] + came_ref[...]
 
 
+def sum_planes(planes, held):
+    z = lax.axis_index("row") // X
+    for k, plane in enumerate(planes):
+        held[z ^ k] = plane[...]
+    summed = held[0]
+    for k in range(1, len(planes)):
+        summed = summed + held[k]
+    return summed
+
+
 def hub_kernel(dims, src_ref, *refs):
-    n_row, n_col, side = dims
     planes, (out_ref, held) = refs[:-2], refs[-2:]
     quarter = out_ref.shape[0]
-    r, c = lax.axis_index("row"), lax.axis_index("col")
-    z, x = lax.div(r, X), lax.rem(r, X)
-    n_z = len(planes)
-    for k in range(n_z):
-        held[lax.rem(z - k + n_z, n_z)] = planes[k][...]
-    summed = held[0]
-    for k in range(1, n_z):
-        summed = summed + held[k]
-    first = (c * X + x) * quarter
-    out_ref[...] = (DAMP * summed + 0.15 * one_hot(first, quarter, src_ref[...])).astype(out_ref.dtype)
+    first = (lax.axis_index("col") * X + lax.axis_index("row") % X) * quarter
+    tele = one_hot(first, quarter, src_ref[...])
+    out_ref[...] = (DAMP * sum_planes(planes, held) + 0.15 * tele).astype(out_ref.dtype)
 
 
 def side_kernel(mine_ref, theirs_ref, out_ref):
     quarter = mine_ref.shape[0]
-    x = lax.rem(lax.axis_index("row"), X)
+    x = lax.axis_index("row") % X
     for ref, place in ((mine_ref, x), (theirs_ref, 1 - x)):
         out_ref[pl.ds(pl.multiple_of(place * quarter, quarter), quarter), :] = ref[...]
 
 
-def pieces_kernel(dims, keep_ref, came_ref, parts_ref):
-    piece = parts_ref.shape[1]
-    for k in range(parts_ref.shape[0]):
-        spot = slice(VB + k * piece, VB + (k + 1) * piece)
-        parts_ref[k] = keep_ref[spot, :] + came_ref[spot, :]
+def halves_kernel(dims, keep_ref, came_ref, hold_ref, pass_ref):
+    n_row, n_col, side = dims
+    piece = H // (n_row * n_col)
+    x = lax.axis_index("row") % X
+    for ref, place in ((hold_ref, x), (pass_ref, 1 - x)):
+        for z in range(n_row // X):
+            spot = pl.ds(pl.multiple_of(VB + (z * X + place) * piece, piece), piece)
+            ref[z * piece:(z + 1) * piece] = keep_ref[spot, :] + came_ref[spot, :]
+
+
+def pieces_kernel(hold_ref, came_ref, *outs):
+    z = lax.axis_index("row") // X
+    piece = outs[0].shape[0]
+    for k, out in enumerate(outs):
+        spot = pl.ds(pl.multiple_of((z ^ k) * piece, piece), piece)
+        out[...] = hold_ref[spot, :] + came_ref[spot, :]
 
 
 def last_scores_kernel(dims, src_ref, keep_ref, came_ref, scores_ref):
     scores_ref[...] = own_scores(dims, src_ref, keep_ref, came_ref)
 
 
-def last_hubs_kernel(dims, src_ref, parts_ref, out_ref):
+def last_hubs_kernel(dims, src_ref, *refs):
+    planes, (out_ref, held) = refs[:-2], refs[-2:]
     piece = out_ref.shape[0]
-    summed = parts_ref[0]
-    for k in range(1, parts_ref.shape[0]):
-        summed = summed + parts_ref[k]
     first = (lax.axis_index("row") * dims[1] + lax.axis_index("col")) * piece
-    out_ref[...] = DAMP * summed + 0.15 * one_hot(first, piece, src_ref[...])
+    out_ref[...] = DAMP * sum_planes(planes, held) + 0.15 * one_hot(first, piece, src_ref[...])
 
 
 def fast_body(tiles, tile_row, tile_col, tile_count, sources):
@@ -184,11 +207,14 @@
     def other_core(x):
         return lax.ppermute(x, "col", [(0, 1), (1, 0)])
 
-    def along_row(x, target):
-        return lax.ppermute(x, "row", [(r, target(r)) for r in range(n_row)])
+    def to_partner(x, flip):
+        return lax.ppermute(x, "row", [(r, r ^ flip) for r in range(n_row)])
 
     def other_side(x):
-        return along_row(x, lambda r: r ^ 1)
+        return to_partner(x, 1)
+
+    def along_z(blocks):
+        return [to_partner(block, X * k) for k, block in enumerate(blocks) if k > 0]
 
     def call(kernel, name, out_shape, *args, scratch=()):
         return pl.pallas_call(
@@ -225,26 +251,33 @@
       tile_count.reshape(1), src)
 
     quarter = H // n_col // X
+    n_z = n_row // X
     for step in range(ITERS - 1):
         came = other_core(send)
-        scores, hold, away = call(
+        own, hold, away = call(
             bind(spread_kernel, dims), "spread",
-            (bf16((n_row, VB, width)), f32((quarter, width)), f32((quarter, width))),
+            (bf16((VB, width)), f32((quarter, width)), f32((quarter, width))),
             src, keep, came)
-        scores = lax.all_to_all(scores, "row", 0, 0)
-        plane = call(plane_kernel, "plane_sum", f32((quarter, width)), hold, other_side(away))
-        planes = [plane] + [along_row(plane, lambda r: (r + X * k) % n_row) for k in range(1, n_row // X)]
+        away = other_side(away)
+        far = along_z([own] * n_z)
+        across = other_side(own)
+        plane = call(plane_kernel, "plane_sum", f32((quarter, width)), hold, away)
+        planes = [plane] + along_z([plane] * n_z)
+        far_across = other_side(call(join_kernel, "join_far", bf16((n_z - 1, VB, width)), *far))
         mine = call(bind(hub_kernel, dims), "hub_sums", bf16((quarter, width)), src, *planes,
-                    scratch=[pltpu.VMEM((n_row // X, quarter, width), jnp.float32)])
+                    scratch=[pltpu.VMEM((n_z, quarter, width), jnp.float32)])
         mine = call(side_kernel, "join_sides", bf16((H // n_col, width)), mine, other_side(mine))
         send, keep = call(
             bind(second_kernel, dims), "later_terms", (f32((half, width)), f32((half, width))),
-            scores, mine, other_core(mine), dense, scratch=product_scratch)
+            own, *far, across, far_across, mine, other_core(mine), dense, scratch=product_scratch)
     came = other_core(send)
-    parts = call(bind(pieces_kernel, dims), "hub_pieces", f32((n_row, piece, width)), keep, came)
-    parts = lax.all_to_all(parts, "row", 0, 0)
+    hold, away = call(bind(halves_kernel, dims), "hub_halves",
+                      (f32((quarter, width)), f32((quarter, width))), keep, came)
+    pieces = call(pieces_kernel, "hub_pieces", (f32((piece, width)),) * n_z, hold, other_side(away))
+    pieces = [pieces[0]] + along_z(pieces)
     scores = call(bind(last_scores_kernel, dims), "last_scores", f32((VB, width)), src, keep, came)
-    hubs = call(bind(last_hubs_kernel, dims), "last_hubs", f32((piece, width)), src, parts)
+    hubs = call(bind(last_hubs_kernel, dims), "last_hubs", f32((piece, width)), src, *pieces,
+                scratch=[pltpu.VMEM((n_z, piece, width), jnp.float32)])
     return scores.reshape(1, 1, VB, width), hubs
 
 
@@ -331,7 +364,7 @@
         n_row, n_col = mesh.shape["row"], mesh.shape["col"]
         slots, side = tiles.shape[2:4]
         blocks = (n_col * VB + H) * (n_row * VB + H) // (side * side)
-        if n_col == 2 and blocks <= slots and H // (n_row * n_col) % 16 == 0:
+        if n_col == 2 and n_row in (4, 8, 16) and blocks <= slots and H // (n_row * n_col) % 16 == 0:
             return fast_body(tiles, *rest)
         return plain_body(tiles, *rest)
 

time: 58.4 us -> 52.1 us (0.89)
  waiting for transfers between devices: 26.8 us -> 19.8 us
  starting transfers between devices: 19.5 us -> 21.8 us
  local copies, waits for them, and re-layouts: 4.66 us -> 3.87 us
    ppermute x5 -> x14, starting transfers between devices: 8.16 us -> 21 us  [to_partner(): return lax.ppermute(x, 'row', [(r, r ^ flip) for r in range(n_row)])]
    all_to_all x2 -> x0, starting transfers between devices: 10.5 us -> none  [the longest x1 7.17 us: fast_body(): scores = lax.all_to_all(scores, 'row', 0, 0)]
    all_to_all x2 -> x0, waiting for transfers between devices: 6.85 us -> none  [the longest x1 6.85 us: fast_body(): parts = lax.all_to_all(parts, 'row', 0, 0)]
    ppermute x3, waiting for transfers between devices: 3.76 us -> 2.97 us  [other_core(): return lax.ppermute(x, 'col', [(0, 1), (1, 0)])]
    unnamed x12 -> x10, local copies, waits for them, and re-layouts: 4.66 us -> 3.87 us
    ppermute x5 -> x14, waiting for transfers between devices: 16.2 us -> 16.8 us  [to_partner(): return lax.ppermute(x, 'row', [(r, r ^ flip) for r in range(n_row)])]
    pallas_call x8 -> x10, Pallas kernels: 3.05 us -> 2.47 us  [call(): pl.pallas_call(kernel, out_shape=out_shape, in_specs=[VMEM] * len(args),...]
  transfers between devices with their start and end apart: 10 -> 17, of which waited for: 8 -> 11; matrix products, arithmetic and copies ran while one was open for 0% -> 0% of each run, Pallas kernels for 1% -> 1%
where the time goes in v5:
time: 52.1 us; the launch traced here: 51.9 us
  starting transfers between devices  21.8 us (42%)
  waiting for transfers between devices  19.8 us (38%)
  Pallas kernels  5.09 us (10%)
  local copies, waits for them, and re-layouts  3.87 us (7%)
  between operations  1.38 us (3%)
    ppermute x14, starting transfers between devices, to_partner(): return lax.ppermute(x, 'row', [(r, r ^ flip) for r in range(n_row)])  21 us
    ppermute x14, waiting for transfers between devices, to_partner(): return lax.ppermute(x, 'row', [(r, r ^ flip) for r in range(n_row)])  16.8 us
    unnamed x10, local copies, waits for them, and re-layouts  3.87 us
    ppermute x3, waiting for transfers between devices, other_core(): return lax.ppermute(x, 'col', [(0, 1), (1, 0)])  2.97 us
    pallas_call x1, Pallas kernels, fast_body(): pl.pallas_call(functools.partial(first_kernel, dims), out_shape=(f32((hal...  2.61 us
    pallas_call x10, Pallas kernels, call(): pl.pallas_call(kernel, out_shape=out_shape, in_specs=[VMEM] * len(args),...  2.47 us
  transfers between devices with their start and end apart: 17, of which 11 were waited for; matrix products, arithmetic and copies ran while one was open for 0% of the time, Pallas kernels for 1%

profile of v5, /device:TPU:0, one launch (start us, length us, event | category | flops | bytes accessed | tf_op | source)
XLA Modules:
  0.0 51.9 jit_solution(1087409998283986149)
XLA Ops:
  0.6 0.0 copy-start.2
  1.3 0.0 copy-start
  1.3 1.9 %copy-done = bf16[1,1,96,128,128]{4,3,2,1,0:T(8,128)(2,1)S(1)} copy-done((bf16[1,1,96,128,128]{4,3,2,1,0:T(8,128)(2,1)S(1)}, bf16[1,1,96,128,128]{4,3,2,1,0:T(8,128)(2,1)}, u32[]{:S(2)}) %copy-start) | copy-done | bytes 3145752
  3.2 0.0 copy-start.1
  3.2 0.7 %copy-done.1 = s32[256]{0:T(256)S(1)} copy-done((s32[256]{0:T(256)S(1)}, s32[256]{0:T(256)}, u32[]{:S(2)}) %copy-start.1) | copy-done | bytes 1048
  3.9 0.7 %copy-done.3 = s32[1,1,96]{2,1,0:T(1,128)S(1)} copy-done((s32[1,1,96]{2,1,0:T(1,128)S(1)}, s32[1,1,96]{2,1,0:T(1,128)}, u32[]{:S(2)}) %copy-start.3) | copy-done | bytes 408
  4.5 0.7 %copy-done.4 = s32[1,1,96]{2,1,0:T(1,128)S(1)} copy-done((s32[1,1,96]{2,1,0:T(1,128)S(1)}, s32[1,1,96]{2,1,0:T(1,128)}, u32[]{:S(2)}) %copy-start.4) | copy-done | bytes 408
  5.2 2.6 %first_terms.1 = (f32[256,256]{1,0:T(8,128)S(1)}, f32[256,256]{1,0:T(8,128)S(1)}, bf16[1024,1280]{1,0:T(8,128)(2,1)S(1)}) custom-call(bf16[96,128,128]{2,1,0:T(8,128)(2,1)S(1)} %bitcast.7, s32[96]{0:T(128)S(1)} %bitcast.13, s32[96]{0:T(128)S(1)} %bitcast.14, s32[1]{0:T(128)} %bitcast.6.count_hbm, s32[1,256]{1,0:T(1,128)S(1)} %bitcast.8), custom_call_target="tpu_custom_call" | custom-call | tf_op jit(solution)/shard_map/first_terms/pallas_call | solution.py:232
  7.8 0.5 %collective-permute-start = (f32[256,256]{1,0:T(8,128)S(1)}, f32[256,256]{1,0:T(8,128)S(1)}, u32[]{:S(2)}, u32[]{:S(2)}) collective-permute-start(f32[256,256]{1,0:T(8,128)S(1)} %get-tuple-element.17), channel_id=1, source_target_pairs={{0,1},{1,0},{2,3},{3,2},{4,5},{5,4},{6,7},{7,6},{8,9},{9,8},{10,11... | collective-permute-start | bytes 786440 | tf_op jit(solution)/shard_map/ppermute | solution.py:208
  8.3 1.2 %collective-permute-done.came_ref = f32[256,256]{1,0:T(8,128)S(1)} collective-permute-done((f32[256,256]{1,0:T(8,128)S(1)}, f32[256,256]{1,0:T(8,128)S(1)}, u32[]{:S(2)}, u32[]{:S(2)}) %collective-permute-start) | collective-permute-done | bytes 262176 | tf_op jit(solution)/shard_map/ppermute | solution.py:208
  9.5 0.1 spread.1
  9.6 5.0 %collective-permute-start.3 = (bf16[128,256]{1,0:T(8,128)(2,1)S(1)}, bf16[128,256]{1,0:T(8,128)(2,1)S(1)}, u32[]{:S(2)}, u32[]{:S(2)}) collective-permute-start(bf16[128,256]{1,0:T(8,128)(2,1)S(1)} %get-tuple-element.18.refs_0_), channel_id=1, source_target_pairs={{0,12},{2,14},{4,8},{6,10},{8,4},{10,6},{12,0},{14,2},{1,13},{3,15... | collective-permute-start | bytes 196616 | tf_op jit(solution)/shard_map/ppermute | solution.py:211
  14.6 0.0 collective-permute-start.2
  14.6 0.6 %collective-permute-start.1 = (bf16[128,256]{1,0:T(8,128)(2,1)S(1)}, bf16[128,256]{1,0:T(8,128)(2,1)S(1)}, u32[]{:S(2)}, u32[]{:S(2)}) collective-permute-start(bf16[128,256]{1,0:T(8,128)(2,1)S(1)} %get-tuple-element.18.refs_0_), channel_id=1, source_target_pairs={{0,4},{2,6},{4,0},{6,2},{8,12},{10,14},{12,8},{14,10},{1,5},{3,7},... | collective-permute-start | bytes 196616 | tf_op jit(solution)/shard_map/ppermute | solution.py:211
  15.2 1.6 %collective-permute-start.6 = (f32[64,256]{1,0:T(8,128)S(1)}, f32[64,256]{1,0:T(8,128)S(1)}, u32[]{:S(2)}, u32[]{:S(2)}) collective-permute-start(f32[64,256]{1,0:T(8,128)S(1)} %get-tuple-element.20), channel_id=1, source_target_pairs={{0,2},{2,0},{4,6},{6,4},{8,10},{10,8},{12,14},{14,12},{1,3},{3,1},... | collective-permute-start | bytes 196616 | tf_op jit(solution)/shard_map/ppermute | solution.py:211
  16.9 0.4 collective-permute-done.3.refs_2_.refs_3_
  17.2 3.3 %collective-permute-done.2.refs_1_.refs_2_ = bf16[128,256]{1,0:T(8,128)(2,1)S(1)} collective-permute-done((bf16[128,256]{1,0:T(8,128)(2,1)S(1)}, bf16[128,256]{1,0:T(8,128)(2,1)S(1)}, u32[]{:S(2)}, u32[]{:S(2)}) %collective-permute-start.2) | collective-permute-done | bytes 65568 | tf_op jit(solution)/shard_map/ppermute | solution.py:211
  20.5 0.0 collective-permute-done.1.refs_0_.refs_1_
  20.5 1.6 %collective-permute-start.5 = (bf16[3,128,256]{2,1,0:T(8,128)(2,1)S(1)}, bf16[3,128,256]{2,1,0:T(8,128)(2,1)S(1)}, u32[]{:S(2)}, u32[]{:S(2)}) collective-permute-start(bf16[3,128,256]{2,1,0:T(8,128)(2,1)S(1)} %join_far.1), channel_id=1, source_target_pairs={{0,2},{2,0},{4,6},{6,4},{8,10},{10,8},{12,14},{14,12},{1,3},{3,1},... | collective-permute-start | bytes 589832 | tf_op jit(solution)/shard_map/ppermute | solution.py:211
  22.1 0.0 collective-permute-done.6.came_ref
  22.1 2.5 %collective-permute-start.9 = (f32[64,256]{1,0:T(8,128)S(1)}, f32[64,256]{1,0:T(8,128)S(1)}, u32[]{:S(2)}, u32[]{:S(2)}) collective-permute-start(f32[64,256]{1,0:T(8,128)S(1)} %plane_sum.1.refs_0_), channel_id=1, source_target_pairs={{0,12},{2,14},{4,8},{6,10},{8,4},{10,6},{12,0},{14,2},{1,13},{3,15... | collective-permute-start | bytes 196616 | tf_op jit(solution)/shard_map/ppermute | solution.py:211
  24.6 0.1 collective-permute-start.8
  24.7 1.8 %collective-permute-start.7 = (f32[64,256]{1,0:T(8,128)S(1)}, f32[64,256]{1,0:T(8,128)S(1)}, u32[]{:S(2)}, u32[]{:S(2)}) collective-permute-start(f32[64,256]{1,0:T(8,128)S(1)} %plane_sum.1.refs_0_), channel_id=1, source_target_pairs={{0,4},{2,6},{4,0},{6,2},{8,12},{10,14},{12,8},{14,10},{1,5},{3,7},... | collective-permute-start | bytes 196616 | tf_op jit(solution)/shard_map/ppermute | solution.py:211
  26.5 1.9 %collective-permute-done.9.refs_3_ = f32[64,256]{1,0:T(8,128)S(1)} collective-permute-done((f32[64,256]{1,0:T(8,128)S(1)}, f32[64,256]{1,0:T(8,128)S(1)}, u32[]{:S(2)}, u32[]{:S(2)}) %collective-permute-start.9) | collective-permute-done | bytes 65568 | tf_op jit(solution)/shard_map/ppermute | solution.py:211
  28.4 2.5 %collective-permute-done.8.refs_2_ = f32[64,256]{1,0:T(8,128)S(1)} collective-permute-done((f32[64,256]{1,0:T(8,128)S(1)}, f32[64,256]{1,0:T(8,128)S(1)}, u32[]{:S(2)}, u32[]{:S(2)}) %collective-permute-start.8) | collective-permute-done | bytes 65568 | tf_op jit(solution)/shard_map/ppermute | solution.py:211
  30.8 0.0 collective-permute-done.7.refs_1_
  30.8 0.0 copy-done.2
  30.8 0.1 hub_sums.1.mine_ref
  30.9 0.6 %collective-permute-start.10 = (bf16[64,256]{1,0:T(8,128)(2,1)S(1)}, bf16[64,256]{1,0:T(8,128)(2,1)S(1)}, u32[]{:S(2)}, u32[]{:S(2)}) collective-permute-start(bf16[64,256]{1,0:T(8,128)(2,1)S(1)} %hub_sums.1.mine_ref), channel_id=1, source_target_pairs={{0,2},{2,0},{4,6},{6,4},{8,10},{10,8},{12,14},{14,12},{1,3},{3,1},... | collective-permute-start | bytes 98312 | tf_op jit(solution)/shard_map/ppermute | solution.py:211
  31.5 1.5 %collective-permute-start.4 = (bf16[128,256]{1,0:T(8,128)(2,1)S(1)}, bf16[128,256]{1,0:T(8,128)(2,1)S(1)}, u32[]{:S(2)}, u32[]{:S(2)}) collective-permute-start(bf16[128,256]{1,0:T(8,128)(2,1)S(1)} %get-tuple-element.18.refs_0_), channel_id=1, source_target_pairs={{0,2},{2,0},{4,6},{6,4},{8,10},{10,8},{12,14},{14,12},{1,3},{3,1},... | collective-permute-start | bytes 196616 | tf_op jit(solution)/shard_map/ppermute | solution.py:211
  33.0 1.9 %collective-permute-done.10.theirs_ref = bf16[64,256]{1,0:T(8,128)(2,1)S(1)} collective-permute-done((bf16[64,256]{1,0:T(8,128)(2,1)S(1)}, bf16[64,256]{1,0:T(8,128)(2,1)S(1)}, u32[]{:S(2)}, u32[]{:S(2)}) %collective-permute-start.10) | collective-permute-done | bytes 32800 | tf_op jit(solution)/shard_map/ppermute | solution.py:211
  34.9 0.1 collective-permute-start.11
  35.0 0.8 %collective-permute-done.4.refs_4_ = bf16[128,256]{1,0:T(8,128)(2,1)S(1)} collective-permute-done((bf16[128,256]{1,0:T(8,128)(2,1)S(1)}, bf16[128,256]{1,0:T(8,128)(2,1)S(1)}, u32[]{:S(2)}, u32[]{:S(2)}) %collective-permute-start.4) | collective-permute-done | bytes 65568 | tf_op jit(solution)/shard_map/ppermute | solution.py:211
  35.8 0.4 collective-permute-done.11.refs_7_
  36.2 0.0 collective-permute-done.5.refs_5_
  36.2 1.0 %later_terms.1 = (f32[256,256]{1,0:T(8,128)S(1)}, f32[256,256]{1,0:T(8,128)S(1)}) custom-call(bf16[128,256]{1,0:T(8,128)(2,1)S(1)} %get-tuple-element.18.refs_0_, bf16[128,256]{1,0:T(8,128)(2,1)S(1)} %collective-permute-done.1.refs_0_.refs_1_, bf16[128,256]{1,0:T(8,128)(2,1)S(1)} %collective-permute-done.2.refs_1_.refs_2_, ...), custom_call_target="tpu_custom_call" | custom-call | tf_op jit(solution)/shard_map/later_terms/pallas_call | solution.py:220
  37.2 0.2 collective-permute-start.12
  37.4 1.4 %collective-permute-done.12.came_ref = f32[256,256]{1,0:T(8,128)S(1)} collective-permute-done((f32[256,256]{1,0:T(8,128)S(1)}, f32[256,256]{1,0:T(8,128)S(1)}, u32[]{:S(2)}, u32[]{:S(2)}) %collective-permute-start.12) | collective-permute-done | bytes 262176 | tf_op jit(solution)/shard_map/ppermute | solution.py:208
  38.8 1.1 %collective-permute-start.13 = (f32[64,256]{1,0:T(8,128)S(1)}, f32[64,256]{1,0:T(8,128)S(1)}, u32[]{:S(2)}, u32[]{:S(2)}) collective-permute-start(f32[64,256]{1,0:T(8,128)S(1)} %get-tuple-element.25), channel_id=1, source_target_pairs={{0,2},{2,0},{4,6},{6,4},{8,10},{10,8},{12,14},{14,12},{1,3},{3,1},... | collective-permute-start | bytes 196616 | tf_op jit(solution)/shard_map/ppermute | solution.py:211
  39.9 3.2 %collective-permute-done.13.came_ref = f32[64,256]{1,0:T(8,128)S(1)} collective-permute-done((f32[64,256]{1,0:T(8,128)S(1)}, f32[64,256]{1,0:T(8,128)S(1)}, u32[]{:S(2)}, u32[]{:S(2)}) %collective-permute-start.13) | collective-permute-done | bytes 65568 | tf_op jit(solution)/shard_map/ppermute | solution.py:211
  43.2 0.1 collective-permute-start.14
  43.2 2.5 %collective-permute-start.15 = (f32[16,256]{1,0:T(8,128)S(1)}, f32[16,256]{1,0:T(8,128)S(1)}, u32[]{:S(2)}, u32[]{:S(2)}) collective-permute-start(f32[16,256]{1,0:T(8,128)S(1)} %get-tuple-element.28), channel_id=1, source_target_pairs={{0,8},{2,10},{4,12},{6,14},{8,0},{10,2},{12,4},{14,6},{1,9},{3,11}... | collective-permute-start | bytes 49160 | tf_op jit(solution)/shard_map/ppermute | solution.py:211
  45.8 1.9 %collective-permute-start.16 = (f32[16,256]{1,0:T(8,128)S(1)}, f32[16,256]{1,0:T(8,128)S(1)}, u32[]{:S(2)}, u32[]{:S(2)}) collective-permute-start(f32[16,256]{1,0:T(8,128)S(1)} %get-tuple-element.29), channel_id=1, source_target_pairs={{0,12},{2,14},{4,8},{6,10},{8,4},{10,6},{12,0},{14,2},{1,13},{3,15... | collective-permute-start | bytes 49160 | tf_op jit(solution)/shard_map/ppermute | solution.py:211
  47.6 0.7 %last_scores.1 = f32[128,256]{1,0:T(8,128)} custom-call(s32[1,256]{1,0:T(1,128)S(1)} %bitcast.11, f32[256,256]{1,0:T(8,128)S(1)} %get-tuple-element.22.keep_ref, f32[256,256]{1,0:T(8,128)S(1)} %collective-permute-done.12.came_ref), custom_call_target="tpu_custom_call" | custom-call | tf_op jit(solution)/shard_map/last_scores/pallas_call | solution.py:220
  48.3 0.0 collective-permute-done.14.refs_1_
  48.3 0.0 collective-permute-done.15.refs_2_
  48.3 3.0 %collective-permute-done.16.refs_3_ = f32[16,256]{1,0:T(8,128)S(1)} collective-permute-done((f32[16,256]{1,0:T(8,128)S(1)}, f32[16,256]{1,0:T(8,128)S(1)}, u32[]{:S(2)}, u32[]{:S(2)}) %collective-permute-start.16) | collective-permute-done | bytes 16416 | tf_op jit(solution)/shard_map/ppermute | solution.py:211
  51.3 0.6 %last_hubs.1 = f32[16,256]{1,0:T(8,128)} custom-call(s32[1,256]{1,0:T(1,128)S(1)} %bitcast.12, f32[16,256]{1,0:T(8,128)S(1)} %get-tuple-element.26.refs_0_, f32[16,256]{1,0:T(8,128)S(1)} %collective-permute-done.14.refs_1_, f32[16,256]{1,0:T(8,128)S(1)} %collective-permute-done.15.refs_2_, f32[16,256]{1,0:T(8,128)S(1)} %collective-permute-done.16.refs_3_), custom_call_target="tpu_custom_call" | custom-call | tf_op jit(solution)/shard_map/last_hubs/pallas_call | solution.py:220
  (7 shorter events, 0.1 us)
Async XLA Ops:
  0.6 30.2 %copy-start.2 = (s32[256]{0:T(256)S(1)}, s32[256]{0:T(256)}, u32[]{:S(2)}) copy-start(s32[256]{0:T(256)} %param.9) | copy-start | bytes 3076
  1.3 1.9 %copy-start = (bf16[1,1,96,128,128]{4,3,2,1,0:T(8,128)(2,1)S(1)}, bf16[1,1,96,128,128]{4,3,2,1,0:T(8,128)(2,1)}, u32[]{:S(2)}) copy-start(bf16[1,1,96,128,128]{4,3,2,1,0:T(8,128)(2,1)} %param.5) | copy-start | bytes 9437188
  3.2 0.7 %copy-start.1 = (s32[256]{0:T(256)S(1)}, s32[256]{0:T(256)}, u32[]{:S(2)}) copy-start(s32[256]{0:T(256)} %param.9) | copy-start | bytes 3076
  3.9 0.7 %copy-start.3 = (s32[1,1,96]{2,1,0:T(1,128)S(1)}, s32[1,1,96]{2,1,0:T(1,128)}, u32[]{:S(2)}) copy-start(s32[1,1,96]{2,1,0:T(1,128)} %param.6) | copy-start | bytes 1156
  4.5 0.7 %copy-start.4 = (s32[1,1,96]{2,1,0:T(1,128)S(1)}, s32[1,1,96]{2,1,0:T(1,128)}, u32[]{:S(2)}) copy-start(s32[1,1,96]{2,1,0:T(1,128)} %param.7) | copy-start | bytes 1156
  7.8 1.7 %collective-permute-start = (f32[256,256]{1,0:T(8,128)S(1)}, f32[256,256]{1,0:T(8,128)S(1)}, u32[]{:S(2)}, u32[]{:S(2)}) collective-permute-start(f32[256,256]{1,0:T(8,128)S(1)} %get-tuple-element.17), channel_id=1, source_target_pairs={{0,1},{1,0},{2,3},{3,2},{4,5},{5,4},{6,7},{7,6},{8,9},{9,8},{10,11... | collective-permute-start | bytes 786440 | tf_op jit(solution)/shard_map/ppermute | solution.py:208
  9.6 7.7 %collective-permute-start.3 = (bf16[128,256]{1,0:T(8,128)(2,1)S(1)}, bf16[128,256]{1,0:T(8,128)(2,1)S(1)}, u32[]{:S(2)}, u32[]{:S(2)}) collective-permute-start(bf16[128,256]{1,0:T(8,128)(2,1)S(1)} %get-tuple-element.18.refs_0_), channel_id=1, source_target_pairs={{0,12},{2,14},{4,8},{6,10},{8,4},{10,6},{12,0},{14,2},{1,13},{3,15... | collective-permute-start | bytes 196616 | tf_op jit(solution)/shard_map/ppermute | solution.py:211
  14.6 5.9 %collective-permute-start.2 = (bf16[128,256]{1,0:T(8,128)(2,1)S(1)}, bf16[128,256]{1,0:T(8,128)(2,1)S(1)}, u32[]{:S(2)}, u32[]{:S(2)}) collective-permute-start(bf16[128,256]{1,0:T(8,128)(2,1)S(1)} %get-tuple-element.18.refs_0_), channel_id=1, source_target_pairs={{0,8},{2,10},{4,12},{6,14},{8,0},{10,2},{12,4},{14,6},{1,9},{3,11}... | collective-permute-start | bytes 196616 | tf_op jit(solution)/shard_map/ppermute | solution.py:211
  14.6 5.9 %collective-permute-start.1 = (bf16[128,256]{1,0:T(8,128)(2,1)S(1)}, bf16[128,256]{1,0:T(8,128)(2,1)S(1)}, u32[]{:S(2)}, u32[]{:S(2)}) collective-permute-start(bf16[128,256]{1,0:T(8,128)(2,1)S(1)} %get-tuple-element.18.refs_0_), channel_id=1, source_target_pairs={{0,4},{2,6},{4,0},{6,2},{8,12},{10,14},{12,8},{14,10},{1,5},{3,7},... | collective-permute-start | bytes 196616 | tf_op jit(solution)/shard_map/ppermute | solution.py:211
  15.2 6.8 %collective-permute-start.6 = (f32[64,256]{1,0:T(8,128)S(1)}, f32[64,256]{1,0:T(8,128)S(1)}, u32[]{:S(2)}, u32[]{:S(2)}) collective-permute-start(f32[64,256]{1,0:T(8,128)S(1)} %get-tuple-element.20), channel_id=1, source_target_pairs={{0,2},{2,0},{4,6},{6,4},{8,10},{10,8},{12,14},{14,12},{1,3},{3,1},... | collective-permute-start | bytes 196616 | tf_op jit(solution)/shard_map/ppermute | solution.py:211
  20.5 15.7 %collective-permute-start.5 = (bf16[3,128,256]{2,1,0:T(8,128)(2,1)S(1)}, bf16[3,128,256]{2,1,0:T(8,128)(2,1)S(1)}, u32[]{:S(2)}, u32[]{:S(2)}) collective-permute-start(bf16[3,128,256]{2,1,0:T(8,128)(2,1)S(1)} %join_far.1), channel_id=1, source_target_pairs={{0,2},{2,0},{4,6},{6,4},{8,10},{10,8},{12,14},{14,12},{1,3},{3,1},... | collective-permute-start | bytes 589832 | tf_op jit(solution)/shard_map/ppermute | solution.py:211
  22.1 6.3 %collective-permute-start.9 = (f32[64,256]{1,0:T(8,128)S(1)}, f32[64,256]{1,0:T(8,128)S(1)}, u32[]{:S(2)}, u32[]{:S(2)}) collective-permute-start(f32[64,256]{1,0:T(8,128)S(1)} %plane_sum.1.refs_0_), channel_id=1, source_target_pairs={{0,12},{2,14},{4,8},{6,10},{8,4},{10,6},{12,0},{14,2},{1,13},{3,15... | collective-permute-start | bytes 196616 | tf_op jit(solution)/shard_map/ppermute | solution.py:211
  24.6 6.2 %collective-permute-start.8 = (f32[64,256]{1,0:T(8,128)S(1)}, f32[64,256]{1,0:T(8,128)S(1)}, u32[]{:S(2)}, u32[]{:S(2)}) collective-permute-start(f32[64,256]{1,0:T(8,128)S(1)} %plane_sum.1.refs_0_), channel_id=1, source_target_pairs={{0,8},{2,10},{4,12},{6,14},{8,0},{10,2},{12,4},{14,6},{1,9},{3,11}... | collective-permute-start | bytes 196616 | tf_op jit(solution)/shard_map/ppermute | solution.py:211
  24.7 6.1 %collective-permute-start.7 = (f32[64,256]{1,0:T(8,128)S(1)}, f32[64,256]{1,0:T(8,128)S(1)}, u32[]{:S(2)}, u32[]{:S(2)}) collective-permute-start(f32[64,256]{1,0:T(8,128)S(1)} %plane_sum.1.refs_0_), channel_id=1, source_target_pairs={{0,4},{2,6},{4,0},{6,2},{8,12},{10,14},{12,8},{14,10},{1,5},{3,7},... | collective-permute-start | bytes 196616 | tf_op jit(solution)/shard_map/ppermute | solution.py:211
  30.9 4.0 %collective-permute-start.10 = (bf16[64,256]{1,0:T(8,128)(2,1)S(1)}, bf16[64,256]{1,0:T(8,128)(2,1)S(1)}, u32[]{:S(2)}, u32[]{:S(2)}) collective-permute-start(bf16[64,256]{1,0:T(8,128)(2,1)S(1)} %hub_sums.1.mine_ref), channel_id=1, source_target_pairs={{0,2},{2,0},{4,6},{6,4},{8,10},{10,8},{12,14},{14,12},{1,3},{3,1},... | collective-permute-start | bytes 98312 | tf_op jit(solution)/shard_map/ppermute | solution.py:211
  31.5 4.3 %collective-permute-start.4 = (bf16[128,256]{1,0:T(8,128)(2,1)S(1)}, bf16[128,256]{1,0:T(8,128)(2,1)S(1)}, u32[]{:S(2)}, u32[]{:S(2)}) collective-permute-start(bf16[128,256]{1,0:T(8,128)(2,1)S(1)} %get-tuple-element.18.refs_0_), channel_id=1, source_target_pairs={{0,2},{2,0},{4,6},{6,4},{8,10},{10,8},{12,14},{14,12},{1,3},{3,1},... | collective-permute-start | bytes 196616 | tf_op jit(solution)/shard_map/ppermute | solution.py:211
  34.9 1.3 %collective-permute-start.11 = (bf16[128,256]{1,0:T(8,128)(2,1)S(1)}, bf16[128,256]{1,0:T(8,128)(2,1)S(1)}, u32[]{:S(2)}, u32[]{:S(2)}) collective-permute-start(bf16[128,256]{1,0:T(8,128)(2,1)S(1)} %join_sides.1.refs_6_), channel_id=1, source_target_pairs={{0,1},{1,0},{2,3},{3,2},{4,5},{5,4},{6,7},{7,6},{8,9},{9,8},{10,11... | collective-permute-start | bytes 196616 | tf_op jit(solution)/shard_map/ppermute | solution.py:208
  37.2 1.6 %collective-permute-start.12 = (f32[256,256]{1,0:T(8,128)S(1)}, f32[256,256]{1,0:T(8,128)S(1)}, u32[]{:S(2)}, u32[]{:S(2)}) collective-permute-start(f32[256,256]{1,0:T(8,128)S(1)} %get-tuple-element.23), channel_id=1, source_target_pairs={{0,1},{1,0},{2,3},{3,2},{4,5},{5,4},{6,7},{7,6},{8,9},{9,8},{10,11... | collective-permute-start | bytes 786440 | tf_op jit(solution)/shard_map/ppermute | solution.py:208
  38.8 4.3 %collective-permute-start.13 = (f32[64,256]{1,0:T(8,128)S(1)}, f32[64,256]{1,0:T(8,128)S(1)}, u32[]{:S(2)}, u32[]{:S(2)}) collective-permute-start(f32[64,256]{1,0:T(8,128)S(1)} %get-tuple-element.25), channel_id=1, source_target_pairs={{0,2},{2,0},{4,6},{6,4},{8,10},{10,8},{12,14},{14,12},{1,3},{3,1},... | collective-permute-start | bytes 196616 | tf_op jit(solution)/shard_map/ppermute | solution.py:211
  43.2 5.2 %collective-permute-start.14 = (f32[16,256]{1,0:T(8,128)S(1)}, f32[16,256]{1,0:T(8,128)S(1)}, u32[]{:S(2)}, u32[]{:S(2)}) collective-permute-start(f32[16,256]{1,0:T(8,128)S(1)} %get-tuple-element.27), channel_id=1, source_target_pairs={{0,4},{2,6},{4,0},{6,2},{8,12},{10,14},{12,8},{14,10},{1,5},{3,7},... | collective-permute-start | bytes 49160 | tf_op jit(solution)/shard_map/ppermute | solution.py:211
  43.2 5.1 %collective-permute-start.15 = (f32[16,256]{1,0:T(8,128)S(1)}, f32[16,256]{1,0:T(8,128)S(1)}, u32[]{:S(2)}, u32[]{:S(2)}) collective-permute-start(f32[16,256]{1,0:T(8,128)S(1)} %get-tuple-element.28), channel_id=1, source_target_pairs={{0,8},{2,10},{4,12},{6,14},{8,0},{10,2},{12,4},{14,6},{1,9},{3,11}... | collective-permute-start | bytes 49160 | tf_op jit(solution)/shard_map/ppermute | solution.py:211
  45.8 5.5 %collective-permute-start.16 = (f32[16,256]{1,0:T(8,128)S(1)}, f32[16,256]{1,0:T(8,128)S(1)}, u32[]{:S(2)}, u32[]{:S(2)}) collective-permute-start(f32[16,256]{1,0:T(8,128)S(1)} %get-tuple-element.29), channel_id=1, source_target_pairs={{0,12},{2,14},{4,8},{6,10},{8,4},{10,6},{12,0},{14,2},{1,13},{3,15... | collective-permute-start | bytes 49160 | tf_op jit(solution)/shard_map/ppermute | solution.py:211

commit v6 on v5

--- a/solution.py
+++ b/solution.py
@@ -13,6 +13,7 @@
 DAMP = 0.85
 CHUNK = 16
 X = 2
+MICRO = 10 ** 9
 VMEM_LIMIT = 32 * 1024 * 1024
 
 SMEM = pl.BlockSpec(memory_space=pltpu.SMEM)
@@ -216,7 +217,7 @@
     def along_z(blocks):
         return [to_partner(block, X * k) for k, block in enumerate(blocks) if k > 0]
 
-    def call(kernel, name, out_shape, *args, scratch=()):
+    def call(kernel, name, out_shape, *args, scratch=(), cost=0):
         return pl.pallas_call(
             kernel,
             out_shape=out_shape,
@@ -224,6 +225,7 @@
             out_specs=jax.tree.map(lambda _: VMEM, out_shape),
             scratch_shapes=scratch,
             compiler_params=params(),
+            cost_estimate=pl.CostEstimate(flops=cost * MICRO, bytes_accessed=0, transcendentals=0),
             name=name,
         )(*args)
 
@@ -261,11 +263,11 @@
         away = other_side(away)
         far = along_z([own] * n_z)
         across = other_side(own)
-        plane = call(plane_kernel, "plane_sum", f32((quarter, width)), hold, away)
+        plane = call(plane_kernel, "plane_sum", f32((quarter, width)), hold, away, cost=100000)
         planes = [plane] + along_z([plane] * n_z)
         far_across = other_side(call(join_kernel, "join_far", bf16((n_z - 1, VB, width)), *far))
         mine = call(bind(hub_kernel, dims), "hub_sums", bf16((quarter, width)), src, *planes,
-                    scratch=[pltpu.VMEM((n_z, quarter, width), jnp.float32)])
+                    scratch=[pltpu.VMEM((n_z, quarter, width), jnp.float32)], cost=100000)
         mine = call(side_kernel, "join_sides", bf16((H // n_col, width)), mine, other_side(mine))
         send, keep = call(
             bind(second_kernel, dims), "later_terms", (f32((half, width)), f32((half, width))),

time: 52.1 us -> 52.5 us (level)
  Pallas kernels: 5.09 us -> 8.34 us
  waiting for transfers between devices: 19.8 us -> 17.9 us
  starting transfers between devices: 21.8 us -> 20.8 us
    pallas_call x10, Pallas kernels: 2.47 us -> 5.73 us  [call(): pl.pallas_call(kernel, out_shape=out_shape, in_specs=[VMEM] * len(args),...]
    ppermute x14, waiting for transfers between devices: 16.8 us -> 14.7 us  [to_partner(): return lax.ppermute(x, 'row', [(r, r ^ flip) for r in range(n_row)])]
    ppermute x14, starting transfers between devices: 21 us -> 20 us  [to_partner(): return lax.ppermute(x, 'row', [(r, r ^ flip) for r in range(n_row)])]
  transfers between devices with their start and end apart: 17 -> 17, of which waited for: 11 -> 9; matrix products, arithmetic and copies ran while one was open for 0% -> 0% of each run, Pallas kernels for 1% -> 4%
where the time goes in v6:
time: 52.5 us; the launch traced here: 52.2 us
  starting transfers between devices  20.8 us (40%)
  waiting for transfers between devices  17.9 us (34%)
  Pallas kernels  8.34 us (16%)
  local copies, waits for them, and re-layouts  3.88 us (7%)
  between operations  1.37 us (3%)
    ppermute x14, starting transfers between devices, to_partner(): return lax.ppermute(x, 'row', [(r, r ^ flip) for r in range(n_row)])  20 us
    ppermute x14, waiting for transfers between devices, to_partner(): return lax.ppermute(x, 'row', [(r, r ^ flip) for r in range(n_row)])  14.7 us
    pallas_call x10, Pallas kernels, call(): pl.pallas_call(kernel, out_shape=out_shape, in_specs=[VMEM] * len(args),...  5.73 us
    unnamed x10, local copies, waits for them, and re-layouts  3.88 us
    ppermute x3, waiting for transfers between devices, other_core(): return lax.ppermute(x, 'col', [(0, 1), (1, 0)])  3.16 us
    pallas_call x1, Pallas kernels, fast_body(): pl.pallas_call(functools.partial(first_kernel, dims), out_shape=(f32((hal...  2.62 us
  transfers between devices with their start and end apart: 17, of which 9 were waited for; matrix products, arithmetic and copies ran while one was open for 0% of the time, Pallas kernels for 4%

profile of v6, /device:TPU:0, one launch (start us, length us, event | category | flops | bytes accessed | tf_op | source)
XLA Modules:
  0.0 52.2 jit_solution(14407894869045565845)
XLA Ops:
  1.3 0.0 copy-start
  1.3 1.9 %copy-done = bf16[1,1,96,128,128]{4,3,2,1,0:T(8,128)(2,1)S(1)} copy-done((bf16[1,1,96,128,128]{4,3,2,1,0:T(8,128)(2,1)S(1)}, bf16[1,1,96,128,128]{4,3,2,1,0:T(8,128)(2,1)}, u32[]{:S(2)}) %copy-start) | copy-done | bytes 3145752
  3.2 0.7 %copy-done.1 = s32[256]{0:T(256)S(1)} copy-done((s32[256]{0:T(256)S(1)}, s32[256]{0:T(256)}, u32[]{:S(2)}) %copy-start.1) | copy-done | bytes 1048
  3.8 0.7 %copy-done.3 = s32[1,1,96]{2,1,0:T(1,128)S(1)} copy-done((s32[1,1,96]{2,1,0:T(1,128)S(1)}, s32[1,1,96]{2,1,0:T(1,128)}, u32[]{:S(2)}) %copy-start.3) | copy-done | bytes 408
  4.5 0.7 %copy-done.4 = s32[1,1,96]{2,1,0:T(1,128)S(1)} copy-done((s32[1,1,96]{2,1,0:T(1,128)S(1)}, s32[1,1,96]{2,1,0:T(1,128)}, u32[]{:S(2)}) %copy-start.4) | copy-done | bytes 408
  5.2 2.6 %first_terms.1 = (f32[256,256]{1,0:T(8,128)S(1)}, f32[256,256]{1,0:T(8,128)S(1)}, bf16[1024,1280]{1,0:T(8,128)(2,1)S(1)}) custom-call(bf16[96,128,128]{2,1,0:T(8,128)(2,1)S(1)} %bitcast.7, s32[96]{0:T(128)S(1)} %bitcast.13, s32[96]{0:T(128)S(1)} %bitcast.14, s32[1]{0:T(128)} %bitcast.6.count_hbm, s32[1,256]{1,0:T(1,128)S(1)} %bitcast.8), custom_call_target="tpu_custom_call" | custom-call | tf_op jit(solution)/shard_map/first_terms/pallas_call | solution.py:234
  7.8 0.5 collective-permute-start
  8.3 1.2 %collective-permute-done.came_ref = f32[256,256]{1,0:T(8,128)S(1)} collective-permute-done((f32[256,256]{1,0:T(8,128)S(1)}, f32[256,256]{1,0:T(8,128)S(1)}, u32[]{:S(2)}, u32[]{:S(2)}) %collective-permute-start) | collective-permute-done | bytes 262176 | tf_op jit(solution)/shard_map/ppermute | solution.py:209
  9.5 0.7 %spread.1 = (bf16[128,256]{1,0:T(8,128)(2,1)}, f32[64,256]{1,0:T(8,128)S(1)}, f32[64,256]{1,0:T(8,128)S(1)}) custom-call(s32[1,256]{1,0:T(1,128)S(1)} %bitcast.9, f32[256,256]{1,0:T(8,128)S(1)} %get-tuple-element.16.keep_ref, f32[256,256]{1,0:T(8,128)S(1)} %collective-permute-done.came_ref), custom_call_target="tpu_custom_call" | custom-call | tf_op jit(solution)/shard_map/spread/pallas_call | solution.py:221
  10.2 2.9 %collective-permute-start.6 = (f32[64,256]{1,0:T(8,128)S(1)}, f32[64,256]{1,0:T(8,128)S(1)}, u32[]{:S(2)}, u32[]{:S(2)}) collective-permute-start(f32[64,256]{1,0:T(8,128)S(1)} %get-tuple-element.20), channel_id=1, source_target_pairs={{0,2},{2,0},{4,6},{6,4},{8,10},{10,8},{12,14},{14,12},{1,3},{3,1},... | collective-permute-start | bytes 196616 | tf_op jit(solution)/shard_map/ppermute | solution.py:212
  13.0 3.6 %collective-permute-start.3 = (bf16[128,256]{1,0:T(8,128)(2,1)}, bf16[128,256]{1,0:T(8,128)(2,1)}, u32[]{:S(2)}, u32[]{:S(2)}) collective-permute-start(bf16[128,256]{1,0:T(8,128)(2,1)} %get-tuple-element.18.refs_0_), channel_id=1, source_target_pairs={{0,12},{2,14},{4,8},{6,10},{8,4},{10,6},{12,0},{14,2},{1,13},{3,15... | collective-permute-start | bytes 196616 | tf_op jit(solution)/shard_map/ppermute | solution.py:212
  16.6 0.0 collective-permute-start.2
  16.6 0.8 %collective-permute-start.1 = (bf16[128,256]{1,0:T(8,128)(2,1)}, bf16[128,256]{1,0:T(8,128)(2,1)}, u32[]{:S(2)}, u32[]{:S(2)}) collective-permute-start(bf16[128,256]{1,0:T(8,128)(2,1)} %get-tuple-element.18.refs_0_), channel_id=1, source_target_pairs={{0,4},{2,6},{4,0},{6,2},{8,12},{10,14},{12,8},{14,10},{1,5},{3,7},... | collective-permute-start | bytes 196616 | tf_op jit(solution)/shard_map/ppermute | solution.py:212
  17.4 0.0 collective-permute-done.6.came_ref
  17.4 3.7 %collective-permute-start.9 = (f32[64,256]{1,0:T(8,128)S(1)}, f32[64,256]{1,0:T(8,128)S(1)}, u32[]{:S(2)}, u32[]{:S(2)}) collective-permute-start(f32[64,256]{1,0:T(8,128)S(1)} %plane_sum.1.refs_0_), channel_id=1, source_target_pairs={{0,12},{2,14},{4,8},{6,10},{8,4},{10,6},{12,0},{14,2},{1,13},{3,15... | collective-permute-start | bytes 196616 | tf_op jit(solution)/shard_map/ppermute | solution.py:212
  21.1 0.0 collective-permute-start.8
  21.1 0.0 collective-permute-done.3.refs_2_.refs_3_
  21.1 0.9 %collective-permute-start.7 = (f32[64,256]{1,0:T(8,128)S(1)}, f32[64,256]{1,0:T(8,128)S(1)}, u32[]{:S(2)}, u32[]{:S(2)}) collective-permute-start(f32[64,256]{1,0:T(8,128)S(1)} %plane_sum.1.refs_0_), channel_id=1, source_target_pairs={{0,4},{2,6},{4,0},{6,2},{8,12},{10,14},{12,8},{14,10},{1,5},{3,7},... | collective-permute-start | bytes 196616 | tf_op jit(solution)/shard_map/ppermute | solution.py:212
  21.9 3.0 %collective-permute-done.2.refs_1_.refs_2_ = bf16[128,256]{1,0:T(8,128)(2,1)} collective-permute-done((bf16[128,256]{1,0:T(8,128)(2,1)}, bf16[128,256]{1,0:T(8,128)(2,1)}, u32[]{:S(2)}, u32[]{:S(2)}) %collective-permute-start.2) | collective-permute-done | bytes 65568 | tf_op jit(solution)/shard_map/ppermute | solution.py:212
  25.0 0.0 collective-permute-done.1.refs_0_.refs_1_
  25.0 1.6 %join_far.1 = bf16[3,128,256]{2,1,0:T(8,128)(2,1)} custom-call(bf16[128,256]{1,0:T(8,128)(2,1)} %collective-permute-done.1.refs_0_.refs_1_, bf16[128,256]{1,0:T(8,128)(2,1)} %collective-permute-done.2.refs_1_.refs_2_, bf16[128,256]{1,0:T(8,128)(2,1)} %collective-permute-done.3.refs_2_.refs_3_), custom_call_target="tpu_custom_call" | custom-call | tf_op jit(solution)/shard_map/join_far/pallas_call | solution.py:221
  26.6 0.9 %collective-permute-start.5 = (bf16[3,128,256]{2,1,0:T(8,128)(2,1)}, bf16[3,128,256]{2,1,0:T(8,128)(2,1)}, u32[]{:S(2)}, u32[]{:S(2)}) collective-permute-start(bf16[3,128,256]{2,1,0:T(8,128)(2,1)} %join_far.1), channel_id=1, source_target_pairs={{0,2},{2,0},{4,6},{6,4},{8,10},{10,8},{12,14},{14,12},{1,3},{3,1},... | collective-permute-start | bytes 589832 | tf_op jit(solution)/shard_map/ppermute | solution.py:212
  27.5 0.0 collective-permute-done.9.refs_3_
  27.5 0.5 %collective-permute-done.8.refs_2_ = f32[64,256]{1,0:T(8,128)S(1)} collective-permute-done((f32[64,256]{1,0:T(8,128)S(1)}, f32[64,256]{1,0:T(8,128)S(1)}, u32[]{:S(2)}, u32[]{:S(2)}) %collective-permute-start.8) | collective-permute-done | bytes 65568 | tf_op jit(solution)/shard_map/ppermute | solution.py:212
  28.1 0.0 collective-permute-done.7.refs_1_
  28.1 0.1 hub_sums.1.mine_ref
  28.1 0.0 copy-start.2
  28.1 0.6 %collective-permute-start.10 = (bf16[64,256]{1,0:T(8,128)(2,1)S(1)}, bf16[64,256]{1,0:T(8,128)(2,1)S(1)}, u32[]{:S(2)}, u32[]{:S(2)}) collective-permute-start(bf16[64,256]{1,0:T(8,128)(2,1)S(1)} %hub_sums.1.mine_ref), channel_id=1, source_target_pairs={{0,2},{2,0},{4,6},{6,4},{8,10},{10,8},{12,14},{14,12},{1,3},{3,1},... | collective-permute-start | bytes 98312 | tf_op jit(solution)/shard_map/ppermute | solution.py:212
  28.8 1.5 %collective-permute-start.4 = (bf16[128,256]{1,0:T(8,128)(2,1)}, bf16[128,256]{1,0:T(8,128)(2,1)S(1)}, u32[]{:S(2)}, u32[]{:S(2)}) collective-permute-start(bf16[128,256]{1,0:T(8,128)(2,1)} %get-tuple-element.18.refs_0_), channel_id=1, source_target_pairs={{0,2},{2,0},{4,6},{6,4},{8,10},{10,8},{12,14},{14,12},{1,3},{3,1},... | collective-permute-start | bytes 196616 | tf_op jit(solution)/shard_map/ppermute | solution.py:212
  30.2 3.6 %collective-permute-done.10.theirs_ref = bf16[64,256]{1,0:T(8,128)(2,1)S(1)} collective-permute-done((bf16[64,256]{1,0:T(8,128)(2,1)S(1)}, bf16[64,256]{1,0:T(8,128)(2,1)S(1)}, u32[]{:S(2)}, u32[]{:S(2)}) %collective-permute-start.10) | collective-permute-done | bytes 32800 | tf_op jit(solution)/shard_map/ppermute | solution.py:212
  33.9 0.1 collective-permute-start.11
  33.9 0.6 %collective-permute-done.4.refs_4_ = bf16[128,256]{1,0:T(8,128)(2,1)S(1)} collective-permute-done((bf16[128,256]{1,0:T(8,128)(2,1)}, bf16[128,256]{1,0:T(8,128)(2,1)S(1)}, u32[]{:S(2)}, u32[]{:S(2)}) %collective-permute-start.4) | collective-permute-done | bytes 65568 | tf_op jit(solution)/shard_map/ppermute | solution.py:212
  34.6 0.6 %collective-permute-done.11.refs_7_ = bf16[128,256]{1,0:T(8,128)(2,1)S(1)} collective-permute-done((bf16[128,256]{1,0:T(8,128)(2,1)S(1)}, bf16[128,256]{1,0:T(8,128)(2,1)S(1)}, u32[]{:S(2)}, u32[]{:S(2)}) %collective-permute-start.11) | collective-permute-done | bytes 65568 | tf_op jit(solution)/shard_map/ppermute | solution.py:209
  35.2 0.0 collective-permute-done.5.refs_5_
  35.2 2.0 %later_terms.1 = (f32[256,256]{1,0:T(8,128)S(1)}, f32[256,256]{1,0:T(8,128)S(1)}) custom-call(bf16[128,256]{1,0:T(8,128)(2,1)} %get-tuple-element.18.refs_0_, bf16[128,256]{1,0:T(8,128)(2,1)} %collective-permute-done.1.refs_0_.refs_1_, bf16[128,256]{1,0:T(8,128)(2,1)} %collective-permute-done.2.refs_1_.refs_2_, ...), custom_call_target="tpu_custom_call" | custom-call | tf_op jit(solution)/shard_map/later_terms/pallas_call | solution.py:221
  37.2 0.2 collective-permute-start.12
  37.5 1.4 %collective-permute-done.12.came_ref = f32[256,256]{1,0:T(8,128)S(1)} collective-permute-done((f32[256,256]{1,0:T(8,128)S(1)}, f32[256,256]{1,0:T(8,128)S(1)}, u32[]{:S(2)}, u32[]{:S(2)}) %collective-permute-start.12) | collective-permute-done | bytes 262176 | tf_op jit(solution)/shard_map/ppermute | solution.py:209
  38.9 0.7 %collective-permute-start.13 = (f32[64,256]{1,0:T(8,128)S(1)}, f32[64,256]{1,0:T(8,128)S(1)}, u32[]{:S(2)}, u32[]{:S(2)}) collective-permute-start(f32[64,256]{1,0:T(8,128)S(1)} %get-tuple-element.25), channel_id=1, source_target_pairs={{0,2},{2,0},{4,6},{6,4},{8,10},{10,8},{12,14},{14,12},{1,3},{3,1},... | collective-permute-start | bytes 196616 | tf_op jit(solution)/shard_map/ppermute | solution.py:212
  39.6 3.6 %collective-permute-done.13.came_ref = f32[64,256]{1,0:T(8,128)S(1)} collective-permute-done((f32[64,256]{1,0:T(8,128)S(1)}, f32[64,256]{1,0:T(8,128)S(1)}, u32[]{:S(2)}, u32[]{:S(2)}) %collective-permute-start.13) | collective-permute-done | bytes 65568 | tf_op jit(solution)/shard_map/ppermute | solution.py:212
  43.2 0.1 collective-permute-start.14
  43.3 2.8 %collective-permute-start.15 = (f32[16,256]{1,0:T(8,128)S(1)}, f32[16,256]{1,0:T(8,128)S(1)}, u32[]{:S(2)}, u32[]{:S(2)}) collective-permute-start(f32[16,256]{1,0:T(8,128)S(1)} %get-tuple-element.28), channel_id=1, source_target_pairs={{0,8},{2,10},{4,12},{6,14},{8,0},{10,2},{12,4},{14,6},{1,9},{3,11}... | collective-permute-start | bytes 49160 | tf_op jit(solution)/shard_map/ppermute | solution.py:212
  46.1 1.6 %collective-permute-start.16 = (f32[16,256]{1,0:T(8,128)S(1)}, f32[16,256]{1,0:T(8,128)S(1)}, u32[]{:S(2)}, u32[]{:S(2)}) collective-permute-start(f32[16,256]{1,0:T(8,128)S(1)} %get-tuple-element.29), channel_id=1, source_target_pairs={{0,12},{2,14},{4,8},{6,10},{8,4},{10,6},{12,0},{14,2},{1,13},{3,15... | collective-permute-start | bytes 49160 | tf_op jit(solution)/shard_map/ppermute | solution.py:212
  47.7 0.0 copy-done.2
  47.7 0.7 %last_scores.1 = f32[128,256]{1,0:T(8,128)} custom-call(s32[1,256]{1,0:T(1,128)S(1)} %bitcast.11, f32[256,256]{1,0:T(8,128)S(1)} %get-tuple-element.22.keep_ref, f32[256,256]{1,0:T(8,128)S(1)} %collective-permute-done.12.came_ref), custom_call_target="tpu_custom_call" | custom-call | tf_op jit(solution)/shard_map/last_scores/pallas_call | solution.py:221
  48.4 0.0 collective-permute-done.14.refs_1_
  48.4 0.0 collective-permute-done.15.refs_2_
  48.4 3.2 %collective-permute-done.16.refs_3_ = f32[16,256]{1,0:T(8,128)S(1)} collective-permute-done((f32[16,256]{1,0:T(8,128)S(1)}, f32[16,256]{1,0:T(8,128)S(1)}, u32[]{:S(2)}, u32[]{:S(2)}) %collective-permute-start.16) | collective-permute-done | bytes 16416 | tf_op jit(solution)/shard_map/ppermute | solution.py:212
  51.6 0.6 %last_hubs.1 = f32[16,256]{1,0:T(8,128)} custom-call(s32[1,256]{1,0:T(1,128)S(1)} %bitcast.12, f32[16,256]{1,0:T(8,128)S(1)} %get-tuple-element.26.refs_0_, f32[16,256]{1,0:T(8,128)S(1)} %collective-permute-done.14.refs_1_, f32[16,256]{1,0:T(8,128)S(1)} %collective-permute-done.15.refs_2_, f32[16,256]{1,0:T(8,128)S(1)} %collective-permute-done.16.refs_3_), custom_call_target="tpu_custom_call" | custom-call | tf_op jit(solution)/shard_map/last_hubs/pallas_call | solution.py:221
  (7 shorter events, 0.0 us)
Async XLA Ops:
  1.3 1.9 %copy-start = (bf16[1,1,96,128,128]{4,3,2,1,0:T(8,128)(2,1)S(1)}, bf16[1,1,96,128,128]{4,3,2,1,0:T(8,128)(2,1)}, u32[]{:S(2)}) copy-start(bf16[1,1,96,128,128]{4,3,2,1,0:T(8,128)(2,1)} %param.5) | copy-start | bytes 9437188
  3.2 0.7 %copy-start.1 = (s32[256]{0:T(256)S(1)}, s32[256]{0:T(256)}, u32[]{:S(2)}) copy-start(s32[256]{0:T(256)} %param.9) | copy-start | bytes 3076
  3.8 0.7 %copy-start.3 = (s32[1,1,96]{2,1,0:T(1,128)S(1)}, s32[1,1,96]{2,1,0:T(1,128)}, u32[]{:S(2)}) copy-start(s32[1,1,96]{2,1,0:T(1,128)} %param.6) | copy-start | bytes 1156
  4.5 0.7 %copy-start.4 = (s32[1,1,96]{2,1,0:T(1,128)S(1)}, s32[1,1,96]{2,1,0:T(1,128)}, u32[]{:S(2)}) copy-start(s32[1,1,96]{2,1,0:T(1,128)} %param.7) | copy-start | bytes 1156
  7.8 1.7 %collective-permute-start = (f32[256,256]{1,0:T(8,128)S(1)}, f32[256,256]{1,0:T(8,128)S(1)}, u32[]{:S(2)}, u32[]{:S(2)}) collective-permute-start(f32[256,256]{1,0:T(8,128)S(1)} %get-tuple-element.17), channel_id=1, source_target_pairs={{0,1},{1,0},{2,3},{3,2},{4,5},{5,4},{6,7},{7,6},{8,9},{9,8},{10,11... | collective-permute-start | bytes 786440 | tf_op jit(solution)/shard_map/ppermute | solution.py:209
  10.2 7.2 %collective-permute-start.6 = (f32[64,256]{1,0:T(8,128)S(1)}, f32[64,256]{1,0:T(8,128)S(1)}, u32[]{:S(2)}, u32[]{:S(2)}) collective-permute-start(f32[64,256]{1,0:T(8,128)S(1)} %get-tuple-element.20), channel_id=1, source_target_pairs={{0,2},{2,0},{4,6},{6,4},{8,10},{10,8},{12,14},{14,12},{1,3},{3,1},... | collective-permute-start | bytes 196616 | tf_op jit(solution)/shard_map/ppermute | solution.py:212
  13.0 8.1 %collective-permute-start.3 = (bf16[128,256]{1,0:T(8,128)(2,1)}, bf16[128,256]{1,0:T(8,128)(2,1)}, u32[]{:S(2)}, u32[]{:S(2)}) collective-permute-start(bf16[128,256]{1,0:T(8,128)(2,1)} %get-tuple-element.18.refs_0_), channel_id=1, source_target_pairs={{0,12},{2,14},{4,8},{6,10},{8,4},{10,6},{12,0},{14,2},{1,13},{3,15... | collective-permute-start | bytes 196616 | tf_op jit(solution)/shard_map/ppermute | solution.py:212
  16.6 8.4 %collective-permute-start.2 = (bf16[128,256]{1,0:T(8,128)(2,1)}, bf16[128,256]{1,0:T(8,128)(2,1)}, u32[]{:S(2)}, u32[]{:S(2)}) collective-permute-start(bf16[128,256]{1,0:T(8,128)(2,1)} %get-tuple-element.18.refs_0_), channel_id=1, source_target_pairs={{0,8},{2,10},{4,12},{6,14},{8,0},{10,2},{12,4},{14,6},{1,9},{3,11}... | collective-permute-start | bytes 196616 | tf_op jit(solution)/shard_map/ppermute | solution.py:212
  16.6 8.4 %collective-permute-start.1 = (bf16[128,256]{1,0:T(8,128)(2,1)}, bf16[128,256]{1,0:T(8,128)(2,1)}, u32[]{:S(2)}, u32[]{:S(2)}) collective-permute-start(bf16[128,256]{1,0:T(8,128)(2,1)} %get-tuple-element.18.refs_0_), channel_id=1, source_target_pairs={{0,4},{2,6},{4,0},{6,2},{8,12},{10,14},{12,8},{14,10},{1,5},{3,7},... | collective-permute-start | bytes 196616 | tf_op jit(solution)/shard_map/ppermute | solution.py:212
  17.4 10.1 %collective-permute-start.9 = (f32[64,256]{1,0:T(8,128)S(1)}, f32[64,256]{1,0:T(8,128)S(1)}, u32[]{:S(2)}, u32[]{:S(2)}) collective-permute-start(f32[64,256]{1,0:T(8,128)S(1)} %plane_sum.1.refs_0_), channel_id=1, source_target_pairs={{0,12},{2,14},{4,8},{6,10},{8,4},{10,6},{12,0},{14,2},{1,13},{3,15... | collective-permute-start | bytes 196616 | tf_op jit(solution)/shard_map/ppermute | solution.py:212
  21.1 7.0 %collective-permute-start.8 = (f32[64,256]{1,0:T(8,128)S(1)}, f32[64,256]{1,0:T(8,128)S(1)}, u32[]{:S(2)}, u32[]{:S(2)}) collective-permute-start(f32[64,256]{1,0:T(8,128)S(1)} %plane_sum.1.refs_0_), channel_id=1, source_target_pairs={{0,8},{2,10},{4,12},{6,14},{8,0},{10,2},{12,4},{14,6},{1,9},{3,11}... | collective-permute-start | bytes 196616 | tf_op jit(solution)/shard_map/ppermute | solution.py:212
  21.1 7.0 %collective-permute-start.7 = (f32[64,256]{1,0:T(8,128)S(1)}, f32[64,256]{1,0:T(8,128)S(1)}, u32[]{:S(2)}, u32[]{:S(2)}) collective-permute-start(f32[64,256]{1,0:T(8,128)S(1)} %plane_sum.1.refs_0_), channel_id=1, source_target_pairs={{0,4},{2,6},{4,0},{6,2},{8,12},{10,14},{12,8},{14,10},{1,5},{3,7},... | collective-permute-start | bytes 196616 | tf_op jit(solution)/shard_map/ppermute | solution.py:212
  26.6 8.6 %collective-permute-start.5 = (bf16[3,128,256]{2,1,0:T(8,128)(2,1)}, bf16[3,128,256]{2,1,0:T(8,128)(2,1)}, u32[]{:S(2)}, u32[]{:S(2)}) collective-permute-start(bf16[3,128,256]{2,1,0:T(8,128)(2,1)} %join_far.1), channel_id=1, source_target_pairs={{0,2},{2,0},{4,6},{6,4},{8,10},{10,8},{12,14},{14,12},{1,3},{3,1},... | collective-permute-start | bytes 589832 | tf_op jit(solution)/shard_map/ppermute | solution.py:212
  28.1 19.5 %copy-start.2 = (s32[256]{0:T(256)S(1)}, s32[256]{0:T(256)}, u32[]{:S(2)}) copy-start(s32[256]{0:T(256)} %param.9) | copy-start | bytes 3076
  28.1 5.7 %collective-permute-start.10 = (bf16[64,256]{1,0:T(8,128)(2,1)S(1)}, bf16[64,256]{1,0:T(8,128)(2,1)S(1)}, u32[]{:S(2)}, u32[]{:S(2)}) collective-permute-start(bf16[64,256]{1,0:T(8,128)(2,1)S(1)} %hub_sums.1.mine_ref), channel_id=1, source_target_pairs={{0,2},{2,0},{4,6},{6,4},{8,10},{10,8},{12,14},{14,12},{1,3},{3,1},... | collective-permute-start | bytes 98312 | tf_op jit(solution)/shard_map/ppermute | solution.py:212
  28.8 5.8 %collective-permute-start.4 = (bf16[128,256]{1,0:T(8,128)(2,1)}, bf16[128,256]{1,0:T(8,128)(2,1)S(1)}, u32[]{:S(2)}, u32[]{:S(2)}) collective-permute-start(bf16[128,256]{1,0:T(8,128)(2,1)} %get-tuple-element.18.refs_0_), channel_id=1, source_target_pairs={{0,2},{2,0},{4,6},{6,4},{8,10},{10,8},{12,14},{14,12},{1,3},{3,1},... | collective-permute-start | bytes 196616 | tf_op jit(solution)/shard_map/ppermute | solution.py:212
  33.9 1.3 %collective-permute-start.11 = (bf16[128,256]{1,0:T(8,128)(2,1)S(1)}, bf16[128,256]{1,0:T(8,128)(2,1)S(1)}, u32[]{:S(2)}, u32[]{:S(2)}) collective-permute-start(bf16[128,256]{1,0:T(8,128)(2,1)S(1)} %join_sides.1.refs_6_), channel_id=1, source_target_pairs={{0,1},{1,0},{2,3},{3,2},{4,5},{5,4},{6,7},{7,6},{8,9},{9,8},{10,11... | collective-permute-start | bytes 196616 | tf_op jit(solution)/shard_map/ppermute | solution.py:209
  37.2 1.6 %collective-permute-start.12 = (f32[256,256]{1,0:T(8,128)S(1)}, f32[256,256]{1,0:T(8,128)S(1)}, u32[]{:S(2)}, u32[]{:S(2)}) collective-permute-start(f32[256,256]{1,0:T(8,128)S(1)} %get-tuple-element.23), channel_id=1, source_target_pairs={{0,1},{1,0},{2,3},{3,2},{4,5},{5,4},{6,7},{7,6},{8,9},{9,8},{10,11... | collective-permute-start | bytes 786440 | tf_op jit(solution)/shard_map/ppermute | solution.py:209
  38.9 4.3 %collective-permute-start.13 = (f32[64,256]{1,0:T(8,128)S(1)}, f32[64,256]{1,0:T(8,128)S(1)}, u32[]{:S(2)}, u32[]{:S(2)}) collective-permute-start(f32[64,256]{1,0:T(8,128)S(1)} %get-tuple-element.25), channel_id=1, source_target_pairs={{0,2},{2,0},{4,6},{6,4},{8,10},{10,8},{12,14},{14,12},{1,3},{3,1},... | collective-permute-start | bytes 196616 | tf_op jit(solution)/shard_map/ppermute | solution.py:212
  43.2 5.2 %collective-permute-start.14 = (f32[16,256]{1,0:T(8,128)S(1)}, f32[16,256]{1,0:T(8,128)S(1)}, u32[]{:S(2)}, u32[]{:S(2)}) collective-permute-start(f32[16,256]{1,0:T(8,128)S(1)} %get-tuple-element.27), channel_id=1, source_target_pairs={{0,4},{2,6},{4,0},{6,2},{8,12},{10,14},{12,8},{14,10},{1,5},{3,7},... | collective-permute-start | bytes 49160 | tf_op jit(solution)/shard_map/ppermute | solution.py:212
  43.3 5.1 %collective-permute-start.15 = (f32[16,256]{1,0:T(8,128)S(1)}, f32[16,256]{1,0:T(8,128)S(1)}, u32[]{:S(2)}, u32[]{:S(2)}) collective-permute-start(f32[16,256]{1,0:T(8,128)S(1)} %get-tuple-element.28), channel_id=1, source_target_pairs={{0,8},{2,10},{4,12},{6,14},{8,0},{10,2},{12,4},{14,6},{1,9},{3,11}... | collective-permute-start | bytes 49160 | tf_op jit(solution)/shard_map/ppermute | solution.py:212
  46.1 5.5 %collective-permute-start.16 = (f32[16,256]{1,0:T(8,128)S(1)}, f32[16,256]{1,0:T(8,128)S(1)}, u32[]{:S(2)}, u32[]{:S(2)}) collective-permute-start(f32[16,256]{1,0:T(8,128)S(1)} %get-tuple-element.29), channel_id=1, source_target_pairs={{0,12},{2,14},{4,8},{6,10},{8,4},{10,6},{12,0},{14,2},{1,13},{3,15... | collective-permute-start | bytes 49160 | tf_op jit(solution)/shard_map/ppermute | solution.py:212

commit v7 on v6

--- a/solution.py
+++ b/solution.py
@@ -263,11 +263,11 @@
         away = other_side(away)
         far = along_z([own] * n_z)
         across = other_side(own)
-        plane = call(plane_kernel, "plane_sum", f32((quarter, width)), hold, away, cost=100000)
+        plane = call(plane_kernel, "plane_sum", f32((quarter, width)), hold, away, cost=10)
         planes = [plane] + along_z([plane] * n_z)
         far_across = other_side(call(join_kernel, "join_far", bf16((n_z - 1, VB, width)), *far))
         mine = call(bind(hub_kernel, dims), "hub_sums", bf16((quarter, width)), src, *planes,
-                    scratch=[pltpu.VMEM((n_z, quarter, width), jnp.float32)], cost=100000)
+                    scratch=[pltpu.VMEM((n_z, quarter, width), jnp.float32)], cost=10)
         mine = call(side_kernel, "join_sides", bf16((H // n_col, width)), mine, other_side(mine))
         send, keep = call(
             bind(second_kernel, dims), "later_terms", (f32((half, width)), f32((half, width))),

time: 52.5 us -> 49.6 us (0.945)
  Pallas kernels: 8.34 us -> 5.09 us
    pallas_call x10, Pallas kernels: 5.73 us -> 2.47 us  [call(): pl.pallas_call(kernel, out_shape=out_shape, in_specs=[VMEM] * len(args),...]
  transfers between devices with their start and end apart: 17 -> 17, of which waited for: 9 -> 9; matrix products, arithmetic and copies ran while one was open for 0% -> 0% of each run, Pallas kernels for 4% -> 2%
where the time goes in v7:
time: 49.6 us; the launch traced here: 49.4 us
  starting transfers between devices  21.1 us (43%)
  waiting for transfers between devices  17.9 us (36%)
  Pallas kernels  5.09 us (10%)
  local copies, waits for them, and re-layouts  3.88 us (8%)
  between operations  1.37 us (3%)
    ppermute x14, starting transfers between devices, to_partner(): return lax.ppermute(x, 'row', [(r, r ^ flip) for r in range(n_row)])  20.3 us
    ppermute x14, waiting for transfers between devices, to_partner(): return lax.ppermute(x, 'row', [(r, r ^ flip) for r in range(n_row)])  14.8 us
    unnamed x10, local copies, waits for them, and re-layouts  3.88 us
    ppermute x3, waiting for transfers between devices, other_core(): return lax.ppermute(x, 'col', [(0, 1), (1, 0)])  3.12 us
    pallas_call x1, Pallas kernels, fast_body(): pl.pallas_call(functools.partial(first_kernel, dims), out_shape=(f32((hal...  2.62 us
    pallas_call x10, Pallas kernels, call(): pl.pallas_call(kernel, out_shape=out_shape, in_specs=[VMEM] * len(args),...  2.47 us
  transfers between devices with their start and end apart: 17, of which 9 were waited for; matrix products, arithmetic and copies ran while one was open for 0% of the time, Pallas kernels for 2%

profile of v7, /device:TPU:0, one launch (start us, length us, event | category | flops | bytes accessed | tf_op | source)
XLA Modules:
  0.0 49.4 jit_solution(8862011134424504756)
XLA Ops:
  1.3 0.0 copy-start
  1.3 1.9 %copy-done = bf16[1,1,96,128,128]{4,3,2,1,0:T(8,128)(2,1)S(1)} copy-done((bf16[1,1,96,128,128]{4,3,2,1,0:T(8,128)(2,1)S(1)}, bf16[1,1,96,128,128]{4,3,2,1,0:T(8,128)(2,1)}, u32[]{:S(2)}) %copy-start) | copy-done | bytes 3145752
  3.2 0.0 copy-start.1
  3.2 0.7 %copy-done.1 = s32[256]{0:T(256)S(1)} copy-done((s32[256]{0:T(256)S(1)}, s32[256]{0:T(256)}, u32[]{:S(2)}) %copy-start.1) | copy-done | bytes 1048
  3.8 0.7 %copy-done.3 = s32[1,1,96]{2,1,0:T(1,128)S(1)} copy-done((s32[1,1,96]{2,1,0:T(1,128)S(1)}, s32[1,1,96]{2,1,0:T(1,128)}, u32[]{:S(2)}) %copy-start.3) | copy-done | bytes 408
  4.5 0.7 %copy-done.4 = s32[1,1,96]{2,1,0:T(1,128)S(1)} copy-done((s32[1,1,96]{2,1,0:T(1,128)S(1)}, s32[1,1,96]{2,1,0:T(1,128)}, u32[]{:S(2)}) %copy-start.4) | copy-done | bytes 408
  5.2 2.6 %first_terms.1 = (f32[256,256]{1,0:T(8,128)S(1)}, f32[256,256]{1,0:T(8,128)S(1)}, bf16[1024,1280]{1,0:T(8,128)(2,1)S(1)}) custom-call(bf16[96,128,128]{2,1,0:T(8,128)(2,1)S(1)} %bitcast.7, s32[96]{0:T(128)S(1)} %bitcast.13, s32[96]{0:T(128)S(1)} %bitcast.14, s32[1]{0:T(128)} %bitcast.6.count_hbm, s32[1,256]{1,0:T(1,128)S(1)} %bitcast.8), custom_call_target="tpu_custom_call" | custom-call | tf_op jit(solution)/shard_map/first_terms/pallas_call | solution.py:234
  7.8 0.5 %collective-permute-start = (f32[256,256]{1,0:T(8,128)S(1)}, f32[256,256]{1,0:T(8,128)S(1)}, u32[]{:S(2)}, u32[]{:S(2)}) collective-permute-start(f32[256,256]{1,0:T(8,128)S(1)} %get-tuple-element.17), channel_id=1, source_target_pairs={{0,1},{1,0},{2,3},{3,2},{4,5},{5,4},{6,7},{7,6},{8,9},{9,8},{10,11... | collective-permute-start | bytes 786440 | tf_op jit(solution)/shard_map/ppermute | solution.py:209
  8.3 1.2 %collective-permute-done.came_ref = f32[256,256]{1,0:T(8,128)S(1)} collective-permute-done((f32[256,256]{1,0:T(8,128)S(1)}, f32[256,256]{1,0:T(8,128)S(1)}, u32[]{:S(2)}, u32[]{:S(2)}) %collective-permute-start) | collective-permute-done | bytes 262176 | tf_op jit(solution)/shard_map/ppermute | solution.py:209
  9.5 0.1 spread.1
  9.5 2.9 %collective-permute-start.6 = (f32[64,256]{1,0:T(8,128)S(1)}, f32[64,256]{1,0:T(8,128)S(1)}, u32[]{:S(2)}, u32[]{:S(2)}) collective-permute-start(f32[64,256]{1,0:T(8,128)S(1)} %get-tuple-element.20), channel_id=1, source_target_pairs={{0,2},{2,0},{4,6},{6,4},{8,10},{10,8},{12,14},{14,12},{1,3},{3,1},... | collective-permute-start | bytes 196616 | tf_op jit(solution)/shard_map/ppermute | solution.py:212
  12.5 3.6 %collective-permute-start.3 = (bf16[128,256]{1,0:T(8,128)(2,1)S(1)}, bf16[128,256]{1,0:T(8,128)(2,1)S(1)}, u32[]{:S(2)}, u32[]{:S(2)}) collective-permute-start(bf16[128,256]{1,0:T(8,128)(2,1)S(1)} %get-tuple-element.18.refs_0_), channel_id=1, source_target_pairs={{0,12},{2,14},{4,8},{6,10},{8,4},{10,6},{12,0},{14,2},{1,13},{3,15... | collective-permute-start | bytes 196616 | tf_op jit(solution)/shard_map/ppermute | solution.py:212
  16.1 0.0 collective-permute-start.2
  16.1 0.8 %collective-permute-start.1 = (bf16[128,256]{1,0:T(8,128)(2,1)S(1)}, bf16[128,256]{1,0:T(8,128)(2,1)S(1)}, u32[]{:S(2)}, u32[]{:S(2)}) collective-permute-start(bf16[128,256]{1,0:T(8,128)(2,1)S(1)} %get-tuple-element.18.refs_0_), channel_id=1, source_target_pairs={{0,4},{2,6},{4,0},{6,2},{8,12},{10,14},{12,8},{14,10},{1,5},{3,7},... | collective-permute-start | bytes 196616 | tf_op jit(solution)/shard_map/ppermute | solution.py:212
  16.8 0.0 collective-permute-done.6.came_ref
  16.9 3.7 %collective-permute-start.9 = (f32[64,256]{1,0:T(8,128)S(1)}, f32[64,256]{1,0:T(8,128)S(1)}, u32[]{:S(2)}, u32[]{:S(2)}) collective-permute-start(f32[64,256]{1,0:T(8,128)S(1)} %plane_sum.1.refs_0_), channel_id=1, source_target_pairs={{0,12},{2,14},{4,8},{6,10},{8,4},{10,6},{12,0},{14,2},{1,13},{3,15... | collective-permute-start | bytes 196616 | tf_op jit(solution)/shard_map/ppermute | solution.py:212
  20.5 0.0 collective-permute-start.8
  20.5 0.0 collective-permute-done.3.refs_2_.refs_3_
  20.5 0.8 %collective-permute-start.7 = (f32[64,256]{1,0:T(8,128)S(1)}, f32[64,256]{1,0:T(8,128)S(1)}, u32[]{:S(2)}, u32[]{:S(2)}) collective-permute-start(f32[64,256]{1,0:T(8,128)S(1)} %plane_sum.1.refs_0_), channel_id=1, source_target_pairs={{0,4},{2,6},{4,0},{6,2},{8,12},{10,14},{12,8},{14,10},{1,5},{3,7},... | collective-permute-start | bytes 196616 | tf_op jit(solution)/shard_map/ppermute | solution.py:212
  21.3 3.0 %collective-permute-done.2.refs_1_.refs_2_ = bf16[128,256]{1,0:T(8,128)(2,1)S(1)} collective-permute-done((bf16[128,256]{1,0:T(8,128)(2,1)S(1)}, bf16[128,256]{1,0:T(8,128)(2,1)S(1)}, u32[]{:S(2)}, u32[]{:S(2)}) %collective-permute-start.2) | collective-permute-done | bytes 65568 | tf_op jit(solution)/shard_map/ppermute | solution.py:212
  24.3 0.0 collective-permute-done.1.refs_0_.refs_1_
  24.3 1.0 %collective-permute-start.5 = (bf16[3,128,256]{2,1,0:T(8,128)(2,1)S(1)}, bf16[3,128,256]{2,1,0:T(8,128)(2,1)S(1)}, u32[]{:S(2)}, u32[]{:S(2)}) collective-permute-start(bf16[3,128,256]{2,1,0:T(8,128)(2,1)S(1)} %join_far.1), channel_id=1, source_target_pairs={{0,2},{2,0},{4,6},{6,4},{8,10},{10,8},{12,14},{14,12},{1,3},{3,1},... | collective-permute-start | bytes 589832 | tf_op jit(solution)/shard_map/ppermute | solution.py:212
  25.4 0.0 collective-permute-done.9.refs_3_
  25.4 1.9 %collective-permute-done.8.refs_2_ = f32[64,256]{1,0:T(8,128)S(1)} collective-permute-done((f32[64,256]{1,0:T(8,128)S(1)}, f32[64,256]{1,0:T(8,128)S(1)}, u32[]{:S(2)}, u32[]{:S(2)}) %collective-permute-start.8) | collective-permute-done | bytes 65568 | tf_op jit(solution)/shard_map/ppermute | solution.py:212
  27.3 0.0 collective-permute-done.7.refs_1_
  27.3 0.1 hub_sums.1.mine_ref
  27.4 0.0 copy-start.2
  27.4 0.6 %collective-permute-start.10 = (bf16[64,256]{1,0:T(8,128)(2,1)S(1)}, bf16[64,256]{1,0:T(8,128)(2,1)S(1)}, u32[]{:S(2)}, u32[]{:S(2)}) collective-permute-start(bf16[64,256]{1,0:T(8,128)(2,1)S(1)} %hub_sums.1.mine_ref), channel_id=1, source_target_pairs={{0,2},{2,0},{4,6},{6,4},{8,10},{10,8},{12,14},{14,12},{1,3},{3,1},... | collective-permute-start | bytes 98312 | tf_op jit(solution)/shard_map/ppermute | solution.py:212
  28.0 1.5 %collective-permute-start.4 = (bf16[128,256]{1,0:T(8,128)(2,1)S(1)}, bf16[128,256]{1,0:T(8,128)(2,1)S(1)}, u32[]{:S(2)}, u32[]{:S(2)}) collective-permute-start(bf16[128,256]{1,0:T(8,128)(2,1)S(1)} %get-tuple-element.18.refs_0_), channel_id=1, source_target_pairs={{0,2},{2,0},{4,6},{6,4},{8,10},{10,8},{12,14},{14,12},{1,3},{3,1},... | collective-permute-start | bytes 196616 | tf_op jit(solution)/shard_map/ppermute | solution.py:212
  29.5 2.0 %collective-permute-done.10.theirs_ref = bf16[64,256]{1,0:T(8,128)(2,1)S(1)} collective-permute-done((bf16[64,256]{1,0:T(8,128)(2,1)S(1)}, bf16[64,256]{1,0:T(8,128)(2,1)S(1)}, u32[]{:S(2)}, u32[]{:S(2)}) %collective-permute-start.10) | collective-permute-done | bytes 32800 | tf_op jit(solution)/shard_map/ppermute | solution.py:212
  31.5 0.1 collective-permute-start.11
  31.6 0.7 %collective-permute-done.4.refs_4_ = bf16[128,256]{1,0:T(8,128)(2,1)S(1)} collective-permute-done((bf16[128,256]{1,0:T(8,128)(2,1)S(1)}, bf16[128,256]{1,0:T(8,128)(2,1)S(1)}, u32[]{:S(2)}, u32[]{:S(2)}) %collective-permute-start.4) | collective-permute-done | bytes 65568 | tf_op jit(solution)/shard_map/ppermute | solution.py:212
  32.2 0.6 %collective-permute-done.11.refs_7_ = bf16[128,256]{1,0:T(8,128)(2,1)S(1)} collective-permute-done((bf16[128,256]{1,0:T(8,128)(2,1)S(1)}, bf16[128,256]{1,0:T(8,128)(2,1)S(1)}, u32[]{:S(2)}, u32[]{:S(2)}) %collective-permute-start.11) | collective-permute-done | bytes 65568 | tf_op jit(solution)/shard_map/ppermute | solution.py:209
  32.8 0.0 collective-permute-done.5.refs_5_
  32.8 1.0 %later_terms.1 = (f32[256,256]{1,0:T(8,128)S(1)}, f32[256,256]{1,0:T(8,128)S(1)}) custom-call(bf16[128,256]{1,0:T(8,128)(2,1)S(1)} %get-tuple-element.18.refs_0_, bf16[128,256]{1,0:T(8,128)(2,1)S(1)} %collective-permute-done.1.refs_0_.refs_1_, bf16[128,256]{1,0:T(8,128)(2,1)S(1)} %collective-permute-done.2.refs_1_.refs_2_, ...), custom_call_target="tpu_custom_call" | custom-call | tf_op jit(solution)/shard_map/later_terms/pallas_call | solution.py:221
  33.8 0.2 collective-permute-start.12
  34.0 1.4 %collective-permute-done.12.came_ref = f32[256,256]{1,0:T(8,128)S(1)} collective-permute-done((f32[256,256]{1,0:T(8,128)S(1)}, f32[256,256]{1,0:T(8,128)S(1)}, u32[]{:S(2)}, u32[]{:S(2)}) %collective-permute-start.12) | collective-permute-done | bytes 262176 | tf_op jit(solution)/shard_map/ppermute | solution.py:209
  35.4 1.0 %collective-permute-start.13 = (f32[64,256]{1,0:T(8,128)S(1)}, f32[64,256]{1,0:T(8,128)S(1)}, u32[]{:S(2)}, u32[]{:S(2)}) collective-permute-start(f32[64,256]{1,0:T(8,128)S(1)} %get-tuple-element.25), channel_id=1, source_target_pairs={{0,2},{2,0},{4,6},{6,4},{8,10},{10,8},{12,14},{14,12},{1,3},{3,1},... | collective-permute-start | bytes 196616 | tf_op jit(solution)/shard_map/ppermute | solution.py:212
  36.4 3.4 %collective-permute-done.13.came_ref = f32[64,256]{1,0:T(8,128)S(1)} collective-permute-done((f32[64,256]{1,0:T(8,128)S(1)}, f32[64,256]{1,0:T(8,128)S(1)}, u32[]{:S(2)}, u32[]{:S(2)}) %collective-permute-start.13) | collective-permute-done | bytes 65568 | tf_op jit(solution)/shard_map/ppermute | solution.py:212
  39.8 0.1 collective-permute-start.14
  39.9 3.4 %collective-permute-start.15 = (f32[16,256]{1,0:T(8,128)S(1)}, f32[16,256]{1,0:T(8,128)S(1)}, u32[]{:S(2)}, u32[]{:S(2)}) collective-permute-start(f32[16,256]{1,0:T(8,128)S(1)} %get-tuple-element.28), channel_id=1, source_target_pairs={{0,8},{2,10},{4,12},{6,14},{8,0},{10,2},{12,4},{14,6},{1,9},{3,11}... | collective-permute-start | bytes 49160 | tf_op jit(solution)/shard_map/ppermute | solution.py:212
  43.2 1.0 %collective-permute-start.16 = (f32[16,256]{1,0:T(8,128)S(1)}, f32[16,256]{1,0:T(8,128)S(1)}, u32[]{:S(2)}, u32[]{:S(2)}) collective-permute-start(f32[16,256]{1,0:T(8,128)S(1)} %get-tuple-element.29), channel_id=1, source_target_pairs={{0,12},{2,14},{4,8},{6,10},{8,4},{10,6},{12,0},{14,2},{1,13},{3,15... | collective-permute-start | bytes 49160 | tf_op jit(solution)/shard_map/ppermute | solution.py:212
  44.2 0.0 copy-done.2
  44.2 0.7 %last_scores.1 = f32[128,256]{1,0:T(8,128)} custom-call(s32[1,256]{1,0:T(1,128)S(1)} %bitcast.11, f32[256,256]{1,0:T(8,128)S(1)} %get-tuple-element.22.keep_ref, f32[256,256]{1,0:T(8,128)S(1)} %collective-permute-done.12.came_ref), custom_call_target="tpu_custom_call" | custom-call | tf_op jit(solution)/shard_map/last_scores/pallas_call | solution.py:221
  44.9 0.0 collective-permute-done.14.refs_1_
  44.9 0.0 collective-permute-done.15.refs_2_
  44.9 3.8 %collective-permute-done.16.refs_3_ = f32[16,256]{1,0:T(8,128)S(1)} collective-permute-done((f32[16,256]{1,0:T(8,128)S(1)}, f32[16,256]{1,0:T(8,128)S(1)}, u32[]{:S(2)}, u32[]{:S(2)}) %collective-permute-start.16) | collective-permute-done | bytes 16416 | tf_op jit(solution)/shard_map/ppermute | solution.py:212
  48.8 0.6 %last_hubs.1 = f32[16,256]{1,0:T(8,128)} custom-call(s32[1,256]{1,0:T(1,128)S(1)} %bitcast.12, f32[16,256]{1,0:T(8,128)S(1)} %get-tuple-element.26.refs_0_, f32[16,256]{1,0:T(8,128)S(1)} %collective-permute-done.14.refs_1_, f32[16,256]{1,0:T(8,128)S(1)} %collective-permute-done.15.refs_2_, f32[16,256]{1,0:T(8,128)S(1)} %collective-permute-done.16.refs_3_), custom_call_target="tpu_custom_call" | custom-call | tf_op jit(solution)/shard_map/last_hubs/pallas_call | solution.py:221
  (7 shorter events, 0.1 us)
Async XLA Ops:
  1.3 1.9 %copy-start = (bf16[1,1,96,128,128]{4,3,2,1,0:T(8,128)(2,1)S(1)}, bf16[1,1,96,128,128]{4,3,2,1,0:T(8,128)(2,1)}, u32[]{:S(2)}) copy-start(bf16[1,1,96,128,128]{4,3,2,1,0:T(8,128)(2,1)} %param.5) | copy-start | bytes 9437188
  3.2 0.7 %copy-start.1 = (s32[256]{0:T(256)S(1)}, s32[256]{0:T(256)}, u32[]{:S(2)}) copy-start(s32[256]{0:T(256)} %param.9) | copy-start | bytes 3076
  3.8 0.7 %copy-start.3 = (s32[1,1,96]{2,1,0:T(1,128)S(1)}, s32[1,1,96]{2,1,0:T(1,128)}, u32[]{:S(2)}) copy-start(s32[1,1,96]{2,1,0:T(1,128)} %param.6) | copy-start | bytes 1156
  4.5 0.7 %copy-start.4 = (s32[1,1,96]{2,1,0:T(1,128)S(1)}, s32[1,1,96]{2,1,0:T(1,128)}, u32[]{:S(2)}) copy-start(s32[1,1,96]{2,1,0:T(1,128)} %param.7) | copy-start | bytes 1156
  7.8 1.7 %collective-permute-start = (f32[256,256]{1,0:T(8,128)S(1)}, f32[256,256]{1,0:T(8,128)S(1)}, u32[]{:S(2)}, u32[]{:S(2)}) collective-permute-start(f32[256,256]{1,0:T(8,128)S(1)} %get-tuple-element.17), channel_id=1, source_target_pairs={{0,1},{1,0},{2,3},{3,2},{4,5},{5,4},{6,7},{7,6},{8,9},{9,8},{10,11... | collective-permute-start | bytes 786440 | tf_op jit(solution)/shard_map/ppermute | solution.py:209
  9.5 7.3 %collective-permute-start.6 = (f32[64,256]{1,0:T(8,128)S(1)}, f32[64,256]{1,0:T(8,128)S(1)}, u32[]{:S(2)}, u32[]{:S(2)}) collective-permute-start(f32[64,256]{1,0:T(8,128)S(1)} %get-tuple-element.20), channel_id=1, source_target_pairs={{0,2},{2,0},{4,6},{6,4},{8,10},{10,8},{12,14},{14,12},{1,3},{3,1},... | collective-permute-start | bytes 196616 | tf_op jit(solution)/shard_map/ppermute | solution.py:212
  12.5 8.1 %collective-permute-start.3 = (bf16[128,256]{1,0:T(8,128)(2,1)S(1)}, bf16[128,256]{1,0:T(8,128)(2,1)S(1)}, u32[]{:S(2)}, u32[]{:S(2)}) collective-permute-start(bf16[128,256]{1,0:T(8,128)(2,1)S(1)} %get-tuple-element.18.refs_0_), channel_id=1, source_target_pairs={{0,12},{2,14},{4,8},{6,10},{8,4},{10,6},{12,0},{14,2},{1,13},{3,15... | collective-permute-start | bytes 196616 | tf_op jit(solution)/shard_map/ppermute | solution.py:212
  16.1 8.3 %collective-permute-start.2 = (bf16[128,256]{1,0:T(8,128)(2,1)S(1)}, bf16[128,256]{1,0:T(8,128)(2,1)S(1)}, u32[]{:S(2)}, u32[]{:S(2)}) collective-permute-start(bf16[128,256]{1,0:T(8,128)(2,1)S(1)} %get-tuple-element.18.refs_0_), channel_id=1, source_target_pairs={{0,8},{2,10},{4,12},{6,14},{8,0},{10,2},{12,4},{14,6},{1,9},{3,11}... | collective-permute-start | bytes 196616 | tf_op jit(solution)/shard_map/ppermute | solution.py:212
  16.1 8.3 %collective-permute-start.1 = (bf16[128,256]{1,0:T(8,128)(2,1)S(1)}, bf16[128,256]{1,0:T(8,128)(2,1)S(1)}, u32[]{:S(2)}, u32[]{:S(2)}) collective-permute-start(bf16[128,256]{1,0:T(8,128)(2,1)S(1)} %get-tuple-element.18.refs_0_), channel_id=1, source_target_pairs={{0,4},{2,6},{4,0},{6,2},{8,12},{10,14},{12,8},{14,10},{1,5},{3,7},... | collective-permute-start | bytes 196616 | tf_op jit(solution)/shard_map/ppermute | solution.py:212
  16.9 8.5 %collective-permute-start.9 = (f32[64,256]{1,0:T(8,128)S(1)}, f32[64,256]{1,0:T(8,128)S(1)}, u32[]{:S(2)}, u32[]{:S(2)}) collective-permute-start(f32[64,256]{1,0:T(8,128)S(1)} %plane_sum.1.refs_0_), channel_id=1, source_target_pairs={{0,12},{2,14},{4,8},{6,10},{8,4},{10,6},{12,0},{14,2},{1,13},{3,15... | collective-permute-start | bytes 196616 | tf_op jit(solution)/shard_map/ppermute | solution.py:212
  20.5 6.8 %collective-permute-start.8 = (f32[64,256]{1,0:T(8,128)S(1)}, f32[64,256]{1,0:T(8,128)S(1)}, u32[]{:S(2)}, u32[]{:S(2)}) collective-permute-start(f32[64,256]{1,0:T(8,128)S(1)} %plane_sum.1.refs_0_), channel_id=1, source_target_pairs={{0,8},{2,10},{4,12},{6,14},{8,0},{10,2},{12,4},{14,6},{1,9},{3,11}... | collective-permute-start | bytes 196616 | tf_op jit(solution)/shard_map/ppermute | solution.py:212
  20.5 6.8 %collective-permute-start.7 = (f32[64,256]{1,0:T(8,128)S(1)}, f32[64,256]{1,0:T(8,128)S(1)}, u32[]{:S(2)}, u32[]{:S(2)}) collective-permute-start(f32[64,256]{1,0:T(8,128)S(1)} %plane_sum.1.refs_0_), channel_id=1, source_target_pairs={{0,4},{2,6},{4,0},{6,2},{8,12},{10,14},{12,8},{14,10},{1,5},{3,7},... | collective-permute-start | bytes 196616 | tf_op jit(solution)/shard_map/ppermute | solution.py:212
  24.3 8.5 %collective-permute-start.5 = (bf16[3,128,256]{2,1,0:T(8,128)(2,1)S(1)}, bf16[3,128,256]{2,1,0:T(8,128)(2,1)S(1)}, u32[]{:S(2)}, u32[]{:S(2)}) collective-permute-start(bf16[3,128,256]{2,1,0:T(8,128)(2,1)S(1)} %join_far.1), channel_id=1, source_target_pairs={{0,2},{2,0},{4,6},{6,4},{8,10},{10,8},{12,14},{14,12},{1,3},{3,1},... | collective-permute-start | bytes 589832 | tf_op jit(solution)/shard_map/ppermute | solution.py:212
  27.4 16.9 %copy-start.2 = (s32[256]{0:T(256)S(1)}, s32[256]{0:T(256)}, u32[]{:S(2)}) copy-start(s32[256]{0:T(256)} %param.9) | copy-start | bytes 3076
  27.4 4.1 %collective-permute-start.10 = (bf16[64,256]{1,0:T(8,128)(2,1)S(1)}, bf16[64,256]{1,0:T(8,128)(2,1)S(1)}, u32[]{:S(2)}, u32[]{:S(2)}) collective-permute-start(bf16[64,256]{1,0:T(8,128)(2,1)S(1)} %hub_sums.1.mine_ref), channel_id=1, source_target_pairs={{0,2},{2,0},{4,6},{6,4},{8,10},{10,8},{12,14},{14,12},{1,3},{3,1},... | collective-permute-start | bytes 98312 | tf_op jit(solution)/shard_map/ppermute | solution.py:212
  28.0 4.3 %collective-permute-start.4 = (bf16[128,256]{1,0:T(8,128)(2,1)S(1)}, bf16[128,256]{1,0:T(8,128)(2,1)S(1)}, u32[]{:S(2)}, u32[]{:S(2)}) collective-permute-start(bf16[128,256]{1,0:T(8,128)(2,1)S(1)} %get-tuple-element.18.refs_0_), channel_id=1, source_target_pairs={{0,2},{2,0},{4,6},{6,4},{8,10},{10,8},{12,14},{14,12},{1,3},{3,1},... | collective-permute-start | bytes 196616 | tf_op jit(solution)/shard_map/ppermute | solution.py:212
  31.5 1.3 %collective-permute-start.11 = (bf16[128,256]{1,0:T(8,128)(2,1)S(1)}, bf16[128,256]{1,0:T(8,128)(2,1)S(1)}, u32[]{:S(2)}, u32[]{:S(2)}) collective-permute-start(bf16[128,256]{1,0:T(8,128)(2,1)S(1)} %join_sides.1.refs_6_), channel_id=1, source_target_pairs={{0,1},{1,0},{2,3},{3,2},{4,5},{5,4},{6,7},{7,6},{8,9},{9,8},{10,11... | collective-permute-start | bytes 196616 | tf_op jit(solution)/shard_map/ppermute | solution.py:209
  33.8 1.6 %collective-permute-start.12 = (f32[256,256]{1,0:T(8,128)S(1)}, f32[256,256]{1,0:T(8,128)S(1)}, u32[]{:S(2)}, u32[]{:S(2)}) collective-permute-start(f32[256,256]{1,0:T(8,128)S(1)} %get-tuple-element.23), channel_id=1, source_target_pairs={{0,1},{1,0},{2,3},{3,2},{4,5},{5,4},{6,7},{7,6},{8,9},{9,8},{10,11... | collective-permute-start | bytes 786440 | tf_op jit(solution)/shard_map/ppermute | solution.py:209
  35.4 4.3 %collective-permute-start.13 = (f32[64,256]{1,0:T(8,128)S(1)}, f32[64,256]{1,0:T(8,128)S(1)}, u32[]{:S(2)}, u32[]{:S(2)}) collective-permute-start(f32[64,256]{1,0:T(8,128)S(1)} %get-tuple-element.25), channel_id=1, source_target_pairs={{0,2},{2,0},{4,6},{6,4},{8,10},{10,8},{12,14},{14,12},{1,3},{3,1},... | collective-permute-start | bytes 196616 | tf_op jit(solution)/shard_map/ppermute | solution.py:212
  39.8 5.2 %collective-permute-start.14 = (f32[16,256]{1,0:T(8,128)S(1)}, f32[16,256]{1,0:T(8,128)S(1)}, u32[]{:S(2)}, u32[]{:S(2)}) collective-permute-start(f32[16,256]{1,0:T(8,128)S(1)} %get-tuple-element.27), channel_id=1, source_target_pairs={{0,4},{2,6},{4,0},{6,2},{8,12},{10,14},{12,8},{14,10},{1,5},{3,7},... | collective-permute-start | bytes 49160 | tf_op jit(solution)/shard_map/ppermute | solution.py:212
  39.9 5.1 %collective-permute-start.15 = (f32[16,256]{1,0:T(8,128)S(1)}, f32[16,256]{1,0:T(8,128)S(1)}, u32[]{:S(2)}, u32[]{:S(2)}) collective-permute-start(f32[16,256]{1,0:T(8,128)S(1)} %get-tuple-element.28), channel_id=1, source_target_pairs={{0,8},{2,10},{4,12},{6,14},{8,0},{10,2},{12,4},{14,6},{1,9},{3,11}... | collective-permute-start | bytes 49160 | tf_op jit(solution)/shard_map/ppermute | solution.py:212
  43.2 5.5 %collective-permute-start.16 = (f32[16,256]{1,0:T(8,128)S(1)}, f32[16,256]{1,0:T(8,128)S(1)}, u32[]{:S(2)}, u32[]{:S(2)}) collective-permute-start(f32[16,256]{1,0:T(8,128)S(1)} %get-tuple-element.29), channel_id=1, source_target_pairs={{0,12},{2,14},{4,8},{6,10},{8,4},{10,6},{12,0},{14,2},{1,13},{3,15... | collective-permute-start | bytes 49160 | tf_op jit(solution)/shard_map/ppermute | solution.py:212

commit v8 on v7

--- a/solution.py
+++ b/solution.py
@@ -15,6 +15,7 @@
 X = 2
 MICRO = 10 ** 9
 VMEM_LIMIT = 32 * 1024 * 1024
+FIRST_VMEM_LIMIT = 60 * 1024 * 1024
 
 SMEM = pl.BlockSpec(memory_space=pltpu.SMEM)
 VMEM = pl.BlockSpec(memory_space=pltpu.VMEM)
@@ -43,22 +44,45 @@
             ref[VB + k * block:VB + (k + 1) * block] = prod_ref[pl.ds(pl.multiple_of(start, block), block), :]
 
 
-def first_kernel(dims, tiles_ref, rows_hbm, cols_hbm, count_hbm, src_hbm,
-                 send_ref, keep_ref, dense_ref,
-                 held, rows_ref, cols_ref, count_ref, src_ref, total, panel, prod, sems, small):
-    n_row, n_col, side = dims
-    slots = tiles_ref.shape[0]
-    n_rows = dense_ref.shape[0] // 2
-    pairs = ((src_hbm, src_ref), (count_hbm, count_ref), (rows_hbm, rows_ref), (cols_hbm, cols_ref))
+def start_copies(tiles_ref, held, sems, pairs, small):
     scalars = [pltpu.make_async_copy(a, b, small.at[i]) for i, (a, b) in enumerate(pairs)]
-    for copy in scalars:
-        copy.start()
     copies = []
-    for i in range(slots // CHUNK):
+    for i in range(held.shape[0] // CHUNK):
         part = pl.ds(i * CHUNK, CHUNK)
         copies.append(pltpu.make_async_copy(tiles_ref.at[part], held.at[part], sems.at[i]))
-    for copy in copies:
+    for copy in scalars + copies:
         copy.start()
+    return scalars, copies
+
+
+def sum_tiles(copies, held, rows_ref, cols_ref, count_ref, total, dense_ref):
+    side = held.shape[1]
+    n_rows = dense_ref.shape[0] // 2
+    count = count_ref[0]
+
+    def add_tile(k, carry):
+        live = k < count
+        row = pl.multiple_of(jnp.where(live, rows_ref[k] * side, n_rows), side)
+        col = pl.multiple_of(jnp.where(live, cols_ref[k] * side, 0), side)
+        spot = (pl.ds(row, side), pl.ds(col, side))
+        total[spot] += held[k].astype(jnp.float32)
+        return carry
+
+    for i, copy in enumerate(copies):
+        copy.wait()
+        lax.fori_loop(i * CHUNK, (i + 1) * CHUNK, add_tile, 0, unroll=4)
+    for r in range(0, n_rows, side):
+        whole = total[pl.ds(r, side), :]
+        high = whole.astype(jnp.bfloat16)
+        dense_ref[pl.ds(r, side), :] = high
+        dense_ref[pl.ds(n_rows + r, side), :] = (whole - high.astype(jnp.float32)).astype(jnp.bfloat16)
+
+
+def first_kernel(dims, tiles_ref, rows_hbm, cols_hbm, count_hbm, src_hbm, send_ref, keep_ref,
+                 held, rows_ref, cols_ref, count_ref, total, sems, small, src_ref, dense_ref, panel, prod):
+    n_row, n_col, side = dims
+    pairs = ((rows_hbm, rows_ref), (cols_hbm, cols_ref), (count_hbm, count_ref), (src_hbm, src_ref))
+    scalars, copies = start_copies(tiles_ref, held, sems, pairs, small)
     total[...] = jnp.zeros_like(total)
     for copy in scalars:
         copy.wait()
@@ -67,25 +91,21 @@
         first = H + (r * n_col + lax.axis_index("col")) * VB
         panel[pl.ds(r * VB, VB), :] = one_hot(first, VB, src).astype(jnp.bfloat16)
     panel[pl.ds(n_row * VB, H), :] = one_hot(0, H, src).astype(jnp.bfloat16)
-    count = count_ref[0]
-
-    def add_tile(k, carry):
-        live = k < count
-        row = pl.multiple_of(jnp.where(live, rows_ref[k] * side, n_rows), side)
-        col = pl.multiple_of(jnp.where(live, cols_ref[k] * side, 0), side)
-        spot = (pl.ds(row, side), pl.ds(col, side))
-        total[spot] += held[k].astype(jnp.float32)
-        return carry
-
-    for i, copy in enumerate(copies):
+    sum_tiles(copies, held, rows_ref, cols_ref, count_ref, total, dense_ref)
+    write_terms(dims, H // n_col, prod, dense_ref, panel, send_ref, keep_ref)
+
+
+def dense_kernel(tiles_ref, rows_hbm, cols_hbm, count_hbm, src_hbm, dense_ref, tele_ref,
+                 held, rows_ref, cols_ref, count_ref, total, sems, small, src_ref):
+    pairs = ((rows_hbm, rows_ref), (cols_hbm, cols_ref), (count_hbm, count_ref), (src_hbm, src_ref))
+    scalars, copies = start_copies(tiles_ref, held, sems, pairs, small)
+    total[...] = jnp.zeros_like(total)
+    for copy in scalars:
         copy.wait()
-        lax.fori_loop(i * CHUNK, (i + 1) * CHUNK, add_tile, 0, unroll=4)
-    for r in range(0, n_rows, side):
-        whole = total[pl.ds(r, side), :]
-        high = whole.astype(jnp.bfloat16)
-        dense_ref[pl.ds(r, side), :] = high
-        dense_ref[pl.ds(n_rows + r, side), :] = (whole - high.astype(jnp.float32)).astype(jnp.bfloat16)
-    write_terms(dims, H // n_col, prod, dense_ref, panel, send_ref, keep_ref)
+    quarter = tele_ref.shape[0]
+    first = (lax.axis_index("col") * X + lax.axis_index("row") % X) * quarter
+    tele_ref[...] = 0.15 * one_hot(first, quarter, src_ref[...])
+    sum_tiles(copies, held, rows_ref, cols_ref, count_ref, total, dense_ref)
 
 
 def second_kernel(dims, *refs):
@@ -143,12 +163,9 @@
     return summed
 
 
-def hub_kernel(dims, src_ref, *refs):
+def hub_kernel(tele_ref, *refs):
     planes, (out_ref, held) = refs[:-2], refs[-2:]
-    quarter = out_ref.shape[0]
-    first = (lax.axis_index("col") * X + lax.axis_index("row") % X) * quarter
-    tele = one_hot(first, quarter, src_ref[...])
-    out_ref[...] = (DAMP * sum_planes(planes, held) + 0.15 * tele).astype(out_ref.dtype)
+    out_ref[...] = (DAMP * sum_planes(planes, held) + tele_ref[...]).astype(out_ref.dtype)
 
 
 def side_kernel(mine_ref, theirs_ref, out_ref):
@@ -200,6 +217,7 @@
     bf16 = functools.partial(jax.ShapeDtypeStruct, dtype=jnp.bfloat16)
     src = sources.reshape(1, width)
     half = VB + n_row * piece
+    quarter = H // n_col // X
     product_scratch = [
         pltpu.VMEM((n_cols, width), jnp.bfloat16),
         pltpu.VMEM((n_rows, width), jnp.float32),
@@ -231,28 +249,40 @@
 
     bind = functools.partial
 
-    send, keep, dense = pl.pallas_call(
-        functools.partial(first_kernel, dims),
-        out_shape=(f32((half, width)), f32((half, width)), bf16((2 * n_rows, n_cols))),
+    sum_scratch = [
+        pltpu.VMEM((slots, side, side), jnp.bfloat16),
+        pltpu.SMEM((slots,), jnp.int32),
+        pltpu.SMEM((slots,), jnp.int32),
+        pltpu.SMEM((1,), jnp.int32),
+        pltpu.VMEM((n_rows + side, n_cols), jnp.float32),
+        pltpu.SemaphoreType.DMA((slots // CHUNK,)),
+        pltpu.SemaphoreType.DMA((4,)),
+    ]
+    slot_args = (tiles.reshape(slots, side, side), tile_row.reshape(slots), tile_col.reshape(slots),
+                 tile_count.reshape(1))
+    send, keep = pl.pallas_call(
+        bind(first_kernel, dims),
+        out_shape=(f32((half, width)), f32((half, width))),
         in_specs=[HBM] * 5,
-        out_specs=[VMEM] * 3,
-        scratch_shapes=[
-            pltpu.VMEM((slots, side, side), jnp.bfloat16),
-            pltpu.SMEM((slots,), jnp.int32),
-            pltpu.SMEM((slots,), jnp.int32),
-            pltpu.SMEM((1,), jnp.int32),
+        out_specs=[VMEM] * 2,
+        scratch_shapes=sum_scratch + [
             pltpu.VMEM((1, width), jnp.int32),
-            pltpu.VMEM((n_rows + side, n_cols), jnp.float32),
-        ] + product_scratch + [
-            pltpu.SemaphoreType.DMA((slots // CHUNK,)),
-            pltpu.SemaphoreType.DMA((4,)),
-        ],
+            pltpu.VMEM((2 * n_rows, n_cols), jnp.bfloat16),
+        ] + product_scratch,
+        compiler_params=pltpu.CompilerParams(vmem_limit_bytes=FIRST_VMEM_LIMIT),
+        name="first_terms",
+    )(*slot_args, src)
+    dense, tele = pl.pallas_call(
+        dense_kernel,
+        out_shape=(bf16((2 * n_rows, n_cols)), f32((quarter, width))),
+        in_specs=[HBM] * 5,
+        out_specs=[VMEM] * 2,
+        scratch_shapes=sum_scratch + [pltpu.VMEM((1, width), jnp.int32)],
         compiler_params=params(),
-        name="first_terms",
-    )(tiles.reshape(slots, side, side), tile_row.reshape(slots), tile_col.reshape(slots),
-      tile_count.reshape(1), src)
-
-    quarter = H // n_col // X
+        cost_estimate=pl.CostEstimate(flops=1 * MICRO, bytes_accessed=0, transcendentals=0),
+        name="sum_tiles",
+    )(*slot_args, src)
+
     n_z = n_row // X
     for step in range(ITERS - 1):
         came = other_core(send)
@@ -263,11 +293,11 @@
         away = other_side(away)
         far = along_z([own] * n_z)
         across = other_side(own)
-        plane = call(plane_kernel, "plane_sum", f32((quarter, width)), hold, away, cost=10)
+        plane = call(plane_kernel, "plane_sum", f32((quarter, width)), hold, away, cost=20)
         planes = [plane] + along_z([plane] * n_z)
         far_across = other_side(call(join_kernel, "join_far", bf16((n_z - 1, VB, width)), *far))
-        mine = call(bind(hub_kernel, dims), "hub_sums", bf16((quarter, width)), src, *planes,
-                    scratch=[pltpu.VMEM((n_z, quarter, width), jnp.float32)], cost=10)
+        mine = call(hub_kernel, "hub_sums", bf16((quarter, width)), tele, *planes,
+                    scratch=[pltpu.VMEM((n_z, quarter, width), jnp.float32)], cost=1)
         mine = call(side_kernel, "join_sides", bf16((H // n_col, width)), mine, other_side(mine))
         send, keep = call(
             bind(second_kernel, dims), "later_terms", (f32((half, width)), f32((half, width))),

time: 49.6 us -> 48.6 us (0.980)
  Pallas kernels: 5.09 us -> 8.77 us
  local copies, waits for them, and re-layouts: 3.88 us -> 0.97 us
  waiting for transfers between devices: 17.9 us -> 16 us
    pallas_call x1 -> x2, Pallas kernels: 2.62 us -> 6.29 us  [the longest x1 4.29 us: fast_body(): pl.pallas_call(bind(first_kernel, dims), out_shape=(f32((half, width)), f...]
    unnamed x10, local copies, waits for them, and re-layouts: 3.88 us -> 0.97 us
    ppermute x14, waiting for transfers between devices: 14.8 us -> 13.2 us  [to_partner(): return lax.ppermute(x, 'row', [(r, r ^ flip) for r in range(n_row)])]
  transfers between devices with their start and end apart: 17 -> 17, of which waited for: 9 -> 7; matrix products, arithmetic and copies ran while one was open for 0% -> 0% of each run, Pallas kernels for 2% -> 6%
where the time goes in v8:
time: 48.6 us; the launch traced here: 48.4 us
  starting transfers between devices  21.3 us (44%)
  waiting for transfers between devices  16 us (33%)
  Pallas kernels  8.77 us (18%)
  between operations  1.42 us (3%)
  local copies, waits for them, and re-layouts  0.97 us (2%)
    ppermute x14, starting transfers between devices, to_partner(): return lax.ppermute(x, 'row', [(r, r ^ flip) for r in range(n_row)])  20.5 us
    ppermute x14, waiting for transfers between devices, to_partner(): return lax.ppermute(x, 'row', [(r, r ^ flip) for r in range(n_row)])  13.2 us
    pallas_call x1, Pallas kernels, fast_body(): pl.pallas_call(bind(first_kernel, dims), out_shape=(f32((half, width)), f...  4.29 us
    ppermute x3, waiting for transfers between devices, other_core(): return lax.ppermute(x, 'col', [(0, 1), (1, 0)])  2.81 us
    pallas_call x10, Pallas kernels, call(): pl.pallas_call(kernel, out_shape=out_shape, in_specs=[VMEM] * len(args),...  2.48 us
    pallas_call x1, Pallas kernels, fast_body(): pl.pallas_call(dense_kernel, out_shape=(bf16((2 * n_rows, n_cols)), f32((...  2 us
  transfers between devices with their start and end apart: 17, of which 7 were waited for; matrix products, arithmetic and copies ran while one was open for 0% of the time, Pallas kernels for 6%

profile of v8, /device:TPU:0, one launch (start us, length us, event | category | flops | bytes accessed | tf_op | source)
XLA Modules:
  0.0 48.4 jit_solution(14733780409869125537)
XLA Ops:
  0.6 0.0 copy-start.2
  1.3 4.3 %first_terms.1 = (f32[256,256]{1,0:T(8,128)}, f32[256,256]{1,0:T(8,128)}) custom-call(bf16[96,128,128]{2,1,0:T(8,128)(2,1)} %bitcast.8, s32[96]{0:T(128)} %bitcast.15, s32[96]{0:T(128)} %bitcast.17, s32[1]{0:T(128)} %bitcast.6.count_hbm, s32[1,256]{1,0:T(1,128)} %bitcast.10), custom_call_target="tpu_custom_call" | custom-call | tf_op jit(solution)/shard_map/first_terms/pallas_call | solution.py:263
  5.6 0.5 %collective-permute-start = (f32[256,256]{1,0:T(8,128)}, f32[256,256]{1,0:T(8,128)S(1)}, u32[]{:S(2)}, u32[]{:S(2)}) collective-permute-start(f32[256,256]{1,0:T(8,128)} %get-tuple-element.18), channel_id=1, source_target_pairs={{0,1},{1,0},{2,3},{3,2},{4,5},{5,4},{6,7},{7,6},{8,9},{9,8},{10,11... | collective-permute-start | bytes 786440 | tf_op jit(solution)/shard_map/ppermute | solution.py:227
  6.1 1.4 %collective-permute-done.came_ref = f32[256,256]{1,0:T(8,128)S(1)} collective-permute-done((f32[256,256]{1,0:T(8,128)}, f32[256,256]{1,0:T(8,128)S(1)}, u32[]{:S(2)}, u32[]{:S(2)}) %collective-permute-start) | collective-permute-done | bytes 262176 | tf_op jit(solution)/shard_map/ppermute | solution.py:227
  7.5 0.0 copy-done.2
  7.5 0.0 copy-start.1
  7.5 0.9 %copy-done.1 = f32[256,256]{1,0:T(8,128)S(1)} copy-done((f32[256,256]{1,0:T(8,128)S(1)}, f32[256,256]{1,0:T(8,128)}, u32[]{:S(2)}) %copy-start.1) | copy-done | bytes 262168
  8.5 2.9 %collective-permute-start.6 = (f32[64,256]{1,0:T(8,128)S(1)}, f32[64,256]{1,0:T(8,128)S(1)}, u32[]{:S(2)}, u32[]{:S(2)}) collective-permute-start(f32[64,256]{1,0:T(8,128)S(1)} %get-tuple-element.22), channel_id=1, source_target_pairs={{0,2},{2,0},{4,6},{6,4},{8,10},{10,8},{12,14},{14,12},{1,3},{3,1},... | collective-permute-start | bytes 196616 | tf_op jit(solution)/shard_map/ppermute | solution.py:230
  11.4 3.6 %collective-permute-start.3 = (bf16[128,256]{1,0:T(8,128)(2,1)S(1)}, bf16[128,256]{1,0:T(8,128)(2,1)S(1)}, u32[]{:S(2)}, u32[]{:S(2)}) collective-permute-start(bf16[128,256]{1,0:T(8,128)(2,1)S(1)} %get-tuple-element.19.refs_0_), channel_id=1, source_target_pairs={{0,12},{2,14},{4,8},{6,10},{8,4},{10,6},{12,0},{14,2},{1,13},{3,15... | collective-permute-start | bytes 196616 | tf_op jit(solution)/shard_map/ppermute | solution.py:230
  15.0 0.0 collective-permute-start.2
  15.0 0.8 %collective-permute-start.1 = (bf16[128,256]{1,0:T(8,128)(2,1)S(1)}, bf16[128,256]{1,0:T(8,128)(2,1)S(1)}, u32[]{:S(2)}, u32[]{:S(2)}) collective-permute-start(bf16[128,256]{1,0:T(8,128)(2,1)S(1)} %get-tuple-element.19.refs_0_), channel_id=1, source_target_pairs={{0,4},{2,6},{4,0},{6,2},{8,12},{10,14},{12,8},{14,10},{1,5},{3,7},... | collective-permute-start | bytes 196616 | tf_op jit(solution)/shard_map/ppermute | solution.py:230
  15.8 0.0 collective-permute-done.6.came_ref
  15.8 0.0 copy-start
  15.8 3.7 %collective-permute-start.9 = (f32[64,256]{1,0:T(8,128)S(1)}, f32[64,256]{1,0:T(8,128)S(1)}, u32[]{:S(2)}, u32[]{:S(2)}) collective-permute-start(f32[64,256]{1,0:T(8,128)S(1)} %plane_sum.1.refs_0_), channel_id=1, source_target_pairs={{0,12},{2,14},{4,8},{6,10},{8,4},{10,6},{12,0},{14,2},{1,13},{3,15... | collective-permute-start | bytes 196616 | tf_op jit(solution)/shard_map/ppermute | solution.py:230
  19.5 0.0 collective-permute-start.8
  19.5 0.0 collective-permute-done.3.refs_2_.refs_3_
  19.5 0.8 %collective-permute-start.7 = (f32[64,256]{1,0:T(8,128)S(1)}, f32[64,256]{1,0:T(8,128)S(1)}, u32[]{:S(2)}, u32[]{:S(2)}) collective-permute-start(f32[64,256]{1,0:T(8,128)S(1)} %plane_sum.1.refs_0_), channel_id=1, source_target_pairs={{0,4},{2,6},{4,0},{6,2},{8,12},{10,14},{12,8},{14,10},{1,5},{3,7},... | collective-permute-start | bytes 196616 | tf_op jit(solution)/shard_map/ppermute | solution.py:230
  20.3 3.0 %collective-permute-done.2.refs_1_.refs_2_ = bf16[128,256]{1,0:T(8,128)(2,1)S(1)} collective-permute-done((bf16[128,256]{1,0:T(8,128)(2,1)S(1)}, bf16[128,256]{1,0:T(8,128)(2,1)S(1)}, u32[]{:S(2)}, u32[]{:S(2)}) %collective-permute-start.2) | collective-permute-done | bytes 65568 | tf_op jit(solution)/shard_map/ppermute | solution.py:230
  23.3 0.0 collective-permute-done.1.refs_0_.refs_1_
  23.3 1.0 %collective-permute-start.5 = (bf16[3,128,256]{2,1,0:T(8,128)(2,1)S(1)}, bf16[3,128,256]{2,1,0:T(8,128)(2,1)S(1)}, u32[]{:S(2)}, u32[]{:S(2)}) collective-permute-start(bf16[3,128,256]{2,1,0:T(8,128)(2,1)S(1)} %join_far.1), channel_id=1, source_target_pairs={{0,2},{2,0},{4,6},{6,4},{8,10},{10,8},{12,14},{14,12},{1,3},{3,1},... | collective-permute-start | bytes 589832 | tf_op jit(solution)/shard_map/ppermute | solution.py:230
  24.3 0.0 copy-done
  24.3 0.0 copy-done.3
  24.3 0.0 copy-done.4
  24.3 2.0 %sum_tiles.1 = (bf16[1024,1280]{1,0:T(8,128)(2,1)S(1)}, f32[64,256]{1,0:T(8,128)S(1)}) custom-call(bf16[96,128,128]{2,1,0:T(8,128)(2,1)S(1)} %bitcast.9, s32[96]{0:T(128)S(1)} %bitcast.16, s32[96]{0:T(128)S(1)} %bitcast.18, s32[1]{0:T(128)} %bitcast.7.count_hbm, s32[1,256]{1,0:T(1,128)S(1)} %bitcast.12), custom_call_target="tpu_custom_call" | custom-call | flops 1000000000 | tf_op jit(solution)/shard_map/sum_tiles/pallas_call | solution.py:275
  26.4 0.0 collective-permute-done.9.refs_3_
  26.4 0.0 collective-permute-done.8.refs_2_
  26.4 0.0 collective-permute-done.7.refs_1_
  26.4 0.1 hub_sums.1.mine_ref
  26.4 1.1 %collective-permute-start.10 = (bf16[64,256]{1,0:T(8,128)(2,1)S(1)}, bf16[64,256]{1,0:T(8,128)(2,1)S(1)}, u32[]{:S(2)}, u32[]{:S(2)}) collective-permute-start(bf16[64,256]{1,0:T(8,128)(2,1)S(1)} %hub_sums.1.mine_ref), channel_id=1, source_target_pairs={{0,2},{2,0},{4,6},{6,4},{8,10},{10,8},{12,14},{14,12},{1,3},{3,1},... | collective-permute-start | bytes 98312 | tf_op jit(solution)/shard_map/ppermute | solution.py:230
  27.6 0.9 %collective-permute-start.4 = (bf16[128,256]{1,0:T(8,128)(2,1)S(1)}, bf16[128,256]{1,0:T(8,128)(2,1)S(1)}, u32[]{:S(2)}, u32[]{:S(2)}) collective-permute-start(bf16[128,256]{1,0:T(8,128)(2,1)S(1)} %get-tuple-element.19.refs_0_), channel_id=1, source_target_pairs={{0,2},{2,0},{4,6},{6,4},{8,10},{10,8},{12,14},{14,12},{1,3},{3,1},... | collective-permute-start | bytes 196616 | tf_op jit(solution)/shard_map/ppermute | solution.py:230
  28.5 1.9 %collective-permute-done.10.theirs_ref = bf16[64,256]{1,0:T(8,128)(2,1)S(1)} collective-permute-done((bf16[64,256]{1,0:T(8,128)(2,1)S(1)}, bf16[64,256]{1,0:T(8,128)(2,1)S(1)}, u32[]{:S(2)}, u32[]{:S(2)}) %collective-permute-start.10) | collective-permute-done | bytes 32800 | tf_op jit(solution)/shard_map/ppermute | solution.py:230
  30.5 0.1 collective-permute-start.11
  30.6 1.3 %collective-permute-done.4.refs_4_ = bf16[128,256]{1,0:T(8,128)(2,1)S(1)} collective-permute-done((bf16[128,256]{1,0:T(8,128)(2,1)S(1)}, bf16[128,256]{1,0:T(8,128)(2,1)S(1)}, u32[]{:S(2)}, u32[]{:S(2)}) %collective-permute-start.4) | collective-permute-done | bytes 65568 | tf_op jit(solution)/shard_map/ppermute | solution.py:230
  31.9 0.0 collective-permute-done.11.refs_7_
  31.9 0.0 collective-permute-done.5.refs_5_
  31.9 1.0 %later_terms.1 = (f32[256,256]{1,0:T(8,128)S(1)}, f32[256,256]{1,0:T(8,128)S(1)}) custom-call(bf16[128,256]{1,0:T(8,128)(2,1)S(1)} %get-tuple-element.19.refs_0_, bf16[128,256]{1,0:T(8,128)(2,1)S(1)} %collective-permute-done.1.refs_0_.refs_1_, bf16[128,256]{1,0:T(8,128)(2,1)S(1)} %collective-permute-done.2.refs_1_.refs_2_, ...), custom_call_target="tpu_custom_call" | custom-call | tf_op jit(solution)/shard_map/later_terms/pallas_call | solution.py:239
  32.9 0.2 collective-permute-start.12
  33.0 1.4 %collective-permute-done.12.came_ref = f32[256,256]{1,0:T(8,128)S(1)} collective-permute-done((f32[256,256]{1,0:T(8,128)S(1)}, f32[256,256]{1,0:T(8,128)S(1)}, u32[]{:S(2)}, u32[]{:S(2)}) %collective-permute-start.12) | collective-permute-done | bytes 262176 | tf_op jit(solution)/shard_map/ppermute | solution.py:227
  34.5 1.2 %collective-permute-start.13 = (f32[64,256]{1,0:T(8,128)S(1)}, f32[64,256]{1,0:T(8,128)S(1)}, u32[]{:S(2)}, u32[]{:S(2)}) collective-permute-start(f32[64,256]{1,0:T(8,128)S(1)} %get-tuple-element.27), channel_id=1, source_target_pairs={{0,2},{2,0},{4,6},{6,4},{8,10},{10,8},{12,14},{14,12},{1,3},{3,1},... | collective-permute-start | bytes 196616 | tf_op jit(solution)/shard_map/ppermute | solution.py:230
  35.7 3.1 %collective-permute-done.13.came_ref = f32[64,256]{1,0:T(8,128)S(1)} collective-permute-done((f32[64,256]{1,0:T(8,128)S(1)}, f32[64,256]{1,0:T(8,128)S(1)}, u32[]{:S(2)}, u32[]{:S(2)}) %collective-permute-start.13) | collective-permute-done | bytes 65568 | tf_op jit(solution)/shard_map/ppermute | solution.py:230
  38.8 0.1 collective-permute-start.14
  38.9 3.3 %collective-permute-start.15 = (f32[16,256]{1,0:T(8,128)S(1)}, f32[16,256]{1,0:T(8,128)S(1)}, u32[]{:S(2)}, u32[]{:S(2)}) collective-permute-start(f32[16,256]{1,0:T(8,128)S(1)} %get-tuple-element.30), channel_id=1, source_target_pairs={{0,8},{2,10},{4,12},{6,14},{8,0},{10,2},{12,4},{14,6},{1,9},{3,11}... | collective-permute-start | bytes 49160 | tf_op jit(solution)/shard_map/ppermute | solution.py:230
  42.3 1.0 %collective-permute-start.16 = (f32[16,256]{1,0:T(8,128)S(1)}, f32[16,256]{1,0:T(8,128)S(1)}, u32[]{:S(2)}, u32[]{:S(2)}) collective-permute-start(f32[16,256]{1,0:T(8,128)S(1)} %get-tuple-element.31), channel_id=1, source_target_pairs={{0,12},{2,14},{4,8},{6,10},{8,4},{10,6},{12,0},{14,2},{1,13},{3,15... | collective-permute-start | bytes 49160 | tf_op jit(solution)/shard_map/ppermute | solution.py:230
  43.3 0.7 %last_scores.1 = f32[128,256]{1,0:T(8,128)} custom-call(s32[1,256]{1,0:T(1,128)S(1)} %bitcast.13, f32[256,256]{1,0:T(8,128)S(1)} %get-tuple-element.24.keep_ref, f32[256,256]{1,0:T(8,128)S(1)} %collective-permute-done.12.came_ref), custom_call_target="tpu_custom_call" | custom-call | tf_op jit(solution)/shard_map/last_scores/pallas_call | solution.py:239
  44.0 0.0 collective-permute-done.14.refs_1_
  44.0 0.0 collective-permute-done.15.refs_2_
  44.0 3.8 %collective-permute-done.16.refs_3_ = f32[16,256]{1,0:T(8,128)S(1)} collective-permute-done((f32[16,256]{1,0:T(8,128)S(1)}, f32[16,256]{1,0:T(8,128)S(1)}, u32[]{:S(2)}, u32[]{:S(2)}) %collective-permute-start.16) | collective-permute-done | bytes 16416 | tf_op jit(solution)/shard_map/ppermute | solution.py:230
  47.8 0.6 %last_hubs.1 = f32[16,256]{1,0:T(8,128)} custom-call(s32[1,256]{1,0:T(1,128)S(1)} %bitcast.14, f32[16,256]{1,0:T(8,128)S(1)} %get-tuple-element.28.refs_0_, f32[16,256]{1,0:T(8,128)S(1)} %collective-permute-done.14.refs_1_, f32[16,256]{1,0:T(8,128)S(1)} %collective-permute-done.15.refs_2_, f32[16,256]{1,0:T(8,128)S(1)} %collective-permute-done.16.refs_3_), custom_call_target="tpu_custom_call" | custom-call | tf_op jit(solution)/shard_map/last_hubs/pallas_call | solution.py:239
  (8 shorter events, 0.1 us)
Async XLA Ops:
  0.6 6.9 %copy-start.2 = (s32[256]{0:T(256)S(1)}, s32[256]{0:T(256)}, u32[]{:S(2)}) copy-start(s32[256]{0:T(256)} %param.9) | copy-start | bytes 3076
  5.6 1.9 %collective-permute-start = (f32[256,256]{1,0:T(8,128)}, f32[256,256]{1,0:T(8,128)S(1)}, u32[]{:S(2)}, u32[]{:S(2)}) collective-permute-start(f32[256,256]{1,0:T(8,128)} %get-tuple-element.18), channel_id=1, source_target_pairs={{0,1},{1,0},{2,3},{3,2},{4,5},{5,4},{6,7},{7,6},{8,9},{9,8},{10,11... | collective-permute-start | bytes 786440 | tf_op jit(solution)/shard_map/ppermute | solution.py:227
  7.5 1.0 %copy-start.1 = (f32[256,256]{1,0:T(8,128)S(1)}, f32[256,256]{1,0:T(8,128)}, u32[]{:S(2)}) copy-start(f32[256,256]{1,0:T(8,128)} %get-tuple-element.17.keep_ref) | copy-start | bytes 786436
  8.5 7.3 %collective-permute-start.6 = (f32[64,256]{1,0:T(8,128)S(1)}, f32[64,256]{1,0:T(8,128)S(1)}, u32[]{:S(2)}, u32[]{:S(2)}) collective-permute-start(f32[64,256]{1,0:T(8,128)S(1)} %get-tuple-element.22), channel_id=1, source_target_pairs={{0,2},{2,0},{4,6},{6,4},{8,10},{10,8},{12,14},{14,12},{1,3},{3,1},... | collective-permute-start | bytes 196616 | tf_op jit(solution)/shard_map/ppermute | solution.py:230
  11.4 8.1 %collective-permute-start.3 = (bf16[128,256]{1,0:T(8,128)(2,1)S(1)}, bf16[128,256]{1,0:T(8,128)(2,1)S(1)}, u32[]{:S(2)}, u32[]{:S(2)}) collective-permute-start(bf16[128,256]{1,0:T(8,128)(2,1)S(1)} %get-tuple-element.19.refs_0_), channel_id=1, source_target_pairs={{0,12},{2,14},{4,8},{6,10},{8,4},{10,6},{12,0},{14,2},{1,13},{3,15... | collective-permute-start | bytes 196616 | tf_op jit(solution)/shard_map/ppermute | solution.py:230
  15.0 8.3 %collective-permute-start.2 = (bf16[128,256]{1,0:T(8,128)(2,1)S(1)}, bf16[128,256]{1,0:T(8,128)(2,1)S(1)}, u32[]{:S(2)}, u32[]{:S(2)}) collective-permute-start(bf16[128,256]{1,0:T(8,128)(2,1)S(1)} %get-tuple-element.19.refs_0_), channel_id=1, source_target_pairs={{0,8},{2,10},{4,12},{6,14},{8,0},{10,2},{12,4},{14,6},{1,9},{3,11}... | collective-permute-start | bytes 196616 | tf_op jit(solution)/shard_map/ppermute | solution.py:230
  15.0 8.3 %collective-permute-start.1 = (bf16[128,256]{1,0:T(8,128)(2,1)S(1)}, bf16[128,256]{1,0:T(8,128)(2,1)S(1)}, u32[]{:S(2)}, u32[]{:S(2)}) collective-permute-start(bf16[128,256]{1,0:T(8,128)(2,1)S(1)} %get-tuple-element.19.refs_0_), channel_id=1, source_target_pairs={{0,4},{2,6},{4,0},{6,2},{8,12},{10,14},{12,8},{14,10},{1,5},{3,7},... | collective-permute-start | bytes 196616 | tf_op jit(solution)/shard_map/ppermute | solution.py:230
  15.8 8.5 %copy-start = (bf16[1,1,96,128,128]{4,3,2,1,0:T(8,128)(2,1)S(1)}, bf16[1,1,96,128,128]{4,3,2,1,0:T(8,128)(2,1)}, u32[]{:S(2)}) copy-start(bf16[1,1,96,128,128]{4,3,2,1,0:T(8,128)(2,1)} %param.5) | copy-start | bytes 9437188
  15.8 8.5 %copy-start.3 = (s32[1,1,96]{2,1,0:T(1,128)S(1)}, s32[1,1,96]{2,1,0:T(1,128)}, u32[]{:S(2)}) copy-start(s32[1,1,96]{2,1,0:T(1,128)} %param.6) | copy-start | bytes 1156
  15.8 8.5 %copy-start.4 = (s32[1,1,96]{2,1,0:T(1,128)S(1)}, s32[1,1,96]{2,1,0:T(1,128)}, u32[]{:S(2)}) copy-start(s32[1,1,96]{2,1,0:T(1,128)} %param.7) | copy-start | bytes 1156
  15.8 10.5 %collective-permute-start.9 = (f32[64,256]{1,0:T(8,128)S(1)}, f32[64,256]{1,0:T(8,128)S(1)}, u32[]{:S(2)}, u32[]{:S(2)}) collective-permute-start(f32[64,256]{1,0:T(8,128)S(1)} %plane_sum.1.refs_0_), channel_id=1, source_target_pairs={{0,12},{2,14},{4,8},{6,10},{8,4},{10,6},{12,0},{14,2},{1,13},{3,15... | collective-permute-start | bytes 196616 | tf_op jit(solution)/shard_map/ppermute | solution.py:230
  19.5 6.9 %collective-permute-start.8 = (f32[64,256]{1,0:T(8,128)S(1)}, f32[64,256]{1,0:T(8,128)S(1)}, u32[]{:S(2)}, u32[]{:S(2)}) collective-permute-start(f32[64,256]{1,0:T(8,128)S(1)} %plane_sum.1.refs_0_), channel_id=1, source_target_pairs={{0,8},{2,10},{4,12},{6,14},{8,0},{10,2},{12,4},{14,6},{1,9},{3,11}... | collective-permute-start | bytes 196616 | tf_op jit(solution)/shard_map/ppermute | solution.py:230
  19.5 6.9 %collective-permute-start.7 = (f32[64,256]{1,0:T(8,128)S(1)}, f32[64,256]{1,0:T(8,128)S(1)}, u32[]{:S(2)}, u32[]{:S(2)}) collective-permute-start(f32[64,256]{1,0:T(8,128)S(1)} %plane_sum.1.refs_0_), channel_id=1, source_target_pairs={{0,4},{2,6},{4,0},{6,2},{8,12},{10,14},{12,8},{14,10},{1,5},{3,7},... | collective-permute-start | bytes 196616 | tf_op jit(solution)/shard_map/ppermute | solution.py:230
  23.3 8.5 %collective-permute-start.5 = (bf16[3,128,256]{2,1,0:T(8,128)(2,1)S(1)}, bf16[3,128,256]{2,1,0:T(8,128)(2,1)S(1)}, u32[]{:S(2)}, u32[]{:S(2)}) collective-permute-start(bf16[3,128,256]{2,1,0:T(8,128)(2,1)S(1)} %join_far.1), channel_id=1, source_target_pairs={{0,2},{2,0},{4,6},{6,4},{8,10},{10,8},{12,14},{14,12},{1,3},{3,1},... | collective-permute-start | bytes 589832 | tf_op jit(solution)/shard_map/ppermute | solution.py:230
  26.4 4.0 %collective-permute-start.10 = (bf16[64,256]{1,0:T(8,128)(2,1)S(1)}, bf16[64,256]{1,0:T(8,128)(2,1)S(1)}, u32[]{:S(2)}, u32[]{:S(2)}) collective-permute-start(bf16[64,256]{1,0:T(8,128)(2,1)S(1)} %hub_sums.1.mine_ref), channel_id=1, source_target_pairs={{0,2},{2,0},{4,6},{6,4},{8,10},{10,8},{12,14},{14,12},{1,3},{3,1},... | collective-permute-start | bytes 98312 | tf_op jit(solution)/shard_map/ppermute | solution.py:230
  27.6 4.3 %collective-permute-start.4 = (bf16[128,256]{1,0:T(8,128)(2,1)S(1)}, bf16[128,256]{1,0:T(8,128)(2,1)S(1)}, u32[]{:S(2)}, u32[]{:S(2)}) collective-permute-start(bf16[128,256]{1,0:T(8,128)(2,1)S(1)} %get-tuple-element.19.refs_0_), channel_id=1, source_target_pairs={{0,2},{2,0},{4,6},{6,4},{8,10},{10,8},{12,14},{14,12},{1,3},{3,1},... | collective-permute-start | bytes 196616 | tf_op jit(solution)/shard_map/ppermute | solution.py:230
  30.5 1.4 %collective-permute-start.11 = (bf16[128,256]{1,0:T(8,128)(2,1)S(1)}, bf16[128,256]{1,0:T(8,128)(2,1)S(1)}, u32[]{:S(2)}, u32[]{:S(2)}) collective-permute-start(bf16[128,256]{1,0:T(8,128)(2,1)S(1)} %join_sides.1.refs_6_), channel_id=1, source_target_pairs={{0,1},{1,0},{2,3},{3,2},{4,5},{5,4},{6,7},{7,6},{8,9},{9,8},{10,11... | collective-permute-start | bytes 196616 | tf_op jit(solution)/shard_map/ppermute | solution.py:227
  32.9 1.6 %collective-permute-start.12 = (f32[256,256]{1,0:T(8,128)S(1)}, f32[256,256]{1,0:T(8,128)S(1)}, u32[]{:S(2)}, u32[]{:S(2)}) collective-permute-start(f32[256,256]{1,0:T(8,128)S(1)} %get-tuple-element.25), channel_id=1, source_target_pairs={{0,1},{1,0},{2,3},{3,2},{4,5},{5,4},{6,7},{7,6},{8,9},{9,8},{10,11... | collective-permute-start | bytes 786440 | tf_op jit(solution)/shard_map/ppermute | solution.py:227
  34.5 4.3 %collective-permute-start.13 = (f32[64,256]{1,0:T(8,128)S(1)}, f32[64,256]{1,0:T(8,128)S(1)}, u32[]{:S(2)}, u32[]{:S(2)}) collective-permute-start(f32[64,256]{1,0:T(8,128)S(1)} %get-tuple-element.27), channel_id=1, source_target_pairs={{0,2},{2,0},{4,6},{6,4},{8,10},{10,8},{12,14},{14,12},{1,3},{3,1},... | collective-permute-start | bytes 196616 | tf_op jit(solution)/shard_map/ppermute | solution.py:230
  38.8 5.2 %collective-permute-start.14 = (f32[16,256]{1,0:T(8,128)S(1)}, f32[16,256]{1,0:T(8,128)S(1)}, u32[]{:S(2)}, u32[]{:S(2)}) collective-permute-start(f32[16,256]{1,0:T(8,128)S(1)} %get-tuple-element.29), channel_id=1, source_target_pairs={{0,4},{2,6},{4,0},{6,2},{8,12},{10,14},{12,8},{14,10},{1,5},{3,7},... | collective-permute-start | bytes 49160 | tf_op jit(solution)/shard_map/ppermute | solution.py:230
  38.9 5.1 %collective-permute-start.15 = (f32[16,256]{1,0:T(8,128)S(1)}, f32[16,256]{1,0:T(8,128)S(1)}, u32[]{:S(2)}, u32[]{:S(2)}) collective-permute-start(f32[16,256]{1,0:T(8,128)S(1)} %get-tuple-element.30), channel_id=1, source_target_pairs={{0,8},{2,10},{4,12},{6,14},{8,0},{10,2},{12,4},{14,6},{1,9},{3,11}... | collective-permute-start | bytes 49160 | tf_op jit(solution)/shard_map/ppermute | solution.py:230
  42.3 5.5 %collective-permute-start.16 = (f32[16,256]{1,0:T(8,128)S(1)}, f32[16,256]{1,0:T(8,128)S(1)}, u32[]{:S(2)}, u32[]{:S(2)}) collective-permute-start(f32[16,256]{1,0:T(8,128)S(1)} %get-tuple-element.31), channel_id=1, source_target_pairs={{0,12},{2,14},{4,8},{6,10},{8,4},{10,6},{12,0},{14,2},{1,13},{3,15... | collective-permute-start | bytes 49160 | tf_op jit(solution)/shard_map/ppermute | solution.py:230

commit v9 on v7

--- a/solution.py
+++ b/solution.py
@@ -43,21 +43,17 @@
             ref[VB + k * block:VB + (k + 1) * block] = prod_ref[pl.ds(pl.multiple_of(start, block), block), :]
 
 
-def first_kernel(dims, tiles_ref, rows_hbm, cols_hbm, count_hbm, src_hbm,
-                 send_ref, keep_ref, dense_ref,
+def first_kernel(dims, tiles_ref, rows_hbm, cols_hbm, count_hbm, src_hbm, send_ref, keep_ref, dense_ref,
                  held, rows_ref, cols_ref, count_ref, src_ref, total, panel, prod, sems, small):
     n_row, n_col, side = dims
-    slots = tiles_ref.shape[0]
     n_rows = dense_ref.shape[0] // 2
-    pairs = ((src_hbm, src_ref), (count_hbm, count_ref), (rows_hbm, rows_ref), (cols_hbm, cols_ref))
+    pairs = ((src_hbm, src_ref), (rows_hbm, rows_ref), (cols_hbm, cols_ref), (count_hbm, count_ref))
     scalars = [pltpu.make_async_copy(a, b, small.at[i]) for i, (a, b) in enumerate(pairs)]
-    for copy in scalars:
-        copy.start()
     copies = []
-    for i in range(slots // CHUNK):
+    for i in range(held.shape[0] // CHUNK):
         part = pl.ds(i * CHUNK, CHUNK)
         copies.append(pltpu.make_async_copy(tiles_ref.at[part], held.at[part], sems.at[i]))
-    for copy in copies:
+    for copy in scalars + copies:
         copy.start()
     total[...] = jnp.zeros_like(total)
     for copy in scalars:
@@ -200,6 +196,7 @@
     bf16 = functools.partial(jax.ShapeDtypeStruct, dtype=jnp.bfloat16)
     src = sources.reshape(1, width)
     half = VB + n_row * piece
+    quarter = H // n_col // X
     product_scratch = [
         pltpu.VMEM((n_cols, width), jnp.bfloat16),
         pltpu.VMEM((n_rows, width), jnp.float32),
@@ -231,8 +228,10 @@
 
     bind = functools.partial
 
+    in_hbm = [pltpu.with_memory_space_constraint(x, pltpu.HBM) for x in (
+        tiles.reshape(slots, side, side), tile_row.reshape(slots), tile_col.reshape(slots), src)]
     send, keep, dense = pl.pallas_call(
-        functools.partial(first_kernel, dims),
+        bind(first_kernel, dims),
         out_shape=(f32((half, width)), f32((half, width)), bf16((2 * n_rows, n_cols))),
         in_specs=[HBM] * 5,
         out_specs=[VMEM] * 3,
@@ -249,10 +248,8 @@
         ],
         compiler_params=params(),
         name="first_terms",
-    )(tiles.reshape(slots, side, side), tile_row.reshape(slots), tile_col.reshape(slots),
-      tile_count.reshape(1), src)
-
-    quarter = H // n_col // X
+    )(*in_hbm[:3], tile_count.reshape(1), in_hbm[3])
+
     n_z = n_row // X
     for step in range(ITERS - 1):
         came = other_core(send)
@@ -263,11 +260,11 @@
         away = other_side(away)
         far = along_z([own] * n_z)
         across = other_side(own)
-        plane = call(plane_kernel, "plane_sum", f32((quarter, width)), hold, away, cost=10)
+        plane = call(plane_kernel, "plane_sum", f32((quarter, width)), hold, away, cost=20)
         planes = [plane] + along_z([plane] * n_z)
         far_across = other_side(call(join_kernel, "join_far", bf16((n_z - 1, VB, width)), *far))
         mine = call(bind(hub_kernel, dims), "hub_sums", bf16((quarter, width)), src, *planes,
-                    scratch=[pltpu.VMEM((n_z, quarter, width), jnp.float32)], cost=10)
+                    scratch=[pltpu.VMEM((n_z, quarter, width), jnp.float32)], cost=1)
         mine = call(side_kernel, "join_sides", bf16((H // n_col, width)), mine, other_side(mine))
         send, keep = call(
             bind(second_kernel, dims), "later_terms", (f32((half, width)), f32((half, width))),

time: 49.6 us -> 46.4 us (0.935)
  local copies, waits for them, and re-layouts: 3.88 us -> 0.01 us
  Pallas kernels: 5.09 us -> 5.86 us
    unnamed x10 -> x2, local copies, waits for them, and re-layouts: 3.88 us -> 0.01 us
    pallas_call x1, Pallas kernels: 2.62 us -> 3.4 us  [fast_body(): pl.pallas_call(bind(first_kernel, dims), out_shape=(f32((half, width)), f...]
where the time goes in v9:
time: 46.4 us; the launch traced here: 46.3 us
  starting transfers between devices  21.1 us (45%)
  waiting for transfers between devices  18 us (39%)
  Pallas kernels  5.86 us (13%)
  between operations  1.37 us (3%)
    ppermute x14, starting transfers between devices, to_partner(): return lax.ppermute(x, 'row', [(r, r ^ flip) for r in range(n_row)])  20.3 us
    ppermute x14, waiting for transfers between devices, to_partner(): return lax.ppermute(x, 'row', [(r, r ^ flip) for r in range(n_row)])  14.8 us
    pallas_call x1, Pallas kernels, fast_body(): pl.pallas_call(bind(first_kernel, dims), out_shape=(f32((half, width)), f...  3.4 us
    ppermute x3, waiting for transfers between devices, other_core(): return lax.ppermute(x, 'col', [(0, 1), (1, 0)])  3.13 us
    pallas_call x10, Pallas kernels, call(): pl.pallas_call(kernel, out_shape=out_shape, in_specs=[VMEM] * len(args),...  2.46 us
  transfers between devices with their start and end apart: 17, of which 9 were waited for; matrix products, arithmetic and copies ran while one was open for 0% of the time, Pallas kernels for 2%

profile of v9, /device:TPU:0, one launch (start us, length us, event | category | flops | bytes accessed | tf_op | source)
XLA Modules:
  0.0 46.3 jit_solution(5217313110564636980)
XLA Ops:
  0.6 0.0 copy-start
  1.3 3.4 %first_terms.1 = (f32[256,256]{1,0:T(8,128)S(1)}, f32[256,256]{1,0:T(8,128)S(1)}, bf16[1024,1280]{1,0:T(8,128)(2,1)S(1)}) custom-call(bf16[96,128,128]{2,1,0:T(8,128)(2,1)} %bitcast.12, s32[96]{0:T(128)} %bitcast.14, s32[96]{0:T(128)} %bitcast.15, s32[1]{0:T(128)} %bitcast.6.count_hbm, s32[1,256]{1,0:T(1,128)} %bitcast.7), custom_call_target="tpu_custom_call" | custom-call | tf_op jit(solution)/shard_map/first_terms/pallas_call | solution.py:233
  4.7 0.5 %collective-permute-start = (f32[256,256]{1,0:T(8,128)S(1)}, f32[256,256]{1,0:T(8,128)S(1)}, u32[]{:S(2)}, u32[]{:S(2)}) collective-permute-start(f32[256,256]{1,0:T(8,128)S(1)} %get-tuple-element.17), channel_id=1, source_target_pairs={{0,1},{1,0},{2,3},{3,2},{4,5},{5,4},{6,7},{7,6},{8,9},{9,8},{10,11... | collective-permute-start | bytes 786440 | tf_op jit(solution)/shard_map/ppermute | solution.py:206
  5.2 1.2 %collective-permute-done.came_ref = f32[256,256]{1,0:T(8,128)S(1)} collective-permute-done((f32[256,256]{1,0:T(8,128)S(1)}, f32[256,256]{1,0:T(8,128)S(1)}, u32[]{:S(2)}, u32[]{:S(2)}) %collective-permute-start) | collective-permute-done | bytes 262176 | tf_op jit(solution)/shard_map/ppermute | solution.py:206
  6.4 0.0 copy-done
  6.4 2.9 %collective-permute-start.6 = (f32[64,256]{1,0:T(8,128)S(1)}, f32[64,256]{1,0:T(8,128)S(1)}, u32[]{:S(2)}, u32[]{:S(2)}) collective-permute-start(f32[64,256]{1,0:T(8,128)S(1)} %get-tuple-element.20), channel_id=1, source_target_pairs={{0,2},{2,0},{4,6},{6,4},{8,10},{10,8},{12,14},{14,12},{1,3},{3,1},... | collective-permute-start | bytes 196616 | tf_op jit(solution)/shard_map/ppermute | solution.py:209
  9.4 3.6 %collective-permute-start.3 = (bf16[128,256]{1,0:T(8,128)(2,1)S(1)}, bf16[128,256]{1,0:T(8,128)(2,1)S(1)}, u32[]{:S(2)}, u32[]{:S(2)}) collective-permute-start(bf16[128,256]{1,0:T(8,128)(2,1)S(1)} %get-tuple-element.18.refs_0_), channel_id=1, source_target_pairs={{0,12},{2,14},{4,8},{6,10},{8,4},{10,6},{12,0},{14,2},{1,13},{3,15... | collective-permute-start | bytes 196616 | tf_op jit(solution)/shard_map/ppermute | solution.py:209
  13.0 0.0 collective-permute-start.2
  13.0 0.8 %collective-permute-start.1 = (bf16[128,256]{1,0:T(8,128)(2,1)S(1)}, bf16[128,256]{1,0:T(8,128)(2,1)S(1)}, u32[]{:S(2)}, u32[]{:S(2)}) collective-permute-start(bf16[128,256]{1,0:T(8,128)(2,1)S(1)} %get-tuple-element.18.refs_0_), channel_id=1, source_target_pairs={{0,4},{2,6},{4,0},{6,2},{8,12},{10,14},{12,8},{14,10},{1,5},{3,7},... | collective-permute-start | bytes 196616 | tf_op jit(solution)/shard_map/ppermute | solution.py:209
  13.8 0.0 collective-permute-done.6.came_ref
  13.8 3.7 %collective-permute-start.9 = (f32[64,256]{1,0:T(8,128)S(1)}, f32[64,256]{1,0:T(8,128)S(1)}, u32[]{:S(2)}, u32[]{:S(2)}) collective-permute-start(f32[64,256]{1,0:T(8,128)S(1)} %plane_sum.1.refs_0_), channel_id=1, source_target_pairs={{0,12},{2,14},{4,8},{6,10},{8,4},{10,6},{12,0},{14,2},{1,13},{3,15... | collective-permute-start | bytes 196616 | tf_op jit(solution)/shard_map/ppermute | solution.py:209
  17.4 0.0 collective-permute-start.8
  17.4 0.0 collective-permute-done.3.refs_2_.refs_3_
  17.4 0.8 %collective-permute-start.7 = (f32[64,256]{1,0:T(8,128)S(1)}, f32[64,256]{1,0:T(8,128)S(1)}, u32[]{:S(2)}, u32[]{:S(2)}) collective-permute-start(f32[64,256]{1,0:T(8,128)S(1)} %plane_sum.1.refs_0_), channel_id=1, source_target_pairs={{0,4},{2,6},{4,0},{6,2},{8,12},{10,14},{12,8},{14,10},{1,5},{3,7},... | collective-permute-start | bytes 196616 | tf_op jit(solution)/shard_map/ppermute | solution.py:209
  18.2 3.0 %collective-permute-done.2.refs_1_.refs_2_ = bf16[128,256]{1,0:T(8,128)(2,1)S(1)} collective-permute-done((bf16[128,256]{1,0:T(8,128)(2,1)S(1)}, bf16[128,256]{1,0:T(8,128)(2,1)S(1)}, u32[]{:S(2)}, u32[]{:S(2)}) %collective-permute-start.2) | collective-permute-done | bytes 65568 | tf_op jit(solution)/shard_map/ppermute | solution.py:209
  21.2 0.0 collective-permute-done.1.refs_0_.refs_1_
  21.3 1.0 %collective-permute-start.5 = (bf16[3,128,256]{2,1,0:T(8,128)(2,1)S(1)}, bf16[3,128,256]{2,1,0:T(8,128)(2,1)S(1)}, u32[]{:S(2)}, u32[]{:S(2)}) collective-permute-start(bf16[3,128,256]{2,1,0:T(8,128)(2,1)S(1)} %join_far.1), channel_id=1, source_target_pairs={{0,2},{2,0},{4,6},{6,4},{8,10},{10,8},{12,14},{14,12},{1,3},{3,1},... | collective-permute-start | bytes 589832 | tf_op jit(solution)/shard_map/ppermute | solution.py:209
  22.3 0.0 collective-permute-done.9.refs_3_
  22.3 1.9 %collective-permute-done.8.refs_2_ = f32[64,256]{1,0:T(8,128)S(1)} collective-permute-done((f32[64,256]{1,0:T(8,128)S(1)}, f32[64,256]{1,0:T(8,128)S(1)}, u32[]{:S(2)}, u32[]{:S(2)}) %collective-permute-start.8) | collective-permute-done | bytes 65568 | tf_op jit(solution)/shard_map/ppermute | solution.py:209
  24.2 0.0 collective-permute-done.7.refs_1_
  24.2 0.1 hub_sums.1.mine_ref
  24.3 0.6 %collective-permute-start.10 = (bf16[64,256]{1,0:T(8,128)(2,1)S(1)}, bf16[64,256]{1,0:T(8,128)(2,1)S(1)}, u32[]{:S(2)}, u32[]{:S(2)}) collective-permute-start(bf16[64,256]{1,0:T(8,128)(2,1)S(1)} %hub_sums.1.mine_ref), channel_id=1, source_target_pairs={{0,2},{2,0},{4,6},{6,4},{8,10},{10,8},{12,14},{14,12},{1,3},{3,1},... | collective-permute-start | bytes 98312 | tf_op jit(solution)/shard_map/ppermute | solution.py:209
  24.9 1.5 %collective-permute-start.4 = (bf16[128,256]{1,0:T(8,128)(2,1)S(1)}, bf16[128,256]{1,0:T(8,128)(2,1)S(1)}, u32[]{:S(2)}, u32[]{:S(2)}) collective-permute-start(bf16[128,256]{1,0:T(8,128)(2,1)S(1)} %get-tuple-element.18.refs_0_), channel_id=1, source_target_pairs={{0,2},{2,0},{4,6},{6,4},{8,10},{10,8},{12,14},{14,12},{1,3},{3,1},... | collective-permute-start | bytes 196616 | tf_op jit(solution)/shard_map/ppermute | solution.py:209
  26.4 2.0 %collective-permute-done.10.theirs_ref = bf16[64,256]{1,0:T(8,128)(2,1)S(1)} collective-permute-done((bf16[64,256]{1,0:T(8,128)(2,1)S(1)}, bf16[64,256]{1,0:T(8,128)(2,1)S(1)}, u32[]{:S(2)}, u32[]{:S(2)}) %collective-permute-start.10) | collective-permute-done | bytes 32800 | tf_op jit(solution)/shard_map/ppermute | solution.py:209
  28.4 0.1 collective-permute-start.11
  28.5 0.6 %collective-permute-done.4.refs_4_ = bf16[128,256]{1,0:T(8,128)(2,1)S(1)} collective-permute-done((bf16[128,256]{1,0:T(8,128)(2,1)S(1)}, bf16[128,256]{1,0:T(8,128)(2,1)S(1)}, u32[]{:S(2)}, u32[]{:S(2)}) %collective-permute-start.4) | collective-permute-done | bytes 65568 | tf_op jit(solution)/shard_map/ppermute | solution.py:209
  29.1 0.6 %collective-permute-done.11.refs_7_ = bf16[128,256]{1,0:T(8,128)(2,1)S(1)} collective-permute-done((bf16[128,256]{1,0:T(8,128)(2,1)S(1)}, bf16[128,256]{1,0:T(8,128)(2,1)S(1)}, u32[]{:S(2)}, u32[]{:S(2)}) %collective-permute-start.11) | collective-permute-done | bytes 65568 | tf_op jit(solution)/shard_map/ppermute | solution.py:206
  29.7 0.0 collective-permute-done.5.refs_5_
  29.7 1.0 %later_terms.1 = (f32[256,256]{1,0:T(8,128)S(1)}, f32[256,256]{1,0:T(8,128)S(1)}) custom-call(bf16[128,256]{1,0:T(8,128)(2,1)S(1)} %get-tuple-element.18.refs_0_, bf16[128,256]{1,0:T(8,128)(2,1)S(1)} %collective-permute-done.1.refs_0_.refs_1_, bf16[128,256]{1,0:T(8,128)(2,1)S(1)} %collective-permute-done.2.refs_1_.refs_2_, ...), custom_call_target="tpu_custom_call" | custom-call | tf_op jit(solution)/shard_map/later_terms/pallas_call | solution.py:218
  30.7 0.2 collective-permute-start.12
  31.0 1.4 %collective-permute-done.12.came_ref = f32[256,256]{1,0:T(8,128)S(1)} collective-permute-done((f32[256,256]{1,0:T(8,128)S(1)}, f32[256,256]{1,0:T(8,128)S(1)}, u32[]{:S(2)}, u32[]{:S(2)}) %collective-permute-start.12) | collective-permute-done | bytes 262176 | tf_op jit(solution)/shard_map/ppermute | solution.py:206
  32.3 1.0 %collective-permute-start.13 = (f32[64,256]{1,0:T(8,128)S(1)}, f32[64,256]{1,0:T(8,128)S(1)}, u32[]{:S(2)}, u32[]{:S(2)}) collective-permute-start(f32[64,256]{1,0:T(8,128)S(1)} %get-tuple-element.25), channel_id=1, source_target_pairs={{0,2},{2,0},{4,6},{6,4},{8,10},{10,8},{12,14},{14,12},{1,3},{3,1},... | collective-permute-start | bytes 196616 | tf_op jit(solution)/shard_map/ppermute | solution.py:209
  33.3 3.4 %collective-permute-done.13.came_ref = f32[64,256]{1,0:T(8,128)S(1)} collective-permute-done((f32[64,256]{1,0:T(8,128)S(1)}, f32[64,256]{1,0:T(8,128)S(1)}, u32[]{:S(2)}, u32[]{:S(2)}) %collective-permute-start.13) | collective-permute-done | bytes 65568 | tf_op jit(solution)/shard_map/ppermute | solution.py:209
  36.7 0.1 collective-permute-start.14
  36.8 3.4 %collective-permute-start.15 = (f32[16,256]{1,0:T(8,128)S(1)}, f32[16,256]{1,0:T(8,128)S(1)}, u32[]{:S(2)}, u32[]{:S(2)}) collective-permute-start(f32[16,256]{1,0:T(8,128)S(1)} %get-tuple-element.28), channel_id=1, source_target_pairs={{0,8},{2,10},{4,12},{6,14},{8,0},{10,2},{12,4},{14,6},{1,9},{3,11}... | collective-permute-start | bytes 49160 | tf_op jit(solution)/shard_map/ppermute | solution.py:209
  40.1 1.0 %collective-permute-start.16 = (f32[16,256]{1,0:T(8,128)S(1)}, f32[16,256]{1,0:T(8,128)S(1)}, u32[]{:S(2)}, u32[]{:S(2)}) collective-permute-start(f32[16,256]{1,0:T(8,128)S(1)} %get-tuple-element.29), channel_id=1, source_target_pairs={{0,12},{2,14},{4,8},{6,10},{8,4},{10,6},{12,0},{14,2},{1,13},{3,15... | collective-permute-start | bytes 49160 | tf_op jit(solution)/shard_map/ppermute | solution.py:209
  41.1 0.7 %last_scores.1 = f32[128,256]{1,0:T(8,128)} custom-call(s32[1,256]{1,0:T(1,128)S(1)} %bitcast.10, f32[256,256]{1,0:T(8,128)S(1)} %get-tuple-element.22.keep_ref, f32[256,256]{1,0:T(8,128)S(1)} %collective-permute-done.12.came_ref), custom_call_target="tpu_custom_call" | custom-call | tf_op jit(solution)/shard_map/last_scores/pallas_call | solution.py:218
  41.8 0.0 collective-permute-done.14.refs_1_
  41.8 0.0 collective-permute-done.15.refs_2_
  41.8 3.8 %collective-permute-done.16.refs_3_ = f32[16,256]{1,0:T(8,128)S(1)} collective-permute-done((f32[16,256]{1,0:T(8,128)S(1)}, f32[16,256]{1,0:T(8,128)S(1)}, u32[]{:S(2)}, u32[]{:S(2)}) %collective-permute-start.16) | collective-permute-done | bytes 16416 | tf_op jit(solution)/shard_map/ppermute | solution.py:209
  45.7 0.6 %last_hubs.1 = f32[16,256]{1,0:T(8,128)} custom-call(s32[1,256]{1,0:T(1,128)S(1)} %bitcast.11, f32[16,256]{1,0:T(8,128)S(1)} %get-tuple-element.26.refs_0_, f32[16,256]{1,0:T(8,128)S(1)} %collective-permute-done.14.refs_1_, f32[16,256]{1,0:T(8,128)S(1)} %collective-permute-done.15.refs_2_, f32[16,256]{1,0:T(8,128)S(1)} %collective-permute-done.16.refs_3_), custom_call_target="tpu_custom_call" | custom-call | tf_op jit(solution)/shard_map/last_hubs/pallas_call | solution.py:218
  (6 shorter events, 0.1 us)
Async XLA Ops:
  0.6 5.8 %copy-start = (s32[256]{0:T(256)S(1)}, s32[256]{0:T(256)}, u32[]{:S(2)}) copy-start(s32[256]{0:T(256)} %param.9) | copy-start | bytes 3076
  4.7 1.7 %collective-permute-start = (f32[256,256]{1,0:T(8,128)S(1)}, f32[256,256]{1,0:T(8,128)S(1)}, u32[]{:S(2)}, u32[]{:S(2)}) collective-permute-start(f32[256,256]{1,0:T(8,128)S(1)} %get-tuple-element.17), channel_id=1, source_target_pairs={{0,1},{1,0},{2,3},{3,2},{4,5},{5,4},{6,7},{7,6},{8,9},{9,8},{10,11... | collective-permute-start | bytes 786440 | tf_op jit(solution)/shard_map/ppermute | solution.py:206
  6.4 7.3 %collective-permute-start.6 = (f32[64,256]{1,0:T(8,128)S(1)}, f32[64,256]{1,0:T(8,128)S(1)}, u32[]{:S(2)}, u32[]{:S(2)}) collective-permute-start(f32[64,256]{1,0:T(8,128)S(1)} %get-tuple-element.20), channel_id=1, source_target_pairs={{0,2},{2,0},{4,6},{6,4},{8,10},{10,8},{12,14},{14,12},{1,3},{3,1},... | collective-permute-start | bytes 196616 | tf_op jit(solution)/shard_map/ppermute | solution.py:209
  9.4 8.1 %collective-permute-start.3 = (bf16[128,256]{1,0:T(8,128)(2,1)S(1)}, bf16[128,256]{1,0:T(8,128)(2,1)S(1)}, u32[]{:S(2)}, u32[]{:S(2)}) collective-permute-start(bf16[128,256]{1,0:T(8,128)(2,1)S(1)} %get-tuple-element.18.refs_0_), channel_id=1, source_target_pairs={{0,12},{2,14},{4,8},{6,10},{8,4},{10,6},{12,0},{14,2},{1,13},{3,15... | collective-permute-start | bytes 196616 | tf_op jit(solution)/shard_map/ppermute | solution.py:209
  13.0 8.3 %collective-permute-start.2 = (bf16[128,256]{1,0:T(8,128)(2,1)S(1)}, bf16[128,256]{1,0:T(8,128)(2,1)S(1)}, u32[]{:S(2)}, u32[]{:S(2)}) collective-permute-start(bf16[128,256]{1,0:T(8,128)(2,1)S(1)} %get-tuple-element.18.refs_0_), channel_id=1, source_target_pairs={{0,8},{2,10},{4,12},{6,14},{8,0},{10,2},{12,4},{14,6},{1,9},{3,11}... | collective-permute-start | bytes 196616 | tf_op jit(solution)/shard_map/ppermute | solution.py:209
  13.0 8.3 %collective-permute-start.1 = (bf16[128,256]{1,0:T(8,128)(2,1)S(1)}, bf16[128,256]{1,0:T(8,128)(2,1)S(1)}, u32[]{:S(2)}, u32[]{:S(2)}) collective-permute-start(bf16[128,256]{1,0:T(8,128)(2,1)S(1)} %get-tuple-element.18.refs_0_), channel_id=1, source_target_pairs={{0,4},{2,6},{4,0},{6,2},{8,12},{10,14},{12,8},{14,10},{1,5},{3,7},... | collective-permute-start | bytes 196616 | tf_op jit(solution)/shard_map/ppermute | solution.py:209
  13.8 8.5 %collective-permute-start.9 = (f32[64,256]{1,0:T(8,128)S(1)}, f32[64,256]{1,0:T(8,128)S(1)}, u32[]{:S(2)}, u32[]{:S(2)}) collective-permute-start(f32[64,256]{1,0:T(8,128)S(1)} %plane_sum.1.refs_0_), channel_id=1, source_target_pairs={{0,12},{2,14},{4,8},{6,10},{8,4},{10,6},{12,0},{14,2},{1,13},{3,15... | collective-permute-start | bytes 196616 | tf_op jit(solution)/shard_map/ppermute | solution.py:209
  17.4 6.8 %collective-permute-start.8 = (f32[64,256]{1,0:T(8,128)S(1)}, f32[64,256]{1,0:T(8,128)S(1)}, u32[]{:S(2)}, u32[]{:S(2)}) collective-permute-start(f32[64,256]{1,0:T(8,128)S(1)} %plane_sum.1.refs_0_), channel_id=1, source_target_pairs={{0,8},{2,10},{4,12},{6,14},{8,0},{10,2},{12,4},{14,6},{1,9},{3,11}... | collective-permute-start | bytes 196616 | tf_op jit(solution)/shard_map/ppermute | solution.py:209
  17.4 6.8 %collective-permute-start.7 = (f32[64,256]{1,0:T(8,128)S(1)}, f32[64,256]{1,0:T(8,128)S(1)}, u32[]{:S(2)}, u32[]{:S(2)}) collective-permute-start(f32[64,256]{1,0:T(8,128)S(1)} %plane_sum.1.refs_0_), channel_id=1, source_target_pairs={{0,4},{2,6},{4,0},{6,2},{8,12},{10,14},{12,8},{14,10},{1,5},{3,7},... | collective-permute-start | bytes 196616 | tf_op jit(solution)/shard_map/ppermute | solution.py:209
  21.3 8.5 %collective-permute-start.5 = (bf16[3,128,256]{2,1,0:T(8,128)(2,1)S(1)}, bf16[3,128,256]{2,1,0:T(8,128)(2,1)S(1)}, u32[]{:S(2)}, u32[]{:S(2)}) collective-permute-start(bf16[3,128,256]{2,1,0:T(8,128)(2,1)S(1)} %join_far.1), channel_id=1, source_target_pairs={{0,2},{2,0},{4,6},{6,4},{8,10},{10,8},{12,14},{14,12},{1,3},{3,1},... | collective-permute-start | bytes 589832 | tf_op jit(solution)/shard_map/ppermute | solution.py:209
  24.3 4.1 %collective-permute-start.10 = (bf16[64,256]{1,0:T(8,128)(2,1)S(1)}, bf16[64,256]{1,0:T(8,128)(2,1)S(1)}, u32[]{:S(2)}, u32[]{:S(2)}) collective-permute-start(bf16[64,256]{1,0:T(8,128)(2,1)S(1)} %hub_sums.1.mine_ref), channel_id=1, source_target_pairs={{0,2},{2,0},{4,6},{6,4},{8,10},{10,8},{12,14},{14,12},{1,3},{3,1},... | collective-permute-start | bytes 98312 | tf_op jit(solution)/shard_map/ppermute | solution.py:209
  24.9 4.3 %collective-permute-start.4 = (bf16[128,256]{1,0:T(8,128)(2,1)S(1)}, bf16[128,256]{1,0:T(8,128)(2,1)S(1)}, u32[]{:S(2)}, u32[]{:S(2)}) collective-permute-start(bf16[128,256]{1,0:T(8,128)(2,1)S(1)} %get-tuple-element.18.refs_0_), channel_id=1, source_target_pairs={{0,2},{2,0},{4,6},{6,4},{8,10},{10,8},{12,14},{14,12},{1,3},{3,1},... | collective-permute-start | bytes 196616 | tf_op jit(solution)/shard_map/ppermute | solution.py:209
  28.4 1.3 %collective-permute-start.11 = (bf16[128,256]{1,0:T(8,128)(2,1)S(1)}, bf16[128,256]{1,0:T(8,128)(2,1)S(1)}, u32[]{:S(2)}, u32[]{:S(2)}) collective-permute-start(bf16[128,256]{1,0:T(8,128)(2,1)S(1)} %join_sides.1.refs_6_), channel_id=1, source_target_pairs={{0,1},{1,0},{2,3},{3,2},{4,5},{5,4},{6,7},{7,6},{8,9},{9,8},{10,11... | collective-permute-start | bytes 196616 | tf_op jit(solution)/shard_map/ppermute | solution.py:206
  30.7 1.6 %collective-permute-start.12 = (f32[256,256]{1,0:T(8,128)S(1)}, f32[256,256]{1,0:T(8,128)S(1)}, u32[]{:S(2)}, u32[]{:S(2)}) collective-permute-start(f32[256,256]{1,0:T(8,128)S(1)} %get-tuple-element.23), channel_id=1, source_target_pairs={{0,1},{1,0},{2,3},{3,2},{4,5},{5,4},{6,7},{7,6},{8,9},{9,8},{10,11... | collective-permute-start | bytes 786440 | tf_op jit(solution)/shard_map/ppermute | solution.py:206
  32.3 4.3 %collective-permute-start.13 = (f32[64,256]{1,0:T(8,128)S(1)}, f32[64,256]{1,0:T(8,128)S(1)}, u32[]{:S(2)}, u32[]{:S(2)}) collective-permute-start(f32[64,256]{1,0:T(8,128)S(1)} %get-tuple-element.25), channel_id=1, source_target_pairs={{0,2},{2,0},{4,6},{6,4},{8,10},{10,8},{12,14},{14,12},{1,3},{3,1},... | collective-permute-start | bytes 196616 | tf_op jit(solution)/shard_map/ppermute | solution.py:209
  36.7 5.2 %collective-permute-start.14 = (f32[16,256]{1,0:T(8,128)S(1)}, f32[16,256]{1,0:T(8,128)S(1)}, u32[]{:S(2)}, u32[]{:S(2)}) collective-permute-start(f32[16,256]{1,0:T(8,128)S(1)} %get-tuple-element.27), channel_id=1, source_target_pairs={{0,4},{2,6},{4,0},{6,2},{8,12},{10,14},{12,8},{14,10},{1,5},{3,7},... | collective-permute-start | bytes 49160 | tf_op jit(solution)/shard_map/ppermute | solution.py:209
  36.8 5.1 %collective-permute-start.15 = (f32[16,256]{1,0:T(8,128)S(1)}, f32[16,256]{1,0:T(8,128)S(1)}, u32[]{:S(2)}, u32[]{:S(2)}) collective-permute-start(f32[16,256]{1,0:T(8,128)S(1)} %get-tuple-element.28), channel_id=1, source_target_pairs={{0,8},{2,10},{4,12},{6,14},{8,0},{10,2},{12,4},{14,6},{1,9},{3,11}... | collective-permute-start | bytes 49160 | tf_op jit(solution)/shard_map/ppermute | solution.py:209
  40.1 5.5 %collective-permute-start.16 = (f32[16,256]{1,0:T(8,128)S(1)}, f32[16,256]{1,0:T(8,128)S(1)}, u32[]{:S(2)}, u32[]{:S(2)}) collective-permute-start(f32[16,256]{1,0:T(8,128)S(1)} %get-tuple-element.29), channel_id=1, source_target_pairs={{0,12},{2,14},{4,8},{6,10},{8,4},{10,6},{12,0},{14,2},{1,13},{3,15... | collective-permute-start | bytes 49160 | tf_op jit(solution)/shard_map/ppermute | solution.py:209

commit v10 on v9

--- a/solution.py
+++ b/solution.py
@@ -13,6 +13,7 @@
 DAMP = 0.85
 CHUNK = 16
 X = 2
+HUB_CORE = 1
 MICRO = 10 ** 9
 VMEM_LIMIT = 32 * 1024 * 1024
 
@@ -30,20 +31,19 @@
     return (ids == src).astype(jnp.float32)
 
 
-def write_terms(dims, block, prod_ref, dense_ref, panel_ref, send_ref, keep_ref):
-    n_row, n_col, side = dims
+def write_terms(dims, prod_ref, dense_ref, panel_ref, send_ref, keep_ref, hubs_ref):
+    n_col = dims[1]
     rows = dense_ref.shape[0] // 2
+    own = n_col * VB
     c = lax.axis_index("col")
     prod = jnp.dot(dense_ref[...], panel_ref[...], preferred_element_type=jnp.float32)
-    prod_ref[...] = prod[:rows] + prod[rows:]
+    prod_ref[...] = prod[:own] + prod[rows:rows + own]
+    hubs_ref[...] = prod[own:rows] + prod[rows + own:]
     for ref, col in ((keep_ref, c), (send_ref, 1 - c)):
-        ref[:VB] = prod_ref[pl.ds(pl.multiple_of(col * VB, VB), VB), :]
-        for k in range(H // n_col // block):
-            start = n_col * VB + (k * n_col + col) * block
-            ref[VB + k * block:VB + (k + 1) * block] = prod_ref[pl.ds(pl.multiple_of(start, block), block), :]
-
-
-def first_kernel(dims, tiles_ref, rows_hbm, cols_hbm, count_hbm, src_hbm, send_ref, keep_ref, dense_ref,
+        ref[...] = prod_ref[pl.ds(pl.multiple_of(col * VB, VB), VB), :]
+
+
+def first_kernel(dims, tiles_ref, rows_hbm, cols_hbm, count_hbm, src_hbm, send_ref, keep_ref, hubs_ref, dense_ref,
                  held, rows_ref, cols_ref, count_ref, src_ref, total, panel, prod, sems, small):
     n_row, n_col, side = dims
     n_rows = dense_ref.shape[0] // 2
@@ -81,48 +81,55 @@
         high = whole.astype(jnp.bfloat16)
         dense_ref[pl.ds(r, side), :] = high
         dense_ref[pl.ds(n_rows + r, side), :] = (whole - high.astype(jnp.float32)).astype(jnp.bfloat16)
-    write_terms(dims, H // n_col, prod, dense_ref, panel, send_ref, keep_ref)
+    write_terms(dims, prod, dense_ref, panel, send_ref, keep_ref, hubs_ref)
 
 
 def second_kernel(dims, *refs):
-    n_row, n_col, side = dims
+    n_row = dims[0]
     n_z = n_row // X
-    own, far, (across, far_across, mine_ref, theirs_ref), rest = refs[0], refs[1:n_z], refs[n_z:n_z + 4], refs[n_z + 4:]
-    dense_ref, send_ref, keep_ref, panel, prod = rest
-    half = H // n_col
+    blocks, (across, mine_ref, theirs_ref) = refs[:n_z], refs[n_z:n_z + 3]
+    dense_ref, send_ref, keep_ref, hubs_ref, panel, prod = refs[n_z + 3:]
     r, c = lax.axis_index("row"), lax.axis_index("col")
 
     def put(owner, block):
         panel[pl.ds(pl.multiple_of(owner * VB, VB), VB), :] = block
 
-    put(r, own[...])
-    put(r ^ 1, across[...])
-    for k in range(1, n_z):
-        put(r ^ (X * k), far[k - 1][...])
-        put(r ^ (X * k) ^ 1, far_across[k - 1])
-    for ref, col in ((mine_ref, c), (theirs_ref, 1 - c)):
-        panel[pl.ds(pl.multiple_of(n_row * VB + col * half, half), half), :] = ref[...]
-    write_terms(dims, half // n_row, prod, dense_ref, panel, send_ref, keep_ref)
+    for k in range(n_z):
+        put(r ^ (X * k), blocks[k][...])
+        put(r ^ (X * k) ^ 1, across[k])
+    for ref, core in ((mine_ref, HUB_CORE), (theirs_ref, 1 - HUB_CORE)):
+        @pl.when(c == core)
+        def _():
+            panel[pl.ds(n_row * VB, H), :] = ref[...]
+    write_terms(dims, prod, dense_ref, panel, send_ref, keep_ref, hubs_ref)
 
 
 def own_scores(dims, src_ref, keep_ref, came_ref):
     first = H + (lax.axis_index("row") * dims[1] + lax.axis_index("col")) * VB
-    tele = one_hot(first, VB, src_ref[...])
-    return DAMP * (keep_ref[:VB] + came_ref[:VB]) + 0.15 * tele
-
-
-def spread_kernel(dims, src_ref, keep_ref, came_ref, scores_ref, hold_ref, pass_ref):
-    quarter = hold_ref.shape[0]
+    return DAMP * (keep_ref[...] + came_ref[...]) + 0.15 * one_hot(first, VB, src_ref[...])
+
+
+def scores_kernel(dims, src_ref, keep_ref, came_ref, scores_ref):
+    scores_ref[...] = own_scores(dims, src_ref, keep_ref, came_ref).astype(scores_ref.dtype)
+
+
+def spread_kernel(block, mine_ref, came_ref, hold_ref, pass_ref):
     x = lax.axis_index("row") % X
     for ref, place in ((hold_ref, x), (pass_ref, 1 - x)):
-        spot = pl.ds(pl.multiple_of(VB + place * quarter, quarter), quarter)
-        ref[...] = keep_ref[spot, :] + came_ref[spot, :]
-    scores_ref[...] = own_scores(dims, src_ref, keep_ref, came_ref).astype(scores_ref.dtype)
+        for k in range(ref.shape[0] // block):
+            spot = pl.ds(pl.multiple_of((k * X + place) * block, block), block)
+            ref[k * block:(k + 1) * block] = mine_ref[spot, :] + came_ref[spot, :]
+
+
+def scores_and_spread_kernel(dims, block, src_ref, keep_ref, came_ref, mine_ref, theirs_ref, scores_ref, hold_ref, pass_ref):
+    spread_kernel(block, mine_ref, theirs_ref, hold_ref, pass_ref)
+    scores_kernel(dims, src_ref, keep_ref, came_ref, scores_ref)
 
 
 def join_kernel(*refs):
-    for k, ref in enumerate(refs[:-1]):
-        refs[-1][k] = ref[...]
+    out_ref = refs[-1]
+    for k in range(out_ref.shape[0]):
+        out_ref[k] = refs[k][...]
 
 
 def plane_kernel(hold_ref, came_ref, out_ref):
@@ -139,48 +146,35 @@
     return summed
 
 
-def hub_kernel(dims, src_ref, *refs):
-    planes, (out_ref, held) = refs[:-2], refs[-2:]
-    quarter = out_ref.shape[0]
-    first = (lax.axis_index("col") * X + lax.axis_index("row") % X) * quarter
-    tele = one_hot(first, quarter, src_ref[...])
+def hub_kernel(first, src_ref, *refs):
+    out_ref, held = refs[-2:]
+    planes = refs[:held.shape[0]]
+    count = out_ref.shape[0]
+    tele = one_hot(first(lax.axis_index("row")), count, src_ref[...])
     out_ref[...] = (DAMP * sum_planes(planes, held) + 0.15 * tele).astype(out_ref.dtype)
 
 
 def side_kernel(mine_ref, theirs_ref, out_ref):
-    quarter = mine_ref.shape[0]
+    part = mine_ref.shape[0]
     x = lax.axis_index("row") % X
     for ref, place in ((mine_ref, x), (theirs_ref, 1 - x)):
-        out_ref[pl.ds(pl.multiple_of(place * quarter, quarter), quarter), :] = ref[...]
-
-
-def halves_kernel(dims, keep_ref, came_ref, hold_ref, pass_ref):
-    n_row, n_col, side = dims
-    piece = H // (n_row * n_col)
-    x = lax.axis_index("row") % X
-    for ref, place in ((hold_ref, x), (pass_ref, 1 - x)):
-        for z in range(n_row // X):
-            spot = pl.ds(pl.multiple_of(VB + (z * X + place) * piece, piece), piece)
-            ref[z * piece:(z + 1) * piece] = keep_ref[spot, :] + came_ref[spot, :]
+        out_ref[pl.ds(pl.multiple_of(place * part, part), part), :] = ref[...]
 
 
 def pieces_kernel(hold_ref, came_ref, *outs):
     z = lax.axis_index("row") // X
-    piece = outs[0].shape[0]
+    share = outs[0].shape[0]
     for k, out in enumerate(outs):
-        spot = pl.ds(pl.multiple_of((z ^ k) * piece, piece), piece)
+        spot = pl.ds(pl.multiple_of((z ^ k) * share, share), share)
         out[...] = hold_ref[spot, :] + came_ref[spot, :]
 
 
-def last_scores_kernel(dims, src_ref, keep_ref, came_ref, scores_ref):
-    scores_ref[...] = own_scores(dims, src_ref, keep_ref, came_ref)
-
-
-def last_hubs_kernel(dims, src_ref, *refs):
-    planes, (out_ref, held) = refs[:-2], refs[-2:]
+def last_hubs_kernel(mine_ref, theirs_ref, out_ref):
     piece = out_ref.shape[0]
-    first = (lax.axis_index("row") * dims[1] + lax.axis_index("col")) * piece
-    out_ref[...] = DAMP * sum_planes(planes, held) + 0.15 * one_hot(first, piece, src_ref[...])
+    for ref, core in ((mine_ref, HUB_CORE), (theirs_ref, 1 - HUB_CORE)):
+        @pl.when(lax.axis_index("col") == core)
+        def _():
+            out_ref[...] = ref[core * piece:(core + 1) * piece]
 
 
 def fast_body(tiles, tile_row, tile_col, tile_count, sources):
@@ -188,31 +182,34 @@
     width = sources.shape[0]
     n_row = lax.axis_size("row")
     n_col = lax.axis_size("col")
-    piece = H // (n_row * n_col)
+    n_z = n_row // X
+    part = H // X
+    share = H // n_row
     dims = (n_row, n_col, side)
     n_rows = n_col * VB + H
     n_cols = n_row * VB + H
-    f32 = functools.partial(jax.ShapeDtypeStruct, dtype=jnp.float32)
-    bf16 = functools.partial(jax.ShapeDtypeStruct, dtype=jnp.bfloat16)
+    bind = functools.partial
+    f32 = bind(jax.ShapeDtypeStruct, dtype=jnp.float32)
+    bf16 = bind(jax.ShapeDtypeStruct, dtype=jnp.bfloat16)
     src = sources.reshape(1, width)
-    half = VB + n_row * piece
-    quarter = H // n_col // X
     product_scratch = [
         pltpu.VMEM((n_cols, width), jnp.bfloat16),
-        pltpu.VMEM((n_rows, width), jnp.float32),
+        pltpu.VMEM((n_col * VB, width), jnp.float32),
     ]
+    term_shapes = (f32((VB, width)), f32((VB, width)), f32((H, width)))
 
     def other_core(x):
         return lax.ppermute(x, "col", [(0, 1), (1, 0)])
 
+    def to_core(x, core):
+        return lax.ppermute(x, "col", [(1 - core, core)])
+
     def to_partner(x, flip):
         return lax.ppermute(x, "row", [(r, r ^ flip) for r in range(n_row)])
 
-    def other_side(x):
-        return to_partner(x, 1)
-
-    def along_z(blocks):
-        return [to_partner(block, X * k) for k, block in enumerate(blocks) if k > 0]
+    def hub_partner(x, flip):
+        pairs = [(r * n_col + HUB_CORE, (r ^ flip) * n_col + HUB_CORE) for r in range(n_row)]
+        return lax.ppermute(x, ("row", "col"), pairs)
 
     def call(kernel, name, out_shape, *args, scratch=(), cost=0):
         return pl.pallas_call(
@@ -226,15 +223,13 @@
             name=name,
         )(*args)
 
-    bind = functools.partial
-
     in_hbm = [pltpu.with_memory_space_constraint(x, pltpu.HBM) for x in (
         tiles.reshape(slots, side, side), tile_row.reshape(slots), tile_col.reshape(slots), src)]
-    send, keep, dense = pl.pallas_call(
+    send, keep, hubs, dense = pl.pallas_call(
         bind(first_kernel, dims),
-        out_shape=(f32((half, width)), f32((half, width)), bf16((2 * n_rows, n_cols))),
+        out_shape=term_shapes + (bf16((2 * n_rows, n_cols)),),
         in_specs=[HBM] * 5,
-        out_specs=[VMEM] * 3,
+        out_specs=[VMEM] * 4,
         scratch_shapes=[
             pltpu.VMEM((slots, side, side), jnp.bfloat16),
             pltpu.SMEM((slots,), jnp.int32),
@@ -250,33 +245,30 @@
         name="first_terms",
     )(*in_hbm[:3], tile_count.reshape(1), in_hbm[3])
 
-    n_z = n_row // X
     for step in range(ITERS - 1):
-        came = other_core(send)
         own, hold, away = call(
-            bind(spread_kernel, dims), "spread",
-            (bf16((VB, width)), f32((quarter, width)), f32((quarter, width))),
-            src, keep, came)
-        away = other_side(away)
-        far = along_z([own] * n_z)
-        across = other_side(own)
-        plane = call(plane_kernel, "plane_sum", f32((quarter, width)), hold, away, cost=20)
-        planes = [plane] + along_z([plane] * n_z)
-        far_across = other_side(call(join_kernel, "join_far", bf16((n_z - 1, VB, width)), *far))
-        mine = call(bind(hub_kernel, dims), "hub_sums", bf16((quarter, width)), src, *planes,
-                    scratch=[pltpu.VMEM((n_z, quarter, width), jnp.float32)], cost=1)
-        mine = call(side_kernel, "join_sides", bf16((H // n_col, width)), mine, other_side(mine))
-        send, keep = call(
-            bind(second_kernel, dims), "later_terms", (f32((half, width)), f32((half, width))),
-            own, *far, across, far_across, mine, other_core(mine), dense, scratch=product_scratch)
-    came = other_core(send)
-    hold, away = call(bind(halves_kernel, dims), "hub_halves",
-                      (f32((quarter, width)), f32((quarter, width))), keep, came)
-    pieces = call(pieces_kernel, "hub_pieces", (f32((piece, width)),) * n_z, hold, other_side(away))
-    pieces = [pieces[0]] + along_z(pieces)
-    scores = call(bind(last_scores_kernel, dims), "last_scores", f32((VB, width)), src, keep, came)
-    hubs = call(bind(last_hubs_kernel, dims), "last_hubs", f32((piece, width)), src, *pieces,
-                scratch=[pltpu.VMEM((n_z, piece, width), jnp.float32)])
+            bind(scores_and_spread_kernel, dims, part), "spread",
+            (bf16((VB, width)), f32((part, width)), f32((part, width))),
+            src, keep, other_core(send), hubs, to_core(hubs, HUB_CORE))
+        away = hub_partner(away, 1)
+        blocks = [own] + [to_partner(own, X * k) for k in range(1, n_z)]
+        plane = call(plane_kernel, "plane_sum", f32((part, width)), hold, away)
+        planes = [plane] + [hub_partner(plane, X * k) for k in range(1, n_z)]
+        across = to_partner(call(join_kernel, "join_rows", bf16((n_z, VB, width)), *blocks, cost=1), 1)
+        mine = call(bind(hub_kernel, lambda r: r % X * part), "hub_sums", bf16((part, width)), src, *planes,
+                    scratch=[pltpu.VMEM((n_z, part, width), jnp.float32)], cost=1)
+        mine = call(side_kernel, "join_sides", bf16((H, width)), mine, hub_partner(mine, 1))
+        send, keep, hubs = call(
+            bind(second_kernel, dims), "later_terms", term_shapes,
+            *blocks, across, mine, to_core(mine, 1 - HUB_CORE), dense, scratch=product_scratch)
+    hold, away = call(bind(spread_kernel, share), "last_spread", (f32((part, width)),) * 2,
+                      hubs, to_core(hubs, HUB_CORE))
+    pieces = call(pieces_kernel, "hub_pieces", (f32((share, width)),) * n_z, hold, hub_partner(away, 1))
+    pieces = [pieces[0]] + [hub_partner(pieces[k], X * k) for k in range(1, n_z)]
+    scores = call(bind(scores_kernel, dims), "last_scores", f32((VB, width)), src, keep, other_core(send))
+    mine = call(bind(hub_kernel, lambda r: r * share), "last_sums", f32((share, width)), src, *pieces,
+                scratch=[pltpu.VMEM((n_z, share, width), jnp.float32)])
+    hubs = call(last_hubs_kernel, "last_hubs", f32((share // n_col, width)), mine, to_core(mine, 1 - HUB_CORE))
     return scores.reshape(1, 1, VB, width), hubs
 
 

time: 46.4 us -> 62.5 us (1.35)
  waiting for transfers between devices: 18 us -> 33.3 us
    ppermute x0 -> x13, waiting for transfers between devices: none -> 24.9 us  [the longest x4 24.9 us: to_core(): return lax.ppermute(x, 'col', [(1 - core, core)])]
    ppermute x14 -> x4, starting transfers between devices: 20.3 us -> 6.39 us  [to_partner(): return lax.ppermute(x, 'row', [(r, r ^ flip) for r in range(n_row)])]
    ppermute x0 -> x13, starting transfers between devices: none -> 13 us  [the longest x4 7.03 us: to_core(): return lax.ppermute(x, 'col', [(1 - core, core)])]
    ppermute x14 -> x4, waiting for transfers between devices: 14.8 us -> 6.97 us  [to_partner(): return lax.ppermute(x, 'row', [(r, r ^ flip) for r in range(n_row)])]
    ppermute x3 -> x2, waiting for transfers between devices: 3.13 us -> 1.34 us  [other_core(): return lax.ppermute(x, 'col', [(0, 1), (1, 0)])]
    ppermute x3 -> x2, starting transfers between devices: 0.83 us -> 2.09 us  [other_core(): return lax.ppermute(x, 'col', [(0, 1), (1, 0)])]
    pallas_call x10 -> x11, Pallas kernels: 2.46 us -> 2.51 us  [call(): pl.pallas_call(kernel, out_shape=out_shape, in_specs=[VMEM] * len(args),...]
  transfers between devices with their start and end apart: 17 -> 19, of which waited for: 9 -> 7; matrix products, arithmetic and copies ran while one was open for 0% -> 0% of each run, Pallas kernels for 2% -> 1%
where the time goes in v10:
time: 62.5 us; the launch traced here: 62.1 us
  waiting for transfers between devices  33.3 us (53%)
  starting transfers between devices  21.5 us (34%)
  Pallas kernels  5.81 us (9%)
  between operations  1.52 us (2%)
    ppermute x4, waiting for transfers between devices, to_core(): return lax.ppermute(x, 'col', [(1 - core, core)])  24.9 us
    ppermute x4, starting transfers between devices, to_core(): return lax.ppermute(x, 'col', [(1 - core, core)])  7.03 us
    ppermute x4, waiting for transfers between devices, to_partner(): return lax.ppermute(x, 'row', [(r, r ^ flip) for r in range(n_row)])  6.97 us
    ppermute x4, starting transfers between devices, to_partner(): return lax.ppermute(x, 'row', [(r, r ^ flip) for r in range(n_row)])  6.39 us
    ppermute x9, starting transfers between devices, hub_partner(): return lax.ppermute(x, ('row', 'col'), pairs)  5.99 us
    pallas_call x1, Pallas kernels, fast_body(): pl.pallas_call(bind(first_kernel, dims), out_shape=term_shapes + (bf16((2...  3.29 us
    pallas_call x11, Pallas kernels, call(): pl.pallas_call(kernel, out_shape=out_shape, in_specs=[VMEM] * len(args),...  2.51 us
    ppermute x2, starting transfers between devices, other_core(): return lax.ppermute(x, 'col', [(0, 1), (1, 0)])  2.09 us
  transfers between devices with their start and end apart: 19, of which 7 were waited for; matrix products, arithmetic and copies ran while one was open for 0% of the time, Pallas kernels for 1%

profile of v10, /device:TPU:0, one launch (start us, length us, event | category | flops | bytes accessed | tf_op | source)
XLA Modules:
  0.0 62.1 jit_solution(2204193954024569249)
XLA Ops:
  0.6 0.0 copy-start
  1.3 3.3 %first_terms.1 = (f32[128,256]{1,0:T(8,128)S(1)}, f32[128,256]{1,0:T(8,128)S(1)}, f32[256,256]{1,0:T(8,128)S(1)}, bf16[1024,1280]{1,0:T(8,128)(2,1)S(1)}) custom-call(bf16[96,128,128]{2,1,0:T(8,128)(2,1)} %bitcast.12, s32[96]{0:T(128)} %bitcast.14, s32[96]{0:T(128)} %bitcast.15, s32[1]{0:T(128)} %bitcast.6.count_hbm, s32[1,256]{1,0:T(1,128)} %bitcast.7), custom_call_target="tpu_custom_call" | custom-call | tf_op jit(solution)/shard_map/first_terms/pallas_call | solution.py:228
  4.6 2.4 %collective-permute-start.1 = (f32[256,256]{1,0:T(8,128)S(1)}, f32[256,256]{1,0:T(8,128)S(1)}, u32[]{:S(2)}, u32[]{:S(2)}) collective-permute-start(f32[256,256]{1,0:T(8,128)S(1)} %get-tuple-element.20.mine_ref), channel_id=1, source_target_pairs={{0,1},{2,3},{4,5},{6,7},{8,9},{10,11},{12,13},{14,15},{16,17},{18,... | collective-permute-start | bytes 786440 | tf_op jit(solution)/shard_map/ppermute | solution.py:205
  7.0 0.1 collective-permute-start
  7.1 1.3 %collective-permute-done.came_ref = f32[128,256]{1,0:T(8,128)S(1)} collective-permute-done((f32[128,256]{1,0:T(8,128)S(1)}, f32[128,256]{1,0:T(8,128)S(1)}, u32[]{:S(2)}, u32[]{:S(2)}) %collective-permute-start) | collective-permute-done | bytes 131104 | tf_op jit(solution)/shard_map/ppermute | solution.py:202
  8.4 0.0 collective-permute-done.1.theirs_ref
  8.4 0.0 copy-done
  8.4 0.1 spread.1
  8.5 0.7 %collective-permute-start.6 = (f32[128,256]{1,0:T(8,128)S(1)}, f32[128,256]{1,0:T(8,128)S(1)}, u32[]{:S(2)}, u32[]{:S(2)}) collective-permute-start(f32[128,256]{1,0:T(8,128)S(1)} %get-tuple-element.23), channel_id=1, source_target_pairs={{1,3},{3,1},{5,7},{7,5},{9,11},{11,9},{13,15},{15,13},{17,19},{19,... | collective-permute-start | bytes 393224 | tf_op jit(solution)/shard_map/ppermute | solution.py:212
  9.1 4.5 %collective-permute-start.4 = (bf16[128,256]{1,0:T(8,128)(2,1)S(1)}, bf16[128,256]{1,0:T(8,128)(2,1)S(1)}, u32[]{:S(2)}, u32[]{:S(2)}) collective-permute-start(bf16[128,256]{1,0:T(8,128)(2,1)S(1)} %get-tuple-element.21.refs_0_), channel_id=1, source_target_pairs={{0,12},{2,14},{4,8},{6,10},{8,4},{10,6},{12,0},{14,2},{1,13},{3,15... | collective-permute-start | bytes 196616 | tf_op jit(solution)/shard_map/ppermute | solution.py:208
  13.6 0.0 collective-permute-start.3
  13.6 0.6 %collective-permute-start.2 = (bf16[128,256]{1,0:T(8,128)(2,1)S(1)}, bf16[128,256]{1,0:T(8,128)(2,1)S(1)}, u32[]{:S(2)}, u32[]{:S(2)}) collective-permute-start(bf16[128,256]{1,0:T(8,128)(2,1)S(1)} %get-tuple-element.21.refs_0_), channel_id=1, source_target_pairs={{0,4},{2,6},{4,0},{6,2},{8,12},{10,14},{12,8},{14,10},{1,5},{3,7},... | collective-permute-start | bytes 196616 | tf_op jit(solution)/shard_map/ppermute | solution.py:208
  14.3 0.0 collective-permute-done.6.came_ref
  14.3 0.7 %collective-permute-start.9 = (f32[128,256]{1,0:T(8,128)S(1)}, f32[128,256]{1,0:T(8,128)S(1)}, u32[]{:S(2)}, u32[]{:S(2)}) collective-permute-start(f32[128,256]{1,0:T(8,128)S(1)} %plane_sum.1.refs_0_), channel_id=1, source_target_pairs={{1,13},{3,15},{5,9},{7,11},{9,5},{11,7},{13,1},{15,3},{17,29},{19,... | collective-permute-start | bytes 393224 | tf_op jit(solution)/shard_map/ppermute | solution.py:212
  15.0 0.7 %collective-permute-start.8 = (f32[128,256]{1,0:T(8,128)S(1)}, f32[128,256]{1,0:T(8,128)S(1)}, u32[]{:S(2)}, u32[]{:S(2)}) collective-permute-start(f32[128,256]{1,0:T(8,128)S(1)} %plane_sum.1.refs_0_), channel_id=1, source_target_pairs={{1,9},{3,11},{5,13},{7,15},{9,1},{11,3},{13,5},{15,7},{17,25},{19,... | collective-permute-start | bytes 393224 | tf_op jit(solution)/shard_map/ppermute | solution.py:212
  15.7 0.3 collective-permute-done.4.refs_3_
  16.0 0.7 %collective-permute-start.7 = (f32[128,256]{1,0:T(8,128)S(1)}, f32[128,256]{1,0:T(8,128)S(1)}, u32[]{:S(2)}, u32[]{:S(2)}) collective-permute-start(f32[128,256]{1,0:T(8,128)S(1)} %plane_sum.1.refs_0_), channel_id=1, source_target_pairs={{1,5},{3,7},{5,1},{7,3},{9,13},{11,15},{13,9},{15,11},{17,21},{19,... | collective-permute-start | bytes 393224 | tf_op jit(solution)/shard_map/ppermute | solution.py:212
  16.7 3.6 %collective-permute-done.3.refs_2_ = bf16[128,256]{1,0:T(8,128)(2,1)S(1)} collective-permute-done((bf16[128,256]{1,0:T(8,128)(2,1)S(1)}, bf16[128,256]{1,0:T(8,128)(2,1)S(1)}, u32[]{:S(2)}, u32[]{:S(2)}) %collective-permute-start.3) | collective-permute-done | bytes 65568 | tf_op jit(solution)/shard_map/ppermute | solution.py:208
  20.3 0.0 collective-permute-done.2.refs_1_
  20.3 1.3 %collective-permute-start.5 = (bf16[4,128,256]{2,1,0:T(8,128)(2,1)S(1)}, bf16[4,128,256]{2,1,0:T(8,128)(2,1)S(1)}, u32[]{:S(2)}, u32[]{:S(2)}) collective-permute-start(bf16[4,128,256]{2,1,0:T(8,128)(2,1)S(1)} %join_rows.1), channel_id=1, source_target_pairs={{0,2},{2,0},{4,6},{6,4},{8,10},{10,8},{12,14},{14,12},{1,3},{3,1},... | collective-permute-start | bytes 786440 | tf_op jit(solution)/shard_map/ppermute | solution.py:208
  21.5 0.0 collective-permute-done.9.refs_3_
  21.5 0.0 collective-permute-done.8.refs_2_
  21.5 0.0 collective-permute-done.7.refs_1_
  21.5 0.1 hub_sums.1.mine_ref
  21.7 0.7 %collective-permute-start.10 = (bf16[128,256]{1,0:T(8,128)(2,1)S(1)}, bf16[128,256]{1,0:T(8,128)(2,1)S(1)}, u32[]{:S(2)}, u32[]{:S(2)}) collective-permute-start(bf16[128,256]{1,0:T(8,128)(2,1)S(1)} %hub_sums.1.mine_ref), channel_id=1, source_target_pairs={{1,3},{3,1},{5,7},{7,5},{9,11},{11,9},{13,15},{15,13},{17,19},{19,... | collective-permute-start | bytes 196616 | tf_op jit(solution)/shard_map/ppermute | solution.py:212
  22.3 0.0 collective-permute-done.10.theirs_ref
  22.4 1.3 %collective-permute-start.11 = (bf16[256,256]{1,0:T(8,128)(2,1)S(1)}, bf16[256,256]{1,0:T(8,128)(2,1)S(1)}, u32[]{:S(2)}, u32[]{:S(2)}) collective-permute-start(bf16[256,256]{1,0:T(8,128)(2,1)S(1)} %join_sides.1.refs_5_), channel_id=1, source_target_pairs={{1,0},{3,2},{5,4},{7,6},{9,8},{11,10},{13,12},{15,14},{17,16},{19,... | collective-permute-start | bytes 393224 | tf_op jit(solution)/shard_map/ppermute | solution.py:205
  23.7 3.0 %collective-permute-done.5.refs_4_ = bf16[4,128,256]{2,1,0:T(8,128)(2,1)S(1)} collective-permute-done((bf16[4,128,256]{2,1,0:T(8,128)(2,1)S(1)}, bf16[4,128,256]{2,1,0:T(8,128)(2,1)S(1)}, u32[]{:S(2)}, u32[]{:S(2)}) %collective-permute-start.5) | collective-permute-done | bytes 262176 | tf_op jit(solution)/shard_map/ppermute | solution.py:208
  26.7 10.4 %collective-permute-done.11.refs_6_ = bf16[256,256]{1,0:T(8,128)(2,1)S(1)} collective-permute-done((bf16[256,256]{1,0:T(8,128)(2,1)S(1)}, bf16[256,256]{1,0:T(8,128)(2,1)S(1)}, u32[]{:S(2)}, u32[]{:S(2)}) %collective-permute-start.11) | collective-permute-done | bytes 131104 | tf_op jit(solution)/shard_map/ppermute | solution.py:205
  37.1 0.9 %later_terms.1 = (f32[128,256]{1,0:T(8,128)S(1)}, f32[128,256]{1,0:T(8,128)S(1)}, f32[256,256]{1,0:T(8,128)S(1)}) custom-call(bf16[128,256]{1,0:T(8,128)(2,1)S(1)} %get-tuple-element.21.refs_0_, bf16[128,256]{1,0:T(8,128)(2,1)S(1)} %collective-permute-done.2.refs_1_, bf16[128,256]{1,0:T(8,128)(2,1)S(1)} %collective-permute-done.3.refs_2_, ...), custom_call_target="tpu_custom_call" | custom-call | tf_op jit(solution)/shard_map/later_terms/pallas_call | solution.py:215
  38.0 2.1 %collective-permute-start.13 = (f32[256,256]{1,0:T(8,128)S(1)}, f32[256,256]{1,0:T(8,128)S(1)}, u32[]{:S(2)}, u32[]{:S(2)}) collective-permute-start(f32[256,256]{1,0:T(8,128)S(1)} %get-tuple-element.27.mine_ref), channel_id=1, source_target_pairs={{0,1},{2,3},{4,5},{6,7},{8,9},{10,11},{12,13},{14,15},{16,17},{18,... | collective-permute-start | bytes 786440 | tf_op jit(solution)/shard_map/ppermute | solution.py:205
  40.1 1.1 %collective-permute-done.13.came_ref = f32[256,256]{1,0:T(8,128)S(1)} collective-permute-done((f32[256,256]{1,0:T(8,128)S(1)}, f32[256,256]{1,0:T(8,128)S(1)}, u32[]{:S(2)}, u32[]{:S(2)}) %collective-permute-start.13) | collective-permute-done | bytes 262176 | tf_op jit(solution)/shard_map/ppermute | solution.py:205
  41.2 0.7 %collective-permute-start.14 = (f32[128,256]{1,0:T(8,128)S(1)}, f32[128,256]{1,0:T(8,128)S(1)}, u32[]{:S(2)}, u32[]{:S(2)}) collective-permute-start(f32[128,256]{1,0:T(8,128)S(1)} %get-tuple-element.29), channel_id=1, source_target_pairs={{1,3},{3,1},{5,7},{7,5},{9,11},{11,9},{13,15},{15,13},{17,19},{19,... | collective-permute-start | bytes 393224 | tf_op jit(solution)/shard_map/ppermute | solution.py:212
  41.9 2.0 %collective-permute-start.12 = (f32[128,256]{1,0:T(8,128)S(1)}, f32[128,256]{1,0:T(8,128)S(1)}, u32[]{:S(2)}, u32[]{:S(2)}) collective-permute-start(f32[128,256]{1,0:T(8,128)S(1)} %get-tuple-element.26), channel_id=1, source_target_pairs={{0,1},{1,0},{2,3},{3,2},{4,5},{5,4},{6,7},{7,6},{8,9},{9,8},{10,11... | collective-permute-start | bytes 393224 | tf_op jit(solution)/shard_map/ppermute | solution.py:202
  43.9 0.0 collective-permute-done.14.came_ref
  43.9 0.7 %collective-permute-start.15 = (f32[32,256]{1,0:T(8,128)S(1)}, f32[32,256]{1,0:T(8,128)S(1)}, u32[]{:S(2)}, u32[]{:S(2)}) collective-permute-start(f32[32,256]{1,0:T(8,128)S(1)} %get-tuple-element.31), channel_id=1, source_target_pairs={{1,5},{3,7},{5,1},{7,3},{9,13},{11,15},{13,9},{15,11},{17,21},{19,... | collective-permute-start | bytes 98312 | tf_op jit(solution)/shard_map/ppermute | solution.py:212
  44.6 0.7 %collective-permute-start.16 = (f32[32,256]{1,0:T(8,128)S(1)}, f32[32,256]{1,0:T(8,128)S(1)}, u32[]{:S(2)}, u32[]{:S(2)}) collective-permute-start(f32[32,256]{1,0:T(8,128)S(1)} %get-tuple-element.32), channel_id=1, source_target_pairs={{1,9},{3,11},{5,13},{7,15},{9,1},{11,3},{13,5},{15,7},{17,25},{19,... | collective-permute-start | bytes 98312 | tf_op jit(solution)/shard_map/ppermute | solution.py:212
  45.3 0.7 %collective-permute-start.17 = (f32[32,256]{1,0:T(8,128)S(1)}, f32[32,256]{1,0:T(8,128)S(1)}, u32[]{:S(2)}, u32[]{:S(2)}) collective-permute-start(f32[32,256]{1,0:T(8,128)S(1)} %get-tuple-element.33), channel_id=1, source_target_pairs={{1,13},{3,15},{5,9},{7,11},{9,5},{11,7},{13,1},{15,3},{17,29},{19,... | collective-permute-start | bytes 98312 | tf_op jit(solution)/shard_map/ppermute | solution.py:212
  46.0 0.0 collective-permute-done.15.refs_1_
  46.0 0.0 collective-permute-done.16.refs_2_
  46.0 0.0 collective-permute-done.17.refs_3_
  46.0 1.3 %collective-permute-start.18 = (f32[32,256]{1,0:T(8,128)S(1)}, f32[32,256]{1,0:T(8,128)S(1)}, u32[]{:S(2)}, u32[]{:S(2)}) collective-permute-start(f32[32,256]{1,0:T(8,128)S(1)} %last_sums.1.mine_ref), channel_id=1, source_target_pairs={{1,0},{3,2},{5,4},{7,6},{9,8},{11,10},{13,12},{15,14},{17,16},{19,... | collective-permute-start | bytes 98312 | tf_op jit(solution)/shard_map/ppermute | solution.py:205
  47.3 0.0 collective-permute-done.12.came_ref
  47.3 0.7 %last_scores.1 = f32[128,256]{1,0:T(8,128)} custom-call(s32[1,256]{1,0:T(1,128)S(1)} %bitcast.11, f32[128,256]{1,0:T(8,128)S(1)} %get-tuple-element.25.keep_ref, f32[128,256]{1,0:T(8,128)S(1)} %collective-permute-done.12.came_ref), custom_call_target="tpu_custom_call" | custom-call | tf_op jit(solution)/shard_map/last_scores/pallas_call | solution.py:215
  48.0 13.4 %collective-permute-done.18.theirs_ref = f32[32,256]{1,0:T(8,128)S(1)} collective-permute-done((f32[32,256]{1,0:T(8,128)S(1)}, f32[32,256]{1,0:T(8,128)S(1)}, u32[]{:S(2)}, u32[]{:S(2)}) %collective-permute-start.18) | collective-permute-done | bytes 32800 | tf_op jit(solution)/shard_map/ppermute | solution.py:205
  61.5 0.6 last_hubs.1
  (6 shorter events, 0.1 us)
Async XLA Ops:
  0.6 7.8 %copy-start = (s32[256]{0:T(256)S(1)}, s32[256]{0:T(256)}, u32[]{:S(2)}) copy-start(s32[256]{0:T(256)} %param.9) | copy-start | bytes 3076
  4.6 3.8 %collective-permute-start.1 = (f32[256,256]{1,0:T(8,128)S(1)}, f32[256,256]{1,0:T(8,128)S(1)}, u32[]{:S(2)}, u32[]{:S(2)}) collective-permute-start(f32[256,256]{1,0:T(8,128)S(1)} %get-tuple-element.20.mine_ref), channel_id=1, source_target_pairs={{0,1},{2,3},{4,5},{6,7},{8,9},{10,11},{12,13},{14,15},{16,17},{18,... | collective-permute-start | bytes 786440 | tf_op jit(solution)/shard_map/ppermute | solution.py:205
  7.0 1.4 %collective-permute-start = (f32[128,256]{1,0:T(8,128)S(1)}, f32[128,256]{1,0:T(8,128)S(1)}, u32[]{:S(2)}, u32[]{:S(2)}) collective-permute-start(f32[128,256]{1,0:T(8,128)S(1)} %get-tuple-element.19), channel_id=1, source_target_pairs={{0,1},{1,0},{2,3},{3,2},{4,5},{5,4},{6,7},{7,6},{8,9},{9,8},{10,11... | collective-permute-start | bytes 393224 | tf_op jit(solution)/shard_map/ppermute | solution.py:202
  8.5 5.8 %collective-permute-start.6 = (f32[128,256]{1,0:T(8,128)S(1)}, f32[128,256]{1,0:T(8,128)S(1)}, u32[]{:S(2)}, u32[]{:S(2)}) collective-permute-start(f32[128,256]{1,0:T(8,128)S(1)} %get-tuple-element.23), channel_id=1, source_target_pairs={{1,3},{3,1},{5,7},{7,5},{9,11},{11,9},{13,15},{15,13},{17,19},{19,... | collective-permute-start | bytes 393224 | tf_op jit(solution)/shard_map/ppermute | solution.py:212
  9.1 6.8 %collective-permute-start.4 = (bf16[128,256]{1,0:T(8,128)(2,1)S(1)}, bf16[128,256]{1,0:T(8,128)(2,1)S(1)}, u32[]{:S(2)}, u32[]{:S(2)}) collective-permute-start(bf16[128,256]{1,0:T(8,128)(2,1)S(1)} %get-tuple-element.21.refs_0_), channel_id=1, source_target_pairs={{0,12},{2,14},{4,8},{6,10},{8,4},{10,6},{12,0},{14,2},{1,13},{3,15... | collective-permute-start | bytes 196616 | tf_op jit(solution)/shard_map/ppermute | solution.py:208
  13.6 6.6 %collective-permute-start.3 = (bf16[128,256]{1,0:T(8,128)(2,1)S(1)}, bf16[128,256]{1,0:T(8,128)(2,1)S(1)}, u32[]{:S(2)}, u32[]{:S(2)}) collective-permute-start(bf16[128,256]{1,0:T(8,128)(2,1)S(1)} %get-tuple-element.21.refs_0_), channel_id=1, source_target_pairs={{0,8},{2,10},{4,12},{6,14},{8,0},{10,2},{12,4},{14,6},{1,9},{3,11}... | collective-permute-start | bytes 196616 | tf_op jit(solution)/shard_map/ppermute | solution.py:208
  13.6 6.6 %collective-permute-start.2 = (bf16[128,256]{1,0:T(8,128)(2,1)S(1)}, bf16[128,256]{1,0:T(8,128)(2,1)S(1)}, u32[]{:S(2)}, u32[]{:S(2)}) collective-permute-start(bf16[128,256]{1,0:T(8,128)(2,1)S(1)} %get-tuple-element.21.refs_0_), channel_id=1, source_target_pairs={{0,4},{2,6},{4,0},{6,2},{8,12},{10,14},{12,8},{14,10},{1,5},{3,7},... | collective-permute-start | bytes 196616 | tf_op jit(solution)/shard_map/ppermute | solution.py:208
  14.3 7.2 %collective-permute-start.9 = (f32[128,256]{1,0:T(8,128)S(1)}, f32[128,256]{1,0:T(8,128)S(1)}, u32[]{:S(2)}, u32[]{:S(2)}) collective-permute-start(f32[128,256]{1,0:T(8,128)S(1)} %plane_sum.1.refs_0_), channel_id=1, source_target_pairs={{1,13},{3,15},{5,9},{7,11},{9,5},{11,7},{13,1},{15,3},{17,29},{19,... | collective-permute-start | bytes 393224 | tf_op jit(solution)/shard_map/ppermute | solution.py:212
  15.0 6.6 %collective-permute-start.8 = (f32[128,256]{1,0:T(8,128)S(1)}, f32[128,256]{1,0:T(8,128)S(1)}, u32[]{:S(2)}, u32[]{:S(2)}) collective-permute-start(f32[128,256]{1,0:T(8,128)S(1)} %plane_sum.1.refs_0_), channel_id=1, source_target_pairs={{1,9},{3,11},{5,13},{7,15},{9,1},{11,3},{13,5},{15,7},{17,25},{19,... | collective-permute-start | bytes 393224 | tf_op jit(solution)/shard_map/ppermute | solution.py:212
  16.0 5.5 %collective-permute-start.7 = (f32[128,256]{1,0:T(8,128)S(1)}, f32[128,256]{1,0:T(8,128)S(1)}, u32[]{:S(2)}, u32[]{:S(2)}) collective-permute-start(f32[128,256]{1,0:T(8,128)S(1)} %plane_sum.1.refs_0_), channel_id=1, source_target_pairs={{1,5},{3,7},{5,1},{7,3},{9,13},{11,15},{13,9},{15,11},{17,21},{19,... | collective-permute-start | bytes 393224 | tf_op jit(solution)/shard_map/ppermute | solution.py:212
  20.3 6.4 %collective-permute-start.5 = (bf16[4,128,256]{2,1,0:T(8,128)(2,1)S(1)}, bf16[4,128,256]{2,1,0:T(8,128)(2,1)S(1)}, u32[]{:S(2)}, u32[]{:S(2)}) collective-permute-start(bf16[4,128,256]{2,1,0:T(8,128)(2,1)S(1)} %join_rows.1), channel_id=1, source_target_pairs={{0,2},{2,0},{4,6},{6,4},{8,10},{10,8},{12,14},{14,12},{1,3},{3,1},... | collective-permute-start | bytes 786440 | tf_op jit(solution)/shard_map/ppermute | solution.py:208
  21.7 0.7 %collective-permute-start.10 = (bf16[128,256]{1,0:T(8,128)(2,1)S(1)}, bf16[128,256]{1,0:T(8,128)(2,1)S(1)}, u32[]{:S(2)}, u32[]{:S(2)}) collective-permute-start(bf16[128,256]{1,0:T(8,128)(2,1)S(1)} %hub_sums.1.mine_ref), channel_id=1, source_target_pairs={{1,3},{3,1},{5,7},{7,5},{9,11},{11,9},{13,15},{15,13},{17,19},{19,... | collective-permute-start | bytes 196616 | tf_op jit(solution)/shard_map/ppermute | solution.py:212
  22.4 14.7 %collective-permute-start.11 = (bf16[256,256]{1,0:T(8,128)(2,1)S(1)}, bf16[256,256]{1,0:T(8,128)(2,1)S(1)}, u32[]{:S(2)}, u32[]{:S(2)}) collective-permute-start(bf16[256,256]{1,0:T(8,128)(2,1)S(1)} %join_sides.1.refs_5_), channel_id=1, source_target_pairs={{1,0},{3,2},{5,4},{7,6},{9,8},{11,10},{13,12},{15,14},{17,16},{19,... | collective-permute-start | bytes 393224 | tf_op jit(solution)/shard_map/ppermute | solution.py:205
  38.0 3.2 %collective-permute-start.13 = (f32[256,256]{1,0:T(8,128)S(1)}, f32[256,256]{1,0:T(8,128)S(1)}, u32[]{:S(2)}, u32[]{:S(2)}) collective-permute-start(f32[256,256]{1,0:T(8,128)S(1)} %get-tuple-element.27.mine_ref), channel_id=1, source_target_pairs={{0,1},{2,3},{4,5},{6,7},{8,9},{10,11},{12,13},{14,15},{16,17},{18,... | collective-permute-start | bytes 786440 | tf_op jit(solution)/shard_map/ppermute | solution.py:205
  41.2 2.7 %collective-permute-start.14 = (f32[128,256]{1,0:T(8,128)S(1)}, f32[128,256]{1,0:T(8,128)S(1)}, u32[]{:S(2)}, u32[]{:S(2)}) collective-permute-start(f32[128,256]{1,0:T(8,128)S(1)} %get-tuple-element.29), channel_id=1, source_target_pairs={{1,3},{3,1},{5,7},{7,5},{9,11},{11,9},{13,15},{15,13},{17,19},{19,... | collective-permute-start | bytes 393224 | tf_op jit(solution)/shard_map/ppermute | solution.py:212
  41.9 5.4 %collective-permute-start.12 = (f32[128,256]{1,0:T(8,128)S(1)}, f32[128,256]{1,0:T(8,128)S(1)}, u32[]{:S(2)}, u32[]{:S(2)}) collective-permute-start(f32[128,256]{1,0:T(8,128)S(1)} %get-tuple-element.26), channel_id=1, source_target_pairs={{0,1},{1,0},{2,3},{3,2},{4,5},{5,4},{6,7},{7,6},{8,9},{9,8},{10,11... | collective-permute-start | bytes 393224 | tf_op jit(solution)/shard_map/ppermute | solution.py:202
  43.9 2.0 %collective-permute-start.15 = (f32[32,256]{1,0:T(8,128)S(1)}, f32[32,256]{1,0:T(8,128)S(1)}, u32[]{:S(2)}, u32[]{:S(2)}) collective-permute-start(f32[32,256]{1,0:T(8,128)S(1)} %get-tuple-element.31), channel_id=1, source_target_pairs={{1,5},{3,7},{5,1},{7,3},{9,13},{11,15},{13,9},{15,11},{17,21},{19,... | collective-permute-start | bytes 98312 | tf_op jit(solution)/shard_map/ppermute | solution.py:212
  44.6 1.4 %collective-permute-start.16 = (f32[32,256]{1,0:T(8,128)S(1)}, f32[32,256]{1,0:T(8,128)S(1)}, u32[]{:S(2)}, u32[]{:S(2)}) collective-permute-start(f32[32,256]{1,0:T(8,128)S(1)} %get-tuple-element.32), channel_id=1, source_target_pairs={{1,9},{3,11},{5,13},{7,15},{9,1},{11,3},{13,5},{15,7},{17,25},{19,... | collective-permute-start | bytes 98312 | tf_op jit(solution)/shard_map/ppermute | solution.py:212
  45.3 0.7 %collective-permute-start.17 = (f32[32,256]{1,0:T(8,128)S(1)}, f32[32,256]{1,0:T(8,128)S(1)}, u32[]{:S(2)}, u32[]{:S(2)}) collective-permute-start(f32[32,256]{1,0:T(8,128)S(1)} %get-tuple-element.33), channel_id=1, source_target_pairs={{1,13},{3,15},{5,9},{7,11},{9,5},{11,7},{13,1},{15,3},{17,29},{19,... | collective-permute-start | bytes 98312 | tf_op jit(solution)/shard_map/ppermute | solution.py:212
  46.0 15.4 %collective-permute-start.18 = (f32[32,256]{1,0:T(8,128)S(1)}, f32[32,256]{1,0:T(8,128)S(1)}, u32[]{:S(2)}, u32[]{:S(2)}) collective-permute-start(f32[32,256]{1,0:T(8,128)S(1)} %last_sums.1.mine_ref), channel_id=1, source_target_pairs={{1,0},{3,2},{5,4},{7,6},{9,8},{11,10},{13,12},{15,14},{17,16},{19,... | collective-permute-start | bytes 98312 | tf_op jit(solution)/shard_map/ppermute | solution.py:205

commit v11 on v10

--- a/solution.py
+++ b/solution.py
@@ -201,14 +201,12 @@
     def other_core(x):
         return lax.ppermute(x, "col", [(0, 1), (1, 0)])
 
-    def to_core(x, core):
-        return lax.ppermute(x, "col", [(1 - core, core)])
-
     def to_partner(x, flip):
         return lax.ppermute(x, "row", [(r, r ^ flip) for r in range(n_row)])
 
     def hub_partner(x, flip):
-        pairs = [(r * n_col + HUB_CORE, (r ^ flip) * n_col + HUB_CORE) for r in range(n_row)]
+        devices = [(r, c) for r in range(n_row) for c in range(n_col)]
+        pairs = [(r * n_col + c, (r ^ flip if c == HUB_CORE else r) * n_col + c) for r, c in devices]
         return lax.ppermute(x, ("row", "col"), pairs)
 
     def call(kernel, name, out_shape, *args, scratch=(), cost=0):
@@ -249,7 +247,7 @@
         own, hold, away = call(
             bind(scores_and_spread_kernel, dims, part), "spread",
             (bf16((VB, width)), f32((part, width)), f32((part, width))),
-            src, keep, other_core(send), hubs, to_core(hubs, HUB_CORE))
+            src, keep, other_core(send), hubs, other_core(hubs))
         away = hub_partner(away, 1)
         blocks = [own] + [to_partner(own, X * k) for k in range(1, n_z)]
         plane = call(plane_kernel, "plane_sum", f32((part, width)), hold, away)
@@ -260,15 +258,15 @@
         mine = call(side_kernel, "join_sides", bf16((H, width)), mine, hub_partner(mine, 1))
         send, keep, hubs = call(
             bind(second_kernel, dims), "later_terms", term_shapes,
-            *blocks, across, mine, to_core(mine, 1 - HUB_CORE), dense, scratch=product_scratch)
+            *blocks, across, mine, other_core(mine), dense, scratch=product_scratch)
     hold, away = call(bind(spread_kernel, share), "last_spread", (f32((part, width)),) * 2,
-                      hubs, to_core(hubs, HUB_CORE))
+                      hubs, other_core(hubs))
     pieces = call(pieces_kernel, "hub_pieces", (f32((share, width)),) * n_z, hold, hub_partner(away, 1))
     pieces = [pieces[0]] + [hub_partner(pieces[k], X * k) for k in range(1, n_z)]
     scores = call(bind(scores_kernel, dims), "last_scores", f32((VB, width)), src, keep, other_core(send))
     mine = call(bind(hub_kernel, lambda r: r * share), "last_sums", f32((share, width)), src, *pieces,
                 scratch=[pltpu.VMEM((n_z, share, width), jnp.float32)])
-    hubs = call(last_hubs_kernel, "last_hubs", f32((share // n_col, width)), mine, to_core(mine, 1 - HUB_CORE))
+    hubs = call(last_hubs_kernel, "last_hubs", f32((share // n_col, width)), mine, other_core(mine))
     return scores.reshape(1, 1, VB, width), hubs
 
 

time: 62.5 us -> 57.2 us (0.915)
  waiting for transfers between devices: 33.3 us -> 7.68 us
  starting transfers between devices: 21.5 us -> 41.9 us
    ppermute x2 -> x6, starting transfers between devices: 2.09 us -> 29 us  [other_core(): return lax.ppermute(x, 'col', [(0, 1), (1, 0)])]
    ppermute x4 -> x0, waiting for transfers between devices: 24.9 us -> none  [to_core(): return lax.ppermute(x, 'col', [(1 - core, core)])]
    ppermute x4 -> x0, starting transfers between devices: 7.03 us -> none  [to_core(): return lax.ppermute(x, 'col', [(1 - core, core)])]
    ppermute x4, waiting for transfers between devices: 6.97 us -> 4.06 us  [to_partner(): return lax.ppermute(x, 'row', [(r, r ^ flip) for r in range(n_row)])]
    ppermute x2 -> x6, waiting for transfers between devices: 1.34 us -> 3.59 us  [other_core(): return lax.ppermute(x, 'col', [(0, 1), (1, 0)])]
  transfers between devices with their start and end apart: 19 -> 19, of which waited for: 7 -> 6; matrix products, arithmetic and copies ran while one was open for 0% -> 0% of each run, Pallas kernels for 1% -> 2%
where the time goes in v11:
time: 57.2 us; the launch traced here: 56.8 us
  starting transfers between devices  41.9 us (73%)
  waiting for transfers between devices  7.68 us (13%)
  Pallas kernels  5.8 us (10%)
  between operations  1.47 us (3%)
    ppermute x6, starting transfers between devices, other_core(): return lax.ppermute(x, 'col', [(0, 1), (1, 0)])  29 us
    ppermute x4, starting transfers between devices, to_partner(): return lax.ppermute(x, 'row', [(r, r ^ flip) for r in range(n_row)])  6.86 us
    ppermute x9, starting transfers between devices, hub_partner(): return lax.ppermute(x, ('row', 'col'), pairs)  5.99 us
    ppermute x4, waiting for transfers between devices, to_partner(): return lax.ppermute(x, 'row', [(r, r ^ flip) for r in range(n_row)])  4.06 us
    ppermute x6, waiting for transfers between devices, other_core(): return lax.ppermute(x, 'col', [(0, 1), (1, 0)])  3.59 us
    pallas_call x1, Pallas kernels, fast_body(): pl.pallas_call(bind(first_kernel, dims), out_shape=term_shapes + (bf16((2...  3.29 us
    pallas_call x11, Pallas kernels, call(): pl.pallas_call(kernel, out_shape=out_shape, in_specs=[VMEM] * len(args),...  2.51 us
  transfers between devices with their start and end apart: 19, of which 6 were waited for; matrix products, arithmetic and copies ran while one was open for 0% of the time, Pallas kernels for 2%

profile of v11, /device:TPU:0, one launch (start us, length us, event | category | flops | bytes accessed | tf_op | source)
XLA Modules:
  0.0 56.8 jit_solution(17599962339999118764)
XLA Ops:
  0.6 0.0 copy-start
  1.3 3.3 %first_terms.1 = (f32[128,256]{1,0:T(8,128)S(1)}, f32[128,256]{1,0:T(8,128)S(1)}, f32[256,256]{1,0:T(8,128)S(1)}, bf16[1024,1280]{1,0:T(8,128)(2,1)S(1)}) custom-call(bf16[96,128,128]{2,1,0:T(8,128)(2,1)} %bitcast.12, s32[96]{0:T(128)} %bitcast.14, s32[96]{0:T(128)} %bitcast.15, s32[1]{0:T(128)} %bitcast.6.count_hbm, s32[1,256]{1,0:T(1,128)} %bitcast.7), custom_call_target="tpu_custom_call" | custom-call | tf_op jit(solution)/shard_map/first_terms/pallas_call | solution.py:226
  4.6 0.5 collective-permute-start.1
  5.1 0.1 collective-permute-start
  5.2 1.3 %collective-permute-done.came_ref = f32[128,256]{1,0:T(8,128)S(1)} collective-permute-done((f32[128,256]{1,0:T(8,128)S(1)}, f32[128,256]{1,0:T(8,128)S(1)}, u32[]{:S(2)}, u32[]{:S(2)}) %collective-permute-start) | collective-permute-done | bytes 131104 | tf_op jit(solution)/shard_map/ppermute | solution.py:202
  6.5 0.0 collective-permute-done.1.theirs_ref
  6.5 0.0 copy-done
  6.5 0.1 spread.1
  6.5 0.7 %collective-permute-start.6 = (f32[128,256]{1,0:T(8,128)S(1)}, f32[128,256]{1,0:T(8,128)S(1)}, u32[]{:S(2)}, u32[]{:S(2)}) collective-permute-start(f32[128,256]{1,0:T(8,128)S(1)} %get-tuple-element.23), channel_id=1, source_target_pairs={{0,0},{1,3},{2,2},{3,1},{4,4},{5,7},{6,6},{7,5},{8,8},{9,11},{10,1... | collective-permute-start | bytes 393224 | tf_op jit(solution)/shard_map/ppermute | solution.py:210
  7.2 5.0 %collective-permute-start.4 = (bf16[128,256]{1,0:T(8,128)(2,1)S(1)}, bf16[128,256]{1,0:T(8,128)(2,1)S(1)}, u32[]{:S(2)}, u32[]{:S(2)}) collective-permute-start(bf16[128,256]{1,0:T(8,128)(2,1)S(1)} %get-tuple-element.21.refs_0_), channel_id=1, source_target_pairs={{0,12},{2,14},{4,8},{6,10},{8,4},{10,6},{12,0},{14,2},{1,13},{3,15... | collective-permute-start | bytes 196616 | tf_op jit(solution)/shard_map/ppermute | solution.py:205
  12.2 0.0 collective-permute-start.3
  12.3 0.6 %collective-permute-start.2 = (bf16[128,256]{1,0:T(8,128)(2,1)S(1)}, bf16[128,256]{1,0:T(8,128)(2,1)S(1)}, u32[]{:S(2)}, u32[]{:S(2)}) collective-permute-start(bf16[128,256]{1,0:T(8,128)(2,1)S(1)} %get-tuple-element.21.refs_0_), channel_id=1, source_target_pairs={{0,4},{2,6},{4,0},{6,2},{8,12},{10,14},{12,8},{14,10},{1,5},{3,7},... | collective-permute-start | bytes 196616 | tf_op jit(solution)/shard_map/ppermute | solution.py:205
  12.9 0.0 collective-permute-done.6.came_ref
  12.9 0.7 %collective-permute-start.9 = (f32[128,256]{1,0:T(8,128)S(1)}, f32[128,256]{1,0:T(8,128)S(1)}, u32[]{:S(2)}, u32[]{:S(2)}) collective-permute-start(f32[128,256]{1,0:T(8,128)S(1)} %plane_sum.1.refs_0_), channel_id=1, source_target_pairs={{0,0},{1,13},{2,2},{3,15},{4,4},{5,9},{6,6},{7,11},{8,8},{9,5},{10... | collective-permute-start | bytes 393224 | tf_op jit(solution)/shard_map/ppermute | solution.py:210
  13.6 0.7 %collective-permute-start.8 = (f32[128,256]{1,0:T(8,128)S(1)}, f32[128,256]{1,0:T(8,128)S(1)}, u32[]{:S(2)}, u32[]{:S(2)}) collective-permute-start(f32[128,256]{1,0:T(8,128)S(1)} %plane_sum.1.refs_0_), channel_id=1, source_target_pairs={{0,0},{1,9},{2,2},{3,11},{4,4},{5,13},{6,6},{7,15},{8,8},{9,1},{10... | collective-permute-start | bytes 393224 | tf_op jit(solution)/shard_map/ppermute | solution.py:210
  14.3 0.3 collective-permute-done.4.refs_3_
  14.6 0.7 %collective-permute-start.7 = (f32[128,256]{1,0:T(8,128)S(1)}, f32[128,256]{1,0:T(8,128)S(1)}, u32[]{:S(2)}, u32[]{:S(2)}) collective-permute-start(f32[128,256]{1,0:T(8,128)S(1)} %plane_sum.1.refs_0_), channel_id=1, source_target_pairs={{0,0},{1,5},{2,2},{3,7},{4,4},{5,1},{6,6},{7,3},{8,8},{9,13},{10,1... | collective-permute-start | bytes 393224 | tf_op jit(solution)/shard_map/ppermute | solution.py:210
  15.3 3.7 %collective-permute-done.3.refs_2_ = bf16[128,256]{1,0:T(8,128)(2,1)S(1)} collective-permute-done((bf16[128,256]{1,0:T(8,128)(2,1)S(1)}, bf16[128,256]{1,0:T(8,128)(2,1)S(1)}, u32[]{:S(2)}, u32[]{:S(2)}) %collective-permute-start.3) | collective-permute-done | bytes 65568 | tf_op jit(solution)/shard_map/ppermute | solution.py:205
  19.0 0.0 collective-permute-done.2.refs_1_
  19.0 1.2 %collective-permute-start.5 = (bf16[4,128,256]{2,1,0:T(8,128)(2,1)S(1)}, bf16[4,128,256]{2,1,0:T(8,128)(2,1)S(1)}, u32[]{:S(2)}, u32[]{:S(2)}) collective-permute-start(bf16[4,128,256]{2,1,0:T(8,128)(2,1)S(1)} %join_rows.1), channel_id=1, source_target_pairs={{0,2},{2,0},{4,6},{6,4},{8,10},{10,8},{12,14},{14,12},{1,3},{3,1},... | collective-permute-start | bytes 786440 | tf_op jit(solution)/shard_map/ppermute | solution.py:205
  20.2 0.0 collective-permute-done.9.refs_3_
  20.2 0.0 collective-permute-done.8.refs_2_
  20.2 0.0 collective-permute-done.7.refs_1_
  20.2 0.1 hub_sums.1.mine_ref
  20.3 0.7 %collective-permute-start.10 = (bf16[128,256]{1,0:T(8,128)(2,1)S(1)}, bf16[128,256]{1,0:T(8,128)(2,1)S(1)}, u32[]{:S(2)}, u32[]{:S(2)}) collective-permute-start(bf16[128,256]{1,0:T(8,128)(2,1)S(1)} %hub_sums.1.mine_ref), channel_id=1, source_target_pairs={{0,0},{1,3},{2,2},{3,1},{4,4},{5,7},{6,6},{7,5},{8,8},{9,11},{10,1... | collective-permute-start | bytes 196616 | tf_op jit(solution)/shard_map/ppermute | solution.py:210
  21.0 0.0 collective-permute-done.10.theirs_ref
  21.0 12.4 %collective-permute-start.11 = (bf16[256,256]{1,0:T(8,128)(2,1)S(1)}, bf16[256,256]{1,0:T(8,128)(2,1)S(1)}, u32[]{:S(2)}, u32[]{:S(2)}) collective-permute-start(bf16[256,256]{1,0:T(8,128)(2,1)S(1)} %join_sides.1.refs_5_), channel_id=1, source_target_pairs={{0,1},{1,0},{2,3},{3,2},{4,5},{5,4},{6,7},{7,6},{8,9},{9,8},{10,11... | collective-permute-start | bytes 393224 | tf_op jit(solution)/shard_map/ppermute | solution.py:202
  33.5 0.0 collective-permute-done.5.refs_4_
  33.5 1.0 %collective-permute-done.11.refs_6_ = bf16[256,256]{1,0:T(8,128)(2,1)S(1)} collective-permute-done((bf16[256,256]{1,0:T(8,128)(2,1)S(1)}, bf16[256,256]{1,0:T(8,128)(2,1)S(1)}, u32[]{:S(2)}, u32[]{:S(2)}) %collective-permute-start.11) | collective-permute-done | bytes 131104 | tf_op jit(solution)/shard_map/ppermute | solution.py:202
  34.5 0.9 %later_terms.1 = (f32[128,256]{1,0:T(8,128)S(1)}, f32[128,256]{1,0:T(8,128)S(1)}, f32[256,256]{1,0:T(8,128)S(1)}) custom-call(bf16[128,256]{1,0:T(8,128)(2,1)S(1)} %get-tuple-element.21.refs_0_, bf16[128,256]{1,0:T(8,128)(2,1)S(1)} %collective-permute-done.2.refs_1_, bf16[128,256]{1,0:T(8,128)(2,1)S(1)} %collective-permute-done.3.refs_2_, ...), custom_call_target="tpu_custom_call" | custom-call | tf_op jit(solution)/shard_map/later_terms/pallas_call | solution.py:213
  35.4 0.4 collective-permute-start.13
  35.8 1.2 %collective-permute-done.13.came_ref = f32[256,256]{1,0:T(8,128)S(1)} collective-permute-done((f32[256,256]{1,0:T(8,128)S(1)}, f32[256,256]{1,0:T(8,128)S(1)}, u32[]{:S(2)}, u32[]{:S(2)}) %collective-permute-start.13) | collective-permute-done | bytes 262176 | tf_op jit(solution)/shard_map/ppermute | solution.py:202
  37.0 0.7 %collective-permute-start.14 = (f32[128,256]{1,0:T(8,128)S(1)}, f32[128,256]{1,0:T(8,128)S(1)}, u32[]{:S(2)}, u32[]{:S(2)}) collective-permute-start(f32[128,256]{1,0:T(8,128)S(1)} %get-tuple-element.29), channel_id=1, source_target_pairs={{0,0},{1,3},{2,2},{3,1},{4,4},{5,7},{6,6},{7,5},{8,8},{9,11},{10,1... | collective-permute-start | bytes 393224 | tf_op jit(solution)/shard_map/ppermute | solution.py:210
  37.7 2.0 %collective-permute-start.12 = (f32[128,256]{1,0:T(8,128)S(1)}, f32[128,256]{1,0:T(8,128)S(1)}, u32[]{:S(2)}, u32[]{:S(2)}) collective-permute-start(f32[128,256]{1,0:T(8,128)S(1)} %get-tuple-element.26), channel_id=1, source_target_pairs={{0,1},{1,0},{2,3},{3,2},{4,5},{5,4},{6,7},{7,6},{8,9},{9,8},{10,11... | collective-permute-start | bytes 393224 | tf_op jit(solution)/shard_map/ppermute | solution.py:202
  39.7 0.0 collective-permute-done.14.came_ref
  39.7 0.7 %collective-permute-start.15 = (f32[32,256]{1,0:T(8,128)S(1)}, f32[32,256]{1,0:T(8,128)S(1)}, u32[]{:S(2)}, u32[]{:S(2)}) collective-permute-start(f32[32,256]{1,0:T(8,128)S(1)} %get-tuple-element.31), channel_id=1, source_target_pairs={{0,0},{1,5},{2,2},{3,7},{4,4},{5,1},{6,6},{7,3},{8,8},{9,13},{10,1... | collective-permute-start | bytes 98312 | tf_op jit(solution)/shard_map/ppermute | solution.py:210
  40.4 0.7 %collective-permute-start.16 = (f32[32,256]{1,0:T(8,128)S(1)}, f32[32,256]{1,0:T(8,128)S(1)}, u32[]{:S(2)}, u32[]{:S(2)}) collective-permute-start(f32[32,256]{1,0:T(8,128)S(1)} %get-tuple-element.32), channel_id=1, source_target_pairs={{0,0},{1,9},{2,2},{3,11},{4,4},{5,13},{6,6},{7,15},{8,8},{9,1},{10... | collective-permute-start | bytes 98312 | tf_op jit(solution)/shard_map/ppermute | solution.py:210
  41.1 0.7 %collective-permute-start.17 = (f32[32,256]{1,0:T(8,128)S(1)}, f32[32,256]{1,0:T(8,128)S(1)}, u32[]{:S(2)}, u32[]{:S(2)}) collective-permute-start(f32[32,256]{1,0:T(8,128)S(1)} %get-tuple-element.33), channel_id=1, source_target_pairs={{0,0},{1,13},{2,2},{3,15},{4,4},{5,9},{6,6},{7,11},{8,8},{9,5},{10... | collective-permute-start | bytes 98312 | tf_op jit(solution)/shard_map/ppermute | solution.py:210
  41.7 0.0 collective-permute-done.15.refs_1_
  41.8 0.0 collective-permute-done.16.refs_2_
  41.8 0.0 collective-permute-done.17.refs_3_
  41.8 13.5 %collective-permute-start.18 = (f32[32,256]{1,0:T(8,128)S(1)}, f32[32,256]{1,0:T(8,128)S(1)}, u32[]{:S(2)}, u32[]{:S(2)}) collective-permute-start(f32[32,256]{1,0:T(8,128)S(1)} %last_sums.1.mine_ref), channel_id=1, source_target_pairs={{0,1},{1,0},{2,3},{3,2},{4,5},{5,4},{6,7},{7,6},{8,9},{9,8},{10,11... | collective-permute-start | bytes 98312 | tf_op jit(solution)/shard_map/ppermute | solution.py:202
  55.4 0.0 collective-permute-done.12.came_ref
  55.4 0.7 %last_scores.1 = f32[128,256]{1,0:T(8,128)} custom-call(s32[1,256]{1,0:T(1,128)S(1)} %bitcast.11, f32[128,256]{1,0:T(8,128)S(1)} %get-tuple-element.25.keep_ref, f32[128,256]{1,0:T(8,128)S(1)} %collective-permute-done.12.came_ref), custom_call_target="tpu_custom_call" | custom-call | tf_op jit(solution)/shard_map/last_scores/pallas_call | solution.py:213
  56.1 0.2 collective-permute-done.18.theirs_ref
  56.2 0.6 %last_hubs.1 = f32[16,256]{1,0:T(8,128)} custom-call(f32[32,256]{1,0:T(8,128)S(1)} %last_sums.1.mine_ref, f32[32,256]{1,0:T(8,128)S(1)} %collective-permute-done.18.theirs_ref), custom_call_target="tpu_custom_call" | custom-call | tf_op jit(solution)/shard_map/last_hubs/pallas_call | solution.py:213
  (6 shorter events, 0.1 us)
Async XLA Ops:
  0.6 5.9 %copy-start = (s32[256]{0:T(256)S(1)}, s32[256]{0:T(256)}, u32[]{:S(2)}) copy-start(s32[256]{0:T(256)} %param.9) | copy-start | bytes 3076
  4.6 1.9 %collective-permute-start.1 = (f32[256,256]{1,0:T(8,128)S(1)}, f32[256,256]{1,0:T(8,128)S(1)}, u32[]{:S(2)}, u32[]{:S(2)}) collective-permute-start(f32[256,256]{1,0:T(8,128)S(1)} %get-tuple-element.20.mine_ref), channel_id=1, source_target_pairs={{0,1},{1,0},{2,3},{3,2},{4,5},{5,4},{6,7},{7,6},{8,9},{9,8},{10,11... | collective-permute-start | bytes 786440 | tf_op jit(solution)/shard_map/ppermute | solution.py:202
  5.1 1.3 %collective-permute-start = (f32[128,256]{1,0:T(8,128)S(1)}, f32[128,256]{1,0:T(8,128)S(1)}, u32[]{:S(2)}, u32[]{:S(2)}) collective-permute-start(f32[128,256]{1,0:T(8,128)S(1)} %get-tuple-element.19), channel_id=1, source_target_pairs={{0,1},{1,0},{2,3},{3,2},{4,5},{5,4},{6,7},{7,6},{8,9},{9,8},{10,11... | collective-permute-start | bytes 393224 | tf_op jit(solution)/shard_map/ppermute | solution.py:202
  6.5 6.4 %collective-permute-start.6 = (f32[128,256]{1,0:T(8,128)S(1)}, f32[128,256]{1,0:T(8,128)S(1)}, u32[]{:S(2)}, u32[]{:S(2)}) collective-permute-start(f32[128,256]{1,0:T(8,128)S(1)} %get-tuple-element.23), channel_id=1, source_target_pairs={{0,0},{1,3},{2,2},{3,1},{4,4},{5,7},{6,6},{7,5},{8,8},{9,11},{10,1... | collective-permute-start | bytes 393224 | tf_op jit(solution)/shard_map/ppermute | solution.py:210
  7.2 7.4 %collective-permute-start.4 = (bf16[128,256]{1,0:T(8,128)(2,1)S(1)}, bf16[128,256]{1,0:T(8,128)(2,1)S(1)}, u32[]{:S(2)}, u32[]{:S(2)}) collective-permute-start(bf16[128,256]{1,0:T(8,128)(2,1)S(1)} %get-tuple-element.21.refs_0_), channel_id=1, source_target_pairs={{0,12},{2,14},{4,8},{6,10},{8,4},{10,6},{12,0},{14,2},{1,13},{3,15... | collective-permute-start | bytes 196616 | tf_op jit(solution)/shard_map/ppermute | solution.py:205
  12.2 6.7 %collective-permute-start.3 = (bf16[128,256]{1,0:T(8,128)(2,1)S(1)}, bf16[128,256]{1,0:T(8,128)(2,1)S(1)}, u32[]{:S(2)}, u32[]{:S(2)}) collective-permute-start(bf16[128,256]{1,0:T(8,128)(2,1)S(1)} %get-tuple-element.21.refs_0_), channel_id=1, source_target_pairs={{0,8},{2,10},{4,12},{6,14},{8,0},{10,2},{12,4},{14,6},{1,9},{3,11}... | collective-permute-start | bytes 196616 | tf_op jit(solution)/shard_map/ppermute | solution.py:205
  12.3 6.7 %collective-permute-start.2 = (bf16[128,256]{1,0:T(8,128)(2,1)S(1)}, bf16[128,256]{1,0:T(8,128)(2,1)S(1)}, u32[]{:S(2)}, u32[]{:S(2)}) collective-permute-start(bf16[128,256]{1,0:T(8,128)(2,1)S(1)} %get-tuple-element.21.refs_0_), channel_id=1, source_target_pairs={{0,4},{2,6},{4,0},{6,2},{8,12},{10,14},{12,8},{14,10},{1,5},{3,7},... | collective-permute-start | bytes 196616 | tf_op jit(solution)/shard_map/ppermute | solution.py:205
  12.9 7.3 %collective-permute-start.9 = (f32[128,256]{1,0:T(8,128)S(1)}, f32[128,256]{1,0:T(8,128)S(1)}, u32[]{:S(2)}, u32[]{:S(2)}) collective-permute-start(f32[128,256]{1,0:T(8,128)S(1)} %plane_sum.1.refs_0_), channel_id=1, source_target_pairs={{0,0},{1,13},{2,2},{3,15},{4,4},{5,9},{6,6},{7,11},{8,8},{9,5},{10... | collective-permute-start | bytes 393224 | tf_op jit(solution)/shard_map/ppermute | solution.py:210
  13.6 6.6 %collective-permute-start.8 = (f32[128,256]{1,0:T(8,128)S(1)}, f32[128,256]{1,0:T(8,128)S(1)}, u32[]{:S(2)}, u32[]{:S(2)}) collective-permute-start(f32[128,256]{1,0:T(8,128)S(1)} %plane_sum.1.refs_0_), channel_id=1, source_target_pairs={{0,0},{1,9},{2,2},{3,11},{4,4},{5,13},{6,6},{7,15},{8,8},{9,1},{10... | collective-permute-start | bytes 393224 | tf_op jit(solution)/shard_map/ppermute | solution.py:210
  14.6 5.6 %collective-permute-start.7 = (f32[128,256]{1,0:T(8,128)S(1)}, f32[128,256]{1,0:T(8,128)S(1)}, u32[]{:S(2)}, u32[]{:S(2)}) collective-permute-start(f32[128,256]{1,0:T(8,128)S(1)} %plane_sum.1.refs_0_), channel_id=1, source_target_pairs={{0,0},{1,5},{2,2},{3,7},{4,4},{5,1},{6,6},{7,3},{8,8},{9,13},{10,1... | collective-permute-start | bytes 393224 | tf_op jit(solution)/shard_map/ppermute | solution.py:210
  19.0 14.5 %collective-permute-start.5 = (bf16[4,128,256]{2,1,0:T(8,128)(2,1)S(1)}, bf16[4,128,256]{2,1,0:T(8,128)(2,1)S(1)}, u32[]{:S(2)}, u32[]{:S(2)}) collective-permute-start(bf16[4,128,256]{2,1,0:T(8,128)(2,1)S(1)} %join_rows.1), channel_id=1, source_target_pairs={{0,2},{2,0},{4,6},{6,4},{8,10},{10,8},{12,14},{14,12},{1,3},{3,1},... | collective-permute-start | bytes 786440 | tf_op jit(solution)/shard_map/ppermute | solution.py:205
  20.3 0.7 %collective-permute-start.10 = (bf16[128,256]{1,0:T(8,128)(2,1)S(1)}, bf16[128,256]{1,0:T(8,128)(2,1)S(1)}, u32[]{:S(2)}, u32[]{:S(2)}) collective-permute-start(bf16[128,256]{1,0:T(8,128)(2,1)S(1)} %hub_sums.1.mine_ref), channel_id=1, source_target_pairs={{0,0},{1,3},{2,2},{3,1},{4,4},{5,7},{6,6},{7,5},{8,8},{9,11},{10,1... | collective-permute-start | bytes 196616 | tf_op jit(solution)/shard_map/ppermute | solution.py:210
  21.0 13.4 %collective-permute-start.11 = (bf16[256,256]{1,0:T(8,128)(2,1)S(1)}, bf16[256,256]{1,0:T(8,128)(2,1)S(1)}, u32[]{:S(2)}, u32[]{:S(2)}) collective-permute-start(bf16[256,256]{1,0:T(8,128)(2,1)S(1)} %join_sides.1.refs_5_), channel_id=1, source_target_pairs={{0,1},{1,0},{2,3},{3,2},{4,5},{5,4},{6,7},{7,6},{8,9},{9,8},{10,11... | collective-permute-start | bytes 393224 | tf_op jit(solution)/shard_map/ppermute | solution.py:202
  35.4 1.6 %collective-permute-start.13 = (f32[256,256]{1,0:T(8,128)S(1)}, f32[256,256]{1,0:T(8,128)S(1)}, u32[]{:S(2)}, u32[]{:S(2)}) collective-permute-start(f32[256,256]{1,0:T(8,128)S(1)} %get-tuple-element.27.mine_ref), channel_id=1, source_target_pairs={{0,1},{1,0},{2,3},{3,2},{4,5},{5,4},{6,7},{7,6},{8,9},{9,8},{10,11... | collective-permute-start | bytes 786440 | tf_op jit(solution)/shard_map/ppermute | solution.py:202
  37.0 2.7 %collective-permute-start.14 = (f32[128,256]{1,0:T(8,128)S(1)}, f32[128,256]{1,0:T(8,128)S(1)}, u32[]{:S(2)}, u32[]{:S(2)}) collective-permute-start(f32[128,256]{1,0:T(8,128)S(1)} %get-tuple-element.29), channel_id=1, source_target_pairs={{0,0},{1,3},{2,2},{3,1},{4,4},{5,7},{6,6},{7,5},{8,8},{9,11},{10,1... | collective-permute-start | bytes 393224 | tf_op jit(solution)/shard_map/ppermute | solution.py:210
  37.7 17.7 %collective-permute-start.12 = (f32[128,256]{1,0:T(8,128)S(1)}, f32[128,256]{1,0:T(8,128)S(1)}, u32[]{:S(2)}, u32[]{:S(2)}) collective-permute-start(f32[128,256]{1,0:T(8,128)S(1)} %get-tuple-element.26), channel_id=1, source_target_pairs={{0,1},{1,0},{2,3},{3,2},{4,5},{5,4},{6,7},{7,6},{8,9},{9,8},{10,11... | collective-permute-start | bytes 393224 | tf_op jit(solution)/shard_map/ppermute | solution.py:202
  39.7 2.0 %collective-permute-start.15 = (f32[32,256]{1,0:T(8,128)S(1)}, f32[32,256]{1,0:T(8,128)S(1)}, u32[]{:S(2)}, u32[]{:S(2)}) collective-permute-start(f32[32,256]{1,0:T(8,128)S(1)} %get-tuple-element.31), channel_id=1, source_target_pairs={{0,0},{1,5},{2,2},{3,7},{4,4},{5,1},{6,6},{7,3},{8,8},{9,13},{10,1... | collective-permute-start | bytes 98312 | tf_op jit(solution)/shard_map/ppermute | solution.py:210
  40.4 1.4 %collective-permute-start.16 = (f32[32,256]{1,0:T(8,128)S(1)}, f32[32,256]{1,0:T(8,128)S(1)}, u32[]{:S(2)}, u32[]{:S(2)}) collective-permute-start(f32[32,256]{1,0:T(8,128)S(1)} %get-tuple-element.32), channel_id=1, source_target_pairs={{0,0},{1,9},{2,2},{3,11},{4,4},{5,13},{6,6},{7,15},{8,8},{9,1},{10... | collective-permute-start | bytes 98312 | tf_op jit(solution)/shard_map/ppermute | solution.py:210
  41.1 0.7 %collective-permute-start.17 = (f32[32,256]{1,0:T(8,128)S(1)}, f32[32,256]{1,0:T(8,128)S(1)}, u32[]{:S(2)}, u32[]{:S(2)}) collective-permute-start(f32[32,256]{1,0:T(8,128)S(1)} %get-tuple-element.33), channel_id=1, source_target_pairs={{0,0},{1,13},{2,2},{3,15},{4,4},{5,9},{6,6},{7,11},{8,8},{9,5},{10... | collective-permute-start | bytes 98312 | tf_op jit(solution)/shard_map/ppermute | solution.py:210
  41.8 14.4 %collective-permute-start.18 = (f32[32,256]{1,0:T(8,128)S(1)}, f32[32,256]{1,0:T(8,128)S(1)}, u32[]{:S(2)}, u32[]{:S(2)}) collective-permute-start(f32[32,256]{1,0:T(8,128)S(1)} %last_sums.1.mine_ref), channel_id=1, source_target_pairs={{0,1},{1,0},{2,3},{3,2},{4,5},{5,4},{6,7},{7,6},{8,9},{9,8},{10,11... | collective-permute-start | bytes 98312 | tf_op jit(solution)/shard_map/ppermute | solution.py:202

commit v12 on v9

--- a/solution.py
+++ b/solution.py
@@ -87,19 +87,17 @@
 def second_kernel(dims, *refs):
     n_row, n_col, side = dims
     n_z = n_row // X
-    own, far, (across, far_across, mine_ref, theirs_ref), rest = refs[0], refs[1:n_z], refs[n_z:n_z + 4], refs[n_z + 4:]
-    dense_ref, send_ref, keep_ref, panel, prod = rest
+    blocks, (across, mine_ref, theirs_ref) = refs[:n_z], refs[n_z:n_z + 3]
+    dense_ref, send_ref, keep_ref, panel, prod = refs[n_z + 3:]
     half = H // n_col
     r, c = lax.axis_index("row"), lax.axis_index("col")
 
     def put(owner, block):
         panel[pl.ds(pl.multiple_of(owner * VB, VB), VB), :] = block
 
-    put(r, own[...])
-    put(r ^ 1, across[...])
-    for k in range(1, n_z):
-        put(r ^ (X * k), far[k - 1][...])
-        put(r ^ (X * k) ^ 1, far_across[k - 1])
+    for k in range(n_z):
+        put(r ^ (X * k), blocks[k][...])
+        put(r ^ (X * k) ^ 1, across[k])
     for ref, col in ((mine_ref, c), (theirs_ref, 1 - c)):
         panel[pl.ds(pl.multiple_of(n_row * VB + col * half, half), half), :] = ref[...]
     write_terms(dims, half // n_row, prod, dense_ref, panel, send_ref, keep_ref)
@@ -256,19 +254,18 @@
         own, hold, away = call(
             bind(spread_kernel, dims), "spread",
             (bf16((VB, width)), f32((quarter, width)), f32((quarter, width))),
-            src, keep, came)
+            src, keep, came, cost=1)
         away = other_side(away)
-        far = along_z([own] * n_z)
-        across = other_side(own)
+        blocks = [own] + along_z([own] * n_z)
         plane = call(plane_kernel, "plane_sum", f32((quarter, width)), hold, away, cost=20)
         planes = [plane] + along_z([plane] * n_z)
-        far_across = other_side(call(join_kernel, "join_far", bf16((n_z - 1, VB, width)), *far))
+        across = other_side(call(join_kernel, "join_rows", bf16((n_z, VB, width)), *blocks, cost=2))
         mine = call(bind(hub_kernel, dims), "hub_sums", bf16((quarter, width)), src, *planes,
-                    scratch=[pltpu.VMEM((n_z, quarter, width), jnp.float32)], cost=1)
-        mine = call(side_kernel, "join_sides", bf16((H // n_col, width)), mine, other_side(mine))
+                    scratch=[pltpu.VMEM((n_z, quarter, width), jnp.float32)], cost=2)
+        mine = call(side_kernel, "join_sides", bf16((H // n_col, width)), mine, other_side(mine), cost=1)
         send, keep = call(
             bind(second_kernel, dims), "later_terms", (f32((half, width)), f32((half, width))),
-            own, *far, across, far_across, mine, other_core(mine), dense, scratch=product_scratch)
+            *blocks, across, mine, other_core(mine), dense, scratch=product_scratch)
     came = other_core(send)
     hold, away = call(bind(halves_kernel, dims), "hub_halves",
                       (f32((quarter, width)), f32((quarter, width))), keep, came)

time: 46.4 us -> 46.4 us (level)
  starting transfers between devices: 21.1 us -> 19.2 us
  waiting for transfers between devices: 18 us -> 19.9 us
    ppermute x14 -> x13, starting transfers between devices: 20.3 us -> 18.4 us  [to_partner(): return lax.ppermute(x, 'row', [(r, r ^ flip) for r in range(n_row)])]
    ppermute x14 -> x13, waiting for transfers between devices: 14.8 us -> 16.1 us  [to_partner(): return lax.ppermute(x, 'row', [(r, r ^ flip) for r in range(n_row)])]
    ppermute x3, waiting for transfers between devices: 3.13 us -> 3.77 us  [other_core(): return lax.ppermute(x, 'col', [(0, 1), (1, 0)])]
  transfers between devices with their start and end apart: 17 -> 16, of which waited for: 9 -> 8; matrix products, arithmetic and copies ran while one was open for 0% -> 0% of each run, Pallas kernels for 2% -> 2%
where the time goes in v12:
time: 46.4 us; the launch traced here: 46.3 us
  waiting for transfers between devices  19.9 us (43%)
  starting transfers between devices  19.2 us (41%)
  Pallas kernels  5.86 us (13%)
  between operations  1.37 us (3%)
    ppermute x13, starting transfers between devices, to_partner(): return lax.ppermute(x, 'row', [(r, r ^ flip) for r in range(n_row)])  18.4 us
    ppermute x13, waiting for transfers between devices, to_partner(): return lax.ppermute(x, 'row', [(r, r ^ flip) for r in range(n_row)])  16.1 us
    ppermute x3, waiting for transfers between devices, other_core(): return lax.ppermute(x, 'col', [(0, 1), (1, 0)])  3.77 us
    pallas_call x1, Pallas kernels, fast_body(): pl.pallas_call(bind(first_kernel, dims), out_shape=(f32((half, width)), f...  3.4 us
    pallas_call x10, Pallas kernels, call(): pl.pallas_call(kernel, out_shape=out_shape, in_specs=[VMEM] * len(args),...  2.46 us
  transfers between devices with their start and end apart: 16, of which 8 were waited for; matrix products, arithmetic and copies ran while one was open for 0% of the time, Pallas kernels for 2%

profile of v12, /device:TPU:0, one launch (start us, length us, event | category | flops | bytes accessed | tf_op | source)
XLA Modules:
  0.0 46.3 jit_solution(8772010932002591640)
XLA Ops:
  0.6 0.0 copy-start
  1.3 3.4 %first_terms.1 = (f32[256,256]{1,0:T(8,128)S(1)}, f32[256,256]{1,0:T(8,128)S(1)}, bf16[1024,1280]{1,0:T(8,128)(2,1)S(1)}) custom-call(bf16[96,128,128]{2,1,0:T(8,128)(2,1)} %bitcast.12, s32[96]{0:T(128)} %bitcast.14, s32[96]{0:T(128)} %bitcast.15, s32[1]{0:T(128)} %bitcast.6.count_hbm, s32[1,256]{1,0:T(1,128)} %bitcast.7), custom_call_target="tpu_custom_call" | custom-call | tf_op jit(solution)/shard_map/first_terms/pallas_call | solution.py:231
  4.7 0.5 %collective-permute-start = (f32[256,256]{1,0:T(8,128)S(1)}, f32[256,256]{1,0:T(8,128)S(1)}, u32[]{:S(2)}, u32[]{:S(2)}) collective-permute-start(f32[256,256]{1,0:T(8,128)S(1)} %get-tuple-element.17), channel_id=1, source_target_pairs={{0,1},{1,0},{2,3},{3,2},{4,5},{5,4},{6,7},{7,6},{8,9},{9,8},{10,11... | collective-permute-start | bytes 786440 | tf_op jit(solution)/shard_map/ppermute | solution.py:204
  5.2 1.2 %collective-permute-done.came_ref = f32[256,256]{1,0:T(8,128)S(1)} collective-permute-done((f32[256,256]{1,0:T(8,128)S(1)}, f32[256,256]{1,0:T(8,128)S(1)}, u32[]{:S(2)}, u32[]{:S(2)}) %collective-permute-start) | collective-permute-done | bytes 262176 | tf_op jit(solution)/shard_map/ppermute | solution.py:204
  6.4 0.0 copy-done
  6.4 2.9 %collective-permute-start.5 = (f32[64,256]{1,0:T(8,128)S(1)}, f32[64,256]{1,0:T(8,128)S(1)}, u32[]{:S(2)}, u32[]{:S(2)}) collective-permute-start(f32[64,256]{1,0:T(8,128)S(1)} %get-tuple-element.20), channel_id=1, source_target_pairs={{0,2},{2,0},{4,6},{6,4},{8,10},{10,8},{12,14},{14,12},{1,3},{3,1},... | collective-permute-start | bytes 196616 | tf_op jit(solution)/shard_map/ppermute | solution.py:207
  9.4 3.6 %collective-permute-start.3 = (bf16[128,256]{1,0:T(8,128)(2,1)S(1)}, bf16[128,256]{1,0:T(8,128)(2,1)S(1)}, u32[]{:S(2)}, u32[]{:S(2)}) collective-permute-start(bf16[128,256]{1,0:T(8,128)(2,1)S(1)} %get-tuple-element.18.refs_0_), channel_id=1, source_target_pairs={{0,12},{2,14},{4,8},{6,10},{8,4},{10,6},{12,0},{14,2},{1,13},{3,15... | collective-permute-start | bytes 196616 | tf_op jit(solution)/shard_map/ppermute | solution.py:207
  13.0 0.0 collective-permute-start.2
  13.0 0.8 %collective-permute-start.1 = (bf16[128,256]{1,0:T(8,128)(2,1)S(1)}, bf16[128,256]{1,0:T(8,128)(2,1)S(1)}, u32[]{:S(2)}, u32[]{:S(2)}) collective-permute-start(bf16[128,256]{1,0:T(8,128)(2,1)S(1)} %get-tuple-element.18.refs_0_), channel_id=1, source_target_pairs={{0,4},{2,6},{4,0},{6,2},{8,12},{10,14},{12,8},{14,10},{1,5},{3,7},... | collective-permute-start | bytes 196616 | tf_op jit(solution)/shard_map/ppermute | solution.py:207
  13.8 0.0 collective-permute-done.5.came_ref
  13.8 3.7 %collective-permute-start.8 = (f32[64,256]{1,0:T(8,128)S(1)}, f32[64,256]{1,0:T(8,128)S(1)}, u32[]{:S(2)}, u32[]{:S(2)}) collective-permute-start(f32[64,256]{1,0:T(8,128)S(1)} %plane_sum.1.refs_0_), channel_id=1, source_target_pairs={{0,12},{2,14},{4,8},{6,10},{8,4},{10,6},{12,0},{14,2},{1,13},{3,15... | collective-permute-start | bytes 196616 | tf_op jit(solution)/shard_map/ppermute | solution.py:207
  17.4 0.0 collective-permute-start.7
  17.4 0.0 collective-permute-done.3.refs_3_
  17.4 0.8 %collective-permute-start.6 = (f32[64,256]{1,0:T(8,128)S(1)}, f32[64,256]{1,0:T(8,128)S(1)}, u32[]{:S(2)}, u32[]{:S(2)}) collective-permute-start(f32[64,256]{1,0:T(8,128)S(1)} %plane_sum.1.refs_0_), channel_id=1, source_target_pairs={{0,4},{2,6},{4,0},{6,2},{8,12},{10,14},{12,8},{14,10},{1,5},{3,7},... | collective-permute-start | bytes 196616 | tf_op jit(solution)/shard_map/ppermute | solution.py:207
  18.2 3.0 %collective-permute-done.2.refs_2_ = bf16[128,256]{1,0:T(8,128)(2,1)S(1)} collective-permute-done((bf16[128,256]{1,0:T(8,128)(2,1)S(1)}, bf16[128,256]{1,0:T(8,128)(2,1)S(1)}, u32[]{:S(2)}, u32[]{:S(2)}) %collective-permute-start.2) | collective-permute-done | bytes 65568 | tf_op jit(solution)/shard_map/ppermute | solution.py:207
  21.2 0.0 collective-permute-done.1.refs_1_
  21.3 1.0 %collective-permute-start.4 = (bf16[4,128,256]{2,1,0:T(8,128)(2,1)S(1)}, bf16[4,128,256]{2,1,0:T(8,128)(2,1)S(1)}, u32[]{:S(2)}, u32[]{:S(2)}) collective-permute-start(bf16[4,128,256]{2,1,0:T(8,128)(2,1)S(1)} %join_rows.1), channel_id=1, source_target_pairs={{0,2},{2,0},{4,6},{6,4},{8,10},{10,8},{12,14},{14,12},{1,3},{3,1},... | collective-permute-start | bytes 786440 | tf_op jit(solution)/shard_map/ppermute | solution.py:207
  22.3 0.0 collective-permute-done.8.refs_3_
  22.3 1.9 %collective-permute-done.7.refs_2_ = f32[64,256]{1,0:T(8,128)S(1)} collective-permute-done((f32[64,256]{1,0:T(8,128)S(1)}, f32[64,256]{1,0:T(8,128)S(1)}, u32[]{:S(2)}, u32[]{:S(2)}) %collective-permute-start.7) | collective-permute-done | bytes 65568 | tf_op jit(solution)/shard_map/ppermute | solution.py:207
  24.2 0.0 collective-permute-done.6.refs_1_
  24.2 0.1 hub_sums.1.mine_ref
  24.3 0.6 %collective-permute-start.9 = (bf16[64,256]{1,0:T(8,128)(2,1)S(1)}, bf16[64,256]{1,0:T(8,128)(2,1)S(1)}, u32[]{:S(2)}, u32[]{:S(2)}) collective-permute-start(bf16[64,256]{1,0:T(8,128)(2,1)S(1)} %hub_sums.1.mine_ref), channel_id=1, source_target_pairs={{0,2},{2,0},{4,6},{6,4},{8,10},{10,8},{12,14},{14,12},{1,3},{3,1},... | collective-permute-start | bytes 98312 | tf_op jit(solution)/shard_map/ppermute | solution.py:207
  24.9 4.0 %collective-permute-done.9.theirs_ref = bf16[64,256]{1,0:T(8,128)(2,1)S(1)} collective-permute-done((bf16[64,256]{1,0:T(8,128)(2,1)S(1)}, bf16[64,256]{1,0:T(8,128)(2,1)S(1)}, u32[]{:S(2)}, u32[]{:S(2)}) %collective-permute-start.9) | collective-permute-done | bytes 32800 | tf_op jit(solution)/shard_map/ppermute | solution.py:207
  28.9 0.1 collective-permute-start.10
  28.9 1.2 %collective-permute-done.10.refs_6_ = bf16[128,256]{1,0:T(8,128)(2,1)S(1)} collective-permute-done((bf16[128,256]{1,0:T(8,128)(2,1)S(1)}, bf16[128,256]{1,0:T(8,128)(2,1)S(1)}, u32[]{:S(2)}, u32[]{:S(2)}) %collective-permute-start.10) | collective-permute-done | bytes 65568 | tf_op jit(solution)/shard_map/ppermute | solution.py:204
  30.2 0.0 collective-permute-done.4.refs_4_
  30.2 1.0 %later_terms.1 = (f32[256,256]{1,0:T(8,128)S(1)}, f32[256,256]{1,0:T(8,128)S(1)}) custom-call(bf16[128,256]{1,0:T(8,128)(2,1)S(1)} %get-tuple-element.18.refs_0_, bf16[128,256]{1,0:T(8,128)(2,1)S(1)} %collective-permute-done.1.refs_1_, bf16[128,256]{1,0:T(8,128)(2,1)S(1)} %collective-permute-done.2.refs_2_, ...), custom_call_target="tpu_custom_call" | custom-call | tf_op jit(solution)/shard_map/later_terms/pallas_call | solution.py:216
  31.2 0.2 collective-permute-start.11
  31.4 1.4 %collective-permute-done.11.came_ref = f32[256,256]{1,0:T(8,128)S(1)} collective-permute-done((f32[256,256]{1,0:T(8,128)S(1)}, f32[256,256]{1,0:T(8,128)S(1)}, u32[]{:S(2)}, u32[]{:S(2)}) %collective-permute-start.11) | collective-permute-done | bytes 262176 | tf_op jit(solution)/shard_map/ppermute | solution.py:204
  32.8 0.6 %collective-permute-start.12 = (f32[64,256]{1,0:T(8,128)S(1)}, f32[64,256]{1,0:T(8,128)S(1)}, u32[]{:S(2)}, u32[]{:S(2)}) collective-permute-start(f32[64,256]{1,0:T(8,128)S(1)} %get-tuple-element.25), channel_id=1, source_target_pairs={{0,2},{2,0},{4,6},{6,4},{8,10},{10,8},{12,14},{14,12},{1,3},{3,1},... | collective-permute-start | bytes 196616 | tf_op jit(solution)/shard_map/ppermute | solution.py:207
  33.4 3.8 %collective-permute-done.12.came_ref = f32[64,256]{1,0:T(8,128)S(1)} collective-permute-done((f32[64,256]{1,0:T(8,128)S(1)}, f32[64,256]{1,0:T(8,128)S(1)}, u32[]{:S(2)}, u32[]{:S(2)}) %collective-permute-start.12) | collective-permute-done | bytes 65568 | tf_op jit(solution)/shard_map/ppermute | solution.py:207
  37.1 0.1 collective-permute-start.13
  37.2 2.9 %collective-permute-start.14 = (f32[16,256]{1,0:T(8,128)S(1)}, f32[16,256]{1,0:T(8,128)S(1)}, u32[]{:S(2)}, u32[]{:S(2)}) collective-permute-start(f32[16,256]{1,0:T(8,128)S(1)} %get-tuple-element.28), channel_id=1, source_target_pairs={{0,8},{2,10},{4,12},{6,14},{8,0},{10,2},{12,4},{14,6},{1,9},{3,11}... | collective-permute-start | bytes 49160 | tf_op jit(solution)/shard_map/ppermute | solution.py:207
  40.1 1.5 %collective-permute-start.15 = (f32[16,256]{1,0:T(8,128)S(1)}, f32[16,256]{1,0:T(8,128)S(1)}, u32[]{:S(2)}, u32[]{:S(2)}) collective-permute-start(f32[16,256]{1,0:T(8,128)S(1)} %get-tuple-element.29), channel_id=1, source_target_pairs={{0,12},{2,14},{4,8},{6,10},{8,4},{10,6},{12,0},{14,2},{1,13},{3,15... | collective-permute-start | bytes 49160 | tf_op jit(solution)/shard_map/ppermute | solution.py:207
  41.6 0.7 %last_scores.1 = f32[128,256]{1,0:T(8,128)} custom-call(s32[1,256]{1,0:T(1,128)S(1)} %bitcast.10, f32[256,256]{1,0:T(8,128)S(1)} %get-tuple-element.22.keep_ref, f32[256,256]{1,0:T(8,128)S(1)} %collective-permute-done.11.came_ref), custom_call_target="tpu_custom_call" | custom-call | tf_op jit(solution)/shard_map/last_scores/pallas_call | solution.py:216
  42.3 0.0 collective-permute-done.13.refs_1_
  42.3 0.0 collective-permute-done.14.refs_2_
  42.3 3.4 %collective-permute-done.15.refs_3_ = f32[16,256]{1,0:T(8,128)S(1)} collective-permute-done((f32[16,256]{1,0:T(8,128)S(1)}, f32[16,256]{1,0:T(8,128)S(1)}, u32[]{:S(2)}, u32[]{:S(2)}) %collective-permute-start.15) | collective-permute-done | bytes 16416 | tf_op jit(solution)/shard_map/ppermute | solution.py:207
  45.7 0.6 %last_hubs.1 = f32[16,256]{1,0:T(8,128)} custom-call(s32[1,256]{1,0:T(1,128)S(1)} %bitcast.11, f32[16,256]{1,0:T(8,128)S(1)} %get-tuple-element.26.refs_0_, f32[16,256]{1,0:T(8,128)S(1)} %collective-permute-done.13.refs_1_, f32[16,256]{1,0:T(8,128)S(1)} %collective-permute-done.14.refs_2_, f32[16,256]{1,0:T(8,128)S(1)} %collective-permute-done.15.refs_3_), custom_call_target="tpu_custom_call" | custom-call | tf_op jit(solution)/shard_map/last_hubs/pallas_call | solution.py:216
  (6 shorter events, 0.1 us)
Async XLA Ops:
  0.6 5.8 %copy-start = (s32[256]{0:T(256)S(1)}, s32[256]{0:T(256)}, u32[]{:S(2)}) copy-start(s32[256]{0:T(256)} %param.9) | copy-start | bytes 3076
  4.7 1.7 %collective-permute-start = (f32[256,256]{1,0:T(8,128)S(1)}, f32[256,256]{1,0:T(8,128)S(1)}, u32[]{:S(2)}, u32[]{:S(2)}) collective-permute-start(f32[256,256]{1,0:T(8,128)S(1)} %get-tuple-element.17), channel_id=1, source_target_pairs={{0,1},{1,0},{2,3},{3,2},{4,5},{5,4},{6,7},{7,6},{8,9},{9,8},{10,11... | collective-permute-start | bytes 786440 | tf_op jit(solution)/shard_map/ppermute | solution.py:204
  6.4 7.3 %collective-permute-start.5 = (f32[64,256]{1,0:T(8,128)S(1)}, f32[64,256]{1,0:T(8,128)S(1)}, u32[]{:S(2)}, u32[]{:S(2)}) collective-permute-start(f32[64,256]{1,0:T(8,128)S(1)} %get-tuple-element.20), channel_id=1, source_target_pairs={{0,2},{2,0},{4,6},{6,4},{8,10},{10,8},{12,14},{14,12},{1,3},{3,1},... | collective-permute-start | bytes 196616 | tf_op jit(solution)/shard_map/ppermute | solution.py:207
  9.4 8.1 %collective-permute-start.3 = (bf16[128,256]{1,0:T(8,128)(2,1)S(1)}, bf16[128,256]{1,0:T(8,128)(2,1)S(1)}, u32[]{:S(2)}, u32[]{:S(2)}) collective-permute-start(bf16[128,256]{1,0:T(8,128)(2,1)S(1)} %get-tuple-element.18.refs_0_), channel_id=1, source_target_pairs={{0,12},{2,14},{4,8},{6,10},{8,4},{10,6},{12,0},{14,2},{1,13},{3,15... | collective-permute-start | bytes 196616 | tf_op jit(solution)/shard_map/ppermute | solution.py:207
  13.0 8.3 %collective-permute-start.2 = (bf16[128,256]{1,0:T(8,128)(2,1)S(1)}, bf16[128,256]{1,0:T(8,128)(2,1)S(1)}, u32[]{:S(2)}, u32[]{:S(2)}) collective-permute-start(bf16[128,256]{1,0:T(8,128)(2,1)S(1)} %get-tuple-element.18.refs_0_), channel_id=1, source_target_pairs={{0,8},{2,10},{4,12},{6,14},{8,0},{10,2},{12,4},{14,6},{1,9},{3,11}... | collective-permute-start | bytes 196616 | tf_op jit(solution)/shard_map/ppermute | solution.py:207
  13.0 8.3 %collective-permute-start.1 = (bf16[128,256]{1,0:T(8,128)(2,1)S(1)}, bf16[128,256]{1,0:T(8,128)(2,1)S(1)}, u32[]{:S(2)}, u32[]{:S(2)}) collective-permute-start(bf16[128,256]{1,0:T(8,128)(2,1)S(1)} %get-tuple-element.18.refs_0_), channel_id=1, source_target_pairs={{0,4},{2,6},{4,0},{6,2},{8,12},{10,14},{12,8},{14,10},{1,5},{3,7},... | collective-permute-start | bytes 196616 | tf_op jit(solution)/shard_map/ppermute | solution.py:207
  13.8 8.5 %collective-permute-start.8 = (f32[64,256]{1,0:T(8,128)S(1)}, f32[64,256]{1,0:T(8,128)S(1)}, u32[]{:S(2)}, u32[]{:S(2)}) collective-permute-start(f32[64,256]{1,0:T(8,128)S(1)} %plane_sum.1.refs_0_), channel_id=1, source_target_pairs={{0,12},{2,14},{4,8},{6,10},{8,4},{10,6},{12,0},{14,2},{1,13},{3,15... | collective-permute-start | bytes 196616 | tf_op jit(solution)/shard_map/ppermute | solution.py:207
  17.4 6.8 %collective-permute-start.7 = (f32[64,256]{1,0:T(8,128)S(1)}, f32[64,256]{1,0:T(8,128)S(1)}, u32[]{:S(2)}, u32[]{:S(2)}) collective-permute-start(f32[64,256]{1,0:T(8,128)S(1)} %plane_sum.1.refs_0_), channel_id=1, source_target_pairs={{0,8},{2,10},{4,12},{6,14},{8,0},{10,2},{12,4},{14,6},{1,9},{3,11}... | collective-permute-start | bytes 196616 | tf_op jit(solution)/shard_map/ppermute | solution.py:207
  17.4 6.8 %collective-permute-start.6 = (f32[64,256]{1,0:T(8,128)S(1)}, f32[64,256]{1,0:T(8,128)S(1)}, u32[]{:S(2)}, u32[]{:S(2)}) collective-permute-start(f32[64,256]{1,0:T(8,128)S(1)} %plane_sum.1.refs_0_), channel_id=1, source_target_pairs={{0,4},{2,6},{4,0},{6,2},{8,12},{10,14},{12,8},{14,10},{1,5},{3,7},... | collective-permute-start | bytes 196616 | tf_op jit(solution)/shard_map/ppermute | solution.py:207
  21.3 8.9 %collective-permute-start.4 = (bf16[4,128,256]{2,1,0:T(8,128)(2,1)S(1)}, bf16[4,128,256]{2,1,0:T(8,128)(2,1)S(1)}, u32[]{:S(2)}, u32[]{:S(2)}) collective-permute-start(bf16[4,128,256]{2,1,0:T(8,128)(2,1)S(1)} %join_rows.1), channel_id=1, source_target_pairs={{0,2},{2,0},{4,6},{6,4},{8,10},{10,8},{12,14},{14,12},{1,3},{3,1},... | collective-permute-start | bytes 786440 | tf_op jit(solution)/shard_map/ppermute | solution.py:207
  24.3 4.6 %collective-permute-start.9 = (bf16[64,256]{1,0:T(8,128)(2,1)S(1)}, bf16[64,256]{1,0:T(8,128)(2,1)S(1)}, u32[]{:S(2)}, u32[]{:S(2)}) collective-permute-start(bf16[64,256]{1,0:T(8,128)(2,1)S(1)} %hub_sums.1.mine_ref), channel_id=1, source_target_pairs={{0,2},{2,0},{4,6},{6,4},{8,10},{10,8},{12,14},{14,12},{1,3},{3,1},... | collective-permute-start | bytes 98312 | tf_op jit(solution)/shard_map/ppermute | solution.py:207
  28.9 1.3 %collective-permute-start.10 = (bf16[128,256]{1,0:T(8,128)(2,1)S(1)}, bf16[128,256]{1,0:T(8,128)(2,1)S(1)}, u32[]{:S(2)}, u32[]{:S(2)}) collective-permute-start(bf16[128,256]{1,0:T(8,128)(2,1)S(1)} %join_sides.1.refs_5_), channel_id=1, source_target_pairs={{0,1},{1,0},{2,3},{3,2},{4,5},{5,4},{6,7},{7,6},{8,9},{9,8},{10,11... | collective-permute-start | bytes 196616 | tf_op jit(solution)/shard_map/ppermute | solution.py:204
  31.2 1.6 %collective-permute-start.11 = (f32[256,256]{1,0:T(8,128)S(1)}, f32[256,256]{1,0:T(8,128)S(1)}, u32[]{:S(2)}, u32[]{:S(2)}) collective-permute-start(f32[256,256]{1,0:T(8,128)S(1)} %get-tuple-element.23), channel_id=1, source_target_pairs={{0,1},{1,0},{2,3},{3,2},{4,5},{5,4},{6,7},{7,6},{8,9},{9,8},{10,11... | collective-permute-start | bytes 786440 | tf_op jit(solution)/shard_map/ppermute | solution.py:204
  32.8 4.3 %collective-permute-start.12 = (f32[64,256]{1,0:T(8,128)S(1)}, f32[64,256]{1,0:T(8,128)S(1)}, u32[]{:S(2)}, u32[]{:S(2)}) collective-permute-start(f32[64,256]{1,0:T(8,128)S(1)} %get-tuple-element.25), channel_id=1, source_target_pairs={{0,2},{2,0},{4,6},{6,4},{8,10},{10,8},{12,14},{14,12},{1,3},{3,1},... | collective-permute-start | bytes 196616 | tf_op jit(solution)/shard_map/ppermute | solution.py:207
  37.1 5.2 %collective-permute-start.13 = (f32[16,256]{1,0:T(8,128)S(1)}, f32[16,256]{1,0:T(8,128)S(1)}, u32[]{:S(2)}, u32[]{:S(2)}) collective-permute-start(f32[16,256]{1,0:T(8,128)S(1)} %get-tuple-element.27), channel_id=1, source_target_pairs={{0,4},{2,6},{4,0},{6,2},{8,12},{10,14},{12,8},{14,10},{1,5},{3,7},... | collective-permute-start | bytes 49160 | tf_op jit(solution)/shard_map/ppermute | solution.py:207
  37.2 5.1 %collective-permute-start.14 = (f32[16,256]{1,0:T(8,128)S(1)}, f32[16,256]{1,0:T(8,128)S(1)}, u32[]{:S(2)}, u32[]{:S(2)}) collective-permute-start(f32[16,256]{1,0:T(8,128)S(1)} %get-tuple-element.28), channel_id=1, source_target_pairs={{0,8},{2,10},{4,12},{6,14},{8,0},{10,2},{12,4},{14,6},{1,9},{3,11}... | collective-permute-start | bytes 49160 | tf_op jit(solution)/shard_map/ppermute | solution.py:207
  40.1 5.5 %collective-permute-start.15 = (f32[16,256]{1,0:T(8,128)S(1)}, f32[16,256]{1,0:T(8,128)S(1)}, u32[]{:S(2)}, u32[]{:S(2)}) collective-permute-start(f32[16,256]{1,0:T(8,128)S(1)} %get-tuple-element.29), channel_id=1, source_target_pairs={{0,12},{2,14},{4,8},{6,10},{8,4},{10,6},{12,0},{14,2},{1,13},{3,15... | collective-permute-start | bytes 49160 | tf_op jit(solution)/shard_map/ppermute | solution.py:207

commit v13 on v12

--- a/solution.py
+++ b/solution.py
@@ -152,33 +152,24 @@
         out_ref[pl.ds(pl.multiple_of(place * quarter, quarter), quarter), :] = ref[...]
 
 
-def halves_kernel(dims, keep_ref, came_ref, hold_ref, pass_ref):
-    n_row, n_col, side = dims
-    piece = H // (n_row * n_col)
-    x = lax.axis_index("row") % X
-    for ref, place in ((hold_ref, x), (pass_ref, 1 - x)):
-        for z in range(n_row // X):
-            spot = pl.ds(pl.multiple_of(VB + (z * X + place) * piece, piece), piece)
-            ref[z * piece:(z + 1) * piece] = keep_ref[spot, :] + came_ref[spot, :]
-
-
-def pieces_kernel(hold_ref, came_ref, *outs):
-    z = lax.axis_index("row") // X
-    piece = outs[0].shape[0]
-    for k, out in enumerate(outs):
-        spot = pl.ds(pl.multiple_of((z ^ k) * piece, piece), piece)
-        out[...] = hold_ref[spot, :] + came_ref[spot, :]
+def pieces_kernel(keep_ref, came_ref, parts_ref):
+    piece = parts_ref.shape[1]
+    for k in range(parts_ref.shape[0]):
+        spot = slice(VB + k * piece, VB + (k + 1) * piece)
+        parts_ref[k] = keep_ref[spot, :] + came_ref[spot, :]
 
 
 def last_scores_kernel(dims, src_ref, keep_ref, came_ref, scores_ref):
     scores_ref[...] = own_scores(dims, src_ref, keep_ref, came_ref)
 
 
-def last_hubs_kernel(dims, src_ref, *refs):
-    planes, (out_ref, held) = refs[:-2], refs[-2:]
+def last_hubs_kernel(dims, src_ref, parts_ref, out_ref):
     piece = out_ref.shape[0]
+    summed = parts_ref[0]
+    for k in range(1, parts_ref.shape[0]):
+        summed = summed + parts_ref[k]
     first = (lax.axis_index("row") * dims[1] + lax.axis_index("col")) * piece
-    out_ref[...] = DAMP * sum_planes(planes, held) + 0.15 * one_hot(first, piece, src_ref[...])
+    out_ref[...] = DAMP * summed + 0.15 * one_hot(first, piece, src_ref[...])
 
 
 def fast_body(tiles, tile_row, tile_col, tile_count, sources):
@@ -267,13 +258,10 @@
             bind(second_kernel, dims), "later_terms", (f32((half, width)), f32((half, width))),
             *blocks, across, mine, other_core(mine), dense, scratch=product_scratch)
     came = other_core(send)
-    hold, away = call(bind(halves_kernel, dims), "hub_halves",
-                      (f32((quarter, width)), f32((quarter, width))), keep, came)
-    pieces = call(pieces_kernel, "hub_pieces", (f32((piece, width)),) * n_z, hold, other_side(away))
-    pieces = [pieces[0]] + along_z(pieces)
+    parts = call(pieces_kernel, "hub_pieces", f32((n_row, piece, width)), keep, came)
+    parts = lax.all_to_all(parts, "row", 0, 0)
     scores = call(bind(last_scores_kernel, dims), "last_scores", f32((VB, width)), src, keep, came)
-    hubs = call(bind(last_hubs_kernel, dims), "last_hubs", f32((piece, width)), src, *pieces,
-                scratch=[pltpu.VMEM((n_z, piece, width), jnp.float32)])
+    hubs = call(bind(last_hubs_kernel, dims), "last_hubs", f32((piece, width)), src, parts)
     return scores.reshape(1, 1, VB, width), hubs
 
 

time: 46.4 us -> 45.3 us (0.976)
  starting transfers between devices: 19.2 us -> 17.8 us
  Pallas kernels: 5.86 us -> 6.5 us
  waiting for transfers between devices: 19.9 us -> 19.4 us
    ppermute x13 -> x9, waiting for transfers between devices: 16.1 us -> 8.95 us  [to_partner(): return lax.ppermute(x, 'row', [(r, r ^ flip) for r in range(n_row)])]
    all_to_all x0 -> x1, waiting for transfers between devices: none -> 6.65 us  [fast_body(): parts = lax.all_to_all(parts, 'row', 0, 0)]
    ppermute x13 -> x9, starting transfers between devices: 18.4 us -> 13.4 us  [to_partner(): return lax.ppermute(x, 'row', [(r, r ^ flip) for r in range(n_row)])]
    all_to_all x0 -> x1, starting transfers between devices: none -> 3.63 us  [fast_body(): parts = lax.all_to_all(parts, 'row', 0, 0)]
    pallas_call x10 -> x9, Pallas kernels: 2.46 us -> 3.1 us  [call(): pl.pallas_call(kernel, out_shape=out_shape, in_specs=[VMEM] * len(args),...]
  transfers between devices with their start and end apart: 16 -> 13, of which waited for: 8 -> 7; matrix products, arithmetic and copies ran while one was open for 0% -> 0% of each run, Pallas kernels for 2% -> 2%
where the time goes in v13:
time: 45.3 us; the launch traced here: 45.1 us
  waiting for transfers between devices  19.4 us (43%)
  starting transfers between devices  17.8 us (39%)
  Pallas kernels  6.5 us (14%)
  between operations  1.35 us (3%)
    ppermute x9, starting transfers between devices, to_partner(): return lax.ppermute(x, 'row', [(r, r ^ flip) for r in range(n_row)])  13.4 us
    ppermute x9, waiting for transfers between devices, to_partner(): return lax.ppermute(x, 'row', [(r, r ^ flip) for r in range(n_row)])  8.95 us
    all_to_all x1, waiting for transfers between devices, fast_body(): parts = lax.all_to_all(parts, 'row', 0, 0)  6.65 us
    ppermute x3, waiting for transfers between devices, other_core(): return lax.ppermute(x, 'col', [(0, 1), (1, 0)])  3.77 us
    all_to_all x1, starting transfers between devices, fast_body(): parts = lax.all_to_all(parts, 'row', 0, 0)  3.63 us
    pallas_call x1, Pallas kernels, fast_body(): pl.pallas_call(bind(first_kernel, dims), out_shape=(f32((half, width)), f...  3.4 us
    pallas_call x9, Pallas kernels, call(): pl.pallas_call(kernel, out_shape=out_shape, in_specs=[VMEM] * len(args),...  3.1 us
  transfers between devices with their start and end apart: 13, of which 7 were waited for; matrix products, arithmetic and copies ran while one was open for 0% of the time, Pallas kernels for 2%

profile of v13, /device:TPU:0, one launch (start us, length us, event | category | flops | bytes accessed | tf_op | source)
XLA Modules:
  0.0 45.1 jit_solution(12050436344797686553)
XLA Ops:
  0.6 0.0 copy-start
  1.3 3.4 %first_terms.1 = (f32[256,256]{1,0:T(8,128)S(1)}, f32[256,256]{1,0:T(8,128)S(1)}, bf16[1024,1280]{1,0:T(8,128)(2,1)S(1)}) custom-call(bf16[96,128,128]{2,1,0:T(8,128)(2,1)} %bitcast.12, s32[96]{0:T(128)} %bitcast.14, s32[96]{0:T(128)} %bitcast.15, s32[1]{0:T(128)} %bitcast.6.count_hbm, s32[1,256]{1,0:T(1,128)} %bitcast.7), custom_call_target="tpu_custom_call" | custom-call | tf_op jit(solution)/shard_map/first_terms/pallas_call | solution.py:222
  4.7 0.5 %collective-permute-start = (f32[256,256]{1,0:T(8,128)S(1)}, f32[256,256]{1,0:T(8,128)S(1)}, u32[]{:S(2)}, u32[]{:S(2)}) collective-permute-start(f32[256,256]{1,0:T(8,128)S(1)} %get-tuple-element.11), channel_id=1, source_target_pairs={{0,1},{1,0},{2,3},{3,2},{4,5},{5,4},{6,7},{7,6},{8,9},{9,8},{10,11... | collective-permute-start | bytes 786440 | tf_op jit(solution)/shard_map/ppermute | solution.py:195
  5.2 1.2 %collective-permute-done.came_ref = f32[256,256]{1,0:T(8,128)S(1)} collective-permute-done((f32[256,256]{1,0:T(8,128)S(1)}, f32[256,256]{1,0:T(8,128)S(1)}, u32[]{:S(2)}, u32[]{:S(2)}) %collective-permute-start) | collective-permute-done | bytes 262176 | tf_op jit(solution)/shard_map/ppermute | solution.py:195
  6.4 0.0 copy-done
  6.4 2.9 %collective-permute-start.5 = (f32[64,256]{1,0:T(8,128)S(1)}, f32[64,256]{1,0:T(8,128)S(1)}, u32[]{:S(2)}, u32[]{:S(2)}) collective-permute-start(f32[64,256]{1,0:T(8,128)S(1)} %get-tuple-element.14), channel_id=1, source_target_pairs={{0,2},{2,0},{4,6},{6,4},{8,10},{10,8},{12,14},{14,12},{1,3},{3,1},... | collective-permute-start | bytes 196616 | tf_op jit(solution)/shard_map/ppermute | solution.py:198
  9.4 3.6 %collective-permute-start.3 = (bf16[128,256]{1,0:T(8,128)(2,1)S(1)}, bf16[128,256]{1,0:T(8,128)(2,1)S(1)}, u32[]{:S(2)}, u32[]{:S(2)}) collective-permute-start(bf16[128,256]{1,0:T(8,128)(2,1)S(1)} %get-tuple-element.12.refs_0_), channel_id=1, source_target_pairs={{0,12},{2,14},{4,8},{6,10},{8,4},{10,6},{12,0},{14,2},{1,13},{3,15... | collective-permute-start | bytes 196616 | tf_op jit(solution)/shard_map/ppermute | solution.py:198
  13.0 0.0 collective-permute-start.2
  13.0 0.8 %collective-permute-start.1 = (bf16[128,256]{1,0:T(8,128)(2,1)S(1)}, bf16[128,256]{1,0:T(8,128)(2,1)S(1)}, u32[]{:S(2)}, u32[]{:S(2)}) collective-permute-start(bf16[128,256]{1,0:T(8,128)(2,1)S(1)} %get-tuple-element.12.refs_0_), channel_id=1, source_target_pairs={{0,4},{2,6},{4,0},{6,2},{8,12},{10,14},{12,8},{14,10},{1,5},{3,7},... | collective-permute-start | bytes 196616 | tf_op jit(solution)/shard_map/ppermute | solution.py:198
  13.8 0.0 collective-permute-done.5.came_ref
  13.8 3.7 %collective-permute-start.8 = (f32[64,256]{1,0:T(8,128)S(1)}, f32[64,256]{1,0:T(8,128)S(1)}, u32[]{:S(2)}, u32[]{:S(2)}) collective-permute-start(f32[64,256]{1,0:T(8,128)S(1)} %plane_sum.1.refs_0_), channel_id=1, source_target_pairs={{0,12},{2,14},{4,8},{6,10},{8,4},{10,6},{12,0},{14,2},{1,13},{3,15... | collective-permute-start | bytes 196616 | tf_op jit(solution)/shard_map/ppermute | solution.py:198
  17.4 0.0 collective-permute-start.7
  17.4 0.0 collective-permute-done.3.refs_3_
  17.4 0.8 %collective-permute-start.6 = (f32[64,256]{1,0:T(8,128)S(1)}, f32[64,256]{1,0:T(8,128)S(1)}, u32[]{:S(2)}, u32[]{:S(2)}) collective-permute-start(f32[64,256]{1,0:T(8,128)S(1)} %plane_sum.1.refs_0_), channel_id=1, source_target_pairs={{0,4},{2,6},{4,0},{6,2},{8,12},{10,14},{12,8},{14,10},{1,5},{3,7},... | collective-permute-start | bytes 196616 | tf_op jit(solution)/shard_map/ppermute | solution.py:198
  18.2 3.0 %collective-permute-done.2.refs_2_ = bf16[128,256]{1,0:T(8,128)(2,1)S(1)} collective-permute-done((bf16[128,256]{1,0:T(8,128)(2,1)S(1)}, bf16[128,256]{1,0:T(8,128)(2,1)S(1)}, u32[]{:S(2)}, u32[]{:S(2)}) %collective-permute-start.2) | collective-permute-done | bytes 65568 | tf_op jit(solution)/shard_map/ppermute | solution.py:198
  21.2 0.0 collective-permute-done.1.refs_1_
  21.3 1.0 %collective-permute-start.4 = (bf16[4,128,256]{2,1,0:T(8,128)(2,1)S(1)}, bf16[4,128,256]{2,1,0:T(8,128)(2,1)S(1)}, u32[]{:S(2)}, u32[]{:S(2)}) collective-permute-start(bf16[4,128,256]{2,1,0:T(8,128)(2,1)S(1)} %join_rows.1), channel_id=1, source_target_pairs={{0,2},{2,0},{4,6},{6,4},{8,10},{10,8},{12,14},{14,12},{1,3},{3,1},... | collective-permute-start | bytes 786440 | tf_op jit(solution)/shard_map/ppermute | solution.py:198
  22.3 0.0 collective-permute-done.8.refs_3_
  22.3 1.9 %collective-permute-done.7.refs_2_ = f32[64,256]{1,0:T(8,128)S(1)} collective-permute-done((f32[64,256]{1,0:T(8,128)S(1)}, f32[64,256]{1,0:T(8,128)S(1)}, u32[]{:S(2)}, u32[]{:S(2)}) %collective-permute-start.7) | collective-permute-done | bytes 65568 | tf_op jit(solution)/shard_map/ppermute | solution.py:198
  24.2 0.0 collective-permute-done.6.refs_1_
  24.2 0.1 hub_sums.1.mine_ref
  24.3 0.6 %collective-permute-start.9 = (bf16[64,256]{1,0:T(8,128)(2,1)S(1)}, bf16[64,256]{1,0:T(8,128)(2,1)S(1)}, u32[]{:S(2)}, u32[]{:S(2)}) collective-permute-start(bf16[64,256]{1,0:T(8,128)(2,1)S(1)} %hub_sums.1.mine_ref), channel_id=1, source_target_pairs={{0,2},{2,0},{4,6},{6,4},{8,10},{10,8},{12,14},{14,12},{1,3},{3,1},... | collective-permute-start | bytes 98312 | tf_op jit(solution)/shard_map/ppermute | solution.py:198
  24.9 4.0 %collective-permute-done.9.theirs_ref = bf16[64,256]{1,0:T(8,128)(2,1)S(1)} collective-permute-done((bf16[64,256]{1,0:T(8,128)(2,1)S(1)}, bf16[64,256]{1,0:T(8,128)(2,1)S(1)}, u32[]{:S(2)}, u32[]{:S(2)}) %collective-permute-start.9) | collective-permute-done | bytes 32800 | tf_op jit(solution)/shard_map/ppermute | solution.py:198
  28.9 0.1 collective-permute-start.10
  29.0 1.2 %collective-permute-done.10.refs_6_ = bf16[128,256]{1,0:T(8,128)(2,1)S(1)} collective-permute-done((bf16[128,256]{1,0:T(8,128)(2,1)S(1)}, bf16[128,256]{1,0:T(8,128)(2,1)S(1)}, u32[]{:S(2)}, u32[]{:S(2)}) %collective-permute-start.10) | collective-permute-done | bytes 65568 | tf_op jit(solution)/shard_map/ppermute | solution.py:195
  30.2 0.0 collective-permute-done.4.refs_4_
  30.2 1.0 %later_terms.1 = (f32[256,256]{1,0:T(8,128)S(1)}, f32[256,256]{1,0:T(8,128)S(1)}) custom-call(bf16[128,256]{1,0:T(8,128)(2,1)S(1)} %get-tuple-element.12.refs_0_, bf16[128,256]{1,0:T(8,128)(2,1)S(1)} %collective-permute-done.1.refs_1_, bf16[128,256]{1,0:T(8,128)(2,1)S(1)} %collective-permute-done.2.refs_2_, ...), custom_call_target="tpu_custom_call" | custom-call | tf_op jit(solution)/shard_map/later_terms/pallas_call | solution.py:207
  31.2 0.2 collective-permute-start.11
  31.4 1.4 %collective-permute-done.11.came_ref = f32[256,256]{1,0:T(8,128)S(1)} collective-permute-done((f32[256,256]{1,0:T(8,128)S(1)}, f32[256,256]{1,0:T(8,128)S(1)}, u32[]{:S(2)}, u32[]{:S(2)}) %collective-permute-start.11) | collective-permute-done | bytes 262176 | tf_op jit(solution)/shard_map/ppermute | solution.py:195
  32.8 0.7 %hub_pieces.1 = f32[8,16,256]{2,1,0:T(8,128)} custom-call(f32[256,256]{1,0:T(8,128)S(1)} %get-tuple-element.16.keep_ref, f32[256,256]{1,0:T(8,128)S(1)} %collective-permute-done.11.came_ref), custom_call_target="tpu_custom_call" | custom-call | tf_op jit(solution)/shard_map/hub_pieces/pallas_call | solution.py:207
  33.5 3.6 %all-to-all-start = ((f32[8,16,256]{2,1,0:T(8,128)}), f32[8,16,256]{2,1,0:T(8,128)S(1)}, u32[]{:S(2)}, u32[]{:S(2)}) async-start(f32[8,16,256]{2,1,0:T(8,128)} %hub_pieces.1), calls=%async_computation | async-start | bytes 262144 | tf_op jit(solution)/shard_map/all_to_all | solution.py:262
  37.1 0.7 %last_scores.1 = f32[128,256]{1,0:T(8,128)} custom-call(s32[1,256]{1,0:T(1,128)S(1)} %bitcast.10, f32[256,256]{1,0:T(8,128)S(1)} %get-tuple-element.16.keep_ref, f32[256,256]{1,0:T(8,128)S(1)} %collective-permute-done.11.came_ref), custom_call_target="tpu_custom_call" | custom-call | tf_op jit(solution)/shard_map/last_scores/pallas_call | solution.py:207
  37.8 6.7 %all-to-all-done.parts_ref = f32[8,16,256]{2,1,0:T(8,128)S(1)} async-done(((f32[8,16,256]{2,1,0:T(8,128)}), f32[8,16,256]{2,1,0:T(8,128)S(1)}, u32[]{:S(2)}, u32[]{:S(2)}) %all-to-all-start) | async-done | bytes 131104 | tf_op jit(solution)/shard_map/all_to_all | solution.py:262
  44.4 0.6 %last_hubs.1 = f32[16,256]{1,0:T(8,128)} custom-call(s32[1,256]{1,0:T(1,128)S(1)} %bitcast.11, f32[8,16,256]{2,1,0:T(8,128)S(1)} %all-to-all-done.parts_ref), custom_call_target="tpu_custom_call" | custom-call | tf_op jit(solution)/shard_map/last_hubs/pallas_call | solution.py:207
  (4 shorter events, 0.1 us)
Async XLA Ops:
  0.6 5.8 %copy-start = (s32[256]{0:T(256)S(1)}, s32[256]{0:T(256)}, u32[]{:S(2)}) copy-start(s32[256]{0:T(256)} %param.9) | copy-start | bytes 3076
  4.7 1.7 %collective-permute-start = (f32[256,256]{1,0:T(8,128)S(1)}, f32[256,256]{1,0:T(8,128)S(1)}, u32[]{:S(2)}, u32[]{:S(2)}) collective-permute-start(f32[256,256]{1,0:T(8,128)S(1)} %get-tuple-element.11), channel_id=1, source_target_pairs={{0,1},{1,0},{2,3},{3,2},{4,5},{5,4},{6,7},{7,6},{8,9},{9,8},{10,11... | collective-permute-start | bytes 786440 | tf_op jit(solution)/shard_map/ppermute | solution.py:195
  6.4 7.3 %collective-permute-start.5 = (f32[64,256]{1,0:T(8,128)S(1)}, f32[64,256]{1,0:T(8,128)S(1)}, u32[]{:S(2)}, u32[]{:S(2)}) collective-permute-start(f32[64,256]{1,0:T(8,128)S(1)} %get-tuple-element.14), channel_id=1, source_target_pairs={{0,2},{2,0},{4,6},{6,4},{8,10},{10,8},{12,14},{14,12},{1,3},{3,1},... | collective-permute-start | bytes 196616 | tf_op jit(solution)/shard_map/ppermute | solution.py:198
  9.4 8.1 %collective-permute-start.3 = (bf16[128,256]{1,0:T(8,128)(2,1)S(1)}, bf16[128,256]{1,0:T(8,128)(2,1)S(1)}, u32[]{:S(2)}, u32[]{:S(2)}) collective-permute-start(bf16[128,256]{1,0:T(8,128)(2,1)S(1)} %get-tuple-element.12.refs_0_), channel_id=1, source_target_pairs={{0,12},{2,14},{4,8},{6,10},{8,4},{10,6},{12,0},{14,2},{1,13},{3,15... | collective-permute-start | bytes 196616 | tf_op jit(solution)/shard_map/ppermute | solution.py:198
  13.0 8.3 %collective-permute-start.2 = (bf16[128,256]{1,0:T(8,128)(2,1)S(1)}, bf16[128,256]{1,0:T(8,128)(2,1)S(1)}, u32[]{:S(2)}, u32[]{:S(2)}) collective-permute-start(bf16[128,256]{1,0:T(8,128)(2,1)S(1)} %get-tuple-element.12.refs_0_), channel_id=1, source_target_pairs={{0,8},{2,10},{4,12},{6,14},{8,0},{10,2},{12,4},{14,6},{1,9},{3,11}... | collective-permute-start | bytes 196616 | tf_op jit(solution)/shard_map/ppermute | solution.py:198
  13.0 8.3 %collective-permute-start.1 = (bf16[128,256]{1,0:T(8,128)(2,1)S(1)}, bf16[128,256]{1,0:T(8,128)(2,1)S(1)}, u32[]{:S(2)}, u32[]{:S(2)}) collective-permute-start(bf16[128,256]{1,0:T(8,128)(2,1)S(1)} %get-tuple-element.12.refs_0_), channel_id=1, source_target_pairs={{0,4},{2,6},{4,0},{6,2},{8,12},{10,14},{12,8},{14,10},{1,5},{3,7},... | collective-permute-start | bytes 196616 | tf_op jit(solution)/shard_map/ppermute | solution.py:198
  13.8 8.5 %collective-permute-start.8 = (f32[64,256]{1,0:T(8,128)S(1)}, f32[64,256]{1,0:T(8,128)S(1)}, u32[]{:S(2)}, u32[]{:S(2)}) collective-permute-start(f32[64,256]{1,0:T(8,128)S(1)} %plane_sum.1.refs_0_), channel_id=1, source_target_pairs={{0,12},{2,14},{4,8},{6,10},{8,4},{10,6},{12,0},{14,2},{1,13},{3,15... | collective-permute-start | bytes 196616 | tf_op jit(solution)/shard_map/ppermute | solution.py:198
  17.4 6.8 %collective-permute-start.7 = (f32[64,256]{1,0:T(8,128)S(1)}, f32[64,256]{1,0:T(8,128)S(1)}, u32[]{:S(2)}, u32[]{:S(2)}) collective-permute-start(f32[64,256]{1,0:T(8,128)S(1)} %plane_sum.1.refs_0_), channel_id=1, source_target_pairs={{0,8},{2,10},{4,12},{6,14},{8,0},{10,2},{12,4},{14,6},{1,9},{3,11}... | collective-permute-start | bytes 196616 | tf_op jit(solution)/shard_map/ppermute | solution.py:198
  17.4 6.8 %collective-permute-start.6 = (f32[64,256]{1,0:T(8,128)S(1)}, f32[64,256]{1,0:T(8,128)S(1)}, u32[]{:S(2)}, u32[]{:S(2)}) collective-permute-start(f32[64,256]{1,0:T(8,128)S(1)} %plane_sum.1.refs_0_), channel_id=1, source_target_pairs={{0,4},{2,6},{4,0},{6,2},{8,12},{10,14},{12,8},{14,10},{1,5},{3,7},... | collective-permute-start | bytes 196616 | tf_op jit(solution)/shard_map/ppermute | solution.py:198
  21.3 8.9 %collective-permute-start.4 = (bf16[4,128,256]{2,1,0:T(8,128)(2,1)S(1)}, bf16[4,128,256]{2,1,0:T(8,128)(2,1)S(1)}, u32[]{:S(2)}, u32[]{:S(2)}) collective-permute-start(bf16[4,128,256]{2,1,0:T(8,128)(2,1)S(1)} %join_rows.1), channel_id=1, source_target_pairs={{0,2},{2,0},{4,6},{6,4},{8,10},{10,8},{12,14},{14,12},{1,3},{3,1},... | collective-permute-start | bytes 786440 | tf_op jit(solution)/shard_map/ppermute | solution.py:198
  24.3 4.6 %collective-permute-start.9 = (bf16[64,256]{1,0:T(8,128)(2,1)S(1)}, bf16[64,256]{1,0:T(8,128)(2,1)S(1)}, u32[]{:S(2)}, u32[]{:S(2)}) collective-permute-start(bf16[64,256]{1,0:T(8,128)(2,1)S(1)} %hub_sums.1.mine_ref), channel_id=1, source_target_pairs={{0,2},{2,0},{4,6},{6,4},{8,10},{10,8},{12,14},{14,12},{1,3},{3,1},... | collective-permute-start | bytes 98312 | tf_op jit(solution)/shard_map/ppermute | solution.py:198
  28.9 1.3 %collective-permute-start.10 = (bf16[128,256]{1,0:T(8,128)(2,1)S(1)}, bf16[128,256]{1,0:T(8,128)(2,1)S(1)}, u32[]{:S(2)}, u32[]{:S(2)}) collective-permute-start(bf16[128,256]{1,0:T(8,128)(2,1)S(1)} %join_sides.1.refs_5_), channel_id=1, source_target_pairs={{0,1},{1,0},{2,3},{3,2},{4,5},{5,4},{6,7},{7,6},{8,9},{9,8},{10,11... | collective-permute-start | bytes 196616 | tf_op jit(solution)/shard_map/ppermute | solution.py:195
  31.2 1.6 %collective-permute-start.11 = (f32[256,256]{1,0:T(8,128)S(1)}, f32[256,256]{1,0:T(8,128)S(1)}, u32[]{:S(2)}, u32[]{:S(2)}) collective-permute-start(f32[256,256]{1,0:T(8,128)S(1)} %get-tuple-element.17), channel_id=1, source_target_pairs={{0,1},{1,0},{2,3},{3,2},{4,5},{5,4},{6,7},{7,6},{8,9},{9,8},{10,11... | collective-permute-start | bytes 786440 | tf_op jit(solution)/shard_map/ppermute | solution.py:195
  33.5 11.0 %all-to-all-start = ((f32[8,16,256]{2,1,0:T(8,128)}), f32[8,16,256]{2,1,0:T(8,128)S(1)}, u32[]{:S(2)}, u32[]{:S(2)}) async-start(f32[8,16,256]{2,1,0:T(8,128)} %hub_pieces.1), calls=%async_computation | async-start | bytes 262144 | tf_op jit(solution)/shard_map/all_to_all | solution.py:262

commit v14 on v13

--- a/solution.py
+++ b/solution.py
@@ -30,17 +30,17 @@
     return (ids == src).astype(jnp.float32)
 
 
-def write_terms(dims, block, prod_ref, dense_ref, panel_ref, send_ref, keep_ref):
+def write_terms(dims, prod_ref, dense_ref, panel_ref, send_ref, keep_ref):
     n_row, n_col, side = dims
     rows = dense_ref.shape[0] // 2
+    half = H // n_col
     c = lax.axis_index("col")
     prod = jnp.dot(dense_ref[...], panel_ref[...], preferred_element_type=jnp.float32)
     prod_ref[...] = prod[:rows] + prod[rows:]
     for ref, col in ((keep_ref, c), (send_ref, 1 - c)):
         ref[:VB] = prod_ref[pl.ds(pl.multiple_of(col * VB, VB), VB), :]
-        for k in range(H // n_col // block):
-            start = n_col * VB + (k * n_col + col) * block
-            ref[VB + k * block:VB + (k + 1) * block] = prod_ref[pl.ds(pl.multiple_of(start, block), block), :]
+        if ref.shape[0] > VB:
+            ref[VB:] = prod_ref[pl.ds(pl.multiple_of(n_col * VB + col * half, half), half), :]
 
 
 def first_kernel(dims, tiles_ref, rows_hbm, cols_hbm, count_hbm, src_hbm, send_ref, keep_ref, dense_ref,
@@ -81,14 +81,14 @@
         high = whole.astype(jnp.bfloat16)
         dense_ref[pl.ds(r, side), :] = high
         dense_ref[pl.ds(n_rows + r, side), :] = (whole - high.astype(jnp.float32)).astype(jnp.bfloat16)
-    write_terms(dims, H // n_col, prod, dense_ref, panel, send_ref, keep_ref)
+    write_terms(dims, prod, dense_ref, panel, send_ref, keep_ref)
 
 
 def second_kernel(dims, *refs):
     n_row, n_col, side = dims
     n_z = n_row // X
     blocks, (across, mine_ref, theirs_ref) = refs[:n_z], refs[n_z:n_z + 3]
-    dense_ref, send_ref, keep_ref, panel, prod = refs[n_z + 3:]
+    dense_ref, send_ref, keep_ref, *parts, panel, prod = refs[n_z + 3:]
     half = H // n_col
     r, c = lax.axis_index("row"), lax.axis_index("col")
 
@@ -100,7 +100,9 @@
         put(r ^ (X * k) ^ 1, across[k])
     for ref, col in ((mine_ref, c), (theirs_ref, 1 - c)):
         panel[pl.ds(pl.multiple_of(n_row * VB + col * half, half), half), :] = ref[...]
-    write_terms(dims, half // n_row, prod, dense_ref, panel, send_ref, keep_ref)
+    write_terms(dims, prod, dense_ref, panel, send_ref, keep_ref)
+    for ref in parts:
+        ref[...] = prod[n_col * VB:].reshape(ref.shape)
 
 
 def own_scores(dims, src_ref, keep_ref, came_ref):
@@ -152,13 +154,6 @@
         out_ref[pl.ds(pl.multiple_of(place * quarter, quarter), quarter), :] = ref[...]
 
 
-def pieces_kernel(keep_ref, came_ref, parts_ref):
-    piece = parts_ref.shape[1]
-    for k in range(parts_ref.shape[0]):
-        spot = slice(VB + k * piece, VB + (k + 1) * piece)
-        parts_ref[k] = keep_ref[spot, :] + came_ref[spot, :]
-
-
 def last_scores_kernel(dims, src_ref, keep_ref, came_ref, scores_ref):
     scores_ref[...] = own_scores(dims, src_ref, keep_ref, came_ref)
 
@@ -177,7 +172,8 @@
     width = sources.shape[0]
     n_row = lax.axis_size("row")
     n_col = lax.axis_size("col")
-    piece = H // (n_row * n_col)
+    devices = n_row * n_col
+    piece = H // devices
     dims = (n_row, n_col, side)
     n_rows = n_col * VB + H
     n_cols = n_row * VB + H
@@ -254,13 +250,14 @@
         mine = call(bind(hub_kernel, dims), "hub_sums", bf16((quarter, width)), src, *planes,
                     scratch=[pltpu.VMEM((n_z, quarter, width), jnp.float32)], cost=2)
         mine = call(side_kernel, "join_sides", bf16((H // n_col, width)), mine, other_side(mine), cost=1)
-        send, keep = call(
-            bind(second_kernel, dims), "later_terms", (f32((half, width)), f32((half, width))),
+        last = step + 2 == ITERS
+        rows = VB if last else half
+        pieces = (f32((devices, piece, width)),) if last else ()
+        send, keep, *parts = call(
+            bind(second_kernel, dims), "later_terms", (f32((rows, width)),) * 2 + pieces,
             *blocks, across, mine, other_core(mine), dense, scratch=product_scratch)
-    came = other_core(send)
-    parts = call(pieces_kernel, "hub_pieces", f32((n_row, piece, width)), keep, came)
-    parts = lax.all_to_all(parts, "row", 0, 0)
-    scores = call(bind(last_scores_kernel, dims), "last_scores", f32((VB, width)), src, keep, came)
+    parts = lax.all_to_all(parts[0], ("row", "col"), 0, 0)
+    scores = call(bind(last_scores_kernel, dims), "last_scores", f32((VB, width)), src, keep, other_core(send))
     hubs = call(bind(last_hubs_kernel, dims), "last_hubs", f32((piece, width)), src, parts)
     return scores.reshape(1, 1, VB, width), hubs
 

time: 45.3 us -> 46.5 us (1.026)
  waiting for transfers between devices: 19.4 us -> 20.3 us
    all_to_all x1, waiting for transfers between devices: 6.65 us -> 7.94 us  [fast_body(): parts = lax.all_to_all(parts[0], ('row', 'col'), 0, 0)]
    pallas_call x9 -> x8, Pallas kernels: 3.1 us -> 3.12 us  [call(): pl.pallas_call(kernel, out_shape=out_shape, in_specs=[VMEM] * len(args),...]
where the time goes in v14:
time: 46.5 us; the launch traced here: 46.3 us
  waiting for transfers between devices  20.3 us (44%)
  starting transfers between devices  18.1 us (39%)
  Pallas kernels  6.51 us (14%)
  between operations  1.36 us (3%)
    ppermute x9, starting transfers between devices, to_partner(): return lax.ppermute(x, 'row', [(r, r ^ flip) for r in range(n_row)])  13.4 us
    ppermute x9, waiting for transfers between devices, to_partner(): return lax.ppermute(x, 'row', [(r, r ^ flip) for r in range(n_row)])  8.95 us
    all_to_all x1, waiting for transfers between devices, fast_body(): parts = lax.all_to_all(parts[0], ('row', 'col'), 0, 0)  7.94 us
    all_to_all x1, starting transfers between devices, fast_body(): parts = lax.all_to_all(parts[0], ('row', 'col'), 0, 0)  3.73 us
    ppermute x3, waiting for transfers between devices, other_core(): return lax.ppermute(x, 'col', [(0, 1), (1, 0)])  3.41 us
    pallas_call x1, Pallas kernels, fast_body(): pl.pallas_call(bind(first_kernel, dims), out_shape=(f32((half, width)), f...  3.4 us
    pallas_call x8, Pallas kernels, call(): pl.pallas_call(kernel, out_shape=out_shape, in_specs=[VMEM] * len(args),...  3.12 us
    ppermute x3, starting transfers between devices, other_core(): return lax.ppermute(x, 'col', [(0, 1), (1, 0)])  1.01 us
  transfers between devices with their start and end apart: 13, of which 7 were waited for; matrix products, arithmetic and copies ran while one was open for 0% of the time, Pallas kernels for 2%

profile of v14, /device:TPU:0, one launch (start us, length us, event | category | flops | bytes accessed | tf_op | source)
XLA Modules:
  0.0 46.3 jit_solution(10106454766188158480)
XLA Ops:
  0.6 0.0 copy-start
  1.3 3.4 %first_terms.1 = (f32[256,256]{1,0:T(8,128)S(1)}, f32[256,256]{1,0:T(8,128)S(1)}, bf16[1024,1280]{1,0:T(8,128)(2,1)S(1)}) custom-call(bf16[96,128,128]{2,1,0:T(8,128)(2,1)} %bitcast.12, s32[96]{0:T(128)} %bitcast.14, s32[96]{0:T(128)} %bitcast.15, s32[1]{0:T(128)} %bitcast.6.count_hbm, s32[1,256]{1,0:T(1,128)} %bitcast.7), custom_call_target="tpu_custom_call" | custom-call | tf_op jit(solution)/shard_map/first_terms/pallas_call | solution.py:218
  4.7 0.5 %collective-permute-start = (f32[256,256]{1,0:T(8,128)S(1)}, f32[256,256]{1,0:T(8,128)S(1)}, u32[]{:S(2)}, u32[]{:S(2)}) collective-permute-start(f32[256,256]{1,0:T(8,128)S(1)} %get-tuple-element.12), channel_id=1, source_target_pairs={{0,1},{1,0},{2,3},{3,2},{4,5},{5,4},{6,7},{7,6},{8,9},{9,8},{10,11... | collective-permute-start | bytes 786440 | tf_op jit(solution)/shard_map/ppermute | solution.py:191
  5.2 1.2 %collective-permute-done.came_ref = f32[256,256]{1,0:T(8,128)S(1)} collective-permute-done((f32[256,256]{1,0:T(8,128)S(1)}, f32[256,256]{1,0:T(8,128)S(1)}, u32[]{:S(2)}, u32[]{:S(2)}) %collective-permute-start) | collective-permute-done | bytes 262176 | tf_op jit(solution)/shard_map/ppermute | solution.py:191
  6.4 0.0 copy-done
  6.4 2.9 %collective-permute-start.5 = (f32[64,256]{1,0:T(8,128)S(1)}, f32[64,256]{1,0:T(8,128)S(1)}, u32[]{:S(2)}, u32[]{:S(2)}) collective-permute-start(f32[64,256]{1,0:T(8,128)S(1)} %get-tuple-element.15), channel_id=1, source_target_pairs={{0,2},{2,0},{4,6},{6,4},{8,10},{10,8},{12,14},{14,12},{1,3},{3,1},... | collective-permute-start | bytes 196616 | tf_op jit(solution)/shard_map/ppermute | solution.py:194
  9.4 3.6 %collective-permute-start.3 = (bf16[128,256]{1,0:T(8,128)(2,1)S(1)}, bf16[128,256]{1,0:T(8,128)(2,1)S(1)}, u32[]{:S(2)}, u32[]{:S(2)}) collective-permute-start(bf16[128,256]{1,0:T(8,128)(2,1)S(1)} %get-tuple-element.13.refs_0_), channel_id=1, source_target_pairs={{0,12},{2,14},{4,8},{6,10},{8,4},{10,6},{12,0},{14,2},{1,13},{3,15... | collective-permute-start | bytes 196616 | tf_op jit(solution)/shard_map/ppermute | solution.py:194
  13.0 0.0 collective-permute-start.2
  13.0 0.8 %collective-permute-start.1 = (bf16[128,256]{1,0:T(8,128)(2,1)S(1)}, bf16[128,256]{1,0:T(8,128)(2,1)S(1)}, u32[]{:S(2)}, u32[]{:S(2)}) collective-permute-start(bf16[128,256]{1,0:T(8,128)(2,1)S(1)} %get-tuple-element.13.refs_0_), channel_id=1, source_target_pairs={{0,4},{2,6},{4,0},{6,2},{8,12},{10,14},{12,8},{14,10},{1,5},{3,7},... | collective-permute-start | bytes 196616 | tf_op jit(solution)/shard_map/ppermute | solution.py:194
  13.8 0.0 collective-permute-done.5.came_ref
  13.8 3.7 %collective-permute-start.8 = (f32[64,256]{1,0:T(8,128)S(1)}, f32[64,256]{1,0:T(8,128)S(1)}, u32[]{:S(2)}, u32[]{:S(2)}) collective-permute-start(f32[64,256]{1,0:T(8,128)S(1)} %plane_sum.1.refs_0_), channel_id=1, source_target_pairs={{0,12},{2,14},{4,8},{6,10},{8,4},{10,6},{12,0},{14,2},{1,13},{3,15... | collective-permute-start | bytes 196616 | tf_op jit(solution)/shard_map/ppermute | solution.py:194
  17.4 0.0 collective-permute-start.7
  17.4 0.0 collective-permute-done.3.refs_3_
  17.4 0.8 %collective-permute-start.6 = (f32[64,256]{1,0:T(8,128)S(1)}, f32[64,256]{1,0:T(8,128)S(1)}, u32[]{:S(2)}, u32[]{:S(2)}) collective-permute-start(f32[64,256]{1,0:T(8,128)S(1)} %plane_sum.1.refs_0_), channel_id=1, source_target_pairs={{0,4},{2,6},{4,0},{6,2},{8,12},{10,14},{12,8},{14,10},{1,5},{3,7},... | collective-permute-start | bytes 196616 | tf_op jit(solution)/shard_map/ppermute | solution.py:194
  18.2 3.0 %collective-permute-done.2.refs_2_ = bf16[128,256]{1,0:T(8,128)(2,1)S(1)} collective-permute-done((bf16[128,256]{1,0:T(8,128)(2,1)S(1)}, bf16[128,256]{1,0:T(8,128)(2,1)S(1)}, u32[]{:S(2)}, u32[]{:S(2)}) %collective-permute-start.2) | collective-permute-done | bytes 65568 | tf_op jit(solution)/shard_map/ppermute | solution.py:194
  21.2 0.0 collective-permute-done.1.refs_1_
  21.3 1.0 %collective-permute-start.4 = (bf16[4,128,256]{2,1,0:T(8,128)(2,1)S(1)}, bf16[4,128,256]{2,1,0:T(8,128)(2,1)S(1)}, u32[]{:S(2)}, u32[]{:S(2)}) collective-permute-start(bf16[4,128,256]{2,1,0:T(8,128)(2,1)S(1)} %join_rows.1), channel_id=1, source_target_pairs={{0,2},{2,0},{4,6},{6,4},{8,10},{10,8},{12,14},{14,12},{1,3},{3,1},... | collective-permute-start | bytes 786440 | tf_op jit(solution)/shard_map/ppermute | solution.py:194
  22.3 0.0 collective-permute-done.8.refs_3_
  22.3 1.9 %collective-permute-done.7.refs_2_ = f32[64,256]{1,0:T(8,128)S(1)} collective-permute-done((f32[64,256]{1,0:T(8,128)S(1)}, f32[64,256]{1,0:T(8,128)S(1)}, u32[]{:S(2)}, u32[]{:S(2)}) %collective-permute-start.7) | collective-permute-done | bytes 65568 | tf_op jit(solution)/shard_map/ppermute | solution.py:194
  24.2 0.0 collective-permute-done.6.refs_1_
  24.2 0.1 hub_sums.1.mine_ref
  24.3 0.6 %collective-permute-start.9 = (bf16[64,256]{1,0:T(8,128)(2,1)S(1)}, bf16[64,256]{1,0:T(8,128)(2,1)S(1)}, u32[]{:S(2)}, u32[]{:S(2)}) collective-permute-start(bf16[64,256]{1,0:T(8,128)(2,1)S(1)} %hub_sums.1.mine_ref), channel_id=1, source_target_pairs={{0,2},{2,0},{4,6},{6,4},{8,10},{10,8},{12,14},{14,12},{1,3},{3,1},... | collective-permute-start | bytes 98312 | tf_op jit(solution)/shard_map/ppermute | solution.py:194
  24.9 4.0 %collective-permute-done.9.theirs_ref = bf16[64,256]{1,0:T(8,128)(2,1)S(1)} collective-permute-done((bf16[64,256]{1,0:T(8,128)(2,1)S(1)}, bf16[64,256]{1,0:T(8,128)(2,1)S(1)}, u32[]{:S(2)}, u32[]{:S(2)}) %collective-permute-start.9) | collective-permute-done | bytes 32800 | tf_op jit(solution)/shard_map/ppermute | solution.py:194
  28.9 0.1 collective-permute-start.10
  28.9 1.2 %collective-permute-done.10.refs_6_ = bf16[128,256]{1,0:T(8,128)(2,1)S(1)} collective-permute-done((bf16[128,256]{1,0:T(8,128)(2,1)S(1)}, bf16[128,256]{1,0:T(8,128)(2,1)S(1)}, u32[]{:S(2)}, u32[]{:S(2)}) %collective-permute-start.10) | collective-permute-done | bytes 65568 | tf_op jit(solution)/shard_map/ppermute | solution.py:191
  30.2 0.0 collective-permute-done.4.refs_4_
  30.2 1.7 %later_terms.1 = (f32[128,256]{1,0:T(8,128)S(1)}, f32[128,256]{1,0:T(8,128)S(1)}, f32[16,16,256]{2,1,0:T(8,128)}) custom-call(bf16[128,256]{1,0:T(8,128)(2,1)S(1)} %get-tuple-element.13.refs_0_, bf16[128,256]{1,0:T(8,128)(2,1)S(1)} %collective-permute-done.1.refs_1_, bf16[128,256]{1,0:T(8,128)(2,1)S(1)} %collective-permute-done.2.refs_2_, ...), custom_call_target="tpu_custom_call" | custom-call | tf_op jit(solution)/shard_map/later_terms/pallas_call | solution.py:203
  31.8 3.7 %all-to-all-start = ((f32[16,16,256]{2,1,0:T(8,128)}), f32[16,16,256]{2,1,0:T(8,128)S(1)}, u32[]{:S(2)}, u32[]{:S(2)}) async-start(f32[16,16,256]{2,1,0:T(8,128)} %get-tuple-element.19), calls=%async_computation | async-start | bytes 524288 | tf_op jit(solution)/shard_map/all_to_all | solution.py:259
  35.6 0.4 collective-permute-start.11
  36.0 1.0 %collective-permute-done.11.came_ref = f32[128,256]{1,0:T(8,128)S(1)} collective-permute-done((f32[128,256]{1,0:T(8,128)S(1)}, f32[128,256]{1,0:T(8,128)S(1)}, u32[]{:S(2)}, u32[]{:S(2)}) %collective-permute-start.11) | collective-permute-done | bytes 131104 | tf_op jit(solution)/shard_map/ppermute | solution.py:191
  37.0 0.7 %last_scores.1 = f32[128,256]{1,0:T(8,128)} custom-call(s32[1,256]{1,0:T(1,128)S(1)} %bitcast.10, f32[128,256]{1,0:T(8,128)S(1)} %get-tuple-element.17.keep_ref, f32[128,256]{1,0:T(8,128)S(1)} %collective-permute-done.11.came_ref), custom_call_target="tpu_custom_call" | custom-call | tf_op jit(solution)/shard_map/last_scores/pallas_call | solution.py:203
  37.7 7.9 %all-to-all-done.parts_ref = f32[16,16,256]{2,1,0:T(8,128)S(1)} async-done(((f32[16,16,256]{2,1,0:T(8,128)}), f32[16,16,256]{2,1,0:T(8,128)S(1)}, u32[]{:S(2)}, u32[]{:S(2)}) %all-to-all-start) | async-done | bytes 262176 | tf_op jit(solution)/shard_map/all_to_all | solution.py:259
  45.6 0.6 %last_hubs.1 = f32[16,256]{1,0:T(8,128)} custom-call(s32[1,256]{1,0:T(1,128)S(1)} %bitcast.11, f32[16,16,256]{2,1,0:T(8,128)S(1)} %all-to-all-done.parts_ref), custom_call_target="tpu_custom_call" | custom-call | tf_op jit(solution)/shard_map/last_hubs/pallas_call | solution.py:203
  (4 shorter events, 0.1 us)
Async XLA Ops:
  0.6 5.8 %copy-start = (s32[256]{0:T(256)S(1)}, s32[256]{0:T(256)}, u32[]{:S(2)}) copy-start(s32[256]{0:T(256)} %param.9) | copy-start | bytes 3076
  4.7 1.7 %collective-permute-start = (f32[256,256]{1,0:T(8,128)S(1)}, f32[256,256]{1,0:T(8,128)S(1)}, u32[]{:S(2)}, u32[]{:S(2)}) collective-permute-start(f32[256,256]{1,0:T(8,128)S(1)} %get-tuple-element.12), channel_id=1, source_target_pairs={{0,1},{1,0},{2,3},{3,2},{4,5},{5,4},{6,7},{7,6},{8,9},{9,8},{10,11... | collective-permute-start | bytes 786440 | tf_op jit(solution)/shard_map/ppermute | solution.py:191
  6.4 7.3 %collective-permute-start.5 = (f32[64,256]{1,0:T(8,128)S(1)}, f32[64,256]{1,0:T(8,128)S(1)}, u32[]{:S(2)}, u32[]{:S(2)}) collective-permute-start(f32[64,256]{1,0:T(8,128)S(1)} %get-tuple-element.15), channel_id=1, source_target_pairs={{0,2},{2,0},{4,6},{6,4},{8,10},{10,8},{12,14},{14,12},{1,3},{3,1},... | collective-permute-start | bytes 196616 | tf_op jit(solution)/shard_map/ppermute | solution.py:194
  9.4 8.1 %collective-permute-start.3 = (bf16[128,256]{1,0:T(8,128)(2,1)S(1)}, bf16[128,256]{1,0:T(8,128)(2,1)S(1)}, u32[]{:S(2)}, u32[]{:S(2)}) collective-permute-start(bf16[128,256]{1,0:T(8,128)(2,1)S(1)} %get-tuple-element.13.refs_0_), channel_id=1, source_target_pairs={{0,12},{2,14},{4,8},{6,10},{8,4},{10,6},{12,0},{14,2},{1,13},{3,15... | collective-permute-start | bytes 196616 | tf_op jit(solution)/shard_map/ppermute | solution.py:194
  13.0 8.3 %collective-permute-start.2 = (bf16[128,256]{1,0:T(8,128)(2,1)S(1)}, bf16[128,256]{1,0:T(8,128)(2,1)S(1)}, u32[]{:S(2)}, u32[]{:S(2)}) collective-permute-start(bf16[128,256]{1,0:T(8,128)(2,1)S(1)} %get-tuple-element.13.refs_0_), channel_id=1, source_target_pairs={{0,8},{2,10},{4,12},{6,14},{8,0},{10,2},{12,4},{14,6},{1,9},{3,11}... | collective-permute-start | bytes 196616 | tf_op jit(solution)/shard_map/ppermute | solution.py:194
  13.0 8.3 %collective-permute-start.1 = (bf16[128,256]{1,0:T(8,128)(2,1)S(1)}, bf16[128,256]{1,0:T(8,128)(2,1)S(1)}, u32[]{:S(2)}, u32[]{:S(2)}) collective-permute-start(bf16[128,256]{1,0:T(8,128)(2,1)S(1)} %get-tuple-element.13.refs_0_), channel_id=1, source_target_pairs={{0,4},{2,6},{4,0},{6,2},{8,12},{10,14},{12,8},{14,10},{1,5},{3,7},... | collective-permute-start | bytes 196616 | tf_op jit(solution)/shard_map/ppermute | solution.py:194
  13.8 8.5 %collective-permute-start.8 = (f32[64,256]{1,0:T(8,128)S(1)}, f32[64,256]{1,0:T(8,128)S(1)}, u32[]{:S(2)}, u32[]{:S(2)}) collective-permute-start(f32[64,256]{1,0:T(8,128)S(1)} %plane_sum.1.refs_0_), channel_id=1, source_target_pairs={{0,12},{2,14},{4,8},{6,10},{8,4},{10,6},{12,0},{14,2},{1,13},{3,15... | collective-permute-start | bytes 196616 | tf_op jit(solution)/shard_map/ppermute | solution.py:194
  17.4 6.8 %collective-permute-start.7 = (f32[64,256]{1,0:T(8,128)S(1)}, f32[64,256]{1,0:T(8,128)S(1)}, u32[]{:S(2)}, u32[]{:S(2)}) collective-permute-start(f32[64,256]{1,0:T(8,128)S(1)} %plane_sum.1.refs_0_), channel_id=1, source_target_pairs={{0,8},{2,10},{4,12},{6,14},{8,0},{10,2},{12,4},{14,6},{1,9},{3,11}... | collective-permute-start | bytes 196616 | tf_op jit(solution)/shard_map/ppermute | solution.py:194
  17.4 6.8 %collective-permute-start.6 = (f32[64,256]{1,0:T(8,128)S(1)}, f32[64,256]{1,0:T(8,128)S(1)}, u32[]{:S(2)}, u32[]{:S(2)}) collective-permute-start(f32[64,256]{1,0:T(8,128)S(1)} %plane_sum.1.refs_0_), channel_id=1, source_target_pairs={{0,4},{2,6},{4,0},{6,2},{8,12},{10,14},{12,8},{14,10},{1,5},{3,7},... | collective-permute-start | bytes 196616 | tf_op jit(solution)/shard_map/ppermute | solution.py:194
  21.3 8.9 %collective-permute-start.4 = (bf16[4,128,256]{2,1,0:T(8,128)(2,1)S(1)}, bf16[4,128,256]{2,1,0:T(8,128)(2,1)S(1)}, u32[]{:S(2)}, u32[]{:S(2)}) collective-permute-start(bf16[4,128,256]{2,1,0:T(8,128)(2,1)S(1)} %join_rows.1), channel_id=1, source_target_pairs={{0,2},{2,0},{4,6},{6,4},{8,10},{10,8},{12,14},{14,12},{1,3},{3,1},... | collective-permute-start | bytes 786440 | tf_op jit(solution)/shard_map/ppermute | solution.py:194
  24.3 4.6 %collective-permute-start.9 = (bf16[64,256]{1,0:T(8,128)(2,1)S(1)}, bf16[64,256]{1,0:T(8,128)(2,1)S(1)}, u32[]{:S(2)}, u32[]{:S(2)}) collective-permute-start(bf16[64,256]{1,0:T(8,128)(2,1)S(1)} %hub_sums.1.mine_ref), channel_id=1, source_target_pairs={{0,2},{2,0},{4,6},{6,4},{8,10},{10,8},{12,14},{14,12},{1,3},{3,1},... | collective-permute-start | bytes 98312 | tf_op jit(solution)/shard_map/ppermute | solution.py:194
  28.9 1.3 %collective-permute-start.10 = (bf16[128,256]{1,0:T(8,128)(2,1)S(1)}, bf16[128,256]{1,0:T(8,128)(2,1)S(1)}, u32[]{:S(2)}, u32[]{:S(2)}) collective-permute-start(bf16[128,256]{1,0:T(8,128)(2,1)S(1)} %join_sides.1.refs_5_), channel_id=1, source_target_pairs={{0,1},{1,0},{2,3},{3,2},{4,5},{5,4},{6,7},{7,6},{8,9},{9,8},{10,11... | collective-permute-start | bytes 196616 | tf_op jit(solution)/shard_map/ppermute | solution.py:191
  31.8 13.8 %all-to-all-start = ((f32[16,16,256]{2,1,0:T(8,128)}), f32[16,16,256]{2,1,0:T(8,128)S(1)}, u32[]{:S(2)}, u32[]{:S(2)}) async-start(f32[16,16,256]{2,1,0:T(8,128)} %get-tuple-element.19), calls=%async_computation | async-start | bytes 524288 | tf_op jit(solution)/shard_map/all_to_all | solution.py:259
  35.6 1.4 %collective-permute-start.11 = (f32[128,256]{1,0:T(8,128)S(1)}, f32[128,256]{1,0:T(8,128)S(1)}, u32[]{:S(2)}, u32[]{:S(2)}) collective-permute-start(f32[128,256]{1,0:T(8,128)S(1)} %get-tuple-element.18), channel_id=1, source_target_pairs={{0,1},{1,0},{2,3},{3,2},{4,5},{5,4},{6,7},{7,6},{8,9},{9,8},{10,11... | collective-permute-start | bytes 393224 | tf_op jit(solution)/shard_map/ppermute | solution.py:191

commit v15 on v13

--- a/solution.py
+++ b/solution.py
@@ -87,8 +87,8 @@
 def second_kernel(dims, *refs):
     n_row, n_col, side = dims
     n_z = n_row // X
-    blocks, (across, mine_ref, theirs_ref) = refs[:n_z], refs[n_z:n_z + 3]
-    dense_ref, send_ref, keep_ref, panel, prod = refs[n_z + 3:]
+    blocks, across, quarters = refs[:n_z], refs[n_z], refs[n_z + 1:n_z + 1 + X * n_col]
+    dense_ref, send_ref, keep_ref, panel, prod = refs[n_z + 1 + X * n_col:]
     half = H // n_col
     r, c = lax.axis_index("row"), lax.axis_index("col")
 
@@ -98,8 +98,10 @@
     for k in range(n_z):
         put(r ^ (X * k), blocks[k][...])
         put(r ^ (X * k) ^ 1, across[k])
-    for ref, col in ((mine_ref, c), (theirs_ref, 1 - c)):
-        panel[pl.ds(pl.multiple_of(n_row * VB + col * half, half), half), :] = ref[...]
+    quarter = quarters[0].shape[0]
+    for k, ref in enumerate(quarters):
+        place = n_row * VB + ((c ^ (k // X)) * X + (r % X ^ (k % X))) * quarter
+        panel[pl.ds(pl.multiple_of(place, quarter), quarter), :] = ref[...]
     write_terms(dims, half // n_row, prod, dense_ref, panel, send_ref, keep_ref)
 
 
@@ -143,13 +145,6 @@
     first = (lax.axis_index("col") * X + lax.axis_index("row") % X) * quarter
     tele = one_hot(first, quarter, src_ref[...])
     out_ref[...] = (DAMP * sum_planes(planes, held) + 0.15 * tele).astype(out_ref.dtype)
-
-
-def side_kernel(mine_ref, theirs_ref, out_ref):
-    quarter = mine_ref.shape[0]
-    x = lax.axis_index("row") % X
-    for ref, place in ((mine_ref, x), (theirs_ref, 1 - x)):
-        out_ref[pl.ds(pl.multiple_of(place * quarter, quarter), quarter), :] = ref[...]
 
 
 def pieces_kernel(keep_ref, came_ref, parts_ref):
@@ -199,6 +194,10 @@
 
     def other_side(x):
         return to_partner(x, 1)
+
+    def other_both(x):
+        devices = [(r, c) for r in range(n_row) for c in range(n_col)]
+        return lax.ppermute(x, ("row", "col"), [(r * n_col + c, (r ^ 1) * n_col + 1 - c) for r, c in devices])
 
     def along_z(blocks):
         return [to_partner(block, X * k) for k, block in enumerate(blocks) if k > 0]
@@ -253,10 +252,10 @@
         across = other_side(call(join_kernel, "join_rows", bf16((n_z, VB, width)), *blocks, cost=2))
         mine = call(bind(hub_kernel, dims), "hub_sums", bf16((quarter, width)), src, *planes,
                     scratch=[pltpu.VMEM((n_z, quarter, width), jnp.float32)], cost=2)
-        mine = call(side_kernel, "join_sides", bf16((H // n_col, width)), mine, other_side(mine), cost=1)
+        quarters = [mine, other_side(mine), other_core(mine), other_both(mine)]
         send, keep = call(
             bind(second_kernel, dims), "later_terms", (f32((half, width)), f32((half, width))),
-            *blocks, across, mine, other_core(mine), dense, scratch=product_scratch)
+            *blocks, across, *quarters, dense, scratch=product_scratch)
     came = other_core(send)
     parts = call(pieces_kernel, "hub_pieces", f32((n_row, piece, width)), keep, came)
     parts = lax.all_to_all(parts, "row", 0, 0)

time: 45.3 us -> 45.3 us (level)
  waiting for transfers between devices: 19.4 us -> 17.4 us
  starting transfers between devices: 17.8 us -> 19.7 us
    ppermute x9, waiting for transfers between devices: 8.95 us -> 6.43 us  [to_partner(): return lax.ppermute(x, 'row', [(r, r ^ flip) for r in range(n_row)])]
    ppermute x0 -> x1, waiting for transfers between devices: none -> 1.61 us  [other_both(): lax.ppermute(x, ('row', 'col'), [(r * n_col + c, (r ^ 1) * n_col + 1 - c)...]
    ppermute x3, waiting for transfers between devices: 3.77 us -> 2.69 us  [other_core(): return lax.ppermute(x, 'col', [(0, 1), (1, 0)])]
    ppermute x9, starting transfers between devices: 13.4 us -> 14.3 us  [to_partner(): return lax.ppermute(x, 'row', [(r, r ^ flip) for r in range(n_row)])]
    all_to_all x1, starting transfers between devices: 3.63 us -> 4.19 us  [fast_body(): parts = lax.all_to_all(parts, 'row', 0, 0)]
    pallas_call x9 -> x8, Pallas kernels: 3.1 us -> 3.12 us  [call(): pl.pallas_call(kernel, out_shape=out_shape, in_specs=[VMEM] * len(args),...]
  transfers between devices with their start and end apart: 13 -> 14, of which waited for: 7 -> 7; matrix products, arithmetic and copies ran while one was open for 0% -> 0% of each run, Pallas kernels for 2% -> 2%
where the time goes in v15:
time: 45.3 us; the launch traced here: 45 us
  starting transfers between devices  19.7 us (43%)
  waiting for transfers between devices  17.4 us (38%)
  Pallas kernels  6.52 us (14%)
  between operations  1.36 us (3%)
    ppermute x9, starting transfers between devices, to_partner(): return lax.ppermute(x, 'row', [(r, r ^ flip) for r in range(n_row)])  14.3 us
    all_to_all x1, waiting for transfers between devices, fast_body(): parts = lax.all_to_all(parts, 'row', 0, 0)  6.65 us
    ppermute x9, waiting for transfers between devices, to_partner(): return lax.ppermute(x, 'row', [(r, r ^ flip) for r in range(n_row)])  6.43 us
    all_to_all x1, starting transfers between devices, fast_body(): parts = lax.all_to_all(parts, 'row', 0, 0)  4.19 us
    pallas_call x1, Pallas kernels, fast_body(): pl.pallas_call(bind(first_kernel, dims), out_shape=(f32((half, width)), f...  3.4 us
    pallas_call x8, Pallas kernels, call(): pl.pallas_call(kernel, out_shape=out_shape, in_specs=[VMEM] * len(args),...  3.12 us
    ppermute x3, waiting for transfers between devices, other_core(): return lax.ppermute(x, 'col', [(0, 1), (1, 0)])  2.69 us
    ppermute x1, waiting for transfers between devices, other_both(): lax.ppermute(x, ('row', 'col'), [(r * n_col + c, (r ^ 1) * n_col + 1 - c)...  1.61 us
  transfers between devices with their start and end apart: 14, of which 7 were waited for; matrix products, arithmetic and copies ran while one was open for 0% of the time, Pallas kernels for 2%

profile of v15, /device:TPU:0, one launch (start us, length us, event | category | flops | bytes accessed | tf_op | source)
XLA Modules:
  0.0 45.0 jit_solution(10483560508895804609)
XLA Ops:
  0.6 0.0 copy-start
  1.3 3.4 %first_terms.1 = (f32[256,256]{1,0:T(8,128)S(1)}, f32[256,256]{1,0:T(8,128)S(1)}, bf16[1024,1280]{1,0:T(8,128)(2,1)S(1)}) custom-call(bf16[96,128,128]{2,1,0:T(8,128)(2,1)} %bitcast.12, s32[96]{0:T(128)} %bitcast.14, s32[96]{0:T(128)} %bitcast.15, s32[1]{0:T(128)} %bitcast.6.count_hbm, s32[1,256]{1,0:T(1,128)} %bitcast.7), custom_call_target="tpu_custom_call" | custom-call | tf_op jit(solution)/shard_map/first_terms/pallas_call | solution.py:221
  4.7 0.5 %collective-permute-start = (f32[256,256]{1,0:T(8,128)S(1)}, f32[256,256]{1,0:T(8,128)S(1)}, u32[]{:S(2)}, u32[]{:S(2)}) collective-permute-start(f32[256,256]{1,0:T(8,128)S(1)} %get-tuple-element.11), channel_id=1, source_target_pairs={{0,1},{1,0},{2,3},{3,2},{4,5},{5,4},{6,7},{7,6},{8,9},{9,8},{10,11... | collective-permute-start | bytes 786440 | tf_op jit(solution)/shard_map/ppermute | solution.py:190
  5.2 1.2 %collective-permute-done.came_ref = f32[256,256]{1,0:T(8,128)S(1)} collective-permute-done((f32[256,256]{1,0:T(8,128)S(1)}, f32[256,256]{1,0:T(8,128)S(1)}, u32[]{:S(2)}, u32[]{:S(2)}) %collective-permute-start) | collective-permute-done | bytes 262176 | tf_op jit(solution)/shard_map/ppermute | solution.py:190
  6.4 0.0 copy-done
  6.4 2.9 %collective-permute-start.5 = (f32[64,256]{1,0:T(8,128)S(1)}, f32[64,256]{1,0:T(8,128)S(1)}, u32[]{:S(2)}, u32[]{:S(2)}) collective-permute-start(f32[64,256]{1,0:T(8,128)S(1)} %get-tuple-element.14), channel_id=1, source_target_pairs={{0,2},{2,0},{4,6},{6,4},{8,10},{10,8},{12,14},{14,12},{1,3},{3,1},... | collective-permute-start | bytes 196616 | tf_op jit(solution)/shard_map/ppermute | solution.py:193
  9.4 3.6 %collective-permute-start.3 = (bf16[128,256]{1,0:T(8,128)(2,1)S(1)}, bf16[128,256]{1,0:T(8,128)(2,1)S(1)}, u32[]{:S(2)}, u32[]{:S(2)}) collective-permute-start(bf16[128,256]{1,0:T(8,128)(2,1)S(1)} %get-tuple-element.12.refs_0_), channel_id=1, source_target_pairs={{0,12},{2,14},{4,8},{6,10},{8,4},{10,6},{12,0},{14,2},{1,13},{3,15... | collective-permute-start | bytes 196616 | tf_op jit(solution)/shard_map/ppermute | solution.py:193
  13.0 0.0 collective-permute-start.2
  13.0 0.8 %collective-permute-start.1 = (bf16[128,256]{1,0:T(8,128)(2,1)S(1)}, bf16[128,256]{1,0:T(8,128)(2,1)S(1)}, u32[]{:S(2)}, u32[]{:S(2)}) collective-permute-start(bf16[128,256]{1,0:T(8,128)(2,1)S(1)} %get-tuple-element.12.refs_0_), channel_id=1, source_target_pairs={{0,4},{2,6},{4,0},{6,2},{8,12},{10,14},{12,8},{14,10},{1,5},{3,7},... | collective-permute-start | bytes 196616 | tf_op jit(solution)/shard_map/ppermute | solution.py:193
  13.8 0.0 collective-permute-done.5.came_ref
  13.8 3.7 %collective-permute-start.8 = (f32[64,256]{1,0:T(8,128)S(1)}, f32[64,256]{1,0:T(8,128)S(1)}, u32[]{:S(2)}, u32[]{:S(2)}) collective-permute-start(f32[64,256]{1,0:T(8,128)S(1)} %plane_sum.1.refs_0_), channel_id=1, source_target_pairs={{0,12},{2,14},{4,8},{6,10},{8,4},{10,6},{12,0},{14,2},{1,13},{3,15... | collective-permute-start | bytes 196616 | tf_op jit(solution)/shard_map/ppermute | solution.py:193
  17.4 0.0 collective-permute-start.7
  17.4 0.0 collective-permute-done.3.refs_3_
  17.4 0.8 %collective-permute-start.6 = (f32[64,256]{1,0:T(8,128)S(1)}, f32[64,256]{1,0:T(8,128)S(1)}, u32[]{:S(2)}, u32[]{:S(2)}) collective-permute-start(f32[64,256]{1,0:T(8,128)S(1)} %plane_sum.1.refs_0_), channel_id=1, source_target_pairs={{0,4},{2,6},{4,0},{6,2},{8,12},{10,14},{12,8},{14,10},{1,5},{3,7},... | collective-permute-start | bytes 196616 | tf_op jit(solution)/shard_map/ppermute | solution.py:193
  18.2 3.0 %collective-permute-done.2.refs_2_ = bf16[128,256]{1,0:T(8,128)(2,1)S(1)} collective-permute-done((bf16[128,256]{1,0:T(8,128)(2,1)S(1)}, bf16[128,256]{1,0:T(8,128)(2,1)S(1)}, u32[]{:S(2)}, u32[]{:S(2)}) %collective-permute-start.2) | collective-permute-done | bytes 65568 | tf_op jit(solution)/shard_map/ppermute | solution.py:193
  21.2 0.0 collective-permute-done.1.refs_1_
  21.3 1.0 %collective-permute-start.4 = (bf16[4,128,256]{2,1,0:T(8,128)(2,1)S(1)}, bf16[4,128,256]{2,1,0:T(8,128)(2,1)S(1)}, u32[]{:S(2)}, u32[]{:S(2)}) collective-permute-start(bf16[4,128,256]{2,1,0:T(8,128)(2,1)S(1)} %join_rows.1), channel_id=1, source_target_pairs={{0,2},{2,0},{4,6},{6,4},{8,10},{10,8},{12,14},{14,12},{1,3},{3,1},... | collective-permute-start | bytes 786440 | tf_op jit(solution)/shard_map/ppermute | solution.py:193
  22.3 0.0 collective-permute-done.8.refs_3_
  22.3 1.9 %collective-permute-done.7.refs_2_ = f32[64,256]{1,0:T(8,128)S(1)} collective-permute-done((f32[64,256]{1,0:T(8,128)S(1)}, f32[64,256]{1,0:T(8,128)S(1)}, u32[]{:S(2)}, u32[]{:S(2)}) %collective-permute-start.7) | collective-permute-done | bytes 65568 | tf_op jit(solution)/shard_map/ppermute | solution.py:193
  24.2 0.0 collective-permute-done.6.refs_1_
  24.2 0.1 hub_sums.1.refs_5_
  24.3 0.1 collective-permute-start.11
  24.3 0.6 %collective-permute-start.10 = (bf16[64,256]{1,0:T(8,128)(2,1)S(1)}, bf16[64,256]{1,0:T(8,128)(2,1)S(1)}, u32[]{:S(2)}, u32[]{:S(2)}) collective-permute-start(bf16[64,256]{1,0:T(8,128)(2,1)S(1)} %hub_sums.1.refs_5_), channel_id=1, source_target_pairs={{0,1},{1,0},{2,3},{3,2},{4,5},{5,4},{6,7},{7,6},{8,9},{9,8},{10,11... | collective-permute-start | bytes 98312 | tf_op jit(solution)/shard_map/ppermute | solution.py:190
  25.0 1.5 %collective-permute-start.9 = (bf16[64,256]{1,0:T(8,128)(2,1)S(1)}, bf16[64,256]{1,0:T(8,128)(2,1)S(1)}, u32[]{:S(2)}, u32[]{:S(2)}) collective-permute-start(bf16[64,256]{1,0:T(8,128)(2,1)S(1)} %hub_sums.1.refs_5_), channel_id=1, source_target_pairs={{0,2},{2,0},{4,6},{6,4},{8,10},{10,8},{12,14},{14,12},{1,3},{3,1},... | collective-permute-start | bytes 98312 | tf_op jit(solution)/shard_map/ppermute | solution.py:193
  26.5 1.6 %collective-permute-done.11.refs_8_ = bf16[64,256]{1,0:T(8,128)(2,1)S(1)} collective-permute-done((bf16[64,256]{1,0:T(8,128)(2,1)S(1)}, bf16[64,256]{1,0:T(8,128)(2,1)S(1)}, u32[]{:S(2)}, u32[]{:S(2)}) %collective-permute-start.11) | collective-permute-done | bytes 32800 | tf_op jit(solution)/shard_map/ppermute | solution.py:200
  28.1 0.0 collective-permute-done.10.refs_7_
  28.1 1.5 %collective-permute-done.9.refs_6_ = bf16[64,256]{1,0:T(8,128)(2,1)S(1)} collective-permute-done((bf16[64,256]{1,0:T(8,128)(2,1)S(1)}, bf16[64,256]{1,0:T(8,128)(2,1)S(1)}, u32[]{:S(2)}, u32[]{:S(2)}) %collective-permute-start.9) | collective-permute-done | bytes 32800 | tf_op jit(solution)/shard_map/ppermute | solution.py:193
  29.6 0.0 collective-permute-done.4.refs_4_
  29.6 1.0 %later_terms.1 = (f32[256,256]{1,0:T(8,128)S(1)}, f32[256,256]{1,0:T(8,128)S(1)}) custom-call(bf16[128,256]{1,0:T(8,128)(2,1)S(1)} %get-tuple-element.12.refs_0_, bf16[128,256]{1,0:T(8,128)(2,1)S(1)} %collective-permute-done.1.refs_1_, bf16[128,256]{1,0:T(8,128)(2,1)S(1)} %collective-permute-done.2.refs_2_, ...), custom_call_target="tpu_custom_call" | custom-call | tf_op jit(solution)/shard_map/later_terms/pallas_call | solution.py:206
  30.6 0.1 collective-permute-start.12
  30.6 1.5 %collective-permute-done.12.came_ref = f32[256,256]{1,0:T(8,128)S(1)} collective-permute-done((f32[256,256]{1,0:T(8,128)S(1)}, f32[256,256]{1,0:T(8,128)S(1)}, u32[]{:S(2)}, u32[]{:S(2)}) %collective-permute-start.12) | collective-permute-done | bytes 262176 | tf_op jit(solution)/shard_map/ppermute | solution.py:190
  32.2 0.7 %hub_pieces.1 = f32[8,16,256]{2,1,0:T(8,128)} custom-call(f32[256,256]{1,0:T(8,128)S(1)} %get-tuple-element.16.keep_ref, f32[256,256]{1,0:T(8,128)S(1)} %collective-permute-done.12.came_ref), custom_call_target="tpu_custom_call" | custom-call | tf_op jit(solution)/shard_map/hub_pieces/pallas_call | solution.py:206
  32.9 4.2 %all-to-all-start = ((f32[8,16,256]{2,1,0:T(8,128)}), f32[8,16,256]{2,1,0:T(8,128)S(1)}, u32[]{:S(2)}, u32[]{:S(2)}) async-start(f32[8,16,256]{2,1,0:T(8,128)} %hub_pieces.1), calls=%async_computation | async-start | bytes 262144 | tf_op jit(solution)/shard_map/all_to_all | solution.py:261
  37.0 0.7 %last_scores.1 = f32[128,256]{1,0:T(8,128)} custom-call(s32[1,256]{1,0:T(1,128)S(1)} %bitcast.10, f32[256,256]{1,0:T(8,128)S(1)} %get-tuple-element.16.keep_ref, f32[256,256]{1,0:T(8,128)S(1)} %collective-permute-done.12.came_ref), custom_call_target="tpu_custom_call" | custom-call | tf_op jit(solution)/shard_map/last_scores/pallas_call | solution.py:206
  37.7 6.7 %all-to-all-done.parts_ref = f32[8,16,256]{2,1,0:T(8,128)S(1)} async-done(((f32[8,16,256]{2,1,0:T(8,128)}), f32[8,16,256]{2,1,0:T(8,128)S(1)}, u32[]{:S(2)}, u32[]{:S(2)}) %all-to-all-start) | async-done | bytes 131104 | tf_op jit(solution)/shard_map/all_to_all | solution.py:261
  44.4 0.6 %last_hubs.1 = f32[16,256]{1,0:T(8,128)} custom-call(s32[1,256]{1,0:T(1,128)S(1)} %bitcast.11, f32[8,16,256]{2,1,0:T(8,128)S(1)} %all-to-all-done.parts_ref), custom_call_target="tpu_custom_call" | custom-call | tf_op jit(solution)/shard_map/last_hubs/pallas_call | solution.py:206
  (3 shorter events, 0.1 us)
Async XLA Ops:
  0.6 5.8 %copy-start = (s32[256]{0:T(256)S(1)}, s32[256]{0:T(256)}, u32[]{:S(2)}) copy-start(s32[256]{0:T(256)} %param.9) | copy-start | bytes 3076
  4.7 1.7 %collective-permute-start = (f32[256,256]{1,0:T(8,128)S(1)}, f32[256,256]{1,0:T(8,128)S(1)}, u32[]{:S(2)}, u32[]{:S(2)}) collective-permute-start(f32[256,256]{1,0:T(8,128)S(1)} %get-tuple-element.11), channel_id=1, source_target_pairs={{0,1},{1,0},{2,3},{3,2},{4,5},{5,4},{6,7},{7,6},{8,9},{9,8},{10,11... | collective-permute-start | bytes 786440 | tf_op jit(solution)/shard_map/ppermute | solution.py:190
  6.4 7.3 %collective-permute-start.5 = (f32[64,256]{1,0:T(8,128)S(1)}, f32[64,256]{1,0:T(8,128)S(1)}, u32[]{:S(2)}, u32[]{:S(2)}) collective-permute-start(f32[64,256]{1,0:T(8,128)S(1)} %get-tuple-element.14), channel_id=1, source_target_pairs={{0,2},{2,0},{4,6},{6,4},{8,10},{10,8},{12,14},{14,12},{1,3},{3,1},... | collective-permute-start | bytes 196616 | tf_op jit(solution)/shard_map/ppermute | solution.py:193
  9.4 8.1 %collective-permute-start.3 = (bf16[128,256]{1,0:T(8,128)(2,1)S(1)}, bf16[128,256]{1,0:T(8,128)(2,1)S(1)}, u32[]{:S(2)}, u32[]{:S(2)}) collective-permute-start(bf16[128,256]{1,0:T(8,128)(2,1)S(1)} %get-tuple-element.12.refs_0_), channel_id=1, source_target_pairs={{0,12},{2,14},{4,8},{6,10},{8,4},{10,6},{12,0},{14,2},{1,13},{3,15... | collective-permute-start | bytes 196616 | tf_op jit(solution)/shard_map/ppermute | solution.py:193
  13.0 8.3 %collective-permute-start.2 = (bf16[128,256]{1,0:T(8,128)(2,1)S(1)}, bf16[128,256]{1,0:T(8,128)(2,1)S(1)}, u32[]{:S(2)}, u32[]{:S(2)}) collective-permute-start(bf16[128,256]{1,0:T(8,128)(2,1)S(1)} %get-tuple-element.12.refs_0_), channel_id=1, source_target_pairs={{0,8},{2,10},{4,12},{6,14},{8,0},{10,2},{12,4},{14,6},{1,9},{3,11}... | collective-permute-start | bytes 196616 | tf_op jit(solution)/shard_map/ppermute | solution.py:193
  13.0 8.3 %collective-permute-start.1 = (bf16[128,256]{1,0:T(8,128)(2,1)S(1)}, bf16[128,256]{1,0:T(8,128)(2,1)S(1)}, u32[]{:S(2)}, u32[]{:S(2)}) collective-permute-start(bf16[128,256]{1,0:T(8,128)(2,1)S(1)} %get-tuple-element.12.refs_0_), channel_id=1, source_target_pairs={{0,4},{2,6},{4,0},{6,2},{8,12},{10,14},{12,8},{14,10},{1,5},{3,7},... | collective-permute-start | bytes 196616 | tf_op jit(solution)/shard_map/ppermute | solution.py:193
  13.8 8.5 %collective-permute-start.8 = (f32[64,256]{1,0:T(8,128)S(1)}, f32[64,256]{1,0:T(8,128)S(1)}, u32[]{:S(2)}, u32[]{:S(2)}) collective-permute-start(f32[64,256]{1,0:T(8,128)S(1)} %plane_sum.1.refs_0_), channel_id=1, source_target_pairs={{0,12},{2,14},{4,8},{6,10},{8,4},{10,6},{12,0},{14,2},{1,13},{3,15... | collective-permute-start | bytes 196616 | tf_op jit(solution)/shard_map/ppermute | solution.py:193
  17.4 6.8 %collective-permute-start.7 = (f32[64,256]{1,0:T(8,128)S(1)}, f32[64,256]{1,0:T(8,128)S(1)}, u32[]{:S(2)}, u32[]{:S(2)}) collective-permute-start(f32[64,256]{1,0:T(8,128)S(1)} %plane_sum.1.refs_0_), channel_id=1, source_target_pairs={{0,8},{2,10},{4,12},{6,14},{8,0},{10,2},{12,4},{14,6},{1,9},{3,11}... | collective-permute-start | bytes 196616 | tf_op jit(solution)/shard_map/ppermute | solution.py:193
  17.4 6.8 %collective-permute-start.6 = (f32[64,256]{1,0:T(8,128)S(1)}, f32[64,256]{1,0:T(8,128)S(1)}, u32[]{:S(2)}, u32[]{:S(2)}) collective-permute-start(f32[64,256]{1,0:T(8,128)S(1)} %plane_sum.1.refs_0_), channel_id=1, source_target_pairs={{0,4},{2,6},{4,0},{6,2},{8,12},{10,14},{12,8},{14,10},{1,5},{3,7},... | collective-permute-start | bytes 196616 | tf_op jit(solution)/shard_map/ppermute | solution.py:193
  21.3 8.3 %collective-permute-start.4 = (bf16[4,128,256]{2,1,0:T(8,128)(2,1)S(1)}, bf16[4,128,256]{2,1,0:T(8,128)(2,1)S(1)}, u32[]{:S(2)}, u32[]{:S(2)}) collective-permute-start(bf16[4,128,256]{2,1,0:T(8,128)(2,1)S(1)} %join_rows.1), channel_id=1, source_target_pairs={{0,2},{2,0},{4,6},{6,4},{8,10},{10,8},{12,14},{14,12},{1,3},{3,1},... | collective-permute-start | bytes 786440 | tf_op jit(solution)/shard_map/ppermute | solution.py:193
  24.3 3.8 %collective-permute-start.11 = (bf16[64,256]{1,0:T(8,128)(2,1)S(1)}, bf16[64,256]{1,0:T(8,128)(2,1)S(1)}, u32[]{:S(2)}, u32[]{:S(2)}) collective-permute-start(bf16[64,256]{1,0:T(8,128)(2,1)S(1)} %hub_sums.1.refs_5_), channel_id=1, source_target_pairs={{0,3},{1,2},{2,1},{3,0},{4,7},{5,6},{6,5},{7,4},{8,11},{9,10},{10,... | collective-permute-start | bytes 98312 | tf_op jit(solution)/shard_map/ppermute | solution.py:200
  24.3 3.7 %collective-permute-start.10 = (bf16[64,256]{1,0:T(8,128)(2,1)S(1)}, bf16[64,256]{1,0:T(8,128)(2,1)S(1)}, u32[]{:S(2)}, u32[]{:S(2)}) collective-permute-start(bf16[64,256]{1,0:T(8,128)(2,1)S(1)} %hub_sums.1.refs_5_), channel_id=1, source_target_pairs={{0,1},{1,0},{2,3},{3,2},{4,5},{5,4},{6,7},{7,6},{8,9},{9,8},{10,11... | collective-permute-start | bytes 98312 | tf_op jit(solution)/shard_map/ppermute | solution.py:190
  25.0 4.6 %collective-permute-start.9 = (bf16[64,256]{1,0:T(8,128)(2,1)S(1)}, bf16[64,256]{1,0:T(8,128)(2,1)S(1)}, u32[]{:S(2)}, u32[]{:S(2)}) collective-permute-start(bf16[64,256]{1,0:T(8,128)(2,1)S(1)} %hub_sums.1.refs_5_), channel_id=1, source_target_pairs={{0,2},{2,0},{4,6},{6,4},{8,10},{10,8},{12,14},{14,12},{1,3},{3,1},... | collective-permute-start | bytes 98312 | tf_op jit(solution)/shard_map/ppermute | solution.py:193
  30.6 1.6 %collective-permute-start.12 = (f32[256,256]{1,0:T(8,128)S(1)}, f32[256,256]{1,0:T(8,128)S(1)}, u32[]{:S(2)}, u32[]{:S(2)}) collective-permute-start(f32[256,256]{1,0:T(8,128)S(1)} %get-tuple-element.17), channel_id=1, source_target_pairs={{0,1},{1,0},{2,3},{3,2},{4,5},{5,4},{6,7},{7,6},{8,9},{9,8},{10,11... | collective-permute-start | bytes 786440 | tf_op jit(solution)/shard_map/ppermute | solution.py:190
  32.9 11.5 %all-to-all-start = ((f32[8,16,256]{2,1,0:T(8,128)}), f32[8,16,256]{2,1,0:T(8,128)S(1)}, u32[]{:S(2)}, u32[]{:S(2)}) async-start(f32[8,16,256]{2,1,0:T(8,128)} %hub_pieces.1), calls=%async_computation | async-start | bytes 262144 | tf_op jit(solution)/shard_map/all_to_all | solution.py:261

commit v16 on v15

--- a/solution.py
+++ b/solution.py
@@ -13,6 +13,7 @@
 DAMP = 0.85
 CHUNK = 16
 X = 2
+NEAR = 2
 MICRO = 10 ** 9
 VMEM_LIMIT = 32 * 1024 * 1024
 
@@ -87,8 +88,9 @@
 def second_kernel(dims, *refs):
     n_row, n_col, side = dims
     n_z = n_row // X
-    blocks, across, quarters = refs[:n_z], refs[n_z], refs[n_z + 1:n_z + 1 + X * n_col]
-    dense_ref, send_ref, keep_ref, panel, prod = refs[n_z + 1 + X * n_col:]
+    blocks, across, quarters = refs[:n_z], refs[n_z:n_z + 2], refs[n_z + 2:n_z + 2 + X * n_col]
+    dense_ref, send_ref, keep_ref, panel, prod = refs[n_z + 2 + X * n_col:]
+    across = [across[0][k] for k in range(NEAR)] + [across[1][k] for k in range(n_z - NEAR)]
     half = H // n_col
     r, c = lax.axis_index("row"), lax.axis_index("col")
 
@@ -140,7 +142,8 @@
 
 
 def hub_kernel(dims, src_ref, *refs):
-    planes, (out_ref, held) = refs[:-2], refs[-2:]
+    out_ref, held = refs[-2:]
+    planes = refs[:held.shape[0]]
     quarter = out_ref.shape[0]
     first = (lax.axis_index("col") * X + lax.axis_index("row") % X) * quarter
     tele = one_hot(first, quarter, src_ref[...])
@@ -244,18 +247,19 @@
         own, hold, away = call(
             bind(spread_kernel, dims), "spread",
             (bf16((VB, width)), f32((quarter, width)), f32((quarter, width))),
-            src, keep, came, cost=1)
+            src, keep, came, cost=8)
         away = other_side(away)
         blocks = [own] + along_z([own] * n_z)
-        plane = call(plane_kernel, "plane_sum", f32((quarter, width)), hold, away, cost=20)
+        plane = call(plane_kernel, "plane_sum", f32((quarter, width)), hold, away, cost=8)
         planes = [plane] + along_z([plane] * n_z)
-        across = other_side(call(join_kernel, "join_rows", bf16((n_z, VB, width)), *blocks, cost=2))
-        mine = call(bind(hub_kernel, dims), "hub_sums", bf16((quarter, width)), src, *planes,
-                    scratch=[pltpu.VMEM((n_z, quarter, width), jnp.float32)], cost=2)
+        near = other_side(call(join_kernel, "join_near", bf16((NEAR, VB, width)), *blocks[:NEAR], cost=0))
+        far = other_side(call(join_kernel, "join_far", bf16((n_z - NEAR, VB, width)), *blocks[NEAR:], cost=3))
+        mine = call(bind(hub_kernel, dims), "hub_sums", bf16((quarter, width)), src, *planes, near,
+                    scratch=[pltpu.VMEM((n_z, quarter, width), jnp.float32)], cost=20)
         quarters = [mine, other_side(mine), other_core(mine), other_both(mine)]
         send, keep = call(
             bind(second_kernel, dims), "later_terms", (f32((half, width)), f32((half, width))),
-            *blocks, across, *quarters, dense, scratch=product_scratch)
+            *blocks, near, far, *quarters, dense, scratch=product_scratch)
     came = other_core(send)
     parts = call(pieces_kernel, "hub_pieces", f32((n_row, piece, width)), keep, came)
     parts = lax.all_to_all(parts, "row", 0, 0)

time: 45.3 us -> 45.6 us (level)
  starting transfers between devices: 19.7 us -> 22.1 us
  waiting for transfers between devices: 17.4 us -> 15.3 us
    ppermute x9 -> x10, starting transfers between devices: 14.3 us -> 16.8 us  [to_partner(): return lax.ppermute(x, 'row', [(r, r ^ flip) for r in range(n_row)])]
    ppermute x9 -> x10, waiting for transfers between devices: 6.43 us -> 4.77 us  [to_partner(): return lax.ppermute(x, 'row', [(r, r ^ flip) for r in range(n_row)])]
    pallas_call x8 -> x9, Pallas kernels: 3.12 us -> 3.11 us  [call(): pl.pallas_call(kernel, out_shape=out_shape, in_specs=[VMEM] * len(args),...]
  transfers between devices with their start and end apart: 14 -> 15, of which waited for: 7 -> 9; matrix products, arithmetic and copies ran while one was open for 0% -> 0% of each run, Pallas kernels for 2% -> 2%
where the time goes in v16:
time: 45.6 us; the launch traced here: 45.3 us
  starting transfers between devices  22.1 us (48%)
  waiting for transfers between devices  15.3 us (34%)
  Pallas kernels  6.5 us (14%)
  between operations  1.37 us (3%)
    ppermute x10, starting transfers between devices, to_partner(): return lax.ppermute(x, 'row', [(r, r ^ flip) for r in range(n_row)])  16.8 us
    all_to_all x1, waiting for transfers between devices, fast_body(): parts = lax.all_to_all(parts, 'row', 0, 0)  6.65 us
    ppermute x10, waiting for transfers between devices, to_partner(): return lax.ppermute(x, 'row', [(r, r ^ flip) for r in range(n_row)])  4.77 us
    all_to_all x1, starting transfers between devices, fast_body(): parts = lax.all_to_all(parts, 'row', 0, 0)  4.07 us
    pallas_call x1, Pallas kernels, fast_body(): pl.pallas_call(bind(first_kernel, dims), out_shape=(f32((half, width)), f...  3.4 us
    pallas_call x9, Pallas kernels, call(): pl.pallas_call(kernel, out_shape=out_shape, in_specs=[VMEM] * len(args),...  3.11 us
    ppermute x3, waiting for transfers between devices, other_core(): return lax.ppermute(x, 'col', [(0, 1), (1, 0)])  2.69 us
    ppermute x1, waiting for transfers between devices, other_both(): lax.ppermute(x, ('row', 'col'), [(r * n_col + c, (r ^ 1) * n_col + 1 - c)...  1.19 us
  transfers between devices with their start and end apart: 15, of which 9 were waited for; matrix products, arithmetic and copies ran while one was open for 0% of the time, Pallas kernels for 2%

profile of v16, /device:TPU:0, one launch (start us, length us, event | category | flops | bytes accessed | tf_op | source)
XLA Modules:
  0.0 45.3 jit_solution(13876329090686132633)
XLA Ops:
  0.6 0.0 copy-start
  1.3 3.4 %first_terms.1 = (f32[256,256]{1,0:T(8,128)S(1)}, f32[256,256]{1,0:T(8,128)S(1)}, bf16[1024,1280]{1,0:T(8,128)(2,1)S(1)}) custom-call(bf16[96,128,128]{2,1,0:T(8,128)(2,1)} %bitcast.12, s32[96]{0:T(128)} %bitcast.14, s32[96]{0:T(128)} %bitcast.15, s32[1]{0:T(128)} %bitcast.6.count_hbm, s32[1,256]{1,0:T(1,128)} %bitcast.7), custom_call_target="tpu_custom_call" | custom-call | tf_op jit(solution)/shard_map/first_terms/pallas_call | solution.py:224
  4.7 0.5 %collective-permute-start = (f32[256,256]{1,0:T(8,128)S(1)}, f32[256,256]{1,0:T(8,128)S(1)}, u32[]{:S(2)}, u32[]{:S(2)}) collective-permute-start(f32[256,256]{1,0:T(8,128)S(1)} %get-tuple-element.11), channel_id=1, source_target_pairs={{0,1},{1,0},{2,3},{3,2},{4,5},{5,4},{6,7},{7,6},{8,9},{9,8},{10,11... | collective-permute-start | bytes 786440 | tf_op jit(solution)/shard_map/ppermute | solution.py:193
  5.2 1.2 %collective-permute-done.came_ref = f32[256,256]{1,0:T(8,128)S(1)} collective-permute-done((f32[256,256]{1,0:T(8,128)S(1)}, f32[256,256]{1,0:T(8,128)S(1)}, u32[]{:S(2)}, u32[]{:S(2)}) %collective-permute-start) | collective-permute-done | bytes 262176 | tf_op jit(solution)/shard_map/ppermute | solution.py:193
  6.4 0.0 copy-done
  6.4 2.9 %collective-permute-start.6 = (f32[64,256]{1,0:T(8,128)S(1)}, f32[64,256]{1,0:T(8,128)S(1)}, u32[]{:S(2)}, u32[]{:S(2)}) collective-permute-start(f32[64,256]{1,0:T(8,128)S(1)} %get-tuple-element.14), channel_id=1, source_target_pairs={{0,2},{2,0},{4,6},{6,4},{8,10},{10,8},{12,14},{14,12},{1,3},{3,1},... | collective-permute-start | bytes 196616 | tf_op jit(solution)/shard_map/ppermute | solution.py:196
  9.4 3.6 %collective-permute-start.3 = (bf16[128,256]{1,0:T(8,128)(2,1)S(1)}, bf16[128,256]{1,0:T(8,128)(2,1)S(1)}, u32[]{:S(2)}, u32[]{:S(2)}) collective-permute-start(bf16[128,256]{1,0:T(8,128)(2,1)S(1)} %get-tuple-element.12.refs_0_), channel_id=1, source_target_pairs={{0,12},{2,14},{4,8},{6,10},{8,4},{10,6},{12,0},{14,2},{1,13},{3,15... | collective-permute-start | bytes 196616 | tf_op jit(solution)/shard_map/ppermute | solution.py:196
  13.0 0.0 collective-permute-start.2
  13.0 0.8 %collective-permute-start.1 = (bf16[128,256]{1,0:T(8,128)(2,1)S(1)}, bf16[128,256]{1,0:T(8,128)(2,1)S(1)}, u32[]{:S(2)}, u32[]{:S(2)}) collective-permute-start(bf16[128,256]{1,0:T(8,128)(2,1)S(1)} %get-tuple-element.12.refs_0_), channel_id=1, source_target_pairs={{0,4},{2,6},{4,0},{6,2},{8,12},{10,14},{12,8},{14,10},{1,5},{3,7},... | collective-permute-start | bytes 196616 | tf_op jit(solution)/shard_map/ppermute | solution.py:196
  13.8 0.0 collective-permute-done.6.came_ref
  13.8 3.7 %collective-permute-start.9 = (f32[64,256]{1,0:T(8,128)S(1)}, f32[64,256]{1,0:T(8,128)S(1)}, u32[]{:S(2)}, u32[]{:S(2)}) collective-permute-start(f32[64,256]{1,0:T(8,128)S(1)} %plane_sum.1.refs_0_), channel_id=1, source_target_pairs={{0,12},{2,14},{4,8},{6,10},{8,4},{10,6},{12,0},{14,2},{1,13},{3,15... | collective-permute-start | bytes 196616 | tf_op jit(solution)/shard_map/ppermute | solution.py:196
  17.4 0.0 collective-permute-start.8
  17.4 0.3 collective-permute-done.1.refs_1_
  17.8 2.5 %collective-permute-start.7 = (f32[64,256]{1,0:T(8,128)S(1)}, f32[64,256]{1,0:T(8,128)S(1)}, u32[]{:S(2)}, u32[]{:S(2)}) collective-permute-start(f32[64,256]{1,0:T(8,128)S(1)} %plane_sum.1.refs_0_), channel_id=1, source_target_pairs={{0,4},{2,6},{4,0},{6,2},{8,12},{10,14},{12,8},{14,10},{1,5},{3,7},... | collective-permute-start | bytes 196616 | tf_op jit(solution)/shard_map/ppermute | solution.py:196
  20.2 0.0 collective-permute-done.3.refs_1_.refs_3_
  20.3 0.6 %collective-permute-start.4 = (bf16[2,128,256]{2,1,0:T(8,128)(2,1)S(1)}, bf16[2,128,256]{2,1,0:T(8,128)(2,1)S(1)}, u32[]{:S(2)}, u32[]{:S(2)}) collective-permute-start(bf16[2,128,256]{2,1,0:T(8,128)(2,1)S(1)} %join_near.1), channel_id=1, source_target_pairs={{0,2},{2,0},{4,6},{6,4},{8,10},{10,8},{12,14},{14,12},{1,3},{3,1},... | collective-permute-start | bytes 393224 | tf_op jit(solution)/shard_map/ppermute | solution.py:196
  20.9 0.4 collective-permute-done.2.refs_0_.refs_2_
  21.2 1.2 %collective-permute-start.5 = (bf16[2,128,256]{2,1,0:T(8,128)(2,1)S(1)}, bf16[2,128,256]{2,1,0:T(8,128)(2,1)S(1)}, u32[]{:S(2)}, u32[]{:S(2)}) collective-permute-start(bf16[2,128,256]{2,1,0:T(8,128)(2,1)S(1)} %join_far.1), channel_id=1, source_target_pairs={{0,2},{2,0},{4,6},{6,4},{8,10},{10,8},{12,14},{14,12},{1,3},{3,1},... | collective-permute-start | bytes 393224 | tf_op jit(solution)/shard_map/ppermute | solution.py:196
  22.4 0.0 collective-permute-done.9.refs_3_
  22.4 1.8 %collective-permute-done.8.refs_2_ = f32[64,256]{1,0:T(8,128)S(1)} collective-permute-done((f32[64,256]{1,0:T(8,128)S(1)}, f32[64,256]{1,0:T(8,128)S(1)}, u32[]{:S(2)}, u32[]{:S(2)}) %collective-permute-start.8) | collective-permute-done | bytes 65568 | tf_op jit(solution)/shard_map/ppermute | solution.py:196
  24.2 0.0 collective-permute-done.7.refs_1_
  24.2 1.1 %collective-permute-done.4.refs_4_ = bf16[2,128,256]{2,1,0:T(8,128)(2,1)S(1)} collective-permute-done((bf16[2,128,256]{2,1,0:T(8,128)(2,1)S(1)}, bf16[2,128,256]{2,1,0:T(8,128)(2,1)S(1)}, u32[]{:S(2)}, u32[]{:S(2)}) %collective-permute-start.4) | collective-permute-done | bytes 131104 | tf_op jit(solution)/shard_map/ppermute | solution.py:196
  25.3 0.1 hub_sums.1.refs_6_
  25.4 0.1 collective-permute-start.12
  25.5 0.6 %collective-permute-start.11 = (bf16[64,256]{1,0:T(8,128)(2,1)S(1)}, bf16[64,256]{1,0:T(8,128)(2,1)S(1)}, u32[]{:S(2)}, u32[]{:S(2)}) collective-permute-start(bf16[64,256]{1,0:T(8,128)(2,1)S(1)} %hub_sums.1.refs_6_), channel_id=1, source_target_pairs={{0,1},{1,0},{2,3},{3,2},{4,5},{5,4},{6,7},{7,6},{8,9},{9,8},{10,11... | collective-permute-start | bytes 98312 | tf_op jit(solution)/shard_map/ppermute | solution.py:193
  26.1 1.5 %collective-permute-start.10 = (bf16[64,256]{1,0:T(8,128)(2,1)S(1)}, bf16[64,256]{1,0:T(8,128)(2,1)S(1)}, u32[]{:S(2)}, u32[]{:S(2)}) collective-permute-start(bf16[64,256]{1,0:T(8,128)(2,1)S(1)} %hub_sums.1.refs_6_), channel_id=1, source_target_pairs={{0,2},{2,0},{4,6},{6,4},{8,10},{10,8},{12,14},{14,12},{1,3},{3,1},... | collective-permute-start | bytes 98312 | tf_op jit(solution)/shard_map/ppermute | solution.py:196
  27.6 0.0 collective-permute-done.5.refs_5_
  27.6 1.2 %collective-permute-done.12.refs_9_ = bf16[64,256]{1,0:T(8,128)(2,1)S(1)} collective-permute-done((bf16[64,256]{1,0:T(8,128)(2,1)S(1)}, bf16[64,256]{1,0:T(8,128)(2,1)S(1)}, u32[]{:S(2)}, u32[]{:S(2)}) %collective-permute-start.12) | collective-permute-done | bytes 32800 | tf_op jit(solution)/shard_map/ppermute | solution.py:203
  28.8 0.0 collective-permute-done.11.refs_8_
  28.8 1.2 %collective-permute-done.10.refs_7_ = bf16[64,256]{1,0:T(8,128)(2,1)S(1)} collective-permute-done((bf16[64,256]{1,0:T(8,128)(2,1)S(1)}, bf16[64,256]{1,0:T(8,128)(2,1)S(1)}, u32[]{:S(2)}, u32[]{:S(2)}) %collective-permute-start.10) | collective-permute-done | bytes 32800 | tf_op jit(solution)/shard_map/ppermute | solution.py:196
  30.0 1.0 %later_terms.1 = (f32[256,256]{1,0:T(8,128)S(1)}, f32[256,256]{1,0:T(8,128)S(1)}) custom-call(bf16[128,256]{1,0:T(8,128)(2,1)S(1)} %get-tuple-element.12.refs_0_, bf16[128,256]{1,0:T(8,128)(2,1)S(1)} %collective-permute-done.1.refs_1_, bf16[128,256]{1,0:T(8,128)(2,1)S(1)} %collective-permute-done.2.refs_0_.refs_2_, ...), custom_call_target="tpu_custom_call" | custom-call | tf_op jit(solution)/shard_map/later_terms/pallas_call | solution.py:209
  31.0 0.1 collective-permute-start.13
  31.1 1.5 %collective-permute-done.13.came_ref = f32[256,256]{1,0:T(8,128)S(1)} collective-permute-done((f32[256,256]{1,0:T(8,128)S(1)}, f32[256,256]{1,0:T(8,128)S(1)}, u32[]{:S(2)}, u32[]{:S(2)}) %collective-permute-start.13) | collective-permute-done | bytes 262176 | tf_op jit(solution)/shard_map/ppermute | solution.py:193
  32.6 0.7 %hub_pieces.1 = f32[8,16,256]{2,1,0:T(8,128)} custom-call(f32[256,256]{1,0:T(8,128)S(1)} %get-tuple-element.16.keep_ref, f32[256,256]{1,0:T(8,128)S(1)} %collective-permute-done.13.came_ref), custom_call_target="tpu_custom_call" | custom-call | tf_op jit(solution)/shard_map/hub_pieces/pallas_call | solution.py:209
  33.3 4.1 %all-to-all-start = ((f32[8,16,256]{2,1,0:T(8,128)}), f32[8,16,256]{2,1,0:T(8,128)S(1)}, u32[]{:S(2)}, u32[]{:S(2)}) async-start(f32[8,16,256]{2,1,0:T(8,128)} %hub_pieces.1), calls=%async_computation | async-start | bytes 262144 | tf_op jit(solution)/shard_map/all_to_all | solution.py:265
  37.3 0.7 %last_scores.1 = f32[128,256]{1,0:T(8,128)} custom-call(s32[1,256]{1,0:T(1,128)S(1)} %bitcast.10, f32[256,256]{1,0:T(8,128)S(1)} %get-tuple-element.16.keep_ref, f32[256,256]{1,0:T(8,128)S(1)} %collective-permute-done.13.came_ref), custom_call_target="tpu_custom_call" | custom-call | tf_op jit(solution)/shard_map/last_scores/pallas_call | solution.py:209
  38.0 6.7 %all-to-all-done.parts_ref = f32[8,16,256]{2,1,0:T(8,128)S(1)} async-done(((f32[8,16,256]{2,1,0:T(8,128)}), f32[8,16,256]{2,1,0:T(8,128)S(1)}, u32[]{:S(2)}, u32[]{:S(2)}) %all-to-all-start) | async-done | bytes 131104 | tf_op jit(solution)/shard_map/all_to_all | solution.py:265
  44.7 0.6 %last_hubs.1 = f32[16,256]{1,0:T(8,128)} custom-call(s32[1,256]{1,0:T(1,128)S(1)} %bitcast.11, f32[8,16,256]{2,1,0:T(8,128)S(1)} %all-to-all-done.parts_ref), custom_call_target="tpu_custom_call" | custom-call | tf_op jit(solution)/shard_map/last_hubs/pallas_call | solution.py:209
  (4 shorter events, 0.1 us)
Async XLA Ops:
  0.6 5.8 %copy-start = (s32[256]{0:T(256)S(1)}, s32[256]{0:T(256)}, u32[]{:S(2)}) copy-start(s32[256]{0:T(256)} %param.9) | copy-start | bytes 3076
  4.7 1.7 %collective-permute-start = (f32[256,256]{1,0:T(8,128)S(1)}, f32[256,256]{1,0:T(8,128)S(1)}, u32[]{:S(2)}, u32[]{:S(2)}) collective-permute-start(f32[256,256]{1,0:T(8,128)S(1)} %get-tuple-element.11), channel_id=1, source_target_pairs={{0,1},{1,0},{2,3},{3,2},{4,5},{5,4},{6,7},{7,6},{8,9},{9,8},{10,11... | collective-permute-start | bytes 786440 | tf_op jit(solution)/shard_map/ppermute | solution.py:193
  6.4 7.3 %collective-permute-start.6 = (f32[64,256]{1,0:T(8,128)S(1)}, f32[64,256]{1,0:T(8,128)S(1)}, u32[]{:S(2)}, u32[]{:S(2)}) collective-permute-start(f32[64,256]{1,0:T(8,128)S(1)} %get-tuple-element.14), channel_id=1, source_target_pairs={{0,2},{2,0},{4,6},{6,4},{8,10},{10,8},{12,14},{14,12},{1,3},{3,1},... | collective-permute-start | bytes 196616 | tf_op jit(solution)/shard_map/ppermute | solution.py:196
  9.4 10.9 %collective-permute-start.3 = (bf16[128,256]{1,0:T(8,128)(2,1)S(1)}, bf16[128,256]{1,0:T(8,128)(2,1)S(1)}, u32[]{:S(2)}, u32[]{:S(2)}) collective-permute-start(bf16[128,256]{1,0:T(8,128)(2,1)S(1)} %get-tuple-element.12.refs_0_), channel_id=1, source_target_pairs={{0,12},{2,14},{4,8},{6,10},{8,4},{10,6},{12,0},{14,2},{1,13},{3,15... | collective-permute-start | bytes 196616 | tf_op jit(solution)/shard_map/ppermute | solution.py:196
  13.0 8.3 %collective-permute-start.2 = (bf16[128,256]{1,0:T(8,128)(2,1)S(1)}, bf16[128,256]{1,0:T(8,128)(2,1)S(1)}, u32[]{:S(2)}, u32[]{:S(2)}) collective-permute-start(bf16[128,256]{1,0:T(8,128)(2,1)S(1)} %get-tuple-element.12.refs_0_), channel_id=1, source_target_pairs={{0,8},{2,10},{4,12},{6,14},{8,0},{10,2},{12,4},{14,6},{1,9},{3,11}... | collective-permute-start | bytes 196616 | tf_op jit(solution)/shard_map/ppermute | solution.py:196
  13.0 4.8 %collective-permute-start.1 = (bf16[128,256]{1,0:T(8,128)(2,1)S(1)}, bf16[128,256]{1,0:T(8,128)(2,1)S(1)}, u32[]{:S(2)}, u32[]{:S(2)}) collective-permute-start(bf16[128,256]{1,0:T(8,128)(2,1)S(1)} %get-tuple-element.12.refs_0_), channel_id=1, source_target_pairs={{0,4},{2,6},{4,0},{6,2},{8,12},{10,14},{12,8},{14,10},{1,5},{3,7},... | collective-permute-start | bytes 196616 | tf_op jit(solution)/shard_map/ppermute | solution.py:196
  13.8 8.7 %collective-permute-start.9 = (f32[64,256]{1,0:T(8,128)S(1)}, f32[64,256]{1,0:T(8,128)S(1)}, u32[]{:S(2)}, u32[]{:S(2)}) collective-permute-start(f32[64,256]{1,0:T(8,128)S(1)} %plane_sum.1.refs_0_), channel_id=1, source_target_pairs={{0,12},{2,14},{4,8},{6,10},{8,4},{10,6},{12,0},{14,2},{1,13},{3,15... | collective-permute-start | bytes 196616 | tf_op jit(solution)/shard_map/ppermute | solution.py:196
  17.4 6.8 %collective-permute-start.8 = (f32[64,256]{1,0:T(8,128)S(1)}, f32[64,256]{1,0:T(8,128)S(1)}, u32[]{:S(2)}, u32[]{:S(2)}) collective-permute-start(f32[64,256]{1,0:T(8,128)S(1)} %plane_sum.1.refs_0_), channel_id=1, source_target_pairs={{0,8},{2,10},{4,12},{6,14},{8,0},{10,2},{12,4},{14,6},{1,9},{3,11}... | collective-permute-start | bytes 196616 | tf_op jit(solution)/shard_map/ppermute | solution.py:196
  17.8 6.5 %collective-permute-start.7 = (f32[64,256]{1,0:T(8,128)S(1)}, f32[64,256]{1,0:T(8,128)S(1)}, u32[]{:S(2)}, u32[]{:S(2)}) collective-permute-start(f32[64,256]{1,0:T(8,128)S(1)} %plane_sum.1.refs_0_), channel_id=1, source_target_pairs={{0,4},{2,6},{4,0},{6,2},{8,12},{10,14},{12,8},{14,10},{1,5},{3,7},... | collective-permute-start | bytes 196616 | tf_op jit(solution)/shard_map/ppermute | solution.py:196
  20.3 5.1 %collective-permute-start.4 = (bf16[2,128,256]{2,1,0:T(8,128)(2,1)S(1)}, bf16[2,128,256]{2,1,0:T(8,128)(2,1)S(1)}, u32[]{:S(2)}, u32[]{:S(2)}) collective-permute-start(bf16[2,128,256]{2,1,0:T(8,128)(2,1)S(1)} %join_near.1), channel_id=1, source_target_pairs={{0,2},{2,0},{4,6},{6,4},{8,10},{10,8},{12,14},{14,12},{1,3},{3,1},... | collective-permute-start | bytes 393224 | tf_op jit(solution)/shard_map/ppermute | solution.py:196
  21.2 6.4 %collective-permute-start.5 = (bf16[2,128,256]{2,1,0:T(8,128)(2,1)S(1)}, bf16[2,128,256]{2,1,0:T(8,128)(2,1)S(1)}, u32[]{:S(2)}, u32[]{:S(2)}) collective-permute-start(bf16[2,128,256]{2,1,0:T(8,128)(2,1)S(1)} %join_far.1), channel_id=1, source_target_pairs={{0,2},{2,0},{4,6},{6,4},{8,10},{10,8},{12,14},{14,12},{1,3},{3,1},... | collective-permute-start | bytes 393224 | tf_op jit(solution)/shard_map/ppermute | solution.py:196
  25.4 3.4 %collective-permute-start.12 = (bf16[64,256]{1,0:T(8,128)(2,1)S(1)}, bf16[64,256]{1,0:T(8,128)(2,1)S(1)}, u32[]{:S(2)}, u32[]{:S(2)}) collective-permute-start(bf16[64,256]{1,0:T(8,128)(2,1)S(1)} %hub_sums.1.refs_6_), channel_id=1, source_target_pairs={{0,3},{1,2},{2,1},{3,0},{4,7},{5,6},{6,5},{7,4},{8,11},{9,10},{10,... | collective-permute-start | bytes 98312 | tf_op jit(solution)/shard_map/ppermute | solution.py:203
  25.5 3.3 %collective-permute-start.11 = (bf16[64,256]{1,0:T(8,128)(2,1)S(1)}, bf16[64,256]{1,0:T(8,128)(2,1)S(1)}, u32[]{:S(2)}, u32[]{:S(2)}) collective-permute-start(bf16[64,256]{1,0:T(8,128)(2,1)S(1)} %hub_sums.1.refs_6_), channel_id=1, source_target_pairs={{0,1},{1,0},{2,3},{3,2},{4,5},{5,4},{6,7},{7,6},{8,9},{9,8},{10,11... | collective-permute-start | bytes 98312 | tf_op jit(solution)/shard_map/ppermute | solution.py:193
  26.1 3.9 %collective-permute-start.10 = (bf16[64,256]{1,0:T(8,128)(2,1)S(1)}, bf16[64,256]{1,0:T(8,128)(2,1)S(1)}, u32[]{:S(2)}, u32[]{:S(2)}) collective-permute-start(bf16[64,256]{1,0:T(8,128)(2,1)S(1)} %hub_sums.1.refs_6_), channel_id=1, source_target_pairs={{0,2},{2,0},{4,6},{6,4},{8,10},{10,8},{12,14},{14,12},{1,3},{3,1},... | collective-permute-start | bytes 98312 | tf_op jit(solution)/shard_map/ppermute | solution.py:196
  31.0 1.6 %collective-permute-start.13 = (f32[256,256]{1,0:T(8,128)S(1)}, f32[256,256]{1,0:T(8,128)S(1)}, u32[]{:S(2)}, u32[]{:S(2)}) collective-permute-start(f32[256,256]{1,0:T(8,128)S(1)} %get-tuple-element.17), channel_id=1, source_target_pairs={{0,1},{1,0},{2,3},{3,2},{4,5},{5,4},{6,7},{7,6},{8,9},{9,8},{10,11... | collective-permute-start | bytes 786440 | tf_op jit(solution)/shard_map/ppermute | solution.py:193
  33.3 11.4 %all-to-all-start = ((f32[8,16,256]{2,1,0:T(8,128)}), f32[8,16,256]{2,1,0:T(8,128)S(1)}, u32[]{:S(2)}, u32[]{:S(2)}) async-start(f32[8,16,256]{2,1,0:T(8,128)} %hub_pieces.1), calls=%async_computation | async-start | bytes 262144 | tf_op jit(solution)/shard_map/all_to_all | solution.py:265

commit v17 on v15

--- a/solution.py
+++ b/solution.py
@@ -84,20 +84,18 @@
     write_terms(dims, H // n_col, prod, dense_ref, panel, send_ref, keep_ref)
 
 
-def second_kernel(dims, *refs):
+def second_kernel(dims, flips, *refs):
     n_row, n_col, side = dims
     n_z = n_row // X
-    blocks, across, quarters = refs[:n_z], refs[n_z], refs[n_z + 1:n_z + 1 + X * n_col]
-    dense_ref, send_ref, keep_ref, panel, prod = refs[n_z + 1 + X * n_col:]
+    blocks, quarters = refs[:4], refs[4:4 + X * n_col]
+    dense_ref, send_ref, keep_ref, panel, prod = refs[4 + X * n_col:]
     half = H // n_col
     r, c = lax.axis_index("row"), lax.axis_index("col")
-
-    def put(owner, block):
-        panel[pl.ds(pl.multiple_of(owner * VB, VB), VB), :] = block
-
-    for k in range(n_z):
-        put(r ^ (X * k), blocks[k][...])
-        put(r ^ (X * k) ^ 1, across[k])
+    near, far = flips[:n_z // 2], flips[n_z // 2:]
+    for ref, group, x in ((blocks[0], near, 0), (blocks[1], far, 0), (blocks[2], near, 1), (blocks[3], far, 1)):
+        for k, flip in enumerate(group):
+            owner = r ^ (X * flip + x)
+            panel[pl.ds(pl.multiple_of(owner * VB, VB), VB), :] = ref[k]
     quarter = quarters[0].shape[0]
     for k, ref in enumerate(quarters):
         place = n_row * VB + ((c ^ (k // X)) * X + (r % X ^ (k % X))) * quarter
@@ -117,34 +115,24 @@
     for ref, place in ((hold_ref, x), (pass_ref, 1 - x)):
         spot = pl.ds(pl.multiple_of(VB + place * quarter, quarter), quarter)
         ref[...] = keep_ref[spot, :] + came_ref[spot, :]
-    scores_ref[...] = own_scores(dims, src_ref, keep_ref, came_ref).astype(scores_ref.dtype)
-
-
-def join_kernel(*refs):
-    for k, ref in enumerate(refs[:-1]):
-        refs[-1][k] = ref[...]
-
-
-def plane_kernel(hold_ref, came_ref, out_ref):
+    scores_ref[0] = own_scores(dims, src_ref, keep_ref, came_ref).astype(scores_ref.dtype)
+
+
+def join_kernel(held_ref, came_ref, out_ref):
+    count = held_ref.shape[0]
+    out_ref[:count] = held_ref[...]
+    out_ref[count:] = came_ref[...]
+
+
+def add_kernel(hold_ref, came_ref, out_ref):
     out_ref[...] = hold_ref[...] + came_ref[...]
 
 
-def sum_planes(planes, held):
-    z = lax.axis_index("row") // X
-    for k, plane in enumerate(planes):
-        held[z ^ k] = plane[...]
-    summed = held[0]
-    for k in range(1, len(planes)):
-        summed = summed + held[k]
-    return summed
-
-
-def hub_kernel(dims, src_ref, *refs):
-    planes, (out_ref, held) = refs[:-2], refs[-2:]
+def hub_kernel(dims, src_ref, held_ref, came_ref, out_ref):
     quarter = out_ref.shape[0]
     first = (lax.axis_index("col") * X + lax.axis_index("row") % X) * quarter
     tele = one_hot(first, quarter, src_ref[...])
-    out_ref[...] = (DAMP * sum_planes(planes, held) + 0.15 * tele).astype(out_ref.dtype)
+    out_ref[...] = (DAMP * (held_ref[...] + came_ref[...]) + 0.15 * tele).astype(out_ref.dtype)
 
 
 def pieces_kernel(keep_ref, came_ref, parts_ref):
@@ -198,9 +186,6 @@
     def other_both(x):
         devices = [(r, c) for r in range(n_row) for c in range(n_col)]
         return lax.ppermute(x, ("row", "col"), [(r * n_col + c, (r ^ 1) * n_col + 1 - c) for r, c in devices])
-
-    def along_z(blocks):
-        return [to_partner(block, X * k) for k, block in enumerate(blocks) if k > 0]
 
     def call(kernel, name, out_shape, *args, scratch=(), cost=0):
         return pl.pallas_call(
@@ -238,24 +223,32 @@
         name="first_terms",
     )(*in_hbm[:3], tile_count.reshape(1), in_hbm[3])
 
-    n_z = n_row // X
+    masks = [n_row // X - 1]
+    while masks[-1] > 1:
+        masks.append(masks[-1] // 2)
     for step in range(ITERS - 1):
         came = other_core(send)
-        own, hold, away = call(
+        held, hold, away = call(
             bind(spread_kernel, dims), "spread",
-            (bf16((VB, width)), f32((quarter, width)), f32((quarter, width))),
-            src, keep, came, cost=1)
+            (bf16((1, VB, width)), f32((quarter, width)), f32((quarter, width))),
+            src, keep, came, cost=2)
         away = other_side(away)
-        blocks = [own] + along_z([own] * n_z)
-        plane = call(plane_kernel, "plane_sum", f32((quarter, width)), hold, away, cost=20)
-        planes = [plane] + along_z([plane] * n_z)
-        across = other_side(call(join_kernel, "join_rows", bf16((n_z, VB, width)), *blocks, cost=2))
-        mine = call(bind(hub_kernel, dims), "hub_sums", bf16((quarter, width)), src, *planes,
-                    scratch=[pltpu.VMEM((n_z, quarter, width), jnp.float32)], cost=2)
+        flips = [0]
+        for mask in masks[:-1]:
+            far = to_partner(held, X * mask)
+            held = call(join_kernel, "join_near", bf16((2 * len(flips), VB, width)), held, far, cost=3)
+            flips += [flip ^ mask for flip in flips]
+        far = to_partner(held, X * masks[-1])
+        flips += [flip ^ masks[-1] for flip in flips]
+        near_across, far_across = other_side(held), other_side(far)
+        sums = call(add_kernel, "plane_sum", f32((quarter, width)), hold, away, cost=20)
+        for mask in masks[:0:-1]:
+            sums = call(add_kernel, "pair_sum", f32((quarter, width)), sums, to_partner(sums, X * mask), cost=1)
+        mine = call(bind(hub_kernel, dims), "hub_sums", bf16((quarter, width)), src, sums, to_partner(sums, X * masks[0]), cost=1)
         quarters = [mine, other_side(mine), other_core(mine), other_both(mine)]
         send, keep = call(
-            bind(second_kernel, dims), "later_terms", (f32((half, width)), f32((half, width))),
-            *blocks, across, *quarters, dense, scratch=product_scratch)
+            bind(second_kernel, dims, flips), "later_terms", (f32((half, width)), f32((half, width))),
+            held, far, near_across, far_across, *quarters, dense, scratch=product_scratch)
     came = other_core(send)
     parts = call(pieces_kernel, "hub_pieces", f32((n_row, piece, width)), keep, came)
     parts = lax.all_to_all(parts, "row", 0, 0)
@@ -347,7 +340,7 @@
         n_row, n_col = mesh.shape["row"], mesh.shape["col"]
         slots, side = tiles.shape[2:4]
         blocks = (n_col * VB + H) * (n_row * VB + H) // (side * side)
-        if n_col == 2 and n_row in (4, 8, 16) and blocks <= slots and H // (n_row * n_col) % 16 == 0:
+        if n_col == 2 and n_row in (8, 16) and blocks <= slots and H // (n_row * n_col) % 16 == 0:
             return fast_body(tiles, *rest)
         return plain_body(tiles, *rest)
 

time: 45.3 us -> 45.3 us (level)
  starting transfers between devices: 19.7 us -> 20.4 us
  waiting for transfers between devices: 17.4 us -> 16.7 us
    all_to_all x1, starting transfers between devices: 4.19 us -> 4.88 us  [fast_body(): parts = lax.all_to_all(parts, 'row', 0, 0)]
    ppermute x9 -> x8, waiting for transfers between devices: 6.43 us -> 5.82 us  [to_partner(): return lax.ppermute(x, 'row', [(r, r ^ flip) for r in range(n_row)])]
    ppermute x9 -> x8, starting transfers between devices: 14.3 us -> 13.9 us  [to_partner(): return lax.ppermute(x, 'row', [(r, r ^ flip) for r in range(n_row)])]
    pallas_call x8 -> x9, Pallas kernels: 3.12 us -> 3.07 us  [call(): pl.pallas_call(kernel, out_shape=out_shape, in_specs=[VMEM] * len(args),...]
  transfers between devices with their start and end apart: 14 -> 13, of which waited for: 7 -> 8; matrix products, arithmetic and copies ran while one was open for 0% -> 0% of each run, Pallas kernels for 2% -> 2%
where the time goes in v17:
time: 45.3 us; the launch traced here: 45 us
  starting transfers between devices  20.4 us (45%)
  waiting for transfers between devices  16.7 us (37%)
  Pallas kernels  6.47 us (14%)
  between operations  1.36 us (3%)
    ppermute x8, starting transfers between devices, to_partner(): return lax.ppermute(x, 'row', [(r, r ^ flip) for r in range(n_row)])  13.9 us
    all_to_all x1, waiting for transfers between devices, fast_body(): parts = lax.all_to_all(parts, 'row', 0, 0)  6.65 us
    ppermute x8, waiting for transfers between devices, to_partner(): return lax.ppermute(x, 'row', [(r, r ^ flip) for r in range(n_row)])  5.82 us
    all_to_all x1, starting transfers between devices, fast_body(): parts = lax.all_to_all(parts, 'row', 0, 0)  4.88 us
    pallas_call x1, Pallas kernels, fast_body(): pl.pallas_call(bind(first_kernel, dims), out_shape=(f32((half, width)), f...  3.4 us
    pallas_call x9, Pallas kernels, call(): pl.pallas_call(kernel, out_shape=out_shape, in_specs=[VMEM] * len(args),...  3.07 us
    ppermute x3, waiting for transfers between devices, other_core(): return lax.ppermute(x, 'col', [(0, 1), (1, 0)])  2.69 us
    ppermute x3, starting transfers between devices, other_core(): return lax.ppermute(x, 'col', [(0, 1), (1, 0)])  1.58 us
  transfers between devices with their start and end apart: 13, of which 8 were waited for; matrix products, arithmetic and copies ran while one was open for 0% of the time, Pallas kernels for 2%

profile of v17, /device:TPU:0, one launch (start us, length us, event | category | flops | bytes accessed | tf_op | source)
XLA Modules:
  0.0 45.0 jit_solution(13140084821430418340)
XLA Ops:
  0.6 0.0 copy-start
  1.3 3.4 %first_terms.1 = (f32[256,256]{1,0:T(8,128)S(1)}, f32[256,256]{1,0:T(8,128)S(1)}, bf16[1024,1280]{1,0:T(8,128)(2,1)S(1)}) custom-call(bf16[96,128,128]{2,1,0:T(8,128)(2,1)} %bitcast.12, s32[96]{0:T(128)} %bitcast.14, s32[96]{0:T(128)} %bitcast.15, s32[1]{0:T(128)} %bitcast.6.count_hbm, s32[1,256]{1,0:T(1,128)} %bitcast.7), custom_call_target="tpu_custom_call" | custom-call | tf_op jit(solution)/shard_map/first_terms/pallas_call | solution.py:206
  4.7 0.5 %collective-permute-start = (f32[256,256]{1,0:T(8,128)S(1)}, f32[256,256]{1,0:T(8,128)S(1)}, u32[]{:S(2)}, u32[]{:S(2)}) collective-permute-start(f32[256,256]{1,0:T(8,128)S(1)} %get-tuple-element.11), channel_id=1, source_target_pairs={{0,1},{1,0},{2,3},{3,2},{4,5},{5,4},{6,7},{7,6},{8,9},{9,8},{10,11... | collective-permute-start | bytes 786440 | tf_op jit(solution)/shard_map/ppermute | solution.py:178
  5.2 1.2 %collective-permute-done.came_ref = f32[256,256]{1,0:T(8,128)S(1)} collective-permute-done((f32[256,256]{1,0:T(8,128)S(1)}, f32[256,256]{1,0:T(8,128)S(1)}, u32[]{:S(2)}, u32[]{:S(2)}) %collective-permute-start) | collective-permute-done | bytes 262176 | tf_op jit(solution)/shard_map/ppermute | solution.py:178
  6.4 0.0 copy-done
  6.4 2.9 %collective-permute-start.5 = (f32[64,256]{1,0:T(8,128)S(1)}, f32[64,256]{1,0:T(8,128)S(1)}, u32[]{:S(2)}, u32[]{:S(2)}) collective-permute-start(f32[64,256]{1,0:T(8,128)S(1)} %get-tuple-element.14), channel_id=1, source_target_pairs={{0,2},{2,0},{4,6},{6,4},{8,10},{10,8},{12,14},{14,12},{1,3},{3,1},... | collective-permute-start | bytes 196616 | tf_op jit(solution)/shard_map/ppermute | solution.py:181
  9.4 3.6 %collective-permute-start.1 = (bf16[1,128,256]{2,1,0:T(8,128)(2,1)S(1)}, bf16[1,128,256]{2,1,0:T(8,128)(2,1)S(1)}, u32[]{:S(2)}, u32[]{:S(2)}) collective-permute-start(bf16[1,128,256]{2,1,0:T(8,128)(2,1)S(1)} %get-tuple-element.12.held_ref), channel_id=1, source_target_pairs={{0,12},{2,14},{4,8},{6,10},{8,4},{10,6},{12,0},{14,2},{1,13},{3,15... | collective-permute-start | bytes 196616 | tf_op jit(solution)/shard_map/ppermute | solution.py:181
  13.0 0.0 collective-permute-done.5.came_ref
  13.0 0.8 %collective-permute-start.6 = (f32[64,256]{1,0:T(8,128)S(1)}, f32[64,256]{1,0:T(8,128)S(1)}, u32[]{:S(2)}, u32[]{:S(2)}) collective-permute-start(f32[64,256]{1,0:T(8,128)S(1)} %plane_sum.1.hold_ref), channel_id=1, source_target_pairs={{0,4},{2,6},{4,0},{6,2},{8,12},{10,14},{12,8},{14,10},{1,5},{3,7},... | collective-permute-start | bytes 196616 | tf_op jit(solution)/shard_map/ppermute | solution.py:181
  13.8 1.8 %collective-permute-done.1.came_ref = bf16[1,128,256]{2,1,0:T(8,128)(2,1)S(1)} collective-permute-done((bf16[1,128,256]{2,1,0:T(8,128)(2,1)S(1)}, bf16[1,128,256]{2,1,0:T(8,128)(2,1)S(1)}, u32[]{:S(2)}, u32[]{:S(2)}) %collective-permute-start.1) | collective-permute-done | bytes 65568 | tf_op jit(solution)/shard_map/ppermute | solution.py:181
  15.6 0.8 %collective-permute-start.2 = (bf16[2,128,256]{2,1,0:T(8,128)(2,1)S(1)}, bf16[2,128,256]{2,1,0:T(8,128)(2,1)S(1)}, u32[]{:S(2)}, u32[]{:S(2)}) collective-permute-start(bf16[2,128,256]{2,1,0:T(8,128)(2,1)S(1)} %join_near.1.refs_0_), channel_id=1, source_target_pairs={{0,4},{2,6},{4,0},{6,2},{8,12},{10,14},{12,8},{14,10},{1,5},{3,7},... | collective-permute-start | bytes 393224 | tf_op jit(solution)/shard_map/ppermute | solution.py:181
  16.4 1.3 %collective-permute-done.6.came_ref = f32[64,256]{1,0:T(8,128)S(1)} collective-permute-done((f32[64,256]{1,0:T(8,128)S(1)}, f32[64,256]{1,0:T(8,128)S(1)}, u32[]{:S(2)}, u32[]{:S(2)}) %collective-permute-start.6) | collective-permute-done | bytes 65568 | tf_op jit(solution)/shard_map/ppermute | solution.py:181
  17.7 2.6 %collective-permute-start.7 = (f32[64,256]{1,0:T(8,128)S(1)}, f32[64,256]{1,0:T(8,128)S(1)}, u32[]{:S(2)}, u32[]{:S(2)}) collective-permute-start(f32[64,256]{1,0:T(8,128)S(1)} %pair_sum.1.held_ref), channel_id=1, source_target_pairs={{0,12},{2,14},{4,8},{6,10},{8,4},{10,6},{12,0},{14,2},{1,13},{3,15... | collective-permute-start | bytes 196616 | tf_op jit(solution)/shard_map/ppermute | solution.py:181
  20.3 2.0 %collective-permute-start.3 = (bf16[2,128,256]{2,1,0:T(8,128)(2,1)S(1)}, bf16[2,128,256]{2,1,0:T(8,128)(2,1)S(1)}, u32[]{:S(2)}, u32[]{:S(2)}) collective-permute-start(bf16[2,128,256]{2,1,0:T(8,128)(2,1)S(1)} %join_near.1.refs_0_), channel_id=1, source_target_pairs={{0,2},{2,0},{4,6},{6,4},{8,10},{10,8},{12,14},{14,12},{1,3},{3,1},... | collective-permute-start | bytes 393224 | tf_op jit(solution)/shard_map/ppermute | solution.py:181
  22.3 0.0 collective-permute-done.2.refs_1_
  22.3 0.1 collective-permute-start.4
  22.4 1.5 %collective-permute-done.7.came_ref = f32[64,256]{1,0:T(8,128)S(1)} collective-permute-done((f32[64,256]{1,0:T(8,128)S(1)}, f32[64,256]{1,0:T(8,128)S(1)}, u32[]{:S(2)}, u32[]{:S(2)}) %collective-permute-start.7) | collective-permute-done | bytes 65568 | tf_op jit(solution)/shard_map/ppermute | solution.py:181
  23.9 0.1 collective-permute-start.10
  24.0 1.0 %collective-permute-start.9 = (bf16[64,256]{1,0:T(8,128)(2,1)S(1)}, bf16[64,256]{1,0:T(8,128)(2,1)S(1)}, u32[]{:S(2)}, u32[]{:S(2)}) collective-permute-start(bf16[64,256]{1,0:T(8,128)(2,1)S(1)} %hub_sums.1.refs_4_), channel_id=1, source_target_pairs={{0,1},{1,0},{2,3},{3,2},{4,5},{5,4},{6,7},{7,6},{8,9},{9,8},{10,11... | collective-permute-start | bytes 98312 | tf_op jit(solution)/shard_map/ppermute | solution.py:178
  25.0 1.1 %collective-permute-start.8 = (bf16[64,256]{1,0:T(8,128)(2,1)S(1)}, bf16[64,256]{1,0:T(8,128)(2,1)S(1)}, u32[]{:S(2)}, u32[]{:S(2)}) collective-permute-start(bf16[64,256]{1,0:T(8,128)(2,1)S(1)} %hub_sums.1.refs_4_), channel_id=1, source_target_pairs={{0,2},{2,0},{4,6},{6,4},{8,10},{10,8},{12,14},{14,12},{1,3},{3,1},... | collective-permute-start | bytes 98312 | tf_op jit(solution)/shard_map/ppermute | solution.py:181
  26.1 0.0 collective-permute-done.3.refs_2_
  26.1 1.6 %collective-permute-done.10.refs_7_ = bf16[64,256]{1,0:T(8,128)(2,1)S(1)} collective-permute-done((bf16[64,256]{1,0:T(8,128)(2,1)S(1)}, bf16[64,256]{1,0:T(8,128)(2,1)S(1)}, u32[]{:S(2)}, u32[]{:S(2)}) %collective-permute-start.10) | collective-permute-done | bytes 32800 | tf_op jit(solution)/shard_map/ppermute | solution.py:188
  27.7 0.0 collective-permute-done.9.refs_6_
  27.7 1.2 %collective-permute-done.8.refs_5_ = bf16[64,256]{1,0:T(8,128)(2,1)S(1)} collective-permute-done((bf16[64,256]{1,0:T(8,128)(2,1)S(1)}, bf16[64,256]{1,0:T(8,128)(2,1)S(1)}, u32[]{:S(2)}, u32[]{:S(2)}) %collective-permute-start.8) | collective-permute-done | bytes 32800 | tf_op jit(solution)/shard_map/ppermute | solution.py:181
  28.9 0.0 collective-permute-done.4.refs_3_
  28.9 1.0 %later_terms.1 = (f32[256,256]{1,0:T(8,128)S(1)}, f32[256,256]{1,0:T(8,128)S(1)}) custom-call(bf16[2,128,256]{2,1,0:T(8,128)(2,1)S(1)} %join_near.1.refs_0_, bf16[2,128,256]{2,1,0:T(8,128)(2,1)S(1)} %collective-permute-done.2.refs_1_, bf16[2,128,256]{2,1,0:T(8,128)(2,1)S(1)} %collective-permute-done.3.refs_2_, ...), custom_call_target="tpu_custom_call" | custom-call | tf_op jit(solution)/shard_map/later_terms/pallas_call | solution.py:191
  29.9 0.1 collective-permute-start.11
  30.0 1.5 %collective-permute-done.11.came_ref = f32[256,256]{1,0:T(8,128)S(1)} collective-permute-done((f32[256,256]{1,0:T(8,128)S(1)}, f32[256,256]{1,0:T(8,128)S(1)}, u32[]{:S(2)}, u32[]{:S(2)}) %collective-permute-start.11) | collective-permute-done | bytes 262176 | tf_op jit(solution)/shard_map/ppermute | solution.py:178
  31.5 0.7 %hub_pieces.1 = f32[8,16,256]{2,1,0:T(8,128)} custom-call(f32[256,256]{1,0:T(8,128)S(1)} %get-tuple-element.16.keep_ref, f32[256,256]{1,0:T(8,128)S(1)} %collective-permute-done.11.came_ref), custom_call_target="tpu_custom_call" | custom-call | tf_op jit(solution)/shard_map/hub_pieces/pallas_call | solution.py:191
  32.1 4.9 %all-to-all-start = ((f32[8,16,256]{2,1,0:T(8,128)}), f32[8,16,256]{2,1,0:T(8,128)S(1)}, u32[]{:S(2)}, u32[]{:S(2)}) async-start(f32[8,16,256]{2,1,0:T(8,128)} %hub_pieces.1), calls=%async_computation | async-start | bytes 262144 | tf_op jit(solution)/shard_map/all_to_all | solution.py:254
  37.0 0.7 %last_scores.1 = f32[128,256]{1,0:T(8,128)} custom-call(s32[1,256]{1,0:T(1,128)S(1)} %bitcast.10, f32[256,256]{1,0:T(8,128)S(1)} %get-tuple-element.16.keep_ref, f32[256,256]{1,0:T(8,128)S(1)} %collective-permute-done.11.came_ref), custom_call_target="tpu_custom_call" | custom-call | tf_op jit(solution)/shard_map/last_scores/pallas_call | solution.py:191
  37.7 6.7 %all-to-all-done.parts_ref = f32[8,16,256]{2,1,0:T(8,128)S(1)} async-done(((f32[8,16,256]{2,1,0:T(8,128)}), f32[8,16,256]{2,1,0:T(8,128)S(1)}, u32[]{:S(2)}, u32[]{:S(2)}) %all-to-all-start) | async-done | bytes 131104 | tf_op jit(solution)/shard_map/all_to_all | solution.py:254
  44.4 0.6 %last_hubs.1 = f32[16,256]{1,0:T(8,128)} custom-call(s32[1,256]{1,0:T(1,128)S(1)} %bitcast.11, f32[8,16,256]{2,1,0:T(8,128)S(1)} %all-to-all-done.parts_ref), custom_call_target="tpu_custom_call" | custom-call | tf_op jit(solution)/shard_map/last_hubs/pallas_call | solution.py:191
  (5 shorter events, 0.1 us)
Async XLA Ops:
  0.6 5.8 %copy-start = (s32[256]{0:T(256)S(1)}, s32[256]{0:T(256)}, u32[]{:S(2)}) copy-start(s32[256]{0:T(256)} %param.9) | copy-start | bytes 3076
  4.7 1.7 %collective-permute-start = (f32[256,256]{1,0:T(8,128)S(1)}, f32[256,256]{1,0:T(8,128)S(1)}, u32[]{:S(2)}, u32[]{:S(2)}) collective-permute-start(f32[256,256]{1,0:T(8,128)S(1)} %get-tuple-element.11), channel_id=1, source_target_pairs={{0,1},{1,0},{2,3},{3,2},{4,5},{5,4},{6,7},{7,6},{8,9},{9,8},{10,11... | collective-permute-start | bytes 786440 | tf_op jit(solution)/shard_map/ppermute | solution.py:178
  6.4 6.5 %collective-permute-start.5 = (f32[64,256]{1,0:T(8,128)S(1)}, f32[64,256]{1,0:T(8,128)S(1)}, u32[]{:S(2)}, u32[]{:S(2)}) collective-permute-start(f32[64,256]{1,0:T(8,128)S(1)} %get-tuple-element.14), channel_id=1, source_target_pairs={{0,2},{2,0},{4,6},{6,4},{8,10},{10,8},{12,14},{14,12},{1,3},{3,1},... | collective-permute-start | bytes 196616 | tf_op jit(solution)/shard_map/ppermute | solution.py:181
  9.4 6.2 %collective-permute-start.1 = (bf16[1,128,256]{2,1,0:T(8,128)(2,1)S(1)}, bf16[1,128,256]{2,1,0:T(8,128)(2,1)S(1)}, u32[]{:S(2)}, u32[]{:S(2)}) collective-permute-start(bf16[1,128,256]{2,1,0:T(8,128)(2,1)S(1)} %get-tuple-element.12.held_ref), channel_id=1, source_target_pairs={{0,12},{2,14},{4,8},{6,10},{8,4},{10,6},{12,0},{14,2},{1,13},{3,15... | collective-permute-start | bytes 196616 | tf_op jit(solution)/shard_map/ppermute | solution.py:181
  13.0 4.7 %collective-permute-start.6 = (f32[64,256]{1,0:T(8,128)S(1)}, f32[64,256]{1,0:T(8,128)S(1)}, u32[]{:S(2)}, u32[]{:S(2)}) collective-permute-start(f32[64,256]{1,0:T(8,128)S(1)} %plane_sum.1.hold_ref), channel_id=1, source_target_pairs={{0,4},{2,6},{4,0},{6,2},{8,12},{10,14},{12,8},{14,10},{1,5},{3,7},... | collective-permute-start | bytes 196616 | tf_op jit(solution)/shard_map/ppermute | solution.py:181
  15.6 6.7 %collective-permute-start.2 = (bf16[2,128,256]{2,1,0:T(8,128)(2,1)S(1)}, bf16[2,128,256]{2,1,0:T(8,128)(2,1)S(1)}, u32[]{:S(2)}, u32[]{:S(2)}) collective-permute-start(bf16[2,128,256]{2,1,0:T(8,128)(2,1)S(1)} %join_near.1.refs_0_), channel_id=1, source_target_pairs={{0,4},{2,6},{4,0},{6,2},{8,12},{10,14},{12,8},{14,10},{1,5},{3,7},... | collective-permute-start | bytes 393224 | tf_op jit(solution)/shard_map/ppermute | solution.py:181
  17.7 6.1 %collective-permute-start.7 = (f32[64,256]{1,0:T(8,128)S(1)}, f32[64,256]{1,0:T(8,128)S(1)}, u32[]{:S(2)}, u32[]{:S(2)}) collective-permute-start(f32[64,256]{1,0:T(8,128)S(1)} %pair_sum.1.held_ref), channel_id=1, source_target_pairs={{0,12},{2,14},{4,8},{6,10},{8,4},{10,6},{12,0},{14,2},{1,13},{3,15... | collective-permute-start | bytes 196616 | tf_op jit(solution)/shard_map/ppermute | solution.py:181
  20.3 5.8 %collective-permute-start.3 = (bf16[2,128,256]{2,1,0:T(8,128)(2,1)S(1)}, bf16[2,128,256]{2,1,0:T(8,128)(2,1)S(1)}, u32[]{:S(2)}, u32[]{:S(2)}) collective-permute-start(bf16[2,128,256]{2,1,0:T(8,128)(2,1)S(1)} %join_near.1.refs_0_), channel_id=1, source_target_pairs={{0,2},{2,0},{4,6},{6,4},{8,10},{10,8},{12,14},{14,12},{1,3},{3,1},... | collective-permute-start | bytes 393224 | tf_op jit(solution)/shard_map/ppermute | solution.py:181
  22.3 6.6 %collective-permute-start.4 = (bf16[2,128,256]{2,1,0:T(8,128)(2,1)S(1)}, bf16[2,128,256]{2,1,0:T(8,128)(2,1)S(1)}, u32[]{:S(2)}, u32[]{:S(2)}) collective-permute-start(bf16[2,128,256]{2,1,0:T(8,128)(2,1)S(1)} %collective-permute-done.2.refs_1_), channel_id=1, source_target_pairs={{0,2},{2,0},{4,6},{6,4},{8,10},{10,8},{12,14},{14,12},{1,3},{3,1},... | collective-permute-start | bytes 393224 | tf_op jit(solution)/shard_map/ppermute | solution.py:181
  23.9 3.8 %collective-permute-start.10 = (bf16[64,256]{1,0:T(8,128)(2,1)S(1)}, bf16[64,256]{1,0:T(8,128)(2,1)S(1)}, u32[]{:S(2)}, u32[]{:S(2)}) collective-permute-start(bf16[64,256]{1,0:T(8,128)(2,1)S(1)} %hub_sums.1.refs_4_), channel_id=1, source_target_pairs={{0,3},{1,2},{2,1},{3,0},{4,7},{5,6},{6,5},{7,4},{8,11},{9,10},{10,... | collective-permute-start | bytes 98312 | tf_op jit(solution)/shard_map/ppermute | solution.py:188
  24.0 3.7 %collective-permute-start.9 = (bf16[64,256]{1,0:T(8,128)(2,1)S(1)}, bf16[64,256]{1,0:T(8,128)(2,1)S(1)}, u32[]{:S(2)}, u32[]{:S(2)}) collective-permute-start(bf16[64,256]{1,0:T(8,128)(2,1)S(1)} %hub_sums.1.refs_4_), channel_id=1, source_target_pairs={{0,1},{1,0},{2,3},{3,2},{4,5},{5,4},{6,7},{7,6},{8,9},{9,8},{10,11... | collective-permute-start | bytes 98312 | tf_op jit(solution)/shard_map/ppermute | solution.py:178
  25.0 3.9 %collective-permute-start.8 = (bf16[64,256]{1,0:T(8,128)(2,1)S(1)}, bf16[64,256]{1,0:T(8,128)(2,1)S(1)}, u32[]{:S(2)}, u32[]{:S(2)}) collective-permute-start(bf16[64,256]{1,0:T(8,128)(2,1)S(1)} %hub_sums.1.refs_4_), channel_id=1, source_target_pairs={{0,2},{2,0},{4,6},{6,4},{8,10},{10,8},{12,14},{14,12},{1,3},{3,1},... | collective-permute-start | bytes 98312 | tf_op jit(solution)/shard_map/ppermute | solution.py:181
  29.9 1.6 %collective-permute-start.11 = (f32[256,256]{1,0:T(8,128)S(1)}, f32[256,256]{1,0:T(8,128)S(1)}, u32[]{:S(2)}, u32[]{:S(2)}) collective-permute-start(f32[256,256]{1,0:T(8,128)S(1)} %get-tuple-element.17), channel_id=1, source_target_pairs={{0,1},{1,0},{2,3},{3,2},{4,5},{5,4},{6,7},{7,6},{8,9},{9,8},{10,11... | collective-permute-start | bytes 786440 | tf_op jit(solution)/shard_map/ppermute | solution.py:178
  32.1 12.2 %all-to-all-start = ((f32[8,16,256]{2,1,0:T(8,128)}), f32[8,16,256]{2,1,0:T(8,128)S(1)}, u32[]{:S(2)}, u32[]{:S(2)}) async-start(f32[8,16,256]{2,1,0:T(8,128)} %hub_pieces.1), calls=%async_computation | async-start | bytes 262144 | tf_op jit(solution)/shard_map/all_to_all | solution.py:254

commit v18 on v17

--- a/solution.py
+++ b/solution.py
@@ -30,23 +30,13 @@
     return (ids == src).astype(jnp.float32)
 
 
-def write_terms(dims, block, prod_ref, dense_ref, panel_ref, send_ref, keep_ref):
+def first_kernel(dims, tiles_ref, rows_hbm, cols_hbm, count_hbm, src_hbm,
+                 send_ref, keep_ref, dense_send_ref, dense_keep_ref,
+                 held, rows_ref, cols_ref, count_ref, src_ref, total, panel, sems, small):
     n_row, n_col, side = dims
-    rows = dense_ref.shape[0] // 2
+    n_rows = n_col * VB + H
+    piece = H // (n_row * n_col)
     c = lax.axis_index("col")
-    prod = jnp.dot(dense_ref[...], panel_ref[...], preferred_element_type=jnp.float32)
-    prod_ref[...] = prod[:rows] + prod[rows:]
-    for ref, col in ((keep_ref, c), (send_ref, 1 - c)):
-        ref[:VB] = prod_ref[pl.ds(pl.multiple_of(col * VB, VB), VB), :]
-        for k in range(H // n_col // block):
-            start = n_col * VB + (k * n_col + col) * block
-            ref[VB + k * block:VB + (k + 1) * block] = prod_ref[pl.ds(pl.multiple_of(start, block), block), :]
-
-
-def first_kernel(dims, tiles_ref, rows_hbm, cols_hbm, count_hbm, src_hbm, send_ref, keep_ref, dense_ref,
-                 held, rows_ref, cols_ref, count_ref, src_ref, total, panel, prod, sems, small):
-    n_row, n_col, side = dims
-    n_rows = dense_ref.shape[0] // 2
     pairs = ((src_hbm, src_ref), (rows_hbm, rows_ref), (cols_hbm, cols_ref), (count_hbm, count_ref))
     scalars = [pltpu.make_async_copy(a, b, small.at[i]) for i, (a, b) in enumerate(pairs)]
     copies = []
@@ -60,7 +50,7 @@
         copy.wait()
     src = src_ref[...]
     for r in range(n_row):
-        first = H + (r * n_col + lax.axis_index("col")) * VB
+        first = H + (r * n_col + c) * VB
         panel[pl.ds(r * VB, VB), :] = one_hot(first, VB, src).astype(jnp.bfloat16)
     panel[pl.ds(n_row * VB, H), :] = one_hot(0, H, src).astype(jnp.bfloat16)
     count = count_ref[0]
@@ -76,46 +66,54 @@
     for i, copy in enumerate(copies):
         copy.wait()
         lax.fori_loop(i * CHUNK, (i + 1) * CHUNK, add_tile, 0, unroll=4)
-    for r in range(0, n_rows, side):
-        whole = total[pl.ds(r, side), :]
-        high = whole.astype(jnp.bfloat16)
-        dense_ref[pl.ds(r, side), :] = high
-        dense_ref[pl.ds(n_rows + r, side), :] = (whole - high.astype(jnp.float32)).astype(jnp.bfloat16)
-    write_terms(dims, H // n_col, prod, dense_ref, panel, send_ref, keep_ref)
-
-
-def second_kernel(dims, flips, *refs):
+    half = n_rows // n_col
+    for dense, out, core in ((dense_send_ref, send_ref, 1 - c), (dense_keep_ref, keep_ref, c)):
+        chunks = [(0, core * VB, VB)]
+        for r in range(n_row):
+            chunks.append((VB + r * piece, n_col * VB + (r * n_col + core) * piece, piece))
+        for at, start, size in chunks:
+            whole = total[pl.ds(pl.multiple_of(start, size), size), :]
+            high = whole.astype(jnp.bfloat16)
+            dense[at:at + size] = high
+            dense[half + at:half + at + size] = (whole - high.astype(jnp.float32)).astype(jnp.bfloat16)
+        prod = jnp.dot(dense[...], panel[...], preferred_element_type=jnp.float32)
+        out[...] = prod[:half] + prod[half:]
+
+
+def second_kernel(dims, flips, src_ref, *refs):
     n_row, n_col, side = dims
     n_z = n_row // X
-    blocks, quarters = refs[:4], refs[4:4 + X * n_col]
-    dense_ref, send_ref, keep_ref, panel, prod = refs[4 + X * n_col:]
-    half = H // n_col
+    mine, theirs, quarters = refs[:X], refs[X:2 * X], refs[2 * X:2 * X + X * n_col]
+    dense_mine, dense_theirs, scores_ref, parts_ref, panel = refs[2 * X + X * n_col:]
+    piece = parts_ref.shape[1]
     r, c = lax.axis_index("row"), lax.axis_index("col")
-    near, far = flips[:n_z // 2], flips[n_z // 2:]
-    for ref, group, x in ((blocks[0], near, 0), (blocks[1], far, 0), (blocks[2], near, 1), (blocks[3], far, 1)):
-        for k, flip in enumerate(group):
-            owner = r ^ (X * flip + x)
-            panel[pl.ds(pl.multiple_of(owner * VB, VB), VB), :] = ref[k]
-    quarter = quarters[0].shape[0]
-    for k, ref in enumerate(quarters):
-        place = n_row * VB + ((c ^ (k // X)) * X + (r % X ^ (k % X))) * quarter
-        panel[pl.ds(pl.multiple_of(place, quarter), quarter), :] = ref[...]
-    write_terms(dims, half // n_row, prod, dense_ref, panel, send_ref, keep_ref)
-
-
-def own_scores(dims, src_ref, keep_ref, came_ref):
-    first = H + (lax.axis_index("row") * dims[1] + lax.axis_index("col")) * VB
-    tele = one_hot(first, VB, src_ref[...])
-    return DAMP * (keep_ref[:VB] + came_ref[:VB]) + 0.15 * tele
+    for at, refs_of in enumerate((mine, theirs)):
+        for x, ref in enumerate(refs_of):
+            for k, flip in enumerate(flips):
+                owner = r ^ (X * flip + x)
+                panel[at, pl.ds(pl.multiple_of(owner * VB, VB), VB), :] = ref[k]
+        for k, ref in enumerate(quarters):
+            for i in range(n_z):
+                row = ((r % X ^ (k % X)) * n_z + i) * n_col + (c ^ (k // X))
+                place = pl.ds(pl.multiple_of(n_row * VB + row * piece, piece), piece)
+                panel[at, place, :] = ref[i * piece:(i + 1) * piece]
+    prod = jnp.dot(dense_mine[...], panel[0], preferred_element_type=jnp.float32)
+    prod += jnp.dot(dense_theirs[...], panel[1], preferred_element_type=jnp.float32)
+    half = prod.shape[0] // 2
+    total = prod[:half] + prod[half:]
+    tele = one_hot(H + (r * n_col + c) * VB, VB, src_ref[...])
+    scores_ref[...] = DAMP * total[:VB] + 0.15 * tele
+    parts_ref[...] = total[VB:].reshape(parts_ref.shape)
 
 
 def spread_kernel(dims, src_ref, keep_ref, came_ref, scores_ref, hold_ref, pass_ref):
     quarter = hold_ref.shape[0]
-    x = lax.axis_index("row") % X
-    for ref, place in ((hold_ref, x), (pass_ref, 1 - x)):
+    r, c = lax.axis_index("row"), lax.axis_index("col")
+    for ref, place in ((hold_ref, r % X), (pass_ref, 1 - r % X)):
         spot = pl.ds(pl.multiple_of(VB + place * quarter, quarter), quarter)
         ref[...] = keep_ref[spot, :] + came_ref[spot, :]
-    scores_ref[0] = own_scores(dims, src_ref, keep_ref, came_ref).astype(scores_ref.dtype)
+    tele = one_hot(H + (r * dims[1] + c) * VB, VB, src_ref[...])
+    scores_ref[0] = (DAMP * (keep_ref[:VB] + came_ref[:VB]) + 0.15 * tele).astype(scores_ref.dtype)
 
 
 def join_kernel(held_ref, came_ref, out_ref):
@@ -129,21 +127,13 @@
 
 
 def hub_kernel(dims, src_ref, held_ref, came_ref, out_ref):
-    quarter = out_ref.shape[0]
-    first = (lax.axis_index("col") * X + lax.axis_index("row") % X) * quarter
-    tele = one_hot(first, quarter, src_ref[...])
+    n_row, n_col, side = dims
+    piece = H // (n_row * n_col)
+    r, c = lax.axis_index("row"), lax.axis_index("col")
+    at = lax.broadcasted_iota(jnp.int32, out_ref.shape, 0)
+    ids = ((r % X * (n_row // X) + at // piece) * n_col + c) * piece + at % piece
+    tele = (ids == src_ref[...]).astype(jnp.float32)
     out_ref[...] = (DAMP * (held_ref[...] + came_ref[...]) + 0.15 * tele).astype(out_ref.dtype)
-
-
-def pieces_kernel(keep_ref, came_ref, parts_ref):
-    piece = parts_ref.shape[1]
-    for k in range(parts_ref.shape[0]):
-        spot = slice(VB + k * piece, VB + (k + 1) * piece)
-        parts_ref[k] = keep_ref[spot, :] + came_ref[spot, :]
-
-
-def last_scores_kernel(dims, src_ref, keep_ref, came_ref, scores_ref):
-    scores_ref[...] = own_scores(dims, src_ref, keep_ref, came_ref)
 
 
 def last_hubs_kernel(dims, src_ref, parts_ref, out_ref):
@@ -169,11 +159,6 @@
     src = sources.reshape(1, width)
     half = VB + n_row * piece
     quarter = H // n_col // X
-    product_scratch = [
-        pltpu.VMEM((n_cols, width), jnp.bfloat16),
-        pltpu.VMEM((n_rows, width), jnp.float32),
-    ]
-
     def other_core(x):
         return lax.ppermute(x, "col", [(0, 1), (1, 0)])
 
@@ -187,27 +172,31 @@
         devices = [(r, c) for r in range(n_row) for c in range(n_col)]
         return lax.ppermute(x, ("row", "col"), [(r * n_col + c, (r ^ 1) * n_col + 1 - c) for r, c in devices])
 
-    def call(kernel, name, out_shape, *args, scratch=(), cost=0):
+    def call(kernel, name, out_shape, *args, scratch=(), after=(), cost=0):
+        def body(*refs):
+            kernel(*refs[:len(args)], *refs[len(args) + len(after):])
+
         return pl.pallas_call(
-            kernel,
+            body,
             out_shape=out_shape,
-            in_specs=[VMEM] * len(args),
+            in_specs=[VMEM] * len(args) + [pl.BlockSpec(memory_space=pl.ANY)] * len(after),
             out_specs=jax.tree.map(lambda _: VMEM, out_shape),
             scratch_shapes=scratch,
             compiler_params=params(),
             cost_estimate=pl.CostEstimate(flops=cost * MICRO, bytes_accessed=0, transcendentals=0),
             name=name,
-        )(*args)
+        )(*args, *after)
 
     bind = functools.partial
 
     in_hbm = [pltpu.with_memory_space_constraint(x, pltpu.HBM) for x in (
         tiles.reshape(slots, side, side), tile_row.reshape(slots), tile_col.reshape(slots), src)]
-    send, keep, dense = pl.pallas_call(
+    dense_shape = bf16((2 * half, n_cols))
+    send, keep, dense_send, dense_keep = pl.pallas_call(
         bind(first_kernel, dims),
-        out_shape=(f32((half, width)), f32((half, width)), bf16((2 * n_rows, n_cols))),
+        out_shape=(f32((half, width)), f32((half, width)), dense_shape, dense_shape),
         in_specs=[HBM] * 5,
-        out_specs=[VMEM] * 3,
+        out_specs=[VMEM] * 4,
         scratch_shapes=[
             pltpu.VMEM((slots, side, side), jnp.bfloat16),
             pltpu.SMEM((slots,), jnp.int32),
@@ -215,7 +204,7 @@
             pltpu.SMEM((1,), jnp.int32),
             pltpu.VMEM((1, width), jnp.int32),
             pltpu.VMEM((n_rows + side, n_cols), jnp.float32),
-        ] + product_scratch + [
+            pltpu.VMEM((n_cols, width), jnp.bfloat16),
             pltpu.SemaphoreType.DMA((slots // CHUNK,)),
             pltpu.SemaphoreType.DMA((4,)),
         ],
@@ -226,33 +215,36 @@
     masks = [n_row // X - 1]
     while masks[-1] > 1:
         masks.append(masks[-1] // 2)
-    for step in range(ITERS - 1):
-        came = other_core(send)
-        held, hold, away = call(
-            bind(spread_kernel, dims), "spread",
-            (bf16((1, VB, width)), f32((quarter, width)), f32((quarter, width))),
-            src, keep, came, cost=2)
-        away = other_side(away)
-        flips = [0]
-        for mask in masks[:-1]:
-            far = to_partner(held, X * mask)
-            held = call(join_kernel, "join_near", bf16((2 * len(flips), VB, width)), held, far, cost=3)
-            flips += [flip ^ mask for flip in flips]
-        far = to_partner(held, X * masks[-1])
-        flips += [flip ^ masks[-1] for flip in flips]
-        near_across, far_across = other_side(held), other_side(far)
-        sums = call(add_kernel, "plane_sum", f32((quarter, width)), hold, away, cost=20)
-        for mask in masks[:0:-1]:
-            sums = call(add_kernel, "pair_sum", f32((quarter, width)), sums, to_partner(sums, X * mask), cost=1)
-        mine = call(bind(hub_kernel, dims), "hub_sums", bf16((quarter, width)), src, sums, to_partner(sums, X * masks[0]), cost=1)
-        quarters = [mine, other_side(mine), other_core(mine), other_both(mine)]
-        send, keep = call(
-            bind(second_kernel, dims, flips), "later_terms", (f32((half, width)), f32((half, width))),
-            held, far, near_across, far_across, *quarters, dense, scratch=product_scratch)
-    came = other_core(send)
-    parts = call(pieces_kernel, "hub_pieces", f32((n_row, piece, width)), keep, came)
+    held, hold, away = call(
+        bind(spread_kernel, dims), "spread",
+        (bf16((1, VB, width)), f32((quarter, width)), f32((quarter, width))),
+        src, keep, other_core(send), cost=2)
+    away = other_side(away)
+    flips = [0]
+    for mask in masks[:-1]:
+        far = to_partner(held, X * mask)
+        held = call(join_kernel, "join_near", bf16((2 * len(flips), VB, width)), held, far, cost=3)
+        flips += [flip ^ mask for flip in flips]
+    far = to_partner(held, X * masks[-1])
+    flips += [flip ^ masks[-1] for flip in flips]
+    near_across, far_across = other_side(held), other_side(far)
+    blocks = bf16((len(flips), VB, width))
+    mine = [call(join_kernel, "join_line", blocks, held, far, cost=12)]
+    theirs = [other_core(mine[0])]
+    mine.append(call(join_kernel, "join_across", blocks, near_across, far_across, cost=12))
+    theirs.append(other_core(mine[1]))
+    dense_came = other_core(dense_send)
+    sums = call(add_kernel, "plane_sum", f32((quarter, width)), hold, away, cost=2)
+    for mask in masks[:0:-1]:
+        sums = call(add_kernel, "pair_sum", f32((quarter, width)), sums, to_partner(sums, X * mask), cost=8)
+    hub = call(bind(hub_kernel, dims), "hub_sums", bf16((quarter, width)), src, sums, to_partner(sums, X * masks[0]),
+               after=[dense_came, theirs[0]], cost=5)
+    quarters = [hub, other_side(hub), other_core(hub), other_both(hub)]
+    scores, parts = call(
+        bind(second_kernel, dims, flips), "later_terms", (f32((VB, width)), f32((n_row, piece, width))),
+        src, *mine, *theirs, *quarters, dense_keep, dense_came,
+        scratch=[pltpu.VMEM((2, n_cols, width), jnp.bfloat16)])
     parts = lax.all_to_all(parts, "row", 0, 0)
-    scores = call(bind(last_scores_kernel, dims), "last_scores", f32((VB, width)), src, keep, came)
     hubs = call(bind(last_hubs_kernel, dims), "last_hubs", f32((piece, width)), src, parts)
     return scores.reshape(1, 1, VB, width), hubs
 
@@ -340,7 +332,7 @@
         n_row, n_col = mesh.shape["row"], mesh.shape["col"]
         slots, side = tiles.shape[2:4]
         blocks = (n_col * VB + H) * (n_row * VB + H) // (side * side)
-        if n_col == 2 and n_row in (8, 16) and blocks <= slots and H // (n_row * n_col) % 16 == 0:
+        if ITERS == 2 and n_col == 2 and n_row in (8, 16) and blocks <= slots and H // (n_row * n_col) % 16 == 0:
             return fast_body(tiles, *rest)
         return plain_body(tiles, *rest)
 

time: 45.3 us -> 46.4 us (1.024)
  blocking collectives: 0 us -> 13.5 us
  waiting for transfers between devices: 16.7 us -> 10.1 us
  starting transfers between devices: 20.4 us -> 15.6 us
  Pallas kernels: 6.47 us -> 5.61 us
    all_to_all x0 -> x1, blocking collectives: none -> 13.5 us  [fast_body(): parts = lax.all_to_all(parts, 'row', 0, 0)]
    all_to_all x1 -> x0, waiting for transfers between devices: 6.65 us -> none  [fast_body(): parts = lax.all_to_all(parts, 'row', 0, 0)]
    all_to_all x1 -> x0, starting transfers between devices: 4.88 us -> none  [fast_body(): parts = lax.all_to_all(parts, 'row', 0, 0)]
    ppermute x8, waiting for transfers between devices: 5.82 us -> 8.43 us  [to_partner(): return lax.ppermute(x, 'row', [(r, r ^ flip) for r in range(n_row)])]
    ppermute x3 -> x5, waiting for transfers between devices: 2.69 us -> 1.17 us  [other_core(): return lax.ppermute(x, 'col', [(0, 1), (1, 0)])]
    ppermute x1, waiting for transfers between devices: 1.55 us -> 0.49 us  [other_both(): lax.ppermute(x, ('row', 'col'), [(r * n_col + c, (r ^ 1) * n_col + 1 - c)...]
    ppermute x1, starting transfers between devices: 0.07 us -> 1.07 us  [other_both(): lax.ppermute(x, ('row', 'col'), [(r * n_col + c, (r ^ 1) * n_col + 1 - c)...]
    pallas_call x9, Pallas kernels: 3.07 us -> 2.35 us  [call(): pl.pallas_call(body, out_shape=out_shape, in_specs=[VMEM] * len(args) + [...]
  transfers between devices with their start and end apart: 13 -> 14, of which waited for: 8 -> 6; matrix products, arithmetic and copies ran while one was open for 0% -> 0% of each run, Pallas kernels for 2% -> 0%
where the time goes in v18:
time: 46.4 us; the launch traced here: 46.2 us
  starting transfers between devices  15.6 us (34%)
  blocking collectives  13.5 us (29%)
  waiting for transfers between devices  10.1 us (22%)
  Pallas kernels  5.61 us (12%)
  between operations  1.38 us (3%)
    ppermute x8, starting transfers between devices, to_partner(): return lax.ppermute(x, 'row', [(r, r ^ flip) for r in range(n_row)])  13.7 us
    all_to_all x1, blocking collectives, fast_body(): parts = lax.all_to_all(parts, 'row', 0, 0)  13.5 us
    ppermute x8, waiting for transfers between devices, to_partner(): return lax.ppermute(x, 'row', [(r, r ^ flip) for r in range(n_row)])  8.43 us
    pallas_call x1, Pallas kernels, fast_body(): pl.pallas_call(bind(first_kernel, dims), out_shape=(f32((half, width)), f...  3.26 us
    pallas_call x9, Pallas kernels, call(): pl.pallas_call(body, out_shape=out_shape, in_specs=[VMEM] * len(args) + [...  2.35 us
    ppermute x5, waiting for transfers between devices, other_core(): return lax.ppermute(x, 'col', [(0, 1), (1, 0)])  1.17 us
    ppermute x1, starting transfers between devices, other_both(): lax.ppermute(x, ('row', 'col'), [(r * n_col + c, (r ^ 1) * n_col + 1 - c)...  1.07 us
  transfers between devices with their start and end apart: 14, of which 6 were waited for; matrix products, arithmetic and copies ran while one was open for 0% of the time, Pallas kernels for 0%

profile of v18, /device:TPU:0, one launch (start us, length us, event | category | flops | bytes accessed | tf_op | source)
XLA Modules:
  0.0 46.2 jit_solution(1529215619016977595)
XLA Ops:
  1.3 0.0 copy-start
  1.3 3.3 %first_terms.1 = (f32[256,256]{1,0:T(8,128)S(1)}, f32[256,256]{1,0:T(8,128)S(1)}, bf16[512,1280]{1,0:T(8,128)(2,1)S(1)}, bf16[512,1280]{1,0:T(8,128)(2,1)S(1)}) custom-call(bf16[96,128,128]{2,1,0:T(8,128)(2,1)} %bitcast.12, s32[96]{0:T(128)} %bitcast.13, s32[96]{0:T(128)} %bitcast.14, s32[1]{0:T(128)} %bitcast.6.count_hbm, s32[1,256]{1,0:T(1,128)} %bitcast.7), custom_call_target="tpu_custom_call" | custom-call | tf_op jit(solution)/shard_map/first_terms/pallas_call | solution.py:195
  4.6 0.5 %collective-permute-start = (f32[256,256]{1,0:T(8,128)S(1)}, f32[256,256]{1,0:T(8,128)S(1)}, u32[]{:S(2)}, u32[]{:S(2)}) collective-permute-start(f32[256,256]{1,0:T(8,128)S(1)} %get-tuple-element.12), channel_id=1, source_target_pairs={{0,1},{1,0},{2,3},{3,2},{4,5},{5,4},{6,7},{7,6},{8,9},{9,8},{10,11... | collective-permute-start | bytes 786440 | tf_op jit(solution)/shard_map/ppermute | solution.py:163
  5.1 1.2 %collective-permute-done.refs_2_ = f32[256,256]{1,0:T(8,128)S(1)} collective-permute-done((f32[256,256]{1,0:T(8,128)S(1)}, f32[256,256]{1,0:T(8,128)S(1)}, u32[]{:S(2)}, u32[]{:S(2)}) %collective-permute-start) | collective-permute-done | bytes 262176 | tf_op jit(solution)/shard_map/ppermute | solution.py:163
  6.2 0.0 copy-done
  6.3 2.9 %collective-permute-start.7 = (f32[64,256]{1,0:T(8,128)S(1)}, f32[64,256]{1,0:T(8,128)S(1)}, u32[]{:S(2)}, u32[]{:S(2)}) collective-permute-start(f32[64,256]{1,0:T(8,128)S(1)} %get-tuple-element.15), channel_id=1, source_target_pairs={{0,2},{2,0},{4,6},{6,4},{8,10},{10,8},{12,14},{14,12},{1,3},{3,1},... | collective-permute-start | bytes 196616 | tf_op jit(solution)/shard_map/ppermute | solution.py:166
  9.2 0.0 collective-permute-start.10
  9.2 3.6 %collective-permute-start.1 = (bf16[1,128,256]{2,1,0:T(8,128)(2,1)S(1)}, bf16[1,128,256]{2,1,0:T(8,128)(2,1)S(1)}, u32[]{:S(2)}, u32[]{:S(2)}) collective-permute-start(bf16[1,128,256]{2,1,0:T(8,128)(2,1)S(1)} %get-tuple-element.13.refs_0_), channel_id=1, source_target_pairs={{0,12},{2,14},{4,8},{6,10},{8,4},{10,6},{12,0},{14,2},{1,13},{3,15... | collective-permute-start | bytes 196616 | tf_op jit(solution)/shard_map/ppermute | solution.py:166
  12.8 0.0 collective-permute-done.7.refs_1_
  12.8 0.8 %collective-permute-start.8 = (f32[64,256]{1,0:T(8,128)S(1)}, f32[64,256]{1,0:T(8,128)S(1)}, u32[]{:S(2)}, u32[]{:S(2)}) collective-permute-start(f32[64,256]{1,0:T(8,128)S(1)} %plane_sum.1.refs_0_), channel_id=1, source_target_pairs={{0,4},{2,6},{4,0},{6,2},{8,12},{10,14},{12,8},{14,10},{1,5},{3,7},... | collective-permute-start | bytes 196616 | tf_op jit(solution)/shard_map/ppermute | solution.py:166
  13.6 2.0 %collective-permute-done.1.refs_1_ = bf16[1,128,256]{2,1,0:T(8,128)(2,1)S(1)} collective-permute-done((bf16[1,128,256]{2,1,0:T(8,128)(2,1)S(1)}, bf16[1,128,256]{2,1,0:T(8,128)(2,1)S(1)}, u32[]{:S(2)}, u32[]{:S(2)}) %collective-permute-start.1) | collective-permute-done | bytes 65568 | tf_op jit(solution)/shard_map/ppermute | solution.py:166
  15.7 1.1 %collective-permute-start.2 = (bf16[2,128,256]{2,1,0:T(8,128)(2,1)S(1)}, bf16[2,128,256]{2,1,0:T(8,128)(2,1)S(1)}, u32[]{:S(2)}, u32[]{:S(2)}) collective-permute-start(bf16[2,128,256]{2,1,0:T(8,128)(2,1)S(1)} %join_near.1.refs_0_), channel_id=1, source_target_pairs={{0,4},{2,6},{4,0},{6,2},{8,12},{10,14},{12,8},{14,10},{1,5},{3,7},... | collective-permute-start | bytes 393224 | tf_op jit(solution)/shard_map/ppermute | solution.py:166
  16.8 0.5 %collective-permute-start.3 = (bf16[2,128,256]{2,1,0:T(8,128)(2,1)S(1)}, bf16[2,128,256]{2,1,0:T(8,128)(2,1)S(1)}, u32[]{:S(2)}, u32[]{:S(2)}) collective-permute-start(bf16[2,128,256]{2,1,0:T(8,128)(2,1)S(1)} %join_near.1.refs_0_), channel_id=1, source_target_pairs={{0,2},{2,0},{4,6},{6,4},{8,10},{10,8},{12,14},{14,12},{1,3},{3,1},... | collective-permute-start | bytes 393224 | tf_op jit(solution)/shard_map/ppermute | solution.py:166
  17.3 0.0 collective-permute-done.8.refs_1_
  17.3 2.9 %collective-permute-start.9 = (f32[64,256]{1,0:T(8,128)S(1)}, f32[64,256]{1,0:T(8,128)S(1)}, u32[]{:S(2)}, u32[]{:S(2)}) collective-permute-start(f32[64,256]{1,0:T(8,128)S(1)} %pair_sum.1.refs_1_), channel_id=1, source_target_pairs={{0,12},{2,14},{4,8},{6,10},{8,4},{10,6},{12,0},{14,2},{1,13},{3,15... | collective-permute-start | bytes 196616 | tf_op jit(solution)/shard_map/ppermute | solution.py:166
  20.3 0.6 %collective-permute-done.2.refs_1_ = bf16[2,128,256]{2,1,0:T(8,128)(2,1)S(1)} collective-permute-done((bf16[2,128,256]{2,1,0:T(8,128)(2,1)S(1)}, bf16[2,128,256]{2,1,0:T(8,128)(2,1)S(1)}, u32[]{:S(2)}, u32[]{:S(2)}) %collective-permute-start.2) | collective-permute-done | bytes 131104 | tf_op jit(solution)/shard_map/ppermute | solution.py:166
  20.9 0.9 %collective-permute-start.4 = (bf16[2,128,256]{2,1,0:T(8,128)(2,1)S(1)}, bf16[2,128,256]{2,1,0:T(8,128)(2,1)S(1)}, u32[]{:S(2)}, u32[]{:S(2)}) collective-permute-start(bf16[2,128,256]{2,1,0:T(8,128)(2,1)S(1)} %collective-permute-done.2.refs_1_), channel_id=1, source_target_pairs={{0,2},{2,0},{4,6},{6,4},{8,10},{10,8},{12,14},{14,12},{1,3},{3,1},... | collective-permute-start | bytes 393224 | tf_op jit(solution)/shard_map/ppermute | solution.py:166
  21.8 0.1 collective-permute-start.5
  21.9 0.0 collective-permute-done.3.refs_0_
  21.9 4.0 %collective-permute-done.4.refs_1_ = bf16[2,128,256]{2,1,0:T(8,128)(2,1)S(1)} collective-permute-done((bf16[2,128,256]{2,1,0:T(8,128)(2,1)S(1)}, bf16[2,128,256]{2,1,0:T(8,128)(2,1)S(1)}, u32[]{:S(2)}, u32[]{:S(2)}) %collective-permute-start.4) | collective-permute-done | bytes 131104 | tf_op jit(solution)/shard_map/ppermute | solution.py:166
  25.9 0.1 collective-permute-start.6
  26.0 0.0 collective-permute-done.9.refs_2_
  26.0 0.0 collective-permute-done.5.refs_4_.refs_3_
  26.0 0.0 collective-permute-done.10.refs_3_.refs_10_
  26.0 0.9 %collective-permute-start.11 = (bf16[64,256]{1,0:T(8,128)(2,1)S(1)}, bf16[64,256]{1,0:T(8,128)(2,1)S(1)}, u32[]{:S(2)}, u32[]{:S(2)}) collective-permute-start(bf16[64,256]{1,0:T(8,128)(2,1)S(1)} %hub_sums.1.refs_5_), channel_id=1, source_target_pairs={{0,2},{2,0},{4,6},{6,4},{8,10},{10,8},{12,14},{14,12},{1,3},{3,1},... | collective-permute-start | bytes 98312 | tf_op jit(solution)/shard_map/ppermute | solution.py:166
  27.0 0.2 collective-permute-start.12
  27.2 1.1 %collective-permute-start.13 = (bf16[64,256]{1,0:T(8,128)(2,1)S(1)}, bf16[64,256]{1,0:T(8,128)(2,1)S(1)}, u32[]{:S(2)}, u32[]{:S(2)}) collective-permute-start(bf16[64,256]{1,0:T(8,128)(2,1)S(1)} %hub_sums.1.refs_5_), channel_id=1, source_target_pairs={{0,3},{1,2},{2,1},{3,0},{4,7},{5,6},{6,5},{7,4},{8,11},{9,10},{10,... | collective-permute-start | bytes 98312 | tf_op jit(solution)/shard_map/ppermute | solution.py:173
  28.2 0.0 collective-permute-done.6.refs_4_
  28.3 1.8 %collective-permute-done.11.refs_6_ = bf16[64,256]{1,0:T(8,128)(2,1)S(1)} collective-permute-done((bf16[64,256]{1,0:T(8,128)(2,1)S(1)}, bf16[64,256]{1,0:T(8,128)(2,1)S(1)}, u32[]{:S(2)}, u32[]{:S(2)}) %collective-permute-start.11) | collective-permute-done | bytes 32800 | tf_op jit(solution)/shard_map/ppermute | solution.py:166
  30.0 0.0 collective-permute-done.12.refs_7_
  30.0 0.5 %collective-permute-done.13.refs_8_ = bf16[64,256]{1,0:T(8,128)(2,1)S(1)} collective-permute-done((bf16[64,256]{1,0:T(8,128)(2,1)S(1)}, bf16[64,256]{1,0:T(8,128)(2,1)S(1)}, u32[]{:S(2)}, u32[]{:S(2)}) %collective-permute-start.13) | collective-permute-done | bytes 32800 | tf_op jit(solution)/shard_map/ppermute | solution.py:173
  30.5 1.6 %later_terms.1 = (f32[128,256]{1,0:T(8,128)}, f32[8,16,256]{2,1,0:T(8,128)S(1)}) custom-call(s32[1,256]{1,0:T(1,128)S(1)} %bitcast.10, bf16[4,128,256]{2,1,0:T(8,128)(2,1)S(1)} %join_line.1.refs_1_, bf16[4,128,256]{2,1,0:T(8,128)(2,1)S(1)} %join_across.1.refs_2_, bf16[4,128,256]{2,1,0:T(8,128)(2,1)S(1)} %collective-permute-done.5.refs_4_.refs_3_, ...), custom_call_target="tpu_custom_call" | custom-call | tf_op jit(solution)/shard_map/later_terms/pallas_call | solution.py:179
  32.1 13.5 %all_to_all.5.refs_1_ = f32[8,16,256]{2,1,0:T(8,128)S(1)} all-to-all(f32[8,16,256]{2,1,0:T(8,128)S(1)} %get-tuple-element.19), channel_id=1, replica_groups=mesh['groups'=2,'row'=8,'col'=2] {'row'}, dimensions={0} | all-to-all | bytes 262144 | tf_op jit(solution)/shard_map/all_to_all | solution.py:247
  45.6 0.6 %last_hubs.1 = f32[16,256]{1,0:T(8,128)} custom-call(s32[1,256]{1,0:T(1,128)S(1)} %bitcast.11, f32[8,16,256]{2,1,0:T(8,128)S(1)} %all_to_all.5.refs_1_), custom_call_target="tpu_custom_call" | custom-call | tf_op jit(solution)/shard_map/last_hubs/pallas_call | solution.py:179
  (7 shorter events, 0.1 us)
Async XLA Ops:
  1.3 5.0 %copy-start = (s32[256]{0:T(256)S(1)}, s32[256]{0:T(256)}, u32[]{:S(2)}) copy-start(s32[256]{0:T(256)} %param.9) | copy-start | bytes 3076
  4.6 1.7 %collective-permute-start = (f32[256,256]{1,0:T(8,128)S(1)}, f32[256,256]{1,0:T(8,128)S(1)}, u32[]{:S(2)}, u32[]{:S(2)}) collective-permute-start(f32[256,256]{1,0:T(8,128)S(1)} %get-tuple-element.12), channel_id=1, source_target_pairs={{0,1},{1,0},{2,3},{3,2},{4,5},{5,4},{6,7},{7,6},{8,9},{9,8},{10,11... | collective-permute-start | bytes 786440 | tf_op jit(solution)/shard_map/ppermute | solution.py:163
  6.3 6.5 %collective-permute-start.7 = (f32[64,256]{1,0:T(8,128)S(1)}, f32[64,256]{1,0:T(8,128)S(1)}, u32[]{:S(2)}, u32[]{:S(2)}) collective-permute-start(f32[64,256]{1,0:T(8,128)S(1)} %get-tuple-element.15), channel_id=1, source_target_pairs={{0,2},{2,0},{4,6},{6,4},{8,10},{10,8},{12,14},{14,12},{1,3},{3,1},... | collective-permute-start | bytes 196616 | tf_op jit(solution)/shard_map/ppermute | solution.py:166
  9.2 16.8 %collective-permute-start.10 = (bf16[512,1280]{1,0:T(8,128)(2,1)S(1)}, bf16[512,1280]{1,0:T(8,128)(2,1)S(1)}, u32[]{:S(2)}, u32[]{:S(2)}) collective-permute-start(bf16[512,1280]{1,0:T(8,128)(2,1)S(1)} %get-tuple-element.16), channel_id=1, source_target_pairs={{0,1},{1,0},{2,3},{3,2},{4,5},{5,4},{6,7},{7,6},{8,9},{9,8},{10,11... | collective-permute-start | bytes 3932168 | tf_op jit(solution)/shard_map/ppermute | solution.py:163
  9.2 6.5 %collective-permute-start.1 = (bf16[1,128,256]{2,1,0:T(8,128)(2,1)S(1)}, bf16[1,128,256]{2,1,0:T(8,128)(2,1)S(1)}, u32[]{:S(2)}, u32[]{:S(2)}) collective-permute-start(bf16[1,128,256]{2,1,0:T(8,128)(2,1)S(1)} %get-tuple-element.13.refs_0_), channel_id=1, source_target_pairs={{0,12},{2,14},{4,8},{6,10},{8,4},{10,6},{12,0},{14,2},{1,13},{3,15... | collective-permute-start | bytes 196616 | tf_op jit(solution)/shard_map/ppermute | solution.py:166
  12.8 4.5 %collective-permute-start.8 = (f32[64,256]{1,0:T(8,128)S(1)}, f32[64,256]{1,0:T(8,128)S(1)}, u32[]{:S(2)}, u32[]{:S(2)}) collective-permute-start(f32[64,256]{1,0:T(8,128)S(1)} %plane_sum.1.refs_0_), channel_id=1, source_target_pairs={{0,4},{2,6},{4,0},{6,2},{8,12},{10,14},{12,8},{14,10},{1,5},{3,7},... | collective-permute-start | bytes 196616 | tf_op jit(solution)/shard_map/ppermute | solution.py:166
  15.7 5.2 %collective-permute-start.2 = (bf16[2,128,256]{2,1,0:T(8,128)(2,1)S(1)}, bf16[2,128,256]{2,1,0:T(8,128)(2,1)S(1)}, u32[]{:S(2)}, u32[]{:S(2)}) collective-permute-start(bf16[2,128,256]{2,1,0:T(8,128)(2,1)S(1)} %join_near.1.refs_0_), channel_id=1, source_target_pairs={{0,4},{2,6},{4,0},{6,2},{8,12},{10,14},{12,8},{14,10},{1,5},{3,7},... | collective-permute-start | bytes 393224 | tf_op jit(solution)/shard_map/ppermute | solution.py:166
  16.8 5.1 %collective-permute-start.3 = (bf16[2,128,256]{2,1,0:T(8,128)(2,1)S(1)}, bf16[2,128,256]{2,1,0:T(8,128)(2,1)S(1)}, u32[]{:S(2)}, u32[]{:S(2)}) collective-permute-start(bf16[2,128,256]{2,1,0:T(8,128)(2,1)S(1)} %join_near.1.refs_0_), channel_id=1, source_target_pairs={{0,2},{2,0},{4,6},{6,4},{8,10},{10,8},{12,14},{14,12},{1,3},{3,1},... | collective-permute-start | bytes 393224 | tf_op jit(solution)/shard_map/ppermute | solution.py:166
  17.3 8.6 %collective-permute-start.9 = (f32[64,256]{1,0:T(8,128)S(1)}, f32[64,256]{1,0:T(8,128)S(1)}, u32[]{:S(2)}, u32[]{:S(2)}) collective-permute-start(f32[64,256]{1,0:T(8,128)S(1)} %pair_sum.1.refs_1_), channel_id=1, source_target_pairs={{0,12},{2,14},{4,8},{6,10},{8,4},{10,6},{12,0},{14,2},{1,13},{3,15... | collective-permute-start | bytes 196616 | tf_op jit(solution)/shard_map/ppermute | solution.py:166
  20.9 5.0 %collective-permute-start.4 = (bf16[2,128,256]{2,1,0:T(8,128)(2,1)S(1)}, bf16[2,128,256]{2,1,0:T(8,128)(2,1)S(1)}, u32[]{:S(2)}, u32[]{:S(2)}) collective-permute-start(bf16[2,128,256]{2,1,0:T(8,128)(2,1)S(1)} %collective-permute-done.2.refs_1_), channel_id=1, source_target_pairs={{0,2},{2,0},{4,6},{6,4},{8,10},{10,8},{12,14},{14,12},{1,3},{3,1},... | collective-permute-start | bytes 393224 | tf_op jit(solution)/shard_map/ppermute | solution.py:166
  21.8 4.2 %collective-permute-start.5 = (bf16[4,128,256]{2,1,0:T(8,128)(2,1)S(1)}, bf16[4,128,256]{2,1,0:T(8,128)(2,1)S(1)}, u32[]{:S(2)}, u32[]{:S(2)}) collective-permute-start(bf16[4,128,256]{2,1,0:T(8,128)(2,1)S(1)} %join_line.1.refs_1_), channel_id=1, source_target_pairs={{0,1},{1,0},{2,3},{3,2},{4,5},{5,4},{6,7},{7,6},{8,9},{9,8},{10,11... | collective-permute-start | bytes 786440 | tf_op jit(solution)/shard_map/ppermute | solution.py:163
  25.9 2.4 %collective-permute-start.6 = (bf16[4,128,256]{2,1,0:T(8,128)(2,1)S(1)}, bf16[4,128,256]{2,1,0:T(8,128)(2,1)S(1)}, u32[]{:S(2)}, u32[]{:S(2)}) collective-permute-start(bf16[4,128,256]{2,1,0:T(8,128)(2,1)S(1)} %join_across.1.refs_2_), channel_id=1, source_target_pairs={{0,1},{1,0},{2,3},{3,2},{4,5},{5,4},{6,7},{7,6},{8,9},{9,8},{10,11... | collective-permute-start | bytes 786440 | tf_op jit(solution)/shard_map/ppermute | solution.py:163
  26.0 4.0 %collective-permute-start.11 = (bf16[64,256]{1,0:T(8,128)(2,1)S(1)}, bf16[64,256]{1,0:T(8,128)(2,1)S(1)}, u32[]{:S(2)}, u32[]{:S(2)}) collective-permute-start(bf16[64,256]{1,0:T(8,128)(2,1)S(1)} %hub_sums.1.refs_5_), channel_id=1, source_target_pairs={{0,2},{2,0},{4,6},{6,4},{8,10},{10,8},{12,14},{14,12},{1,3},{3,1},... | collective-permute-start | bytes 98312 | tf_op jit(solution)/shard_map/ppermute | solution.py:166
  27.0 3.0 %collective-permute-start.12 = (bf16[64,256]{1,0:T(8,128)(2,1)S(1)}, bf16[64,256]{1,0:T(8,128)(2,1)S(1)}, u32[]{:S(2)}, u32[]{:S(2)}) collective-permute-start(bf16[64,256]{1,0:T(8,128)(2,1)S(1)} %hub_sums.1.refs_5_), channel_id=1, source_target_pairs={{0,1},{1,0},{2,3},{3,2},{4,5},{5,4},{6,7},{7,6},{8,9},{9,8},{10,11... | collective-permute-start | bytes 98312 | tf_op jit(solution)/shard_map/ppermute | solution.py:163
  27.2 3.3 %collective-permute-start.13 = (bf16[64,256]{1,0:T(8,128)(2,1)S(1)}, bf16[64,256]{1,0:T(8,128)(2,1)S(1)}, u32[]{:S(2)}, u32[]{:S(2)}) collective-permute-start(bf16[64,256]{1,0:T(8,128)(2,1)S(1)} %hub_sums.1.refs_5_), channel_id=1, source_target_pairs={{0,3},{1,2},{2,1},{3,0},{4,7},{5,6},{6,5},{7,4},{8,11},{9,10},{10,... | collective-permute-start | bytes 98312 | tf_op jit(solution)/shard_map/ppermute | solution.py:173

commit v19 on v17

--- a/solution.py
+++ b/solution.py
@@ -142,17 +142,14 @@
         parts_ref[k] = keep_ref[spot, :] + came_ref[spot, :]
 
 
-def last_scores_kernel(dims, src_ref, keep_ref, came_ref, scores_ref):
+def last_kernel(dims, src_ref, keep_ref, came_ref, parts_ref, scores_ref, hubs_ref):
     scores_ref[...] = own_scores(dims, src_ref, keep_ref, came_ref)
-
-
-def last_hubs_kernel(dims, src_ref, parts_ref, out_ref):
-    piece = out_ref.shape[0]
+    piece = hubs_ref.shape[0]
     summed = parts_ref[0]
     for k in range(1, parts_ref.shape[0]):
         summed = summed + parts_ref[k]
     first = (lax.axis_index("row") * dims[1] + lax.axis_index("col")) * piece
-    out_ref[...] = DAMP * summed + 0.15 * one_hot(first, piece, src_ref[...])
+    hubs_ref[...] = DAMP * summed + 0.15 * one_hot(first, piece, src_ref[...])
 
 
 def fast_body(tiles, tile_row, tile_col, tile_count, sources):
@@ -252,8 +249,8 @@
     came = other_core(send)
     parts = call(pieces_kernel, "hub_pieces", f32((n_row, piece, width)), keep, came)
     parts = lax.all_to_all(parts, "row", 0, 0)
-    scores = call(bind(last_scores_kernel, dims), "last_scores", f32((VB, width)), src, keep, came)
-    hubs = call(bind(last_hubs_kernel, dims), "last_hubs", f32((piece, width)), src, parts)
+    scores, hubs = call(bind(last_kernel, dims), "last_sums", (f32((VB, width)), f32((piece, width))),
+                        src, keep, came, parts)
     return scores.reshape(1, 1, VB, width), hubs
 
 

time: 45.3 us -> 44.4 us (0.980)
  blocking collectives: 0 us -> 12 us
  waiting for transfers between devices: 16.7 us -> 10.1 us
  starting transfers between devices: 20.4 us -> 15.6 us
  Pallas kernels: 6.47 us -> 5.21 us
    all_to_all x0 -> x1, blocking collectives: none -> 12 us  [fast_body(): parts = lax.all_to_all(parts, 'row', 0, 0)]
    all_to_all x1 -> x0, waiting for transfers between devices: 6.65 us -> none  [fast_body(): parts = lax.all_to_all(parts, 'row', 0, 0)]
    all_to_all x1 -> x0, starting transfers between devices: 4.88 us -> none  [fast_body(): parts = lax.all_to_all(parts, 'row', 0, 0)]
    pallas_call x9 -> x8, Pallas kernels: 3.07 us -> 1.81 us  [call(): pl.pallas_call(kernel, out_shape=out_shape, in_specs=[VMEM] * len(args),...]
  transfers between devices with their start and end apart: 13 -> 12, of which waited for: 8 -> 7; matrix products, arithmetic and copies ran while one was open for 0% -> 0% of each run, Pallas kernels for 2% -> 0%
where the time goes in v19:
time: 44.4 us; the launch traced here: 44.2 us
  starting transfers between devices  15.6 us (35%)
  blocking collectives  12 us (27%)
  waiting for transfers between devices  10.1 us (23%)
  Pallas kernels  5.21 us (12%)
  between operations  1.36 us (3%)
    ppermute x8, starting transfers between devices, to_partner(): return lax.ppermute(x, 'row', [(r, r ^ flip) for r in range(n_row)])  13.9 us
    all_to_all x1, blocking collectives, fast_body(): parts = lax.all_to_all(parts, 'row', 0, 0)  12 us
    ppermute x8, waiting for transfers between devices, to_partner(): return lax.ppermute(x, 'row', [(r, r ^ flip) for r in range(n_row)])  5.82 us
    pallas_call x1, Pallas kernels, fast_body(): pl.pallas_call(bind(first_kernel, dims), out_shape=(f32((half, width)), f...  3.4 us
    ppermute x3, waiting for transfers between devices, other_core(): return lax.ppermute(x, 'col', [(0, 1), (1, 0)])  2.69 us
    pallas_call x8, Pallas kernels, call(): pl.pallas_call(kernel, out_shape=out_shape, in_specs=[VMEM] * len(args),...  1.81 us
    ppermute x3, starting transfers between devices, other_core(): return lax.ppermute(x, 'col', [(0, 1), (1, 0)])  1.58 us
    ppermute x1, waiting for transfers between devices, other_both(): lax.ppermute(x, ('row', 'col'), [(r * n_col + c, (r ^ 1) * n_col + 1 - c)...  1.55 us
  transfers between devices with their start and end apart: 12, of which 7 were waited for; matrix products, arithmetic and copies ran while one was open for 0% of the time, Pallas kernels for 0%

profile of v19, /device:TPU:0, one launch (start us, length us, event | category | flops | bytes accessed | tf_op | source)
XLA Modules:
  0.0 44.2 jit_solution(5096740377398148453)
XLA Ops:
  0.6 0.0 copy-start
  1.3 3.4 %first_terms.1 = (f32[256,256]{1,0:T(8,128)S(1)}, f32[256,256]{1,0:T(8,128)S(1)}, bf16[1024,1280]{1,0:T(8,128)(2,1)S(1)}) custom-call(bf16[96,128,128]{2,1,0:T(8,128)(2,1)} %bitcast.11, s32[96]{0:T(128)} %bitcast.12, s32[96]{0:T(128)} %bitcast.13, s32[1]{0:T(128)} %bitcast.6.count_hbm, s32[1,256]{1,0:T(1,128)} %bitcast.7), custom_call_target="tpu_custom_call" | custom-call | tf_op jit(solution)/shard_map/first_terms/pallas_call | solution.py:203
  4.7 0.5 %collective-permute-start = (f32[256,256]{1,0:T(8,128)S(1)}, f32[256,256]{1,0:T(8,128)S(1)}, u32[]{:S(2)}, u32[]{:S(2)}) collective-permute-start(f32[256,256]{1,0:T(8,128)S(1)} %get-tuple-element.13), channel_id=1, source_target_pairs={{0,1},{1,0},{2,3},{3,2},{4,5},{5,4},{6,7},{7,6},{8,9},{9,8},{10,11... | collective-permute-start | bytes 786440 | tf_op jit(solution)/shard_map/ppermute | solution.py:175
  5.2 1.2 %collective-permute-done.came_ref = f32[256,256]{1,0:T(8,128)S(1)} collective-permute-done((f32[256,256]{1,0:T(8,128)S(1)}, f32[256,256]{1,0:T(8,128)S(1)}, u32[]{:S(2)}, u32[]{:S(2)}) %collective-permute-start) | collective-permute-done | bytes 262176 | tf_op jit(solution)/shard_map/ppermute | solution.py:175
  6.4 0.0 copy-done
  6.4 2.9 %collective-permute-start.5 = (f32[64,256]{1,0:T(8,128)S(1)}, f32[64,256]{1,0:T(8,128)S(1)}, u32[]{:S(2)}, u32[]{:S(2)}) collective-permute-start(f32[64,256]{1,0:T(8,128)S(1)} %get-tuple-element.16), channel_id=1, source_target_pairs={{0,2},{2,0},{4,6},{6,4},{8,10},{10,8},{12,14},{14,12},{1,3},{3,1},... | collective-permute-start | bytes 196616 | tf_op jit(solution)/shard_map/ppermute | solution.py:178
  9.4 3.6 %collective-permute-start.1 = (bf16[1,128,256]{2,1,0:T(8,128)(2,1)S(1)}, bf16[1,128,256]{2,1,0:T(8,128)(2,1)S(1)}, u32[]{:S(2)}, u32[]{:S(2)}) collective-permute-start(bf16[1,128,256]{2,1,0:T(8,128)(2,1)S(1)} %get-tuple-element.14.held_ref), channel_id=1, source_target_pairs={{0,12},{2,14},{4,8},{6,10},{8,4},{10,6},{12,0},{14,2},{1,13},{3,15... | collective-permute-start | bytes 196616 | tf_op jit(solution)/shard_map/ppermute | solution.py:178
  13.0 0.0 collective-permute-done.5.came_ref
  13.0 0.8 %collective-permute-start.6 = (f32[64,256]{1,0:T(8,128)S(1)}, f32[64,256]{1,0:T(8,128)S(1)}, u32[]{:S(2)}, u32[]{:S(2)}) collective-permute-start(f32[64,256]{1,0:T(8,128)S(1)} %plane_sum.1.hold_ref), channel_id=1, source_target_pairs={{0,4},{2,6},{4,0},{6,2},{8,12},{10,14},{12,8},{14,10},{1,5},{3,7},... | collective-permute-start | bytes 196616 | tf_op jit(solution)/shard_map/ppermute | solution.py:178
  13.8 1.8 %collective-permute-done.1.came_ref = bf16[1,128,256]{2,1,0:T(8,128)(2,1)S(1)} collective-permute-done((bf16[1,128,256]{2,1,0:T(8,128)(2,1)S(1)}, bf16[1,128,256]{2,1,0:T(8,128)(2,1)S(1)}, u32[]{:S(2)}, u32[]{:S(2)}) %collective-permute-start.1) | collective-permute-done | bytes 65568 | tf_op jit(solution)/shard_map/ppermute | solution.py:178
  15.6 0.8 %collective-permute-start.2 = (bf16[2,128,256]{2,1,0:T(8,128)(2,1)S(1)}, bf16[2,128,256]{2,1,0:T(8,128)(2,1)S(1)}, u32[]{:S(2)}, u32[]{:S(2)}) collective-permute-start(bf16[2,128,256]{2,1,0:T(8,128)(2,1)S(1)} %join_near.1.refs_0_), channel_id=1, source_target_pairs={{0,4},{2,6},{4,0},{6,2},{8,12},{10,14},{12,8},{14,10},{1,5},{3,7},... | collective-permute-start | bytes 393224 | tf_op jit(solution)/shard_map/ppermute | solution.py:178
  16.4 1.3 %collective-permute-done.6.came_ref = f32[64,256]{1,0:T(8,128)S(1)} collective-permute-done((f32[64,256]{1,0:T(8,128)S(1)}, f32[64,256]{1,0:T(8,128)S(1)}, u32[]{:S(2)}, u32[]{:S(2)}) %collective-permute-start.6) | collective-permute-done | bytes 65568 | tf_op jit(solution)/shard_map/ppermute | solution.py:178
  17.7 2.6 %collective-permute-start.7 = (f32[64,256]{1,0:T(8,128)S(1)}, f32[64,256]{1,0:T(8,128)S(1)}, u32[]{:S(2)}, u32[]{:S(2)}) collective-permute-start(f32[64,256]{1,0:T(8,128)S(1)} %pair_sum.1.held_ref), channel_id=1, source_target_pairs={{0,12},{2,14},{4,8},{6,10},{8,4},{10,6},{12,0},{14,2},{1,13},{3,15... | collective-permute-start | bytes 196616 | tf_op jit(solution)/shard_map/ppermute | solution.py:178
  20.3 2.0 %collective-permute-start.3 = (bf16[2,128,256]{2,1,0:T(8,128)(2,1)S(1)}, bf16[2,128,256]{2,1,0:T(8,128)(2,1)S(1)}, u32[]{:S(2)}, u32[]{:S(2)}) collective-permute-start(bf16[2,128,256]{2,1,0:T(8,128)(2,1)S(1)} %join_near.1.refs_0_), channel_id=1, source_target_pairs={{0,2},{2,0},{4,6},{6,4},{8,10},{10,8},{12,14},{14,12},{1,3},{3,1},... | collective-permute-start | bytes 393224 | tf_op jit(solution)/shard_map/ppermute | solution.py:178
  22.3 0.0 collective-permute-done.2.refs_1_
  22.3 0.1 collective-permute-start.4
  22.4 1.5 %collective-permute-done.7.came_ref = f32[64,256]{1,0:T(8,128)S(1)} collective-permute-done((f32[64,256]{1,0:T(8,128)S(1)}, f32[64,256]{1,0:T(8,128)S(1)}, u32[]{:S(2)}, u32[]{:S(2)}) %collective-permute-start.7) | collective-permute-done | bytes 65568 | tf_op jit(solution)/shard_map/ppermute | solution.py:178
  23.9 0.1 collective-permute-start.10
  24.0 1.0 %collective-permute-start.9 = (bf16[64,256]{1,0:T(8,128)(2,1)S(1)}, bf16[64,256]{1,0:T(8,128)(2,1)S(1)}, u32[]{:S(2)}, u32[]{:S(2)}) collective-permute-start(bf16[64,256]{1,0:T(8,128)(2,1)S(1)} %hub_sums.1.refs_4_), channel_id=1, source_target_pairs={{0,1},{1,0},{2,3},{3,2},{4,5},{5,4},{6,7},{7,6},{8,9},{9,8},{10,11... | collective-permute-start | bytes 98312 | tf_op jit(solution)/shard_map/ppermute | solution.py:175
  25.0 1.1 %collective-permute-start.8 = (bf16[64,256]{1,0:T(8,128)(2,1)S(1)}, bf16[64,256]{1,0:T(8,128)(2,1)S(1)}, u32[]{:S(2)}, u32[]{:S(2)}) collective-permute-start(bf16[64,256]{1,0:T(8,128)(2,1)S(1)} %hub_sums.1.refs_4_), channel_id=1, source_target_pairs={{0,2},{2,0},{4,6},{6,4},{8,10},{10,8},{12,14},{14,12},{1,3},{3,1},... | collective-permute-start | bytes 98312 | tf_op jit(solution)/shard_map/ppermute | solution.py:178
  26.1 0.0 collective-permute-done.3.refs_2_
  26.1 1.6 %collective-permute-done.10.refs_7_ = bf16[64,256]{1,0:T(8,128)(2,1)S(1)} collective-permute-done((bf16[64,256]{1,0:T(8,128)(2,1)S(1)}, bf16[64,256]{1,0:T(8,128)(2,1)S(1)}, u32[]{:S(2)}, u32[]{:S(2)}) %collective-permute-start.10) | collective-permute-done | bytes 32800 | tf_op jit(solution)/shard_map/ppermute | solution.py:185
  27.7 0.0 collective-permute-done.9.refs_6_
  27.7 1.2 %collective-permute-done.8.refs_5_ = bf16[64,256]{1,0:T(8,128)(2,1)S(1)} collective-permute-done((bf16[64,256]{1,0:T(8,128)(2,1)S(1)}, bf16[64,256]{1,0:T(8,128)(2,1)S(1)}, u32[]{:S(2)}, u32[]{:S(2)}) %collective-permute-start.8) | collective-permute-done | bytes 32800 | tf_op jit(solution)/shard_map/ppermute | solution.py:178
  28.9 0.0 collective-permute-done.4.refs_3_
  28.9 1.0 %later_terms.1 = (f32[256,256]{1,0:T(8,128)S(1)}, f32[256,256]{1,0:T(8,128)S(1)}) custom-call(bf16[2,128,256]{2,1,0:T(8,128)(2,1)S(1)} %join_near.1.refs_0_, bf16[2,128,256]{2,1,0:T(8,128)(2,1)S(1)} %collective-permute-done.2.refs_1_, bf16[2,128,256]{2,1,0:T(8,128)(2,1)S(1)} %collective-permute-done.3.refs_2_, ...), custom_call_target="tpu_custom_call" | custom-call | tf_op jit(solution)/shard_map/later_terms/pallas_call | solution.py:188
  29.9 0.1 collective-permute-start.11
  30.0 1.5 %collective-permute-done.11.came_ref = f32[256,256]{1,0:T(8,128)S(1)} collective-permute-done((f32[256,256]{1,0:T(8,128)S(1)}, f32[256,256]{1,0:T(8,128)S(1)}, u32[]{:S(2)}, u32[]{:S(2)}) %collective-permute-start.11) | collective-permute-done | bytes 262176 | tf_op jit(solution)/shard_map/ppermute | solution.py:175
  31.5 12.0 %all_to_all.5.parts_ref = f32[8,16,256]{2,1,0:T(8,128)S(1)} all-to-all(f32[8,16,256]{2,1,0:T(8,128)S(1)} %hub_pieces.1), channel_id=1, replica_groups=mesh['groups'=2,'row'=8,'col'=2] {'row'}, dimensions={0} | all-to-all | bytes 262144 | tf_op jit(solution)/shard_map/all_to_all | solution.py:251
  43.5 0.7 %last_sums.1 = (f32[128,256]{1,0:T(8,128)}, f32[16,256]{1,0:T(8,128)}) custom-call(s32[1,256]{1,0:T(1,128)S(1)} %bitcast.10, f32[256,256]{1,0:T(8,128)S(1)} %get-tuple-element.18.keep_ref, f32[256,256]{1,0:T(8,128)S(1)} %collective-permute-done.11.came_ref, f32[8,16,256]{2,1,0:T(8,128)S(1)} %all_to_all.5.parts_ref), custom_call_target="tpu_custom_call" | custom-call | tf_op jit(solution)/shard_map/last_sums/pallas_call | solution.py:188
  (6 shorter events, 0.1 us)
Async XLA Ops:
  0.6 5.8 %copy-start = (s32[256]{0:T(256)S(1)}, s32[256]{0:T(256)}, u32[]{:S(2)}) copy-start(s32[256]{0:T(256)} %param.9) | copy-start | bytes 3076
  4.7 1.7 %collective-permute-start = (f32[256,256]{1,0:T(8,128)S(1)}, f32[256,256]{1,0:T(8,128)S(1)}, u32[]{:S(2)}, u32[]{:S(2)}) collective-permute-start(f32[256,256]{1,0:T(8,128)S(1)} %get-tuple-element.13), channel_id=1, source_target_pairs={{0,1},{1,0},{2,3},{3,2},{4,5},{5,4},{6,7},{7,6},{8,9},{9,8},{10,11... | collective-permute-start | bytes 786440 | tf_op jit(solution)/shard_map/ppermute | solution.py:175
  6.4 6.5 %collective-permute-start.5 = (f32[64,256]{1,0:T(8,128)S(1)}, f32[64,256]{1,0:T(8,128)S(1)}, u32[]{:S(2)}, u32[]{:S(2)}) collective-permute-start(f32[64,256]{1,0:T(8,128)S(1)} %get-tuple-element.16), channel_id=1, source_target_pairs={{0,2},{2,0},{4,6},{6,4},{8,10},{10,8},{12,14},{14,12},{1,3},{3,1},... | collective-permute-start | bytes 196616 | tf_op jit(solution)/shard_map/ppermute | solution.py:178
  9.4 6.2 %collective-permute-start.1 = (bf16[1,128,256]{2,1,0:T(8,128)(2,1)S(1)}, bf16[1,128,256]{2,1,0:T(8,128)(2,1)S(1)}, u32[]{:S(2)}, u32[]{:S(2)}) collective-permute-start(bf16[1,128,256]{2,1,0:T(8,128)(2,1)S(1)} %get-tuple-element.14.held_ref), channel_id=1, source_target_pairs={{0,12},{2,14},{4,8},{6,10},{8,4},{10,6},{12,0},{14,2},{1,13},{3,15... | collective-permute-start | bytes 196616 | tf_op jit(solution)/shard_map/ppermute | solution.py:178
  13.0 4.7 %collective-permute-start.6 = (f32[64,256]{1,0:T(8,128)S(1)}, f32[64,256]{1,0:T(8,128)S(1)}, u32[]{:S(2)}, u32[]{:S(2)}) collective-permute-start(f32[64,256]{1,0:T(8,128)S(1)} %plane_sum.1.hold_ref), channel_id=1, source_target_pairs={{0,4},{2,6},{4,0},{6,2},{8,12},{10,14},{12,8},{14,10},{1,5},{3,7},... | collective-permute-start | bytes 196616 | tf_op jit(solution)/shard_map/ppermute | solution.py:178
  15.6 6.7 %collective-permute-start.2 = (bf16[2,128,256]{2,1,0:T(8,128)(2,1)S(1)}, bf16[2,128,256]{2,1,0:T(8,128)(2,1)S(1)}, u32[]{:S(2)}, u32[]{:S(2)}) collective-permute-start(bf16[2,128,256]{2,1,0:T(8,128)(2,1)S(1)} %join_near.1.refs_0_), channel_id=1, source_target_pairs={{0,4},{2,6},{4,0},{6,2},{8,12},{10,14},{12,8},{14,10},{1,5},{3,7},... | collective-permute-start | bytes 393224 | tf_op jit(solution)/shard_map/ppermute | solution.py:178
  17.7 6.1 %collective-permute-start.7 = (f32[64,256]{1,0:T(8,128)S(1)}, f32[64,256]{1,0:T(8,128)S(1)}, u32[]{:S(2)}, u32[]{:S(2)}) collective-permute-start(f32[64,256]{1,0:T(8,128)S(1)} %pair_sum.1.held_ref), channel_id=1, source_target_pairs={{0,12},{2,14},{4,8},{6,10},{8,4},{10,6},{12,0},{14,2},{1,13},{3,15... | collective-permute-start | bytes 196616 | tf_op jit(solution)/shard_map/ppermute | solution.py:178
  20.3 5.8 %collective-permute-start.3 = (bf16[2,128,256]{2,1,0:T(8,128)(2,1)S(1)}, bf16[2,128,256]{2,1,0:T(8,128)(2,1)S(1)}, u32[]{:S(2)}, u32[]{:S(2)}) collective-permute-start(bf16[2,128,256]{2,1,0:T(8,128)(2,1)S(1)} %join_near.1.refs_0_), channel_id=1, source_target_pairs={{0,2},{2,0},{4,6},{6,4},{8,10},{10,8},{12,14},{14,12},{1,3},{3,1},... | collective-permute-start | bytes 393224 | tf_op jit(solution)/shard_map/ppermute | solution.py:178
  22.3 6.6 %collective-permute-start.4 = (bf16[2,128,256]{2,1,0:T(8,128)(2,1)S(1)}, bf16[2,128,256]{2,1,0:T(8,128)(2,1)S(1)}, u32[]{:S(2)}, u32[]{:S(2)}) collective-permute-start(bf16[2,128,256]{2,1,0:T(8,128)(2,1)S(1)} %collective-permute-done.2.refs_1_), channel_id=1, source_target_pairs={{0,2},{2,0},{4,6},{6,4},{8,10},{10,8},{12,14},{14,12},{1,3},{3,1},... | collective-permute-start | bytes 393224 | tf_op jit(solution)/shard_map/ppermute | solution.py:178
  23.9 3.8 %collective-permute-start.10 = (bf16[64,256]{1,0:T(8,128)(2,1)S(1)}, bf16[64,256]{1,0:T(8,128)(2,1)S(1)}, u32[]{:S(2)}, u32[]{:S(2)}) collective-permute-start(bf16[64,256]{1,0:T(8,128)(2,1)S(1)} %hub_sums.1.refs_4_), channel_id=1, source_target_pairs={{0,3},{1,2},{2,1},{3,0},{4,7},{5,6},{6,5},{7,4},{8,11},{9,10},{10,... | collective-permute-start | bytes 98312 | tf_op jit(solution)/shard_map/ppermute | solution.py:185
  24.0 3.7 %collective-permute-start.9 = (bf16[64,256]{1,0:T(8,128)(2,1)S(1)}, bf16[64,256]{1,0:T(8,128)(2,1)S(1)}, u32[]{:S(2)}, u32[]{:S(2)}) collective-permute-start(bf16[64,256]{1,0:T(8,128)(2,1)S(1)} %hub_sums.1.refs_4_), channel_id=1, source_target_pairs={{0,1},{1,0},{2,3},{3,2},{4,5},{5,4},{6,7},{7,6},{8,9},{9,8},{10,11... | collective-permute-start | bytes 98312 | tf_op jit(solution)/shard_map/ppermute | solution.py:175
  25.0 3.9 %collective-permute-start.8 = (bf16[64,256]{1,0:T(8,128)(2,1)S(1)}, bf16[64,256]{1,0:T(8,128)(2,1)S(1)}, u32[]{:S(2)}, u32[]{:S(2)}) collective-permute-start(bf16[64,256]{1,0:T(8,128)(2,1)S(1)} %hub_sums.1.refs_4_), channel_id=1, source_target_pairs={{0,2},{2,0},{4,6},{6,4},{8,10},{10,8},{12,14},{14,12},{1,3},{3,1},... | collective-permute-start | bytes 98312 | tf_op jit(solution)/shard_map/ppermute | solution.py:178
  29.9 1.6 %collective-permute-start.11 = (f32[256,256]{1,0:T(8,128)S(1)}, f32[256,256]{1,0:T(8,128)S(1)}, u32[]{:S(2)}, u32[]{:S(2)}) collective-permute-start(f32[256,256]{1,0:T(8,128)S(1)} %get-tuple-element.19), channel_id=1, source_target_pairs={{0,1},{1,0},{2,3},{3,2},{4,5},{5,4},{6,7},{7,6},{8,9},{9,8},{10,11... | collective-permute-start | bytes 786440 | tf_op jit(solution)/shard_map/ppermute | solution.py:175

commit v20 on v19

--- a/solution.py
+++ b/solution.py
@@ -1,4 +1,5 @@
 import functools
+import math
 
 import jax
 import jax.numpy as jnp
@@ -11,7 +12,8 @@
 H = 256
 ITERS = 2
 DAMP = 0.85
-CHUNK = 16
+CHUNK = 8
+AHEAD = 4
 X = 2
 MICRO = 10 ** 9
 VMEM_LIMIT = 32 * 1024 * 1024
@@ -30,17 +32,20 @@
     return (ids == src).astype(jnp.float32)
 
 
-def write_terms(dims, block, prod_ref, dense_ref, panel_ref, send_ref, keep_ref):
+def write_terms(dims, block, prod_ref, send_ref, keep_ref):
     n_row, n_col, side = dims
-    rows = dense_ref.shape[0] // 2
     c = lax.axis_index("col")
-    prod = jnp.dot(dense_ref[...], panel_ref[...], preferred_element_type=jnp.float32)
-    prod_ref[...] = prod[:rows] + prod[rows:]
     for ref, col in ((keep_ref, c), (send_ref, 1 - c)):
         ref[:VB] = prod_ref[pl.ds(pl.multiple_of(col * VB, VB), VB), :]
         for k in range(H // n_col // block):
             start = n_col * VB + (k * n_col + col) * block
             ref[VB + k * block:VB + (k + 1) * block] = prod_ref[pl.ds(pl.multiple_of(start, block), block), :]
+
+
+def product(dense, panel):
+    prod = jnp.dot(dense, panel, preferred_element_type=jnp.float32)
+    rows = prod.shape[0] // 2
+    return prod[:rows] + prod[rows:]
 
 
 def first_kernel(dims, tiles_ref, rows_hbm, cols_hbm, count_hbm, src_hbm, send_ref, keep_ref, dense_ref,
@@ -53,7 +58,7 @@
     for i in range(held.shape[0] // CHUNK):
         part = pl.ds(i * CHUNK, CHUNK)
         copies.append(pltpu.make_async_copy(tiles_ref.at[part], held.at[part], sems.at[i]))
-    for copy in scalars + copies:
+    for copy in scalars + copies[:AHEAD]:
         copy.start()
     total[...] = jnp.zeros_like(total)
     for copy in scalars:
@@ -75,32 +80,41 @@
 
     for i, copy in enumerate(copies):
         copy.wait()
+        if i + AHEAD < len(copies):
+            copies[i + AHEAD].start()
         lax.fori_loop(i * CHUNK, (i + 1) * CHUNK, add_tile, 0, unroll=4)
     for r in range(0, n_rows, side):
         whole = total[pl.ds(r, side), :]
         high = whole.astype(jnp.bfloat16)
         dense_ref[pl.ds(r, side), :] = high
         dense_ref[pl.ds(n_rows + r, side), :] = (whole - high.astype(jnp.float32)).astype(jnp.bfloat16)
-    write_terms(dims, H // n_col, prod, dense_ref, panel, send_ref, keep_ref)
-
-
-def second_kernel(dims, flips, *refs):
+    prod[...] = product(dense_ref[...], panel[...])
+    write_terms(dims, H // n_col, prod, send_ref, keep_ref)
+
+
+def score_columns_kernel(dims, flips, *refs):
     n_row, n_col, side = dims
     n_z = n_row // X
-    blocks, quarters = refs[:4], refs[4:4 + X * n_col]
-    dense_ref, send_ref, keep_ref, panel, prod = refs[4 + X * n_col:]
-    half = H // n_col
-    r, c = lax.axis_index("row"), lax.axis_index("col")
+    blocks, (dense_ref, prod_ref, panel) = refs[:4], refs[4:]
+    r = lax.axis_index("row")
     near, far = flips[:n_z // 2], flips[n_z // 2:]
     for ref, group, x in ((blocks[0], near, 0), (blocks[1], far, 0), (blocks[2], near, 1), (blocks[3], far, 1)):
         for k, flip in enumerate(group):
             owner = r ^ (X * flip + x)
             panel[pl.ds(pl.multiple_of(owner * VB, VB), VB), :] = ref[k]
+    prod_ref[...] = product(dense_ref[:, :n_row * VB], panel[...])
+
+
+def hub_columns_kernel(dims, *refs):
+    n_row, n_col, side = dims
+    quarters, (dense_ref, prod_ref, send_ref, keep_ref, panel, total) = refs[:X * n_col], refs[X * n_col:]
+    r, c = lax.axis_index("row"), lax.axis_index("col")
     quarter = quarters[0].shape[0]
     for k, ref in enumerate(quarters):
-        place = n_row * VB + ((c ^ (k // X)) * X + (r % X ^ (k % X))) * quarter
+        place = ((c ^ (k // X)) * X + (r % X ^ (k % X))) * quarter
         panel[pl.ds(pl.multiple_of(place, quarter), quarter), :] = ref[...]
-    write_terms(dims, half // n_row, prod, dense_ref, panel, send_ref, keep_ref)
+    total[...] = prod_ref[...] + product(dense_ref[:, n_row * VB:], panel[...])
+    write_terms(dims, H // (n_row * n_col), total, send_ref, keep_ref)
 
 
 def own_scores(dims, src_ref, keep_ref, came_ref):
@@ -166,11 +180,6 @@
     src = sources.reshape(1, width)
     half = VB + n_row * piece
     quarter = H // n_col // X
-    product_scratch = [
-        pltpu.VMEM((n_cols, width), jnp.bfloat16),
-        pltpu.VMEM((n_rows, width), jnp.float32),
-    ]
-
     def other_core(x):
         return lax.ppermute(x, "col", [(0, 1), (1, 0)])
 
@@ -212,7 +221,8 @@
             pltpu.SMEM((1,), jnp.int32),
             pltpu.VMEM((1, width), jnp.int32),
             pltpu.VMEM((n_rows + side, n_cols), jnp.float32),
-        ] + product_scratch + [
+            pltpu.VMEM((n_cols, width), jnp.bfloat16),
+            pltpu.VMEM((n_rows, width), jnp.float32),
             pltpu.SemaphoreType.DMA((slots // CHUNK,)),
             pltpu.SemaphoreType.DMA((4,)),
         ],
@@ -243,9 +253,13 @@
             sums = call(add_kernel, "pair_sum", f32((quarter, width)), sums, to_partner(sums, X * mask), cost=1)
         mine = call(bind(hub_kernel, dims), "hub_sums", bf16((quarter, width)), src, sums, to_partner(sums, X * masks[0]), cost=1)
         quarters = [mine, other_side(mine), other_core(mine), other_both(mine)]
+        prod = call(
+            bind(score_columns_kernel, dims, flips), "score_columns", f32((n_rows, width)),
+            held, far, near_across, far_across, dense, scratch=[pltpu.VMEM((n_row * VB, width), jnp.bfloat16)])
         send, keep = call(
-            bind(second_kernel, dims, flips), "later_terms", (f32((half, width)), f32((half, width))),
-            held, far, near_across, far_across, *quarters, dense, scratch=product_scratch)
+            bind(hub_columns_kernel, dims), "hub_columns", (f32((half, width)), f32((half, width))),
+            *quarters, dense, prod,
+            scratch=[pltpu.VMEM((H, width), jnp.bfloat16), pltpu.VMEM((n_rows, width), jnp.float32)])
     came = other_core(send)
     parts = call(pieces_kernel, "hub_pieces", f32((n_row, piece, width)), keep, came)
     parts = lax.all_to_all(parts, "row", 0, 0)
@@ -284,7 +298,7 @@
     ).reshape(n_row * VB)
     column_panel = (column_ids[:, None] == sources[None, :]).astype(jnp.bfloat16)
     hub_panel = tele_hubs.astype(jnp.bfloat16)
-    block = CHUNK
+    block = math.gcd(slots, 16)
     own_scores = tele_own
     hub_piece = tele_piece
     for step in range(ITERS):

time: 44.4 us -> 44.9 us (1.011)
  Pallas kernels: 5.21 us -> 6.37 us
  waiting for transfers between devices: 10.1 us -> 9.29 us
    ppermute x1, waiting for transfers between devices: 1.55 us -> 0.01 us  [other_both(): lax.ppermute(x, ('row', 'col'), [(r * n_col + c, (r ^ 1) * n_col + 1 - c)...]
    pallas_call x1, Pallas kernels: 3.4 us -> 4.39 us  [fast_body(): pl.pallas_call(bind(first_kernel, dims), out_shape=(f32((half, width)), f...]
    ppermute x8, waiting for transfers between devices: 5.82 us -> 6.6 us  [to_partner(): return lax.ppermute(x, 'row', [(r, r ^ flip) for r in range(n_row)])]
    pallas_call x8 -> x9, Pallas kernels: 1.81 us -> 1.97 us  [call(): pl.pallas_call(kernel, out_shape=out_shape, in_specs=[VMEM] * len(args),...]
  transfers between devices with their start and end apart: 12 -> 12, of which waited for: 7 -> 7; matrix products, arithmetic and copies ran while one was open for 0% -> 0% of each run, Pallas kernels for 0% -> 2%
where the time goes in v20:
time: 44.9 us; the launch traced here: 44.6 us
  starting transfers between devices  15.6 us (35%)
  blocking collectives  12 us (27%)
  waiting for transfers between devices  9.29 us (21%)
  Pallas kernels  6.37 us (14%)
  between operations  1.38 us (3%)
    ppermute x8, starting transfers between devices, to_partner(): return lax.ppermute(x, 'row', [(r, r ^ flip) for r in range(n_row)])  13.9 us
    all_to_all x1, blocking collectives, fast_body(): parts = lax.all_to_all(parts, 'row', 0, 0)  12 us
    ppermute x8, waiting for transfers between devices, to_partner(): return lax.ppermute(x, 'row', [(r, r ^ flip) for r in range(n_row)])  6.6 us
    pallas_call x1, Pallas kernels, fast_body(): pl.pallas_call(bind(first_kernel, dims), out_shape=(f32((half, width)), f...  4.39 us
    ppermute x3, waiting for transfers between devices, other_core(): return lax.ppermute(x, 'col', [(0, 1), (1, 0)])  2.69 us
    pallas_call x9, Pallas kernels, call(): pl.pallas_call(kernel, out_shape=out_shape, in_specs=[VMEM] * len(args),...  1.97 us
    ppermute x3, starting transfers between devices, other_core(): return lax.ppermute(x, 'col', [(0, 1), (1, 0)])  1.59 us
  transfers between devices with their start and end apart: 12, of which 7 were waited for; matrix products, arithmetic and copies ran while one was open for 0% of the time, Pallas kernels for 2%

profile of v20, /device:TPU:0, one launch (start us, length us, event | category | flops | bytes accessed | tf_op | source)
XLA Modules:
  0.0 44.6 jit_solution(13460339101010928145)
XLA Ops:
  0.6 0.0 copy-start
  1.3 4.4 %first_terms.1 = (f32[256,256]{1,0:T(8,128)S(1)}, f32[256,256]{1,0:T(8,128)S(1)}, bf16[1024,1280]{1,0:T(8,128)(2,1)S(1)}) custom-call(bf16[96,128,128]{2,1,0:T(8,128)(2,1)} %bitcast.11, s32[96]{0:T(128)} %bitcast.12, s32[96]{0:T(128)} %bitcast.13, s32[1]{0:T(128)} %bitcast.6.count_hbm, s32[1,256]{1,0:T(1,128)} %bitcast.7), custom_call_target="tpu_custom_call" | custom-call | tf_op jit(solution)/shard_map/first_terms/pallas_call | solution.py:212
  5.7 0.5 %collective-permute-start = (f32[256,256]{1,0:T(8,128)S(1)}, f32[256,256]{1,0:T(8,128)S(1)}, u32[]{:S(2)}, u32[]{:S(2)}) collective-permute-start(f32[256,256]{1,0:T(8,128)S(1)} %get-tuple-element.13), channel_id=1, source_target_pairs={{0,1},{1,0},{2,3},{3,2},{4,5},{5,4},{6,7},{7,6},{8,9},{9,8},{10,11... | collective-permute-start | bytes 786440 | tf_op jit(solution)/shard_map/ppermute | solution.py:184
  6.2 1.2 %collective-permute-done.came_ref = f32[256,256]{1,0:T(8,128)S(1)} collective-permute-done((f32[256,256]{1,0:T(8,128)S(1)}, f32[256,256]{1,0:T(8,128)S(1)}, u32[]{:S(2)}, u32[]{:S(2)}) %collective-permute-start) | collective-permute-done | bytes 262176 | tf_op jit(solution)/shard_map/ppermute | solution.py:184
  7.4 0.0 copy-done
  7.4 2.9 %collective-permute-start.1 = (f32[64,256]{1,0:T(8,128)S(1)}, f32[64,256]{1,0:T(8,128)S(1)}, u32[]{:S(2)}, u32[]{:S(2)}) collective-permute-start(f32[64,256]{1,0:T(8,128)S(1)} %get-tuple-element.15), channel_id=1, source_target_pairs={{0,2},{2,0},{4,6},{6,4},{8,10},{10,8},{12,14},{14,12},{1,3},{3,1},... | collective-permute-start | bytes 196616 | tf_op jit(solution)/shard_map/ppermute | solution.py:187
  10.4 3.6 %collective-permute-start.7 = (bf16[1,128,256]{2,1,0:T(8,128)(2,1)S(1)}, bf16[1,128,256]{2,1,0:T(8,128)(2,1)S(1)}, u32[]{:S(2)}, u32[]{:S(2)}) collective-permute-start(bf16[1,128,256]{2,1,0:T(8,128)(2,1)S(1)} %get-tuple-element.17.held_ref), channel_id=1, source_target_pairs={{0,12},{2,14},{4,8},{6,10},{8,4},{10,6},{12,0},{14,2},{1,13},{3,15... | collective-permute-start | bytes 196616 | tf_op jit(solution)/shard_map/ppermute | solution.py:187
  14.0 0.0 collective-permute-done.1.came_ref
  14.0 0.8 %collective-permute-start.2 = (f32[64,256]{1,0:T(8,128)S(1)}, f32[64,256]{1,0:T(8,128)S(1)}, u32[]{:S(2)}, u32[]{:S(2)}) collective-permute-start(f32[64,256]{1,0:T(8,128)S(1)} %plane_sum.1.hold_ref), channel_id=1, source_target_pairs={{0,4},{2,6},{4,0},{6,2},{8,12},{10,14},{12,8},{14,10},{1,5},{3,7},... | collective-permute-start | bytes 196616 | tf_op jit(solution)/shard_map/ppermute | solution.py:187
  14.8 1.8 %collective-permute-done.7.came_ref = bf16[1,128,256]{2,1,0:T(8,128)(2,1)S(1)} collective-permute-done((bf16[1,128,256]{2,1,0:T(8,128)(2,1)S(1)}, bf16[1,128,256]{2,1,0:T(8,128)(2,1)S(1)}, u32[]{:S(2)}, u32[]{:S(2)}) %collective-permute-start.7) | collective-permute-done | bytes 65568 | tf_op jit(solution)/shard_map/ppermute | solution.py:187
  16.6 0.8 %collective-permute-start.8 = (bf16[2,128,256]{2,1,0:T(8,128)(2,1)S(1)}, bf16[2,128,256]{2,1,0:T(8,128)(2,1)S(1)}, u32[]{:S(2)}, u32[]{:S(2)}) collective-permute-start(bf16[2,128,256]{2,1,0:T(8,128)(2,1)S(1)} %join_near.1.refs_0_), channel_id=1, source_target_pairs={{0,4},{2,6},{4,0},{6,2},{8,12},{10,14},{12,8},{14,10},{1,5},{3,7},... | collective-permute-start | bytes 393224 | tf_op jit(solution)/shard_map/ppermute | solution.py:187
  17.4 1.3 %collective-permute-done.2.came_ref = f32[64,256]{1,0:T(8,128)S(1)} collective-permute-done((f32[64,256]{1,0:T(8,128)S(1)}, f32[64,256]{1,0:T(8,128)S(1)}, u32[]{:S(2)}, u32[]{:S(2)}) %collective-permute-start.2) | collective-permute-done | bytes 65568 | tf_op jit(solution)/shard_map/ppermute | solution.py:187
  18.7 2.6 %collective-permute-start.3 = (f32[64,256]{1,0:T(8,128)S(1)}, f32[64,256]{1,0:T(8,128)S(1)}, u32[]{:S(2)}, u32[]{:S(2)}) collective-permute-start(f32[64,256]{1,0:T(8,128)S(1)} %pair_sum.1.held_ref), channel_id=1, source_target_pairs={{0,12},{2,14},{4,8},{6,10},{8,4},{10,6},{12,0},{14,2},{1,13},{3,15... | collective-permute-start | bytes 196616 | tf_op jit(solution)/shard_map/ppermute | solution.py:187
  21.3 2.0 %collective-permute-start.9 = (bf16[2,128,256]{2,1,0:T(8,128)(2,1)S(1)}, bf16[2,128,256]{2,1,0:T(8,128)(2,1)S(1)}, u32[]{:S(2)}, u32[]{:S(2)}) collective-permute-start(bf16[2,128,256]{2,1,0:T(8,128)(2,1)S(1)} %join_near.1.refs_0_), channel_id=1, source_target_pairs={{0,2},{2,0},{4,6},{6,4},{8,10},{10,8},{12,14},{14,12},{1,3},{3,1},... | collective-permute-start | bytes 393224 | tf_op jit(solution)/shard_map/ppermute | solution.py:187
  23.3 0.0 collective-permute-done.8.refs_1_
  23.3 0.1 collective-permute-start.10
  23.3 1.5 %collective-permute-done.3.came_ref = f32[64,256]{1,0:T(8,128)S(1)} collective-permute-done((f32[64,256]{1,0:T(8,128)S(1)}, f32[64,256]{1,0:T(8,128)S(1)}, u32[]{:S(2)}, u32[]{:S(2)}) %collective-permute-start.3) | collective-permute-done | bytes 65568 | tf_op jit(solution)/shard_map/ppermute | solution.py:187
  24.9 0.1 collective-permute-start.6
  25.0 1.0 %collective-permute-start.5 = (bf16[64,256]{1,0:T(8,128)(2,1)S(1)}, bf16[64,256]{1,0:T(8,128)(2,1)S(1)}, u32[]{:S(2)}, u32[]{:S(2)}) collective-permute-start(bf16[64,256]{1,0:T(8,128)(2,1)S(1)} %hub_sums.1.refs_0_), channel_id=1, source_target_pairs={{0,1},{1,0},{2,3},{3,2},{4,5},{5,4},{6,7},{7,6},{8,9},{9,8},{10,11... | collective-permute-start | bytes 98312 | tf_op jit(solution)/shard_map/ppermute | solution.py:184
  26.0 1.1 %collective-permute-start.4 = (bf16[64,256]{1,0:T(8,128)(2,1)S(1)}, bf16[64,256]{1,0:T(8,128)(2,1)S(1)}, u32[]{:S(2)}, u32[]{:S(2)}) collective-permute-start(bf16[64,256]{1,0:T(8,128)(2,1)S(1)} %hub_sums.1.refs_0_), channel_id=1, source_target_pairs={{0,2},{2,0},{4,6},{6,4},{8,10},{10,8},{12,14},{14,12},{1,3},{3,1},... | collective-permute-start | bytes 98312 | tf_op jit(solution)/shard_map/ppermute | solution.py:187
  27.1 0.0 collective-permute-done.9.refs_2_
  27.1 1.5 %collective-permute-done.10.refs_3_ = bf16[2,128,256]{2,1,0:T(8,128)(2,1)S(1)} collective-permute-done((bf16[2,128,256]{2,1,0:T(8,128)(2,1)S(1)}, bf16[2,128,256]{2,1,0:T(8,128)(2,1)S(1)}, u32[]{:S(2)}, u32[]{:S(2)}) %collective-permute-start.10) | collective-permute-done | bytes 131104 | tf_op jit(solution)/shard_map/ppermute | solution.py:187
  28.6 0.7 %score_columns.1.refs_5_ = f32[512,256]{1,0:T(8,128)S(1)} custom-call(bf16[2,128,256]{2,1,0:T(8,128)(2,1)S(1)} %join_near.1.refs_0_, bf16[2,128,256]{2,1,0:T(8,128)(2,1)S(1)} %collective-permute-done.8.refs_1_, bf16[2,128,256]{2,1,0:T(8,128)(2,1)S(1)} %collective-permute-done.9.refs_2_, bf16[2,128,256]{2,1,0:T(8,128)(2,1)S(1)} %collective-permute-done.10.refs_3_, ...), custom_call_target="tpu_custom_call" | custom-call | tf_op jit(solution)/shard_map/score_columns/pallas_call | solution.py:197
  29.3 0.0 collective-permute-done.6.refs_3_
  29.3 0.0 collective-permute-done.5.refs_2_
  29.3 0.5 %collective-permute-done.4.refs_1_ = bf16[64,256]{1,0:T(8,128)(2,1)S(1)} collective-permute-done((bf16[64,256]{1,0:T(8,128)(2,1)S(1)}, bf16[64,256]{1,0:T(8,128)(2,1)S(1)}, u32[]{:S(2)}, u32[]{:S(2)}) %collective-permute-start.4) | collective-permute-done | bytes 32800 | tf_op jit(solution)/shard_map/ppermute | solution.py:187
  29.9 0.4 hub_columns.1
  30.3 0.1 collective-permute-start.11
  30.4 1.5 %collective-permute-done.11.came_ref = f32[256,256]{1,0:T(8,128)S(1)} collective-permute-done((f32[256,256]{1,0:T(8,128)S(1)}, f32[256,256]{1,0:T(8,128)S(1)}, u32[]{:S(2)}, u32[]{:S(2)}) %collective-permute-start.11) | collective-permute-done | bytes 262176 | tf_op jit(solution)/shard_map/ppermute | solution.py:184
  31.9 12.0 %all_to_all.5.parts_ref = f32[8,16,256]{2,1,0:T(8,128)S(1)} all-to-all(f32[8,16,256]{2,1,0:T(8,128)S(1)} %hub_pieces.1), channel_id=1, replica_groups=mesh['groups'=2,'row'=8,'col'=2] {'row'}, dimensions={0} | all-to-all | bytes 262144 | tf_op jit(solution)/shard_map/all_to_all | solution.py:265
  43.9 0.7 %last_sums.1 = (f32[128,256]{1,0:T(8,128)}, f32[16,256]{1,0:T(8,128)}) custom-call(s32[1,256]{1,0:T(1,128)S(1)} %bitcast.10, f32[256,256]{1,0:T(8,128)S(1)} %get-tuple-element.18.keep_ref, f32[256,256]{1,0:T(8,128)S(1)} %collective-permute-done.11.came_ref, f32[8,16,256]{2,1,0:T(8,128)S(1)} %all_to_all.5.parts_ref), custom_call_target="tpu_custom_call" | custom-call | tf_op jit(solution)/shard_map/last_sums/pallas_call | solution.py:197
  (6 shorter events, 0.1 us)
Async XLA Ops:
  0.6 6.8 %copy-start = (s32[256]{0:T(256)S(1)}, s32[256]{0:T(256)}, u32[]{:S(2)}) copy-start(s32[256]{0:T(256)} %param.9) | copy-start | bytes 3076
  5.7 1.7 %collective-permute-start = (f32[256,256]{1,0:T(8,128)S(1)}, f32[256,256]{1,0:T(8,128)S(1)}, u32[]{:S(2)}, u32[]{:S(2)}) collective-permute-start(f32[256,256]{1,0:T(8,128)S(1)} %get-tuple-element.13), channel_id=1, source_target_pairs={{0,1},{1,0},{2,3},{3,2},{4,5},{5,4},{6,7},{7,6},{8,9},{9,8},{10,11... | collective-permute-start | bytes 786440 | tf_op jit(solution)/shard_map/ppermute | solution.py:184
  7.4 6.5 %collective-permute-start.1 = (f32[64,256]{1,0:T(8,128)S(1)}, f32[64,256]{1,0:T(8,128)S(1)}, u32[]{:S(2)}, u32[]{:S(2)}) collective-permute-start(f32[64,256]{1,0:T(8,128)S(1)} %get-tuple-element.15), channel_id=1, source_target_pairs={{0,2},{2,0},{4,6},{6,4},{8,10},{10,8},{12,14},{14,12},{1,3},{3,1},... | collective-permute-start | bytes 196616 | tf_op jit(solution)/shard_map/ppermute | solution.py:187
  10.4 6.2 %collective-permute-start.7 = (bf16[1,128,256]{2,1,0:T(8,128)(2,1)S(1)}, bf16[1,128,256]{2,1,0:T(8,128)(2,1)S(1)}, u32[]{:S(2)}, u32[]{:S(2)}) collective-permute-start(bf16[1,128,256]{2,1,0:T(8,128)(2,1)S(1)} %get-tuple-element.17.held_ref), channel_id=1, source_target_pairs={{0,12},{2,14},{4,8},{6,10},{8,4},{10,6},{12,0},{14,2},{1,13},{3,15... | collective-permute-start | bytes 196616 | tf_op jit(solution)/shard_map/ppermute | solution.py:187
  14.0 4.7 %collective-permute-start.2 = (f32[64,256]{1,0:T(8,128)S(1)}, f32[64,256]{1,0:T(8,128)S(1)}, u32[]{:S(2)}, u32[]{:S(2)}) collective-permute-start(f32[64,256]{1,0:T(8,128)S(1)} %plane_sum.1.hold_ref), channel_id=1, source_target_pairs={{0,4},{2,6},{4,0},{6,2},{8,12},{10,14},{12,8},{14,10},{1,5},{3,7},... | collective-permute-start | bytes 196616 | tf_op jit(solution)/shard_map/ppermute | solution.py:187
  16.6 6.7 %collective-permute-start.8 = (bf16[2,128,256]{2,1,0:T(8,128)(2,1)S(1)}, bf16[2,128,256]{2,1,0:T(8,128)(2,1)S(1)}, u32[]{:S(2)}, u32[]{:S(2)}) collective-permute-start(bf16[2,128,256]{2,1,0:T(8,128)(2,1)S(1)} %join_near.1.refs_0_), channel_id=1, source_target_pairs={{0,4},{2,6},{4,0},{6,2},{8,12},{10,14},{12,8},{14,10},{1,5},{3,7},... | collective-permute-start | bytes 393224 | tf_op jit(solution)/shard_map/ppermute | solution.py:187
  18.7 6.1 %collective-permute-start.3 = (f32[64,256]{1,0:T(8,128)S(1)}, f32[64,256]{1,0:T(8,128)S(1)}, u32[]{:S(2)}, u32[]{:S(2)}) collective-permute-start(f32[64,256]{1,0:T(8,128)S(1)} %pair_sum.1.held_ref), channel_id=1, source_target_pairs={{0,12},{2,14},{4,8},{6,10},{8,4},{10,6},{12,0},{14,2},{1,13},{3,15... | collective-permute-start | bytes 196616 | tf_op jit(solution)/shard_map/ppermute | solution.py:187
  21.3 5.8 %collective-permute-start.9 = (bf16[2,128,256]{2,1,0:T(8,128)(2,1)S(1)}, bf16[2,128,256]{2,1,0:T(8,128)(2,1)S(1)}, u32[]{:S(2)}, u32[]{:S(2)}) collective-permute-start(bf16[2,128,256]{2,1,0:T(8,128)(2,1)S(1)} %join_near.1.refs_0_), channel_id=1, source_target_pairs={{0,2},{2,0},{4,6},{6,4},{8,10},{10,8},{12,14},{14,12},{1,3},{3,1},... | collective-permute-start | bytes 393224 | tf_op jit(solution)/shard_map/ppermute | solution.py:187
  23.3 5.3 %collective-permute-start.10 = (bf16[2,128,256]{2,1,0:T(8,128)(2,1)S(1)}, bf16[2,128,256]{2,1,0:T(8,128)(2,1)S(1)}, u32[]{:S(2)}, u32[]{:S(2)}) collective-permute-start(bf16[2,128,256]{2,1,0:T(8,128)(2,1)S(1)} %collective-permute-done.8.refs_1_), channel_id=1, source_target_pairs={{0,2},{2,0},{4,6},{6,4},{8,10},{10,8},{12,14},{14,12},{1,3},{3,1},... | collective-permute-start | bytes 393224 | tf_op jit(solution)/shard_map/ppermute | solution.py:187
  24.9 4.4 %collective-permute-start.6 = (bf16[64,256]{1,0:T(8,128)(2,1)S(1)}, bf16[64,256]{1,0:T(8,128)(2,1)S(1)}, u32[]{:S(2)}, u32[]{:S(2)}) collective-permute-start(bf16[64,256]{1,0:T(8,128)(2,1)S(1)} %hub_sums.1.refs_0_), channel_id=1, source_target_pairs={{0,3},{1,2},{2,1},{3,0},{4,7},{5,6},{6,5},{7,4},{8,11},{9,10},{10,... | collective-permute-start | bytes 98312 | tf_op jit(solution)/shard_map/ppermute | solution.py:194
  25.0 4.4 %collective-permute-start.5 = (bf16[64,256]{1,0:T(8,128)(2,1)S(1)}, bf16[64,256]{1,0:T(8,128)(2,1)S(1)}, u32[]{:S(2)}, u32[]{:S(2)}) collective-permute-start(bf16[64,256]{1,0:T(8,128)(2,1)S(1)} %hub_sums.1.refs_0_), channel_id=1, source_target_pairs={{0,1},{1,0},{2,3},{3,2},{4,5},{5,4},{6,7},{7,6},{8,9},{9,8},{10,11... | collective-permute-start | bytes 98312 | tf_op jit(solution)/shard_map/ppermute | solution.py:184
  26.0 3.9 %collective-permute-start.4 = (bf16[64,256]{1,0:T(8,128)(2,1)S(1)}, bf16[64,256]{1,0:T(8,128)(2,1)S(1)}, u32[]{:S(2)}, u32[]{:S(2)}) collective-permute-start(bf16[64,256]{1,0:T(8,128)(2,1)S(1)} %hub_sums.1.refs_0_), channel_id=1, source_target_pairs={{0,2},{2,0},{4,6},{6,4},{8,10},{10,8},{12,14},{14,12},{1,3},{3,1},... | collective-permute-start | bytes 98312 | tf_op jit(solution)/shard_map/ppermute | solution.py:187
  30.3 1.6 %collective-permute-start.11 = (f32[256,256]{1,0:T(8,128)S(1)}, f32[256,256]{1,0:T(8,128)S(1)}, u32[]{:S(2)}, u32[]{:S(2)}) collective-permute-start(f32[256,256]{1,0:T(8,128)S(1)} %get-tuple-element.19), channel_id=1, source_target_pairs={{0,1},{1,0},{2,3},{3,2},{4,5},{5,4},{6,7},{7,6},{8,9},{9,8},{10,11... | collective-permute-start | bytes 786440 | tf_op jit(solution)/shard_map/ppermute | solution.py:184

commit v21 on v20

--- a/solution.py
+++ b/solution.py
@@ -13,7 +13,6 @@
 ITERS = 2
 DAMP = 0.85
 CHUNK = 8
-AHEAD = 4
 X = 2
 MICRO = 10 ** 9
 VMEM_LIMIT = 32 * 1024 * 1024
@@ -58,7 +57,7 @@
     for i in range(held.shape[0] // CHUNK):
         part = pl.ds(i * CHUNK, CHUNK)
         copies.append(pltpu.make_async_copy(tiles_ref.at[part], held.at[part], sems.at[i]))
-    for copy in scalars + copies[:AHEAD]:
+    for copy in scalars + copies:
         copy.start()
     total[...] = jnp.zeros_like(total)
     for copy in scalars:
@@ -80,8 +79,6 @@
 
     for i, copy in enumerate(copies):
         copy.wait()
-        if i + AHEAD < len(copies):
-            copies[i + AHEAD].start()
         lax.fori_loop(i * CHUNK, (i + 1) * CHUNK, add_tile, 0, unroll=4)
     for r in range(0, n_rows, side):
         whole = total[pl.ds(r, side), :]

time: 44.9 us -> 43.8 us (0.976)
  Pallas kernels: 6.37 us -> 5.41 us
    pallas_call x1, Pallas kernels: 4.39 us -> 3.44 us  [fast_body(): pl.pallas_call(bind(first_kernel, dims), out_shape=(f32((half, width)), f...]
where the time goes in v21:
time: 43.8 us; the launch traced here: 43.7 us
  starting transfers between devices  15.6 us (36%)
  blocking collectives  12 us (27%)
  waiting for transfers between devices  9.28 us (21%)
  Pallas kernels  5.41 us (12%)
  between operations  1.38 us (3%)
    ppermute x8, starting transfers between devices, to_partner(): return lax.ppermute(x, 'row', [(r, r ^ flip) for r in range(n_row)])  13.9 us
    all_to_all x1, blocking collectives, fast_body(): parts = lax.all_to_all(parts, 'row', 0, 0)  12 us
    ppermute x8, waiting for transfers between devices, to_partner(): return lax.ppermute(x, 'row', [(r, r ^ flip) for r in range(n_row)])  6.59 us
    pallas_call x1, Pallas kernels, fast_body(): pl.pallas_call(bind(first_kernel, dims), out_shape=(f32((half, width)), f...  3.44 us
    ppermute x3, waiting for transfers between devices, other_core(): return lax.ppermute(x, 'col', [(0, 1), (1, 0)])  2.69 us
    pallas_call x9, Pallas kernels, call(): pl.pallas_call(kernel, out_shape=out_shape, in_specs=[VMEM] * len(args),...  1.97 us
    ppermute x3, starting transfers between devices, other_core(): return lax.ppermute(x, 'col', [(0, 1), (1, 0)])  1.58 us
  transfers between devices with their start and end apart: 12, of which 7 were waited for; matrix products, arithmetic and copies ran while one was open for 0% of the time, Pallas kernels for 2%

profile of v21, /device:TPU:0, one launch (start us, length us, event | category | flops | bytes accessed | tf_op | source)
XLA Modules:
  0.0 43.7 jit_solution(16009131331459428153)
XLA Ops:
  0.6 0.0 copy-start
  1.3 3.4 %first_terms.1 = (f32[256,256]{1,0:T(8,128)S(1)}, f32[256,256]{1,0:T(8,128)S(1)}, bf16[1024,1280]{1,0:T(8,128)(2,1)S(1)}) custom-call(bf16[96,128,128]{2,1,0:T(8,128)(2,1)} %bitcast.11, s32[96]{0:T(128)} %bitcast.12, s32[96]{0:T(128)} %bitcast.13, s32[1]{0:T(128)} %bitcast.6.count_hbm, s32[1,256]{1,0:T(1,128)} %bitcast.7), custom_call_target="tpu_custom_call" | custom-call | tf_op jit(solution)/shard_map/first_terms/pallas_call | solution.py:209
  4.7 0.5 %collective-permute-start = (f32[256,256]{1,0:T(8,128)S(1)}, f32[256,256]{1,0:T(8,128)S(1)}, u32[]{:S(2)}, u32[]{:S(2)}) collective-permute-start(f32[256,256]{1,0:T(8,128)S(1)} %get-tuple-element.13), channel_id=1, source_target_pairs={{0,1},{1,0},{2,3},{3,2},{4,5},{5,4},{6,7},{7,6},{8,9},{9,8},{10,11... | collective-permute-start | bytes 786440 | tf_op jit(solution)/shard_map/ppermute | solution.py:181
  5.3 1.2 %collective-permute-done.came_ref = f32[256,256]{1,0:T(8,128)S(1)} collective-permute-done((f32[256,256]{1,0:T(8,128)S(1)}, f32[256,256]{1,0:T(8,128)S(1)}, u32[]{:S(2)}, u32[]{:S(2)}) %collective-permute-start) | collective-permute-done | bytes 262176 | tf_op jit(solution)/shard_map/ppermute | solution.py:181
  6.4 0.0 copy-done
  6.5 2.9 %collective-permute-start.1 = (f32[64,256]{1,0:T(8,128)S(1)}, f32[64,256]{1,0:T(8,128)S(1)}, u32[]{:S(2)}, u32[]{:S(2)}) collective-permute-start(f32[64,256]{1,0:T(8,128)S(1)} %get-tuple-element.15), channel_id=1, source_target_pairs={{0,2},{2,0},{4,6},{6,4},{8,10},{10,8},{12,14},{14,12},{1,3},{3,1},... | collective-permute-start | bytes 196616 | tf_op jit(solution)/shard_map/ppermute | solution.py:184
  9.4 3.6 %collective-permute-start.7 = (bf16[1,128,256]{2,1,0:T(8,128)(2,1)S(1)}, bf16[1,128,256]{2,1,0:T(8,128)(2,1)S(1)}, u32[]{:S(2)}, u32[]{:S(2)}) collective-permute-start(bf16[1,128,256]{2,1,0:T(8,128)(2,1)S(1)} %get-tuple-element.17.held_ref), channel_id=1, source_target_pairs={{0,12},{2,14},{4,8},{6,10},{8,4},{10,6},{12,0},{14,2},{1,13},{3,15... | collective-permute-start | bytes 196616 | tf_op jit(solution)/shard_map/ppermute | solution.py:184
  13.0 0.0 collective-permute-done.1.came_ref
  13.0 0.8 %collective-permute-start.2 = (f32[64,256]{1,0:T(8,128)S(1)}, f32[64,256]{1,0:T(8,128)S(1)}, u32[]{:S(2)}, u32[]{:S(2)}) collective-permute-start(f32[64,256]{1,0:T(8,128)S(1)} %plane_sum.1.hold_ref), channel_id=1, source_target_pairs={{0,4},{2,6},{4,0},{6,2},{8,12},{10,14},{12,8},{14,10},{1,5},{3,7},... | collective-permute-start | bytes 196616 | tf_op jit(solution)/shard_map/ppermute | solution.py:184
  13.8 1.8 %collective-permute-done.7.came_ref = bf16[1,128,256]{2,1,0:T(8,128)(2,1)S(1)} collective-permute-done((bf16[1,128,256]{2,1,0:T(8,128)(2,1)S(1)}, bf16[1,128,256]{2,1,0:T(8,128)(2,1)S(1)}, u32[]{:S(2)}, u32[]{:S(2)}) %collective-permute-start.7) | collective-permute-done | bytes 65568 | tf_op jit(solution)/shard_map/ppermute | solution.py:184
  15.6 0.8 %collective-permute-start.8 = (bf16[2,128,256]{2,1,0:T(8,128)(2,1)S(1)}, bf16[2,128,256]{2,1,0:T(8,128)(2,1)S(1)}, u32[]{:S(2)}, u32[]{:S(2)}) collective-permute-start(bf16[2,128,256]{2,1,0:T(8,128)(2,1)S(1)} %join_near.1.refs_0_), channel_id=1, source_target_pairs={{0,4},{2,6},{4,0},{6,2},{8,12},{10,14},{12,8},{14,10},{1,5},{3,7},... | collective-permute-start | bytes 393224 | tf_op jit(solution)/shard_map/ppermute | solution.py:184
  16.5 1.3 %collective-permute-done.2.came_ref = f32[64,256]{1,0:T(8,128)S(1)} collective-permute-done((f32[64,256]{1,0:T(8,128)S(1)}, f32[64,256]{1,0:T(8,128)S(1)}, u32[]{:S(2)}, u32[]{:S(2)}) %collective-permute-start.2) | collective-permute-done | bytes 65568 | tf_op jit(solution)/shard_map/ppermute | solution.py:184
  17.8 2.6 %collective-permute-start.3 = (f32[64,256]{1,0:T(8,128)S(1)}, f32[64,256]{1,0:T(8,128)S(1)}, u32[]{:S(2)}, u32[]{:S(2)}) collective-permute-start(f32[64,256]{1,0:T(8,128)S(1)} %pair_sum.1.held_ref), channel_id=1, source_target_pairs={{0,12},{2,14},{4,8},{6,10},{8,4},{10,6},{12,0},{14,2},{1,13},{3,15... | collective-permute-start | bytes 196616 | tf_op jit(solution)/shard_map/ppermute | solution.py:184
  20.4 2.0 %collective-permute-start.9 = (bf16[2,128,256]{2,1,0:T(8,128)(2,1)S(1)}, bf16[2,128,256]{2,1,0:T(8,128)(2,1)S(1)}, u32[]{:S(2)}, u32[]{:S(2)}) collective-permute-start(bf16[2,128,256]{2,1,0:T(8,128)(2,1)S(1)} %join_near.1.refs_0_), channel_id=1, source_target_pairs={{0,2},{2,0},{4,6},{6,4},{8,10},{10,8},{12,14},{14,12},{1,3},{3,1},... | collective-permute-start | bytes 393224 | tf_op jit(solution)/shard_map/ppermute | solution.py:184
  22.3 0.0 collective-permute-done.8.refs_1_
  22.3 0.1 collective-permute-start.10
  22.4 1.5 %collective-permute-done.3.came_ref = f32[64,256]{1,0:T(8,128)S(1)} collective-permute-done((f32[64,256]{1,0:T(8,128)S(1)}, f32[64,256]{1,0:T(8,128)S(1)}, u32[]{:S(2)}, u32[]{:S(2)}) %collective-permute-start.3) | collective-permute-done | bytes 65568 | tf_op jit(solution)/shard_map/ppermute | solution.py:184
  23.9 0.1 collective-permute-start.6
  24.0 1.0 %collective-permute-start.5 = (bf16[64,256]{1,0:T(8,128)(2,1)S(1)}, bf16[64,256]{1,0:T(8,128)(2,1)S(1)}, u32[]{:S(2)}, u32[]{:S(2)}) collective-permute-start(bf16[64,256]{1,0:T(8,128)(2,1)S(1)} %hub_sums.1.refs_0_), channel_id=1, source_target_pairs={{0,1},{1,0},{2,3},{3,2},{4,5},{5,4},{6,7},{7,6},{8,9},{9,8},{10,11... | collective-permute-start | bytes 98312 | tf_op jit(solution)/shard_map/ppermute | solution.py:181
  25.0 1.1 %collective-permute-start.4 = (bf16[64,256]{1,0:T(8,128)(2,1)S(1)}, bf16[64,256]{1,0:T(8,128)(2,1)S(1)}, u32[]{:S(2)}, u32[]{:S(2)}) collective-permute-start(bf16[64,256]{1,0:T(8,128)(2,1)S(1)} %hub_sums.1.refs_0_), channel_id=1, source_target_pairs={{0,2},{2,0},{4,6},{6,4},{8,10},{10,8},{12,14},{14,12},{1,3},{3,1},... | collective-permute-start | bytes 98312 | tf_op jit(solution)/shard_map/ppermute | solution.py:184
  26.1 0.0 collective-permute-done.9.refs_2_
  26.1 1.4 %collective-permute-done.10.refs_3_ = bf16[2,128,256]{2,1,0:T(8,128)(2,1)S(1)} collective-permute-done((bf16[2,128,256]{2,1,0:T(8,128)(2,1)S(1)}, bf16[2,128,256]{2,1,0:T(8,128)(2,1)S(1)}, u32[]{:S(2)}, u32[]{:S(2)}) %collective-permute-start.10) | collective-permute-done | bytes 131104 | tf_op jit(solution)/shard_map/ppermute | solution.py:184
  27.6 0.7 %score_columns.1.refs_5_ = f32[512,256]{1,0:T(8,128)S(1)} custom-call(bf16[2,128,256]{2,1,0:T(8,128)(2,1)S(1)} %join_near.1.refs_0_, bf16[2,128,256]{2,1,0:T(8,128)(2,1)S(1)} %collective-permute-done.8.refs_1_, bf16[2,128,256]{2,1,0:T(8,128)(2,1)S(1)} %collective-permute-done.9.refs_2_, bf16[2,128,256]{2,1,0:T(8,128)(2,1)S(1)} %collective-permute-done.10.refs_3_, ...), custom_call_target="tpu_custom_call" | custom-call | tf_op jit(solution)/shard_map/score_columns/pallas_call | solution.py:194
  28.3 0.0 collective-permute-done.6.refs_3_
  28.4 0.0 collective-permute-done.5.refs_2_
  28.4 0.5 %collective-permute-done.4.refs_1_ = bf16[64,256]{1,0:T(8,128)(2,1)S(1)} collective-permute-done((bf16[64,256]{1,0:T(8,128)(2,1)S(1)}, bf16[64,256]{1,0:T(8,128)(2,1)S(1)}, u32[]{:S(2)}, u32[]{:S(2)}) %collective-permute-start.4) | collective-permute-done | bytes 32800 | tf_op jit(solution)/shard_map/ppermute | solution.py:184
  28.9 0.4 hub_columns.1
  29.3 0.1 collective-permute-start.11
  29.4 1.5 %collective-permute-done.11.came_ref = f32[256,256]{1,0:T(8,128)S(1)} collective-permute-done((f32[256,256]{1,0:T(8,128)S(1)}, f32[256,256]{1,0:T(8,128)S(1)}, u32[]{:S(2)}, u32[]{:S(2)}) %collective-permute-start.11) | collective-permute-done | bytes 262176 | tf_op jit(solution)/shard_map/ppermute | solution.py:181
  30.9 12.0 %all_to_all.5.parts_ref = f32[8,16,256]{2,1,0:T(8,128)S(1)} all-to-all(f32[8,16,256]{2,1,0:T(8,128)S(1)} %hub_pieces.1), channel_id=1, replica_groups=mesh['groups'=2,'row'=8,'col'=2] {'row'}, dimensions={0} | all-to-all | bytes 262144 | tf_op jit(solution)/shard_map/all_to_all | solution.py:262
  43.0 0.7 %last_sums.1 = (f32[128,256]{1,0:T(8,128)}, f32[16,256]{1,0:T(8,128)}) custom-call(s32[1,256]{1,0:T(1,128)S(1)} %bitcast.10, f32[256,256]{1,0:T(8,128)S(1)} %get-tuple-element.18.keep_ref, f32[256,256]{1,0:T(8,128)S(1)} %collective-permute-done.11.came_ref, f32[8,16,256]{2,1,0:T(8,128)S(1)} %all_to_all.5.parts_ref), custom_call_target="tpu_custom_call" | custom-call | tf_op jit(solution)/shard_map/last_sums/pallas_call | solution.py:194
  (6 shorter events, 0.1 us)
Async XLA Ops:
  0.6 5.8 %copy-start = (s32[256]{0:T(256)S(1)}, s32[256]{0:T(256)}, u32[]{:S(2)}) copy-start(s32[256]{0:T(256)} %param.9) | copy-start | bytes 3076
  4.7 1.7 %collective-permute-start = (f32[256,256]{1,0:T(8,128)S(1)}, f32[256,256]{1,0:T(8,128)S(1)}, u32[]{:S(2)}, u32[]{:S(2)}) collective-permute-start(f32[256,256]{1,0:T(8,128)S(1)} %get-tuple-element.13), channel_id=1, source_target_pairs={{0,1},{1,0},{2,3},{3,2},{4,5},{5,4},{6,7},{7,6},{8,9},{9,8},{10,11... | collective-permute-start | bytes 786440 | tf_op jit(solution)/shard_map/ppermute | solution.py:181
  6.5 6.5 %collective-permute-start.1 = (f32[64,256]{1,0:T(8,128)S(1)}, f32[64,256]{1,0:T(8,128)S(1)}, u32[]{:S(2)}, u32[]{:S(2)}) collective-permute-start(f32[64,256]{1,0:T(8,128)S(1)} %get-tuple-element.15), channel_id=1, source_target_pairs={{0,2},{2,0},{4,6},{6,4},{8,10},{10,8},{12,14},{14,12},{1,3},{3,1},... | collective-permute-start | bytes 196616 | tf_op jit(solution)/shard_map/ppermute | solution.py:184
  9.4 6.2 %collective-permute-start.7 = (bf16[1,128,256]{2,1,0:T(8,128)(2,1)S(1)}, bf16[1,128,256]{2,1,0:T(8,128)(2,1)S(1)}, u32[]{:S(2)}, u32[]{:S(2)}) collective-permute-start(bf16[1,128,256]{2,1,0:T(8,128)(2,1)S(1)} %get-tuple-element.17.held_ref), channel_id=1, source_target_pairs={{0,12},{2,14},{4,8},{6,10},{8,4},{10,6},{12,0},{14,2},{1,13},{3,15... | collective-permute-start | bytes 196616 | tf_op jit(solution)/shard_map/ppermute | solution.py:184
  13.0 4.7 %collective-permute-start.2 = (f32[64,256]{1,0:T(8,128)S(1)}, f32[64,256]{1,0:T(8,128)S(1)}, u32[]{:S(2)}, u32[]{:S(2)}) collective-permute-start(f32[64,256]{1,0:T(8,128)S(1)} %plane_sum.1.hold_ref), channel_id=1, source_target_pairs={{0,4},{2,6},{4,0},{6,2},{8,12},{10,14},{12,8},{14,10},{1,5},{3,7},... | collective-permute-start | bytes 196616 | tf_op jit(solution)/shard_map/ppermute | solution.py:184
  15.6 6.7 %collective-permute-start.8 = (bf16[2,128,256]{2,1,0:T(8,128)(2,1)S(1)}, bf16[2,128,256]{2,1,0:T(8,128)(2,1)S(1)}, u32[]{:S(2)}, u32[]{:S(2)}) collective-permute-start(bf16[2,128,256]{2,1,0:T(8,128)(2,1)S(1)} %join_near.1.refs_0_), channel_id=1, source_target_pairs={{0,4},{2,6},{4,0},{6,2},{8,12},{10,14},{12,8},{14,10},{1,5},{3,7},... | collective-permute-start | bytes 393224 | tf_op jit(solution)/shard_map/ppermute | solution.py:184
  17.8 6.1 %collective-permute-start.3 = (f32[64,256]{1,0:T(8,128)S(1)}, f32[64,256]{1,0:T(8,128)S(1)}, u32[]{:S(2)}, u32[]{:S(2)}) collective-permute-start(f32[64,256]{1,0:T(8,128)S(1)} %pair_sum.1.held_ref), channel_id=1, source_target_pairs={{0,12},{2,14},{4,8},{6,10},{8,4},{10,6},{12,0},{14,2},{1,13},{3,15... | collective-permute-start | bytes 196616 | tf_op jit(solution)/shard_map/ppermute | solution.py:184
  20.4 5.8 %collective-permute-start.9 = (bf16[2,128,256]{2,1,0:T(8,128)(2,1)S(1)}, bf16[2,128,256]{2,1,0:T(8,128)(2,1)S(1)}, u32[]{:S(2)}, u32[]{:S(2)}) collective-permute-start(bf16[2,128,256]{2,1,0:T(8,128)(2,1)S(1)} %join_near.1.refs_0_), channel_id=1, source_target_pairs={{0,2},{2,0},{4,6},{6,4},{8,10},{10,8},{12,14},{14,12},{1,3},{3,1},... | collective-permute-start | bytes 393224 | tf_op jit(solution)/shard_map/ppermute | solution.py:184
  22.3 5.3 %collective-permute-start.10 = (bf16[2,128,256]{2,1,0:T(8,128)(2,1)S(1)}, bf16[2,128,256]{2,1,0:T(8,128)(2,1)S(1)}, u32[]{:S(2)}, u32[]{:S(2)}) collective-permute-start(bf16[2,128,256]{2,1,0:T(8,128)(2,1)S(1)} %collective-permute-done.8.refs_1_), channel_id=1, source_target_pairs={{0,2},{2,0},{4,6},{6,4},{8,10},{10,8},{12,14},{14,12},{1,3},{3,1},... | collective-permute-start | bytes 393224 | tf_op jit(solution)/shard_map/ppermute | solution.py:184
  23.9 4.4 %collective-permute-start.6 = (bf16[64,256]{1,0:T(8,128)(2,1)S(1)}, bf16[64,256]{1,0:T(8,128)(2,1)S(1)}, u32[]{:S(2)}, u32[]{:S(2)}) collective-permute-start(bf16[64,256]{1,0:T(8,128)(2,1)S(1)} %hub_sums.1.refs_0_), channel_id=1, source_target_pairs={{0,3},{1,2},{2,1},{3,0},{4,7},{5,6},{6,5},{7,4},{8,11},{9,10},{10,... | collective-permute-start | bytes 98312 | tf_op jit(solution)/shard_map/ppermute | solution.py:191
  24.0 4.3 %collective-permute-start.5 = (bf16[64,256]{1,0:T(8,128)(2,1)S(1)}, bf16[64,256]{1,0:T(8,128)(2,1)S(1)}, u32[]{:S(2)}, u32[]{:S(2)}) collective-permute-start(bf16[64,256]{1,0:T(8,128)(2,1)S(1)} %hub_sums.1.refs_0_), channel_id=1, source_target_pairs={{0,1},{1,0},{2,3},{3,2},{4,5},{5,4},{6,7},{7,6},{8,9},{9,8},{10,11... | collective-permute-start | bytes 98312 | tf_op jit(solution)/shard_map/ppermute | solution.py:181
  25.0 3.9 %collective-permute-start.4 = (bf16[64,256]{1,0:T(8,128)(2,1)S(1)}, bf16[64,256]{1,0:T(8,128)(2,1)S(1)}, u32[]{:S(2)}, u32[]{:S(2)}) collective-permute-start(bf16[64,256]{1,0:T(8,128)(2,1)S(1)} %hub_sums.1.refs_0_), channel_id=1, source_target_pairs={{0,2},{2,0},{4,6},{6,4},{8,10},{10,8},{12,14},{14,12},{1,3},{3,1},... | collective-permute-start | bytes 98312 | tf_op jit(solution)/shard_map/ppermute | solution.py:184
  29.3 1.6 %collective-permute-start.11 = (f32[256,256]{1,0:T(8,128)S(1)}, f32[256,256]{1,0:T(8,128)S(1)}, u32[]{:S(2)}, u32[]{:S(2)}) collective-permute-start(f32[256,256]{1,0:T(8,128)S(1)} %get-tuple-element.19), channel_id=1, source_target_pairs={{0,1},{1,0},{2,3},{3,2},{4,5},{5,4},{6,7},{7,6},{8,9},{9,8},{10,11... | collective-permute-start | bytes 786440 | tf_op jit(solution)/shard_map/ppermute | solution.py:181

commit v22 on v21

--- a/solution.py
+++ b/solution.py
@@ -31,16 +31,6 @@
     return (ids == src).astype(jnp.float32)
 
 
-def write_terms(dims, block, prod_ref, send_ref, keep_ref):
-    n_row, n_col, side = dims
-    c = lax.axis_index("col")
-    for ref, col in ((keep_ref, c), (send_ref, 1 - c)):
-        ref[:VB] = prod_ref[pl.ds(pl.multiple_of(col * VB, VB), VB), :]
-        for k in range(H // n_col // block):
-            start = n_col * VB + (k * n_col + col) * block
-            ref[VB + k * block:VB + (k + 1) * block] = prod_ref[pl.ds(pl.multiple_of(start, block), block), :]
-
-
 def product(dense, panel):
     prod = jnp.dot(dense, panel, preferred_element_type=jnp.float32)
     rows = prod.shape[0] // 2
@@ -48,9 +38,11 @@
 
 
 def first_kernel(dims, tiles_ref, rows_hbm, cols_hbm, count_hbm, src_hbm, send_ref, keep_ref, dense_ref,
-                 held, rows_ref, cols_ref, count_ref, src_ref, total, panel, prod, sems, small):
+                 held, rows_ref, cols_ref, count_ref, src_ref, total, panel, sems, small):
     n_row, n_col, side = dims
     n_rows = dense_ref.shape[0] // 2
+    piece = H // (n_row * n_col)
+    c = lax.axis_index("col")
     pairs = ((src_hbm, src_ref), (rows_hbm, rows_ref), (cols_hbm, cols_ref), (count_hbm, count_ref))
     scalars = [pltpu.make_async_copy(a, b, small.at[i]) for i, (a, b) in enumerate(pairs)]
     copies = []
@@ -64,7 +56,7 @@
         copy.wait()
     src = src_ref[...]
     for r in range(n_row):
-        first = H + (r * n_col + lax.axis_index("col")) * VB
+        first = H + (r * n_col + c) * VB
         panel[pl.ds(r * VB, VB), :] = one_hot(first, VB, src).astype(jnp.bfloat16)
     panel[pl.ds(n_row * VB, H), :] = one_hot(0, H, src).astype(jnp.bfloat16)
     count = count_ref[0]
@@ -80,38 +72,47 @@
     for i, copy in enumerate(copies):
         copy.wait()
         lax.fori_loop(i * CHUNK, (i + 1) * CHUNK, add_tile, 0, unroll=4)
-    for r in range(0, n_rows, side):
-        whole = total[pl.ds(r, side), :]
-        high = whole.astype(jnp.bfloat16)
-        dense_ref[pl.ds(r, side), :] = high
-        dense_ref[pl.ds(n_rows + r, side), :] = (whole - high.astype(jnp.float32)).astype(jnp.bfloat16)
-    prod[...] = product(dense_ref[...], panel[...])
-    write_terms(dims, H // n_col, prod, send_ref, keep_ref)
+    half = n_rows // n_col
+    for at, out, core in ((0, keep_ref, c), (n_rows, send_ref, 1 - c)):
+        chunks = [(0, core * VB, VB)]
+        for r in range(n_row):
+            chunks.append((VB + r * piece, n_col * VB + (r * n_col + core) * piece, piece))
+        for to, start, size in chunks:
+            whole = total[pl.ds(pl.multiple_of(start, size), size), :]
+            high = whole.astype(jnp.bfloat16)
+            dense_ref[at + to:at + to + size] = high
+            dense_ref[at + half + to:at + half + to + size] = (whole - high.astype(jnp.float32)).astype(jnp.bfloat16)
+        out[...] = product(dense_ref[at:at + 2 * half], panel[...])
 
 
 def score_columns_kernel(dims, flips, *refs):
     n_row, n_col, side = dims
     n_z = n_row // X
-    blocks, (dense_ref, prod_ref, panel) = refs[:4], refs[4:]
+    blocks, (dense_ref, send_ref, keep_ref, panel) = refs[:4], refs[4:]
     r = lax.axis_index("row")
     near, far = flips[:n_z // 2], flips[n_z // 2:]
     for ref, group, x in ((blocks[0], near, 0), (blocks[1], far, 0), (blocks[2], near, 1), (blocks[3], far, 1)):
         for k, flip in enumerate(group):
             owner = r ^ (X * flip + x)
             panel[pl.ds(pl.multiple_of(owner * VB, VB), VB), :] = ref[k]
-    prod_ref[...] = product(dense_ref[:, :n_row * VB], panel[...])
+    n_rows = dense_ref.shape[0] // 2
+    keep_ref[...] = product(dense_ref[:n_rows, :n_row * VB], panel[...])
+    send_ref[...] = product(dense_ref[n_rows:, :n_row * VB], panel[...])
 
 
 def hub_columns_kernel(dims, *refs):
     n_row, n_col, side = dims
-    quarters, (dense_ref, prod_ref, send_ref, keep_ref, panel, total) = refs[:X * n_col], refs[X * n_col:]
+    n_z = n_row // X
+    quarters, (dense_ref, send_part, keep_part, send_ref, keep_ref, panel) = refs[:X * n_col], refs[X * n_col:]
     r, c = lax.axis_index("row"), lax.axis_index("col")
-    quarter = quarters[0].shape[0]
+    piece = H // (n_row * n_col)
     for k, ref in enumerate(quarters):
-        place = ((c ^ (k // X)) * X + (r % X ^ (k % X))) * quarter
-        panel[pl.ds(pl.multiple_of(place, quarter), quarter), :] = ref[...]
-    total[...] = prod_ref[...] + product(dense_ref[:, n_row * VB:], panel[...])
-    write_terms(dims, H // (n_row * n_col), total, send_ref, keep_ref)
+        for i in range(n_z):
+            row = ((r % X ^ (k % X)) * n_z + i) * n_col + (c ^ (k // X))
+            panel[pl.ds(pl.multiple_of(row * piece, piece), piece), :] = ref[i * piece:(i + 1) * piece]
+    n_rows = dense_ref.shape[0] // 2
+    send_ref[...] = send_part[...] + product(dense_ref[n_rows:, n_row * VB:], panel[...])
+    keep_ref[...] = keep_part[...] + product(dense_ref[:n_rows, n_row * VB:], panel[...])
 
 
 def own_scores(dims, src_ref, keep_ref, came_ref):
@@ -140,9 +141,12 @@
 
 
 def hub_kernel(dims, src_ref, held_ref, came_ref, out_ref):
-    quarter = out_ref.shape[0]
-    first = (lax.axis_index("col") * X + lax.axis_index("row") % X) * quarter
-    tele = one_hot(first, quarter, src_ref[...])
+    n_row, n_col, side = dims
+    piece = H // (n_row * n_col)
+    r, c = lax.axis_index("row"), lax.axis_index("col")
+    at = lax.broadcasted_iota(jnp.int32, out_ref.shape, 0)
+    ids = ((r % X * (n_row // X) + at // piece) * n_col + c) * piece + at % piece
+    tele = (ids == src_ref[...]).astype(jnp.float32)
     out_ref[...] = (DAMP * (held_ref[...] + came_ref[...]) + 0.15 * tele).astype(out_ref.dtype)
 
 
@@ -219,7 +223,6 @@
             pltpu.VMEM((1, width), jnp.int32),
             pltpu.VMEM((n_rows + side, n_cols), jnp.float32),
             pltpu.VMEM((n_cols, width), jnp.bfloat16),
-            pltpu.VMEM((n_rows, width), jnp.float32),
             pltpu.SemaphoreType.DMA((slots // CHUNK,)),
             pltpu.SemaphoreType.DMA((4,)),
         ],
@@ -250,13 +253,12 @@
             sums = call(add_kernel, "pair_sum", f32((quarter, width)), sums, to_partner(sums, X * mask), cost=1)
         mine = call(bind(hub_kernel, dims), "hub_sums", bf16((quarter, width)), src, sums, to_partner(sums, X * masks[0]), cost=1)
         quarters = [mine, other_side(mine), other_core(mine), other_both(mine)]
-        prod = call(
-            bind(score_columns_kernel, dims, flips), "score_columns", f32((n_rows, width)),
+        send, keep = call(
+            bind(score_columns_kernel, dims, flips), "score_columns", (f32((half, width)),) * 2,
             held, far, near_across, far_across, dense, scratch=[pltpu.VMEM((n_row * VB, width), jnp.bfloat16)])
         send, keep = call(
-            bind(hub_columns_kernel, dims), "hub_columns", (f32((half, width)), f32((half, width))),
-            *quarters, dense, prod,
-            scratch=[pltpu.VMEM((H, width), jnp.bfloat16), pltpu.VMEM((n_rows, width), jnp.float32)])
+            bind(hub_columns_kernel, dims), "hub_columns", (f32((half, width)),) * 2,
+            *quarters, dense, send, keep, scratch=[pltpu.VMEM((H, width), jnp.bfloat16)])
     came = other_core(send)
     parts = call(pieces_kernel, "hub_pieces", f32((n_row, piece, width)), keep, came)
     parts = lax.all_to_all(parts, "row", 0, 0)

time: 43.8 us -> 43.6 us (level)
  no operation moved by 1% of the time
where the time goes in v22:
time: 43.6 us; the launch traced here: 43.4 us
  starting transfers between devices  15.6 us (36%)
  blocking collectives  12 us (28%)
  waiting for transfers between devices  9.29 us (21%)
  Pallas kernels  5.17 us (12%)
  between operations  1.39 us (3%)
    ppermute x8, starting transfers between devices, to_partner(): return lax.ppermute(x, 'row', [(r, r ^ flip) for r in range(n_row)])  13.9 us
    all_to_all x1, blocking collectives, fast_body(): parts = lax.all_to_all(parts, 'row', 0, 0)  12 us
    ppermute x8, waiting for transfers between devices, to_partner(): return lax.ppermute(x, 'row', [(r, r ^ flip) for r in range(n_row)])  6.6 us
    pallas_call x1, Pallas kernels, fast_body(): pl.pallas_call(bind(first_kernel, dims), out_shape=(f32((half, width)), f...  3.3 us
    ppermute x3, waiting for transfers between devices, other_core(): return lax.ppermute(x, 'col', [(0, 1), (1, 0)])  2.69 us
    pallas_call x9, Pallas kernels, call(): pl.pallas_call(kernel, out_shape=out_shape, in_specs=[VMEM] * len(args),...  1.87 us
    ppermute x3, starting transfers between devices, other_core(): return lax.ppermute(x, 'col', [(0, 1), (1, 0)])  1.58 us
  transfers between devices with their start and end apart: 12, of which 7 were waited for; matrix products, arithmetic and copies ran while one was open for 0% of the time, Pallas kernels for 2%

profile of v22, /device:TPU:0, one launch (start us, length us, event | category | flops | bytes accessed | tf_op | source)
XLA Modules:
  0.0 43.4 jit_solution(4158333144164871936)
XLA Ops:
  0.6 0.0 copy-start
  1.3 3.3 %first_terms.1 = (f32[256,256]{1,0:T(8,128)S(1)}, f32[256,256]{1,0:T(8,128)S(1)}, bf16[1024,1280]{1,0:T(8,128)(2,1)S(1)}) custom-call(bf16[96,128,128]{2,1,0:T(8,128)(2,1)} %bitcast.11, s32[96]{0:T(128)} %bitcast.12, s32[96]{0:T(128)} %bitcast.13, s32[1]{0:T(128)} %bitcast.6.count_hbm, s32[1,256]{1,0:T(1,128)} %bitcast.7), custom_call_target="tpu_custom_call" | custom-call | tf_op jit(solution)/shard_map/first_terms/pallas_call | solution.py:213
  4.6 0.5 %collective-permute-start = (f32[256,256]{1,0:T(8,128)S(1)}, f32[256,256]{1,0:T(8,128)S(1)}, u32[]{:S(2)}, u32[]{:S(2)}) collective-permute-start(f32[256,256]{1,0:T(8,128)S(1)} %get-tuple-element.15), channel_id=1, source_target_pairs={{0,1},{1,0},{2,3},{3,2},{4,5},{5,4},{6,7},{7,6},{8,9},{9,8},{10,11... | collective-permute-start | bytes 786440 | tf_op jit(solution)/shard_map/ppermute | solution.py:185
  5.1 1.2 %collective-permute-done.came_ref = f32[256,256]{1,0:T(8,128)S(1)} collective-permute-done((f32[256,256]{1,0:T(8,128)S(1)}, f32[256,256]{1,0:T(8,128)S(1)}, u32[]{:S(2)}, u32[]{:S(2)}) %collective-permute-start) | collective-permute-done | bytes 262176 | tf_op jit(solution)/shard_map/ppermute | solution.py:185
  6.3 0.0 copy-done
  6.3 2.9 %collective-permute-start.1 = (f32[64,256]{1,0:T(8,128)S(1)}, f32[64,256]{1,0:T(8,128)S(1)}, u32[]{:S(2)}, u32[]{:S(2)}) collective-permute-start(f32[64,256]{1,0:T(8,128)S(1)} %get-tuple-element.17), channel_id=1, source_target_pairs={{0,2},{2,0},{4,6},{6,4},{8,10},{10,8},{12,14},{14,12},{1,3},{3,1},... | collective-permute-start | bytes 196616 | tf_op jit(solution)/shard_map/ppermute | solution.py:188
  9.3 3.6 %collective-permute-start.7 = (bf16[1,128,256]{2,1,0:T(8,128)(2,1)S(1)}, bf16[1,128,256]{2,1,0:T(8,128)(2,1)S(1)}, u32[]{:S(2)}, u32[]{:S(2)}) collective-permute-start(bf16[1,128,256]{2,1,0:T(8,128)(2,1)S(1)} %get-tuple-element.19.held_ref), channel_id=1, source_target_pairs={{0,12},{2,14},{4,8},{6,10},{8,4},{10,6},{12,0},{14,2},{1,13},{3,15... | collective-permute-start | bytes 196616 | tf_op jit(solution)/shard_map/ppermute | solution.py:188
  12.9 0.0 collective-permute-done.1.came_ref
  12.9 0.8 %collective-permute-start.2 = (f32[64,256]{1,0:T(8,128)S(1)}, f32[64,256]{1,0:T(8,128)S(1)}, u32[]{:S(2)}, u32[]{:S(2)}) collective-permute-start(f32[64,256]{1,0:T(8,128)S(1)} %plane_sum.1.hold_ref), channel_id=1, source_target_pairs={{0,4},{2,6},{4,0},{6,2},{8,12},{10,14},{12,8},{14,10},{1,5},{3,7},... | collective-permute-start | bytes 196616 | tf_op jit(solution)/shard_map/ppermute | solution.py:188
  13.7 1.8 %collective-permute-done.7.came_ref = bf16[1,128,256]{2,1,0:T(8,128)(2,1)S(1)} collective-permute-done((bf16[1,128,256]{2,1,0:T(8,128)(2,1)S(1)}, bf16[1,128,256]{2,1,0:T(8,128)(2,1)S(1)}, u32[]{:S(2)}, u32[]{:S(2)}) %collective-permute-start.7) | collective-permute-done | bytes 65568 | tf_op jit(solution)/shard_map/ppermute | solution.py:188
  15.5 0.8 %collective-permute-start.8 = (bf16[2,128,256]{2,1,0:T(8,128)(2,1)S(1)}, bf16[2,128,256]{2,1,0:T(8,128)(2,1)S(1)}, u32[]{:S(2)}, u32[]{:S(2)}) collective-permute-start(bf16[2,128,256]{2,1,0:T(8,128)(2,1)S(1)} %join_near.1.refs_0_), channel_id=1, source_target_pairs={{0,4},{2,6},{4,0},{6,2},{8,12},{10,14},{12,8},{14,10},{1,5},{3,7},... | collective-permute-start | bytes 393224 | tf_op jit(solution)/shard_map/ppermute | solution.py:188
  16.3 1.3 %collective-permute-done.2.came_ref = f32[64,256]{1,0:T(8,128)S(1)} collective-permute-done((f32[64,256]{1,0:T(8,128)S(1)}, f32[64,256]{1,0:T(8,128)S(1)}, u32[]{:S(2)}, u32[]{:S(2)}) %collective-permute-start.2) | collective-permute-done | bytes 65568 | tf_op jit(solution)/shard_map/ppermute | solution.py:188
  17.6 2.6 %collective-permute-start.3 = (f32[64,256]{1,0:T(8,128)S(1)}, f32[64,256]{1,0:T(8,128)S(1)}, u32[]{:S(2)}, u32[]{:S(2)}) collective-permute-start(f32[64,256]{1,0:T(8,128)S(1)} %pair_sum.1.held_ref), channel_id=1, source_target_pairs={{0,12},{2,14},{4,8},{6,10},{8,4},{10,6},{12,0},{14,2},{1,13},{3,15... | collective-permute-start | bytes 196616 | tf_op jit(solution)/shard_map/ppermute | solution.py:188
  20.2 2.0 %collective-permute-start.9 = (bf16[2,128,256]{2,1,0:T(8,128)(2,1)S(1)}, bf16[2,128,256]{2,1,0:T(8,128)(2,1)S(1)}, u32[]{:S(2)}, u32[]{:S(2)}) collective-permute-start(bf16[2,128,256]{2,1,0:T(8,128)(2,1)S(1)} %join_near.1.refs_0_), channel_id=1, source_target_pairs={{0,2},{2,0},{4,6},{6,4},{8,10},{10,8},{12,14},{14,12},{1,3},{3,1},... | collective-permute-start | bytes 393224 | tf_op jit(solution)/shard_map/ppermute | solution.py:188
  22.2 0.0 collective-permute-done.8.refs_1_
  22.2 0.1 collective-permute-start.10
  22.3 1.5 %collective-permute-done.3.came_ref = f32[64,256]{1,0:T(8,128)S(1)} collective-permute-done((f32[64,256]{1,0:T(8,128)S(1)}, f32[64,256]{1,0:T(8,128)S(1)}, u32[]{:S(2)}, u32[]{:S(2)}) %collective-permute-start.3) | collective-permute-done | bytes 65568 | tf_op jit(solution)/shard_map/ppermute | solution.py:188
  23.8 0.1 collective-permute-start.6
  23.9 1.0 %collective-permute-start.5 = (bf16[64,256]{1,0:T(8,128)(2,1)S(1)}, bf16[64,256]{1,0:T(8,128)(2,1)S(1)}, u32[]{:S(2)}, u32[]{:S(2)}) collective-permute-start(bf16[64,256]{1,0:T(8,128)(2,1)S(1)} %hub_sums.1.refs_0_), channel_id=1, source_target_pairs={{0,1},{1,0},{2,3},{3,2},{4,5},{5,4},{6,7},{7,6},{8,9},{9,8},{10,11... | collective-permute-start | bytes 98312 | tf_op jit(solution)/shard_map/ppermute | solution.py:185
  24.9 1.1 %collective-permute-start.4 = (bf16[64,256]{1,0:T(8,128)(2,1)S(1)}, bf16[64,256]{1,0:T(8,128)(2,1)S(1)}, u32[]{:S(2)}, u32[]{:S(2)}) collective-permute-start(bf16[64,256]{1,0:T(8,128)(2,1)S(1)} %hub_sums.1.refs_0_), channel_id=1, source_target_pairs={{0,2},{2,0},{4,6},{6,4},{8,10},{10,8},{12,14},{14,12},{1,3},{3,1},... | collective-permute-start | bytes 98312 | tf_op jit(solution)/shard_map/ppermute | solution.py:188
  26.0 0.0 collective-permute-done.9.refs_2_
  26.0 1.4 %collective-permute-done.10.refs_3_ = bf16[2,128,256]{2,1,0:T(8,128)(2,1)S(1)} collective-permute-done((bf16[2,128,256]{2,1,0:T(8,128)(2,1)S(1)}, bf16[2,128,256]{2,1,0:T(8,128)(2,1)S(1)}, u32[]{:S(2)}, u32[]{:S(2)}) %collective-permute-start.10) | collective-permute-done | bytes 131104 | tf_op jit(solution)/shard_map/ppermute | solution.py:188
  27.5 0.7 %score_columns.1 = (f32[256,256]{1,0:T(8,128)S(1)}, f32[256,256]{1,0:T(8,128)S(1)}) custom-call(bf16[2,128,256]{2,1,0:T(8,128)(2,1)S(1)} %join_near.1.refs_0_, bf16[2,128,256]{2,1,0:T(8,128)(2,1)S(1)} %collective-permute-done.8.refs_1_, bf16[2,128,256]{2,1,0:T(8,128)(2,1)S(1)} %collective-permute-done.9.refs_2_, ...), custom_call_target="tpu_custom_call" | custom-call | tf_op jit(solution)/shard_map/score_columns/pallas_call | solution.py:198
  28.2 0.0 collective-permute-done.6.refs_3_
  28.2 0.0 collective-permute-done.5.refs_2_
  28.2 0.6 %collective-permute-done.4.refs_1_ = bf16[64,256]{1,0:T(8,128)(2,1)S(1)} collective-permute-done((bf16[64,256]{1,0:T(8,128)(2,1)S(1)}, bf16[64,256]{1,0:T(8,128)(2,1)S(1)}, u32[]{:S(2)}, u32[]{:S(2)}) %collective-permute-start.4) | collective-permute-done | bytes 32800 | tf_op jit(solution)/shard_map/ppermute | solution.py:188
  28.8 0.3 hub_columns.1
  29.1 0.1 collective-permute-start.11
  29.2 1.5 %collective-permute-done.11.came_ref = f32[256,256]{1,0:T(8,128)S(1)} collective-permute-done((f32[256,256]{1,0:T(8,128)S(1)}, f32[256,256]{1,0:T(8,128)S(1)}, u32[]{:S(2)}, u32[]{:S(2)}) %collective-permute-start.11) | collective-permute-done | bytes 262176 | tf_op jit(solution)/shard_map/ppermute | solution.py:185
  30.7 12.0 %all_to_all.5.parts_ref = f32[8,16,256]{2,1,0:T(8,128)S(1)} all-to-all(f32[8,16,256]{2,1,0:T(8,128)S(1)} %hub_pieces.1), channel_id=1, replica_groups=mesh['groups'=2,'row'=8,'col'=2] {'row'}, dimensions={0} | all-to-all | bytes 262144 | tf_op jit(solution)/shard_map/all_to_all | solution.py:264
  42.7 0.7 %last_sums.1 = (f32[128,256]{1,0:T(8,128)}, f32[16,256]{1,0:T(8,128)}) custom-call(s32[1,256]{1,0:T(1,128)S(1)} %bitcast.10, f32[256,256]{1,0:T(8,128)S(1)} %get-tuple-element.22.keep_ref, f32[256,256]{1,0:T(8,128)S(1)} %collective-permute-done.11.came_ref, f32[8,16,256]{2,1,0:T(8,128)S(1)} %all_to_all.5.parts_ref), custom_call_target="tpu_custom_call" | custom-call | tf_op jit(solution)/shard_map/last_sums/pallas_call | solution.py:198
  (6 shorter events, 0.1 us)
Async XLA Ops:
  0.6 5.7 %copy-start = (s32[256]{0:T(256)S(1)}, s32[256]{0:T(256)}, u32[]{:S(2)}) copy-start(s32[256]{0:T(256)} %param.9) | copy-start | bytes 3076
  4.6 1.7 %collective-permute-start = (f32[256,256]{1,0:T(8,128)S(1)}, f32[256,256]{1,0:T(8,128)S(1)}, u32[]{:S(2)}, u32[]{:S(2)}) collective-permute-start(f32[256,256]{1,0:T(8,128)S(1)} %get-tuple-element.15), channel_id=1, source_target_pairs={{0,1},{1,0},{2,3},{3,2},{4,5},{5,4},{6,7},{7,6},{8,9},{9,8},{10,11... | collective-permute-start | bytes 786440 | tf_op jit(solution)/shard_map/ppermute | solution.py:185
  6.3 6.5 %collective-permute-start.1 = (f32[64,256]{1,0:T(8,128)S(1)}, f32[64,256]{1,0:T(8,128)S(1)}, u32[]{:S(2)}, u32[]{:S(2)}) collective-permute-start(f32[64,256]{1,0:T(8,128)S(1)} %get-tuple-element.17), channel_id=1, source_target_pairs={{0,2},{2,0},{4,6},{6,4},{8,10},{10,8},{12,14},{14,12},{1,3},{3,1},... | collective-permute-start | bytes 196616 | tf_op jit(solution)/shard_map/ppermute | solution.py:188
  9.3 6.2 %collective-permute-start.7 = (bf16[1,128,256]{2,1,0:T(8,128)(2,1)S(1)}, bf16[1,128,256]{2,1,0:T(8,128)(2,1)S(1)}, u32[]{:S(2)}, u32[]{:S(2)}) collective-permute-start(bf16[1,128,256]{2,1,0:T(8,128)(2,1)S(1)} %get-tuple-element.19.held_ref), channel_id=1, source_target_pairs={{0,12},{2,14},{4,8},{6,10},{8,4},{10,6},{12,0},{14,2},{1,13},{3,15... | collective-permute-start | bytes 196616 | tf_op jit(solution)/shard_map/ppermute | solution.py:188
  12.9 4.7 %collective-permute-start.2 = (f32[64,256]{1,0:T(8,128)S(1)}, f32[64,256]{1,0:T(8,128)S(1)}, u32[]{:S(2)}, u32[]{:S(2)}) collective-permute-start(f32[64,256]{1,0:T(8,128)S(1)} %plane_sum.1.hold_ref), channel_id=1, source_target_pairs={{0,4},{2,6},{4,0},{6,2},{8,12},{10,14},{12,8},{14,10},{1,5},{3,7},... | collective-permute-start | bytes 196616 | tf_op jit(solution)/shard_map/ppermute | solution.py:188
  15.5 6.7 %collective-permute-start.8 = (bf16[2,128,256]{2,1,0:T(8,128)(2,1)S(1)}, bf16[2,128,256]{2,1,0:T(8,128)(2,1)S(1)}, u32[]{:S(2)}, u32[]{:S(2)}) collective-permute-start(bf16[2,128,256]{2,1,0:T(8,128)(2,1)S(1)} %join_near.1.refs_0_), channel_id=1, source_target_pairs={{0,4},{2,6},{4,0},{6,2},{8,12},{10,14},{12,8},{14,10},{1,5},{3,7},... | collective-permute-start | bytes 393224 | tf_op jit(solution)/shard_map/ppermute | solution.py:188
  17.6 6.1 %collective-permute-start.3 = (f32[64,256]{1,0:T(8,128)S(1)}, f32[64,256]{1,0:T(8,128)S(1)}, u32[]{:S(2)}, u32[]{:S(2)}) collective-permute-start(f32[64,256]{1,0:T(8,128)S(1)} %pair_sum.1.held_ref), channel_id=1, source_target_pairs={{0,12},{2,14},{4,8},{6,10},{8,4},{10,6},{12,0},{14,2},{1,13},{3,15... | collective-permute-start | bytes 196616 | tf_op jit(solution)/shard_map/ppermute | solution.py:188
  20.2 5.8 %collective-permute-start.9 = (bf16[2,128,256]{2,1,0:T(8,128)(2,1)S(1)}, bf16[2,128,256]{2,1,0:T(8,128)(2,1)S(1)}, u32[]{:S(2)}, u32[]{:S(2)}) collective-permute-start(bf16[2,128,256]{2,1,0:T(8,128)(2,1)S(1)} %join_near.1.refs_0_), channel_id=1, source_target_pairs={{0,2},{2,0},{4,6},{6,4},{8,10},{10,8},{12,14},{14,12},{1,3},{3,1},... | collective-permute-start | bytes 393224 | tf_op jit(solution)/shard_map/ppermute | solution.py:188
  22.2 5.3 %collective-permute-start.10 = (bf16[2,128,256]{2,1,0:T(8,128)(2,1)S(1)}, bf16[2,128,256]{2,1,0:T(8,128)(2,1)S(1)}, u32[]{:S(2)}, u32[]{:S(2)}) collective-permute-start(bf16[2,128,256]{2,1,0:T(8,128)(2,1)S(1)} %collective-permute-done.8.refs_1_), channel_id=1, source_target_pairs={{0,2},{2,0},{4,6},{6,4},{8,10},{10,8},{12,14},{14,12},{1,3},{3,1},... | collective-permute-start | bytes 393224 | tf_op jit(solution)/shard_map/ppermute | solution.py:188
  23.8 4.4 %collective-permute-start.6 = (bf16[64,256]{1,0:T(8,128)(2,1)S(1)}, bf16[64,256]{1,0:T(8,128)(2,1)S(1)}, u32[]{:S(2)}, u32[]{:S(2)}) collective-permute-start(bf16[64,256]{1,0:T(8,128)(2,1)S(1)} %hub_sums.1.refs_0_), channel_id=1, source_target_pairs={{0,3},{1,2},{2,1},{3,0},{4,7},{5,6},{6,5},{7,4},{8,11},{9,10},{10,... | collective-permute-start | bytes 98312 | tf_op jit(solution)/shard_map/ppermute | solution.py:195
  23.9 4.3 %collective-permute-start.5 = (bf16[64,256]{1,0:T(8,128)(2,1)S(1)}, bf16[64,256]{1,0:T(8,128)(2,1)S(1)}, u32[]{:S(2)}, u32[]{:S(2)}) collective-permute-start(bf16[64,256]{1,0:T(8,128)(2,1)S(1)} %hub_sums.1.refs_0_), channel_id=1, source_target_pairs={{0,1},{1,0},{2,3},{3,2},{4,5},{5,4},{6,7},{7,6},{8,9},{9,8},{10,11... | collective-permute-start | bytes 98312 | tf_op jit(solution)/shard_map/ppermute | solution.py:185
  24.9 3.9 %collective-permute-start.4 = (bf16[64,256]{1,0:T(8,128)(2,1)S(1)}, bf16[64,256]{1,0:T(8,128)(2,1)S(1)}, u32[]{:S(2)}, u32[]{:S(2)}) collective-permute-start(bf16[64,256]{1,0:T(8,128)(2,1)S(1)} %hub_sums.1.refs_0_), channel_id=1, source_target_pairs={{0,2},{2,0},{4,6},{6,4},{8,10},{10,8},{12,14},{14,12},{1,3},{3,1},... | collective-permute-start | bytes 98312 | tf_op jit(solution)/shard_map/ppermute | solution.py:188
  29.1 1.6 %collective-permute-start.11 = (f32[256,256]{1,0:T(8,128)S(1)}, f32[256,256]{1,0:T(8,128)S(1)}, u32[]{:S(2)}, u32[]{:S(2)}) collective-permute-start(f32[256,256]{1,0:T(8,128)S(1)} %get-tuple-element.23), channel_id=1, source_target_pairs={{0,1},{1,0},{2,3},{3,2},{4,5},{5,4},{6,7},{7,6},{8,9},{9,8},{10,11... | collective-permute-start | bytes 786440 | tf_op jit(solution)/shard_map/ppermute | solution.py:185

commit v23 on v22

--- a/solution.py
+++ b/solution.py
@@ -230,7 +230,7 @@
         name="first_terms",
     )(*in_hbm[:3], tile_count.reshape(1), in_hbm[3])
 
-    masks = [n_row // X - 1]
+    masks = [n_row // X // 2]
     while masks[-1] > 1:
         masks.append(masks[-1] // 2)
     for step in range(ITERS - 1):

time: 43.6 us -> 43.2 us (level)
  starting transfers between devices: 15.6 us -> 14.6 us
  waiting for transfers between devices: 9.29 us -> 9.92 us
    ppermute x8, starting transfers between devices: 13.9 us -> 12.6 us  [to_partner(): return lax.ppermute(x, 'row', [(r, r ^ flip) for r in range(n_row)])]
    ppermute x8, waiting for transfers between devices: 6.6 us -> 7.23 us  [to_partner(): return lax.ppermute(x, 'row', [(r, r ^ flip) for r in range(n_row)])]
  transfers between devices with their start and end apart: 12 -> 12, of which waited for: 7 -> 8; matrix products, arithmetic and copies ran while one was open for 0% -> 0% of each run, Pallas kernels for 2% -> 2%
where the time goes in v23:
time: 43.2 us; the launch traced here: 43 us
  starting transfers between devices  14.6 us (34%)
  blocking collectives  11.8 us (27%)
  waiting for transfers between devices  9.92 us (23%)
  Pallas kernels  5.19 us (12%)
  between operations  1.39 us (3%)
    ppermute x8, starting transfers between devices, to_partner(): return lax.ppermute(x, 'row', [(r, r ^ flip) for r in range(n_row)])  12.6 us
    all_to_all x1, blocking collectives, fast_body(): parts = lax.all_to_all(parts, 'row', 0, 0)  11.8 us
    ppermute x8, waiting for transfers between devices, to_partner(): return lax.ppermute(x, 'row', [(r, r ^ flip) for r in range(n_row)])  7.23 us
    pallas_call x1, Pallas kernels, fast_body(): pl.pallas_call(bind(first_kernel, dims), out_shape=(f32((half, width)), f...  3.3 us
    ppermute x3, waiting for transfers between devices, other_core(): return lax.ppermute(x, 'col', [(0, 1), (1, 0)])  2.69 us
    ppermute x3, starting transfers between devices, other_core(): return lax.ppermute(x, 'col', [(0, 1), (1, 0)])  1.9 us
    pallas_call x9, Pallas kernels, call(): pl.pallas_call(kernel, out_shape=out_shape, in_specs=[VMEM] * len(args),...  1.89 us
  transfers between devices with their start and end apart: 12, of which 8 were waited for; matrix products, arithmetic and copies ran while one was open for 0% of the time, Pallas kernels for 2%

profile of v23, /device:TPU:0, one launch (start us, length us, event | category | flops | bytes accessed | tf_op | source)
XLA Modules:
  0.0 43.0 jit_solution(8221509141704824)
XLA Ops:
  0.6 0.0 copy-start
  1.3 3.3 %first_terms.1 = (f32[256,256]{1,0:T(8,128)S(1)}, f32[256,256]{1,0:T(8,128)S(1)}, bf16[1024,1280]{1,0:T(8,128)(2,1)S(1)}) custom-call(bf16[96,128,128]{2,1,0:T(8,128)(2,1)} %bitcast.11, s32[96]{0:T(128)} %bitcast.12, s32[96]{0:T(128)} %bitcast.13, s32[1]{0:T(128)} %bitcast.6.count_hbm, s32[1,256]{1,0:T(1,128)} %bitcast.7), custom_call_target="tpu_custom_call" | custom-call | tf_op jit(solution)/shard_map/first_terms/pallas_call | solution.py:213
  4.6 0.5 %collective-permute-start = (f32[256,256]{1,0:T(8,128)S(1)}, f32[256,256]{1,0:T(8,128)S(1)}, u32[]{:S(2)}, u32[]{:S(2)}) collective-permute-start(f32[256,256]{1,0:T(8,128)S(1)} %get-tuple-element.15), channel_id=1, source_target_pairs={{0,1},{1,0},{2,3},{3,2},{4,5},{5,4},{6,7},{7,6},{8,9},{9,8},{10,11... | collective-permute-start | bytes 786440 | tf_op jit(solution)/shard_map/ppermute | solution.py:185
  5.1 1.2 %collective-permute-done.came_ref = f32[256,256]{1,0:T(8,128)S(1)} collective-permute-done((f32[256,256]{1,0:T(8,128)S(1)}, f32[256,256]{1,0:T(8,128)S(1)}, u32[]{:S(2)}, u32[]{:S(2)}) %collective-permute-start) | collective-permute-done | bytes 262176 | tf_op jit(solution)/shard_map/ppermute | solution.py:185
  6.3 0.0 copy-done
  6.3 2.9 %collective-permute-start.1 = (f32[64,256]{1,0:T(8,128)S(1)}, f32[64,256]{1,0:T(8,128)S(1)}, u32[]{:S(2)}, u32[]{:S(2)}) collective-permute-start(f32[64,256]{1,0:T(8,128)S(1)} %get-tuple-element.17), channel_id=1, source_target_pairs={{0,2},{2,0},{4,6},{6,4},{8,10},{10,8},{12,14},{14,12},{1,3},{3,1},... | collective-permute-start | bytes 196616 | tf_op jit(solution)/shard_map/ppermute | solution.py:188
  9.3 2.6 %collective-permute-start.7 = (bf16[1,128,256]{2,1,0:T(8,128)(2,1)S(1)}, bf16[1,128,256]{2,1,0:T(8,128)(2,1)S(1)}, u32[]{:S(2)}, u32[]{:S(2)}) collective-permute-start(bf16[1,128,256]{2,1,0:T(8,128)(2,1)S(1)} %get-tuple-element.19.held_ref), channel_id=1, source_target_pairs={{0,8},{2,10},{4,12},{6,14},{8,0},{10,2},{12,4},{14,6},{1,9},{3,11}... | collective-permute-start | bytes 196616 | tf_op jit(solution)/shard_map/ppermute | solution.py:188
  11.9 0.0 collective-permute-done.1.came_ref
  11.9 1.8 %collective-permute-start.2 = (f32[64,256]{1,0:T(8,128)S(1)}, f32[64,256]{1,0:T(8,128)S(1)}, u32[]{:S(2)}, u32[]{:S(2)}) collective-permute-start(f32[64,256]{1,0:T(8,128)S(1)} %plane_sum.1.hold_ref), channel_id=1, source_target_pairs={{0,4},{2,6},{4,0},{6,2},{8,12},{10,14},{12,8},{14,10},{1,5},{3,7},... | collective-permute-start | bytes 196616 | tf_op jit(solution)/shard_map/ppermute | solution.py:188
  13.7 2.1 %collective-permute-done.7.came_ref = bf16[1,128,256]{2,1,0:T(8,128)(2,1)S(1)} collective-permute-done((bf16[1,128,256]{2,1,0:T(8,128)(2,1)S(1)}, bf16[1,128,256]{2,1,0:T(8,128)(2,1)S(1)}, u32[]{:S(2)}, u32[]{:S(2)}) %collective-permute-start.7) | collective-permute-done | bytes 65568 | tf_op jit(solution)/shard_map/ppermute | solution.py:188
  15.8 0.4 %collective-permute-start.8 = (bf16[2,128,256]{2,1,0:T(8,128)(2,1)S(1)}, bf16[2,128,256]{2,1,0:T(8,128)(2,1)S(1)}, u32[]{:S(2)}, u32[]{:S(2)}) collective-permute-start(bf16[2,128,256]{2,1,0:T(8,128)(2,1)S(1)} %join_near.1.refs_0_), channel_id=1, source_target_pairs={{0,4},{2,6},{4,0},{6,2},{8,12},{10,14},{12,8},{14,10},{1,5},{3,7},... | collective-permute-start | bytes 393224 | tf_op jit(solution)/shard_map/ppermute | solution.py:188
  16.2 0.3 collective-permute-done.2.came_ref
  16.6 3.2 %collective-permute-start.3 = (f32[64,256]{1,0:T(8,128)S(1)}, f32[64,256]{1,0:T(8,128)S(1)}, u32[]{:S(2)}, u32[]{:S(2)}) collective-permute-start(f32[64,256]{1,0:T(8,128)S(1)} %pair_sum.1.held_ref), channel_id=1, source_target_pairs={{0,8},{2,10},{4,12},{6,14},{8,0},{10,2},{12,4},{14,6},{1,9},{3,11}... | collective-permute-start | bytes 196616 | tf_op jit(solution)/shard_map/ppermute | solution.py:188
  19.7 0.8 %collective-permute-start.9 = (bf16[2,128,256]{2,1,0:T(8,128)(2,1)S(1)}, bf16[2,128,256]{2,1,0:T(8,128)(2,1)S(1)}, u32[]{:S(2)}, u32[]{:S(2)}) collective-permute-start(bf16[2,128,256]{2,1,0:T(8,128)(2,1)S(1)} %join_near.1.refs_0_), channel_id=1, source_target_pairs={{0,2},{2,0},{4,6},{6,4},{8,10},{10,8},{12,14},{14,12},{1,3},{3,1},... | collective-permute-start | bytes 393224 | tf_op jit(solution)/shard_map/ppermute | solution.py:188
  20.6 1.2 %collective-permute-done.8.refs_1_ = bf16[2,128,256]{2,1,0:T(8,128)(2,1)S(1)} collective-permute-done((bf16[2,128,256]{2,1,0:T(8,128)(2,1)S(1)}, bf16[2,128,256]{2,1,0:T(8,128)(2,1)S(1)}, u32[]{:S(2)}, u32[]{:S(2)}) %collective-permute-start.8) | collective-permute-done | bytes 131104 | tf_op jit(solution)/shard_map/ppermute | solution.py:188
  21.7 0.0 collective-permute-start.10
  21.8 0.9 %collective-permute-done.3.came_ref = f32[64,256]{1,0:T(8,128)S(1)} collective-permute-done((f32[64,256]{1,0:T(8,128)S(1)}, f32[64,256]{1,0:T(8,128)S(1)}, u32[]{:S(2)}, u32[]{:S(2)}) %collective-permute-start.3) | collective-permute-done | bytes 65568 | tf_op jit(solution)/shard_map/ppermute | solution.py:188
  22.7 0.1 collective-permute-start.6
  22.8 1.3 %collective-permute-start.5 = (bf16[64,256]{1,0:T(8,128)(2,1)S(1)}, bf16[64,256]{1,0:T(8,128)(2,1)S(1)}, u32[]{:S(2)}, u32[]{:S(2)}) collective-permute-start(bf16[64,256]{1,0:T(8,128)(2,1)S(1)} %hub_sums.1.refs_0_), channel_id=1, source_target_pairs={{0,1},{1,0},{2,3},{3,2},{4,5},{5,4},{6,7},{7,6},{8,9},{9,8},{10,11... | collective-permute-start | bytes 98312 | tf_op jit(solution)/shard_map/ppermute | solution.py:185
  24.1 0.8 %collective-permute-start.4 = (bf16[64,256]{1,0:T(8,128)(2,1)S(1)}, bf16[64,256]{1,0:T(8,128)(2,1)S(1)}, u32[]{:S(2)}, u32[]{:S(2)}) collective-permute-start(bf16[64,256]{1,0:T(8,128)(2,1)S(1)} %hub_sums.1.refs_0_), channel_id=1, source_target_pairs={{0,2},{2,0},{4,6},{6,4},{8,10},{10,8},{12,14},{14,12},{1,3},{3,1},... | collective-permute-start | bytes 98312 | tf_op jit(solution)/shard_map/ppermute | solution.py:188
  24.9 0.7 %collective-permute-done.9.refs_2_ = bf16[2,128,256]{2,1,0:T(8,128)(2,1)S(1)} collective-permute-done((bf16[2,128,256]{2,1,0:T(8,128)(2,1)S(1)}, bf16[2,128,256]{2,1,0:T(8,128)(2,1)S(1)}, u32[]{:S(2)}, u32[]{:S(2)}) %collective-permute-start.9) | collective-permute-done | bytes 131104 | tf_op jit(solution)/shard_map/ppermute | solution.py:188
  25.6 2.1 %collective-permute-done.10.refs_3_ = bf16[2,128,256]{2,1,0:T(8,128)(2,1)S(1)} collective-permute-done((bf16[2,128,256]{2,1,0:T(8,128)(2,1)S(1)}, bf16[2,128,256]{2,1,0:T(8,128)(2,1)S(1)}, u32[]{:S(2)}, u32[]{:S(2)}) %collective-permute-start.10) | collective-permute-done | bytes 131104 | tf_op jit(solution)/shard_map/ppermute | solution.py:188
  27.7 0.7 %score_columns.1 = (f32[256,256]{1,0:T(8,128)S(1)}, f32[256,256]{1,0:T(8,128)S(1)}) custom-call(bf16[2,128,256]{2,1,0:T(8,128)(2,1)S(1)} %join_near.1.refs_0_, bf16[2,128,256]{2,1,0:T(8,128)(2,1)S(1)} %collective-permute-done.8.refs_1_, bf16[2,128,256]{2,1,0:T(8,128)(2,1)S(1)} %collective-permute-done.9.refs_2_, ...), custom_call_target="tpu_custom_call" | custom-call | tf_op jit(solution)/shard_map/score_columns/pallas_call | solution.py:198
  28.4 0.0 collective-permute-done.6.refs_3_
  28.4 0.0 collective-permute-done.5.refs_2_
  28.4 0.0 collective-permute-done.4.refs_1_
  28.5 0.3 hub_columns.1
  28.8 0.1 collective-permute-start.11
  28.9 1.5 %collective-permute-done.11.came_ref = f32[256,256]{1,0:T(8,128)S(1)} collective-permute-done((f32[256,256]{1,0:T(8,128)S(1)}, f32[256,256]{1,0:T(8,128)S(1)}, u32[]{:S(2)}, u32[]{:S(2)}) %collective-permute-start.11) | collective-permute-done | bytes 262176 | tf_op jit(solution)/shard_map/ppermute | solution.py:185
  30.4 11.8 %all_to_all.5.parts_ref = f32[8,16,256]{2,1,0:T(8,128)S(1)} all-to-all(f32[8,16,256]{2,1,0:T(8,128)S(1)} %hub_pieces.1), channel_id=1, replica_groups=mesh['groups'=2,'row'=8,'col'=2] {'row'}, dimensions={0} | all-to-all | bytes 262144 | tf_op jit(solution)/shard_map/all_to_all | solution.py:264
  42.3 0.7 %last_sums.1 = (f32[128,256]{1,0:T(8,128)}, f32[16,256]{1,0:T(8,128)}) custom-call(s32[1,256]{1,0:T(1,128)S(1)} %bitcast.10, f32[256,256]{1,0:T(8,128)S(1)} %get-tuple-element.22.keep_ref, f32[256,256]{1,0:T(8,128)S(1)} %collective-permute-done.11.came_ref, f32[8,16,256]{2,1,0:T(8,128)S(1)} %all_to_all.5.parts_ref), custom_call_target="tpu_custom_call" | custom-call | tf_op jit(solution)/shard_map/last_sums/pallas_call | solution.py:198
  (6 shorter events, 0.1 us)
Async XLA Ops:
  0.6 5.7 %copy-start = (s32[256]{0:T(256)S(1)}, s32[256]{0:T(256)}, u32[]{:S(2)}) copy-start(s32[256]{0:T(256)} %param.9) | copy-start | bytes 3076
  4.6 1.7 %collective-permute-start = (f32[256,256]{1,0:T(8,128)S(1)}, f32[256,256]{1,0:T(8,128)S(1)}, u32[]{:S(2)}, u32[]{:S(2)}) collective-permute-start(f32[256,256]{1,0:T(8,128)S(1)} %get-tuple-element.15), channel_id=1, source_target_pairs={{0,1},{1,0},{2,3},{3,2},{4,5},{5,4},{6,7},{7,6},{8,9},{9,8},{10,11... | collective-permute-start | bytes 786440 | tf_op jit(solution)/shard_map/ppermute | solution.py:185
  6.3 5.5 %collective-permute-start.1 = (f32[64,256]{1,0:T(8,128)S(1)}, f32[64,256]{1,0:T(8,128)S(1)}, u32[]{:S(2)}, u32[]{:S(2)}) collective-permute-start(f32[64,256]{1,0:T(8,128)S(1)} %get-tuple-element.17), channel_id=1, source_target_pairs={{0,2},{2,0},{4,6},{6,4},{8,10},{10,8},{12,14},{14,12},{1,3},{3,1},... | collective-permute-start | bytes 196616 | tf_op jit(solution)/shard_map/ppermute | solution.py:188
  9.3 6.5 %collective-permute-start.7 = (bf16[1,128,256]{2,1,0:T(8,128)(2,1)S(1)}, bf16[1,128,256]{2,1,0:T(8,128)(2,1)S(1)}, u32[]{:S(2)}, u32[]{:S(2)}) collective-permute-start(bf16[1,128,256]{2,1,0:T(8,128)(2,1)S(1)} %get-tuple-element.19.held_ref), channel_id=1, source_target_pairs={{0,8},{2,10},{4,12},{6,14},{8,0},{10,2},{12,4},{14,6},{1,9},{3,11}... | collective-permute-start | bytes 196616 | tf_op jit(solution)/shard_map/ppermute | solution.py:188
  11.9 4.7 %collective-permute-start.2 = (f32[64,256]{1,0:T(8,128)S(1)}, f32[64,256]{1,0:T(8,128)S(1)}, u32[]{:S(2)}, u32[]{:S(2)}) collective-permute-start(f32[64,256]{1,0:T(8,128)S(1)} %plane_sum.1.hold_ref), channel_id=1, source_target_pairs={{0,4},{2,6},{4,0},{6,2},{8,12},{10,14},{12,8},{14,10},{1,5},{3,7},... | collective-permute-start | bytes 196616 | tf_op jit(solution)/shard_map/ppermute | solution.py:188
  15.8 6.0 %collective-permute-start.8 = (bf16[2,128,256]{2,1,0:T(8,128)(2,1)S(1)}, bf16[2,128,256]{2,1,0:T(8,128)(2,1)S(1)}, u32[]{:S(2)}, u32[]{:S(2)}) collective-permute-start(bf16[2,128,256]{2,1,0:T(8,128)(2,1)S(1)} %join_near.1.refs_0_), channel_id=1, source_target_pairs={{0,4},{2,6},{4,0},{6,2},{8,12},{10,14},{12,8},{14,10},{1,5},{3,7},... | collective-permute-start | bytes 393224 | tf_op jit(solution)/shard_map/ppermute | solution.py:188
  16.6 6.1 %collective-permute-start.3 = (f32[64,256]{1,0:T(8,128)S(1)}, f32[64,256]{1,0:T(8,128)S(1)}, u32[]{:S(2)}, u32[]{:S(2)}) collective-permute-start(f32[64,256]{1,0:T(8,128)S(1)} %pair_sum.1.held_ref), channel_id=1, source_target_pairs={{0,8},{2,10},{4,12},{6,14},{8,0},{10,2},{12,4},{14,6},{1,9},{3,11}... | collective-permute-start | bytes 196616 | tf_op jit(solution)/shard_map/ppermute | solution.py:188
  19.7 5.9 %collective-permute-start.9 = (bf16[2,128,256]{2,1,0:T(8,128)(2,1)S(1)}, bf16[2,128,256]{2,1,0:T(8,128)(2,1)S(1)}, u32[]{:S(2)}, u32[]{:S(2)}) collective-permute-start(bf16[2,128,256]{2,1,0:T(8,128)(2,1)S(1)} %join_near.1.refs_0_), channel_id=1, source_target_pairs={{0,2},{2,0},{4,6},{6,4},{8,10},{10,8},{12,14},{14,12},{1,3},{3,1},... | collective-permute-start | bytes 393224 | tf_op jit(solution)/shard_map/ppermute | solution.py:188
  21.7 5.9 %collective-permute-start.10 = (bf16[2,128,256]{2,1,0:T(8,128)(2,1)S(1)}, bf16[2,128,256]{2,1,0:T(8,128)(2,1)S(1)}, u32[]{:S(2)}, u32[]{:S(2)}) collective-permute-start(bf16[2,128,256]{2,1,0:T(8,128)(2,1)S(1)} %collective-permute-done.8.refs_1_), channel_id=1, source_target_pairs={{0,2},{2,0},{4,6},{6,4},{8,10},{10,8},{12,14},{14,12},{1,3},{3,1},... | collective-permute-start | bytes 393224 | tf_op jit(solution)/shard_map/ppermute | solution.py:188
  22.7 5.7 %collective-permute-start.6 = (bf16[64,256]{1,0:T(8,128)(2,1)S(1)}, bf16[64,256]{1,0:T(8,128)(2,1)S(1)}, u32[]{:S(2)}, u32[]{:S(2)}) collective-permute-start(bf16[64,256]{1,0:T(8,128)(2,1)S(1)} %hub_sums.1.refs_0_), channel_id=1, source_target_pairs={{0,3},{1,2},{2,1},{3,0},{4,7},{5,6},{6,5},{7,4},{8,11},{9,10},{10,... | collective-permute-start | bytes 98312 | tf_op jit(solution)/shard_map/ppermute | solution.py:195
  22.8 5.7 %collective-permute-start.5 = (bf16[64,256]{1,0:T(8,128)(2,1)S(1)}, bf16[64,256]{1,0:T(8,128)(2,1)S(1)}, u32[]{:S(2)}, u32[]{:S(2)}) collective-permute-start(bf16[64,256]{1,0:T(8,128)(2,1)S(1)} %hub_sums.1.refs_0_), channel_id=1, source_target_pairs={{0,1},{1,0},{2,3},{3,2},{4,5},{5,4},{6,7},{7,6},{8,9},{9,8},{10,11... | collective-permute-start | bytes 98312 | tf_op jit(solution)/shard_map/ppermute | solution.py:185
  24.1 4.4 %collective-permute-start.4 = (bf16[64,256]{1,0:T(8,128)(2,1)S(1)}, bf16[64,256]{1,0:T(8,128)(2,1)S(1)}, u32[]{:S(2)}, u32[]{:S(2)}) collective-permute-start(bf16[64,256]{1,0:T(8,128)(2,1)S(1)} %hub_sums.1.refs_0_), channel_id=1, source_target_pairs={{0,2},{2,0},{4,6},{6,4},{8,10},{10,8},{12,14},{14,12},{1,3},{3,1},... | collective-permute-start | bytes 98312 | tf_op jit(solution)/shard_map/ppermute | solution.py:188
  28.8 1.6 %collective-permute-start.11 = (f32[256,256]{1,0:T(8,128)S(1)}, f32[256,256]{1,0:T(8,128)S(1)}, u32[]{:S(2)}, u32[]{:S(2)}) collective-permute-start(f32[256,256]{1,0:T(8,128)S(1)} %get-tuple-element.23), channel_id=1, source_target_pairs={{0,1},{1,0},{2,3},{3,2},{4,5},{5,4},{6,7},{7,6},{8,9},{9,8},{10,11... | collective-permute-start | bytes 786440 | tf_op jit(solution)/shard_map/ppermute | solution.py:185

commit v24 on v23

--- a/solution.py
+++ b/solution.py
@@ -85,15 +85,13 @@
         out[...] = product(dense_ref[at:at + 2 * half], panel[...])
 
 
-def score_columns_kernel(dims, flips, *refs):
+def score_columns_kernel(dims, *refs):
     n_row, n_col, side = dims
-    n_z = n_row // X
     blocks, (dense_ref, send_ref, keep_ref, panel) = refs[:4], refs[4:]
     r = lax.axis_index("row")
-    near, far = flips[:n_z // 2], flips[n_z // 2:]
-    for ref, group, x in ((blocks[0], near, 0), (blocks[1], far, 0), (blocks[2], near, 1), (blocks[3], far, 1)):
-        for k, flip in enumerate(group):
-            owner = r ^ (X * flip + x)
+    for ref, flip in zip(blocks, (0, 2 * X, 1, 2 * X + 1)):
+        for k in range(2):
+            owner = r ^ (flip + X * k)
             panel[pl.ds(pl.multiple_of(owner * VB, VB), VB), :] = ref[k]
     n_rows = dense_ref.shape[0] // 2
     keep_ref[...] = product(dense_ref[:n_rows, :n_row * VB], panel[...])
@@ -230,9 +228,6 @@
         name="first_terms",
     )(*in_hbm[:3], tile_count.reshape(1), in_hbm[3])
 
-    masks = [n_row // X // 2]
-    while masks[-1] > 1:
-        masks.append(masks[-1] // 2)
     for step in range(ITERS - 1):
         came = other_core(send)
         held, hold, away = call(
@@ -240,22 +235,18 @@
             (bf16((1, VB, width)), f32((quarter, width)), f32((quarter, width))),
             src, keep, came, cost=2)
         away = other_side(away)
-        flips = [0]
-        for mask in masks[:-1]:
-            far = to_partner(held, X * mask)
-            held = call(join_kernel, "join_near", bf16((2 * len(flips), VB, width)), held, far, cost=3)
-            flips += [flip ^ mask for flip in flips]
-        far = to_partner(held, X * masks[-1])
-        flips += [flip ^ masks[-1] for flip in flips]
-        near_across, far_across = other_side(held), other_side(far)
+        pair = bf16((2, VB, width))
+        next_z, far_z = to_partner(held, X), to_partner(held, 2 * X)
+        near = call(join_kernel, "join_near", pair, held, next_z, cost=1)
+        far = call(join_kernel, "join_far", pair, far_z, to_partner(far_z, X), cost=2)
+        near_across, far_across = other_side(near), other_side(far)
         sums = call(add_kernel, "plane_sum", f32((quarter, width)), hold, away, cost=20)
-        for mask in masks[:0:-1]:
-            sums = call(add_kernel, "pair_sum", f32((quarter, width)), sums, to_partner(sums, X * mask), cost=1)
-        mine = call(bind(hub_kernel, dims), "hub_sums", bf16((quarter, width)), src, sums, to_partner(sums, X * masks[0]), cost=1)
+        sums = call(add_kernel, "pair_sum", f32((quarter, width)), sums, to_partner(sums, X), cost=2)
+        mine = call(bind(hub_kernel, dims), "hub_sums", bf16((quarter, width)), src, sums, to_partner(sums, 2 * X), cost=8)
         quarters = [mine, other_side(mine), other_core(mine), other_both(mine)]
         send, keep = call(
-            bind(score_columns_kernel, dims, flips), "score_columns", (f32((half, width)),) * 2,
-            held, far, near_across, far_across, dense, scratch=[pltpu.VMEM((n_row * VB, width), jnp.bfloat16)])
+            bind(score_columns_kernel, dims), "score_columns", (f32((half, width)),) * 2,
+            near, far, near_across, far_across, dense, scratch=[pltpu.VMEM((n_row * VB, width), jnp.bfloat16)])
         send, keep = call(
             bind(hub_columns_kernel, dims), "hub_columns", (f32((half, width)),) * 2,
             *quarters, dense, send, keep, scratch=[pltpu.VMEM((H, width), jnp.bfloat16)])
@@ -350,7 +341,7 @@
         n_row, n_col = mesh.shape["row"], mesh.shape["col"]
         slots, side = tiles.shape[2:4]
         blocks = (n_col * VB + H) * (n_row * VB + H) // (side * side)
-        if n_col == 2 and n_row in (8, 16) and blocks <= slots and H // (n_row * n_col) % 16 == 0:
+        if n_col == 2 and n_row == 4 * X and blocks <= slots and H // (n_row * n_col) % 16 == 0:
             return fast_body(tiles, *rest)
         return plain_body(tiles, *rest)
 

time: 43.2 us -> 43.2 us (level)
  blocking collectives: 11.8 us -> 9.96 us
  waiting for transfers between devices: 9.92 us -> 11.1 us
  starting transfers between devices: 14.6 us -> 15.4 us
    all_to_all x1, blocking collectives: 11.8 us -> 9.96 us  [fast_body(): parts = lax.all_to_all(parts, 'row', 0, 0)]
    ppermute x1, waiting for transfers between devices: 0.01 us -> 0.74 us  [other_both(): lax.ppermute(x, ('row', 'col'), [(r * n_col + c, (r ^ 1) * n_col + 1 - c)...]
    ppermute x8 -> x9, starting transfers between devices: 12.6 us -> 13.2 us  [to_partner(): return lax.ppermute(x, 'row', [(r, r ^ flip) for r in range(n_row)])]
    ppermute x8 -> x9, waiting for transfers between devices: 7.23 us -> 7.64 us  [to_partner(): return lax.ppermute(x, 'row', [(r, r ^ flip) for r in range(n_row)])]
    pallas_call x9 -> x10, Pallas kernels: 1.89 us -> 1.9 us  [call(): pl.pallas_call(kernel, out_shape=out_shape, in_specs=[VMEM] * len(args),...]
  transfers between devices with their start and end apart: 12 -> 13, of which waited for: 8 -> 7; matrix products, arithmetic and copies ran while one was open for 0% -> 0% of each run, Pallas kernels for 2% -> 2%
where the time goes in v24:
time: 43.2 us; the launch traced here: 43 us
  starting transfers between devices  15.4 us (36%)
  waiting for transfers between devices  11.1 us (26%)
  blocking collectives  9.96 us (23%)
  Pallas kernels  5.2 us (12%)
  between operations  1.38 us (3%)
    ppermute x9, starting transfers between devices, to_partner(): return lax.ppermute(x, 'row', [(r, r ^ flip) for r in range(n_row)])  13.2 us
    all_to_all x1, blocking collectives, fast_body(): parts = lax.all_to_all(parts, 'row', 0, 0)  9.96 us
    ppermute x9, waiting for transfers between devices, to_partner(): return lax.ppermute(x, 'row', [(r, r ^ flip) for r in range(n_row)])  7.64 us
    pallas_call x1, Pallas kernels, fast_body(): pl.pallas_call(bind(first_kernel, dims), out_shape=(f32((half, width)), f...  3.3 us
    ppermute x3, waiting for transfers between devices, other_core(): return lax.ppermute(x, 'col', [(0, 1), (1, 0)])  2.69 us
    ppermute x3, starting transfers between devices, other_core(): return lax.ppermute(x, 'col', [(0, 1), (1, 0)])  2.18 us
    pallas_call x10, Pallas kernels, call(): pl.pallas_call(kernel, out_shape=out_shape, in_specs=[VMEM] * len(args),...  1.9 us
  transfers between devices with their start and end apart: 13, of which 7 were waited for; matrix products, arithmetic and copies ran while one was open for 0% of the time, Pallas kernels for 2%

profile of v24, /device:TPU:0, one launch (start us, length us, event | category | flops | bytes accessed | tf_op | source)
XLA Modules:
  0.0 43.0 jit_solution(8217531936338012332)
XLA Ops:
  0.6 0.0 copy-start
  1.3 3.3 %first_terms.1 = (f32[256,256]{1,0:T(8,128)S(1)}, f32[256,256]{1,0:T(8,128)S(1)}, bf16[1024,1280]{1,0:T(8,128)(2,1)S(1)}) custom-call(bf16[96,128,128]{2,1,0:T(8,128)(2,1)} %bitcast.11, s32[96]{0:T(128)} %bitcast.12, s32[96]{0:T(128)} %bitcast.13, s32[1]{0:T(128)} %bitcast.6.count_hbm, s32[1,256]{1,0:T(1,128)} %bitcast.7), custom_call_target="tpu_custom_call" | custom-call | tf_op jit(solution)/shard_map/first_terms/pallas_call | solution.py:211
  4.6 0.5 %collective-permute-start = (f32[256,256]{1,0:T(8,128)S(1)}, f32[256,256]{1,0:T(8,128)S(1)}, u32[]{:S(2)}, u32[]{:S(2)}) collective-permute-start(f32[256,256]{1,0:T(8,128)S(1)} %get-tuple-element.15), channel_id=1, source_target_pairs={{0,1},{1,0},{2,3},{3,2},{4,5},{5,4},{6,7},{7,6},{8,9},{9,8},{10,11... | collective-permute-start | bytes 786440 | tf_op jit(solution)/shard_map/ppermute | solution.py:183
  5.1 1.2 %collective-permute-done.came_ref = f32[256,256]{1,0:T(8,128)S(1)} collective-permute-done((f32[256,256]{1,0:T(8,128)S(1)}, f32[256,256]{1,0:T(8,128)S(1)}, u32[]{:S(2)}, u32[]{:S(2)}) %collective-permute-start) | collective-permute-done | bytes 262176 | tf_op jit(solution)/shard_map/ppermute | solution.py:183
  6.3 0.0 copy-done
  6.3 0.1 spread.1
  6.4 2.9 %collective-permute-start.1 = (f32[64,256]{1,0:T(8,128)S(1)}, f32[64,256]{1,0:T(8,128)S(1)}, u32[]{:S(2)}, u32[]{:S(2)}) collective-permute-start(f32[64,256]{1,0:T(8,128)S(1)} %get-tuple-element.17), channel_id=1, source_target_pairs={{0,2},{2,0},{4,6},{6,4},{8,10},{10,8},{12,14},{14,12},{1,3},{3,1},... | collective-permute-start | bytes 196616 | tf_op jit(solution)/shard_map/ppermute | solution.py:186
  9.3 2.6 %collective-permute-start.8 = (bf16[1,128,256]{2,1,0:T(8,128)(2,1)S(1)}, bf16[1,128,256]{2,1,0:T(8,128)(2,1)S(1)}, u32[]{:S(2)}, u32[]{:S(2)}) collective-permute-start(bf16[1,128,256]{2,1,0:T(8,128)(2,1)S(1)} %get-tuple-element.19.held_ref), channel_id=1, source_target_pairs={{0,8},{2,10},{4,12},{6,14},{8,0},{10,2},{12,4},{14,6},{1,9},{3,11}... | collective-permute-start | bytes 196616 | tf_op jit(solution)/shard_map/ppermute | solution.py:186
  11.9 1.6 %collective-permute-start.7 = (bf16[1,128,256]{2,1,0:T(8,128)(2,1)S(1)}, bf16[1,128,256]{2,1,0:T(8,128)(2,1)S(1)}, u32[]{:S(2)}, u32[]{:S(2)}) collective-permute-start(bf16[1,128,256]{2,1,0:T(8,128)(2,1)S(1)} %get-tuple-element.19.held_ref), channel_id=1, source_target_pairs={{0,4},{2,6},{4,0},{6,2},{8,12},{10,14},{12,8},{14,10},{1,5},{3,7},... | collective-permute-start | bytes 196616 | tf_op jit(solution)/shard_map/ppermute | solution.py:186
  13.4 0.0 collective-permute-done.1.came_ref
  13.5 0.5 %collective-permute-start.2 = (f32[64,256]{1,0:T(8,128)S(1)}, f32[64,256]{1,0:T(8,128)S(1)}, u32[]{:S(2)}, u32[]{:S(2)}) collective-permute-start(f32[64,256]{1,0:T(8,128)S(1)} %plane_sum.1.hold_ref), channel_id=1, source_target_pairs={{0,4},{2,6},{4,0},{6,2},{8,12},{10,14},{12,8},{14,10},{1,5},{3,7},... | collective-permute-start | bytes 196616 | tf_op jit(solution)/shard_map/ppermute | solution.py:186
  14.0 2.8 %collective-permute-done.7.came_ref = bf16[1,128,256]{2,1,0:T(8,128)(2,1)S(1)} collective-permute-done((bf16[1,128,256]{2,1,0:T(8,128)(2,1)S(1)}, bf16[1,128,256]{2,1,0:T(8,128)(2,1)S(1)}, u32[]{:S(2)}, u32[]{:S(2)}) %collective-permute-start.7) | collective-permute-done | bytes 65568 | tf_op jit(solution)/shard_map/ppermute | solution.py:186
  16.8 0.6 %collective-permute-start.10 = (bf16[2,128,256]{2,1,0:T(8,128)(2,1)S(1)}, bf16[2,128,256]{2,1,0:T(8,128)(2,1)S(1)}, u32[]{:S(2)}, u32[]{:S(2)}) collective-permute-start(bf16[2,128,256]{2,1,0:T(8,128)(2,1)S(1)} %join_near.1.refs_0_), channel_id=1, source_target_pairs={{0,2},{2,0},{4,6},{6,4},{8,10},{10,8},{12,14},{14,12},{1,3},{3,1},... | collective-permute-start | bytes 393224 | tf_op jit(solution)/shard_map/ppermute | solution.py:186
  17.4 0.0 collective-permute-done.8.held_ref
  17.4 1.4 %collective-permute-start.9 = (bf16[1,128,256]{2,1,0:T(8,128)(2,1)S(1)}, bf16[1,128,256]{2,1,0:T(8,128)(2,1)S(1)}, u32[]{:S(2)}, u32[]{:S(2)}) collective-permute-start(bf16[1,128,256]{2,1,0:T(8,128)(2,1)S(1)} %collective-permute-done.8.held_ref), channel_id=1, source_target_pairs={{0,4},{2,6},{4,0},{6,2},{8,12},{10,14},{12,8},{14,10},{1,5},{3,7},... | collective-permute-start | bytes 196616 | tf_op jit(solution)/shard_map/ppermute | solution.py:186
  18.9 0.0 collective-permute-done.2.came_ref
  18.9 1.3 %collective-permute-start.3 = (f32[64,256]{1,0:T(8,128)S(1)}, f32[64,256]{1,0:T(8,128)S(1)}, u32[]{:S(2)}, u32[]{:S(2)}) collective-permute-start(f32[64,256]{1,0:T(8,128)S(1)} %pair_sum.1.held_ref), channel_id=1, source_target_pairs={{0,8},{2,10},{4,12},{6,14},{8,0},{10,2},{12,4},{14,6},{1,9},{3,11}... | collective-permute-start | bytes 196616 | tf_op jit(solution)/shard_map/ppermute | solution.py:186
  20.2 1.7 %collective-permute-done.9.came_ref = bf16[1,128,256]{2,1,0:T(8,128)(2,1)S(1)} collective-permute-done((bf16[1,128,256]{2,1,0:T(8,128)(2,1)S(1)}, bf16[1,128,256]{2,1,0:T(8,128)(2,1)S(1)}, u32[]{:S(2)}, u32[]{:S(2)}) %collective-permute-start.9) | collective-permute-done | bytes 65568 | tf_op jit(solution)/shard_map/ppermute | solution.py:186
  21.9 1.7 %collective-permute-start.11 = (bf16[2,128,256]{2,1,0:T(8,128)(2,1)S(1)}, bf16[2,128,256]{2,1,0:T(8,128)(2,1)S(1)}, u32[]{:S(2)}, u32[]{:S(2)}) collective-permute-start(bf16[2,128,256]{2,1,0:T(8,128)(2,1)S(1)} %join_far.1.refs_1_), channel_id=1, source_target_pairs={{0,2},{2,0},{4,6},{6,4},{8,10},{10,8},{12,14},{14,12},{1,3},{3,1},... | collective-permute-start | bytes 393224 | tf_op jit(solution)/shard_map/ppermute | solution.py:186
  23.6 1.2 %collective-permute-done.3.came_ref = f32[64,256]{1,0:T(8,128)S(1)} collective-permute-done((f32[64,256]{1,0:T(8,128)S(1)}, f32[64,256]{1,0:T(8,128)S(1)}, u32[]{:S(2)}, u32[]{:S(2)}) %collective-permute-start.3) | collective-permute-done | bytes 65568 | tf_op jit(solution)/shard_map/ppermute | solution.py:186
  24.8 0.1 collective-permute-start.6
  24.9 1.6 %collective-permute-start.5 = (bf16[64,256]{1,0:T(8,128)(2,1)S(1)}, bf16[64,256]{1,0:T(8,128)(2,1)S(1)}, u32[]{:S(2)}, u32[]{:S(2)}) collective-permute-start(bf16[64,256]{1,0:T(8,128)(2,1)S(1)} %hub_sums.1.refs_0_), channel_id=1, source_target_pairs={{0,1},{1,0},{2,3},{3,2},{4,5},{5,4},{6,7},{7,6},{8,9},{9,8},{10,11... | collective-permute-start | bytes 98312 | tf_op jit(solution)/shard_map/ppermute | solution.py:183
  26.5 0.5 %collective-permute-start.4 = (bf16[64,256]{1,0:T(8,128)(2,1)S(1)}, bf16[64,256]{1,0:T(8,128)(2,1)S(1)}, u32[]{:S(2)}, u32[]{:S(2)}) collective-permute-start(bf16[64,256]{1,0:T(8,128)(2,1)S(1)} %hub_sums.1.refs_0_), channel_id=1, source_target_pairs={{0,2},{2,0},{4,6},{6,4},{8,10},{10,8},{12,14},{14,12},{1,3},{3,1},... | collective-permute-start | bytes 98312 | tf_op jit(solution)/shard_map/ppermute | solution.py:186
  27.1 0.0 collective-permute-done.10.refs_2_
  27.1 0.0 collective-permute-done.11.refs_3_
  27.1 0.7 %score_columns.1 = (f32[256,256]{1,0:T(8,128)S(1)}, f32[256,256]{1,0:T(8,128)S(1)}) custom-call(bf16[2,128,256]{2,1,0:T(8,128)(2,1)S(1)} %join_near.1.refs_0_, bf16[2,128,256]{2,1,0:T(8,128)(2,1)S(1)} %join_far.1.refs_1_, bf16[2,128,256]{2,1,0:T(8,128)(2,1)S(1)} %collective-permute-done.10.refs_2_, bf16[2,128,256]{2,1,0:T(8,128)(2,1)S(1)} %collective-permute-done.11.refs_3_, ...), custom_call_target="tpu_custom_call" | custom-call | tf_op jit(solution)/shard_map/score_columns/pallas_call | solution.py:196
  27.8 0.7 %collective-permute-done.6.refs_3_ = bf16[64,256]{1,0:T(8,128)(2,1)S(1)} collective-permute-done((bf16[64,256]{1,0:T(8,128)(2,1)S(1)}, bf16[64,256]{1,0:T(8,128)(2,1)S(1)}, u32[]{:S(2)}, u32[]{:S(2)}) %collective-permute-start.6) | collective-permute-done | bytes 32800 | tf_op jit(solution)/shard_map/ppermute | solution.py:193
  28.6 0.0 collective-permute-done.5.refs_2_
  28.6 1.9 %collective-permute-done.4.refs_1_ = bf16[64,256]{1,0:T(8,128)(2,1)S(1)} collective-permute-done((bf16[64,256]{1,0:T(8,128)(2,1)S(1)}, bf16[64,256]{1,0:T(8,128)(2,1)S(1)}, u32[]{:S(2)}, u32[]{:S(2)}) %collective-permute-start.4) | collective-permute-done | bytes 32800 | tf_op jit(solution)/shard_map/ppermute | solution.py:186
  30.4 0.3 hub_columns.1
  30.8 0.1 collective-permute-start.12
  30.8 1.5 %collective-permute-done.12.came_ref = f32[256,256]{1,0:T(8,128)S(1)} collective-permute-done((f32[256,256]{1,0:T(8,128)S(1)}, f32[256,256]{1,0:T(8,128)S(1)}, u32[]{:S(2)}, u32[]{:S(2)}) %collective-permute-start.12) | collective-permute-done | bytes 262176 | tf_op jit(solution)/shard_map/ppermute | solution.py:183
  32.4 10.0 %all_to_all.5.parts_ref = f32[8,16,256]{2,1,0:T(8,128)S(1)} all-to-all(f32[8,16,256]{2,1,0:T(8,128)S(1)} %hub_pieces.1), channel_id=1, replica_groups=mesh['groups'=2,'row'=8,'col'=2] {'row'}, dimensions={0} | all-to-all | bytes 262144 | tf_op jit(solution)/shard_map/all_to_all | solution.py:255
  42.3 0.7 %last_sums.1 = (f32[128,256]{1,0:T(8,128)}, f32[16,256]{1,0:T(8,128)}) custom-call(s32[1,256]{1,0:T(1,128)S(1)} %bitcast.10, f32[256,256]{1,0:T(8,128)S(1)} %get-tuple-element.22.keep_ref, f32[256,256]{1,0:T(8,128)S(1)} %collective-permute-done.12.came_ref, f32[8,16,256]{2,1,0:T(8,128)S(1)} %all_to_all.5.parts_ref), custom_call_target="tpu_custom_call" | custom-call | tf_op jit(solution)/shard_map/last_sums/pallas_call | solution.py:196
  (6 shorter events, 0.1 us)
Async XLA Ops:
  0.6 5.7 %copy-start = (s32[256]{0:T(256)S(1)}, s32[256]{0:T(256)}, u32[]{:S(2)}) copy-start(s32[256]{0:T(256)} %param.9) | copy-start | bytes 3076
  4.6 1.7 %collective-permute-start = (f32[256,256]{1,0:T(8,128)S(1)}, f32[256,256]{1,0:T(8,128)S(1)}, u32[]{:S(2)}, u32[]{:S(2)}) collective-permute-start(f32[256,256]{1,0:T(8,128)S(1)} %get-tuple-element.15), channel_id=1, source_target_pairs={{0,1},{1,0},{2,3},{3,2},{4,5},{5,4},{6,7},{7,6},{8,9},{9,8},{10,11... | collective-permute-start | bytes 786440 | tf_op jit(solution)/shard_map/ppermute | solution.py:183
  6.4 7.1 %collective-permute-start.1 = (f32[64,256]{1,0:T(8,128)S(1)}, f32[64,256]{1,0:T(8,128)S(1)}, u32[]{:S(2)}, u32[]{:S(2)}) collective-permute-start(f32[64,256]{1,0:T(8,128)S(1)} %get-tuple-element.17), channel_id=1, source_target_pairs={{0,2},{2,0},{4,6},{6,4},{8,10},{10,8},{12,14},{14,12},{1,3},{3,1},... | collective-permute-start | bytes 196616 | tf_op jit(solution)/shard_map/ppermute | solution.py:186
  9.3 8.2 %collective-permute-start.8 = (bf16[1,128,256]{2,1,0:T(8,128)(2,1)S(1)}, bf16[1,128,256]{2,1,0:T(8,128)(2,1)S(1)}, u32[]{:S(2)}, u32[]{:S(2)}) collective-permute-start(bf16[1,128,256]{2,1,0:T(8,128)(2,1)S(1)} %get-tuple-element.19.held_ref), channel_id=1, source_target_pairs={{0,8},{2,10},{4,12},{6,14},{8,0},{10,2},{12,4},{14,6},{1,9},{3,11}... | collective-permute-start | bytes 196616 | tf_op jit(solution)/shard_map/ppermute | solution.py:186
  11.9 5.0 %collective-permute-start.7 = (bf16[1,128,256]{2,1,0:T(8,128)(2,1)S(1)}, bf16[1,128,256]{2,1,0:T(8,128)(2,1)S(1)}, u32[]{:S(2)}, u32[]{:S(2)}) collective-permute-start(bf16[1,128,256]{2,1,0:T(8,128)(2,1)S(1)} %get-tuple-element.19.held_ref), channel_id=1, source_target_pairs={{0,4},{2,6},{4,0},{6,2},{8,12},{10,14},{12,8},{14,10},{1,5},{3,7},... | collective-permute-start | bytes 196616 | tf_op jit(solution)/shard_map/ppermute | solution.py:186
  13.5 5.4 %collective-permute-start.2 = (f32[64,256]{1,0:T(8,128)S(1)}, f32[64,256]{1,0:T(8,128)S(1)}, u32[]{:S(2)}, u32[]{:S(2)}) collective-permute-start(f32[64,256]{1,0:T(8,128)S(1)} %plane_sum.1.hold_ref), channel_id=1, source_target_pairs={{0,4},{2,6},{4,0},{6,2},{8,12},{10,14},{12,8},{14,10},{1,5},{3,7},... | collective-permute-start | bytes 196616 | tf_op jit(solution)/shard_map/ppermute | solution.py:186
  16.8 10.2 %collective-permute-start.10 = (bf16[2,128,256]{2,1,0:T(8,128)(2,1)S(1)}, bf16[2,128,256]{2,1,0:T(8,128)(2,1)S(1)}, u32[]{:S(2)}, u32[]{:S(2)}) collective-permute-start(bf16[2,128,256]{2,1,0:T(8,128)(2,1)S(1)} %join_near.1.refs_0_), channel_id=1, source_target_pairs={{0,2},{2,0},{4,6},{6,4},{8,10},{10,8},{12,14},{14,12},{1,3},{3,1},... | collective-permute-start | bytes 393224 | tf_op jit(solution)/shard_map/ppermute | solution.py:186
  17.4 4.5 %collective-permute-start.9 = (bf16[1,128,256]{2,1,0:T(8,128)(2,1)S(1)}, bf16[1,128,256]{2,1,0:T(8,128)(2,1)S(1)}, u32[]{:S(2)}, u32[]{:S(2)}) collective-permute-start(bf16[1,128,256]{2,1,0:T(8,128)(2,1)S(1)} %collective-permute-done.8.held_ref), channel_id=1, source_target_pairs={{0,4},{2,6},{4,0},{6,2},{8,12},{10,14},{12,8},{14,10},{1,5},{3,7},... | collective-permute-start | bytes 196616 | tf_op jit(solution)/shard_map/ppermute | solution.py:186
  18.9 5.9 %collective-permute-start.3 = (f32[64,256]{1,0:T(8,128)S(1)}, f32[64,256]{1,0:T(8,128)S(1)}, u32[]{:S(2)}, u32[]{:S(2)}) collective-permute-start(f32[64,256]{1,0:T(8,128)S(1)} %pair_sum.1.held_ref), channel_id=1, source_target_pairs={{0,8},{2,10},{4,12},{6,14},{8,0},{10,2},{12,4},{14,6},{1,9},{3,11}... | collective-permute-start | bytes 196616 | tf_op jit(solution)/shard_map/ppermute | solution.py:186
  21.9 5.1 %collective-permute-start.11 = (bf16[2,128,256]{2,1,0:T(8,128)(2,1)S(1)}, bf16[2,128,256]{2,1,0:T(8,128)(2,1)S(1)}, u32[]{:S(2)}, u32[]{:S(2)}) collective-permute-start(bf16[2,128,256]{2,1,0:T(8,128)(2,1)S(1)} %join_far.1.refs_1_), channel_id=1, source_target_pairs={{0,2},{2,0},{4,6},{6,4},{8,10},{10,8},{12,14},{14,12},{1,3},{3,1},... | collective-permute-start | bytes 393224 | tf_op jit(solution)/shard_map/ppermute | solution.py:186
  24.8 3.7 %collective-permute-start.6 = (bf16[64,256]{1,0:T(8,128)(2,1)S(1)}, bf16[64,256]{1,0:T(8,128)(2,1)S(1)}, u32[]{:S(2)}, u32[]{:S(2)}) collective-permute-start(bf16[64,256]{1,0:T(8,128)(2,1)S(1)} %hub_sums.1.refs_0_), channel_id=1, source_target_pairs={{0,3},{1,2},{2,1},{3,0},{4,7},{5,6},{6,5},{7,4},{8,11},{9,10},{10,... | collective-permute-start | bytes 98312 | tf_op jit(solution)/shard_map/ppermute | solution.py:193
  24.9 3.6 %collective-permute-start.5 = (bf16[64,256]{1,0:T(8,128)(2,1)S(1)}, bf16[64,256]{1,0:T(8,128)(2,1)S(1)}, u32[]{:S(2)}, u32[]{:S(2)}) collective-permute-start(bf16[64,256]{1,0:T(8,128)(2,1)S(1)} %hub_sums.1.refs_0_), channel_id=1, source_target_pairs={{0,1},{1,0},{2,3},{3,2},{4,5},{5,4},{6,7},{7,6},{8,9},{9,8},{10,11... | collective-permute-start | bytes 98312 | tf_op jit(solution)/shard_map/ppermute | solution.py:183
  26.5 3.9 %collective-permute-start.4 = (bf16[64,256]{1,0:T(8,128)(2,1)S(1)}, bf16[64,256]{1,0:T(8,128)(2,1)S(1)}, u32[]{:S(2)}, u32[]{:S(2)}) collective-permute-start(bf16[64,256]{1,0:T(8,128)(2,1)S(1)} %hub_sums.1.refs_0_), channel_id=1, source_target_pairs={{0,2},{2,0},{4,6},{6,4},{8,10},{10,8},{12,14},{14,12},{1,3},{3,1},... | collective-permute-start | bytes 98312 | tf_op jit(solution)/shard_map/ppermute | solution.py:186
  30.8 1.6 %collective-permute-start.12 = (f32[256,256]{1,0:T(8,128)S(1)}, f32[256,256]{1,0:T(8,128)S(1)}, u32[]{:S(2)}, u32[]{:S(2)}) collective-permute-start(f32[256,256]{1,0:T(8,128)S(1)} %get-tuple-element.23), channel_id=1, source_target_pairs={{0,1},{1,0},{2,3},{3,2},{4,5},{5,4},{6,7},{7,6},{8,9},{9,8},{10,11... | collective-permute-start | bytes 786440 | tf_op jit(solution)/shard_map/ppermute | solution.py:183

commit v25 on v24

--- a/solution.py
+++ b/solution.py
@@ -89,10 +89,9 @@
     n_row, n_col, side = dims
     blocks, (dense_ref, send_ref, keep_ref, panel) = refs[:4], refs[4:]
     r = lax.axis_index("row")
-    for ref, flip in zip(blocks, (0, 2 * X, 1, 2 * X + 1)):
-        for k in range(2):
-            owner = r ^ (flip + X * k)
-            panel[pl.ds(pl.multiple_of(owner * VB, VB), VB), :] = ref[k]
+    for ref, flips in zip(blocks, ((0, X, 2 * X), (3 * X,), (1, X + 1, 2 * X + 1), (3 * X + 1,))):
+        for k, flip in enumerate(flips):
+            panel[pl.ds(pl.multiple_of((r ^ flip) * VB, VB), VB), :] = ref[k]
     n_rows = dense_ref.shape[0] // 2
     keep_ref[...] = product(dense_ref[:n_rows, :n_row * VB], panel[...])
     send_ref[...] = product(dense_ref[n_rows:, :n_row * VB], panel[...])
@@ -128,10 +127,9 @@
     scores_ref[0] = own_scores(dims, src_ref, keep_ref, came_ref).astype(scores_ref.dtype)
 
 
-def join_kernel(held_ref, came_ref, out_ref):
-    count = held_ref.shape[0]
-    out_ref[:count] = held_ref[...]
-    out_ref[count:] = came_ref[...]
+def join_kernel(*refs):
+    for k, ref in enumerate(refs[:-1]):
+        refs[-1][k] = ref[0]
 
 
 def add_kernel(hold_ref, came_ref, out_ref):
@@ -235,18 +233,17 @@
             (bf16((1, VB, width)), f32((quarter, width)), f32((quarter, width))),
             src, keep, came, cost=2)
         away = other_side(away)
-        pair = bf16((2, VB, width))
         next_z, far_z = to_partner(held, X), to_partner(held, 2 * X)
-        near = call(join_kernel, "join_near", pair, held, next_z, cost=1)
-        far = call(join_kernel, "join_far", pair, far_z, to_partner(far_z, X), cost=2)
-        near_across, far_across = other_side(near), other_side(far)
+        last = to_partner(far_z, X)
+        first = call(join_kernel, "join_first", bf16((3, VB, width)), held, next_z, far_z)
+        first_across, last_across = other_side(first), other_side(last)
         sums = call(add_kernel, "plane_sum", f32((quarter, width)), hold, away, cost=20)
-        sums = call(add_kernel, "pair_sum", f32((quarter, width)), sums, to_partner(sums, X), cost=2)
-        mine = call(bind(hub_kernel, dims), "hub_sums", bf16((quarter, width)), src, sums, to_partner(sums, 2 * X), cost=8)
+        sums = call(add_kernel, "pair_sum", f32((quarter, width)), sums, to_partner(sums, X), cost=1)
+        mine = call(bind(hub_kernel, dims), "hub_sums", bf16((quarter, width)), src, sums, to_partner(sums, 2 * X), cost=1)
         quarters = [mine, other_side(mine), other_core(mine), other_both(mine)]
         send, keep = call(
             bind(score_columns_kernel, dims), "score_columns", (f32((half, width)),) * 2,
-            near, far, near_across, far_across, dense, scratch=[pltpu.VMEM((n_row * VB, width), jnp.bfloat16)])
+            first, last, first_across, last_across, dense, scratch=[pltpu.VMEM((n_row * VB, width), jnp.bfloat16)])
         send, keep = call(
             bind(hub_columns_kernel, dims), "hub_columns", (f32((half, width)),) * 2,
             *quarters, dense, send, keep, scratch=[pltpu.VMEM((H, width), jnp.bfloat16)])

time: 43.2 us -> 43.2 us (level)
    pallas_call x10 -> x9, Pallas kernels: 1.9 us -> 1.89 us  [call(): pl.pallas_call(kernel, out_shape=out_shape, in_specs=[VMEM] * len(args),...]
  transfers between devices with their start and end apart: 13 -> 13, of which waited for: 7 -> 8; matrix products, arithmetic and copies ran while one was open for 0% -> 0% of each run, Pallas kernels for 2% -> 2%
where the time goes in v25:
time: 43.2 us; the launch traced here: 43 us
  starting transfers between devices  15.4 us (36%)
  waiting for transfers between devices  11.1 us (26%)
  blocking collectives  9.96 us (23%)
  Pallas kernels  5.19 us (12%)
  between operations  1.37 us (3%)
    ppermute x9, starting transfers between devices, to_partner(): return lax.ppermute(x, 'row', [(r, r ^ flip) for r in range(n_row)])  13.2 us
    all_to_all x1, blocking collectives, fast_body(): parts = lax.all_to_all(parts, 'row', 0, 0)  9.96 us
    ppermute x9, waiting for transfers between devices, to_partner(): return lax.ppermute(x, 'row', [(r, r ^ flip) for r in range(n_row)])  7.63 us
    pallas_call x1, Pallas kernels, fast_body(): pl.pallas_call(bind(first_kernel, dims), out_shape=(f32((half, width)), f...  3.3 us
    ppermute x3, waiting for transfers between devices, other_core(): return lax.ppermute(x, 'col', [(0, 1), (1, 0)])  2.69 us
    ppermute x3, starting transfers between devices, other_core(): return lax.ppermute(x, 'col', [(0, 1), (1, 0)])  2.18 us
    pallas_call x9, Pallas kernels, call(): pl.pallas_call(kernel, out_shape=out_shape, in_specs=[VMEM] * len(args),...  1.89 us
  transfers between devices with their start and end apart: 13, of which 8 were waited for; matrix products, arithmetic and copies ran while one was open for 0% of the time, Pallas kernels for 2%

profile of v25, /device:TPU:0, one launch (start us, length us, event | category | flops | bytes accessed | tf_op | source)
XLA Modules:
  0.0 43.0 jit_solution(15629510809911919163)
XLA Ops:
  0.6 0.0 copy-start
  1.3 3.3 %first_terms.1 = (f32[256,256]{1,0:T(8,128)S(1)}, f32[256,256]{1,0:T(8,128)S(1)}, bf16[1024,1280]{1,0:T(8,128)(2,1)S(1)}) custom-call(bf16[96,128,128]{2,1,0:T(8,128)(2,1)} %bitcast.11, s32[96]{0:T(128)} %bitcast.12, s32[96]{0:T(128)} %bitcast.13, s32[1]{0:T(128)} %bitcast.6.count_hbm, s32[1,256]{1,0:T(1,128)} %bitcast.7), custom_call_target="tpu_custom_call" | custom-call | tf_op jit(solution)/shard_map/first_terms/pallas_call | solution.py:209
  4.6 0.5 %collective-permute-start = (f32[256,256]{1,0:T(8,128)S(1)}, f32[256,256]{1,0:T(8,128)S(1)}, u32[]{:S(2)}, u32[]{:S(2)}) collective-permute-start(f32[256,256]{1,0:T(8,128)S(1)} %get-tuple-element.15), channel_id=1, source_target_pairs={{0,1},{1,0},{2,3},{3,2},{4,5},{5,4},{6,7},{7,6},{8,9},{9,8},{10,11... | collective-permute-start | bytes 786440 | tf_op jit(solution)/shard_map/ppermute | solution.py:181
  5.1 1.2 %collective-permute-done.came_ref = f32[256,256]{1,0:T(8,128)S(1)} collective-permute-done((f32[256,256]{1,0:T(8,128)S(1)}, f32[256,256]{1,0:T(8,128)S(1)}, u32[]{:S(2)}, u32[]{:S(2)}) %collective-permute-start) | collective-permute-done | bytes 262176 | tf_op jit(solution)/shard_map/ppermute | solution.py:181
  6.3 0.0 copy-done
  6.3 2.9 %collective-permute-start.1 = (f32[64,256]{1,0:T(8,128)S(1)}, f32[64,256]{1,0:T(8,128)S(1)}, u32[]{:S(2)}, u32[]{:S(2)}) collective-permute-start(f32[64,256]{1,0:T(8,128)S(1)} %get-tuple-element.17), channel_id=1, source_target_pairs={{0,2},{2,0},{4,6},{6,4},{8,10},{10,8},{12,14},{14,12},{1,3},{3,1},... | collective-permute-start | bytes 196616 | tf_op jit(solution)/shard_map/ppermute | solution.py:184
  9.3 2.6 %collective-permute-start.8 = (bf16[1,128,256]{2,1,0:T(8,128)(2,1)S(1)}, bf16[1,128,256]{2,1,0:T(8,128)(2,1)S(1)}, u32[]{:S(2)}, u32[]{:S(2)}) collective-permute-start(bf16[1,128,256]{2,1,0:T(8,128)(2,1)S(1)} %get-tuple-element.19.refs_0_), channel_id=1, source_target_pairs={{0,8},{2,10},{4,12},{6,14},{8,0},{10,2},{12,4},{14,6},{1,9},{3,11}... | collective-permute-start | bytes 196616 | tf_op jit(solution)/shard_map/ppermute | solution.py:184
  11.9 1.6 %collective-permute-start.7 = (bf16[1,128,256]{2,1,0:T(8,128)(2,1)S(1)}, bf16[1,128,256]{2,1,0:T(8,128)(2,1)S(1)}, u32[]{:S(2)}, u32[]{:S(2)}) collective-permute-start(bf16[1,128,256]{2,1,0:T(8,128)(2,1)S(1)} %get-tuple-element.19.refs_0_), channel_id=1, source_target_pairs={{0,4},{2,6},{4,0},{6,2},{8,12},{10,14},{12,8},{14,10},{1,5},{3,7},... | collective-permute-start | bytes 196616 | tf_op jit(solution)/shard_map/ppermute | solution.py:184
  13.4 0.0 collective-permute-done.1.came_ref
  13.5 0.5 %collective-permute-start.2 = (f32[64,256]{1,0:T(8,128)S(1)}, f32[64,256]{1,0:T(8,128)S(1)}, u32[]{:S(2)}, u32[]{:S(2)}) collective-permute-start(f32[64,256]{1,0:T(8,128)S(1)} %plane_sum.1.hold_ref), channel_id=1, source_target_pairs={{0,4},{2,6},{4,0},{6,2},{8,12},{10,14},{12,8},{14,10},{1,5},{3,7},... | collective-permute-start | bytes 196616 | tf_op jit(solution)/shard_map/ppermute | solution.py:184
  14.0 1.3 %collective-permute-done.8.refs_2_ = bf16[1,128,256]{2,1,0:T(8,128)(2,1)S(1)} collective-permute-done((bf16[1,128,256]{2,1,0:T(8,128)(2,1)S(1)}, bf16[1,128,256]{2,1,0:T(8,128)(2,1)S(1)}, u32[]{:S(2)}, u32[]{:S(2)}) %collective-permute-start.8) | collective-permute-done | bytes 65568 | tf_op jit(solution)/shard_map/ppermute | solution.py:184
  15.3 1.5 %collective-permute-done.7.refs_1_ = bf16[1,128,256]{2,1,0:T(8,128)(2,1)S(1)} collective-permute-done((bf16[1,128,256]{2,1,0:T(8,128)(2,1)S(1)}, bf16[1,128,256]{2,1,0:T(8,128)(2,1)S(1)}, u32[]{:S(2)}, u32[]{:S(2)}) %collective-permute-start.7) | collective-permute-done | bytes 65568 | tf_op jit(solution)/shard_map/ppermute | solution.py:184
  16.8 0.6 %collective-permute-start.10 = (bf16[3,128,256]{2,1,0:T(8,128)(2,1)S(1)}, bf16[3,128,256]{2,1,0:T(8,128)(2,1)S(1)}, u32[]{:S(2)}, u32[]{:S(2)}) collective-permute-start(bf16[3,128,256]{2,1,0:T(8,128)(2,1)S(1)} %join_first.1.refs_0_), channel_id=1, source_target_pairs={{0,2},{2,0},{4,6},{6,4},{8,10},{10,8},{12,14},{14,12},{1,3},{3,1},... | collective-permute-start | bytes 589832 | tf_op jit(solution)/shard_map/ppermute | solution.py:184
  17.4 1.4 %collective-permute-start.9 = (bf16[1,128,256]{2,1,0:T(8,128)(2,1)S(1)}, bf16[1,128,256]{2,1,0:T(8,128)(2,1)S(1)}, u32[]{:S(2)}, u32[]{:S(2)}) collective-permute-start(bf16[1,128,256]{2,1,0:T(8,128)(2,1)S(1)} %collective-permute-done.8.refs_2_), channel_id=1, source_target_pairs={{0,4},{2,6},{4,0},{6,2},{8,12},{10,14},{12,8},{14,10},{1,5},{3,7},... | collective-permute-start | bytes 196616 | tf_op jit(solution)/shard_map/ppermute | solution.py:184
  18.8 0.0 collective-permute-done.2.came_ref
  18.9 1.4 %collective-permute-start.3 = (f32[64,256]{1,0:T(8,128)S(1)}, f32[64,256]{1,0:T(8,128)S(1)}, u32[]{:S(2)}, u32[]{:S(2)}) collective-permute-start(f32[64,256]{1,0:T(8,128)S(1)} %pair_sum.1.held_ref), channel_id=1, source_target_pairs={{0,8},{2,10},{4,12},{6,14},{8,0},{10,2},{12,4},{14,6},{1,9},{3,11}... | collective-permute-start | bytes 196616 | tf_op jit(solution)/shard_map/ppermute | solution.py:184
  20.2 1.7 %collective-permute-done.9.refs_1_ = bf16[1,128,256]{2,1,0:T(8,128)(2,1)S(1)} collective-permute-done((bf16[1,128,256]{2,1,0:T(8,128)(2,1)S(1)}, bf16[1,128,256]{2,1,0:T(8,128)(2,1)S(1)}, u32[]{:S(2)}, u32[]{:S(2)}) %collective-permute-start.9) | collective-permute-done | bytes 65568 | tf_op jit(solution)/shard_map/ppermute | solution.py:184
  21.9 1.7 %collective-permute-start.11 = (bf16[1,128,256]{2,1,0:T(8,128)(2,1)S(1)}, bf16[1,128,256]{2,1,0:T(8,128)(2,1)S(1)}, u32[]{:S(2)}, u32[]{:S(2)}) collective-permute-start(bf16[1,128,256]{2,1,0:T(8,128)(2,1)S(1)} %collective-permute-done.9.refs_1_), channel_id=1, source_target_pairs={{0,2},{2,0},{4,6},{6,4},{8,10},{10,8},{12,14},{14,12},{1,3},{3,1},... | collective-permute-start | bytes 196616 | tf_op jit(solution)/shard_map/ppermute | solution.py:184
  23.5 1.2 %collective-permute-done.3.came_ref = f32[64,256]{1,0:T(8,128)S(1)} collective-permute-done((f32[64,256]{1,0:T(8,128)S(1)}, f32[64,256]{1,0:T(8,128)S(1)}, u32[]{:S(2)}, u32[]{:S(2)}) %collective-permute-start.3) | collective-permute-done | bytes 65568 | tf_op jit(solution)/shard_map/ppermute | solution.py:184
  24.8 0.1 collective-permute-start.6
  24.9 1.6 %collective-permute-start.5 = (bf16[64,256]{1,0:T(8,128)(2,1)S(1)}, bf16[64,256]{1,0:T(8,128)(2,1)S(1)}, u32[]{:S(2)}, u32[]{:S(2)}) collective-permute-start(bf16[64,256]{1,0:T(8,128)(2,1)S(1)} %hub_sums.1.refs_0_), channel_id=1, source_target_pairs={{0,1},{1,0},{2,3},{3,2},{4,5},{5,4},{6,7},{7,6},{8,9},{9,8},{10,11... | collective-permute-start | bytes 98312 | tf_op jit(solution)/shard_map/ppermute | solution.py:181
  26.5 0.5 %collective-permute-start.4 = (bf16[64,256]{1,0:T(8,128)(2,1)S(1)}, bf16[64,256]{1,0:T(8,128)(2,1)S(1)}, u32[]{:S(2)}, u32[]{:S(2)}) collective-permute-start(bf16[64,256]{1,0:T(8,128)(2,1)S(1)} %hub_sums.1.refs_0_), channel_id=1, source_target_pairs={{0,2},{2,0},{4,6},{6,4},{8,10},{10,8},{12,14},{14,12},{1,3},{3,1},... | collective-permute-start | bytes 98312 | tf_op jit(solution)/shard_map/ppermute | solution.py:184
  27.0 0.0 collective-permute-done.11.refs_3_
  27.0 0.0 collective-permute-done.10.refs_2_
  27.0 0.7 %score_columns.1 = (f32[256,256]{1,0:T(8,128)S(1)}, f32[256,256]{1,0:T(8,128)S(1)}) custom-call(bf16[3,128,256]{2,1,0:T(8,128)(2,1)S(1)} %join_first.1.refs_0_, bf16[1,128,256]{2,1,0:T(8,128)(2,1)S(1)} %collective-permute-done.9.refs_1_, bf16[3,128,256]{2,1,0:T(8,128)(2,1)S(1)} %collective-permute-done.10.refs_2_, ...), custom_call_target="tpu_custom_call" | custom-call | tf_op jit(solution)/shard_map/score_columns/pallas_call | solution.py:194
  27.8 0.7 %collective-permute-done.6.refs_3_ = bf16[64,256]{1,0:T(8,128)(2,1)S(1)} collective-permute-done((bf16[64,256]{1,0:T(8,128)(2,1)S(1)}, bf16[64,256]{1,0:T(8,128)(2,1)S(1)}, u32[]{:S(2)}, u32[]{:S(2)}) %collective-permute-start.6) | collective-permute-done | bytes 32800 | tf_op jit(solution)/shard_map/ppermute | solution.py:191
  28.5 0.0 collective-permute-done.5.refs_2_
  28.5 1.9 %collective-permute-done.4.refs_1_ = bf16[64,256]{1,0:T(8,128)(2,1)S(1)} collective-permute-done((bf16[64,256]{1,0:T(8,128)(2,1)S(1)}, bf16[64,256]{1,0:T(8,128)(2,1)S(1)}, u32[]{:S(2)}, u32[]{:S(2)}) %collective-permute-start.4) | collective-permute-done | bytes 32800 | tf_op jit(solution)/shard_map/ppermute | solution.py:184
  30.4 0.3 hub_columns.1
  30.7 0.1 collective-permute-start.12
  30.8 1.5 %collective-permute-done.12.came_ref = f32[256,256]{1,0:T(8,128)S(1)} collective-permute-done((f32[256,256]{1,0:T(8,128)S(1)}, f32[256,256]{1,0:T(8,128)S(1)}, u32[]{:S(2)}, u32[]{:S(2)}) %collective-permute-start.12) | collective-permute-done | bytes 262176 | tf_op jit(solution)/shard_map/ppermute | solution.py:181
  32.4 10.0 %all_to_all.5.parts_ref = f32[8,16,256]{2,1,0:T(8,128)S(1)} all-to-all(f32[8,16,256]{2,1,0:T(8,128)S(1)} %hub_pieces.1), channel_id=1, replica_groups=mesh['groups'=2,'row'=8,'col'=2] {'row'}, dimensions={0} | all-to-all | bytes 262144 | tf_op jit(solution)/shard_map/all_to_all | solution.py:252
  42.3 0.7 %last_sums.1 = (f32[128,256]{1,0:T(8,128)}, f32[16,256]{1,0:T(8,128)}) custom-call(s32[1,256]{1,0:T(1,128)S(1)} %bitcast.10, f32[256,256]{1,0:T(8,128)S(1)} %get-tuple-element.22.keep_ref, f32[256,256]{1,0:T(8,128)S(1)} %collective-permute-done.12.came_ref, f32[8,16,256]{2,1,0:T(8,128)S(1)} %all_to_all.5.parts_ref), custom_call_target="tpu_custom_call" | custom-call | tf_op jit(solution)/shard_map/last_sums/pallas_call | solution.py:194
  (6 shorter events, 0.1 us)
Async XLA Ops:
  0.6 5.7 %copy-start = (s32[256]{0:T(256)S(1)}, s32[256]{0:T(256)}, u32[]{:S(2)}) copy-start(s32[256]{0:T(256)} %param.9) | copy-start | bytes 3076
  4.6 1.7 %collective-permute-start = (f32[256,256]{1,0:T(8,128)S(1)}, f32[256,256]{1,0:T(8,128)S(1)}, u32[]{:S(2)}, u32[]{:S(2)}) collective-permute-start(f32[256,256]{1,0:T(8,128)S(1)} %get-tuple-element.15), channel_id=1, source_target_pairs={{0,1},{1,0},{2,3},{3,2},{4,5},{5,4},{6,7},{7,6},{8,9},{9,8},{10,11... | collective-permute-start | bytes 786440 | tf_op jit(solution)/shard_map/ppermute | solution.py:181
  6.3 7.1 %collective-permute-start.1 = (f32[64,256]{1,0:T(8,128)S(1)}, f32[64,256]{1,0:T(8,128)S(1)}, u32[]{:S(2)}, u32[]{:S(2)}) collective-permute-start(f32[64,256]{1,0:T(8,128)S(1)} %get-tuple-element.17), channel_id=1, source_target_pairs={{0,2},{2,0},{4,6},{6,4},{8,10},{10,8},{12,14},{14,12},{1,3},{3,1},... | collective-permute-start | bytes 196616 | tf_op jit(solution)/shard_map/ppermute | solution.py:184
  9.3 6.0 %collective-permute-start.8 = (bf16[1,128,256]{2,1,0:T(8,128)(2,1)S(1)}, bf16[1,128,256]{2,1,0:T(8,128)(2,1)S(1)}, u32[]{:S(2)}, u32[]{:S(2)}) collective-permute-start(bf16[1,128,256]{2,1,0:T(8,128)(2,1)S(1)} %get-tuple-element.19.refs_0_), channel_id=1, source_target_pairs={{0,8},{2,10},{4,12},{6,14},{8,0},{10,2},{12,4},{14,6},{1,9},{3,11}... | collective-permute-start | bytes 196616 | tf_op jit(solution)/shard_map/ppermute | solution.py:184
  11.9 5.0 %collective-permute-start.7 = (bf16[1,128,256]{2,1,0:T(8,128)(2,1)S(1)}, bf16[1,128,256]{2,1,0:T(8,128)(2,1)S(1)}, u32[]{:S(2)}, u32[]{:S(2)}) collective-permute-start(bf16[1,128,256]{2,1,0:T(8,128)(2,1)S(1)} %get-tuple-element.19.refs_0_), channel_id=1, source_target_pairs={{0,4},{2,6},{4,0},{6,2},{8,12},{10,14},{12,8},{14,10},{1,5},{3,7},... | collective-permute-start | bytes 196616 | tf_op jit(solution)/shard_map/ppermute | solution.py:184
  13.5 5.4 %collective-permute-start.2 = (f32[64,256]{1,0:T(8,128)S(1)}, f32[64,256]{1,0:T(8,128)S(1)}, u32[]{:S(2)}, u32[]{:S(2)}) collective-permute-start(f32[64,256]{1,0:T(8,128)S(1)} %plane_sum.1.hold_ref), channel_id=1, source_target_pairs={{0,4},{2,6},{4,0},{6,2},{8,12},{10,14},{12,8},{14,10},{1,5},{3,7},... | collective-permute-start | bytes 196616 | tf_op jit(solution)/shard_map/ppermute | solution.py:184
  16.8 10.2 %collective-permute-start.10 = (bf16[3,128,256]{2,1,0:T(8,128)(2,1)S(1)}, bf16[3,128,256]{2,1,0:T(8,128)(2,1)S(1)}, u32[]{:S(2)}, u32[]{:S(2)}) collective-permute-start(bf16[3,128,256]{2,1,0:T(8,128)(2,1)S(1)} %join_first.1.refs_0_), channel_id=1, source_target_pairs={{0,2},{2,0},{4,6},{6,4},{8,10},{10,8},{12,14},{14,12},{1,3},{3,1},... | collective-permute-start | bytes 589832 | tf_op jit(solution)/shard_map/ppermute | solution.py:184
  17.4 4.5 %collective-permute-start.9 = (bf16[1,128,256]{2,1,0:T(8,128)(2,1)S(1)}, bf16[1,128,256]{2,1,0:T(8,128)(2,1)S(1)}, u32[]{:S(2)}, u32[]{:S(2)}) collective-permute-start(bf16[1,128,256]{2,1,0:T(8,128)(2,1)S(1)} %collective-permute-done.8.refs_2_), channel_id=1, source_target_pairs={{0,4},{2,6},{4,0},{6,2},{8,12},{10,14},{12,8},{14,10},{1,5},{3,7},... | collective-permute-start | bytes 196616 | tf_op jit(solution)/shard_map/ppermute | solution.py:184
  18.9 5.9 %collective-permute-start.3 = (f32[64,256]{1,0:T(8,128)S(1)}, f32[64,256]{1,0:T(8,128)S(1)}, u32[]{:S(2)}, u32[]{:S(2)}) collective-permute-start(f32[64,256]{1,0:T(8,128)S(1)} %pair_sum.1.held_ref), channel_id=1, source_target_pairs={{0,8},{2,10},{4,12},{6,14},{8,0},{10,2},{12,4},{14,6},{1,9},{3,11}... | collective-permute-start | bytes 196616 | tf_op jit(solution)/shard_map/ppermute | solution.py:184
  21.9 5.2 %collective-permute-start.11 = (bf16[1,128,256]{2,1,0:T(8,128)(2,1)S(1)}, bf16[1,128,256]{2,1,0:T(8,128)(2,1)S(1)}, u32[]{:S(2)}, u32[]{:S(2)}) collective-permute-start(bf16[1,128,256]{2,1,0:T(8,128)(2,1)S(1)} %collective-permute-done.9.refs_1_), channel_id=1, source_target_pairs={{0,2},{2,0},{4,6},{6,4},{8,10},{10,8},{12,14},{14,12},{1,3},{3,1},... | collective-permute-start | bytes 196616 | tf_op jit(solution)/shard_map/ppermute | solution.py:184
  24.8 3.7 %collective-permute-start.6 = (bf16[64,256]{1,0:T(8,128)(2,1)S(1)}, bf16[64,256]{1,0:T(8,128)(2,1)S(1)}, u32[]{:S(2)}, u32[]{:S(2)}) collective-permute-start(bf16[64,256]{1,0:T(8,128)(2,1)S(1)} %hub_sums.1.refs_0_), channel_id=1, source_target_pairs={{0,3},{1,2},{2,1},{3,0},{4,7},{5,6},{6,5},{7,4},{8,11},{9,10},{10,... | collective-permute-start | bytes 98312 | tf_op jit(solution)/shard_map/ppermute | solution.py:191
  24.9 3.6 %collective-permute-start.5 = (bf16[64,256]{1,0:T(8,128)(2,1)S(1)}, bf16[64,256]{1,0:T(8,128)(2,1)S(1)}, u32[]{:S(2)}, u32[]{:S(2)}) collective-permute-start(bf16[64,256]{1,0:T(8,128)(2,1)S(1)} %hub_sums.1.refs_0_), channel_id=1, source_target_pairs={{0,1},{1,0},{2,3},{3,2},{4,5},{5,4},{6,7},{7,6},{8,9},{9,8},{10,11... | collective-permute-start | bytes 98312 | tf_op jit(solution)/shard_map/ppermute | solution.py:181
  26.5 3.9 %collective-permute-start.4 = (bf16[64,256]{1,0:T(8,128)(2,1)S(1)}, bf16[64,256]{1,0:T(8,128)(2,1)S(1)}, u32[]{:S(2)}, u32[]{:S(2)}) collective-permute-start(bf16[64,256]{1,0:T(8,128)(2,1)S(1)} %hub_sums.1.refs_0_), channel_id=1, source_target_pairs={{0,2},{2,0},{4,6},{6,4},{8,10},{10,8},{12,14},{14,12},{1,3},{3,1},... | collective-permute-start | bytes 98312 | tf_op jit(solution)/shard_map/ppermute | solution.py:184
  30.7 1.6 %collective-permute-start.12 = (f32[256,256]{1,0:T(8,128)S(1)}, f32[256,256]{1,0:T(8,128)S(1)}, u32[]{:S(2)}, u32[]{:S(2)}) collective-permute-start(f32[256,256]{1,0:T(8,128)S(1)} %get-tuple-element.23), channel_id=1, source_target_pairs={{0,1},{1,0},{2,3},{3,2},{4,5},{5,4},{6,7},{7,6},{8,9},{9,8},{10,11... | collective-permute-start | bytes 786440 | tf_op jit(solution)/shard_map/ppermute | solution.py:181

commit v26 on v25

--- a/solution.py
+++ b/solution.py
@@ -29,6 +29,11 @@
 def one_hot(first, count, src):
     ids = lax.broadcasted_iota(jnp.int32, (count, src.shape[1]), 0) + first
     return (ids == src).astype(jnp.float32)
+
+
+def hub_half():
+    r = lax.axis_index("row")
+    return lax.axis_index("col") ^ (r & 1) ^ (r >> 1 & 1) ^ (r >> 2 & 1)
 
 
 def product(dense, panel):
@@ -73,10 +78,11 @@
         copy.wait()
         lax.fori_loop(i * CHUNK, (i + 1) * CHUNK, add_tile, 0, unroll=4)
     half = n_rows // n_col
-    for at, out, core in ((0, keep_ref, c), (n_rows, send_ref, 1 - c)):
+    h = hub_half()
+    for at, out, core, hubs in ((0, keep_ref, c, h), (n_rows, send_ref, 1 - c, 1 - h)):
         chunks = [(0, core * VB, VB)]
         for r in range(n_row):
-            chunks.append((VB + r * piece, n_col * VB + (r * n_col + core) * piece, piece))
+            chunks.append((VB + r * piece, n_col * VB + (r * n_col + hubs) * piece, piece))
         for to, start, size in chunks:
             whole = total[pl.ds(pl.multiple_of(start, size), size), :]
             high = whole.astype(jnp.bfloat16)
@@ -101,15 +107,20 @@
     n_row, n_col, side = dims
     n_z = n_row // X
     quarters, (dense_ref, send_part, keep_part, send_ref, keep_ref, panel) = refs[:X * n_col], refs[X * n_col:]
-    r, c = lax.axis_index("row"), lax.axis_index("col")
+    r, h = lax.axis_index("row"), hub_half()
     piece = H // (n_row * n_col)
     for k, ref in enumerate(quarters):
         for i in range(n_z):
-            row = ((r % X ^ (k % X)) * n_z + i) * n_col + (c ^ (k // X))
+            row = ((r % X ^ (k % X)) * n_z + i) * n_col + (h ^ (k % X) ^ (k // X))
             panel[pl.ds(pl.multiple_of(row * piece, piece), piece), :] = ref[i * piece:(i + 1) * piece]
     n_rows = dense_ref.shape[0] // 2
-    send_ref[...] = send_part[...] + product(dense_ref[n_rows:, n_row * VB:], panel[...])
-    keep_ref[...] = keep_part[...] + product(dense_ref[:n_rows, n_row * VB:], panel[...])
+    send = send_part[...] + product(dense_ref[n_rows:, n_row * VB:], panel[...])
+    keep = keep_part[...] + product(dense_ref[:n_rows, n_row * VB:], panel[...])
+    same = h == lax.axis_index("col")
+    send_ref[:VB] = send[:VB]
+    keep_ref[:VB] = keep[:VB]
+    send_ref[VB:] = jnp.where(same, send[VB:], keep[VB:])
+    keep_ref[VB:] = jnp.where(same, keep[VB:], send[VB:])
 
 
 def own_scores(dims, src_ref, keep_ref, came_ref):
@@ -139,9 +150,9 @@
 def hub_kernel(dims, src_ref, held_ref, came_ref, out_ref):
     n_row, n_col, side = dims
     piece = H // (n_row * n_col)
-    r, c = lax.axis_index("row"), lax.axis_index("col")
+    r = lax.axis_index("row")
     at = lax.broadcasted_iota(jnp.int32, out_ref.shape, 0)
-    ids = ((r % X * (n_row // X) + at // piece) * n_col + c) * piece + at % piece
+    ids = ((r % X * (n_row // X) + at // piece) * n_col + hub_half()) * piece + at % piece
     tele = (ids == src_ref[...]).astype(jnp.float32)
     out_ref[...] = (DAMP * (held_ref[...] + came_ref[...]) + 0.15 * tele).astype(out_ref.dtype)
 
@@ -186,9 +197,9 @@
     def other_side(x):
         return to_partner(x, 1)
 
-    def other_both(x):
+    def cross(x, flip):
         devices = [(r, c) for r in range(n_row) for c in range(n_col)]
-        return lax.ppermute(x, ("row", "col"), [(r * n_col + c, (r ^ 1) * n_col + 1 - c) for r, c in devices])
+        return lax.ppermute(x, ("row", "col"), [(r * n_col + c, (r ^ flip) * n_col + 1 - c) for r, c in devices])
 
     def call(kernel, name, out_shape, *args, scratch=(), cost=0):
         return pl.pallas_call(
@@ -232,15 +243,15 @@
             bind(spread_kernel, dims), "spread",
             (bf16((1, VB, width)), f32((quarter, width)), f32((quarter, width))),
             src, keep, came, cost=2)
-        away = other_side(away)
+        away = cross(away, 1)
         next_z, far_z = to_partner(held, X), to_partner(held, 2 * X)
         last = to_partner(far_z, X)
         first = call(join_kernel, "join_first", bf16((3, VB, width)), held, next_z, far_z)
         first_across, last_across = other_side(first), other_side(last)
         sums = call(add_kernel, "plane_sum", f32((quarter, width)), hold, away, cost=20)
-        sums = call(add_kernel, "pair_sum", f32((quarter, width)), sums, to_partner(sums, X), cost=1)
-        mine = call(bind(hub_kernel, dims), "hub_sums", bf16((quarter, width)), src, sums, to_partner(sums, 2 * X), cost=1)
-        quarters = [mine, other_side(mine), other_core(mine), other_both(mine)]
+        sums = call(add_kernel, "pair_sum", f32((quarter, width)), sums, cross(sums, X), cost=1)
+        mine = call(bind(hub_kernel, dims), "hub_sums", bf16((quarter, width)), src, sums, cross(sums, 2 * X), cost=1)
+        quarters = [mine, other_side(mine), other_core(mine), cross(mine, 1)]
         send, keep = call(
             bind(score_columns_kernel, dims), "score_columns", (f32((half, width)),) * 2,
             first, last, first_across, last_across, dense, scratch=[pltpu.VMEM((n_row * VB, width), jnp.bfloat16)])

time: 43.2 us -> 43.9 us (1.016)
  waiting for transfers between devices: 11.1 us -> 11.8 us
  blocking collectives: 9.96 us -> 10.6 us
  starting transfers between devices: 15.4 us -> 14.8 us
    ppermute x1 -> x4, starting transfers between devices: 0.07 us -> 5.18 us  [cross(): lax.ppermute(x, ('row', 'col'), [(r * n_col + c, (r ^ flip) * n_col + 1 -...]
    ppermute x9 -> x6, starting transfers between devices: 13.2 us -> 8.44 us  [to_partner(): return lax.ppermute(x, 'row', [(r, r ^ flip) for r in range(n_row)])]
    ppermute x1 -> x4, waiting for transfers between devices: 0.74 us -> 2.98 us  [cross(): lax.ppermute(x, ('row', 'col'), [(r * n_col + c, (r ^ flip) * n_col + 1 -...]
    ppermute x9 -> x6, waiting for transfers between devices: 7.63 us -> 6.15 us  [to_partner(): return lax.ppermute(x, 'row', [(r, r ^ flip) for r in range(n_row)])]
    ppermute x3, starting transfers between devices: 2.18 us -> 1.14 us  [other_core(): return lax.ppermute(x, 'col', [(0, 1), (1, 0)])]
    all_to_all x1, blocking collectives: 9.96 us -> 10.6 us  [fast_body(): parts = lax.all_to_all(parts, 'row', 0, 0)]
where the time goes in v26:
time: 43.9 us; the launch traced here: 43.7 us
  starting transfers between devices  14.8 us (34%)
  waiting for transfers between devices  11.8 us (27%)
  blocking collectives  10.6 us (24%)
  Pallas kernels  5.18 us (12%)
  between operations  1.37 us (3%)
    all_to_all x1, blocking collectives, fast_body(): parts = lax.all_to_all(parts, 'row', 0, 0)  10.6 us
    ppermute x6, starting transfers between devices, to_partner(): return lax.ppermute(x, 'row', [(r, r ^ flip) for r in range(n_row)])  8.44 us
    ppermute x6, waiting for transfers between devices, to_partner(): return lax.ppermute(x, 'row', [(r, r ^ flip) for r in range(n_row)])  6.15 us
    ppermute x4, starting transfers between devices, cross(): lax.ppermute(x, ('row', 'col'), [(r * n_col + c, (r ^ flip) * n_col + 1 -...  5.18 us
    pallas_call x1, Pallas kernels, fast_body(): pl.pallas_call(bind(first_kernel, dims), out_shape=(f32((half, width)), f...  3.3 us
    ppermute x4, waiting for transfers between devices, cross(): lax.ppermute(x, ('row', 'col'), [(r * n_col + c, (r ^ flip) * n_col + 1 -...  2.98 us
    ppermute x3, waiting for transfers between devices, other_core(): return lax.ppermute(x, 'col', [(0, 1), (1, 0)])  2.69 us
    pallas_call x9, Pallas kernels, call(): pl.pallas_call(kernel, out_shape=out_shape, in_specs=[VMEM] * len(args),...  1.88 us
  transfers between devices with their start and end apart: 13, of which 8 were waited for; matrix products, arithmetic and copies ran while one was open for 0% of the time, Pallas kernels for 2%

profile of v26, /device:TPU:0, one launch (start us, length us, event | category | flops | bytes accessed | tf_op | source)
XLA Modules:
  0.0 43.7 jit_solution(7128493600367741878)
XLA Ops:
  0.6 0.0 copy-start
  1.3 3.3 %first_terms.1 = (f32[256,256]{1,0:T(8,128)S(1)}, f32[256,256]{1,0:T(8,128)S(1)}, bf16[1024,1280]{1,0:T(8,128)(2,1)S(1)}) custom-call(bf16[96,128,128]{2,1,0:T(8,128)(2,1)} %bitcast.11, s32[96]{0:T(128)} %bitcast.12, s32[96]{0:T(128)} %bitcast.13, s32[1]{0:T(128)} %bitcast.6.count_hbm, s32[1,256]{1,0:T(1,128)} %bitcast.7), custom_call_target="tpu_custom_call" | custom-call | tf_op jit(solution)/shard_map/first_terms/pallas_call | solution.py:220
  4.6 0.5 %collective-permute-start = (f32[256,256]{1,0:T(8,128)S(1)}, f32[256,256]{1,0:T(8,128)S(1)}, u32[]{:S(2)}, u32[]{:S(2)}) collective-permute-start(f32[256,256]{1,0:T(8,128)S(1)} %get-tuple-element.15), channel_id=1, source_target_pairs={{0,1},{1,0},{2,3},{3,2},{4,5},{5,4},{6,7},{7,6},{8,9},{9,8},{10,11... | collective-permute-start | bytes 786440 | tf_op jit(solution)/shard_map/ppermute | solution.py:192
  5.1 1.2 %collective-permute-done.came_ref = f32[256,256]{1,0:T(8,128)S(1)} collective-permute-done((f32[256,256]{1,0:T(8,128)S(1)}, f32[256,256]{1,0:T(8,128)S(1)}, u32[]{:S(2)}, u32[]{:S(2)}) %collective-permute-start) | collective-permute-done | bytes 262176 | tf_op jit(solution)/shard_map/ppermute | solution.py:192
  6.3 0.0 copy-done
  6.3 2.7 %collective-permute-start.1 = (f32[64,256]{1,0:T(8,128)S(1)}, f32[64,256]{1,0:T(8,128)S(1)}, u32[]{:S(2)}, u32[]{:S(2)}) collective-permute-start(f32[64,256]{1,0:T(8,128)S(1)} %get-tuple-element.17), channel_id=1, source_target_pairs={{0,3},{1,2},{2,1},{3,0},{4,7},{5,6},{6,5},{7,4},{8,11},{9,10},{10,... | collective-permute-start | bytes 196616 | tf_op jit(solution)/shard_map/ppermute | solution.py:202
  9.0 2.6 %collective-permute-start.8 = (bf16[1,128,256]{2,1,0:T(8,128)(2,1)S(1)}, bf16[1,128,256]{2,1,0:T(8,128)(2,1)S(1)}, u32[]{:S(2)}, u32[]{:S(2)}) collective-permute-start(bf16[1,128,256]{2,1,0:T(8,128)(2,1)S(1)} %get-tuple-element.19.refs_0_), channel_id=1, source_target_pairs={{0,8},{2,10},{4,12},{6,14},{8,0},{10,2},{12,4},{14,6},{1,9},{3,11}... | collective-permute-start | bytes 196616 | tf_op jit(solution)/shard_map/ppermute | solution.py:195
  11.6 1.6 %collective-permute-start.7 = (bf16[1,128,256]{2,1,0:T(8,128)(2,1)S(1)}, bf16[1,128,256]{2,1,0:T(8,128)(2,1)S(1)}, u32[]{:S(2)}, u32[]{:S(2)}) collective-permute-start(bf16[1,128,256]{2,1,0:T(8,128)(2,1)S(1)} %get-tuple-element.19.refs_0_), channel_id=1, source_target_pairs={{0,4},{2,6},{4,0},{6,2},{8,12},{10,14},{12,8},{14,10},{1,5},{3,7},... | collective-permute-start | bytes 196616 | tf_op jit(solution)/shard_map/ppermute | solution.py:195
  13.2 0.0 collective-permute-done.1.came_ref
  13.2 0.1 collective-permute-start.2
  13.3 2.2 %collective-permute-done.8.refs_2_ = bf16[1,128,256]{2,1,0:T(8,128)(2,1)S(1)} collective-permute-done((bf16[1,128,256]{2,1,0:T(8,128)(2,1)S(1)}, bf16[1,128,256]{2,1,0:T(8,128)(2,1)S(1)}, u32[]{:S(2)}, u32[]{:S(2)}) %collective-permute-start.8) | collective-permute-done | bytes 65568 | tf_op jit(solution)/shard_map/ppermute | solution.py:195
  15.5 0.5 %collective-permute-done.7.refs_1_ = bf16[1,128,256]{2,1,0:T(8,128)(2,1)S(1)} collective-permute-done((bf16[1,128,256]{2,1,0:T(8,128)(2,1)S(1)}, bf16[1,128,256]{2,1,0:T(8,128)(2,1)S(1)}, u32[]{:S(2)}, u32[]{:S(2)}) %collective-permute-start.7) | collective-permute-done | bytes 65568 | tf_op jit(solution)/shard_map/ppermute | solution.py:195
  16.1 0.5 %collective-permute-start.10 = (bf16[3,128,256]{2,1,0:T(8,128)(2,1)S(1)}, bf16[3,128,256]{2,1,0:T(8,128)(2,1)S(1)}, u32[]{:S(2)}, u32[]{:S(2)}) collective-permute-start(bf16[3,128,256]{2,1,0:T(8,128)(2,1)S(1)} %join_first.1.refs_0_), channel_id=1, source_target_pairs={{0,2},{2,0},{4,6},{6,4},{8,10},{10,8},{12,14},{14,12},{1,3},{3,1},... | collective-permute-start | bytes 589832 | tf_op jit(solution)/shard_map/ppermute | solution.py:195
  16.6 1.7 %collective-permute-start.9 = (bf16[1,128,256]{2,1,0:T(8,128)(2,1)S(1)}, bf16[1,128,256]{2,1,0:T(8,128)(2,1)S(1)}, u32[]{:S(2)}, u32[]{:S(2)}) collective-permute-start(bf16[1,128,256]{2,1,0:T(8,128)(2,1)S(1)} %collective-permute-done.8.refs_2_), channel_id=1, source_target_pairs={{0,4},{2,6},{4,0},{6,2},{8,12},{10,14},{12,8},{14,10},{1,5},{3,7},... | collective-permute-start | bytes 196616 | tf_op jit(solution)/shard_map/ppermute | solution.py:195
  18.3 0.0 collective-permute-done.2.came_ref
  18.3 1.2 %collective-permute-start.3 = (f32[64,256]{1,0:T(8,128)S(1)}, f32[64,256]{1,0:T(8,128)S(1)}, u32[]{:S(2)}, u32[]{:S(2)}) collective-permute-start(f32[64,256]{1,0:T(8,128)S(1)} %pair_sum.1.held_ref), channel_id=1, source_target_pairs={{0,9},{1,8},{2,11},{3,10},{4,13},{5,12},{6,15},{7,14},{8,1},{9,0},... | collective-permute-start | bytes 196616 | tf_op jit(solution)/shard_map/ppermute | solution.py:202
  19.5 1.3 %collective-permute-done.9.refs_1_ = bf16[1,128,256]{2,1,0:T(8,128)(2,1)S(1)} collective-permute-done((bf16[1,128,256]{2,1,0:T(8,128)(2,1)S(1)}, bf16[1,128,256]{2,1,0:T(8,128)(2,1)S(1)}, u32[]{:S(2)}, u32[]{:S(2)}) %collective-permute-start.9) | collective-permute-done | bytes 65568 | tf_op jit(solution)/shard_map/ppermute | solution.py:195
  20.9 1.6 %collective-permute-start.11 = (bf16[1,128,256]{2,1,0:T(8,128)(2,1)S(1)}, bf16[1,128,256]{2,1,0:T(8,128)(2,1)S(1)}, u32[]{:S(2)}, u32[]{:S(2)}) collective-permute-start(bf16[1,128,256]{2,1,0:T(8,128)(2,1)S(1)} %collective-permute-done.9.refs_1_), channel_id=1, source_target_pairs={{0,2},{2,0},{4,6},{6,4},{8,10},{10,8},{12,14},{14,12},{1,3},{3,1},... | collective-permute-start | bytes 196616 | tf_op jit(solution)/shard_map/ppermute | solution.py:195
  22.5 2.3 %collective-permute-done.3.came_ref = f32[64,256]{1,0:T(8,128)S(1)} collective-permute-done((f32[64,256]{1,0:T(8,128)S(1)}, f32[64,256]{1,0:T(8,128)S(1)}, u32[]{:S(2)}, u32[]{:S(2)}) %collective-permute-start.3) | collective-permute-done | bytes 65568 | tf_op jit(solution)/shard_map/ppermute | solution.py:202
  24.8 1.2 %collective-permute-start.6 = (bf16[64,256]{1,0:T(8,128)(2,1)S(1)}, bf16[64,256]{1,0:T(8,128)(2,1)S(1)}, u32[]{:S(2)}, u32[]{:S(2)}) collective-permute-start(bf16[64,256]{1,0:T(8,128)(2,1)S(1)} %hub_sums.1.refs_0_), channel_id=1, source_target_pairs={{0,3},{1,2},{2,1},{3,0},{4,7},{5,6},{6,5},{7,4},{8,11},{9,10},{10,... | collective-permute-start | bytes 98312 | tf_op jit(solution)/shard_map/ppermute | solution.py:202
  26.0 0.5 %collective-permute-start.5 = (bf16[64,256]{1,0:T(8,128)(2,1)S(1)}, bf16[64,256]{1,0:T(8,128)(2,1)S(1)}, u32[]{:S(2)}, u32[]{:S(2)}) collective-permute-start(bf16[64,256]{1,0:T(8,128)(2,1)S(1)} %hub_sums.1.refs_0_), channel_id=1, source_target_pairs={{0,1},{1,0},{2,3},{3,2},{4,5},{5,4},{6,7},{7,6},{8,9},{9,8},{10,11... | collective-permute-start | bytes 98312 | tf_op jit(solution)/shard_map/ppermute | solution.py:192
  26.6 0.5 %collective-permute-start.4 = (bf16[64,256]{1,0:T(8,128)(2,1)S(1)}, bf16[64,256]{1,0:T(8,128)(2,1)S(1)}, u32[]{:S(2)}, u32[]{:S(2)}) collective-permute-start(bf16[64,256]{1,0:T(8,128)(2,1)S(1)} %hub_sums.1.refs_0_), channel_id=1, source_target_pairs={{0,2},{2,0},{4,6},{6,4},{8,10},{10,8},{12,14},{14,12},{1,3},{3,1},... | collective-permute-start | bytes 98312 | tf_op jit(solution)/shard_map/ppermute | solution.py:195
  27.0 0.0 collective-permute-done.11.refs_3_
  27.0 0.0 collective-permute-done.10.refs_2_
  27.0 0.7 %score_columns.1 = (f32[256,256]{1,0:T(8,128)S(1)}, f32[256,256]{1,0:T(8,128)S(1)}) custom-call(bf16[3,128,256]{2,1,0:T(8,128)(2,1)S(1)} %join_first.1.refs_0_, bf16[1,128,256]{2,1,0:T(8,128)(2,1)S(1)} %collective-permute-done.9.refs_1_, bf16[3,128,256]{2,1,0:T(8,128)(2,1)S(1)} %collective-permute-done.10.refs_2_, ...), custom_call_target="tpu_custom_call" | custom-call | tf_op jit(solution)/shard_map/score_columns/pallas_call | solution.py:205
  27.8 0.7 %collective-permute-done.6.refs_3_ = bf16[64,256]{1,0:T(8,128)(2,1)S(1)} collective-permute-done((bf16[64,256]{1,0:T(8,128)(2,1)S(1)}, bf16[64,256]{1,0:T(8,128)(2,1)S(1)}, u32[]{:S(2)}, u32[]{:S(2)}) %collective-permute-start.6) | collective-permute-done | bytes 32800 | tf_op jit(solution)/shard_map/ppermute | solution.py:202
  28.5 0.0 collective-permute-done.5.refs_2_
  28.5 2.0 %collective-permute-done.4.refs_1_ = bf16[64,256]{1,0:T(8,128)(2,1)S(1)} collective-permute-done((bf16[64,256]{1,0:T(8,128)(2,1)S(1)}, bf16[64,256]{1,0:T(8,128)(2,1)S(1)}, u32[]{:S(2)}, u32[]{:S(2)}) %collective-permute-start.4) | collective-permute-done | bytes 32800 | tf_op jit(solution)/shard_map/ppermute | solution.py:195
  30.5 0.3 hub_columns.1
  30.8 0.1 collective-permute-start.12
  30.9 1.5 %collective-permute-done.12.came_ref = f32[256,256]{1,0:T(8,128)S(1)} collective-permute-done((f32[256,256]{1,0:T(8,128)S(1)}, f32[256,256]{1,0:T(8,128)S(1)}, u32[]{:S(2)}, u32[]{:S(2)}) %collective-permute-start.12) | collective-permute-done | bytes 262176 | tf_op jit(solution)/shard_map/ppermute | solution.py:192
  32.4 10.6 %all_to_all.5.parts_ref = f32[8,16,256]{2,1,0:T(8,128)S(1)} all-to-all(f32[8,16,256]{2,1,0:T(8,128)S(1)} %hub_pieces.1), channel_id=1, replica_groups=mesh['groups'=2,'row'=8,'col'=2] {'row'}, dimensions={0} | all-to-all | bytes 262144 | tf_op jit(solution)/shard_map/all_to_all | solution.py:263
  43.0 0.7 %last_sums.1 = (f32[128,256]{1,0:T(8,128)}, f32[16,256]{1,0:T(8,128)}) custom-call(s32[1,256]{1,0:T(1,128)S(1)} %bitcast.10, f32[256,256]{1,0:T(8,128)S(1)} %get-tuple-element.22.keep_ref, f32[256,256]{1,0:T(8,128)S(1)} %collective-permute-done.12.came_ref, f32[8,16,256]{2,1,0:T(8,128)S(1)} %all_to_all.5.parts_ref), custom_call_target="tpu_custom_call" | custom-call | tf_op jit(solution)/shard_map/last_sums/pallas_call | solution.py:205
  (6 shorter events, 0.1 us)
Async XLA Ops:
  0.6 5.7 %copy-start = (s32[256]{0:T(256)S(1)}, s32[256]{0:T(256)}, u32[]{:S(2)}) copy-start(s32[256]{0:T(256)} %param.9) | copy-start | bytes 3076
  4.6 1.7 %collective-permute-start = (f32[256,256]{1,0:T(8,128)S(1)}, f32[256,256]{1,0:T(8,128)S(1)}, u32[]{:S(2)}, u32[]{:S(2)}) collective-permute-start(f32[256,256]{1,0:T(8,128)S(1)} %get-tuple-element.15), channel_id=1, source_target_pairs={{0,1},{1,0},{2,3},{3,2},{4,5},{5,4},{6,7},{7,6},{8,9},{9,8},{10,11... | collective-permute-start | bytes 786440 | tf_op jit(solution)/shard_map/ppermute | solution.py:192
  6.3 6.9 %collective-permute-start.1 = (f32[64,256]{1,0:T(8,128)S(1)}, f32[64,256]{1,0:T(8,128)S(1)}, u32[]{:S(2)}, u32[]{:S(2)}) collective-permute-start(f32[64,256]{1,0:T(8,128)S(1)} %get-tuple-element.17), channel_id=1, source_target_pairs={{0,3},{1,2},{2,1},{3,0},{4,7},{5,6},{6,5},{7,4},{8,11},{9,10},{10,... | collective-permute-start | bytes 196616 | tf_op jit(solution)/shard_map/ppermute | solution.py:202
  9.0 6.5 %collective-permute-start.8 = (bf16[1,128,256]{2,1,0:T(8,128)(2,1)S(1)}, bf16[1,128,256]{2,1,0:T(8,128)(2,1)S(1)}, u32[]{:S(2)}, u32[]{:S(2)}) collective-permute-start(bf16[1,128,256]{2,1,0:T(8,128)(2,1)S(1)} %get-tuple-element.19.refs_0_), channel_id=1, source_target_pairs={{0,8},{2,10},{4,12},{6,14},{8,0},{10,2},{12,4},{14,6},{1,9},{3,11}... | collective-permute-start | bytes 196616 | tf_op jit(solution)/shard_map/ppermute | solution.py:195
  11.6 4.4 %collective-permute-start.7 = (bf16[1,128,256]{2,1,0:T(8,128)(2,1)S(1)}, bf16[1,128,256]{2,1,0:T(8,128)(2,1)S(1)}, u32[]{:S(2)}, u32[]{:S(2)}) collective-permute-start(bf16[1,128,256]{2,1,0:T(8,128)(2,1)S(1)} %get-tuple-element.19.refs_0_), channel_id=1, source_target_pairs={{0,4},{2,6},{4,0},{6,2},{8,12},{10,14},{12,8},{14,10},{1,5},{3,7},... | collective-permute-start | bytes 196616 | tf_op jit(solution)/shard_map/ppermute | solution.py:195
  13.2 5.1 %collective-permute-start.2 = (f32[64,256]{1,0:T(8,128)S(1)}, f32[64,256]{1,0:T(8,128)S(1)}, u32[]{:S(2)}, u32[]{:S(2)}) collective-permute-start(f32[64,256]{1,0:T(8,128)S(1)} %plane_sum.1.hold_ref), channel_id=1, source_target_pairs={{0,5},{1,4},{2,7},{3,6},{4,1},{5,0},{6,3},{7,2},{8,13},{9,12},{10,... | collective-permute-start | bytes 196616 | tf_op jit(solution)/shard_map/ppermute | solution.py:202
  16.1 11.0 %collective-permute-start.10 = (bf16[3,128,256]{2,1,0:T(8,128)(2,1)S(1)}, bf16[3,128,256]{2,1,0:T(8,128)(2,1)S(1)}, u32[]{:S(2)}, u32[]{:S(2)}) collective-permute-start(bf16[3,128,256]{2,1,0:T(8,128)(2,1)S(1)} %join_first.1.refs_0_), channel_id=1, source_target_pairs={{0,2},{2,0},{4,6},{6,4},{8,10},{10,8},{12,14},{14,12},{1,3},{3,1},... | collective-permute-start | bytes 589832 | tf_op jit(solution)/shard_map/ppermute | solution.py:195
  16.6 4.3 %collective-permute-start.9 = (bf16[1,128,256]{2,1,0:T(8,128)(2,1)S(1)}, bf16[1,128,256]{2,1,0:T(8,128)(2,1)S(1)}, u32[]{:S(2)}, u32[]{:S(2)}) collective-permute-start(bf16[1,128,256]{2,1,0:T(8,128)(2,1)S(1)} %collective-permute-done.8.refs_2_), channel_id=1, source_target_pairs={{0,4},{2,6},{4,0},{6,2},{8,12},{10,14},{12,8},{14,10},{1,5},{3,7},... | collective-permute-start | bytes 196616 | tf_op jit(solution)/shard_map/ppermute | solution.py:195
  18.3 6.5 %collective-permute-start.3 = (f32[64,256]{1,0:T(8,128)S(1)}, f32[64,256]{1,0:T(8,128)S(1)}, u32[]{:S(2)}, u32[]{:S(2)}) collective-permute-start(f32[64,256]{1,0:T(8,128)S(1)} %pair_sum.1.held_ref), channel_id=1, source_target_pairs={{0,9},{1,8},{2,11},{3,10},{4,13},{5,12},{6,15},{7,14},{8,1},{9,0},... | collective-permute-start | bytes 196616 | tf_op jit(solution)/shard_map/ppermute | solution.py:202
  20.9 6.2 %collective-permute-start.11 = (bf16[1,128,256]{2,1,0:T(8,128)(2,1)S(1)}, bf16[1,128,256]{2,1,0:T(8,128)(2,1)S(1)}, u32[]{:S(2)}, u32[]{:S(2)}) collective-permute-start(bf16[1,128,256]{2,1,0:T(8,128)(2,1)S(1)} %collective-permute-done.9.refs_1_), channel_id=1, source_target_pairs={{0,2},{2,0},{4,6},{6,4},{8,10},{10,8},{12,14},{14,12},{1,3},{3,1},... | collective-permute-start | bytes 196616 | tf_op jit(solution)/shard_map/ppermute | solution.py:195
  24.8 3.6 %collective-permute-start.6 = (bf16[64,256]{1,0:T(8,128)(2,1)S(1)}, bf16[64,256]{1,0:T(8,128)(2,1)S(1)}, u32[]{:S(2)}, u32[]{:S(2)}) collective-permute-start(bf16[64,256]{1,0:T(8,128)(2,1)S(1)} %hub_sums.1.refs_0_), channel_id=1, source_target_pairs={{0,3},{1,2},{2,1},{3,0},{4,7},{5,6},{6,5},{7,4},{8,11},{9,10},{10,... | collective-permute-start | bytes 98312 | tf_op jit(solution)/shard_map/ppermute | solution.py:202
  26.0 2.4 %collective-permute-start.5 = (bf16[64,256]{1,0:T(8,128)(2,1)S(1)}, bf16[64,256]{1,0:T(8,128)(2,1)S(1)}, u32[]{:S(2)}, u32[]{:S(2)}) collective-permute-start(bf16[64,256]{1,0:T(8,128)(2,1)S(1)} %hub_sums.1.refs_0_), channel_id=1, source_target_pairs={{0,1},{1,0},{2,3},{3,2},{4,5},{5,4},{6,7},{7,6},{8,9},{9,8},{10,11... | collective-permute-start | bytes 98312 | tf_op jit(solution)/shard_map/ppermute | solution.py:192
  26.6 3.9 %collective-permute-start.4 = (bf16[64,256]{1,0:T(8,128)(2,1)S(1)}, bf16[64,256]{1,0:T(8,128)(2,1)S(1)}, u32[]{:S(2)}, u32[]{:S(2)}) collective-permute-start(bf16[64,256]{1,0:T(8,128)(2,1)S(1)} %hub_sums.1.refs_0_), channel_id=1, source_target_pairs={{0,2},{2,0},{4,6},{6,4},{8,10},{10,8},{12,14},{14,12},{1,3},{3,1},... | collective-permute-start | bytes 98312 | tf_op jit(solution)/shard_map/ppermute | solution.py:195
  30.8 1.6 %collective-permute-start.12 = (f32[256,256]{1,0:T(8,128)S(1)}, f32[256,256]{1,0:T(8,128)S(1)}, u32[]{:S(2)}, u32[]{:S(2)}) collective-permute-start(f32[256,256]{1,0:T(8,128)S(1)} %get-tuple-element.23), channel_id=1, source_target_pairs={{0,1},{1,0},{2,3},{3,2},{4,5},{5,4},{6,7},{7,6},{8,9},{9,8},{10,11... | collective-permute-start | bytes 786440 | tf_op jit(solution)/shard_map/ppermute | solution.py:192

commit v27 on v18

--- a/solution.py
+++ b/solution.py
@@ -1,4 +1,5 @@
 import functools
+import math
 
 import jax
 import jax.numpy as jnp
@@ -11,7 +12,7 @@
 H = 256
 ITERS = 2
 DAMP = 0.85
-CHUNK = 16
+CHUNK = 8
 X = 2
 MICRO = 10 ** 9
 VMEM_LIMIT = 32 * 1024 * 1024
@@ -30,8 +31,13 @@
     return (ids == src).astype(jnp.float32)
 
 
-def first_kernel(dims, tiles_ref, rows_hbm, cols_hbm, count_hbm, src_hbm,
-                 send_ref, keep_ref, dense_send_ref, dense_keep_ref,
+def product(dense, panel):
+    prod = jnp.dot(dense, panel, preferred_element_type=jnp.float32)
+    rows = prod.shape[0] // 2
+    return prod[:rows] + prod[rows:]
+
+
+def first_kernel(dims, tiles_ref, rows_hbm, cols_hbm, count_hbm, src_hbm, send_ref, keep_ref, dense_send_ref, dense_keep_ref,
                  held, rows_ref, cols_ref, count_ref, src_ref, total, panel, sems, small):
     n_row, n_col, side = dims
     n_rows = n_col * VB + H
@@ -71,55 +77,63 @@
         chunks = [(0, core * VB, VB)]
         for r in range(n_row):
             chunks.append((VB + r * piece, n_col * VB + (r * n_col + core) * piece, piece))
-        for at, start, size in chunks:
+        for to, start, size in chunks:
             whole = total[pl.ds(pl.multiple_of(start, size), size), :]
             high = whole.astype(jnp.bfloat16)
-            dense[at:at + size] = high
-            dense[half + at:half + at + size] = (whole - high.astype(jnp.float32)).astype(jnp.bfloat16)
-        prod = jnp.dot(dense[...], panel[...], preferred_element_type=jnp.float32)
-        out[...] = prod[:half] + prod[half:]
-
-
-def second_kernel(dims, flips, src_ref, *refs):
+            dense[to:to + size] = high
+            dense[half + to:half + to + size] = (whole - high.astype(jnp.float32)).astype(jnp.bfloat16)
+        out[...] = product(dense[...], panel[...])
+
+
+def score_columns_kernel(dims, *refs):
     n_row, n_col, side = dims
-    n_z = n_row // X
-    mine, theirs, quarters = refs[:X], refs[X:2 * X], refs[2 * X:2 * X + X * n_col]
-    dense_mine, dense_theirs, scores_ref, parts_ref, panel = refs[2 * X + X * n_col:]
+    columns = n_row * VB
+    blocks, (dense_mine, dense_theirs, part_ref, panel) = refs[:4], refs[4:]
+    r = lax.axis_index("row")
+    for at, pair in enumerate((blocks[:2], blocks[2:])):
+        for x, ref in enumerate(pair):
+            for k in range(n_row // X):
+                owner = r ^ (X * k + x)
+                panel[at, pl.ds(pl.multiple_of(owner * VB, VB), VB), :] = ref[k]
+    part_ref[...] = product(dense_mine[:, :columns], panel[0]) + product(dense_theirs[:, :columns], panel[1])
+
+
+def hub_columns_kernel(dims, src_ref, mine_ref, theirs_ref, dense_mine, dense_theirs, part_ref,
+                       scores_ref, parts_ref, panel):
+    n_row, n_col, side = dims
+    columns = n_row * VB
     piece = parts_ref.shape[1]
     r, c = lax.axis_index("row"), lax.axis_index("col")
-    for at, refs_of in enumerate((mine, theirs)):
-        for x, ref in enumerate(refs_of):
-            for k, flip in enumerate(flips):
-                owner = r ^ (X * flip + x)
-                panel[at, pl.ds(pl.multiple_of(owner * VB, VB), VB), :] = ref[k]
-        for k, ref in enumerate(quarters):
-            for i in range(n_z):
-                row = ((r % X ^ (k % X)) * n_z + i) * n_col + (c ^ (k // X))
-                place = pl.ds(pl.multiple_of(n_row * VB + row * piece, piece), piece)
-                panel[at, place, :] = ref[i * piece:(i + 1) * piece]
-    prod = jnp.dot(dense_mine[...], panel[0], preferred_element_type=jnp.float32)
-    prod += jnp.dot(dense_theirs[...], panel[1], preferred_element_type=jnp.float32)
-    half = prod.shape[0] // 2
-    total = prod[:half] + prod[half:]
+    for ref, core in ((mine_ref, c), (theirs_ref, 1 - c)):
+        for i in range(n_row):
+            place = (i * n_col + core) * piece
+            panel[pl.ds(pl.multiple_of(place, piece), piece), :] = ref[i * piece:(i + 1) * piece]
+    total = part_ref[...] + product(dense_mine[:, columns:], panel[...]) + product(dense_theirs[:, columns:], panel[...])
     tele = one_hot(H + (r * n_col + c) * VB, VB, src_ref[...])
     scores_ref[...] = DAMP * total[:VB] + 0.15 * tele
     parts_ref[...] = total[VB:].reshape(parts_ref.shape)
 
 
+def own_scores(dims, src_ref, keep_ref, came_ref):
+    first = H + (lax.axis_index("row") * dims[1] + lax.axis_index("col")) * VB
+    tele = one_hot(first, VB, src_ref[...])
+    return DAMP * (keep_ref[:VB] + came_ref[:VB]) + 0.15 * tele
+
+
 def spread_kernel(dims, src_ref, keep_ref, came_ref, scores_ref, hold_ref, pass_ref):
     quarter = hold_ref.shape[0]
-    r, c = lax.axis_index("row"), lax.axis_index("col")
-    for ref, place in ((hold_ref, r % X), (pass_ref, 1 - r % X)):
+    x = lax.axis_index("row") % X
+    for ref, place in ((hold_ref, x), (pass_ref, 1 - x)):
         spot = pl.ds(pl.multiple_of(VB + place * quarter, quarter), quarter)
         ref[...] = keep_ref[spot, :] + came_ref[spot, :]
-    tele = one_hot(H + (r * dims[1] + c) * VB, VB, src_ref[...])
-    scores_ref[0] = (DAMP * (keep_ref[:VB] + came_ref[:VB]) + 0.15 * tele).astype(scores_ref.dtype)
-
-
-def join_kernel(held_ref, came_ref, out_ref):
-    count = held_ref.shape[0]
-    out_ref[:count] = held_ref[...]
-    out_ref[count:] = came_ref[...]
+    scores_ref[0] = own_scores(dims, src_ref, keep_ref, came_ref).astype(scores_ref.dtype)
+
+
+def join_kernel(*refs):
+    at = 0
+    for ref in refs[:-1]:
+        refs[-1][at:at + ref.shape[0]] = ref[...]
+        at += ref.shape[0]
 
 
 def add_kernel(hold_ref, came_ref, out_ref):
@@ -136,13 +150,20 @@
     out_ref[...] = (DAMP * (held_ref[...] + came_ref[...]) + 0.15 * tele).astype(out_ref.dtype)
 
 
-def last_hubs_kernel(dims, src_ref, parts_ref, out_ref):
-    piece = out_ref.shape[0]
+def side_kernel(mine_ref, theirs_ref, out_ref):
+    part = mine_ref.shape[0]
+    x = lax.axis_index("row") % X
+    for ref, place in ((mine_ref, x), (theirs_ref, 1 - x)):
+        out_ref[pl.ds(pl.multiple_of(place * part, part), part), :] = ref[...]
+
+
+def last_kernel(dims, src_ref, parts_ref, hubs_ref):
+    piece = hubs_ref.shape[0]
     summed = parts_ref[0]
     for k in range(1, parts_ref.shape[0]):
         summed = summed + parts_ref[k]
     first = (lax.axis_index("row") * dims[1] + lax.axis_index("col")) * piece
-    out_ref[...] = DAMP * summed + 0.15 * one_hot(first, piece, src_ref[...])
+    hubs_ref[...] = DAMP * summed + 0.15 * one_hot(first, piece, src_ref[...])
 
 
 def fast_body(tiles, tile_row, tile_col, tile_count, sources):
@@ -167,10 +188,6 @@
 
     def other_side(x):
         return to_partner(x, 1)
-
-    def other_both(x):
-        devices = [(r, c) for r in range(n_row) for c in range(n_col)]
-        return lax.ppermute(x, ("row", "col"), [(r * n_col + c, (r ^ 1) * n_col + 1 - c) for r, c in devices])
 
     def call(kernel, name, out_shape, *args, scratch=(), after=(), cost=0):
         def body(*refs):
@@ -212,40 +229,35 @@
         name="first_terms",
     )(*in_hbm[:3], tile_count.reshape(1), in_hbm[3])
 
-    masks = [n_row // X - 1]
-    while masks[-1] > 1:
-        masks.append(masks[-1] // 2)
     held, hold, away = call(
         bind(spread_kernel, dims), "spread",
         (bf16((1, VB, width)), f32((quarter, width)), f32((quarter, width))),
-        src, keep, other_core(send), cost=2)
+        src, keep, other_core(send), cost=1)
     away = other_side(away)
-    flips = [0]
-    for mask in masks[:-1]:
-        far = to_partner(held, X * mask)
-        held = call(join_kernel, "join_near", bf16((2 * len(flips), VB, width)), held, far, cost=3)
-        flips += [flip ^ mask for flip in flips]
-    far = to_partner(held, X * masks[-1])
-    flips += [flip ^ masks[-1] for flip in flips]
-    near_across, far_across = other_side(held), other_side(far)
-    blocks = bf16((len(flips), VB, width))
-    mine = [call(join_kernel, "join_line", blocks, held, far, cost=12)]
-    theirs = [other_core(mine[0])]
-    mine.append(call(join_kernel, "join_across", blocks, near_across, far_across, cost=12))
-    theirs.append(other_core(mine[1]))
+    next_z, far_z = to_partner(held, X), to_partner(held, 2 * X)
+    last = to_partner(far_z, X)
+    first = call(join_kernel, "join_first", bf16((3, VB, width)), held, next_z, far_z, cost=3)
+    first_across, last_across = other_side(first), other_side(last)
+    line_shape = bf16((n_row // X, VB, width))
     dense_came = other_core(dense_send)
-    sums = call(add_kernel, "plane_sum", f32((quarter, width)), hold, away, cost=2)
-    for mask in masks[:0:-1]:
-        sums = call(add_kernel, "pair_sum", f32((quarter, width)), sums, to_partner(sums, X * mask), cost=8)
-    hub = call(bind(hub_kernel, dims), "hub_sums", bf16((quarter, width)), src, sums, to_partner(sums, X * masks[0]),
-               after=[dense_came, theirs[0]], cost=5)
-    quarters = [hub, other_side(hub), other_core(hub), other_both(hub)]
+    sums = call(add_kernel, "plane_sum", f32((quarter, width)), hold, away, cost=8)
+    sums = call(add_kernel, "pair_sum", f32((quarter, width)), sums, to_partner(sums, X), cost=8)
+    line = call(join_kernel, "join_line", line_shape, first, last, cost=12)
+    line_came = other_core(line)
+    hubs = call(bind(hub_kernel, dims), "hub_sums", bf16((quarter, width)), src, sums, to_partner(sums, 2 * X),
+                after=[dense_came], cost=1)
+    across = call(join_kernel, "join_across", line_shape, first_across, last_across, after=[hubs], cost=2)
+    across_came = other_core(across)
+    hubs = call(side_kernel, "join_sides", bf16((H // n_col, width)), hubs, other_side(hubs), cost=12)
+    part = call(
+        bind(score_columns_kernel, dims), "score_columns", f32((half, width)),
+        line, across, line_came, across_came, dense_keep, dense_came,
+        scratch=[pltpu.VMEM((2, n_row * VB, width), jnp.bfloat16)], cost=20)
     scores, parts = call(
-        bind(second_kernel, dims, flips), "later_terms", (f32((VB, width)), f32((n_row, piece, width))),
-        src, *mine, *theirs, *quarters, dense_keep, dense_came,
-        scratch=[pltpu.VMEM((2, n_cols, width), jnp.bfloat16)])
+        bind(hub_columns_kernel, dims), "hub_columns", (f32((VB, width)), f32((n_row, piece, width))),
+        src, hubs, other_core(hubs), dense_keep, dense_came, part, scratch=[pltpu.VMEM((H, width), jnp.bfloat16)])
     parts = lax.all_to_all(parts, "row", 0, 0)
-    hubs = call(bind(last_hubs_kernel, dims), "last_hubs", f32((piece, width)), src, parts)
+    hubs = call(bind(last_kernel, dims), "last_hubs", f32((piece, width)), src, parts)
     return scores.reshape(1, 1, VB, width), hubs
 
 
@@ -279,7 +291,7 @@
     ).reshape(n_row * VB)
     column_panel = (column_ids[:, None] == sources[None, :]).astype(jnp.bfloat16)
     hub_panel = tele_hubs.astype(jnp.bfloat16)
-    block = CHUNK
+    block = math.gcd(slots, 16)
     own_scores = tele_own
     hub_piece = tele_piece
     for step in range(ITERS):
@@ -332,7 +344,7 @@
         n_row, n_col = mesh.shape["row"], mesh.shape["col"]
         slots, side = tiles.shape[2:4]
         blocks = (n_col * VB + H) * (n_row * VB + H) // (side * side)
-        if ITERS == 2 and n_col == 2 and n_row in (8, 16) and blocks <= slots and H // (n_row * n_col) % 16 == 0:
+        if ITERS == 2 and n_col == 2 and n_row == 4 * X and blocks <= slots and H // (n_row * n_col) % 16 == 0:
             return fast_body(tiles, *rest)
         return plain_body(tiles, *rest)
 

time: 46.4 us -> 43.9 us (0.946)
  blocking collectives: 13.5 us -> 11.9 us
  waiting for transfers between devices: 10.1 us -> 8.71 us
    all_to_all x1, blocking collectives: 13.5 us -> 11.9 us  [fast_body(): parts = lax.all_to_all(parts, 'row', 0, 0)]
    ppermute x8 -> x9, waiting for transfers between devices: 8.43 us -> 7.11 us  [to_partner(): return lax.ppermute(x, 'row', [(r, r ^ flip) for r in range(n_row)])]
    ppermute x8 -> x9, starting transfers between devices: 13.7 us -> 15 us  [to_partner(): return lax.ppermute(x, 'row', [(r, r ^ flip) for r in range(n_row)])]
    ppermute x1 -> x0, starting transfers between devices: 1.07 us -> none  [other_both(): lax.ppermute(x, ('row', 'col'), [(r * n_col + c, (r ^ 1) * n_col + 1 - c)...]
    ppermute x1 -> x0, waiting for transfers between devices: 0.49 us -> none  [other_both(): lax.ppermute(x, ('row', 'col'), [(r * n_col + c, (r ^ 1) * n_col + 1 - c)...]
    pallas_call x9 -> x11, Pallas kernels: 2.35 us -> 2.5 us  [call(): pl.pallas_call(body, out_shape=out_shape, in_specs=[VMEM] * len(args) + [...]
  transfers between devices with their start and end apart: 14 -> 14, of which waited for: 6 -> 7; matrix products, arithmetic and copies ran while one was open for 0% -> 0% of each run, Pallas kernels for 0% -> 2%
where the time goes in v27:
time: 43.9 us; the launch traced here: 43.8 us
  starting transfers between devices  15.7 us (36%)
  blocking collectives  11.9 us (27%)
  waiting for transfers between devices  8.71 us (20%)
  Pallas kernels  6.03 us (14%)
  between operations  1.39 us (3%)
    ppermute x9, starting transfers between devices, to_partner(): return lax.ppermute(x, 'row', [(r, r ^ flip) for r in range(n_row)])  15 us
    all_to_all x1, blocking collectives, fast_body(): parts = lax.all_to_all(parts, 'row', 0, 0)  11.9 us
    ppermute x9, waiting for transfers between devices, to_partner(): return lax.ppermute(x, 'row', [(r, r ^ flip) for r in range(n_row)])  7.11 us
    pallas_call x1, Pallas kernels, fast_body(): pl.pallas_call(bind(first_kernel, dims), out_shape=(f32((half, width)), f...  3.53 us
    pallas_call x11, Pallas kernels, call(): pl.pallas_call(body, out_shape=out_shape, in_specs=[VMEM] * len(args) + [...  2.5 us
    ppermute x5, waiting for transfers between devices, other_core(): return lax.ppermute(x, 'col', [(0, 1), (1, 0)])  1.6 us
  transfers between devices with their start and end apart: 14, of which 7 were waited for; matrix products, arithmetic and copies ran while one was open for 0% of the time, Pallas kernels for 2%

profile of v27, /device:TPU:0, one launch (start us, length us, event | category | flops | bytes accessed | tf_op | source)
XLA Modules:
  0.0 43.8 jit_solution(18202709624131879629)
XLA Ops:
  1.3 0.0 copy-start
  1.3 3.5 %first_terms.1 = (f32[256,256]{1,0:T(8,128)S(1)}, f32[256,256]{1,0:T(8,128)S(1)}, bf16[512,1280]{1,0:T(8,128)(2,1)S(1)}, bf16[512,1280]{1,0:T(8,128)(2,1)S(1)}) custom-call(bf16[96,128,128]{2,1,0:T(8,128)(2,1)} %bitcast.12, s32[96]{0:T(128)} %bitcast.13, s32[96]{0:T(128)} %bitcast.14, s32[1]{0:T(128)} %bitcast.6.count_hbm, s32[1,256]{1,0:T(1,128)} %bitcast.7), custom_call_target="tpu_custom_call" | custom-call | tf_op jit(solution)/shard_map/first_terms/pallas_call | solution.py:212
  4.8 0.5 %collective-permute-start = (f32[256,256]{1,0:T(8,128)S(1)}, f32[256,256]{1,0:T(8,128)S(1)}, u32[]{:S(2)}, u32[]{:S(2)}) collective-permute-start(f32[256,256]{1,0:T(8,128)S(1)} %get-tuple-element.12), channel_id=1, source_target_pairs={{0,1},{1,0},{2,3},{3,2},{4,5},{5,4},{6,7},{7,6},{8,9},{9,8},{10,11... | collective-permute-start | bytes 786440 | tf_op jit(solution)/shard_map/ppermute | solution.py:184
  5.3 1.2 %collective-permute-done.refs_2_ = f32[256,256]{1,0:T(8,128)S(1)} collective-permute-done((f32[256,256]{1,0:T(8,128)S(1)}, f32[256,256]{1,0:T(8,128)S(1)}, u32[]{:S(2)}, u32[]{:S(2)}) %collective-permute-start) | collective-permute-done | bytes 262176 | tf_op jit(solution)/shard_map/ppermute | solution.py:184
  6.5 0.0 copy-done
  6.6 2.9 %collective-permute-start.1 = (f32[64,256]{1,0:T(8,128)S(1)}, f32[64,256]{1,0:T(8,128)S(1)}, u32[]{:S(2)}, u32[]{:S(2)}) collective-permute-start(f32[64,256]{1,0:T(8,128)S(1)} %get-tuple-element.14), channel_id=1, source_target_pairs={{0,2},{2,0},{4,6},{6,4},{8,10},{10,8},{12,14},{14,12},{1,3},{3,1},... | collective-permute-start | bytes 196616 | tf_op jit(solution)/shard_map/ppermute | solution.py:187
  9.5 0.0 collective-permute-start.4
  9.5 1.6 %collective-permute-start.7 = (bf16[1,128,256]{2,1,0:T(8,128)(2,1)S(1)}, bf16[1,128,256]{2,1,0:T(8,128)(2,1)S(1)}, u32[]{:S(2)}, u32[]{:S(2)}) collective-permute-start(bf16[1,128,256]{2,1,0:T(8,128)(2,1)S(1)} %get-tuple-element.17.refs_0_), channel_id=1, source_target_pairs={{0,4},{2,6},{4,0},{6,2},{8,12},{10,14},{12,8},{14,10},{1,5},{3,7},... | collective-permute-start | bytes 196616 | tf_op jit(solution)/shard_map/ppermute | solution.py:187
  11.1 2.6 %collective-permute-start.8 = (bf16[1,128,256]{2,1,0:T(8,128)(2,1)S(1)}, bf16[1,128,256]{2,1,0:T(8,128)(2,1)S(1)}, u32[]{:S(2)}, u32[]{:S(2)}) collective-permute-start(bf16[1,128,256]{2,1,0:T(8,128)(2,1)S(1)} %get-tuple-element.17.refs_0_), channel_id=1, source_target_pairs={{0,8},{2,10},{4,12},{6,14},{8,0},{10,2},{12,4},{14,6},{1,9},{3,11}... | collective-permute-start | bytes 196616 | tf_op jit(solution)/shard_map/ppermute | solution.py:187
  13.7 0.0 collective-permute-done.1.refs_1_
  13.7 0.5 %collective-permute-start.2 = (f32[64,256]{1,0:T(8,128)S(1)}, f32[64,256]{1,0:T(8,128)S(1)}, u32[]{:S(2)}, u32[]{:S(2)}) collective-permute-start(f32[64,256]{1,0:T(8,128)S(1)} %plane_sum.1.refs_0_), channel_id=1, source_target_pairs={{0,4},{2,6},{4,0},{6,2},{8,12},{10,14},{12,8},{14,10},{1,5},{3,7},... | collective-permute-start | bytes 196616 | tf_op jit(solution)/shard_map/ppermute | solution.py:187
  14.2 0.0 collective-permute-done.7.refs_1_
  14.2 3.3 %collective-permute-done.8.refs_2_ = bf16[1,128,256]{2,1,0:T(8,128)(2,1)S(1)} collective-permute-done((bf16[1,128,256]{2,1,0:T(8,128)(2,1)S(1)}, bf16[1,128,256]{2,1,0:T(8,128)(2,1)S(1)}, u32[]{:S(2)}, u32[]{:S(2)}) %collective-permute-start.8) | collective-permute-done | bytes 65568 | tf_op jit(solution)/shard_map/ppermute | solution.py:187
  17.5 0.6 %collective-permute-start.10 = (bf16[3,128,256]{2,1,0:T(8,128)(2,1)S(1)}, bf16[3,128,256]{2,1,0:T(8,128)(2,1)S(1)}, u32[]{:S(2)}, u32[]{:S(2)}) collective-permute-start(bf16[3,128,256]{2,1,0:T(8,128)(2,1)S(1)} %join_first.1.refs_0_), channel_id=1, source_target_pairs={{0,2},{2,0},{4,6},{6,4},{8,10},{10,8},{12,14},{14,12},{1,3},{3,1},... | collective-permute-start | bytes 589832 | tf_op jit(solution)/shard_map/ppermute | solution.py:187
  18.1 0.9 %collective-permute-start.9 = (bf16[1,128,256]{2,1,0:T(8,128)(2,1)S(1)}, bf16[1,128,256]{2,1,0:T(8,128)(2,1)S(1)}, u32[]{:S(2)}, u32[]{:S(2)}) collective-permute-start(bf16[1,128,256]{2,1,0:T(8,128)(2,1)S(1)} %collective-permute-done.8.refs_2_), channel_id=1, source_target_pairs={{0,4},{2,6},{4,0},{6,2},{8,12},{10,14},{12,8},{14,10},{1,5},{3,7},... | collective-permute-start | bytes 196616 | tf_op jit(solution)/shard_map/ppermute | solution.py:187
  19.0 0.0 collective-permute-done.2.refs_1_
  19.0 2.1 %collective-permute-start.3 = (f32[64,256]{1,0:T(8,128)S(1)}, f32[64,256]{1,0:T(8,128)S(1)}, u32[]{:S(2)}, u32[]{:S(2)}) collective-permute-start(f32[64,256]{1,0:T(8,128)S(1)} %pair_sum.1.refs_1_), channel_id=1, source_target_pairs={{0,8},{2,10},{4,12},{6,14},{8,0},{10,2},{12,4},{14,6},{1,9},{3,11}... | collective-permute-start | bytes 196616 | tf_op jit(solution)/shard_map/ppermute | solution.py:187
  21.1 1.2 %collective-permute-done.9.refs_1_ = bf16[1,128,256]{2,1,0:T(8,128)(2,1)S(1)} collective-permute-done((bf16[1,128,256]{2,1,0:T(8,128)(2,1)S(1)}, bf16[1,128,256]{2,1,0:T(8,128)(2,1)S(1)}, u32[]{:S(2)}, u32[]{:S(2)}) %collective-permute-start.9) | collective-permute-done | bytes 65568 | tf_op jit(solution)/shard_map/ppermute | solution.py:187
  22.4 0.1 collective-permute-start.12
  22.5 2.2 %collective-permute-start.11 = (bf16[1,128,256]{2,1,0:T(8,128)(2,1)S(1)}, bf16[1,128,256]{2,1,0:T(8,128)(2,1)S(1)}, u32[]{:S(2)}, u32[]{:S(2)}) collective-permute-start(bf16[1,128,256]{2,1,0:T(8,128)(2,1)S(1)} %collective-permute-done.9.refs_1_), channel_id=1, source_target_pairs={{0,2},{2,0},{4,6},{6,4},{8,10},{10,8},{12,14},{14,12},{1,3},{3,1},... | collective-permute-start | bytes 196616 | tf_op jit(solution)/shard_map/ppermute | solution.py:187
  24.7 0.3 collective-permute-done.3.refs_2_
  24.9 0.0 collective-permute-done.4.refs_3_.refs_5_.refs_4_
  25.0 1.6 %collective-permute-start.5 = (bf16[64,256]{1,0:T(8,128)(2,1)S(1)}, bf16[64,256]{1,0:T(8,128)(2,1)S(1)}, u32[]{:S(2)}, u32[]{:S(2)}) collective-permute-start(bf16[64,256]{1,0:T(8,128)(2,1)S(1)} %hub_sums.1.refs_0_.refs_2_), channel_id=1, source_target_pairs={{0,2},{2,0},{4,6},{6,4},{8,10},{10,8},{12,14},{14,12},{1,3},{3,1},... | collective-permute-start | bytes 98312 | tf_op jit(solution)/shard_map/ppermute | solution.py:187
  26.5 0.8 %collective-permute-done.11.refs_1_ = bf16[1,128,256]{2,1,0:T(8,128)(2,1)S(1)} collective-permute-done((bf16[1,128,256]{2,1,0:T(8,128)(2,1)S(1)}, bf16[1,128,256]{2,1,0:T(8,128)(2,1)S(1)}, u32[]{:S(2)}, u32[]{:S(2)}) %collective-permute-start.11) | collective-permute-done | bytes 65568 | tf_op jit(solution)/shard_map/ppermute | solution.py:187
  27.4 0.0 collective-permute-done.10.refs_0_
  27.4 0.1 collective-permute-start.13
  27.5 1.5 %collective-permute-done.5.refs_1_ = bf16[64,256]{1,0:T(8,128)(2,1)S(1)} collective-permute-done((bf16[64,256]{1,0:T(8,128)(2,1)S(1)}, bf16[64,256]{1,0:T(8,128)(2,1)S(1)}, u32[]{:S(2)}, u32[]{:S(2)}) %collective-permute-start.5) | collective-permute-done | bytes 32800 | tf_op jit(solution)/shard_map/ppermute | solution.py:187
  29.0 0.1 collective-permute-start.6
  29.1 0.0 collective-permute-done.12.refs_2_
  29.1 0.0 collective-permute-done.13.refs_3_
  29.1 0.8 %score_columns.1.refs_5_ = f32[256,256]{1,0:T(8,128)S(1)} custom-call(bf16[4,128,256]{2,1,0:T(8,128)(2,1)S(1)} %join_line.1.refs_0_, bf16[4,128,256]{2,1,0:T(8,128)(2,1)S(1)} %join_across.1.refs_1_, bf16[4,128,256]{2,1,0:T(8,128)(2,1)S(1)} %collective-permute-done.12.refs_2_, bf16[4,128,256]{2,1,0:T(8,128)(2,1)S(1)} %collective-permute-done.13.refs_3_, ...), custom_call_target="tpu_custom_call" | custom-call | flops 20000000000 | tf_op jit(solution)/shard_map/score_columns/pallas_call | solution.py:196
  29.9 0.4 collective-permute-done.6.refs_2_
  30.3 0.9 %hub_columns.1 = (f32[128,256]{1,0:T(8,128)}, f32[8,16,256]{2,1,0:T(8,128)S(1)}) custom-call(s32[1,256]{1,0:T(1,128)S(1)} %bitcast.10, bf16[128,256]{1,0:T(8,128)(2,1)S(1)} %join_sides.1.refs_1_, bf16[128,256]{1,0:T(8,128)(2,1)S(1)} %collective-permute-done.6.refs_2_, bf16[512,1280]{1,0:T(8,128)(2,1)S(1)} %get-tuple-element.16.refs_4_.refs_3_, ...), custom_call_target="tpu_custom_call" | custom-call | tf_op jit(solution)/shard_map/hub_columns/pallas_call | solution.py:196
  31.2 11.9 %all_to_all.5.refs_1_ = f32[8,16,256]{2,1,0:T(8,128)S(1)} all-to-all(f32[8,16,256]{2,1,0:T(8,128)S(1)} %get-tuple-element.19), channel_id=1, replica_groups=mesh['groups'=2,'row'=8,'col'=2] {'row'}, dimensions={0} | all-to-all | bytes 262144 | tf_op jit(solution)/shard_map/all_to_all | solution.py:259
  43.1 0.6 %last_hubs.1 = f32[16,256]{1,0:T(8,128)} custom-call(s32[1,256]{1,0:T(1,128)S(1)} %bitcast.11, f32[8,16,256]{2,1,0:T(8,128)S(1)} %all_to_all.5.refs_1_), custom_call_target="tpu_custom_call" | custom-call | tf_op jit(solution)/shard_map/last_hubs/pallas_call | solution.py:196
  (8 shorter events, 0.2 us)
Async XLA Ops:
  1.3 5.2 %copy-start = (s32[256]{0:T(256)S(1)}, s32[256]{0:T(256)}, u32[]{:S(2)}) copy-start(s32[256]{0:T(256)} %param.9) | copy-start | bytes 3076
  4.8 1.7 %collective-permute-start = (f32[256,256]{1,0:T(8,128)S(1)}, f32[256,256]{1,0:T(8,128)S(1)}, u32[]{:S(2)}, u32[]{:S(2)}) collective-permute-start(f32[256,256]{1,0:T(8,128)S(1)} %get-tuple-element.12), channel_id=1, source_target_pairs={{0,1},{1,0},{2,3},{3,2},{4,5},{5,4},{6,7},{7,6},{8,9},{9,8},{10,11... | collective-permute-start | bytes 786440 | tf_op jit(solution)/shard_map/ppermute | solution.py:184
  6.6 7.1 %collective-permute-start.1 = (f32[64,256]{1,0:T(8,128)S(1)}, f32[64,256]{1,0:T(8,128)S(1)}, u32[]{:S(2)}, u32[]{:S(2)}) collective-permute-start(f32[64,256]{1,0:T(8,128)S(1)} %get-tuple-element.14), channel_id=1, source_target_pairs={{0,2},{2,0},{4,6},{6,4},{8,10},{10,8},{12,14},{14,12},{1,3},{3,1},... | collective-permute-start | bytes 196616 | tf_op jit(solution)/shard_map/ppermute | solution.py:187
  9.5 15.5 %collective-permute-start.4 = (bf16[512,1280]{1,0:T(8,128)(2,1)S(1)}, bf16[512,1280]{1,0:T(8,128)(2,1)S(1)}, u32[]{:S(2)}, u32[]{:S(2)}) collective-permute-start(bf16[512,1280]{1,0:T(8,128)(2,1)S(1)} %get-tuple-element.15), channel_id=1, source_target_pairs={{0,1},{1,0},{2,3},{3,2},{4,5},{5,4},{6,7},{7,6},{8,9},{9,8},{10,11... | collective-permute-start | bytes 3932168 | tf_op jit(solution)/shard_map/ppermute | solution.py:184
  9.5 4.7 %collective-permute-start.7 = (bf16[1,128,256]{2,1,0:T(8,128)(2,1)S(1)}, bf16[1,128,256]{2,1,0:T(8,128)(2,1)S(1)}, u32[]{:S(2)}, u32[]{:S(2)}) collective-permute-start(bf16[1,128,256]{2,1,0:T(8,128)(2,1)S(1)} %get-tuple-element.17.refs_0_), channel_id=1, source_target_pairs={{0,4},{2,6},{4,0},{6,2},{8,12},{10,14},{12,8},{14,10},{1,5},{3,7},... | collective-permute-start | bytes 196616 | tf_op jit(solution)/shard_map/ppermute | solution.py:187
  11.1 6.4 %collective-permute-start.8 = (bf16[1,128,256]{2,1,0:T(8,128)(2,1)S(1)}, bf16[1,128,256]{2,1,0:T(8,128)(2,1)S(1)}, u32[]{:S(2)}, u32[]{:S(2)}) collective-permute-start(bf16[1,128,256]{2,1,0:T(8,128)(2,1)S(1)} %get-tuple-element.17.refs_0_), channel_id=1, source_target_pairs={{0,8},{2,10},{4,12},{6,14},{8,0},{10,2},{12,4},{14,6},{1,9},{3,11}... | collective-permute-start | bytes 196616 | tf_op jit(solution)/shard_map/ppermute | solution.py:187
  13.7 5.3 %collective-permute-start.2 = (f32[64,256]{1,0:T(8,128)S(1)}, f32[64,256]{1,0:T(8,128)S(1)}, u32[]{:S(2)}, u32[]{:S(2)}) collective-permute-start(f32[64,256]{1,0:T(8,128)S(1)} %plane_sum.1.refs_0_), channel_id=1, source_target_pairs={{0,4},{2,6},{4,0},{6,2},{8,12},{10,14},{12,8},{14,10},{1,5},{3,7},... | collective-permute-start | bytes 196616 | tf_op jit(solution)/shard_map/ppermute | solution.py:187
  17.5 9.9 %collective-permute-start.10 = (bf16[3,128,256]{2,1,0:T(8,128)(2,1)S(1)}, bf16[3,128,256]{2,1,0:T(8,128)(2,1)S(1)}, u32[]{:S(2)}, u32[]{:S(2)}) collective-permute-start(bf16[3,128,256]{2,1,0:T(8,128)(2,1)S(1)} %join_first.1.refs_0_), channel_id=1, source_target_pairs={{0,2},{2,0},{4,6},{6,4},{8,10},{10,8},{12,14},{14,12},{1,3},{3,1},... | collective-permute-start | bytes 589832 | tf_op jit(solution)/shard_map/ppermute | solution.py:187
  18.1 4.3 %collective-permute-start.9 = (bf16[1,128,256]{2,1,0:T(8,128)(2,1)S(1)}, bf16[1,128,256]{2,1,0:T(8,128)(2,1)S(1)}, u32[]{:S(2)}, u32[]{:S(2)}) collective-permute-start(bf16[1,128,256]{2,1,0:T(8,128)(2,1)S(1)} %collective-permute-done.8.refs_2_), channel_id=1, source_target_pairs={{0,4},{2,6},{4,0},{6,2},{8,12},{10,14},{12,8},{14,10},{1,5},{3,7},... | collective-permute-start | bytes 196616 | tf_op jit(solution)/shard_map/ppermute | solution.py:187
  19.0 5.9 %collective-permute-start.3 = (f32[64,256]{1,0:T(8,128)S(1)}, f32[64,256]{1,0:T(8,128)S(1)}, u32[]{:S(2)}, u32[]{:S(2)}) collective-permute-start(f32[64,256]{1,0:T(8,128)S(1)} %pair_sum.1.refs_1_), channel_id=1, source_target_pairs={{0,8},{2,10},{4,12},{6,14},{8,0},{10,2},{12,4},{14,6},{1,9},{3,11}... | collective-permute-start | bytes 196616 | tf_op jit(solution)/shard_map/ppermute | solution.py:187
  22.4 6.7 %collective-permute-start.12 = (bf16[4,128,256]{2,1,0:T(8,128)(2,1)S(1)}, bf16[4,128,256]{2,1,0:T(8,128)(2,1)S(1)}, u32[]{:S(2)}, u32[]{:S(2)}) collective-permute-start(bf16[4,128,256]{2,1,0:T(8,128)(2,1)S(1)} %join_line.1.refs_0_), channel_id=1, source_target_pairs={{0,1},{1,0},{2,3},{3,2},{4,5},{5,4},{6,7},{7,6},{8,9},{9,8},{10,11... | collective-permute-start | bytes 786440 | tf_op jit(solution)/shard_map/ppermute | solution.py:184
  22.5 4.9 %collective-permute-start.11 = (bf16[1,128,256]{2,1,0:T(8,128)(2,1)S(1)}, bf16[1,128,256]{2,1,0:T(8,128)(2,1)S(1)}, u32[]{:S(2)}, u32[]{:S(2)}) collective-permute-start(bf16[1,128,256]{2,1,0:T(8,128)(2,1)S(1)} %collective-permute-done.9.refs_1_), channel_id=1, source_target_pairs={{0,2},{2,0},{4,6},{6,4},{8,10},{10,8},{12,14},{14,12},{1,3},{3,1},... | collective-permute-start | bytes 196616 | tf_op jit(solution)/shard_map/ppermute | solution.py:187
  25.0 4.0 %collective-permute-start.5 = (bf16[64,256]{1,0:T(8,128)(2,1)S(1)}, bf16[64,256]{1,0:T(8,128)(2,1)S(1)}, u32[]{:S(2)}, u32[]{:S(2)}) collective-permute-start(bf16[64,256]{1,0:T(8,128)(2,1)S(1)} %hub_sums.1.refs_0_.refs_2_), channel_id=1, source_target_pairs={{0,2},{2,0},{4,6},{6,4},{8,10},{10,8},{12,14},{14,12},{1,3},{3,1},... | collective-permute-start | bytes 98312 | tf_op jit(solution)/shard_map/ppermute | solution.py:187
  27.4 1.7 %collective-permute-start.13 = (bf16[4,128,256]{2,1,0:T(8,128)(2,1)S(1)}, bf16[4,128,256]{2,1,0:T(8,128)(2,1)S(1)}, u32[]{:S(2)}, u32[]{:S(2)}) collective-permute-start(bf16[4,128,256]{2,1,0:T(8,128)(2,1)S(1)} %join_across.1.refs_1_), channel_id=1, source_target_pairs={{0,1},{1,0},{2,3},{3,2},{4,5},{5,4},{6,7},{7,6},{8,9},{9,8},{10,11... | collective-permute-start | bytes 786440 | tf_op jit(solution)/shard_map/ppermute | solution.py:184
  29.0 1.3 %collective-permute-start.6 = (bf16[128,256]{1,0:T(8,128)(2,1)S(1)}, bf16[128,256]{1,0:T(8,128)(2,1)S(1)}, u32[]{:S(2)}, u32[]{:S(2)}) collective-permute-start(bf16[128,256]{1,0:T(8,128)(2,1)S(1)} %join_sides.1.refs_1_), channel_id=1, source_target_pairs={{0,1},{1,0},{2,3},{3,2},{4,5},{5,4},{6,7},{7,6},{8,9},{9,8},{10,11... | collective-permute-start | bytes 196616 | tf_op jit(solution)/shard_map/ppermute | solution.py:184

commit v28 on v27

--- a/solution.py
+++ b/solution.py
@@ -88,13 +88,13 @@
 def score_columns_kernel(dims, *refs):
     n_row, n_col, side = dims
     columns = n_row * VB
-    blocks, (dense_mine, dense_theirs, part_ref, panel) = refs[:4], refs[4:]
+    mine, theirs, dense_mine, dense_theirs, part_ref, panel = refs
     r = lax.axis_index("row")
-    for at, pair in enumerate((blocks[:2], blocks[2:])):
-        for x, ref in enumerate(pair):
-            for k in range(n_row // X):
-                owner = r ^ (X * k + x)
-                panel[at, pl.ds(pl.multiple_of(owner * VB, VB), VB), :] = ref[k]
+    n_z = n_row // X
+    for at, ref in enumerate((mine, theirs)):
+        for k in range(n_row):
+            owner = r ^ (X * (k % n_z) + k // n_z)
+            panel[at, pl.ds(pl.multiple_of(owner * VB, VB), VB), :] = ref[k]
     part_ref[...] = product(dense_mine[:, :columns], panel[0]) + product(dense_theirs[:, :columns], panel[1])
 
 
@@ -232,27 +232,24 @@
     held, hold, away = call(
         bind(spread_kernel, dims), "spread",
         (bf16((1, VB, width)), f32((quarter, width)), f32((quarter, width))),
-        src, keep, other_core(send), cost=1)
+        src, keep, other_core(send), cost=2)
     away = other_side(away)
     next_z, far_z = to_partner(held, X), to_partner(held, 2 * X)
     last = to_partner(far_z, X)
-    first = call(join_kernel, "join_first", bf16((3, VB, width)), held, next_z, far_z, cost=3)
+    first = call(join_kernel, "join_first", bf16((3, VB, width)), held, next_z, far_z, cost=2)
     first_across, last_across = other_side(first), other_side(last)
-    line_shape = bf16((n_row // X, VB, width))
     dense_came = other_core(dense_send)
-    sums = call(add_kernel, "plane_sum", f32((quarter, width)), hold, away, cost=8)
-    sums = call(add_kernel, "pair_sum", f32((quarter, width)), sums, to_partner(sums, X), cost=8)
-    line = call(join_kernel, "join_line", line_shape, first, last, cost=12)
-    line_came = other_core(line)
+    sums = call(add_kernel, "plane_sum", f32((quarter, width)), hold, away, cost=0)
+    sums = call(add_kernel, "pair_sum", f32((quarter, width)), sums, to_partner(sums, X), cost=12)
     hubs = call(bind(hub_kernel, dims), "hub_sums", bf16((quarter, width)), src, sums, to_partner(sums, 2 * X),
-                after=[dense_came], cost=1)
-    across = call(join_kernel, "join_across", line_shape, first_across, last_across, after=[hubs], cost=2)
-    across_came = other_core(across)
+                after=[dense_came], cost=0)
+    blocks = call(join_kernel, "join_blocks", bf16((n_row, VB, width)), first, last, first_across, last_across, after=[hubs], cost=5)
+    blocks_came = other_core(blocks)
     hubs = call(side_kernel, "join_sides", bf16((H // n_col, width)), hubs, other_side(hubs), cost=12)
     part = call(
         bind(score_columns_kernel, dims), "score_columns", f32((half, width)),
-        line, across, line_came, across_came, dense_keep, dense_came,
-        scratch=[pltpu.VMEM((2, n_row * VB, width), jnp.bfloat16)], cost=20)
+        blocks, blocks_came, dense_keep, dense_came,
+        scratch=[pltpu.VMEM((2, n_row * VB, width), jnp.bfloat16)], cost=8)
     scores, parts = call(
         bind(hub_columns_kernel, dims), "hub_columns", (f32((VB, width)), f32((n_row, piece, width))),
         src, hubs, other_core(hubs), dense_keep, dense_came, part, scratch=[pltpu.VMEM((H, width), jnp.bfloat16)])

time: 43.9 us -> 43.7 us (level)
  starting transfers between devices: 15.7 us -> 13.6 us
  waiting for transfers between devices: 8.71 us -> 10 us
  blocking collectives: 11.9 us -> 12.4 us
    ppermute x9, starting transfers between devices: 15 us -> 13 us  [to_partner(): return lax.ppermute(x, 'row', [(r, r ^ flip) for r in range(n_row)])]
    ppermute x9, waiting for transfers between devices: 7.11 us -> 8.3 us  [to_partner(): return lax.ppermute(x, 'row', [(r, r ^ flip) for r in range(n_row)])]
    all_to_all x1, blocking collectives: 11.9 us -> 12.4 us  [fast_body(): parts = lax.all_to_all(parts, 'row', 0, 0)]
    ppermute x5 -> x4, waiting for transfers between devices: 1.6 us -> 1.73 us  [other_core(): return lax.ppermute(x, 'col', [(0, 1), (1, 0)])]
    pallas_call x11 -> x10, Pallas kernels: 2.5 us -> 2.5 us  [call(): pl.pallas_call(body, out_shape=out_shape, in_specs=[VMEM] * len(args) + [...]
  transfers between devices with their start and end apart: 14 -> 13, of which waited for: 7 -> 7; matrix products, arithmetic and copies ran while one was open for 0% -> 0% of each run, Pallas kernels for 2% -> 2%
where the time goes in v28:
time: 43.7 us; the launch traced here: 43.5 us
  starting transfers between devices  13.6 us (31%)
  blocking collectives  12.4 us (28%)
  waiting for transfers between devices  10 us (23%)
  Pallas kernels  6.03 us (14%)
  between operations  1.37 us (3%)
    ppermute x9, starting transfers between devices, to_partner(): return lax.ppermute(x, 'row', [(r, r ^ flip) for r in range(n_row)])  13 us
    all_to_all x1, blocking collectives, fast_body(): parts = lax.all_to_all(parts, 'row', 0, 0)  12.4 us
    ppermute x9, waiting for transfers between devices, to_partner(): return lax.ppermute(x, 'row', [(r, r ^ flip) for r in range(n_row)])  8.3 us
    pallas_call x1, Pallas kernels, fast_body(): pl.pallas_call(bind(first_kernel, dims), out_shape=(f32((half, width)), f...  3.53 us
    pallas_call x10, Pallas kernels, call(): pl.pallas_call(body, out_shape=out_shape, in_specs=[VMEM] * len(args) + [...  2.5 us
    ppermute x4, waiting for transfers between devices, other_core(): return lax.ppermute(x, 'col', [(0, 1), (1, 0)])  1.73 us
  transfers between devices with their start and end apart: 13, of which 7 were waited for; matrix products, arithmetic and copies ran while one was open for 0% of the time, Pallas kernels for 2%

profile of v28, /device:TPU:0, one launch (start us, length us, event | category | flops | bytes accessed | tf_op | source)
XLA Modules:
  0.0 43.5 jit_solution(3597771087062690669)
XLA Ops:
  1.3 0.0 copy-start
  1.3 3.5 %first_terms.1 = (f32[256,256]{1,0:T(8,128)S(1)}, f32[256,256]{1,0:T(8,128)S(1)}, bf16[512,1280]{1,0:T(8,128)(2,1)S(1)}, bf16[512,1280]{1,0:T(8,128)(2,1)S(1)}) custom-call(bf16[96,128,128]{2,1,0:T(8,128)(2,1)} %bitcast.12, s32[96]{0:T(128)} %bitcast.13, s32[96]{0:T(128)} %bitcast.14, s32[1]{0:T(128)} %bitcast.6.count_hbm, s32[1,256]{1,0:T(1,128)} %bitcast.7), custom_call_target="tpu_custom_call" | custom-call | tf_op jit(solution)/shard_map/first_terms/pallas_call | solution.py:212
  4.8 0.5 %collective-permute-start = (f32[256,256]{1,0:T(8,128)S(1)}, f32[256,256]{1,0:T(8,128)S(1)}, u32[]{:S(2)}, u32[]{:S(2)}) collective-permute-start(f32[256,256]{1,0:T(8,128)S(1)} %get-tuple-element.12), channel_id=1, source_target_pairs={{0,1},{1,0},{2,3},{3,2},{4,5},{5,4},{6,7},{7,6},{8,9},{9,8},{10,11... | collective-permute-start | bytes 786440 | tf_op jit(solution)/shard_map/ppermute | solution.py:184
  5.3 1.2 %collective-permute-done.refs_2_ = f32[256,256]{1,0:T(8,128)S(1)} collective-permute-done((f32[256,256]{1,0:T(8,128)S(1)}, f32[256,256]{1,0:T(8,128)S(1)}, u32[]{:S(2)}, u32[]{:S(2)}) %collective-permute-start) | collective-permute-done | bytes 262176 | tf_op jit(solution)/shard_map/ppermute | solution.py:184
  6.5 0.0 copy-done
  6.6 2.9 %collective-permute-start.1 = (f32[64,256]{1,0:T(8,128)S(1)}, f32[64,256]{1,0:T(8,128)S(1)}, u32[]{:S(2)}, u32[]{:S(2)}) collective-permute-start(f32[64,256]{1,0:T(8,128)S(1)} %get-tuple-element.14), channel_id=1, source_target_pairs={{0,2},{2,0},{4,6},{6,4},{8,10},{10,8},{12,14},{14,12},{1,3},{3,1},... | collective-permute-start | bytes 196616 | tf_op jit(solution)/shard_map/ppermute | solution.py:187
  9.5 1.6 %collective-permute-start.7 = (bf16[1,128,256]{2,1,0:T(8,128)(2,1)S(1)}, bf16[1,128,256]{2,1,0:T(8,128)(2,1)S(1)}, u32[]{:S(2)}, u32[]{:S(2)}) collective-permute-start(bf16[1,128,256]{2,1,0:T(8,128)(2,1)S(1)} %get-tuple-element.17.refs_0_), channel_id=1, source_target_pairs={{0,4},{2,6},{4,0},{6,2},{8,12},{10,14},{12,8},{14,10},{1,5},{3,7},... | collective-permute-start | bytes 196616 | tf_op jit(solution)/shard_map/ppermute | solution.py:187
  11.1 2.6 %collective-permute-start.8 = (bf16[1,128,256]{2,1,0:T(8,128)(2,1)S(1)}, bf16[1,128,256]{2,1,0:T(8,128)(2,1)S(1)}, u32[]{:S(2)}, u32[]{:S(2)}) collective-permute-start(bf16[1,128,256]{2,1,0:T(8,128)(2,1)S(1)} %get-tuple-element.17.refs_0_), channel_id=1, source_target_pairs={{0,8},{2,10},{4,12},{6,14},{8,0},{10,2},{12,4},{14,6},{1,9},{3,11}... | collective-permute-start | bytes 196616 | tf_op jit(solution)/shard_map/ppermute | solution.py:187
  13.7 0.0 collective-permute-start.4
  13.7 0.0 collective-permute-done.1.refs_1_
  13.7 0.5 %collective-permute-start.2 = (f32[64,256]{1,0:T(8,128)S(1)}, f32[64,256]{1,0:T(8,128)S(1)}, u32[]{:S(2)}, u32[]{:S(2)}) collective-permute-start(f32[64,256]{1,0:T(8,128)S(1)} %plane_sum.1.refs_0_), channel_id=1, source_target_pairs={{0,4},{2,6},{4,0},{6,2},{8,12},{10,14},{12,8},{14,10},{1,5},{3,7},... | collective-permute-start | bytes 196616 | tf_op jit(solution)/shard_map/ppermute | solution.py:187
  14.2 0.0 collective-permute-done.7.refs_1_
  14.2 2.9 %collective-permute-done.8.refs_2_ = bf16[1,128,256]{2,1,0:T(8,128)(2,1)S(1)} collective-permute-done((bf16[1,128,256]{2,1,0:T(8,128)(2,1)S(1)}, bf16[1,128,256]{2,1,0:T(8,128)(2,1)S(1)}, u32[]{:S(2)}, u32[]{:S(2)}) %collective-permute-start.8) | collective-permute-done | bytes 65568 | tf_op jit(solution)/shard_map/ppermute | solution.py:187
  17.1 0.5 %collective-permute-start.10 = (bf16[3,128,256]{2,1,0:T(8,128)(2,1)S(1)}, bf16[3,128,256]{2,1,0:T(8,128)(2,1)S(1)}, u32[]{:S(2)}, u32[]{:S(2)}) collective-permute-start(bf16[3,128,256]{2,1,0:T(8,128)(2,1)S(1)} %join_first.1.refs_0_), channel_id=1, source_target_pairs={{0,2},{2,0},{4,6},{6,4},{8,10},{10,8},{12,14},{14,12},{1,3},{3,1},... | collective-permute-start | bytes 589832 | tf_op jit(solution)/shard_map/ppermute | solution.py:187
  17.6 0.3 collective-permute-start.9
  18.0 0.6 %collective-permute-done.2.refs_1_ = f32[64,256]{1,0:T(8,128)S(1)} collective-permute-done((f32[64,256]{1,0:T(8,128)S(1)}, f32[64,256]{1,0:T(8,128)S(1)}, u32[]{:S(2)}, u32[]{:S(2)}) %collective-permute-start.2) | collective-permute-done | bytes 65568 | tf_op jit(solution)/shard_map/ppermute | solution.py:187
  18.6 1.7 %collective-permute-start.3 = (f32[64,256]{1,0:T(8,128)S(1)}, f32[64,256]{1,0:T(8,128)S(1)}, u32[]{:S(2)}, u32[]{:S(2)}) collective-permute-start(f32[64,256]{1,0:T(8,128)S(1)} %pair_sum.1.refs_1_), channel_id=1, source_target_pairs={{0,8},{2,10},{4,12},{6,14},{8,0},{10,2},{12,4},{14,6},{1,9},{3,11}... | collective-permute-start | bytes 196616 | tf_op jit(solution)/shard_map/ppermute | solution.py:187
  20.3 1.7 %collective-permute-done.9.refs_1_ = bf16[1,128,256]{2,1,0:T(8,128)(2,1)S(1)} collective-permute-done((bf16[1,128,256]{2,1,0:T(8,128)(2,1)S(1)}, bf16[1,128,256]{2,1,0:T(8,128)(2,1)S(1)}, u32[]{:S(2)}, u32[]{:S(2)}) %collective-permute-start.9) | collective-permute-done | bytes 65568 | tf_op jit(solution)/shard_map/ppermute | solution.py:187
  22.1 2.0 %collective-permute-start.11 = (bf16[1,128,256]{2,1,0:T(8,128)(2,1)S(1)}, bf16[1,128,256]{2,1,0:T(8,128)(2,1)S(1)}, u32[]{:S(2)}, u32[]{:S(2)}) collective-permute-start(bf16[1,128,256]{2,1,0:T(8,128)(2,1)S(1)} %collective-permute-done.9.refs_1_), channel_id=1, source_target_pairs={{0,2},{2,0},{4,6},{6,4},{8,10},{10,8},{12,14},{14,12},{1,3},{3,1},... | collective-permute-start | bytes 196616 | tf_op jit(solution)/shard_map/ppermute | solution.py:187
  24.0 0.0 collective-permute-done.3.refs_2_
  24.0 0.0 collective-permute-done.4.refs_3_.refs_4_
  24.1 0.8 %collective-permute-start.5 = (bf16[64,256]{1,0:T(8,128)(2,1)S(1)}, bf16[64,256]{1,0:T(8,128)(2,1)S(1)}, u32[]{:S(2)}, u32[]{:S(2)}) collective-permute-start(bf16[64,256]{1,0:T(8,128)(2,1)S(1)} %hub_sums.1.refs_0_.refs_4_), channel_id=1, source_target_pairs={{0,2},{2,0},{4,6},{6,4},{8,10},{10,8},{12,14},{14,12},{1,3},{3,1},... | collective-permute-start | bytes 98312 | tf_op jit(solution)/shard_map/ppermute | solution.py:187
  24.9 1.8 %collective-permute-done.11.refs_3_ = bf16[1,128,256]{2,1,0:T(8,128)(2,1)S(1)} collective-permute-done((bf16[1,128,256]{2,1,0:T(8,128)(2,1)S(1)}, bf16[1,128,256]{2,1,0:T(8,128)(2,1)S(1)}, u32[]{:S(2)}, u32[]{:S(2)}) %collective-permute-start.11) | collective-permute-done | bytes 65568 | tf_op jit(solution)/shard_map/ppermute | solution.py:187
  26.7 0.0 collective-permute-done.10.refs_2_
  26.7 0.1 collective-permute-start.12
  26.8 1.2 %collective-permute-done.5.refs_1_ = bf16[64,256]{1,0:T(8,128)(2,1)S(1)} collective-permute-done((bf16[64,256]{1,0:T(8,128)(2,1)S(1)}, bf16[64,256]{1,0:T(8,128)(2,1)S(1)}, u32[]{:S(2)}, u32[]{:S(2)}) %collective-permute-start.5) | collective-permute-done | bytes 32800 | tf_op jit(solution)/shard_map/ppermute | solution.py:187
  28.1 0.1 collective-permute-start.6
  28.1 0.6 %collective-permute-done.12.refs_1_ = bf16[8,128,256]{2,1,0:T(8,128)(2,1)S(1)} collective-permute-done((bf16[8,128,256]{2,1,0:T(8,128)(2,1)S(1)}, bf16[8,128,256]{2,1,0:T(8,128)(2,1)S(1)}, u32[]{:S(2)}, u32[]{:S(2)}) %collective-permute-start.12) | collective-permute-done | bytes 524320 | tf_op jit(solution)/shard_map/ppermute | solution.py:184
  28.7 0.8 %score_columns.1.refs_5_ = f32[256,256]{1,0:T(8,128)S(1)} custom-call(bf16[8,128,256]{2,1,0:T(8,128)(2,1)S(1)} %join_blocks.1.refs_0_, bf16[8,128,256]{2,1,0:T(8,128)(2,1)S(1)} %collective-permute-done.12.refs_1_, bf16[512,1280]{1,0:T(8,128)(2,1)S(1)} %get-tuple-element.16.refs_2_.refs_3_, bf16[512,1280]{1,0:T(8,128)(2,1)S(1)} %collective-permute-done.4.refs_3_.refs_4_), custom_call_target="tpu_custom_call" | custom-call | flops 8000000000 | tf_op jit(solution)/shard_map/score_columns/pallas_call | solution.py:196
  29.5 0.0 collective-permute-done.6.refs_2_
  29.5 0.9 %hub_columns.1 = (f32[128,256]{1,0:T(8,128)}, f32[8,16,256]{2,1,0:T(8,128)S(1)}) custom-call(s32[1,256]{1,0:T(1,128)S(1)} %bitcast.10, bf16[128,256]{1,0:T(8,128)(2,1)S(1)} %join_sides.1.refs_1_, bf16[128,256]{1,0:T(8,128)(2,1)S(1)} %collective-permute-done.6.refs_2_, bf16[512,1280]{1,0:T(8,128)(2,1)S(1)} %get-tuple-element.16.refs_2_.refs_3_, ...), custom_call_target="tpu_custom_call" | custom-call | tf_op jit(solution)/shard_map/hub_columns/pallas_call | solution.py:196
  30.4 12.4 %all_to_all.5.refs_1_ = f32[8,16,256]{2,1,0:T(8,128)S(1)} all-to-all(f32[8,16,256]{2,1,0:T(8,128)S(1)} %get-tuple-element.19), channel_id=1, replica_groups=mesh['groups'=2,'row'=8,'col'=2] {'row'}, dimensions={0} | all-to-all | bytes 262144 | tf_op jit(solution)/shard_map/all_to_all | solution.py:256
  42.9 0.6 %last_hubs.1 = f32[16,256]{1,0:T(8,128)} custom-call(s32[1,256]{1,0:T(1,128)S(1)} %bitcast.11, f32[8,16,256]{2,1,0:T(8,128)S(1)} %all_to_all.5.refs_1_), custom_call_target="tpu_custom_call" | custom-call | tf_op jit(solution)/shard_map/last_hubs/pallas_call | solution.py:196
  (7 shorter events, 0.2 us)
Async XLA Ops:
  1.3 5.2 %copy-start = (s32[256]{0:T(256)S(1)}, s32[256]{0:T(256)}, u32[]{:S(2)}) copy-start(s32[256]{0:T(256)} %param.9) | copy-start | bytes 3076
  4.8 1.7 %collective-permute-start = (f32[256,256]{1,0:T(8,128)S(1)}, f32[256,256]{1,0:T(8,128)S(1)}, u32[]{:S(2)}, u32[]{:S(2)}) collective-permute-start(f32[256,256]{1,0:T(8,128)S(1)} %get-tuple-element.12), channel_id=1, source_target_pairs={{0,1},{1,0},{2,3},{3,2},{4,5},{5,4},{6,7},{7,6},{8,9},{9,8},{10,11... | collective-permute-start | bytes 786440 | tf_op jit(solution)/shard_map/ppermute | solution.py:184
  6.6 7.1 %collective-permute-start.1 = (f32[64,256]{1,0:T(8,128)S(1)}, f32[64,256]{1,0:T(8,128)S(1)}, u32[]{:S(2)}, u32[]{:S(2)}) collective-permute-start(f32[64,256]{1,0:T(8,128)S(1)} %get-tuple-element.14), channel_id=1, source_target_pairs={{0,2},{2,0},{4,6},{6,4},{8,10},{10,8},{12,14},{14,12},{1,3},{3,1},... | collective-permute-start | bytes 196616 | tf_op jit(solution)/shard_map/ppermute | solution.py:187
  9.5 4.7 %collective-permute-start.7 = (bf16[1,128,256]{2,1,0:T(8,128)(2,1)S(1)}, bf16[1,128,256]{2,1,0:T(8,128)(2,1)S(1)}, u32[]{:S(2)}, u32[]{:S(2)}) collective-permute-start(bf16[1,128,256]{2,1,0:T(8,128)(2,1)S(1)} %get-tuple-element.17.refs_0_), channel_id=1, source_target_pairs={{0,4},{2,6},{4,0},{6,2},{8,12},{10,14},{12,8},{14,10},{1,5},{3,7},... | collective-permute-start | bytes 196616 | tf_op jit(solution)/shard_map/ppermute | solution.py:187
  11.1 6.0 %collective-permute-start.8 = (bf16[1,128,256]{2,1,0:T(8,128)(2,1)S(1)}, bf16[1,128,256]{2,1,0:T(8,128)(2,1)S(1)}, u32[]{:S(2)}, u32[]{:S(2)}) collective-permute-start(bf16[1,128,256]{2,1,0:T(8,128)(2,1)S(1)} %get-tuple-element.17.refs_0_), channel_id=1, source_target_pairs={{0,8},{2,10},{4,12},{6,14},{8,0},{10,2},{12,4},{14,6},{1,9},{3,11}... | collective-permute-start | bytes 196616 | tf_op jit(solution)/shard_map/ppermute | solution.py:187
  13.7 10.4 %collective-permute-start.4 = (bf16[512,1280]{1,0:T(8,128)(2,1)S(1)}, bf16[512,1280]{1,0:T(8,128)(2,1)S(1)}, u32[]{:S(2)}, u32[]{:S(2)}) collective-permute-start(bf16[512,1280]{1,0:T(8,128)(2,1)S(1)} %get-tuple-element.15), channel_id=1, source_target_pairs={{0,1},{1,0},{2,3},{3,2},{4,5},{5,4},{6,7},{7,6},{8,9},{9,8},{10,11... | collective-permute-start | bytes 3932168 | tf_op jit(solution)/shard_map/ppermute | solution.py:184
  13.7 4.9 %collective-permute-start.2 = (f32[64,256]{1,0:T(8,128)S(1)}, f32[64,256]{1,0:T(8,128)S(1)}, u32[]{:S(2)}, u32[]{:S(2)}) collective-permute-start(f32[64,256]{1,0:T(8,128)S(1)} %plane_sum.1.refs_0_), channel_id=1, source_target_pairs={{0,4},{2,6},{4,0},{6,2},{8,12},{10,14},{12,8},{14,10},{1,5},{3,7},... | collective-permute-start | bytes 196616 | tf_op jit(solution)/shard_map/ppermute | solution.py:187
  17.1 9.6 %collective-permute-start.10 = (bf16[3,128,256]{2,1,0:T(8,128)(2,1)S(1)}, bf16[3,128,256]{2,1,0:T(8,128)(2,1)S(1)}, u32[]{:S(2)}, u32[]{:S(2)}) collective-permute-start(bf16[3,128,256]{2,1,0:T(8,128)(2,1)S(1)} %join_first.1.refs_0_), channel_id=1, source_target_pairs={{0,2},{2,0},{4,6},{6,4},{8,10},{10,8},{12,14},{14,12},{1,3},{3,1},... | collective-permute-start | bytes 589832 | tf_op jit(solution)/shard_map/ppermute | solution.py:187
  17.6 4.4 %collective-permute-start.9 = (bf16[1,128,256]{2,1,0:T(8,128)(2,1)S(1)}, bf16[1,128,256]{2,1,0:T(8,128)(2,1)S(1)}, u32[]{:S(2)}, u32[]{:S(2)}) collective-permute-start(bf16[1,128,256]{2,1,0:T(8,128)(2,1)S(1)} %collective-permute-done.8.refs_2_), channel_id=1, source_target_pairs={{0,4},{2,6},{4,0},{6,2},{8,12},{10,14},{12,8},{14,10},{1,5},{3,7},... | collective-permute-start | bytes 196616 | tf_op jit(solution)/shard_map/ppermute | solution.py:187
  18.6 5.4 %collective-permute-start.3 = (f32[64,256]{1,0:T(8,128)S(1)}, f32[64,256]{1,0:T(8,128)S(1)}, u32[]{:S(2)}, u32[]{:S(2)}) collective-permute-start(f32[64,256]{1,0:T(8,128)S(1)} %pair_sum.1.refs_1_), channel_id=1, source_target_pairs={{0,8},{2,10},{4,12},{6,14},{8,0},{10,2},{12,4},{14,6},{1,9},{3,11}... | collective-permute-start | bytes 196616 | tf_op jit(solution)/shard_map/ppermute | solution.py:187
  22.1 4.6 %collective-permute-start.11 = (bf16[1,128,256]{2,1,0:T(8,128)(2,1)S(1)}, bf16[1,128,256]{2,1,0:T(8,128)(2,1)S(1)}, u32[]{:S(2)}, u32[]{:S(2)}) collective-permute-start(bf16[1,128,256]{2,1,0:T(8,128)(2,1)S(1)} %collective-permute-done.9.refs_1_), channel_id=1, source_target_pairs={{0,2},{2,0},{4,6},{6,4},{8,10},{10,8},{12,14},{14,12},{1,3},{3,1},... | collective-permute-start | bytes 196616 | tf_op jit(solution)/shard_map/ppermute | solution.py:187
  24.1 4.0 %collective-permute-start.5 = (bf16[64,256]{1,0:T(8,128)(2,1)S(1)}, bf16[64,256]{1,0:T(8,128)(2,1)S(1)}, u32[]{:S(2)}, u32[]{:S(2)}) collective-permute-start(bf16[64,256]{1,0:T(8,128)(2,1)S(1)} %hub_sums.1.refs_0_.refs_4_), channel_id=1, source_target_pairs={{0,2},{2,0},{4,6},{6,4},{8,10},{10,8},{12,14},{14,12},{1,3},{3,1},... | collective-permute-start | bytes 98312 | tf_op jit(solution)/shard_map/ppermute | solution.py:187
  26.7 2.0 %collective-permute-start.12 = (bf16[8,128,256]{2,1,0:T(8,128)(2,1)S(1)}, bf16[8,128,256]{2,1,0:T(8,128)(2,1)S(1)}, u32[]{:S(2)}, u32[]{:S(2)}) collective-permute-start(bf16[8,128,256]{2,1,0:T(8,128)(2,1)S(1)} %join_blocks.1.refs_0_), channel_id=1, source_target_pairs={{0,1},{1,0},{2,3},{3,2},{4,5},{5,4},{6,7},{7,6},{8,9},{9,8},{10,11... | collective-permute-start | bytes 1572872 | tf_op jit(solution)/shard_map/ppermute | solution.py:184
  28.1 1.4 %collective-permute-start.6 = (bf16[128,256]{1,0:T(8,128)(2,1)S(1)}, bf16[128,256]{1,0:T(8,128)(2,1)S(1)}, u32[]{:S(2)}, u32[]{:S(2)}) collective-permute-start(bf16[128,256]{1,0:T(8,128)(2,1)S(1)} %join_sides.1.refs_1_), channel_id=1, source_target_pairs={{0,1},{1,0},{2,3},{3,2},{4,5},{5,4},{6,7},{7,6},{8,9},{9,8},{10,11... | collective-permute-start | bytes 196616 | tf_op jit(solution)/shard_map/ppermute | solution.py:184

commit v29 on v28

--- a/solution.py
+++ b/solution.py
@@ -157,7 +157,8 @@
         out_ref[pl.ds(pl.multiple_of(place * part, part), part), :] = ref[...]
 
 
-def last_kernel(dims, src_ref, parts_ref, hubs_ref):
+def last_kernel(dims, src_ref, held_ref, parts_ref, scores_ref, hubs_ref):
+    scores_ref[...] = held_ref[...]
     piece = hubs_ref.shape[0]
     summed = parts_ref[0]
     for k in range(1, parts_ref.shape[0]):
@@ -254,7 +255,7 @@
         bind(hub_columns_kernel, dims), "hub_columns", (f32((VB, width)), f32((n_row, piece, width))),
         src, hubs, other_core(hubs), dense_keep, dense_came, part, scratch=[pltpu.VMEM((H, width), jnp.bfloat16)])
     parts = lax.all_to_all(parts, "row", 0, 0)
-    hubs = call(bind(last_kernel, dims), "last_hubs", f32((piece, width)), src, parts)
+    scores, hubs = call(bind(last_kernel, dims), "last_hubs", (f32((VB, width)), f32((piece, width))), src, scores, parts)
     return scores.reshape(1, 1, VB, width), hubs
 
 

time: 43.7 us -> 43.1 us (0.986)
  Pallas kernels: 6.03 us -> 5.46 us
    pallas_call x10, Pallas kernels: 2.5 us -> 1.93 us  [call(): pl.pallas_call(body, out_shape=out_shape, in_specs=[VMEM] * len(args) + [...]
where the time goes in v29:
time: 43.1 us; the launch traced here: 42.9 us
  starting transfers between devices  13.6 us (32%)
  blocking collectives  12.4 us (29%)
  waiting for transfers between devices  10 us (23%)
  Pallas kernels  5.46 us (13%)
  between operations  1.38 us (3%)
    ppermute x9, starting transfers between devices, to_partner(): return lax.ppermute(x, 'row', [(r, r ^ flip) for r in range(n_row)])  13 us
    all_to_all x1, blocking collectives, fast_body(): parts = lax.all_to_all(parts, 'row', 0, 0)  12.4 us
    ppermute x9, waiting for transfers between devices, to_partner(): return lax.ppermute(x, 'row', [(r, r ^ flip) for r in range(n_row)])  8.3 us
    pallas_call x1, Pallas kernels, fast_body(): pl.pallas_call(bind(first_kernel, dims), out_shape=(f32((half, width)), f...  3.53 us
    pallas_call x10, Pallas kernels, call(): pl.pallas_call(body, out_shape=out_shape, in_specs=[VMEM] * len(args) + [...  1.93 us
    ppermute x4, waiting for transfers between devices, other_core(): return lax.ppermute(x, 'col', [(0, 1), (1, 0)])  1.73 us
  transfers between devices with their start and end apart: 13, of which 7 were waited for; matrix products, arithmetic and copies ran while one was open for 0% of the time, Pallas kernels for 2%

profile of v29, /device:TPU:0, one launch (start us, length us, event | category | flops | bytes accessed | tf_op | source)
XLA Modules:
  0.0 42.9 jit_solution(841455584086320984)
XLA Ops:
  1.3 0.0 copy-start
  1.3 3.5 %first_terms.1 = (f32[256,256]{1,0:T(8,128)S(1)}, f32[256,256]{1,0:T(8,128)S(1)}, bf16[512,1280]{1,0:T(8,128)(2,1)S(1)}, bf16[512,1280]{1,0:T(8,128)(2,1)S(1)}) custom-call(bf16[96,128,128]{2,1,0:T(8,128)(2,1)} %bitcast.12, s32[96]{0:T(128)} %bitcast.13, s32[96]{0:T(128)} %bitcast.14, s32[1]{0:T(128)} %bitcast.6.count_hbm, s32[1,256]{1,0:T(1,128)} %bitcast.7), custom_call_target="tpu_custom_call" | custom-call | tf_op jit(solution)/shard_map/first_terms/pallas_call | solution.py:213
  4.8 0.5 %collective-permute-start = (f32[256,256]{1,0:T(8,128)S(1)}, f32[256,256]{1,0:T(8,128)S(1)}, u32[]{:S(2)}, u32[]{:S(2)}) collective-permute-start(f32[256,256]{1,0:T(8,128)S(1)} %get-tuple-element.14), channel_id=1, source_target_pairs={{0,1},{1,0},{2,3},{3,2},{4,5},{5,4},{6,7},{7,6},{8,9},{9,8},{10,11... | collective-permute-start | bytes 786440 | tf_op jit(solution)/shard_map/ppermute | solution.py:185
  5.3 1.2 %collective-permute-done.refs_2_ = f32[256,256]{1,0:T(8,128)S(1)} collective-permute-done((f32[256,256]{1,0:T(8,128)S(1)}, f32[256,256]{1,0:T(8,128)S(1)}, u32[]{:S(2)}, u32[]{:S(2)}) %collective-permute-start) | collective-permute-done | bytes 262176 | tf_op jit(solution)/shard_map/ppermute | solution.py:185
  6.5 0.0 copy-done
  6.6 2.9 %collective-permute-start.1 = (f32[64,256]{1,0:T(8,128)S(1)}, f32[64,256]{1,0:T(8,128)S(1)}, u32[]{:S(2)}, u32[]{:S(2)}) collective-permute-start(f32[64,256]{1,0:T(8,128)S(1)} %get-tuple-element.16), channel_id=1, source_target_pairs={{0,2},{2,0},{4,6},{6,4},{8,10},{10,8},{12,14},{14,12},{1,3},{3,1},... | collective-permute-start | bytes 196616 | tf_op jit(solution)/shard_map/ppermute | solution.py:188
  9.5 1.6 %collective-permute-start.7 = (bf16[1,128,256]{2,1,0:T(8,128)(2,1)S(1)}, bf16[1,128,256]{2,1,0:T(8,128)(2,1)S(1)}, u32[]{:S(2)}, u32[]{:S(2)}) collective-permute-start(bf16[1,128,256]{2,1,0:T(8,128)(2,1)S(1)} %get-tuple-element.19.refs_0_), channel_id=1, source_target_pairs={{0,4},{2,6},{4,0},{6,2},{8,12},{10,14},{12,8},{14,10},{1,5},{3,7},... | collective-permute-start | bytes 196616 | tf_op jit(solution)/shard_map/ppermute | solution.py:188
  11.1 2.6 %collective-permute-start.8 = (bf16[1,128,256]{2,1,0:T(8,128)(2,1)S(1)}, bf16[1,128,256]{2,1,0:T(8,128)(2,1)S(1)}, u32[]{:S(2)}, u32[]{:S(2)}) collective-permute-start(bf16[1,128,256]{2,1,0:T(8,128)(2,1)S(1)} %get-tuple-element.19.refs_0_), channel_id=1, source_target_pairs={{0,8},{2,10},{4,12},{6,14},{8,0},{10,2},{12,4},{14,6},{1,9},{3,11}... | collective-permute-start | bytes 196616 | tf_op jit(solution)/shard_map/ppermute | solution.py:188
  13.7 0.0 collective-permute-start.4
  13.7 0.0 collective-permute-done.1.refs_1_
  13.7 0.5 %collective-permute-start.2 = (f32[64,256]{1,0:T(8,128)S(1)}, f32[64,256]{1,0:T(8,128)S(1)}, u32[]{:S(2)}, u32[]{:S(2)}) collective-permute-start(f32[64,256]{1,0:T(8,128)S(1)} %plane_sum.1.refs_0_), channel_id=1, source_target_pairs={{0,4},{2,6},{4,0},{6,2},{8,12},{10,14},{12,8},{14,10},{1,5},{3,7},... | collective-permute-start | bytes 196616 | tf_op jit(solution)/shard_map/ppermute | solution.py:188
  14.2 0.0 collective-permute-done.7.refs_1_
  14.2 2.9 %collective-permute-done.8.refs_2_ = bf16[1,128,256]{2,1,0:T(8,128)(2,1)S(1)} collective-permute-done((bf16[1,128,256]{2,1,0:T(8,128)(2,1)S(1)}, bf16[1,128,256]{2,1,0:T(8,128)(2,1)S(1)}, u32[]{:S(2)}, u32[]{:S(2)}) %collective-permute-start.8) | collective-permute-done | bytes 65568 | tf_op jit(solution)/shard_map/ppermute | solution.py:188
  17.1 0.5 %collective-permute-start.10 = (bf16[3,128,256]{2,1,0:T(8,128)(2,1)S(1)}, bf16[3,128,256]{2,1,0:T(8,128)(2,1)S(1)}, u32[]{:S(2)}, u32[]{:S(2)}) collective-permute-start(bf16[3,128,256]{2,1,0:T(8,128)(2,1)S(1)} %join_first.1.refs_0_), channel_id=1, source_target_pairs={{0,2},{2,0},{4,6},{6,4},{8,10},{10,8},{12,14},{14,12},{1,3},{3,1},... | collective-permute-start | bytes 589832 | tf_op jit(solution)/shard_map/ppermute | solution.py:188
  17.6 0.3 collective-permute-start.9
  18.0 0.6 %collective-permute-done.2.refs_1_ = f32[64,256]{1,0:T(8,128)S(1)} collective-permute-done((f32[64,256]{1,0:T(8,128)S(1)}, f32[64,256]{1,0:T(8,128)S(1)}, u32[]{:S(2)}, u32[]{:S(2)}) %collective-permute-start.2) | collective-permute-done | bytes 65568 | tf_op jit(solution)/shard_map/ppermute | solution.py:188
  18.6 1.7 %collective-permute-start.3 = (f32[64,256]{1,0:T(8,128)S(1)}, f32[64,256]{1,0:T(8,128)S(1)}, u32[]{:S(2)}, u32[]{:S(2)}) collective-permute-start(f32[64,256]{1,0:T(8,128)S(1)} %pair_sum.1.refs_1_), channel_id=1, source_target_pairs={{0,8},{2,10},{4,12},{6,14},{8,0},{10,2},{12,4},{14,6},{1,9},{3,11}... | collective-permute-start | bytes 196616 | tf_op jit(solution)/shard_map/ppermute | solution.py:188
  20.3 1.7 %collective-permute-done.9.refs_1_ = bf16[1,128,256]{2,1,0:T(8,128)(2,1)S(1)} collective-permute-done((bf16[1,128,256]{2,1,0:T(8,128)(2,1)S(1)}, bf16[1,128,256]{2,1,0:T(8,128)(2,1)S(1)}, u32[]{:S(2)}, u32[]{:S(2)}) %collective-permute-start.9) | collective-permute-done | bytes 65568 | tf_op jit(solution)/shard_map/ppermute | solution.py:188
  22.1 2.0 %collective-permute-start.11 = (bf16[1,128,256]{2,1,0:T(8,128)(2,1)S(1)}, bf16[1,128,256]{2,1,0:T(8,128)(2,1)S(1)}, u32[]{:S(2)}, u32[]{:S(2)}) collective-permute-start(bf16[1,128,256]{2,1,0:T(8,128)(2,1)S(1)} %collective-permute-done.9.refs_1_), channel_id=1, source_target_pairs={{0,2},{2,0},{4,6},{6,4},{8,10},{10,8},{12,14},{14,12},{1,3},{3,1},... | collective-permute-start | bytes 196616 | tf_op jit(solution)/shard_map/ppermute | solution.py:188
  24.0 0.0 collective-permute-done.3.refs_2_
  24.0 0.0 collective-permute-done.4.refs_3_.refs_4_
  24.1 0.8 %collective-permute-start.5 = (bf16[64,256]{1,0:T(8,128)(2,1)S(1)}, bf16[64,256]{1,0:T(8,128)(2,1)S(1)}, u32[]{:S(2)}, u32[]{:S(2)}) collective-permute-start(bf16[64,256]{1,0:T(8,128)(2,1)S(1)} %hub_sums.1.refs_0_.refs_4_), channel_id=1, source_target_pairs={{0,2},{2,0},{4,6},{6,4},{8,10},{10,8},{12,14},{14,12},{1,3},{3,1},... | collective-permute-start | bytes 98312 | tf_op jit(solution)/shard_map/ppermute | solution.py:188
  24.9 1.8 %collective-permute-done.11.refs_3_ = bf16[1,128,256]{2,1,0:T(8,128)(2,1)S(1)} collective-permute-done((bf16[1,128,256]{2,1,0:T(8,128)(2,1)S(1)}, bf16[1,128,256]{2,1,0:T(8,128)(2,1)S(1)}, u32[]{:S(2)}, u32[]{:S(2)}) %collective-permute-start.11) | collective-permute-done | bytes 65568 | tf_op jit(solution)/shard_map/ppermute | solution.py:188
  26.7 0.0 collective-permute-done.10.refs_2_
  26.7 0.1 collective-permute-start.12
  26.8 1.2 %collective-permute-done.5.refs_1_ = bf16[64,256]{1,0:T(8,128)(2,1)S(1)} collective-permute-done((bf16[64,256]{1,0:T(8,128)(2,1)S(1)}, bf16[64,256]{1,0:T(8,128)(2,1)S(1)}, u32[]{:S(2)}, u32[]{:S(2)}) %collective-permute-start.5) | collective-permute-done | bytes 32800 | tf_op jit(solution)/shard_map/ppermute | solution.py:188
  28.1 0.1 collective-permute-start.6
  28.1 0.6 %collective-permute-done.12.refs_1_ = bf16[8,128,256]{2,1,0:T(8,128)(2,1)S(1)} collective-permute-done((bf16[8,128,256]{2,1,0:T(8,128)(2,1)S(1)}, bf16[8,128,256]{2,1,0:T(8,128)(2,1)S(1)}, u32[]{:S(2)}, u32[]{:S(2)}) %collective-permute-start.12) | collective-permute-done | bytes 524320 | tf_op jit(solution)/shard_map/ppermute | solution.py:185
  28.7 0.8 %score_columns.1.refs_5_ = f32[256,256]{1,0:T(8,128)S(1)} custom-call(bf16[8,128,256]{2,1,0:T(8,128)(2,1)S(1)} %join_blocks.1.refs_0_, bf16[8,128,256]{2,1,0:T(8,128)(2,1)S(1)} %collective-permute-done.12.refs_1_, bf16[512,1280]{1,0:T(8,128)(2,1)S(1)} %get-tuple-element.18.refs_2_.refs_3_, bf16[512,1280]{1,0:T(8,128)(2,1)S(1)} %collective-permute-done.4.refs_3_.refs_4_), custom_call_target="tpu_custom_call" | custom-call | flops 8000000000 | tf_op jit(solution)/shard_map/score_columns/pallas_call | solution.py:197
  29.5 0.0 collective-permute-done.6.refs_2_
  29.5 0.3 hub_columns.1
  29.8 12.4 %all_to_all.5.refs_2_ = f32[8,16,256]{2,1,0:T(8,128)S(1)} all-to-all(f32[8,16,256]{2,1,0:T(8,128)S(1)} %get-tuple-element.21), channel_id=1, replica_groups=mesh['groups'=2,'row'=8,'col'=2] {'row'}, dimensions={0} | all-to-all | bytes 262144 | tf_op jit(solution)/shard_map/all_to_all | solution.py:257
  42.3 0.7 %last_hubs.1 = (f32[128,256]{1,0:T(8,128)}, f32[16,256]{1,0:T(8,128)}) custom-call(s32[1,256]{1,0:T(1,128)S(1)} %bitcast.11, f32[128,256]{1,0:T(8,128)S(1)} %get-tuple-element.20.refs_1_, f32[8,16,256]{2,1,0:T(8,128)S(1)} %all_to_all.5.refs_2_), custom_call_target="tpu_custom_call" | custom-call | tf_op jit(solution)/shard_map/last_hubs/pallas_call | solution.py:197
  (7 shorter events, 0.2 us)
Async XLA Ops:
  1.3 5.2 %copy-start = (s32[256]{0:T(256)S(1)}, s32[256]{0:T(256)}, u32[]{:S(2)}) copy-start(s32[256]{0:T(256)} %param.9) | copy-start | bytes 3076
  4.8 1.7 %collective-permute-start = (f32[256,256]{1,0:T(8,128)S(1)}, f32[256,256]{1,0:T(8,128)S(1)}, u32[]{:S(2)}, u32[]{:S(2)}) collective-permute-start(f32[256,256]{1,0:T(8,128)S(1)} %get-tuple-element.14), channel_id=1, source_target_pairs={{0,1},{1,0},{2,3},{3,2},{4,5},{5,4},{6,7},{7,6},{8,9},{9,8},{10,11... | collective-permute-start | bytes 786440 | tf_op jit(solution)/shard_map/ppermute | solution.py:185
  6.6 7.1 %collective-permute-start.1 = (f32[64,256]{1,0:T(8,128)S(1)}, f32[64,256]{1,0:T(8,128)S(1)}, u32[]{:S(2)}, u32[]{:S(2)}) collective-permute-start(f32[64,256]{1,0:T(8,128)S(1)} %get-tuple-element.16), channel_id=1, source_target_pairs={{0,2},{2,0},{4,6},{6,4},{8,10},{10,8},{12,14},{14,12},{1,3},{3,1},... | collective-permute-start | bytes 196616 | tf_op jit(solution)/shard_map/ppermute | solution.py:188
  9.5 4.7 %collective-permute-start.7 = (bf16[1,128,256]{2,1,0:T(8,128)(2,1)S(1)}, bf16[1,128,256]{2,1,0:T(8,128)(2,1)S(1)}, u32[]{:S(2)}, u32[]{:S(2)}) collective-permute-start(bf16[1,128,256]{2,1,0:T(8,128)(2,1)S(1)} %get-tuple-element.19.refs_0_), channel_id=1, source_target_pairs={{0,4},{2,6},{4,0},{6,2},{8,12},{10,14},{12,8},{14,10},{1,5},{3,7},... | collective-permute-start | bytes 196616 | tf_op jit(solution)/shard_map/ppermute | solution.py:188
  11.1 6.0 %collective-permute-start.8 = (bf16[1,128,256]{2,1,0:T(8,128)(2,1)S(1)}, bf16[1,128,256]{2,1,0:T(8,128)(2,1)S(1)}, u32[]{:S(2)}, u32[]{:S(2)}) collective-permute-start(bf16[1,128,256]{2,1,0:T(8,128)(2,1)S(1)} %get-tuple-element.19.refs_0_), channel_id=1, source_target_pairs={{0,8},{2,10},{4,12},{6,14},{8,0},{10,2},{12,4},{14,6},{1,9},{3,11}... | collective-permute-start | bytes 196616 | tf_op jit(solution)/shard_map/ppermute | solution.py:188
  13.7 10.4 %collective-permute-start.4 = (bf16[512,1280]{1,0:T(8,128)(2,1)S(1)}, bf16[512,1280]{1,0:T(8,128)(2,1)S(1)}, u32[]{:S(2)}, u32[]{:S(2)}) collective-permute-start(bf16[512,1280]{1,0:T(8,128)(2,1)S(1)} %get-tuple-element.17), channel_id=1, source_target_pairs={{0,1},{1,0},{2,3},{3,2},{4,5},{5,4},{6,7},{7,6},{8,9},{9,8},{10,11... | collective-permute-start | bytes 3932168 | tf_op jit(solution)/shard_map/ppermute | solution.py:185
  13.7 4.9 %collective-permute-start.2 = (f32[64,256]{1,0:T(8,128)S(1)}, f32[64,256]{1,0:T(8,128)S(1)}, u32[]{:S(2)}, u32[]{:S(2)}) collective-permute-start(f32[64,256]{1,0:T(8,128)S(1)} %plane_sum.1.refs_0_), channel_id=1, source_target_pairs={{0,4},{2,6},{4,0},{6,2},{8,12},{10,14},{12,8},{14,10},{1,5},{3,7},... | collective-permute-start | bytes 196616 | tf_op jit(solution)/shard_map/ppermute | solution.py:188
  17.1 9.6 %collective-permute-start.10 = (bf16[3,128,256]{2,1,0:T(8,128)(2,1)S(1)}, bf16[3,128,256]{2,1,0:T(8,128)(2,1)S(1)}, u32[]{:S(2)}, u32[]{:S(2)}) collective-permute-start(bf16[3,128,256]{2,1,0:T(8,128)(2,1)S(1)} %join_first.1.refs_0_), channel_id=1, source_target_pairs={{0,2},{2,0},{4,6},{6,4},{8,10},{10,8},{12,14},{14,12},{1,3},{3,1},... | collective-permute-start | bytes 589832 | tf_op jit(solution)/shard_map/ppermute | solution.py:188
  17.6 4.4 %collective-permute-start.9 = (bf16[1,128,256]{2,1,0:T(8,128)(2,1)S(1)}, bf16[1,128,256]{2,1,0:T(8,128)(2,1)S(1)}, u32[]{:S(2)}, u32[]{:S(2)}) collective-permute-start(bf16[1,128,256]{2,1,0:T(8,128)(2,1)S(1)} %collective-permute-done.8.refs_2_), channel_id=1, source_target_pairs={{0,4},{2,6},{4,0},{6,2},{8,12},{10,14},{12,8},{14,10},{1,5},{3,7},... | collective-permute-start | bytes 196616 | tf_op jit(solution)/shard_map/ppermute | solution.py:188
  18.6 5.4 %collective-permute-start.3 = (f32[64,256]{1,0:T(8,128)S(1)}, f32[64,256]{1,0:T(8,128)S(1)}, u32[]{:S(2)}, u32[]{:S(2)}) collective-permute-start(f32[64,256]{1,0:T(8,128)S(1)} %pair_sum.1.refs_1_), channel_id=1, source_target_pairs={{0,8},{2,10},{4,12},{6,14},{8,0},{10,2},{12,4},{14,6},{1,9},{3,11}... | collective-permute-start | bytes 196616 | tf_op jit(solution)/shard_map/ppermute | solution.py:188
  22.1 4.6 %collective-permute-start.11 = (bf16[1,128,256]{2,1,0:T(8,128)(2,1)S(1)}, bf16[1,128,256]{2,1,0:T(8,128)(2,1)S(1)}, u32[]{:S(2)}, u32[]{:S(2)}) collective-permute-start(bf16[1,128,256]{2,1,0:T(8,128)(2,1)S(1)} %collective-permute-done.9.refs_1_), channel_id=1, source_target_pairs={{0,2},{2,0},{4,6},{6,4},{8,10},{10,8},{12,14},{14,12},{1,3},{3,1},... | collective-permute-start | bytes 196616 | tf_op jit(solution)/shard_map/ppermute | solution.py:188
  24.1 4.0 %collective-permute-start.5 = (bf16[64,256]{1,0:T(8,128)(2,1)S(1)}, bf16[64,256]{1,0:T(8,128)(2,1)S(1)}, u32[]{:S(2)}, u32[]{:S(2)}) collective-permute-start(bf16[64,256]{1,0:T(8,128)(2,1)S(1)} %hub_sums.1.refs_0_.refs_4_), channel_id=1, source_target_pairs={{0,2},{2,0},{4,6},{6,4},{8,10},{10,8},{12,14},{14,12},{1,3},{3,1},... | collective-permute-start | bytes 98312 | tf_op jit(solution)/shard_map/ppermute | solution.py:188
  26.7 2.0 %collective-permute-start.12 = (bf16[8,128,256]{2,1,0:T(8,128)(2,1)S(1)}, bf16[8,128,256]{2,1,0:T(8,128)(2,1)S(1)}, u32[]{:S(2)}, u32[]{:S(2)}) collective-permute-start(bf16[8,128,256]{2,1,0:T(8,128)(2,1)S(1)} %join_blocks.1.refs_0_), channel_id=1, source_target_pairs={{0,1},{1,0},{2,3},{3,2},{4,5},{5,4},{6,7},{7,6},{8,9},{9,8},{10,11... | collective-permute-start | bytes 1572872 | tf_op jit(solution)/shard_map/ppermute | solution.py:185
  28.1 1.4 %collective-permute-start.6 = (bf16[128,256]{1,0:T(8,128)(2,1)S(1)}, bf16[128,256]{1,0:T(8,128)(2,1)S(1)}, u32[]{:S(2)}, u32[]{:S(2)}) collective-permute-start(bf16[128,256]{1,0:T(8,128)(2,1)S(1)} %join_sides.1.refs_1_), channel_id=1, source_target_pairs={{0,1},{1,0},{2,3},{3,2},{4,5},{5,4},{6,7},{7,6},{8,9},{9,8},{10,11... | collective-permute-start | bytes 196616 | tf_op jit(solution)/shard_map/ppermute | solution.py:185

commit v30 on v29

--- a/solution.py
+++ b/solution.py
@@ -233,24 +233,23 @@
     held, hold, away = call(
         bind(spread_kernel, dims), "spread",
         (bf16((1, VB, width)), f32((quarter, width)), f32((quarter, width))),
-        src, keep, other_core(send), cost=2)
+        src, keep, other_core(send), cost=0)
     away = other_side(away)
     next_z, far_z = to_partner(held, X), to_partner(held, 2 * X)
     last = to_partner(far_z, X)
-    first = call(join_kernel, "join_first", bf16((3, VB, width)), held, next_z, far_z, cost=2)
+    first = call(join_kernel, "join_first", bf16((3, VB, width)), held, next_z, far_z, cost=0)
     first_across, last_across = other_side(first), other_side(last)
-    dense_came = other_core(dense_send)
     sums = call(add_kernel, "plane_sum", f32((quarter, width)), hold, away, cost=0)
-    sums = call(add_kernel, "pair_sum", f32((quarter, width)), sums, to_partner(sums, X), cost=12)
-    hubs = call(bind(hub_kernel, dims), "hub_sums", bf16((quarter, width)), src, sums, to_partner(sums, 2 * X),
-                after=[dense_came], cost=0)
-    blocks = call(join_kernel, "join_blocks", bf16((n_row, VB, width)), first, last, first_across, last_across, after=[hubs], cost=5)
+    sums = call(add_kernel, "pair_sum", f32((quarter, width)), sums, to_partner(sums, X), cost=8)
+    dense_came = other_core(call(join_kernel, "pass_dense", dense_shape, dense_send, after=[sums], cost=2))
+    hubs = call(bind(hub_kernel, dims), "hub_sums", bf16((quarter, width)), src, sums, to_partner(sums, 2 * X), cost=0)
+    blocks = call(join_kernel, "join_blocks", bf16((n_row, VB, width)), first, last, first_across, last_across, after=[hubs], cost=12)
     blocks_came = other_core(blocks)
-    hubs = call(side_kernel, "join_sides", bf16((H // n_col, width)), hubs, other_side(hubs), cost=12)
+    hubs = call(side_kernel, "join_sides", bf16((H // n_col, width)), hubs, other_side(hubs), cost=8)
     part = call(
         bind(score_columns_kernel, dims), "score_columns", f32((half, width)),
         blocks, blocks_came, dense_keep, dense_came,
-        scratch=[pltpu.VMEM((2, n_row * VB, width), jnp.bfloat16)], cost=8)
+        scratch=[pltpu.VMEM((2, n_row * VB, width), jnp.bfloat16)], cost=0)
     scores, parts = call(
         bind(hub_columns_kernel, dims), "hub_columns", (f32((VB, width)), f32((n_row, piece, width))),
         src, hubs, other_core(hubs), dense_keep, dense_came, part, scratch=[pltpu.VMEM((H, width), jnp.bfloat16)])

time: 43.1 us -> 42.7 us (level)
  starting transfers between devices: 13.6 us -> 15.2 us
  waiting for transfers between devices: 10 us -> 8.74 us
  blocking collectives: 12.4 us -> 11.6 us
    ppermute x9, waiting for transfers between devices: 8.3 us -> 6.61 us  [to_partner(): return lax.ppermute(x, 'row', [(r, r ^ flip) for r in range(n_row)])]
    ppermute x9, starting transfers between devices: 13 us -> 14.5 us  [to_partner(): return lax.ppermute(x, 'row', [(r, r ^ flip) for r in range(n_row)])]
    all_to_all x1, blocking collectives: 12.4 us -> 11.6 us  [fast_body(): parts = lax.all_to_all(parts, 'row', 0, 0)]
    pallas_call x10 -> x11, Pallas kernels: 1.93 us -> 2.03 us  [call(): pl.pallas_call(body, out_shape=out_shape, in_specs=[VMEM] * len(args) + [...]
where the time goes in v30:
time: 42.7 us; the launch traced here: 42.6 us
  starting transfers between devices  15.2 us (36%)
  blocking collectives  11.6 us (27%)
  waiting for transfers between devices  8.74 us (20%)
  Pallas kernels  5.56 us (13%)
  between operations  1.38 us (3%)
    ppermute x9, starting transfers between devices, to_partner(): return lax.ppermute(x, 'row', [(r, r ^ flip) for r in range(n_row)])  14.5 us
    all_to_all x1, blocking collectives, fast_body(): parts = lax.all_to_all(parts, 'row', 0, 0)  11.6 us
    ppermute x9, waiting for transfers between devices, to_partner(): return lax.ppermute(x, 'row', [(r, r ^ flip) for r in range(n_row)])  6.61 us
    pallas_call x1, Pallas kernels, fast_body(): pl.pallas_call(bind(first_kernel, dims), out_shape=(f32((half, width)), f...  3.53 us
    ppermute x4, waiting for transfers between devices, other_core(): return lax.ppermute(x, 'col', [(0, 1), (1, 0)])  2.13 us
    pallas_call x11, Pallas kernels, call(): pl.pallas_call(body, out_shape=out_shape, in_specs=[VMEM] * len(args) + [...  2.03 us
  transfers between devices with their start and end apart: 13, of which 7 were waited for; matrix products, arithmetic and copies ran while one was open for 0% of the time, Pallas kernels for 2%

profile of v30, /device:TPU:0, one launch (start us, length us, event | category | flops | bytes accessed | tf_op | source)
XLA Modules:
  0.0 42.6 jit_solution(638565008093471706)
XLA Ops:
  1.3 0.0 copy-start
  1.3 3.5 %first_terms.1 = (f32[256,256]{1,0:T(8,128)S(1)}, f32[256,256]{1,0:T(8,128)S(1)}, bf16[512,1280]{1,0:T(8,128)(2,1)S(1)}, bf16[512,1280]{1,0:T(8,128)(2,1)S(1)}) custom-call(bf16[96,128,128]{2,1,0:T(8,128)(2,1)} %bitcast.12, s32[96]{0:T(128)} %bitcast.13, s32[96]{0:T(128)} %bitcast.14, s32[1]{0:T(128)} %bitcast.6.count_hbm, s32[1,256]{1,0:T(1,128)} %bitcast.7), custom_call_target="tpu_custom_call" | custom-call | tf_op jit(solution)/shard_map/first_terms/pallas_call | solution.py:213
  4.8 0.5 %collective-permute-start = (f32[256,256]{1,0:T(8,128)S(1)}, f32[256,256]{1,0:T(8,128)S(1)}, u32[]{:S(2)}, u32[]{:S(2)}) collective-permute-start(f32[256,256]{1,0:T(8,128)S(1)} %get-tuple-element.14), channel_id=1, source_target_pairs={{0,1},{1,0},{2,3},{3,2},{4,5},{5,4},{6,7},{7,6},{8,9},{9,8},{10,11... | collective-permute-start | bytes 786440 | tf_op jit(solution)/shard_map/ppermute | solution.py:185
  5.3 1.2 %collective-permute-done.refs_2_ = f32[256,256]{1,0:T(8,128)S(1)} collective-permute-done((f32[256,256]{1,0:T(8,128)S(1)}, f32[256,256]{1,0:T(8,128)S(1)}, u32[]{:S(2)}, u32[]{:S(2)}) %collective-permute-start) | collective-permute-done | bytes 262176 | tf_op jit(solution)/shard_map/ppermute | solution.py:185
  6.5 0.0 copy-done
  6.5 0.1 spread.1
  6.6 2.9 %collective-permute-start.1 = (f32[64,256]{1,0:T(8,128)S(1)}, f32[64,256]{1,0:T(8,128)S(1)}, u32[]{:S(2)}, u32[]{:S(2)}) collective-permute-start(f32[64,256]{1,0:T(8,128)S(1)} %get-tuple-element.16), channel_id=1, source_target_pairs={{0,2},{2,0},{4,6},{6,4},{8,10},{10,8},{12,14},{14,12},{1,3},{3,1},... | collective-permute-start | bytes 196616 | tf_op jit(solution)/shard_map/ppermute | solution.py:188
  9.5 1.6 %collective-permute-start.7 = (bf16[1,128,256]{2,1,0:T(8,128)(2,1)S(1)}, bf16[1,128,256]{2,1,0:T(8,128)(2,1)S(1)}, u32[]{:S(2)}, u32[]{:S(2)}) collective-permute-start(bf16[1,128,256]{2,1,0:T(8,128)(2,1)S(1)} %get-tuple-element.19.refs_0_), channel_id=1, source_target_pairs={{0,4},{2,6},{4,0},{6,2},{8,12},{10,14},{12,8},{14,10},{1,5},{3,7},... | collective-permute-start | bytes 196616 | tf_op jit(solution)/shard_map/ppermute | solution.py:188
  11.1 2.6 %collective-permute-start.8 = (bf16[1,128,256]{2,1,0:T(8,128)(2,1)S(1)}, bf16[1,128,256]{2,1,0:T(8,128)(2,1)S(1)}, u32[]{:S(2)}, u32[]{:S(2)}) collective-permute-start(bf16[1,128,256]{2,1,0:T(8,128)(2,1)S(1)} %get-tuple-element.19.refs_0_), channel_id=1, source_target_pairs={{0,8},{2,10},{4,12},{6,14},{8,0},{10,2},{12,4},{14,6},{1,9},{3,11}... | collective-permute-start | bytes 196616 | tf_op jit(solution)/shard_map/ppermute | solution.py:188
  13.7 0.0 collective-permute-done.1.refs_1_
  13.7 0.5 %collective-permute-start.2 = (f32[64,256]{1,0:T(8,128)S(1)}, f32[64,256]{1,0:T(8,128)S(1)}, u32[]{:S(2)}, u32[]{:S(2)}) collective-permute-start(f32[64,256]{1,0:T(8,128)S(1)} %plane_sum.1.refs_0_), channel_id=1, source_target_pairs={{0,4},{2,6},{4,0},{6,2},{8,12},{10,14},{12,8},{14,10},{1,5},{3,7},... | collective-permute-start | bytes 196616 | tf_op jit(solution)/shard_map/ppermute | solution.py:188
  14.2 0.0 collective-permute-done.7.refs_1_
  14.2 2.2 %collective-permute-done.8.refs_2_ = bf16[1,128,256]{2,1,0:T(8,128)(2,1)S(1)} collective-permute-done((bf16[1,128,256]{2,1,0:T(8,128)(2,1)S(1)}, bf16[1,128,256]{2,1,0:T(8,128)(2,1)S(1)}, u32[]{:S(2)}, u32[]{:S(2)}) %collective-permute-start.8) | collective-permute-done | bytes 65568 | tf_op jit(solution)/shard_map/ppermute | solution.py:188
  16.4 1.2 %collective-permute-start.10 = (bf16[3,128,256]{2,1,0:T(8,128)(2,1)S(1)}, bf16[3,128,256]{2,1,0:T(8,128)(2,1)S(1)}, u32[]{:S(2)}, u32[]{:S(2)}) collective-permute-start(bf16[3,128,256]{2,1,0:T(8,128)(2,1)S(1)} %join_first.1.refs_0_), channel_id=1, source_target_pairs={{0,2},{2,0},{4,6},{6,4},{8,10},{10,8},{12,14},{14,12},{1,3},{3,1},... | collective-permute-start | bytes 589832 | tf_op jit(solution)/shard_map/ppermute | solution.py:188
  17.6 0.6 %collective-permute-start.9 = (bf16[1,128,256]{2,1,0:T(8,128)(2,1)S(1)}, bf16[1,128,256]{2,1,0:T(8,128)(2,1)S(1)}, u32[]{:S(2)}, u32[]{:S(2)}) collective-permute-start(bf16[1,128,256]{2,1,0:T(8,128)(2,1)S(1)} %collective-permute-done.8.refs_2_), channel_id=1, source_target_pairs={{0,4},{2,6},{4,0},{6,2},{8,12},{10,14},{12,8},{14,10},{1,5},{3,7},... | collective-permute-start | bytes 196616 | tf_op jit(solution)/shard_map/ppermute | solution.py:188
  18.2 0.0 collective-permute-done.2.refs_1_
  18.2 2.1 %collective-permute-start.3 = (f32[64,256]{1,0:T(8,128)S(1)}, f32[64,256]{1,0:T(8,128)S(1)}, u32[]{:S(2)}, u32[]{:S(2)}) collective-permute-start(f32[64,256]{1,0:T(8,128)S(1)} %pair_sum.1.refs_1_), channel_id=1, source_target_pairs={{0,8},{2,10},{4,12},{6,14},{8,0},{10,2},{12,4},{14,6},{1,9},{3,11}... | collective-permute-start | bytes 196616 | tf_op jit(solution)/shard_map/ppermute | solution.py:188
  20.4 2.1 %collective-permute-done.9.refs_1_ = bf16[1,128,256]{2,1,0:T(8,128)(2,1)S(1)} collective-permute-done((bf16[1,128,256]{2,1,0:T(8,128)(2,1)S(1)}, bf16[1,128,256]{2,1,0:T(8,128)(2,1)S(1)}, u32[]{:S(2)}, u32[]{:S(2)}) %collective-permute-start.9) | collective-permute-done | bytes 65568 | tf_op jit(solution)/shard_map/ppermute | solution.py:188
  22.5 0.3 collective-permute-start.11
  22.8 0.1 pass_dense.1
  22.9 0.1 collective-permute-start.6
  22.9 0.5 %collective-permute-done.3.refs_2_ = f32[64,256]{1,0:T(8,128)S(1)} collective-permute-done((f32[64,256]{1,0:T(8,128)S(1)}, f32[64,256]{1,0:T(8,128)S(1)}, u32[]{:S(2)}, u32[]{:S(2)}) %collective-permute-start.3) | collective-permute-done | bytes 65568 | tf_op jit(solution)/shard_map/ppermute | solution.py:188
  23.5 2.7 %collective-permute-start.4 = (bf16[64,256]{1,0:T(8,128)(2,1)S(1)}, bf16[64,256]{1,0:T(8,128)(2,1)S(1)}, u32[]{:S(2)}, u32[]{:S(2)}) collective-permute-start(bf16[64,256]{1,0:T(8,128)(2,1)S(1)} %hub_sums.1.refs_0_.refs_4_), channel_id=1, source_target_pairs={{0,2},{2,0},{4,6},{6,4},{8,10},{10,8},{12,14},{14,12},{1,3},{3,1},... | collective-permute-start | bytes 98312 | tf_op jit(solution)/shard_map/ppermute | solution.py:188
  26.2 0.9 %collective-permute-done.11.refs_3_ = bf16[1,128,256]{2,1,0:T(8,128)(2,1)S(1)} collective-permute-done((bf16[1,128,256]{2,1,0:T(8,128)(2,1)S(1)}, bf16[1,128,256]{2,1,0:T(8,128)(2,1)S(1)}, u32[]{:S(2)}, u32[]{:S(2)}) %collective-permute-start.11) | collective-permute-done | bytes 65568 | tf_op jit(solution)/shard_map/ppermute | solution.py:188
  27.1 0.0 collective-permute-done.10.refs_2_
  27.1 0.1 collective-permute-start.12
  27.2 0.8 %collective-permute-done.4.refs_1_ = bf16[64,256]{1,0:T(8,128)(2,1)S(1)} collective-permute-done((bf16[64,256]{1,0:T(8,128)(2,1)S(1)}, bf16[64,256]{1,0:T(8,128)(2,1)S(1)}, u32[]{:S(2)}, u32[]{:S(2)}) %collective-permute-start.4) | collective-permute-done | bytes 32800 | tf_op jit(solution)/shard_map/ppermute | solution.py:188
  28.1 0.1 collective-permute-start.5
  28.1 1.0 %collective-permute-done.12.refs_1_ = bf16[8,128,256]{2,1,0:T(8,128)(2,1)S(1)} collective-permute-done((bf16[8,128,256]{2,1,0:T(8,128)(2,1)S(1)}, bf16[8,128,256]{2,1,0:T(8,128)(2,1)S(1)}, u32[]{:S(2)}, u32[]{:S(2)}) %collective-permute-start.12) | collective-permute-done | bytes 524320 | tf_op jit(solution)/shard_map/ppermute | solution.py:185
  29.1 0.0 collective-permute-done.6.refs_3_.refs_4_
  29.1 0.8 %score_columns.1.refs_5_ = f32[256,256]{1,0:T(8,128)S(1)} custom-call(bf16[8,128,256]{2,1,0:T(8,128)(2,1)S(1)} %join_blocks.1.refs_0_, bf16[8,128,256]{2,1,0:T(8,128)(2,1)S(1)} %collective-permute-done.12.refs_1_, bf16[512,1280]{1,0:T(8,128)(2,1)S(1)} %get-tuple-element.17.refs_2_.refs_3_, bf16[512,1280]{1,0:T(8,128)(2,1)S(1)} %collective-permute-done.6.refs_3_.refs_4_), custom_call_target="tpu_custom_call" | custom-call | tf_op jit(solution)/shard_map/score_columns/pallas_call | solution.py:197
  29.9 0.0 collective-permute-done.5.refs_2_
  29.9 0.3 hub_columns.1
  30.2 11.6 %all_to_all.5.refs_2_ = f32[8,16,256]{2,1,0:T(8,128)S(1)} all-to-all(f32[8,16,256]{2,1,0:T(8,128)S(1)} %get-tuple-element.21), channel_id=1, replica_groups=mesh['groups'=2,'row'=8,'col'=2] {'row'}, dimensions={0} | all-to-all | bytes 262144 | tf_op jit(solution)/shard_map/all_to_all | solution.py:256
  41.9 0.7 %last_hubs.1 = (f32[128,256]{1,0:T(8,128)}, f32[16,256]{1,0:T(8,128)}) custom-call(s32[1,256]{1,0:T(1,128)S(1)} %bitcast.11, f32[128,256]{1,0:T(8,128)S(1)} %get-tuple-element.20.refs_1_, f32[8,16,256]{2,1,0:T(8,128)S(1)} %all_to_all.5.refs_2_), custom_call_target="tpu_custom_call" | custom-call | tf_op jit(solution)/shard_map/last_hubs/pallas_call | solution.py:197
  (6 shorter events, 0.1 us)
Async XLA Ops:
  1.3 5.2 %copy-start = (s32[256]{0:T(256)S(1)}, s32[256]{0:T(256)}, u32[]{:S(2)}) copy-start(s32[256]{0:T(256)} %param.9) | copy-start | bytes 3076
  4.8 1.7 %collective-permute-start = (f32[256,256]{1,0:T(8,128)S(1)}, f32[256,256]{1,0:T(8,128)S(1)}, u32[]{:S(2)}, u32[]{:S(2)}) collective-permute-start(f32[256,256]{1,0:T(8,128)S(1)} %get-tuple-element.14), channel_id=1, source_target_pairs={{0,1},{1,0},{2,3},{3,2},{4,5},{5,4},{6,7},{7,6},{8,9},{9,8},{10,11... | collective-permute-start | bytes 786440 | tf_op jit(solution)/shard_map/ppermute | solution.py:185
  6.6 7.1 %collective-permute-start.1 = (f32[64,256]{1,0:T(8,128)S(1)}, f32[64,256]{1,0:T(8,128)S(1)}, u32[]{:S(2)}, u32[]{:S(2)}) collective-permute-start(f32[64,256]{1,0:T(8,128)S(1)} %get-tuple-element.16), channel_id=1, source_target_pairs={{0,2},{2,0},{4,6},{6,4},{8,10},{10,8},{12,14},{14,12},{1,3},{3,1},... | collective-permute-start | bytes 196616 | tf_op jit(solution)/shard_map/ppermute | solution.py:188
  9.5 4.7 %collective-permute-start.7 = (bf16[1,128,256]{2,1,0:T(8,128)(2,1)S(1)}, bf16[1,128,256]{2,1,0:T(8,128)(2,1)S(1)}, u32[]{:S(2)}, u32[]{:S(2)}) collective-permute-start(bf16[1,128,256]{2,1,0:T(8,128)(2,1)S(1)} %get-tuple-element.19.refs_0_), channel_id=1, source_target_pairs={{0,4},{2,6},{4,0},{6,2},{8,12},{10,14},{12,8},{14,10},{1,5},{3,7},... | collective-permute-start | bytes 196616 | tf_op jit(solution)/shard_map/ppermute | solution.py:188
  11.1 5.3 %collective-permute-start.8 = (bf16[1,128,256]{2,1,0:T(8,128)(2,1)S(1)}, bf16[1,128,256]{2,1,0:T(8,128)(2,1)S(1)}, u32[]{:S(2)}, u32[]{:S(2)}) collective-permute-start(bf16[1,128,256]{2,1,0:T(8,128)(2,1)S(1)} %get-tuple-element.19.refs_0_), channel_id=1, source_target_pairs={{0,8},{2,10},{4,12},{6,14},{8,0},{10,2},{12,4},{14,6},{1,9},{3,11}... | collective-permute-start | bytes 196616 | tf_op jit(solution)/shard_map/ppermute | solution.py:188
  13.7 4.5 %collective-permute-start.2 = (f32[64,256]{1,0:T(8,128)S(1)}, f32[64,256]{1,0:T(8,128)S(1)}, u32[]{:S(2)}, u32[]{:S(2)}) collective-permute-start(f32[64,256]{1,0:T(8,128)S(1)} %plane_sum.1.refs_0_), channel_id=1, source_target_pairs={{0,4},{2,6},{4,0},{6,2},{8,12},{10,14},{12,8},{14,10},{1,5},{3,7},... | collective-permute-start | bytes 196616 | tf_op jit(solution)/shard_map/ppermute | solution.py:188
  16.4 10.7 %collective-permute-start.10 = (bf16[3,128,256]{2,1,0:T(8,128)(2,1)S(1)}, bf16[3,128,256]{2,1,0:T(8,128)(2,1)S(1)}, u32[]{:S(2)}, u32[]{:S(2)}) collective-permute-start(bf16[3,128,256]{2,1,0:T(8,128)(2,1)S(1)} %join_first.1.refs_0_), channel_id=1, source_target_pairs={{0,2},{2,0},{4,6},{6,4},{8,10},{10,8},{12,14},{14,12},{1,3},{3,1},... | collective-permute-start | bytes 589832 | tf_op jit(solution)/shard_map/ppermute | solution.py:188
  17.6 4.8 %collective-permute-start.9 = (bf16[1,128,256]{2,1,0:T(8,128)(2,1)S(1)}, bf16[1,128,256]{2,1,0:T(8,128)(2,1)S(1)}, u32[]{:S(2)}, u32[]{:S(2)}) collective-permute-start(bf16[1,128,256]{2,1,0:T(8,128)(2,1)S(1)} %collective-permute-done.8.refs_2_), channel_id=1, source_target_pairs={{0,4},{2,6},{4,0},{6,2},{8,12},{10,14},{12,8},{14,10},{1,5},{3,7},... | collective-permute-start | bytes 196616 | tf_op jit(solution)/shard_map/ppermute | solution.py:188
  18.2 5.2 %collective-permute-start.3 = (f32[64,256]{1,0:T(8,128)S(1)}, f32[64,256]{1,0:T(8,128)S(1)}, u32[]{:S(2)}, u32[]{:S(2)}) collective-permute-start(f32[64,256]{1,0:T(8,128)S(1)} %pair_sum.1.refs_1_), channel_id=1, source_target_pairs={{0,8},{2,10},{4,12},{6,14},{8,0},{10,2},{12,4},{14,6},{1,9},{3,11}... | collective-permute-start | bytes 196616 | tf_op jit(solution)/shard_map/ppermute | solution.py:188
  22.5 4.6 %collective-permute-start.11 = (bf16[1,128,256]{2,1,0:T(8,128)(2,1)S(1)}, bf16[1,128,256]{2,1,0:T(8,128)(2,1)S(1)}, u32[]{:S(2)}, u32[]{:S(2)}) collective-permute-start(bf16[1,128,256]{2,1,0:T(8,128)(2,1)S(1)} %collective-permute-done.9.refs_1_), channel_id=1, source_target_pairs={{0,2},{2,0},{4,6},{6,4},{8,10},{10,8},{12,14},{14,12},{1,3},{3,1},... | collective-permute-start | bytes 196616 | tf_op jit(solution)/shard_map/ppermute | solution.py:188
  22.9 6.2 %collective-permute-start.6 = (bf16[512,1280]{1,0:T(8,128)(2,1)S(1)}, bf16[512,1280]{1,0:T(8,128)(2,1)S(1)}, u32[]{:S(2)}, u32[]{:S(2)}) collective-permute-start(bf16[512,1280]{1,0:T(8,128)(2,1)S(1)} %pass_dense.1), channel_id=1, source_target_pairs={{0,1},{1,0},{2,3},{3,2},{4,5},{5,4},{6,7},{7,6},{8,9},{9,8},{10,11... | collective-permute-start | bytes 3932168 | tf_op jit(solution)/shard_map/ppermute | solution.py:185
  23.5 4.6 %collective-permute-start.4 = (bf16[64,256]{1,0:T(8,128)(2,1)S(1)}, bf16[64,256]{1,0:T(8,128)(2,1)S(1)}, u32[]{:S(2)}, u32[]{:S(2)}) collective-permute-start(bf16[64,256]{1,0:T(8,128)(2,1)S(1)} %hub_sums.1.refs_0_.refs_4_), channel_id=1, source_target_pairs={{0,2},{2,0},{4,6},{6,4},{8,10},{10,8},{12,14},{14,12},{1,3},{3,1},... | collective-permute-start | bytes 98312 | tf_op jit(solution)/shard_map/ppermute | solution.py:188
  27.1 2.0 %collective-permute-start.12 = (bf16[8,128,256]{2,1,0:T(8,128)(2,1)S(1)}, bf16[8,128,256]{2,1,0:T(8,128)(2,1)S(1)}, u32[]{:S(2)}, u32[]{:S(2)}) collective-permute-start(bf16[8,128,256]{2,1,0:T(8,128)(2,1)S(1)} %join_blocks.1.refs_0_), channel_id=1, source_target_pairs={{0,1},{1,0},{2,3},{3,2},{4,5},{5,4},{6,7},{7,6},{8,9},{9,8},{10,11... | collective-permute-start | bytes 1572872 | tf_op jit(solution)/shard_map/ppermute | solution.py:185
  28.1 1.8 %collective-permute-start.5 = (bf16[128,256]{1,0:T(8,128)(2,1)S(1)}, bf16[128,256]{1,0:T(8,128)(2,1)S(1)}, u32[]{:S(2)}, u32[]{:S(2)}) collective-permute-start(bf16[128,256]{1,0:T(8,128)(2,1)S(1)} %join_sides.1.refs_1_), channel_id=1, source_target_pairs={{0,1},{1,0},{2,3},{3,2},{4,5},{5,4},{6,7},{7,6},{8,9},{9,8},{10,11... | collective-permute-start | bytes 196616 | tf_op jit(solution)/shard_map/ppermute | solution.py:185

commit v31 on v30

--- a/solution.py
+++ b/solution.py
@@ -37,8 +37,23 @@
     return prod[:rows] + prod[rows:]
 
 
-def first_kernel(dims, tiles_ref, rows_hbm, cols_hbm, count_hbm, src_hbm, send_ref, keep_ref, dense_send_ref, dense_keep_ref,
-                 held, rows_ref, cols_ref, count_ref, src_ref, total, panel, sems, small):
+def half_terms(dims, core, total, panel, out_ref, dense_ref):
+    n_row, n_col, side = dims
+    piece = H // (n_row * n_col)
+    half = out_ref.shape[0]
+    chunks = [(0, core * VB, VB)]
+    for r in range(n_row):
+        chunks.append((VB + r * piece, n_col * VB + (r * n_col + core) * piece, piece))
+    for to, start, size in chunks:
+        whole = total[pl.ds(pl.multiple_of(start, size), size), :]
+        high = whole.astype(jnp.bfloat16)
+        dense_ref[to:to + size] = high
+        dense_ref[half + to:half + to + size] = (whole - high.astype(jnp.float32)).astype(jnp.bfloat16)
+    out_ref[...] = product(dense_ref[...], panel[...])
+
+
+def first_kernel(dims, tiles_ref, rows_hbm, cols_hbm, count_hbm, src_hbm, send_ref, dense_send_ref, total, panel,
+                 held, rows_ref, cols_ref, count_ref, src_ref, sems, small):
     n_row, n_col, side = dims
     n_rows = n_col * VB + H
     piece = H // (n_row * n_col)
@@ -72,17 +87,11 @@
     for i, copy in enumerate(copies):
         copy.wait()
         lax.fori_loop(i * CHUNK, (i + 1) * CHUNK, add_tile, 0, unroll=4)
-    half = n_rows // n_col
-    for dense, out, core in ((dense_send_ref, send_ref, 1 - c), (dense_keep_ref, keep_ref, c)):
-        chunks = [(0, core * VB, VB)]
-        for r in range(n_row):
-            chunks.append((VB + r * piece, n_col * VB + (r * n_col + core) * piece, piece))
-        for to, start, size in chunks:
-            whole = total[pl.ds(pl.multiple_of(start, size), size), :]
-            high = whole.astype(jnp.bfloat16)
-            dense[to:to + size] = high
-            dense[half + to:half + to + size] = (whole - high.astype(jnp.float32)).astype(jnp.bfloat16)
-        out[...] = product(dense[...], panel[...])
+    half_terms(dims, 1 - c, total, panel, send_ref, dense_send_ref)
+
+
+def keep_kernel(dims, total_ref, panel_ref, keep_ref, dense_ref):
+    half_terms(dims, lax.axis_index("col"), total_ref, panel_ref, keep_ref, dense_ref)
 
 
 def score_columns_kernel(dims, *refs):
@@ -210,9 +219,9 @@
     in_hbm = [pltpu.with_memory_space_constraint(x, pltpu.HBM) for x in (
         tiles.reshape(slots, side, side), tile_row.reshape(slots), tile_col.reshape(slots), src)]
     dense_shape = bf16((2 * half, n_cols))
-    send, keep, dense_send, dense_keep = pl.pallas_call(
+    send, dense_send, total, panel = pl.pallas_call(
         bind(first_kernel, dims),
-        out_shape=(f32((half, width)), f32((half, width)), dense_shape, dense_shape),
+        out_shape=(f32((half, width)), dense_shape, f32((n_rows + side, n_cols)), bf16((n_cols, width))),
         in_specs=[HBM] * 5,
         out_specs=[VMEM] * 4,
         scratch_shapes=[
@@ -221,8 +230,6 @@
             pltpu.SMEM((slots,), jnp.int32),
             pltpu.SMEM((1,), jnp.int32),
             pltpu.VMEM((1, width), jnp.int32),
-            pltpu.VMEM((n_rows + side, n_cols), jnp.float32),
-            pltpu.VMEM((n_cols, width), jnp.bfloat16),
             pltpu.SemaphoreType.DMA((slots // CHUNK,)),
             pltpu.SemaphoreType.DMA((4,)),
         ],
@@ -230,6 +237,7 @@
         name="first_terms",
     )(*in_hbm[:3], tile_count.reshape(1), in_hbm[3])
 
+    keep, dense_keep = call(bind(keep_kernel, dims), "keep_terms", (f32((half, width)), dense_shape), total, panel, cost=1)
     held, hold, away = call(
         bind(spread_kernel, dims), "spread",
         (bf16((1, VB, width)), f32((quarter, width)), f32((quarter, width))),

time: 42.7 us -> 41.8 us (0.979)
  blocking collectives: 11.6 us -> 10.9 us
    ppermute x9, waiting for transfers between devices: 6.61 us -> 7.82 us  [to_partner(): return lax.ppermute(x, 'row', [(r, r ^ flip) for r in range(n_row)])]
    ppermute x4, waiting for transfers between devices: 2.13 us -> 1.07 us  [other_core(): return lax.ppermute(x, 'col', [(0, 1), (1, 0)])]
    all_to_all x1, blocking collectives: 11.6 us -> 10.9 us  [fast_body(): parts = lax.all_to_all(parts, 'row', 0, 0)]
    pallas_call x1, Pallas kernels: 3.53 us -> 2.98 us  [fast_body(): pl.pallas_call(bind(first_kernel, dims), out_shape=(f32((half, width)), d...]
    pallas_call x11 -> x12, Pallas kernels: 2.03 us -> 2.53 us  [call(): pl.pallas_call(body, out_shape=out_shape, in_specs=[VMEM] * len(args) + [...]
  transfers between devices with their start and end apart: 13 -> 13, of which waited for: 7 -> 7; matrix products, arithmetic and copies ran while one was open for 0% -> 0% of each run, Pallas kernels for 2% -> 4%
where the time goes in v31:
time: 41.8 us; the launch traced here: 41.7 us
  starting transfers between devices  15 us (36%)
  blocking collectives  10.9 us (26%)
  waiting for transfers between devices  8.89 us (21%)
  Pallas kernels  5.5 us (13%)
  between operations  1.39 us (3%)
    ppermute x9, starting transfers between devices, to_partner(): return lax.ppermute(x, 'row', [(r, r ^ flip) for r in range(n_row)])  14.3 us
    all_to_all x1, blocking collectives, fast_body(): parts = lax.all_to_all(parts, 'row', 0, 0)  10.9 us
    ppermute x9, waiting for transfers between devices, to_partner(): return lax.ppermute(x, 'row', [(r, r ^ flip) for r in range(n_row)])  7.82 us
    pallas_call x1, Pallas kernels, fast_body(): pl.pallas_call(bind(first_kernel, dims), out_shape=(f32((half, width)), d...  2.98 us
    pallas_call x12, Pallas kernels, call(): pl.pallas_call(body, out_shape=out_shape, in_specs=[VMEM] * len(args) + [...  2.53 us
    ppermute x4, waiting for transfers between devices, other_core(): return lax.ppermute(x, 'col', [(0, 1), (1, 0)])  1.07 us
  transfers between devices with their start and end apart: 13, of which 7 were waited for; matrix products, arithmetic and copies ran while one was open for 0% of the time, Pallas kernels for 4%

profile of v31, /device:TPU:0, one launch (start us, length us, event | category | flops | bytes accessed | tf_op | source)
XLA Modules:
  0.0 41.7 jit_solution(2266675532829687636)
XLA Ops:
  1.3 3.0 %first_terms.1 = (f32[256,256]{1,0:T(8,128)S(1)}, bf16[512,1280]{1,0:T(8,128)(2,1)S(1)}, f32[640,1280]{1,0:T(8,128)S(1)}, bf16[1280,256]{1,0:T(8,128)(2,1)S(1)}) custom-call(bf16[96,128,128]{2,1,0:T(8,128)(2,1)} %bitcast.12, s32[96]{0:T(128)} %bitcast.13, s32[96]{0:T(128)} %bitcast.14, s32[1]{0:T(128)} %bitcast.6.count_hbm, s32[1,256]{1,0:T(1,128)} %bitcast.7), custom_call_target="tpu_custom_call" | custom-call | tf_op jit(solution)/shard_map/first_terms/pallas_call | solution.py:222
  4.3 0.5 %collective-permute-start = (f32[256,256]{1,0:T(8,128)S(1)}, f32[256,256]{1,0:T(8,128)S(1)}, u32[]{:S(2)}, u32[]{:S(2)}) collective-permute-start(f32[256,256]{1,0:T(8,128)S(1)} %get-tuple-element.18), channel_id=1, source_target_pairs={{0,1},{1,0},{2,3},{3,2},{4,5},{5,4},{6,7},{7,6},{8,9},{9,8},{10,11... | collective-permute-start | bytes 786440 | tf_op jit(solution)/shard_map/ppermute | solution.py:194
  4.8 0.0 copy-start
  4.8 0.5 %keep_terms.1 = (f32[256,256]{1,0:T(8,128)S(1)}, bf16[512,1280]{1,0:T(8,128)(2,1)S(1)}) custom-call(f32[640,1280]{1,0:T(8,128)S(1)} %get-tuple-element.15.refs_0_, bf16[1280,256]{1,0:T(8,128)(2,1)S(1)} %get-tuple-element.16.refs_1_), custom_call_target="tpu_custom_call" | custom-call | flops 1000000000 | tf_op jit(solution)/shard_map/keep_terms/pallas_call | solution.py:206
  5.3 0.6 %collective-permute-done.refs_2_ = f32[256,256]{1,0:T(8,128)S(1)} collective-permute-done((f32[256,256]{1,0:T(8,128)S(1)}, f32[256,256]{1,0:T(8,128)S(1)}, u32[]{:S(2)}, u32[]{:S(2)}) %collective-permute-start) | collective-permute-done | bytes 262176 | tf_op jit(solution)/shard_map/ppermute | solution.py:194
  5.9 0.0 copy-done
  6.0 2.9 %collective-permute-start.1 = (f32[64,256]{1,0:T(8,128)S(1)}, f32[64,256]{1,0:T(8,128)S(1)}, u32[]{:S(2)}, u32[]{:S(2)}) collective-permute-start(f32[64,256]{1,0:T(8,128)S(1)} %get-tuple-element.20), channel_id=1, source_target_pairs={{0,2},{2,0},{4,6},{6,4},{8,10},{10,8},{12,14},{14,12},{1,3},{3,1},... | collective-permute-start | bytes 196616 | tf_op jit(solution)/shard_map/ppermute | solution.py:197
  8.9 2.6 %collective-permute-start.8 = (bf16[1,128,256]{2,1,0:T(8,128)(2,1)S(1)}, bf16[1,128,256]{2,1,0:T(8,128)(2,1)S(1)}, u32[]{:S(2)}, u32[]{:S(2)}) collective-permute-start(bf16[1,128,256]{2,1,0:T(8,128)(2,1)S(1)} %get-tuple-element.23.refs_0_), channel_id=1, source_target_pairs={{0,8},{2,10},{4,12},{6,14},{8,0},{10,2},{12,4},{14,6},{1,9},{3,11}... | collective-permute-start | bytes 196616 | tf_op jit(solution)/shard_map/ppermute | solution.py:197
  11.5 1.6 %collective-permute-start.7 = (bf16[1,128,256]{2,1,0:T(8,128)(2,1)S(1)}, bf16[1,128,256]{2,1,0:T(8,128)(2,1)S(1)}, u32[]{:S(2)}, u32[]{:S(2)}) collective-permute-start(bf16[1,128,256]{2,1,0:T(8,128)(2,1)S(1)} %get-tuple-element.23.refs_0_), channel_id=1, source_target_pairs={{0,4},{2,6},{4,0},{6,2},{8,12},{10,14},{12,8},{14,10},{1,5},{3,7},... | collective-permute-start | bytes 196616 | tf_op jit(solution)/shard_map/ppermute | solution.py:197
  13.1 0.0 collective-permute-done.1.refs_1_
  13.1 0.5 %collective-permute-start.2 = (f32[64,256]{1,0:T(8,128)S(1)}, f32[64,256]{1,0:T(8,128)S(1)}, u32[]{:S(2)}, u32[]{:S(2)}) collective-permute-start(f32[64,256]{1,0:T(8,128)S(1)} %plane_sum.1.refs_0_), channel_id=1, source_target_pairs={{0,4},{2,6},{4,0},{6,2},{8,12},{10,14},{12,8},{14,10},{1,5},{3,7},... | collective-permute-start | bytes 196616 | tf_op jit(solution)/shard_map/ppermute | solution.py:197
  13.6 1.3 %collective-permute-done.8.refs_2_ = bf16[1,128,256]{2,1,0:T(8,128)(2,1)S(1)} collective-permute-done((bf16[1,128,256]{2,1,0:T(8,128)(2,1)S(1)}, bf16[1,128,256]{2,1,0:T(8,128)(2,1)S(1)}, u32[]{:S(2)}, u32[]{:S(2)}) %collective-permute-start.8) | collective-permute-done | bytes 65568 | tf_op jit(solution)/shard_map/ppermute | solution.py:197
  15.0 1.5 %collective-permute-done.7.refs_1_ = bf16[1,128,256]{2,1,0:T(8,128)(2,1)S(1)} collective-permute-done((bf16[1,128,256]{2,1,0:T(8,128)(2,1)S(1)}, bf16[1,128,256]{2,1,0:T(8,128)(2,1)S(1)}, u32[]{:S(2)}, u32[]{:S(2)}) %collective-permute-start.7) | collective-permute-done | bytes 65568 | tf_op jit(solution)/shard_map/ppermute | solution.py:197
  16.5 0.6 %collective-permute-start.10 = (bf16[3,128,256]{2,1,0:T(8,128)(2,1)S(1)}, bf16[3,128,256]{2,1,0:T(8,128)(2,1)S(1)}, u32[]{:S(2)}, u32[]{:S(2)}) collective-permute-start(bf16[3,128,256]{2,1,0:T(8,128)(2,1)S(1)} %join_first.1.refs_0_), channel_id=1, source_target_pairs={{0,2},{2,0},{4,6},{6,4},{8,10},{10,8},{12,14},{14,12},{1,3},{3,1},... | collective-permute-start | bytes 589832 | tf_op jit(solution)/shard_map/ppermute | solution.py:197
  17.1 1.4 %collective-permute-start.9 = (bf16[1,128,256]{2,1,0:T(8,128)(2,1)S(1)}, bf16[1,128,256]{2,1,0:T(8,128)(2,1)S(1)}, u32[]{:S(2)}, u32[]{:S(2)}) collective-permute-start(bf16[1,128,256]{2,1,0:T(8,128)(2,1)S(1)} %collective-permute-done.8.refs_2_), channel_id=1, source_target_pairs={{0,4},{2,6},{4,0},{6,2},{8,12},{10,14},{12,8},{14,10},{1,5},{3,7},... | collective-permute-start | bytes 196616 | tf_op jit(solution)/shard_map/ppermute | solution.py:197
  18.5 0.0 collective-permute-done.2.refs_1_
  18.5 1.4 %collective-permute-start.3 = (f32[64,256]{1,0:T(8,128)S(1)}, f32[64,256]{1,0:T(8,128)S(1)}, u32[]{:S(2)}, u32[]{:S(2)}) collective-permute-start(f32[64,256]{1,0:T(8,128)S(1)} %pair_sum.1.refs_1_), channel_id=1, source_target_pairs={{0,8},{2,10},{4,12},{6,14},{8,0},{10,2},{12,4},{14,6},{1,9},{3,11}... | collective-permute-start | bytes 196616 | tf_op jit(solution)/shard_map/ppermute | solution.py:197
  19.9 1.6 %collective-permute-done.9.refs_1_ = bf16[1,128,256]{2,1,0:T(8,128)(2,1)S(1)} collective-permute-done((bf16[1,128,256]{2,1,0:T(8,128)(2,1)S(1)}, bf16[1,128,256]{2,1,0:T(8,128)(2,1)S(1)}, u32[]{:S(2)}, u32[]{:S(2)}) %collective-permute-start.9) | collective-permute-done | bytes 65568 | tf_op jit(solution)/shard_map/ppermute | solution.py:197
  21.5 1.7 %collective-permute-start.11 = (bf16[1,128,256]{2,1,0:T(8,128)(2,1)S(1)}, bf16[1,128,256]{2,1,0:T(8,128)(2,1)S(1)}, u32[]{:S(2)}, u32[]{:S(2)}) collective-permute-start(bf16[1,128,256]{2,1,0:T(8,128)(2,1)S(1)} %collective-permute-done.9.refs_1_), channel_id=1, source_target_pairs={{0,2},{2,0},{4,6},{6,4},{8,10},{10,8},{12,14},{14,12},{1,3},{3,1},... | collective-permute-start | bytes 196616 | tf_op jit(solution)/shard_map/ppermute | solution.py:197
  23.2 0.1 pass_dense.1
  23.3 0.1 collective-permute-start.6
  23.4 1.1 %collective-permute-done.3.refs_2_ = f32[64,256]{1,0:T(8,128)S(1)} collective-permute-done((f32[64,256]{1,0:T(8,128)S(1)}, f32[64,256]{1,0:T(8,128)S(1)}, u32[]{:S(2)}, u32[]{:S(2)}) %collective-permute-start.3) | collective-permute-done | bytes 65568 | tf_op jit(solution)/shard_map/ppermute | solution.py:197
  24.5 1.6 %collective-permute-start.4 = (bf16[64,256]{1,0:T(8,128)(2,1)S(1)}, bf16[64,256]{1,0:T(8,128)(2,1)S(1)}, u32[]{:S(2)}, u32[]{:S(2)}) collective-permute-start(bf16[64,256]{1,0:T(8,128)(2,1)S(1)} %hub_sums.1.refs_0_.refs_4_), channel_id=1, source_target_pairs={{0,2},{2,0},{4,6},{6,4},{8,10},{10,8},{12,14},{14,12},{1,3},{3,1},... | collective-permute-start | bytes 98312 | tf_op jit(solution)/shard_map/ppermute | solution.py:197
  26.0 0.0 collective-permute-done.11.refs_3_
  26.0 0.0 collective-permute-done.10.refs_2_
  26.1 0.1 collective-permute-start.12
  26.2 2.3 %collective-permute-done.4.refs_1_ = bf16[64,256]{1,0:T(8,128)(2,1)S(1)} collective-permute-done((bf16[64,256]{1,0:T(8,128)(2,1)S(1)}, bf16[64,256]{1,0:T(8,128)(2,1)S(1)}, u32[]{:S(2)}, u32[]{:S(2)}) %collective-permute-start.4) | collective-permute-done | bytes 32800 | tf_op jit(solution)/shard_map/ppermute | solution.py:197
  28.5 0.1 collective-permute-start.5
  28.6 0.0 collective-permute-done.12.refs_1_
  28.6 0.0 collective-permute-done.6.refs_3_.refs_4_
  28.6 0.8 %score_columns.1.refs_5_ = f32[256,256]{1,0:T(8,128)S(1)} custom-call(bf16[8,128,256]{2,1,0:T(8,128)(2,1)S(1)} %join_blocks.1.refs_0_, bf16[8,128,256]{2,1,0:T(8,128)(2,1)S(1)} %collective-permute-done.12.refs_1_, bf16[512,1280]{1,0:T(8,128)(2,1)S(1)} %get-tuple-element.21.refs_2_.refs_3_, bf16[512,1280]{1,0:T(8,128)(2,1)S(1)} %collective-permute-done.6.refs_3_.refs_4_), custom_call_target="tpu_custom_call" | custom-call | tf_op jit(solution)/shard_map/score_columns/pallas_call | solution.py:206
  29.4 0.4 %collective-permute-done.5.refs_2_ = bf16[128,256]{1,0:T(8,128)(2,1)S(1)} collective-permute-done((bf16[128,256]{1,0:T(8,128)(2,1)S(1)}, bf16[128,256]{1,0:T(8,128)(2,1)S(1)}, u32[]{:S(2)}, u32[]{:S(2)}) %collective-permute-start.5) | collective-permute-done | bytes 65568 | tf_op jit(solution)/shard_map/ppermute | solution.py:194
  29.8 0.3 hub_columns.1
  30.1 10.9 %all_to_all.5.refs_2_ = f32[8,16,256]{2,1,0:T(8,128)S(1)} all-to-all(f32[8,16,256]{2,1,0:T(8,128)S(1)} %get-tuple-element.25), channel_id=1, replica_groups=mesh['groups'=2,'row'=8,'col'=2] {'row'}, dimensions={0} | all-to-all | bytes 262144 | tf_op jit(solution)/shard_map/all_to_all | solution.py:264
  41.0 0.7 %last_hubs.1 = (f32[128,256]{1,0:T(8,128)}, f32[16,256]{1,0:T(8,128)}) custom-call(s32[1,256]{1,0:T(1,128)S(1)} %bitcast.11, f32[128,256]{1,0:T(8,128)S(1)} %get-tuple-element.24.refs_1_, f32[8,16,256]{2,1,0:T(8,128)S(1)} %all_to_all.5.refs_2_), custom_call_target="tpu_custom_call" | custom-call | tf_op jit(solution)/shard_map/last_hubs/pallas_call | solution.py:206
  (7 shorter events, 0.2 us)
Async XLA Ops:
  4.3 1.7 %collective-permute-start = (f32[256,256]{1,0:T(8,128)S(1)}, f32[256,256]{1,0:T(8,128)S(1)}, u32[]{:S(2)}, u32[]{:S(2)}) collective-permute-start(f32[256,256]{1,0:T(8,128)S(1)} %get-tuple-element.18), channel_id=1, source_target_pairs={{0,1},{1,0},{2,3},{3,2},{4,5},{5,4},{6,7},{7,6},{8,9},{9,8},{10,11... | collective-permute-start | bytes 786440 | tf_op jit(solution)/shard_map/ppermute | solution.py:194
  4.8 1.2 %copy-start = (s32[256]{0:T(256)S(1)}, s32[256]{0:T(256)}, u32[]{:S(2)}) copy-start(s32[256]{0:T(256)} %param.9) | copy-start | bytes 3076
  6.0 7.1 %collective-permute-start.1 = (f32[64,256]{1,0:T(8,128)S(1)}, f32[64,256]{1,0:T(8,128)S(1)}, u32[]{:S(2)}, u32[]{:S(2)}) collective-permute-start(f32[64,256]{1,0:T(8,128)S(1)} %get-tuple-element.20), channel_id=1, source_target_pairs={{0,2},{2,0},{4,6},{6,4},{8,10},{10,8},{12,14},{14,12},{1,3},{3,1},... | collective-permute-start | bytes 196616 | tf_op jit(solution)/shard_map/ppermute | solution.py:197
  8.9 6.0 %collective-permute-start.8 = (bf16[1,128,256]{2,1,0:T(8,128)(2,1)S(1)}, bf16[1,128,256]{2,1,0:T(8,128)(2,1)S(1)}, u32[]{:S(2)}, u32[]{:S(2)}) collective-permute-start(bf16[1,128,256]{2,1,0:T(8,128)(2,1)S(1)} %get-tuple-element.23.refs_0_), channel_id=1, source_target_pairs={{0,8},{2,10},{4,12},{6,14},{8,0},{10,2},{12,4},{14,6},{1,9},{3,11}... | collective-permute-start | bytes 196616 | tf_op jit(solution)/shard_map/ppermute | solution.py:197
  11.5 5.0 %collective-permute-start.7 = (bf16[1,128,256]{2,1,0:T(8,128)(2,1)S(1)}, bf16[1,128,256]{2,1,0:T(8,128)(2,1)S(1)}, u32[]{:S(2)}, u32[]{:S(2)}) collective-permute-start(bf16[1,128,256]{2,1,0:T(8,128)(2,1)S(1)} %get-tuple-element.23.refs_0_), channel_id=1, source_target_pairs={{0,4},{2,6},{4,0},{6,2},{8,12},{10,14},{12,8},{14,10},{1,5},{3,7},... | collective-permute-start | bytes 196616 | tf_op jit(solution)/shard_map/ppermute | solution.py:197
  13.1 5.4 %collective-permute-start.2 = (f32[64,256]{1,0:T(8,128)S(1)}, f32[64,256]{1,0:T(8,128)S(1)}, u32[]{:S(2)}, u32[]{:S(2)}) collective-permute-start(f32[64,256]{1,0:T(8,128)S(1)} %plane_sum.1.refs_0_), channel_id=1, source_target_pairs={{0,4},{2,6},{4,0},{6,2},{8,12},{10,14},{12,8},{14,10},{1,5},{3,7},... | collective-permute-start | bytes 196616 | tf_op jit(solution)/shard_map/ppermute | solution.py:197
  16.5 9.6 %collective-permute-start.10 = (bf16[3,128,256]{2,1,0:T(8,128)(2,1)S(1)}, bf16[3,128,256]{2,1,0:T(8,128)(2,1)S(1)}, u32[]{:S(2)}, u32[]{:S(2)}) collective-permute-start(bf16[3,128,256]{2,1,0:T(8,128)(2,1)S(1)} %join_first.1.refs_0_), channel_id=1, source_target_pairs={{0,2},{2,0},{4,6},{6,4},{8,10},{10,8},{12,14},{14,12},{1,3},{3,1},... | collective-permute-start | bytes 589832 | tf_op jit(solution)/shard_map/ppermute | solution.py:197
  17.1 4.4 %collective-permute-start.9 = (bf16[1,128,256]{2,1,0:T(8,128)(2,1)S(1)}, bf16[1,128,256]{2,1,0:T(8,128)(2,1)S(1)}, u32[]{:S(2)}, u32[]{:S(2)}) collective-permute-start(bf16[1,128,256]{2,1,0:T(8,128)(2,1)S(1)} %collective-permute-done.8.refs_2_), channel_id=1, source_target_pairs={{0,4},{2,6},{4,0},{6,2},{8,12},{10,14},{12,8},{14,10},{1,5},{3,7},... | collective-permute-start | bytes 196616 | tf_op jit(solution)/shard_map/ppermute | solution.py:197
  18.5 5.9 %collective-permute-start.3 = (f32[64,256]{1,0:T(8,128)S(1)}, f32[64,256]{1,0:T(8,128)S(1)}, u32[]{:S(2)}, u32[]{:S(2)}) collective-permute-start(f32[64,256]{1,0:T(8,128)S(1)} %pair_sum.1.refs_1_), channel_id=1, source_target_pairs={{0,8},{2,10},{4,12},{6,14},{8,0},{10,2},{12,4},{14,6},{1,9},{3,11}... | collective-permute-start | bytes 196616 | tf_op jit(solution)/shard_map/ppermute | solution.py:197
  21.5 4.6 %collective-permute-start.11 = (bf16[1,128,256]{2,1,0:T(8,128)(2,1)S(1)}, bf16[1,128,256]{2,1,0:T(8,128)(2,1)S(1)}, u32[]{:S(2)}, u32[]{:S(2)}) collective-permute-start(bf16[1,128,256]{2,1,0:T(8,128)(2,1)S(1)} %collective-permute-done.9.refs_1_), channel_id=1, source_target_pairs={{0,2},{2,0},{4,6},{6,4},{8,10},{10,8},{12,14},{14,12},{1,3},{3,1},... | collective-permute-start | bytes 196616 | tf_op jit(solution)/shard_map/ppermute | solution.py:197
  23.3 5.3 %collective-permute-start.6 = (bf16[512,1280]{1,0:T(8,128)(2,1)S(1)}, bf16[512,1280]{1,0:T(8,128)(2,1)S(1)}, u32[]{:S(2)}, u32[]{:S(2)}) collective-permute-start(bf16[512,1280]{1,0:T(8,128)(2,1)S(1)} %pass_dense.1), channel_id=1, source_target_pairs={{0,1},{1,0},{2,3},{3,2},{4,5},{5,4},{6,7},{7,6},{8,9},{9,8},{10,11... | collective-permute-start | bytes 3932168 | tf_op jit(solution)/shard_map/ppermute | solution.py:194
  24.5 4.0 %collective-permute-start.4 = (bf16[64,256]{1,0:T(8,128)(2,1)S(1)}, bf16[64,256]{1,0:T(8,128)(2,1)S(1)}, u32[]{:S(2)}, u32[]{:S(2)}) collective-permute-start(bf16[64,256]{1,0:T(8,128)(2,1)S(1)} %hub_sums.1.refs_0_.refs_4_), channel_id=1, source_target_pairs={{0,2},{2,0},{4,6},{6,4},{8,10},{10,8},{12,14},{14,12},{1,3},{3,1},... | collective-permute-start | bytes 98312 | tf_op jit(solution)/shard_map/ppermute | solution.py:197
  26.1 2.5 %collective-permute-start.12 = (bf16[8,128,256]{2,1,0:T(8,128)(2,1)S(1)}, bf16[8,128,256]{2,1,0:T(8,128)(2,1)S(1)}, u32[]{:S(2)}, u32[]{:S(2)}) collective-permute-start(bf16[8,128,256]{2,1,0:T(8,128)(2,1)S(1)} %join_blocks.1.refs_0_), channel_id=1, source_target_pairs={{0,1},{1,0},{2,3},{3,2},{4,5},{5,4},{6,7},{7,6},{8,9},{9,8},{10,11... | collective-permute-start | bytes 1572872 | tf_op jit(solution)/shard_map/ppermute | solution.py:194
  28.5 1.3 %collective-permute-start.5 = (bf16[128,256]{1,0:T(8,128)(2,1)S(1)}, bf16[128,256]{1,0:T(8,128)(2,1)S(1)}, u32[]{:S(2)}, u32[]{:S(2)}) collective-permute-start(bf16[128,256]{1,0:T(8,128)(2,1)S(1)} %join_sides.1.refs_1_), channel_id=1, source_target_pairs={{0,1},{1,0},{2,3},{3,2},{4,5},{5,4},{6,7},{7,6},{8,9},{9,8},{10,11... | collective-permute-start | bytes 196616 | tf_op jit(solution)/shard_map/ppermute | solution.py:194

commit v32 on v31

--- a/solution.py
+++ b/solution.py
@@ -113,10 +113,12 @@
     columns = n_row * VB
     piece = parts_ref.shape[1]
     r, c = lax.axis_index("row"), lax.axis_index("col")
-    for ref, core in ((mine_ref, c), (theirs_ref, 1 - c)):
-        for i in range(n_row):
-            place = (i * n_col + core) * piece
-            panel[pl.ds(pl.multiple_of(place, piece), piece), :] = ref[i * piece:(i + 1) * piece]
+    n_z = n_row // X
+    x = r % X
+    for block, at, core in ((mine_ref[0], x, c), (mine_ref[1], 1 - x, 1 - c), (theirs_ref[0], x, 1 - c), (theirs_ref[1], 1 - x, c)):
+        for i in range(n_z):
+            place = ((at * n_z + i) * n_col + core) * piece
+            panel[pl.ds(pl.multiple_of(place, piece), piece), :] = block[i * piece:(i + 1) * piece]
     total = part_ref[...] + product(dense_mine[:, columns:], panel[...]) + product(dense_theirs[:, columns:], panel[...])
     tele = one_hot(H + (r * n_col + c) * VB, VB, src_ref[...])
     scores_ref[...] = DAMP * total[:VB] + 0.15 * tele
@@ -159,11 +161,9 @@
     out_ref[...] = (DAMP * (held_ref[...] + came_ref[...]) + 0.15 * tele).astype(out_ref.dtype)
 
 
-def side_kernel(mine_ref, theirs_ref, out_ref):
-    part = mine_ref.shape[0]
-    x = lax.axis_index("row") % X
-    for ref, place in ((mine_ref, x), (theirs_ref, 1 - x)):
-        out_ref[pl.ds(pl.multiple_of(place * part, part), part), :] = ref[...]
+def side_kernel(mine_ref, came_ref, out_ref):
+    out_ref[0] = mine_ref[...]
+    out_ref[1] = came_ref[...]
 
 
 def last_kernel(dims, src_ref, held_ref, parts_ref, scores_ref, hubs_ref):
@@ -198,6 +198,10 @@
 
     def other_side(x):
         return to_partner(x, 1)
+
+    def cross(x):
+        devices = [(r, c) for r in range(n_row) for c in range(n_col)]
+        return lax.ppermute(x, ("row", "col"), [(r * n_col + c, (r ^ 1) * n_col + 1 - c) for r, c in devices])
 
     def call(kernel, name, out_shape, *args, scratch=(), after=(), cost=0):
         def body(*refs):
@@ -253,7 +257,7 @@
     hubs = call(bind(hub_kernel, dims), "hub_sums", bf16((quarter, width)), src, sums, to_partner(sums, 2 * X), cost=0)
     blocks = call(join_kernel, "join_blocks", bf16((n_row, VB, width)), first, last, first_across, last_across, after=[hubs], cost=12)
     blocks_came = other_core(blocks)
-    hubs = call(side_kernel, "join_sides", bf16((H // n_col, width)), hubs, other_side(hubs), cost=8)
+    hubs = call(side_kernel, "join_sides", bf16((2, quarter, width)), hubs, cross(hubs), cost=8)
     part = call(
         bind(score_columns_kernel, dims), "score_columns", f32((half, width)),
         blocks, blocks_came, dense_keep, dense_came,

time: 41.8 us -> 41.6 us (level)
  starting transfers between devices: 15 us -> 14 us
  waiting for transfers between devices: 8.89 us -> 9.6 us
    ppermute x0 -> x1, waiting for transfers between devices: none -> 1.92 us  [cross(): lax.ppermute(x, ('row', 'col'), [(r * n_col + c, (r ^ 1) * n_col + 1 - c)...]
    ppermute x9 -> x8, starting transfers between devices: 14.3 us -> 12.7 us  [to_partner(): return lax.ppermute(x, 'row', [(r, r ^ flip) for r in range(n_row)])]
    ppermute x9 -> x8, waiting for transfers between devices: 7.82 us -> 6.7 us  [to_partner(): return lax.ppermute(x, 'row', [(r, r ^ flip) for r in range(n_row)])]
    ppermute x4, starting transfers between devices: 0.73 us -> 1.19 us  [other_core(): return lax.ppermute(x, 'col', [(0, 1), (1, 0)])]
  transfers between devices with their start and end apart: 13 -> 13, of which waited for: 7 -> 8; matrix products, arithmetic and copies ran while one was open for 0% -> 0% of each run, Pallas kernels for 4% -> 4%
where the time goes in v32:
time: 41.6 us; the launch traced here: 41.5 us
  starting transfers between devices  14 us (34%)
  blocking collectives  11 us (26%)
  waiting for transfers between devices  9.6 us (23%)
  Pallas kernels  5.49 us (13%)
  between operations  1.37 us (3%)
    ppermute x8, starting transfers between devices, to_partner(): return lax.ppermute(x, 'row', [(r, r ^ flip) for r in range(n_row)])  12.7 us
    all_to_all x1, blocking collectives, fast_body(): parts = lax.all_to_all(parts, 'row', 0, 0)  11 us
    ppermute x8, waiting for transfers between devices, to_partner(): return lax.ppermute(x, 'row', [(r, r ^ flip) for r in range(n_row)])  6.7 us
    pallas_call x1, Pallas kernels, fast_body(): pl.pallas_call(bind(first_kernel, dims), out_shape=(f32((half, width)), d...  2.98 us
    pallas_call x12, Pallas kernels, call(): pl.pallas_call(body, out_shape=out_shape, in_specs=[VMEM] * len(args) + [...  2.52 us
    ppermute x1, waiting for transfers between devices, cross(): lax.ppermute(x, ('row', 'col'), [(r * n_col + c, (r ^ 1) * n_col + 1 - c)...  1.92 us
    ppermute x4, starting transfers between devices, other_core(): return lax.ppermute(x, 'col', [(0, 1), (1, 0)])  1.19 us
    ppermute x4, waiting for transfers between devices, other_core(): return lax.ppermute(x, 'col', [(0, 1), (1, 0)])  0.98 us
  transfers between devices with their start and end apart: 13, of which 8 were waited for; matrix products, arithmetic and copies ran while one was open for 0% of the time, Pallas kernels for 4%

profile of v32, /device:TPU:0, one launch (start us, length us, event | category | flops | bytes accessed | tf_op | source)
XLA Modules:
  0.0 41.5 jit_solution(16075390578149182501)
XLA Ops:
  1.3 3.0 %first_terms.1 = (f32[256,256]{1,0:T(8,128)S(1)}, bf16[512,1280]{1,0:T(8,128)(2,1)S(1)}, f32[640,1280]{1,0:T(8,128)S(1)}, bf16[1280,256]{1,0:T(8,128)(2,1)S(1)}) custom-call(bf16[96,128,128]{2,1,0:T(8,128)(2,1)} %bitcast.12, s32[96]{0:T(128)} %bitcast.13, s32[96]{0:T(128)} %bitcast.14, s32[1]{0:T(128)} %bitcast.6.count_hbm, s32[1,256]{1,0:T(1,128)} %bitcast.7), custom_call_target="tpu_custom_call" | custom-call | tf_op jit(solution)/shard_map/first_terms/pallas_call | solution.py:226
  4.3 0.5 %collective-permute-start = (f32[256,256]{1,0:T(8,128)S(1)}, f32[256,256]{1,0:T(8,128)S(1)}, u32[]{:S(2)}, u32[]{:S(2)}) collective-permute-start(f32[256,256]{1,0:T(8,128)S(1)} %get-tuple-element.18), channel_id=1, source_target_pairs={{0,1},{1,0},{2,3},{3,2},{4,5},{5,4},{6,7},{7,6},{8,9},{9,8},{10,11... | collective-permute-start | bytes 786440 | tf_op jit(solution)/shard_map/ppermute | solution.py:194
  4.8 0.0 copy-start
  4.8 0.5 %keep_terms.1 = (f32[256,256]{1,0:T(8,128)S(1)}, bf16[512,1280]{1,0:T(8,128)(2,1)S(1)}) custom-call(f32[640,1280]{1,0:T(8,128)S(1)} %get-tuple-element.15.refs_0_, bf16[1280,256]{1,0:T(8,128)(2,1)S(1)} %get-tuple-element.16.refs_1_), custom_call_target="tpu_custom_call" | custom-call | flops 1000000000 | tf_op jit(solution)/shard_map/keep_terms/pallas_call | solution.py:210
  5.3 0.6 %collective-permute-done.refs_2_ = f32[256,256]{1,0:T(8,128)S(1)} collective-permute-done((f32[256,256]{1,0:T(8,128)S(1)}, f32[256,256]{1,0:T(8,128)S(1)}, u32[]{:S(2)}, u32[]{:S(2)}) %collective-permute-start) | collective-permute-done | bytes 262176 | tf_op jit(solution)/shard_map/ppermute | solution.py:194
  5.9 0.0 copy-done
  6.0 2.9 %collective-permute-start.1 = (f32[64,256]{1,0:T(8,128)S(1)}, f32[64,256]{1,0:T(8,128)S(1)}, u32[]{:S(2)}, u32[]{:S(2)}) collective-permute-start(f32[64,256]{1,0:T(8,128)S(1)} %get-tuple-element.20), channel_id=1, source_target_pairs={{0,2},{2,0},{4,6},{6,4},{8,10},{10,8},{12,14},{14,12},{1,3},{3,1},... | collective-permute-start | bytes 196616 | tf_op jit(solution)/shard_map/ppermute | solution.py:197
  8.9 2.6 %collective-permute-start.8 = (bf16[1,128,256]{2,1,0:T(8,128)(2,1)S(1)}, bf16[1,128,256]{2,1,0:T(8,128)(2,1)S(1)}, u32[]{:S(2)}, u32[]{:S(2)}) collective-permute-start(bf16[1,128,256]{2,1,0:T(8,128)(2,1)S(1)} %get-tuple-element.23.refs_0_), channel_id=1, source_target_pairs={{0,8},{2,10},{4,12},{6,14},{8,0},{10,2},{12,4},{14,6},{1,9},{3,11}... | collective-permute-start | bytes 196616 | tf_op jit(solution)/shard_map/ppermute | solution.py:197
  11.5 1.6 %collective-permute-start.7 = (bf16[1,128,256]{2,1,0:T(8,128)(2,1)S(1)}, bf16[1,128,256]{2,1,0:T(8,128)(2,1)S(1)}, u32[]{:S(2)}, u32[]{:S(2)}) collective-permute-start(bf16[1,128,256]{2,1,0:T(8,128)(2,1)S(1)} %get-tuple-element.23.refs_0_), channel_id=1, source_target_pairs={{0,4},{2,6},{4,0},{6,2},{8,12},{10,14},{12,8},{14,10},{1,5},{3,7},... | collective-permute-start | bytes 196616 | tf_op jit(solution)/shard_map/ppermute | solution.py:197
  13.1 0.0 collective-permute-done.1.refs_1_
  13.1 0.5 %collective-permute-start.2 = (f32[64,256]{1,0:T(8,128)S(1)}, f32[64,256]{1,0:T(8,128)S(1)}, u32[]{:S(2)}, u32[]{:S(2)}) collective-permute-start(f32[64,256]{1,0:T(8,128)S(1)} %plane_sum.1.refs_0_), channel_id=1, source_target_pairs={{0,4},{2,6},{4,0},{6,2},{8,12},{10,14},{12,8},{14,10},{1,5},{3,7},... | collective-permute-start | bytes 196616 | tf_op jit(solution)/shard_map/ppermute | solution.py:197
  13.6 1.3 %collective-permute-done.8.refs_2_ = bf16[1,128,256]{2,1,0:T(8,128)(2,1)S(1)} collective-permute-done((bf16[1,128,256]{2,1,0:T(8,128)(2,1)S(1)}, bf16[1,128,256]{2,1,0:T(8,128)(2,1)S(1)}, u32[]{:S(2)}, u32[]{:S(2)}) %collective-permute-start.8) | collective-permute-done | bytes 65568 | tf_op jit(solution)/shard_map/ppermute | solution.py:197
  15.0 1.5 %collective-permute-done.7.refs_1_ = bf16[1,128,256]{2,1,0:T(8,128)(2,1)S(1)} collective-permute-done((bf16[1,128,256]{2,1,0:T(8,128)(2,1)S(1)}, bf16[1,128,256]{2,1,0:T(8,128)(2,1)S(1)}, u32[]{:S(2)}, u32[]{:S(2)}) %collective-permute-start.7) | collective-permute-done | bytes 65568 | tf_op jit(solution)/shard_map/ppermute | solution.py:197
  16.5 0.6 %collective-permute-start.10 = (bf16[3,128,256]{2,1,0:T(8,128)(2,1)S(1)}, bf16[3,128,256]{2,1,0:T(8,128)(2,1)S(1)}, u32[]{:S(2)}, u32[]{:S(2)}) collective-permute-start(bf16[3,128,256]{2,1,0:T(8,128)(2,1)S(1)} %join_first.1.refs_0_), channel_id=1, source_target_pairs={{0,2},{2,0},{4,6},{6,4},{8,10},{10,8},{12,14},{14,12},{1,3},{3,1},... | collective-permute-start | bytes 589832 | tf_op jit(solution)/shard_map/ppermute | solution.py:197
  17.1 1.4 %collective-permute-start.9 = (bf16[1,128,256]{2,1,0:T(8,128)(2,1)S(1)}, bf16[1,128,256]{2,1,0:T(8,128)(2,1)S(1)}, u32[]{:S(2)}, u32[]{:S(2)}) collective-permute-start(bf16[1,128,256]{2,1,0:T(8,128)(2,1)S(1)} %collective-permute-done.8.refs_2_), channel_id=1, source_target_pairs={{0,4},{2,6},{4,0},{6,2},{8,12},{10,14},{12,8},{14,10},{1,5},{3,7},... | collective-permute-start | bytes 196616 | tf_op jit(solution)/shard_map/ppermute | solution.py:197
  18.5 0.0 collective-permute-done.2.refs_1_
  18.5 1.4 %collective-permute-start.3 = (f32[64,256]{1,0:T(8,128)S(1)}, f32[64,256]{1,0:T(8,128)S(1)}, u32[]{:S(2)}, u32[]{:S(2)}) collective-permute-start(f32[64,256]{1,0:T(8,128)S(1)} %pair_sum.1.refs_1_), channel_id=1, source_target_pairs={{0,8},{2,10},{4,12},{6,14},{8,0},{10,2},{12,4},{14,6},{1,9},{3,11}... | collective-permute-start | bytes 196616 | tf_op jit(solution)/shard_map/ppermute | solution.py:197
  19.9 1.6 %collective-permute-done.9.refs_1_ = bf16[1,128,256]{2,1,0:T(8,128)(2,1)S(1)} collective-permute-done((bf16[1,128,256]{2,1,0:T(8,128)(2,1)S(1)}, bf16[1,128,256]{2,1,0:T(8,128)(2,1)S(1)}, u32[]{:S(2)}, u32[]{:S(2)}) %collective-permute-start.9) | collective-permute-done | bytes 65568 | tf_op jit(solution)/shard_map/ppermute | solution.py:197
  21.5 1.7 %collective-permute-start.11 = (bf16[1,128,256]{2,1,0:T(8,128)(2,1)S(1)}, bf16[1,128,256]{2,1,0:T(8,128)(2,1)S(1)}, u32[]{:S(2)}, u32[]{:S(2)}) collective-permute-start(bf16[1,128,256]{2,1,0:T(8,128)(2,1)S(1)} %collective-permute-done.9.refs_1_), channel_id=1, source_target_pairs={{0,2},{2,0},{4,6},{6,4},{8,10},{10,8},{12,14},{14,12},{1,3},{3,1},... | collective-permute-start | bytes 196616 | tf_op jit(solution)/shard_map/ppermute | solution.py:197
  23.2 0.1 pass_dense.1
  23.3 0.1 collective-permute-start.6
  23.4 1.1 %collective-permute-done.3.refs_2_ = f32[64,256]{1,0:T(8,128)S(1)} collective-permute-done((f32[64,256]{1,0:T(8,128)S(1)}, f32[64,256]{1,0:T(8,128)S(1)}, u32[]{:S(2)}, u32[]{:S(2)}) %collective-permute-start.3) | collective-permute-done | bytes 65568 | tf_op jit(solution)/shard_map/ppermute | solution.py:197
  24.5 0.1 collective-permute-start.4
  24.6 1.2 %collective-permute-done.11.refs_3_ = bf16[1,128,256]{2,1,0:T(8,128)(2,1)S(1)} collective-permute-done((bf16[1,128,256]{2,1,0:T(8,128)(2,1)S(1)}, bf16[1,128,256]{2,1,0:T(8,128)(2,1)S(1)}, u32[]{:S(2)}, u32[]{:S(2)}) %collective-permute-start.11) | collective-permute-done | bytes 65568 | tf_op jit(solution)/shard_map/ppermute | solution.py:197
  25.7 0.0 collective-permute-done.10.refs_2_
  25.8 0.5 %collective-permute-start.12 = (bf16[8,128,256]{2,1,0:T(8,128)(2,1)S(1)}, bf16[8,128,256]{2,1,0:T(8,128)(2,1)S(1)}, u32[]{:S(2)}, u32[]{:S(2)}) collective-permute-start(bf16[8,128,256]{2,1,0:T(8,128)(2,1)S(1)} %join_blocks.1.refs_0_), channel_id=1, source_target_pairs={{0,1},{1,0},{2,3},{3,2},{4,5},{5,4},{6,7},{7,6},{8,9},{9,8},{10,11... | collective-permute-start | bytes 1572872 | tf_op jit(solution)/shard_map/ppermute | solution.py:194
  26.3 1.9 %collective-permute-done.4.refs_1_ = bf16[64,256]{1,0:T(8,128)(2,1)S(1)} collective-permute-done((bf16[64,256]{1,0:T(8,128)(2,1)S(1)}, bf16[64,256]{1,0:T(8,128)(2,1)S(1)}, u32[]{:S(2)}, u32[]{:S(2)}) %collective-permute-start.4) | collective-permute-done | bytes 32800 | tf_op jit(solution)/shard_map/ppermute | solution.py:204
  28.2 0.1 collective-permute-start.5
  28.3 0.0 collective-permute-done.12.refs_1_
  28.3 0.0 collective-permute-done.6.refs_3_.refs_4_
  28.3 0.8 %score_columns.1.refs_5_ = f32[256,256]{1,0:T(8,128)S(1)} custom-call(bf16[8,128,256]{2,1,0:T(8,128)(2,1)S(1)} %join_blocks.1.refs_0_, bf16[8,128,256]{2,1,0:T(8,128)(2,1)S(1)} %collective-permute-done.12.refs_1_, bf16[512,1280]{1,0:T(8,128)(2,1)S(1)} %get-tuple-element.21.refs_2_.refs_3_, bf16[512,1280]{1,0:T(8,128)(2,1)S(1)} %collective-permute-done.6.refs_3_.refs_4_), custom_call_target="tpu_custom_call" | custom-call | tf_op jit(solution)/shard_map/score_columns/pallas_call | solution.py:210
  29.1 0.3 collective-permute-done.5.refs_2_
  29.5 0.3 hub_columns.1
  29.8 11.0 %all_to_all.5.refs_2_ = f32[8,16,256]{2,1,0:T(8,128)S(1)} all-to-all(f32[8,16,256]{2,1,0:T(8,128)S(1)} %get-tuple-element.25), channel_id=1, replica_groups=mesh['groups'=2,'row'=8,'col'=2] {'row'}, dimensions={0} | all-to-all | bytes 262144 | tf_op jit(solution)/shard_map/all_to_all | solution.py:268
  40.8 0.7 %last_hubs.1 = (f32[128,256]{1,0:T(8,128)}, f32[16,256]{1,0:T(8,128)}) custom-call(s32[1,256]{1,0:T(1,128)S(1)} %bitcast.11, f32[128,256]{1,0:T(8,128)S(1)} %get-tuple-element.24.refs_1_, f32[8,16,256]{2,1,0:T(8,128)S(1)} %all_to_all.5.refs_2_), custom_call_target="tpu_custom_call" | custom-call | tf_op jit(solution)/shard_map/last_hubs/pallas_call | solution.py:210
  (7 shorter events, 0.2 us)
Async XLA Ops:
  4.3 1.7 %collective-permute-start = (f32[256,256]{1,0:T(8,128)S(1)}, f32[256,256]{1,0:T(8,128)S(1)}, u32[]{:S(2)}, u32[]{:S(2)}) collective-permute-start(f32[256,256]{1,0:T(8,128)S(1)} %get-tuple-element.18), channel_id=1, source_target_pairs={{0,1},{1,0},{2,3},{3,2},{4,5},{5,4},{6,7},{7,6},{8,9},{9,8},{10,11... | collective-permute-start | bytes 786440 | tf_op jit(solution)/shard_map/ppermute | solution.py:194
  4.8 1.2 %copy-start = (s32[256]{0:T(256)S(1)}, s32[256]{0:T(256)}, u32[]{:S(2)}) copy-start(s32[256]{0:T(256)} %param.9) | copy-start | bytes 3076
  6.0 7.1 %collective-permute-start.1 = (f32[64,256]{1,0:T(8,128)S(1)}, f32[64,256]{1,0:T(8,128)S(1)}, u32[]{:S(2)}, u32[]{:S(2)}) collective-permute-start(f32[64,256]{1,0:T(8,128)S(1)} %get-tuple-element.20), channel_id=1, source_target_pairs={{0,2},{2,0},{4,6},{6,4},{8,10},{10,8},{12,14},{14,12},{1,3},{3,1},... | collective-permute-start | bytes 196616 | tf_op jit(solution)/shard_map/ppermute | solution.py:197
  8.9 6.0 %collective-permute-start.8 = (bf16[1,128,256]{2,1,0:T(8,128)(2,1)S(1)}, bf16[1,128,256]{2,1,0:T(8,128)(2,1)S(1)}, u32[]{:S(2)}, u32[]{:S(2)}) collective-permute-start(bf16[1,128,256]{2,1,0:T(8,128)(2,1)S(1)} %get-tuple-element.23.refs_0_), channel_id=1, source_target_pairs={{0,8},{2,10},{4,12},{6,14},{8,0},{10,2},{12,4},{14,6},{1,9},{3,11}... | collective-permute-start | bytes 196616 | tf_op jit(solution)/shard_map/ppermute | solution.py:197
  11.5 5.0 %collective-permute-start.7 = (bf16[1,128,256]{2,1,0:T(8,128)(2,1)S(1)}, bf16[1,128,256]{2,1,0:T(8,128)(2,1)S(1)}, u32[]{:S(2)}, u32[]{:S(2)}) collective-permute-start(bf16[1,128,256]{2,1,0:T(8,128)(2,1)S(1)} %get-tuple-element.23.refs_0_), channel_id=1, source_target_pairs={{0,4},{2,6},{4,0},{6,2},{8,12},{10,14},{12,8},{14,10},{1,5},{3,7},... | collective-permute-start | bytes 196616 | tf_op jit(solution)/shard_map/ppermute | solution.py:197
  13.1 5.4 %collective-permute-start.2 = (f32[64,256]{1,0:T(8,128)S(1)}, f32[64,256]{1,0:T(8,128)S(1)}, u32[]{:S(2)}, u32[]{:S(2)}) collective-permute-start(f32[64,256]{1,0:T(8,128)S(1)} %plane_sum.1.refs_0_), channel_id=1, source_target_pairs={{0,4},{2,6},{4,0},{6,2},{8,12},{10,14},{12,8},{14,10},{1,5},{3,7},... | collective-permute-start | bytes 196616 | tf_op jit(solution)/shard_map/ppermute | solution.py:197
  16.5 9.3 %collective-permute-start.10 = (bf16[3,128,256]{2,1,0:T(8,128)(2,1)S(1)}, bf16[3,128,256]{2,1,0:T(8,128)(2,1)S(1)}, u32[]{:S(2)}, u32[]{:S(2)}) collective-permute-start(bf16[3,128,256]{2,1,0:T(8,128)(2,1)S(1)} %join_first.1.refs_0_), channel_id=1, source_target_pairs={{0,2},{2,0},{4,6},{6,4},{8,10},{10,8},{12,14},{14,12},{1,3},{3,1},... | collective-permute-start | bytes 589832 | tf_op jit(solution)/shard_map/ppermute | solution.py:197
  17.1 4.4 %collective-permute-start.9 = (bf16[1,128,256]{2,1,0:T(8,128)(2,1)S(1)}, bf16[1,128,256]{2,1,0:T(8,128)(2,1)S(1)}, u32[]{:S(2)}, u32[]{:S(2)}) collective-permute-start(bf16[1,128,256]{2,1,0:T(8,128)(2,1)S(1)} %collective-permute-done.8.refs_2_), channel_id=1, source_target_pairs={{0,4},{2,6},{4,0},{6,2},{8,12},{10,14},{12,8},{14,10},{1,5},{3,7},... | collective-permute-start | bytes 196616 | tf_op jit(solution)/shard_map/ppermute | solution.py:197
  18.5 5.9 %collective-permute-start.3 = (f32[64,256]{1,0:T(8,128)S(1)}, f32[64,256]{1,0:T(8,128)S(1)}, u32[]{:S(2)}, u32[]{:S(2)}) collective-permute-start(f32[64,256]{1,0:T(8,128)S(1)} %pair_sum.1.refs_1_), channel_id=1, source_target_pairs={{0,8},{2,10},{4,12},{6,14},{8,0},{10,2},{12,4},{14,6},{1,9},{3,11}... | collective-permute-start | bytes 196616 | tf_op jit(solution)/shard_map/ppermute | solution.py:197
  21.5 4.3 %collective-permute-start.11 = (bf16[1,128,256]{2,1,0:T(8,128)(2,1)S(1)}, bf16[1,128,256]{2,1,0:T(8,128)(2,1)S(1)}, u32[]{:S(2)}, u32[]{:S(2)}) collective-permute-start(bf16[1,128,256]{2,1,0:T(8,128)(2,1)S(1)} %collective-permute-done.9.refs_1_), channel_id=1, source_target_pairs={{0,2},{2,0},{4,6},{6,4},{8,10},{10,8},{12,14},{14,12},{1,3},{3,1},... | collective-permute-start | bytes 196616 | tf_op jit(solution)/shard_map/ppermute | solution.py:197
  23.3 5.0 %collective-permute-start.6 = (bf16[512,1280]{1,0:T(8,128)(2,1)S(1)}, bf16[512,1280]{1,0:T(8,128)(2,1)S(1)}, u32[]{:S(2)}, u32[]{:S(2)}) collective-permute-start(bf16[512,1280]{1,0:T(8,128)(2,1)S(1)} %pass_dense.1), channel_id=1, source_target_pairs={{0,1},{1,0},{2,3},{3,2},{4,5},{5,4},{6,7},{7,6},{8,9},{9,8},{10,11... | collective-permute-start | bytes 3932168 | tf_op jit(solution)/shard_map/ppermute | solution.py:194
  24.5 3.7 %collective-permute-start.4 = (bf16[64,256]{1,0:T(8,128)(2,1)S(1)}, bf16[64,256]{1,0:T(8,128)(2,1)S(1)}, u32[]{:S(2)}, u32[]{:S(2)}) collective-permute-start(bf16[64,256]{1,0:T(8,128)(2,1)S(1)} %hub_sums.1.refs_0_.refs_4_), channel_id=1, source_target_pairs={{0,3},{1,2},{2,1},{3,0},{4,7},{5,6},{6,5},{7,4},{8,11},{9,10},{10,... | collective-permute-start | bytes 98312 | tf_op jit(solution)/shard_map/ppermute | solution.py:204
  25.8 2.5 %collective-permute-start.12 = (bf16[8,128,256]{2,1,0:T(8,128)(2,1)S(1)}, bf16[8,128,256]{2,1,0:T(8,128)(2,1)S(1)}, u32[]{:S(2)}, u32[]{:S(2)}) collective-permute-start(bf16[8,128,256]{2,1,0:T(8,128)(2,1)S(1)} %join_blocks.1.refs_0_), channel_id=1, source_target_pairs={{0,1},{1,0},{2,3},{3,2},{4,5},{5,4},{6,7},{7,6},{8,9},{9,8},{10,11... | collective-permute-start | bytes 1572872 | tf_op jit(solution)/shard_map/ppermute | solution.py:194
  28.2 1.3 %collective-permute-start.5 = (bf16[2,64,256]{2,1,0:T(8,128)(2,1)S(1)}, bf16[2,64,256]{2,1,0:T(8,128)(2,1)S(1)}, u32[]{:S(2)}, u32[]{:S(2)}) collective-permute-start(bf16[2,64,256]{2,1,0:T(8,128)(2,1)S(1)} %join_sides.1.refs_1_), channel_id=1, source_target_pairs={{0,1},{1,0},{2,3},{3,2},{4,5},{5,4},{6,7},{7,6},{8,9},{9,8},{10,11... | collective-permute-start | bytes 196616 | tf_op jit(solution)/shard_map/ppermute | solution.py:194

commit v33 on v32

--- a/solution.py
+++ b/solution.py
@@ -94,17 +94,19 @@
     half_terms(dims, lax.axis_index("col"), total_ref, panel_ref, keep_ref, dense_ref)
 
 
-def score_columns_kernel(dims, *refs):
-    n_row, n_col, side = dims
-    columns = n_row * VB
-    mine, theirs, dense_mine, dense_theirs, part_ref, panel = refs
+def score_columns_kernel(dims, blocks_ref, dense_ref, part_ref, panel):
+    n_row, n_col, side = dims
+    n_z = n_row // X
     r = lax.axis_index("row")
-    n_z = n_row // X
-    for at, ref in enumerate((mine, theirs)):
-        for k in range(n_row):
-            owner = r ^ (X * (k % n_z) + k // n_z)
-            panel[at, pl.ds(pl.multiple_of(owner * VB, VB), VB), :] = ref[k]
-    part_ref[...] = product(dense_mine[:, :columns], panel[0]) + product(dense_theirs[:, :columns], panel[1])
+    for k in range(n_row):
+        owner = r ^ (X * (k % n_z) + k // n_z)
+        panel[pl.ds(pl.multiple_of(owner * VB, VB), VB), :] = blocks_ref[k]
+    part_ref[...] = product(dense_ref[:, :n_row * VB], panel[...])
+
+
+def other_columns_kernel(dims, blocks_ref, dense_ref, held_ref, part_ref, panel):
+    score_columns_kernel(dims, blocks_ref, dense_ref, part_ref, panel)
+    part_ref[...] += held_ref[...]
 
 
 def hub_columns_kernel(dims, src_ref, mine_ref, theirs_ref, dense_mine, dense_theirs, part_ref,
@@ -258,10 +260,11 @@
     blocks = call(join_kernel, "join_blocks", bf16((n_row, VB, width)), first, last, first_across, last_across, after=[hubs], cost=12)
     blocks_came = other_core(blocks)
     hubs = call(side_kernel, "join_sides", bf16((2, quarter, width)), hubs, cross(hubs), cost=8)
-    part = call(
-        bind(score_columns_kernel, dims), "score_columns", f32((half, width)),
-        blocks, blocks_came, dense_keep, dense_came,
-        scratch=[pltpu.VMEM((2, n_row * VB, width), jnp.bfloat16)], cost=0)
+    column_scratch = [pltpu.VMEM((n_row * VB, width), jnp.bfloat16)]
+    part = call(bind(score_columns_kernel, dims), "own_columns", f32((half, width)),
+                blocks, dense_keep, scratch=column_scratch)
+    part = call(bind(other_columns_kernel, dims), "other_columns", f32((half, width)),
+                blocks_came, dense_came, part, scratch=column_scratch)
     scores, parts = call(
         bind(hub_columns_kernel, dims), "hub_columns", (f32((VB, width)), f32((n_row, piece, width))),
         src, hubs, other_core(hubs), dense_keep, dense_came, part, scratch=[pltpu.VMEM((H, width), jnp.bfloat16)])

time: 41.6 us -> 41.3 us (level)
    pallas_call x12 -> x13, Pallas kernels: 2.52 us -> 2.69 us  [call(): pl.pallas_call(body, out_shape=out_shape, in_specs=[VMEM] * len(args) + [...]
where the time goes in v33:
time: 41.3 us; the launch traced here: 41.2 us
  starting transfers between devices  13.8 us (33%)
  blocking collectives  10.7 us (26%)
  waiting for transfers between devices  9.53 us (23%)
  Pallas kernels  5.67 us (14%)
  between operations  1.39 us (3%)
    ppermute x8, starting transfers between devices, to_partner(): return lax.ppermute(x, 'row', [(r, r ^ flip) for r in range(n_row)])  12.7 us
    all_to_all x1, blocking collectives, fast_body(): parts = lax.all_to_all(parts, 'row', 0, 0)  10.7 us
    ppermute x8, waiting for transfers between devices, to_partner(): return lax.ppermute(x, 'row', [(r, r ^ flip) for r in range(n_row)])  6.83 us
    pallas_call x1, Pallas kernels, fast_body(): pl.pallas_call(bind(first_kernel, dims), out_shape=(f32((half, width)), d...  2.98 us
    pallas_call x13, Pallas kernels, call(): pl.pallas_call(body, out_shape=out_shape, in_specs=[VMEM] * len(args) + [...  2.69 us
    ppermute x1, waiting for transfers between devices, cross(): lax.ppermute(x, ('row', 'col'), [(r * n_col + c, (r ^ 1) * n_col + 1 - c)...  1.92 us
    ppermute x4, starting transfers between devices, other_core(): return lax.ppermute(x, 'col', [(0, 1), (1, 0)])  1.13 us
  transfers between devices with their start and end apart: 13, of which 8 were waited for; matrix products, arithmetic and copies ran while one was open for 0% of the time, Pallas kernels for 4%

profile of v33, /device:TPU:0, one launch (start us, length us, event | category | flops | bytes accessed | tf_op | source)
XLA Modules:
  0.0 41.2 jit_solution(15461433743180165107)
XLA Ops:
  1.3 3.0 %first_terms.1 = (f32[256,256]{1,0:T(8,128)S(1)}, bf16[512,1280]{1,0:T(8,128)(2,1)S(1)}, f32[640,1280]{1,0:T(8,128)S(1)}, bf16[1280,256]{1,0:T(8,128)(2,1)S(1)}) custom-call(bf16[96,128,128]{2,1,0:T(8,128)(2,1)} %bitcast.12, s32[96]{0:T(128)} %bitcast.13, s32[96]{0:T(128)} %bitcast.14, s32[1]{0:T(128)} %bitcast.6.count_hbm, s32[1,256]{1,0:T(1,128)} %bitcast.7), custom_call_target="tpu_custom_call" | custom-call | tf_op jit(solution)/shard_map/first_terms/pallas_call | solution.py:228
  4.3 0.5 %collective-permute-start = (f32[256,256]{1,0:T(8,128)S(1)}, f32[256,256]{1,0:T(8,128)S(1)}, u32[]{:S(2)}, u32[]{:S(2)}) collective-permute-start(f32[256,256]{1,0:T(8,128)S(1)} %get-tuple-element.18), channel_id=1, source_target_pairs={{0,1},{1,0},{2,3},{3,2},{4,5},{5,4},{6,7},{7,6},{8,9},{9,8},{10,11... | collective-permute-start | bytes 786440 | tf_op jit(solution)/shard_map/ppermute | solution.py:196
  4.8 0.0 copy-start
  4.8 0.5 %keep_terms.1 = (f32[256,256]{1,0:T(8,128)S(1)}, bf16[512,1280]{1,0:T(8,128)(2,1)S(1)}) custom-call(f32[640,1280]{1,0:T(8,128)S(1)} %get-tuple-element.15.refs_0_, bf16[1280,256]{1,0:T(8,128)(2,1)S(1)} %get-tuple-element.16.refs_1_), custom_call_target="tpu_custom_call" | custom-call | flops 1000000000 | tf_op jit(solution)/shard_map/keep_terms/pallas_call | solution.py:212
  5.3 0.6 %collective-permute-done.refs_2_ = f32[256,256]{1,0:T(8,128)S(1)} collective-permute-done((f32[256,256]{1,0:T(8,128)S(1)}, f32[256,256]{1,0:T(8,128)S(1)}, u32[]{:S(2)}, u32[]{:S(2)}) %collective-permute-start) | collective-permute-done | bytes 262176 | tf_op jit(solution)/shard_map/ppermute | solution.py:196
  5.9 0.0 copy-done
  6.0 2.9 %collective-permute-start.1 = (f32[64,256]{1,0:T(8,128)S(1)}, f32[64,256]{1,0:T(8,128)S(1)}, u32[]{:S(2)}, u32[]{:S(2)}) collective-permute-start(f32[64,256]{1,0:T(8,128)S(1)} %get-tuple-element.20), channel_id=1, source_target_pairs={{0,2},{2,0},{4,6},{6,4},{8,10},{10,8},{12,14},{14,12},{1,3},{3,1},... | collective-permute-start | bytes 196616 | tf_op jit(solution)/shard_map/ppermute | solution.py:199
  8.9 2.6 %collective-permute-start.8 = (bf16[1,128,256]{2,1,0:T(8,128)(2,1)S(1)}, bf16[1,128,256]{2,1,0:T(8,128)(2,1)S(1)}, u32[]{:S(2)}, u32[]{:S(2)}) collective-permute-start(bf16[1,128,256]{2,1,0:T(8,128)(2,1)S(1)} %get-tuple-element.23.refs_0_), channel_id=1, source_target_pairs={{0,8},{2,10},{4,12},{6,14},{8,0},{10,2},{12,4},{14,6},{1,9},{3,11}... | collective-permute-start | bytes 196616 | tf_op jit(solution)/shard_map/ppermute | solution.py:199
  11.5 1.6 %collective-permute-start.7 = (bf16[1,128,256]{2,1,0:T(8,128)(2,1)S(1)}, bf16[1,128,256]{2,1,0:T(8,128)(2,1)S(1)}, u32[]{:S(2)}, u32[]{:S(2)}) collective-permute-start(bf16[1,128,256]{2,1,0:T(8,128)(2,1)S(1)} %get-tuple-element.23.refs_0_), channel_id=1, source_target_pairs={{0,4},{2,6},{4,0},{6,2},{8,12},{10,14},{12,8},{14,10},{1,5},{3,7},... | collective-permute-start | bytes 196616 | tf_op jit(solution)/shard_map/ppermute | solution.py:199
  13.1 0.0 collective-permute-done.1.refs_1_
  13.1 0.5 %collective-permute-start.2 = (f32[64,256]{1,0:T(8,128)S(1)}, f32[64,256]{1,0:T(8,128)S(1)}, u32[]{:S(2)}, u32[]{:S(2)}) collective-permute-start(f32[64,256]{1,0:T(8,128)S(1)} %plane_sum.1.refs_0_), channel_id=1, source_target_pairs={{0,4},{2,6},{4,0},{6,2},{8,12},{10,14},{12,8},{14,10},{1,5},{3,7},... | collective-permute-start | bytes 196616 | tf_op jit(solution)/shard_map/ppermute | solution.py:199
  13.6 1.3 %collective-permute-done.8.refs_2_ = bf16[1,128,256]{2,1,0:T(8,128)(2,1)S(1)} collective-permute-done((bf16[1,128,256]{2,1,0:T(8,128)(2,1)S(1)}, bf16[1,128,256]{2,1,0:T(8,128)(2,1)S(1)}, u32[]{:S(2)}, u32[]{:S(2)}) %collective-permute-start.8) | collective-permute-done | bytes 65568 | tf_op jit(solution)/shard_map/ppermute | solution.py:199
  15.0 1.5 %collective-permute-done.7.refs_1_ = bf16[1,128,256]{2,1,0:T(8,128)(2,1)S(1)} collective-permute-done((bf16[1,128,256]{2,1,0:T(8,128)(2,1)S(1)}, bf16[1,128,256]{2,1,0:T(8,128)(2,1)S(1)}, u32[]{:S(2)}, u32[]{:S(2)}) %collective-permute-start.7) | collective-permute-done | bytes 65568 | tf_op jit(solution)/shard_map/ppermute | solution.py:199
  16.5 0.6 %collective-permute-start.10 = (bf16[3,128,256]{2,1,0:T(8,128)(2,1)S(1)}, bf16[3,128,256]{2,1,0:T(8,128)(2,1)S(1)}, u32[]{:S(2)}, u32[]{:S(2)}) collective-permute-start(bf16[3,128,256]{2,1,0:T(8,128)(2,1)S(1)} %join_first.1.refs_0_), channel_id=1, source_target_pairs={{0,2},{2,0},{4,6},{6,4},{8,10},{10,8},{12,14},{14,12},{1,3},{3,1},... | collective-permute-start | bytes 589832 | tf_op jit(solution)/shard_map/ppermute | solution.py:199
  17.1 1.4 %collective-permute-start.9 = (bf16[1,128,256]{2,1,0:T(8,128)(2,1)S(1)}, bf16[1,128,256]{2,1,0:T(8,128)(2,1)S(1)}, u32[]{:S(2)}, u32[]{:S(2)}) collective-permute-start(bf16[1,128,256]{2,1,0:T(8,128)(2,1)S(1)} %collective-permute-done.8.refs_2_), channel_id=1, source_target_pairs={{0,4},{2,6},{4,0},{6,2},{8,12},{10,14},{12,8},{14,10},{1,5},{3,7},... | collective-permute-start | bytes 196616 | tf_op jit(solution)/shard_map/ppermute | solution.py:199
  18.5 0.0 collective-permute-done.2.refs_1_
  18.5 1.4 %collective-permute-start.3 = (f32[64,256]{1,0:T(8,128)S(1)}, f32[64,256]{1,0:T(8,128)S(1)}, u32[]{:S(2)}, u32[]{:S(2)}) collective-permute-start(f32[64,256]{1,0:T(8,128)S(1)} %pair_sum.1.refs_1_), channel_id=1, source_target_pairs={{0,8},{2,10},{4,12},{6,14},{8,0},{10,2},{12,4},{14,6},{1,9},{3,11}... | collective-permute-start | bytes 196616 | tf_op jit(solution)/shard_map/ppermute | solution.py:199
  19.9 1.7 %collective-permute-done.9.refs_1_ = bf16[1,128,256]{2,1,0:T(8,128)(2,1)S(1)} collective-permute-done((bf16[1,128,256]{2,1,0:T(8,128)(2,1)S(1)}, bf16[1,128,256]{2,1,0:T(8,128)(2,1)S(1)}, u32[]{:S(2)}, u32[]{:S(2)}) %collective-permute-start.9) | collective-permute-done | bytes 65568 | tf_op jit(solution)/shard_map/ppermute | solution.py:199
  21.5 1.7 %collective-permute-start.11 = (bf16[1,128,256]{2,1,0:T(8,128)(2,1)S(1)}, bf16[1,128,256]{2,1,0:T(8,128)(2,1)S(1)}, u32[]{:S(2)}, u32[]{:S(2)}) collective-permute-start(bf16[1,128,256]{2,1,0:T(8,128)(2,1)S(1)} %collective-permute-done.9.refs_1_), channel_id=1, source_target_pairs={{0,2},{2,0},{4,6},{6,4},{8,10},{10,8},{12,14},{14,12},{1,3},{3,1},... | collective-permute-start | bytes 196616 | tf_op jit(solution)/shard_map/ppermute | solution.py:199
  23.2 0.1 pass_dense.1
  23.3 0.1 collective-permute-start.6
  23.4 1.1 %collective-permute-done.3.refs_2_ = f32[64,256]{1,0:T(8,128)S(1)} collective-permute-done((f32[64,256]{1,0:T(8,128)S(1)}, f32[64,256]{1,0:T(8,128)S(1)}, u32[]{:S(2)}, u32[]{:S(2)}) %collective-permute-start.3) | collective-permute-done | bytes 65568 | tf_op jit(solution)/shard_map/ppermute | solution.py:199
  24.5 0.1 collective-permute-start.4
  24.6 1.2 %collective-permute-done.11.refs_3_ = bf16[1,128,256]{2,1,0:T(8,128)(2,1)S(1)} collective-permute-done((bf16[1,128,256]{2,1,0:T(8,128)(2,1)S(1)}, bf16[1,128,256]{2,1,0:T(8,128)(2,1)S(1)}, u32[]{:S(2)}, u32[]{:S(2)}) %collective-permute-start.11) | collective-permute-done | bytes 65568 | tf_op jit(solution)/shard_map/ppermute | solution.py:199
  25.8 0.0 collective-permute-done.10.refs_2_
  25.8 0.4 %collective-permute-start.12 = (bf16[8,128,256]{2,1,0:T(8,128)(2,1)S(1)}, bf16[8,128,256]{2,1,0:T(8,128)(2,1)S(1)}, u32[]{:S(2)}, u32[]{:S(2)}) collective-permute-start(bf16[8,128,256]{2,1,0:T(8,128)(2,1)S(1)} %join_blocks.1.refs_0_), channel_id=1, source_target_pairs={{0,1},{1,0},{2,3},{3,2},{4,5},{5,4},{6,7},{7,6},{8,9},{9,8},{10,11... | collective-permute-start | bytes 1572872 | tf_op jit(solution)/shard_map/ppermute | solution.py:196
  26.3 1.9 %collective-permute-done.4.refs_1_ = bf16[64,256]{1,0:T(8,128)(2,1)S(1)} collective-permute-done((bf16[64,256]{1,0:T(8,128)(2,1)S(1)}, bf16[64,256]{1,0:T(8,128)(2,1)S(1)}, u32[]{:S(2)}, u32[]{:S(2)}) %collective-permute-start.4) | collective-permute-done | bytes 32800 | tf_op jit(solution)/shard_map/ppermute | solution.py:206
  28.2 0.1 collective-permute-start.5
  28.3 0.5 %own_columns.1.refs_2_ = f32[256,256]{1,0:T(8,128)S(1)} custom-call(bf16[8,128,256]{2,1,0:T(8,128)(2,1)S(1)} %join_blocks.1.refs_0_, bf16[512,1280]{1,0:T(8,128)(2,1)S(1)} %get-tuple-element.21.refs_1_.refs_3_), custom_call_target="tpu_custom_call" | custom-call | tf_op jit(solution)/shard_map/own_columns/pallas_call | solution.py:212
  28.8 0.0 collective-permute-done.12.refs_0_
  28.8 0.0 collective-permute-done.6.refs_1_.refs_4_
  28.8 0.5 %other_columns.1.refs_5_ = f32[256,256]{1,0:T(8,128)S(1)} custom-call(bf16[8,128,256]{2,1,0:T(8,128)(2,1)S(1)} %collective-permute-done.12.refs_0_, bf16[512,1280]{1,0:T(8,128)(2,1)S(1)} %collective-permute-done.6.refs_1_.refs_4_, f32[256,256]{1,0:T(8,128)S(1)} %own_columns.1.refs_2_), custom_call_target="tpu_custom_call" | custom-call | tf_op jit(solution)/shard_map/other_columns/pallas_call | solution.py:212
  29.3 0.1 collective-permute-done.5.refs_2_
  29.5 0.3 hub_columns.1
  29.8 10.7 %all_to_all.5.refs_2_ = f32[8,16,256]{2,1,0:T(8,128)S(1)} all-to-all(f32[8,16,256]{2,1,0:T(8,128)S(1)} %get-tuple-element.25), channel_id=1, replica_groups=mesh['groups'=2,'row'=8,'col'=2] {'row'}, dimensions={0} | all-to-all | bytes 262144 | tf_op jit(solution)/shard_map/all_to_all | solution.py:271
  40.5 0.7 %last_hubs.1 = (f32[128,256]{1,0:T(8,128)}, f32[16,256]{1,0:T(8,128)}) custom-call(s32[1,256]{1,0:T(1,128)S(1)} %bitcast.11, f32[128,256]{1,0:T(8,128)S(1)} %get-tuple-element.24.refs_1_, f32[8,16,256]{2,1,0:T(8,128)S(1)} %all_to_all.5.refs_2_), custom_call_target="tpu_custom_call" | custom-call | tf_op jit(solution)/shard_map/last_hubs/pallas_call | solution.py:212
  (7 shorter events, 0.1 us)
Async XLA Ops:
  4.3 1.7 %collective-permute-start = (f32[256,256]{1,0:T(8,128)S(1)}, f32[256,256]{1,0:T(8,128)S(1)}, u32[]{:S(2)}, u32[]{:S(2)}) collective-permute-start(f32[256,256]{1,0:T(8,128)S(1)} %get-tuple-element.18), channel_id=1, source_target_pairs={{0,1},{1,0},{2,3},{3,2},{4,5},{5,4},{6,7},{7,6},{8,9},{9,8},{10,11... | collective-permute-start | bytes 786440 | tf_op jit(solution)/shard_map/ppermute | solution.py:196
  4.8 1.2 %copy-start = (s32[256]{0:T(256)S(1)}, s32[256]{0:T(256)}, u32[]{:S(2)}) copy-start(s32[256]{0:T(256)} %param.9) | copy-start | bytes 3076
  6.0 7.1 %collective-permute-start.1 = (f32[64,256]{1,0:T(8,128)S(1)}, f32[64,256]{1,0:T(8,128)S(1)}, u32[]{:S(2)}, u32[]{:S(2)}) collective-permute-start(f32[64,256]{1,0:T(8,128)S(1)} %get-tuple-element.20), channel_id=1, source_target_pairs={{0,2},{2,0},{4,6},{6,4},{8,10},{10,8},{12,14},{14,12},{1,3},{3,1},... | collective-permute-start | bytes 196616 | tf_op jit(solution)/shard_map/ppermute | solution.py:199
  8.9 6.0 %collective-permute-start.8 = (bf16[1,128,256]{2,1,0:T(8,128)(2,1)S(1)}, bf16[1,128,256]{2,1,0:T(8,128)(2,1)S(1)}, u32[]{:S(2)}, u32[]{:S(2)}) collective-permute-start(bf16[1,128,256]{2,1,0:T(8,128)(2,1)S(1)} %get-tuple-element.23.refs_0_), channel_id=1, source_target_pairs={{0,8},{2,10},{4,12},{6,14},{8,0},{10,2},{12,4},{14,6},{1,9},{3,11}... | collective-permute-start | bytes 196616 | tf_op jit(solution)/shard_map/ppermute | solution.py:199
  11.5 5.0 %collective-permute-start.7 = (bf16[1,128,256]{2,1,0:T(8,128)(2,1)S(1)}, bf16[1,128,256]{2,1,0:T(8,128)(2,1)S(1)}, u32[]{:S(2)}, u32[]{:S(2)}) collective-permute-start(bf16[1,128,256]{2,1,0:T(8,128)(2,1)S(1)} %get-tuple-element.23.refs_0_), channel_id=1, source_target_pairs={{0,4},{2,6},{4,0},{6,2},{8,12},{10,14},{12,8},{14,10},{1,5},{3,7},... | collective-permute-start | bytes 196616 | tf_op jit(solution)/shard_map/ppermute | solution.py:199
  13.1 5.4 %collective-permute-start.2 = (f32[64,256]{1,0:T(8,128)S(1)}, f32[64,256]{1,0:T(8,128)S(1)}, u32[]{:S(2)}, u32[]{:S(2)}) collective-permute-start(f32[64,256]{1,0:T(8,128)S(1)} %plane_sum.1.refs_0_), channel_id=1, source_target_pairs={{0,4},{2,6},{4,0},{6,2},{8,12},{10,14},{12,8},{14,10},{1,5},{3,7},... | collective-permute-start | bytes 196616 | tf_op jit(solution)/shard_map/ppermute | solution.py:199
  16.5 9.3 %collective-permute-start.10 = (bf16[3,128,256]{2,1,0:T(8,128)(2,1)S(1)}, bf16[3,128,256]{2,1,0:T(8,128)(2,1)S(1)}, u32[]{:S(2)}, u32[]{:S(2)}) collective-permute-start(bf16[3,128,256]{2,1,0:T(8,128)(2,1)S(1)} %join_first.1.refs_0_), channel_id=1, source_target_pairs={{0,2},{2,0},{4,6},{6,4},{8,10},{10,8},{12,14},{14,12},{1,3},{3,1},... | collective-permute-start | bytes 589832 | tf_op jit(solution)/shard_map/ppermute | solution.py:199
  17.1 4.5 %collective-permute-start.9 = (bf16[1,128,256]{2,1,0:T(8,128)(2,1)S(1)}, bf16[1,128,256]{2,1,0:T(8,128)(2,1)S(1)}, u32[]{:S(2)}, u32[]{:S(2)}) collective-permute-start(bf16[1,128,256]{2,1,0:T(8,128)(2,1)S(1)} %collective-permute-done.8.refs_2_), channel_id=1, source_target_pairs={{0,4},{2,6},{4,0},{6,2},{8,12},{10,14},{12,8},{14,10},{1,5},{3,7},... | collective-permute-start | bytes 196616 | tf_op jit(solution)/shard_map/ppermute | solution.py:199
  18.5 5.9 %collective-permute-start.3 = (f32[64,256]{1,0:T(8,128)S(1)}, f32[64,256]{1,0:T(8,128)S(1)}, u32[]{:S(2)}, u32[]{:S(2)}) collective-permute-start(f32[64,256]{1,0:T(8,128)S(1)} %pair_sum.1.refs_1_), channel_id=1, source_target_pairs={{0,8},{2,10},{4,12},{6,14},{8,0},{10,2},{12,4},{14,6},{1,9},{3,11}... | collective-permute-start | bytes 196616 | tf_op jit(solution)/shard_map/ppermute | solution.py:199
  21.5 4.3 %collective-permute-start.11 = (bf16[1,128,256]{2,1,0:T(8,128)(2,1)S(1)}, bf16[1,128,256]{2,1,0:T(8,128)(2,1)S(1)}, u32[]{:S(2)}, u32[]{:S(2)}) collective-permute-start(bf16[1,128,256]{2,1,0:T(8,128)(2,1)S(1)} %collective-permute-done.9.refs_1_), channel_id=1, source_target_pairs={{0,2},{2,0},{4,6},{6,4},{8,10},{10,8},{12,14},{14,12},{1,3},{3,1},... | collective-permute-start | bytes 196616 | tf_op jit(solution)/shard_map/ppermute | solution.py:199
  23.3 5.5 %collective-permute-start.6 = (bf16[512,1280]{1,0:T(8,128)(2,1)S(1)}, bf16[512,1280]{1,0:T(8,128)(2,1)S(1)}, u32[]{:S(2)}, u32[]{:S(2)}) collective-permute-start(bf16[512,1280]{1,0:T(8,128)(2,1)S(1)} %pass_dense.1), channel_id=1, source_target_pairs={{0,1},{1,0},{2,3},{3,2},{4,5},{5,4},{6,7},{7,6},{8,9},{9,8},{10,11... | collective-permute-start | bytes 3932168 | tf_op jit(solution)/shard_map/ppermute | solution.py:196
  24.5 3.7 %collective-permute-start.4 = (bf16[64,256]{1,0:T(8,128)(2,1)S(1)}, bf16[64,256]{1,0:T(8,128)(2,1)S(1)}, u32[]{:S(2)}, u32[]{:S(2)}) collective-permute-start(bf16[64,256]{1,0:T(8,128)(2,1)S(1)} %hub_sums.1.refs_0_.refs_4_), channel_id=1, source_target_pairs={{0,3},{1,2},{2,1},{3,0},{4,7},{5,6},{6,5},{7,4},{8,11},{9,10},{10,... | collective-permute-start | bytes 98312 | tf_op jit(solution)/shard_map/ppermute | solution.py:206
  25.8 3.0 %collective-permute-start.12 = (bf16[8,128,256]{2,1,0:T(8,128)(2,1)S(1)}, bf16[8,128,256]{2,1,0:T(8,128)(2,1)S(1)}, u32[]{:S(2)}, u32[]{:S(2)}) collective-permute-start(bf16[8,128,256]{2,1,0:T(8,128)(2,1)S(1)} %join_blocks.1.refs_0_), channel_id=1, source_target_pairs={{0,1},{1,0},{2,3},{3,2},{4,5},{5,4},{6,7},{7,6},{8,9},{9,8},{10,11... | collective-permute-start | bytes 1572872 | tf_op jit(solution)/shard_map/ppermute | solution.py:196
  28.2 1.3 %collective-permute-start.5 = (bf16[2,64,256]{2,1,0:T(8,128)(2,1)S(1)}, bf16[2,64,256]{2,1,0:T(8,128)(2,1)S(1)}, u32[]{:S(2)}, u32[]{:S(2)}) collective-permute-start(bf16[2,64,256]{2,1,0:T(8,128)(2,1)S(1)} %join_sides.1.refs_1_), channel_id=1, source_target_pairs={{0,1},{1,0},{2,3},{3,2},{4,5},{5,4},{6,7},{7,6},{8,9},{9,8},{10,11... | collective-permute-start | bytes 196616 | tf_op jit(solution)/shard_map/ppermute | solution.py:196

commit v34 on v33

--- a/solution.py
+++ b/solution.py
@@ -37,10 +37,10 @@
     return prod[:rows] + prod[rows:]
 
 
-def half_terms(dims, core, total, panel, out_ref, dense_ref):
+def half_terms(dims, core, total, panel, outs, dense_ref):
     n_row, n_col, side = dims
     piece = H // (n_row * n_col)
-    half = out_ref.shape[0]
+    half = dense_ref.shape[0] // 2
     chunks = [(0, core * VB, VB)]
     for r in range(n_row):
         chunks.append((VB + r * piece, n_col * VB + (r * n_col + core) * piece, piece))
@@ -49,10 +49,14 @@
         high = whole.astype(jnp.bfloat16)
         dense_ref[to:to + size] = high
         dense_ref[half + to:half + to + size] = (whole - high.astype(jnp.float32)).astype(jnp.bfloat16)
-    out_ref[...] = product(dense_ref[...], panel[...])
-
-
-def first_kernel(dims, tiles_ref, rows_hbm, cols_hbm, count_hbm, src_hbm, send_ref, dense_send_ref, total, panel,
+    prod = product(dense_ref[...], panel[...])
+    at = 0
+    for ref in outs:
+        ref[...] = prod[at:at + ref.shape[0]]
+        at += ref.shape[0]
+
+
+def first_kernel(dims, tiles_ref, rows_hbm, cols_hbm, count_hbm, src_hbm, send_ref, hubs_ref, dense_send_ref, total, panel,
                  held, rows_ref, cols_ref, count_ref, src_ref, sems, small):
     n_row, n_col, side = dims
     n_rows = n_col * VB + H
@@ -87,11 +91,11 @@
     for i, copy in enumerate(copies):
         copy.wait()
         lax.fori_loop(i * CHUNK, (i + 1) * CHUNK, add_tile, 0, unroll=4)
-    half_terms(dims, 1 - c, total, panel, send_ref, dense_send_ref)
+    half_terms(dims, 1 - c, total, panel, (send_ref, hubs_ref), dense_send_ref)
 
 
 def keep_kernel(dims, total_ref, panel_ref, keep_ref, dense_ref):
-    half_terms(dims, lax.axis_index("col"), total_ref, panel_ref, keep_ref, dense_ref)
+    half_terms(dims, lax.axis_index("col"), total_ref, panel_ref, (keep_ref,), dense_ref)
 
 
 def score_columns_kernel(dims, blocks_ref, dense_ref, part_ref, panel):
@@ -133,13 +137,18 @@
     return DAMP * (keep_ref[:VB] + came_ref[:VB]) + 0.15 * tele
 
 
-def spread_kernel(dims, src_ref, keep_ref, came_ref, scores_ref, hold_ref, pass_ref):
+def spread_kernel(keep_ref, came_ref, hold_ref, pass_ref):
     quarter = hold_ref.shape[0]
     x = lax.axis_index("row") % X
     for ref, place in ((hold_ref, x), (pass_ref, 1 - x)):
-        spot = pl.ds(pl.multiple_of(VB + place * quarter, quarter), quarter)
-        ref[...] = keep_ref[spot, :] + came_ref[spot, :]
-    scores_ref[0] = own_scores(dims, src_ref, keep_ref, came_ref).astype(scores_ref.dtype)
+        ref[...] = keep_ref[pl.ds(pl.multiple_of(VB + place * quarter, quarter), quarter), :] + came_ref[pl.ds(
+            pl.multiple_of(place * quarter, quarter), quarter), :]
+
+
+def scores_kernel(dims, src_ref, keep_ref, came_ref, scores_ref):
+    first = H + (lax.axis_index("row") * dims[1] + lax.axis_index("col")) * VB
+    tele = one_hot(first, VB, src_ref[...])
+    scores_ref[0] = (DAMP * (keep_ref[:VB] + came_ref[...]) + 0.15 * tele).astype(scores_ref.dtype)
 
 
 def join_kernel(*refs):
@@ -225,11 +234,11 @@
     in_hbm = [pltpu.with_memory_space_constraint(x, pltpu.HBM) for x in (
         tiles.reshape(slots, side, side), tile_row.reshape(slots), tile_col.reshape(slots), src)]
     dense_shape = bf16((2 * half, n_cols))
-    send, dense_send, total, panel = pl.pallas_call(
+    send, send_hubs, dense_send, total, panel = pl.pallas_call(
         bind(first_kernel, dims),
-        out_shape=(f32((half, width)), dense_shape, f32((n_rows + side, n_cols)), bf16((n_cols, width))),
+        out_shape=(f32((VB, width)), f32((half - VB, width)), dense_shape, f32((n_rows + side, n_cols)), bf16((n_cols, width))),
         in_specs=[HBM] * 5,
-        out_specs=[VMEM] * 4,
+        out_specs=[VMEM] * 5,
         scratch_shapes=[
             pltpu.VMEM((slots, side, side), jnp.bfloat16),
             pltpu.SMEM((slots,), jnp.int32),
@@ -244,11 +253,9 @@
     )(*in_hbm[:3], tile_count.reshape(1), in_hbm[3])
 
     keep, dense_keep = call(bind(keep_kernel, dims), "keep_terms", (f32((half, width)), dense_shape), total, panel, cost=1)
-    held, hold, away = call(
-        bind(spread_kernel, dims), "spread",
-        (bf16((1, VB, width)), f32((quarter, width)), f32((quarter, width))),
-        src, keep, other_core(send), cost=0)
+    hold, away = call(spread_kernel, "spread", (f32((quarter, width)),) * 2, keep, other_core(send_hubs), cost=2)
     away = other_side(away)
+    held = call(bind(scores_kernel, dims), "scores", bf16((1, VB, width)), src, keep, other_core(send))
     next_z, far_z = to_partner(held, X), to_partner(held, 2 * X)
     last = to_partner(far_z, X)
     first = call(join_kernel, "join_first", bf16((3, VB, width)), held, next_z, far_z, cost=0)

time: 41.3 us -> 41.1 us (level)
    ppermute x4 -> x5, starting transfers between devices: 1.13 us -> 0.87 us  [other_core(): return lax.ppermute(x, 'col', [(0, 1), (1, 0)])]
    pallas_call x13 -> x14, Pallas kernels: 2.69 us -> 2.72 us  [call(): pl.pallas_call(body, out_shape=out_shape, in_specs=[VMEM] * len(args) + [...]
  transfers between devices with their start and end apart: 13 -> 14, of which waited for: 8 -> 8; matrix products, arithmetic and copies ran while one was open for 0% -> 0% of each run, Pallas kernels for 4% -> 4%
where the time goes in v34:
time: 41.1 us; the launch traced here: 40.9 us
  starting transfers between devices  13.6 us (33%)
  blocking collectives  10.6 us (26%)
  waiting for transfers between devices  9.54 us (23%)
  Pallas kernels  5.69 us (14%)
  between operations  1.4 us (3%)
    ppermute x8, starting transfers between devices, to_partner(): return lax.ppermute(x, 'row', [(r, r ^ flip) for r in range(n_row)])  12.7 us
    all_to_all x1, blocking collectives, fast_body(): parts = lax.all_to_all(parts, 'row', 0, 0)  10.6 us
    ppermute x8, waiting for transfers between devices, to_partner(): return lax.ppermute(x, 'row', [(r, r ^ flip) for r in range(n_row)])  7.16 us
    pallas_call x1, Pallas kernels, fast_body(): pl.pallas_call(bind(first_kernel, dims), out_shape=(f32((VB, width)), f32...  2.98 us
    pallas_call x14, Pallas kernels, call(): pl.pallas_call(body, out_shape=out_shape, in_specs=[VMEM] * len(args) + [...  2.72 us
    ppermute x1, waiting for transfers between devices, cross(): lax.ppermute(x, ('row', 'col'), [(r * n_col + c, (r ^ 1) * n_col + 1 - c)...  1.85 us
    ppermute x5, starting transfers between devices, other_core(): return lax.ppermute(x, 'col', [(0, 1), (1, 0)])  0.87 us
  transfers between devices with their start and end apart: 14, of which 8 were waited for; matrix products, arithmetic and copies ran while one was open for 0% of the time, Pallas kernels for 4%

profile of v34, /device:TPU:0, one launch (start us, length us, event | category | flops | bytes accessed | tf_op | source)
XLA Modules:
  0.0 40.9 jit_solution(1924372713415520785)
XLA Ops:
  1.3 3.0 %first_terms.1 = (f32[128,256]{1,0:T(8,128)S(1)}, f32[128,256]{1,0:T(8,128)S(1)}, bf16[512,1280]{1,0:T(8,128)(2,1)S(1)}, f32[640,1280]{1,0:T(8,128)S(1)}, bf16[1280,256]{1,0:T(8,128)(2,1)S(1)}) custom-call(bf16[96,128,128]{2,1,0:T(8,128)(2,1)} %bitcast.12, s32[96]{0:T(128)} %bitcast.13, s32[96]{0:T(128)} %bitcast.14, s32[1]{0:T(128)} %bitcast.6.count_hbm, ...), custom_call_target="tpu_custom_call" | custom-call | tf_op jit(solution)/shard_map/first_terms/pallas_call | solution.py:237
  4.3 0.5 %collective-permute-start = (f32[128,256]{1,0:T(8,128)S(1)}, f32[128,256]{1,0:T(8,128)S(1)}, u32[]{:S(2)}, u32[]{:S(2)}) collective-permute-start(f32[128,256]{1,0:T(8,128)S(1)} %get-tuple-element.18), channel_id=1, source_target_pairs={{0,1},{1,0},{2,3},{3,2},{4,5},{5,4},{6,7},{7,6},{8,9},{9,8},{10,11... | collective-permute-start | bytes 393224 | tf_op jit(solution)/shard_map/ppermute | solution.py:205
  4.8 0.1 collective-permute-start.7
  4.9 0.5 %keep_terms.1 = (f32[256,256]{1,0:T(8,128)S(1)}, bf16[512,1280]{1,0:T(8,128)(2,1)S(1)}) custom-call(f32[640,1280]{1,0:T(8,128)S(1)} %get-tuple-element.15.refs_0_, bf16[1280,256]{1,0:T(8,128)(2,1)S(1)} %get-tuple-element.16.refs_1_), custom_call_target="tpu_custom_call" | custom-call | flops 1000000000 | tf_op jit(solution)/shard_map/keep_terms/pallas_call | solution.py:221
  5.4 0.4 collective-permute-done.refs_1_
  5.8 0.0 copy-start
  5.8 2.9 %collective-permute-start.1 = (f32[64,256]{1,0:T(8,128)S(1)}, f32[64,256]{1,0:T(8,128)S(1)}, u32[]{:S(2)}, u32[]{:S(2)}) collective-permute-start(f32[64,256]{1,0:T(8,128)S(1)} %get-tuple-element.20), channel_id=1, source_target_pairs={{0,2},{2,0},{4,6},{6,4},{8,10},{10,8},{12,14},{14,12},{1,3},{3,1},... | collective-permute-start | bytes 196616 | tf_op jit(solution)/shard_map/ppermute | solution.py:208
  8.7 0.0 collective-permute-done.7.refs_2_
  8.7 0.0 copy-done
  8.8 2.7 %collective-permute-start.9 = (bf16[1,128,256]{2,1,0:T(8,128)(2,1)S(1)}, bf16[1,128,256]{2,1,0:T(8,128)(2,1)S(1)}, u32[]{:S(2)}, u32[]{:S(2)}) collective-permute-start(bf16[1,128,256]{2,1,0:T(8,128)(2,1)S(1)} %scores.1.refs_0_), channel_id=1, source_target_pairs={{0,8},{2,10},{4,12},{6,14},{8,0},{10,2},{12,4},{14,6},{1,9},{3,11}... | collective-permute-start | bytes 196616 | tf_op jit(solution)/shard_map/ppermute | solution.py:208
  11.4 1.6 %collective-permute-start.8 = (bf16[1,128,256]{2,1,0:T(8,128)(2,1)S(1)}, bf16[1,128,256]{2,1,0:T(8,128)(2,1)S(1)}, u32[]{:S(2)}, u32[]{:S(2)}) collective-permute-start(bf16[1,128,256]{2,1,0:T(8,128)(2,1)S(1)} %scores.1.refs_0_), channel_id=1, source_target_pairs={{0,4},{2,6},{4,0},{6,2},{8,12},{10,14},{12,8},{14,10},{1,5},{3,7},... | collective-permute-start | bytes 196616 | tf_op jit(solution)/shard_map/ppermute | solution.py:208
  13.0 0.0 collective-permute-done.1.refs_1_
  13.0 0.5 %collective-permute-start.2 = (f32[64,256]{1,0:T(8,128)S(1)}, f32[64,256]{1,0:T(8,128)S(1)}, u32[]{:S(2)}, u32[]{:S(2)}) collective-permute-start(f32[64,256]{1,0:T(8,128)S(1)} %plane_sum.1.refs_0_), channel_id=1, source_target_pairs={{0,4},{2,6},{4,0},{6,2},{8,12},{10,14},{12,8},{14,10},{1,5},{3,7},... | collective-permute-start | bytes 196616 | tf_op jit(solution)/shard_map/ppermute | solution.py:208
  13.5 1.4 %collective-permute-done.9.refs_2_ = bf16[1,128,256]{2,1,0:T(8,128)(2,1)S(1)} collective-permute-done((bf16[1,128,256]{2,1,0:T(8,128)(2,1)S(1)}, bf16[1,128,256]{2,1,0:T(8,128)(2,1)S(1)}, u32[]{:S(2)}, u32[]{:S(2)}) %collective-permute-start.9) | collective-permute-done | bytes 65568 | tf_op jit(solution)/shard_map/ppermute | solution.py:208
  14.9 1.5 %collective-permute-done.8.refs_1_ = bf16[1,128,256]{2,1,0:T(8,128)(2,1)S(1)} collective-permute-done((bf16[1,128,256]{2,1,0:T(8,128)(2,1)S(1)}, bf16[1,128,256]{2,1,0:T(8,128)(2,1)S(1)}, u32[]{:S(2)}, u32[]{:S(2)}) %collective-permute-start.8) | collective-permute-done | bytes 65568 | tf_op jit(solution)/shard_map/ppermute | solution.py:208
  16.4 0.5 %collective-permute-start.11 = (bf16[3,128,256]{2,1,0:T(8,128)(2,1)S(1)}, bf16[3,128,256]{2,1,0:T(8,128)(2,1)S(1)}, u32[]{:S(2)}, u32[]{:S(2)}) collective-permute-start(bf16[3,128,256]{2,1,0:T(8,128)(2,1)S(1)} %join_first.1.refs_0_), channel_id=1, source_target_pairs={{0,2},{2,0},{4,6},{6,4},{8,10},{10,8},{12,14},{14,12},{1,3},{3,1},... | collective-permute-start | bytes 589832 | tf_op jit(solution)/shard_map/ppermute | solution.py:208
  16.9 1.6 %collective-permute-start.10 = (bf16[1,128,256]{2,1,0:T(8,128)(2,1)S(1)}, bf16[1,128,256]{2,1,0:T(8,128)(2,1)S(1)}, u32[]{:S(2)}, u32[]{:S(2)}) collective-permute-start(bf16[1,128,256]{2,1,0:T(8,128)(2,1)S(1)} %collective-permute-done.9.refs_2_), channel_id=1, source_target_pairs={{0,4},{2,6},{4,0},{6,2},{8,12},{10,14},{12,8},{14,10},{1,5},{3,7},... | collective-permute-start | bytes 196616 | tf_op jit(solution)/shard_map/ppermute | solution.py:208
  18.5 0.0 collective-permute-done.2.refs_1_
  18.5 1.7 %collective-permute-start.3 = (f32[64,256]{1,0:T(8,128)S(1)}, f32[64,256]{1,0:T(8,128)S(1)}, u32[]{:S(2)}, u32[]{:S(2)}) collective-permute-start(f32[64,256]{1,0:T(8,128)S(1)} %pair_sum.1.refs_1_), channel_id=1, source_target_pairs={{0,8},{2,10},{4,12},{6,14},{8,0},{10,2},{12,4},{14,6},{1,9},{3,11}... | collective-permute-start | bytes 196616 | tf_op jit(solution)/shard_map/ppermute | solution.py:208
  20.1 1.6 %collective-permute-done.10.refs_1_ = bf16[1,128,256]{2,1,0:T(8,128)(2,1)S(1)} collective-permute-done((bf16[1,128,256]{2,1,0:T(8,128)(2,1)S(1)}, bf16[1,128,256]{2,1,0:T(8,128)(2,1)S(1)}, u32[]{:S(2)}, u32[]{:S(2)}) %collective-permute-start.10) | collective-permute-done | bytes 65568 | tf_op jit(solution)/shard_map/ppermute | solution.py:208
  21.8 1.3 %collective-permute-start.12 = (bf16[1,128,256]{2,1,0:T(8,128)(2,1)S(1)}, bf16[1,128,256]{2,1,0:T(8,128)(2,1)S(1)}, u32[]{:S(2)}, u32[]{:S(2)}) collective-permute-start(bf16[1,128,256]{2,1,0:T(8,128)(2,1)S(1)} %collective-permute-done.10.refs_1_), channel_id=1, source_target_pairs={{0,2},{2,0},{4,6},{6,4},{8,10},{10,8},{12,14},{14,12},{1,3},{3,1},... | collective-permute-start | bytes 196616 | tf_op jit(solution)/shard_map/ppermute | solution.py:208
  23.1 0.1 pass_dense.1
  23.2 0.1 collective-permute-start.6
  23.3 1.1 %collective-permute-done.3.refs_2_ = f32[64,256]{1,0:T(8,128)S(1)} collective-permute-done((f32[64,256]{1,0:T(8,128)S(1)}, f32[64,256]{1,0:T(8,128)S(1)}, u32[]{:S(2)}, u32[]{:S(2)}) %collective-permute-start.3) | collective-permute-done | bytes 65568 | tf_op jit(solution)/shard_map/ppermute | solution.py:208
  24.4 0.1 collective-permute-start.4
  24.4 1.6 %collective-permute-done.12.refs_3_ = bf16[1,128,256]{2,1,0:T(8,128)(2,1)S(1)} collective-permute-done((bf16[1,128,256]{2,1,0:T(8,128)(2,1)S(1)}, bf16[1,128,256]{2,1,0:T(8,128)(2,1)S(1)}, u32[]{:S(2)}, u32[]{:S(2)}) %collective-permute-start.12) | collective-permute-done | bytes 65568 | tf_op jit(solution)/shard_map/ppermute | solution.py:208
  26.0 0.0 collective-permute-done.11.refs_2_
  26.1 0.1 collective-permute-start.13
  26.2 1.8 %collective-permute-done.4.refs_1_ = bf16[64,256]{1,0:T(8,128)(2,1)S(1)} collective-permute-done((bf16[64,256]{1,0:T(8,128)(2,1)S(1)}, bf16[64,256]{1,0:T(8,128)(2,1)S(1)}, u32[]{:S(2)}, u32[]{:S(2)}) %collective-permute-start.4) | collective-permute-done | bytes 32800 | tf_op jit(solution)/shard_map/ppermute | solution.py:215
  28.0 0.1 collective-permute-start.5
  28.1 0.5 %own_columns.1.refs_2_ = f32[256,256]{1,0:T(8,128)S(1)} custom-call(bf16[8,128,256]{2,1,0:T(8,128)(2,1)S(1)} %join_blocks.1.refs_0_, bf16[512,1280]{1,0:T(8,128)(2,1)S(1)} %get-tuple-element.21.refs_1_.refs_3_), custom_call_target="tpu_custom_call" | custom-call | tf_op jit(solution)/shard_map/own_columns/pallas_call | solution.py:221
  28.6 0.0 collective-permute-done.13.refs_0_
  28.6 0.0 collective-permute-done.6.refs_1_.refs_4_
  28.7 0.5 %other_columns.1.refs_5_ = f32[256,256]{1,0:T(8,128)S(1)} custom-call(bf16[8,128,256]{2,1,0:T(8,128)(2,1)S(1)} %collective-permute-done.13.refs_0_, bf16[512,1280]{1,0:T(8,128)(2,1)S(1)} %collective-permute-done.6.refs_1_.refs_4_, f32[256,256]{1,0:T(8,128)S(1)} %own_columns.1.refs_2_), custom_call_target="tpu_custom_call" | custom-call | tf_op jit(solution)/shard_map/other_columns/pallas_call | solution.py:221
  29.1 0.1 collective-permute-done.5.refs_2_
  29.3 0.3 hub_columns.1
  29.6 10.6 %all_to_all.5.refs_2_ = f32[8,16,256]{2,1,0:T(8,128)S(1)} all-to-all(f32[8,16,256]{2,1,0:T(8,128)S(1)} %get-tuple-element.25), channel_id=1, replica_groups=mesh['groups'=2,'row'=8,'col'=2] {'row'}, dimensions={0} | all-to-all | bytes 262144 | tf_op jit(solution)/shard_map/all_to_all | solution.py:278
  40.2 0.7 %last_hubs.1 = (f32[128,256]{1,0:T(8,128)}, f32[16,256]{1,0:T(8,128)}) custom-call(s32[1,256]{1,0:T(1,128)S(1)} %bitcast.11, f32[128,256]{1,0:T(8,128)S(1)} %get-tuple-element.24.refs_1_, f32[8,16,256]{2,1,0:T(8,128)S(1)} %all_to_all.5.refs_2_), custom_call_target="tpu_custom_call" | custom-call | tf_op jit(solution)/shard_map/last_hubs/pallas_call | solution.py:221
  (8 shorter events, 0.2 us)
Async XLA Ops:
  4.3 1.5 %collective-permute-start = (f32[128,256]{1,0:T(8,128)S(1)}, f32[128,256]{1,0:T(8,128)S(1)}, u32[]{:S(2)}, u32[]{:S(2)}) collective-permute-start(f32[128,256]{1,0:T(8,128)S(1)} %get-tuple-element.18), channel_id=1, source_target_pairs={{0,1},{1,0},{2,3},{3,2},{4,5},{5,4},{6,7},{7,6},{8,9},{9,8},{10,11... | collective-permute-start | bytes 393224 | tf_op jit(solution)/shard_map/ppermute | solution.py:205
  4.8 3.9 %collective-permute-start.7 = (f32[128,256]{1,0:T(8,128)S(1)}, f32[128,256]{1,0:T(8,128)S(1)}, u32[]{:S(2)}, u32[]{:S(2)}) collective-permute-start(f32[128,256]{1,0:T(8,128)S(1)} %get-tuple-element.23), channel_id=1, source_target_pairs={{0,1},{1,0},{2,3},{3,2},{4,5},{5,4},{6,7},{7,6},{8,9},{9,8},{10,11... | collective-permute-start | bytes 393224 | tf_op jit(solution)/shard_map/ppermute | solution.py:205
  5.8 2.9 %copy-start = (s32[256]{0:T(256)S(1)}, s32[256]{0:T(256)}, u32[]{:S(2)}) copy-start(s32[256]{0:T(256)} %param.9) | copy-start | bytes 3076
  5.8 7.2 %collective-permute-start.1 = (f32[64,256]{1,0:T(8,128)S(1)}, f32[64,256]{1,0:T(8,128)S(1)}, u32[]{:S(2)}, u32[]{:S(2)}) collective-permute-start(f32[64,256]{1,0:T(8,128)S(1)} %get-tuple-element.20), channel_id=1, source_target_pairs={{0,2},{2,0},{4,6},{6,4},{8,10},{10,8},{12,14},{14,12},{1,3},{3,1},... | collective-permute-start | bytes 196616 | tf_op jit(solution)/shard_map/ppermute | solution.py:208
  8.8 6.1 %collective-permute-start.9 = (bf16[1,128,256]{2,1,0:T(8,128)(2,1)S(1)}, bf16[1,128,256]{2,1,0:T(8,128)(2,1)S(1)}, u32[]{:S(2)}, u32[]{:S(2)}) collective-permute-start(bf16[1,128,256]{2,1,0:T(8,128)(2,1)S(1)} %scores.1.refs_0_), channel_id=1, source_target_pairs={{0,8},{2,10},{4,12},{6,14},{8,0},{10,2},{12,4},{14,6},{1,9},{3,11}... | collective-permute-start | bytes 196616 | tf_op jit(solution)/shard_map/ppermute | solution.py:208
  11.4 5.0 %collective-permute-start.8 = (bf16[1,128,256]{2,1,0:T(8,128)(2,1)S(1)}, bf16[1,128,256]{2,1,0:T(8,128)(2,1)S(1)}, u32[]{:S(2)}, u32[]{:S(2)}) collective-permute-start(bf16[1,128,256]{2,1,0:T(8,128)(2,1)S(1)} %scores.1.refs_0_), channel_id=1, source_target_pairs={{0,4},{2,6},{4,0},{6,2},{8,12},{10,14},{12,8},{14,10},{1,5},{3,7},... | collective-permute-start | bytes 196616 | tf_op jit(solution)/shard_map/ppermute | solution.py:208
  13.0 5.5 %collective-permute-start.2 = (f32[64,256]{1,0:T(8,128)S(1)}, f32[64,256]{1,0:T(8,128)S(1)}, u32[]{:S(2)}, u32[]{:S(2)}) collective-permute-start(f32[64,256]{1,0:T(8,128)S(1)} %plane_sum.1.refs_0_), channel_id=1, source_target_pairs={{0,4},{2,6},{4,0},{6,2},{8,12},{10,14},{12,8},{14,10},{1,5},{3,7},... | collective-permute-start | bytes 196616 | tf_op jit(solution)/shard_map/ppermute | solution.py:208
  16.4 9.6 %collective-permute-start.11 = (bf16[3,128,256]{2,1,0:T(8,128)(2,1)S(1)}, bf16[3,128,256]{2,1,0:T(8,128)(2,1)S(1)}, u32[]{:S(2)}, u32[]{:S(2)}) collective-permute-start(bf16[3,128,256]{2,1,0:T(8,128)(2,1)S(1)} %join_first.1.refs_0_), channel_id=1, source_target_pairs={{0,2},{2,0},{4,6},{6,4},{8,10},{10,8},{12,14},{14,12},{1,3},{3,1},... | collective-permute-start | bytes 589832 | tf_op jit(solution)/shard_map/ppermute | solution.py:208
  16.9 4.9 %collective-permute-start.10 = (bf16[1,128,256]{2,1,0:T(8,128)(2,1)S(1)}, bf16[1,128,256]{2,1,0:T(8,128)(2,1)S(1)}, u32[]{:S(2)}, u32[]{:S(2)}) collective-permute-start(bf16[1,128,256]{2,1,0:T(8,128)(2,1)S(1)} %collective-permute-done.9.refs_2_), channel_id=1, source_target_pairs={{0,4},{2,6},{4,0},{6,2},{8,12},{10,14},{12,8},{14,10},{1,5},{3,7},... | collective-permute-start | bytes 196616 | tf_op jit(solution)/shard_map/ppermute | solution.py:208
  18.5 5.8 %collective-permute-start.3 = (f32[64,256]{1,0:T(8,128)S(1)}, f32[64,256]{1,0:T(8,128)S(1)}, u32[]{:S(2)}, u32[]{:S(2)}) collective-permute-start(f32[64,256]{1,0:T(8,128)S(1)} %pair_sum.1.refs_1_), channel_id=1, source_target_pairs={{0,8},{2,10},{4,12},{6,14},{8,0},{10,2},{12,4},{14,6},{1,9},{3,11}... | collective-permute-start | bytes 196616 | tf_op jit(solution)/shard_map/ppermute | solution.py:208
  21.8 4.3 %collective-permute-start.12 = (bf16[1,128,256]{2,1,0:T(8,128)(2,1)S(1)}, bf16[1,128,256]{2,1,0:T(8,128)(2,1)S(1)}, u32[]{:S(2)}, u32[]{:S(2)}) collective-permute-start(bf16[1,128,256]{2,1,0:T(8,128)(2,1)S(1)} %collective-permute-done.10.refs_1_), channel_id=1, source_target_pairs={{0,2},{2,0},{4,6},{6,4},{8,10},{10,8},{12,14},{14,12},{1,3},{3,1},... | collective-permute-start | bytes 196616 | tf_op jit(solution)/shard_map/ppermute | solution.py:208
  23.2 5.5 %collective-permute-start.6 = (bf16[512,1280]{1,0:T(8,128)(2,1)S(1)}, bf16[512,1280]{1,0:T(8,128)(2,1)S(1)}, u32[]{:S(2)}, u32[]{:S(2)}) collective-permute-start(bf16[512,1280]{1,0:T(8,128)(2,1)S(1)} %pass_dense.1), channel_id=1, source_target_pairs={{0,1},{1,0},{2,3},{3,2},{4,5},{5,4},{6,7},{7,6},{8,9},{9,8},{10,11... | collective-permute-start | bytes 3932168 | tf_op jit(solution)/shard_map/ppermute | solution.py:205
  24.4 3.7 %collective-permute-start.4 = (bf16[64,256]{1,0:T(8,128)(2,1)S(1)}, bf16[64,256]{1,0:T(8,128)(2,1)S(1)}, u32[]{:S(2)}, u32[]{:S(2)}) collective-permute-start(bf16[64,256]{1,0:T(8,128)(2,1)S(1)} %hub_sums.1.refs_0_.refs_4_), channel_id=1, source_target_pairs={{0,3},{1,2},{2,1},{3,0},{4,7},{5,6},{6,5},{7,4},{8,11},{9,10},{10,... | collective-permute-start | bytes 98312 | tf_op jit(solution)/shard_map/ppermute | solution.py:215
  26.1 2.5 %collective-permute-start.13 = (bf16[8,128,256]{2,1,0:T(8,128)(2,1)S(1)}, bf16[8,128,256]{2,1,0:T(8,128)(2,1)S(1)}, u32[]{:S(2)}, u32[]{:S(2)}) collective-permute-start(bf16[8,128,256]{2,1,0:T(8,128)(2,1)S(1)} %join_blocks.1.refs_0_), channel_id=1, source_target_pairs={{0,1},{1,0},{2,3},{3,2},{4,5},{5,4},{6,7},{7,6},{8,9},{9,8},{10,11... | collective-permute-start | bytes 1572872 | tf_op jit(solution)/shard_map/ppermute | solution.py:205
  28.0 1.3 %collective-permute-start.5 = (bf16[2,64,256]{2,1,0:T(8,128)(2,1)S(1)}, bf16[2,64,256]{2,1,0:T(8,128)(2,1)S(1)}, u32[]{:S(2)}, u32[]{:S(2)}) collective-permute-start(bf16[2,64,256]{2,1,0:T(8,128)(2,1)S(1)} %join_sides.1.refs_1_), channel_id=1, source_target_pairs={{0,1},{1,0},{2,3},{3,2},{4,5},{5,4},{6,7},{7,6},{8,9},{9,8},{10,11... | collective-permute-start | bytes 196616 | tf_op jit(solution)/shard_map/ppermute | solution.py:205

commit v35 on v34

--- a/solution.py
+++ b/solution.py
@@ -90,7 +90,7 @@
 
     for i, copy in enumerate(copies):
         copy.wait()
-        lax.fori_loop(i * CHUNK, (i + 1) * CHUNK, add_tile, 0, unroll=4)
+        lax.fori_loop(i * CHUNK, (i + 1) * CHUNK, add_tile, 0, unroll=8)
     half_terms(dims, 1 - c, total, panel, (send_ref, hubs_ref), dense_send_ref)
 
 

time: 41.1 us -> 41 us (level)
  no operation moved by 1% of the time
where the time goes in v35:
time: 41 us; the launch traced here: 40.9 us
  starting transfers between devices  13.6 us (33%)
  blocking collectives  10.8 us (26%)
  waiting for transfers between devices  9.47 us (23%)
  Pallas kernels  5.6 us (14%)
  between operations  1.4 us (3%)
    ppermute x8, starting transfers between devices, to_partner(): return lax.ppermute(x, 'row', [(r, r ^ flip) for r in range(n_row)])  12.7 us
    all_to_all x1, blocking collectives, fast_body(): parts = lax.all_to_all(parts, 'row', 0, 0)  10.8 us
    ppermute x8, waiting for transfers between devices, to_partner(): return lax.ppermute(x, 'row', [(r, r ^ flip) for r in range(n_row)])  7.18 us
    pallas_call x1, Pallas kernels, fast_body(): pl.pallas_call(bind(first_kernel, dims), out_shape=(f32((VB, width)), f32...  2.89 us
    pallas_call x14, Pallas kernels, call(): pl.pallas_call(body, out_shape=out_shape, in_specs=[VMEM] * len(args) + [...  2.71 us
    ppermute x1, waiting for transfers between devices, cross(): lax.ppermute(x, ('row', 'col'), [(r * n_col + c, (r ^ 1) * n_col + 1 - c)...  1.75 us
    ppermute x5, starting transfers between devices, other_core(): return lax.ppermute(x, 'col', [(0, 1), (1, 0)])  0.9 us
  transfers between devices with their start and end apart: 14, of which 8 were waited for; matrix products, arithmetic and copies ran while one was open for 0% of the time, Pallas kernels for 4%

profile of v35, /device:TPU:0, one launch (start us, length us, event | category | flops | bytes accessed | tf_op | source)
XLA Modules:
  0.0 40.9 jit_solution(3917195238949790376)
XLA Ops:
  1.3 2.9 %first_terms.1 = (f32[128,256]{1,0:T(8,128)S(1)}, f32[128,256]{1,0:T(8,128)S(1)}, bf16[512,1280]{1,0:T(8,128)(2,1)S(1)}, f32[640,1280]{1,0:T(8,128)S(1)}, bf16[1280,256]{1,0:T(8,128)(2,1)S(1)}) custom-call(bf16[96,128,128]{2,1,0:T(8,128)(2,1)} %bitcast.12, s32[96]{0:T(128)} %bitcast.13, s32[96]{0:T(128)} %bitcast.14, s32[1]{0:T(128)} %bitcast.6.count_hbm, ...), custom_call_target="tpu_custom_call" | custom-call | tf_op jit(solution)/shard_map/first_terms/pallas_call | solution.py:237
  4.2 0.5 %collective-permute-start = (f32[128,256]{1,0:T(8,128)S(1)}, f32[128,256]{1,0:T(8,128)S(1)}, u32[]{:S(2)}, u32[]{:S(2)}) collective-permute-start(f32[128,256]{1,0:T(8,128)S(1)} %get-tuple-element.18), channel_id=1, source_target_pairs={{0,1},{1,0},{2,3},{3,2},{4,5},{5,4},{6,7},{7,6},{8,9},{9,8},{10,11... | collective-permute-start | bytes 393224 | tf_op jit(solution)/shard_map/ppermute | solution.py:205
  4.7 0.1 collective-permute-start.7
  4.8 0.5 %keep_terms.1 = (f32[256,256]{1,0:T(8,128)S(1)}, bf16[512,1280]{1,0:T(8,128)(2,1)S(1)}) custom-call(f32[640,1280]{1,0:T(8,128)S(1)} %get-tuple-element.15.refs_0_, bf16[1280,256]{1,0:T(8,128)(2,1)S(1)} %get-tuple-element.16.refs_1_), custom_call_target="tpu_custom_call" | custom-call | flops 1000000000 | tf_op jit(solution)/shard_map/keep_terms/pallas_call | solution.py:221
  5.3 0.4 collective-permute-done.refs_1_
  5.7 0.0 copy-start
  5.7 2.9 %collective-permute-start.1 = (f32[64,256]{1,0:T(8,128)S(1)}, f32[64,256]{1,0:T(8,128)S(1)}, u32[]{:S(2)}, u32[]{:S(2)}) collective-permute-start(f32[64,256]{1,0:T(8,128)S(1)} %get-tuple-element.20), channel_id=1, source_target_pairs={{0,2},{2,0},{4,6},{6,4},{8,10},{10,8},{12,14},{14,12},{1,3},{3,1},... | collective-permute-start | bytes 196616 | tf_op jit(solution)/shard_map/ppermute | solution.py:208
  8.6 0.0 collective-permute-done.7.refs_2_
  8.6 0.0 copy-done
  8.7 2.7 %collective-permute-start.9 = (bf16[1,128,256]{2,1,0:T(8,128)(2,1)S(1)}, bf16[1,128,256]{2,1,0:T(8,128)(2,1)S(1)}, u32[]{:S(2)}, u32[]{:S(2)}) collective-permute-start(bf16[1,128,256]{2,1,0:T(8,128)(2,1)S(1)} %scores.1.refs_0_), channel_id=1, source_target_pairs={{0,8},{2,10},{4,12},{6,14},{8,0},{10,2},{12,4},{14,6},{1,9},{3,11}... | collective-permute-start | bytes 196616 | tf_op jit(solution)/shard_map/ppermute | solution.py:208
  11.3 1.6 %collective-permute-start.8 = (bf16[1,128,256]{2,1,0:T(8,128)(2,1)S(1)}, bf16[1,128,256]{2,1,0:T(8,128)(2,1)S(1)}, u32[]{:S(2)}, u32[]{:S(2)}) collective-permute-start(bf16[1,128,256]{2,1,0:T(8,128)(2,1)S(1)} %scores.1.refs_0_), channel_id=1, source_target_pairs={{0,4},{2,6},{4,0},{6,2},{8,12},{10,14},{12,8},{14,10},{1,5},{3,7},... | collective-permute-start | bytes 196616 | tf_op jit(solution)/shard_map/ppermute | solution.py:208
  12.9 0.0 collective-permute-done.1.refs_1_
  12.9 0.5 %collective-permute-start.2 = (f32[64,256]{1,0:T(8,128)S(1)}, f32[64,256]{1,0:T(8,128)S(1)}, u32[]{:S(2)}, u32[]{:S(2)}) collective-permute-start(f32[64,256]{1,0:T(8,128)S(1)} %plane_sum.1.refs_0_), channel_id=1, source_target_pairs={{0,4},{2,6},{4,0},{6,2},{8,12},{10,14},{12,8},{14,10},{1,5},{3,7},... | collective-permute-start | bytes 196616 | tf_op jit(solution)/shard_map/ppermute | solution.py:208
  13.4 1.4 %collective-permute-done.9.refs_2_ = bf16[1,128,256]{2,1,0:T(8,128)(2,1)S(1)} collective-permute-done((bf16[1,128,256]{2,1,0:T(8,128)(2,1)S(1)}, bf16[1,128,256]{2,1,0:T(8,128)(2,1)S(1)}, u32[]{:S(2)}, u32[]{:S(2)}) %collective-permute-start.9) | collective-permute-done | bytes 65568 | tf_op jit(solution)/shard_map/ppermute | solution.py:208
  14.8 1.5 %collective-permute-done.8.refs_1_ = bf16[1,128,256]{2,1,0:T(8,128)(2,1)S(1)} collective-permute-done((bf16[1,128,256]{2,1,0:T(8,128)(2,1)S(1)}, bf16[1,128,256]{2,1,0:T(8,128)(2,1)S(1)}, u32[]{:S(2)}, u32[]{:S(2)}) %collective-permute-start.8) | collective-permute-done | bytes 65568 | tf_op jit(solution)/shard_map/ppermute | solution.py:208
  16.3 0.5 %collective-permute-start.11 = (bf16[3,128,256]{2,1,0:T(8,128)(2,1)S(1)}, bf16[3,128,256]{2,1,0:T(8,128)(2,1)S(1)}, u32[]{:S(2)}, u32[]{:S(2)}) collective-permute-start(bf16[3,128,256]{2,1,0:T(8,128)(2,1)S(1)} %join_first.1.refs_0_), channel_id=1, source_target_pairs={{0,2},{2,0},{4,6},{6,4},{8,10},{10,8},{12,14},{14,12},{1,3},{3,1},... | collective-permute-start | bytes 589832 | tf_op jit(solution)/shard_map/ppermute | solution.py:208
  16.8 1.6 %collective-permute-start.10 = (bf16[1,128,256]{2,1,0:T(8,128)(2,1)S(1)}, bf16[1,128,256]{2,1,0:T(8,128)(2,1)S(1)}, u32[]{:S(2)}, u32[]{:S(2)}) collective-permute-start(bf16[1,128,256]{2,1,0:T(8,128)(2,1)S(1)} %collective-permute-done.9.refs_2_), channel_id=1, source_target_pairs={{0,4},{2,6},{4,0},{6,2},{8,12},{10,14},{12,8},{14,10},{1,5},{3,7},... | collective-permute-start | bytes 196616 | tf_op jit(solution)/shard_map/ppermute | solution.py:208
  18.4 0.0 collective-permute-done.2.refs_1_
  18.4 1.7 %collective-permute-start.3 = (f32[64,256]{1,0:T(8,128)S(1)}, f32[64,256]{1,0:T(8,128)S(1)}, u32[]{:S(2)}, u32[]{:S(2)}) collective-permute-start(f32[64,256]{1,0:T(8,128)S(1)} %pair_sum.1.refs_1_), channel_id=1, source_target_pairs={{0,8},{2,10},{4,12},{6,14},{8,0},{10,2},{12,4},{14,6},{1,9},{3,11}... | collective-permute-start | bytes 196616 | tf_op jit(solution)/shard_map/ppermute | solution.py:208
  20.1 1.6 %collective-permute-done.10.refs_1_ = bf16[1,128,256]{2,1,0:T(8,128)(2,1)S(1)} collective-permute-done((bf16[1,128,256]{2,1,0:T(8,128)(2,1)S(1)}, bf16[1,128,256]{2,1,0:T(8,128)(2,1)S(1)}, u32[]{:S(2)}, u32[]{:S(2)}) %collective-permute-start.10) | collective-permute-done | bytes 65568 | tf_op jit(solution)/shard_map/ppermute | solution.py:208
  21.7 1.3 %collective-permute-start.12 = (bf16[1,128,256]{2,1,0:T(8,128)(2,1)S(1)}, bf16[1,128,256]{2,1,0:T(8,128)(2,1)S(1)}, u32[]{:S(2)}, u32[]{:S(2)}) collective-permute-start(bf16[1,128,256]{2,1,0:T(8,128)(2,1)S(1)} %collective-permute-done.10.refs_1_), channel_id=1, source_target_pairs={{0,2},{2,0},{4,6},{6,4},{8,10},{10,8},{12,14},{14,12},{1,3},{3,1},... | collective-permute-start | bytes 196616 | tf_op jit(solution)/shard_map/ppermute | solution.py:208
  23.0 0.1 pass_dense.1
  23.1 0.1 collective-permute-start.6
  23.1 1.0 %collective-permute-done.3.refs_2_ = f32[64,256]{1,0:T(8,128)S(1)} collective-permute-done((f32[64,256]{1,0:T(8,128)S(1)}, f32[64,256]{1,0:T(8,128)S(1)}, u32[]{:S(2)}, u32[]{:S(2)}) %collective-permute-start.3) | collective-permute-done | bytes 65568 | tf_op jit(solution)/shard_map/ppermute | solution.py:208
  24.2 0.1 collective-permute-start.4
  24.3 1.7 %collective-permute-done.12.refs_3_ = bf16[1,128,256]{2,1,0:T(8,128)(2,1)S(1)} collective-permute-done((bf16[1,128,256]{2,1,0:T(8,128)(2,1)S(1)}, bf16[1,128,256]{2,1,0:T(8,128)(2,1)S(1)}, u32[]{:S(2)}, u32[]{:S(2)}) %collective-permute-start.12) | collective-permute-done | bytes 65568 | tf_op jit(solution)/shard_map/ppermute | solution.py:208
  26.0 0.0 collective-permute-done.11.refs_2_
  26.0 0.1 collective-permute-start.13
  26.1 1.8 %collective-permute-done.4.refs_1_ = bf16[64,256]{1,0:T(8,128)(2,1)S(1)} collective-permute-done((bf16[64,256]{1,0:T(8,128)(2,1)S(1)}, bf16[64,256]{1,0:T(8,128)(2,1)S(1)}, u32[]{:S(2)}, u32[]{:S(2)}) %collective-permute-start.4) | collective-permute-done | bytes 32800 | tf_op jit(solution)/shard_map/ppermute | solution.py:215
  27.9 0.1 collective-permute-start.5
  28.0 0.5 %own_columns.1.refs_2_ = f32[256,256]{1,0:T(8,128)S(1)} custom-call(bf16[8,128,256]{2,1,0:T(8,128)(2,1)S(1)} %join_blocks.1.refs_0_, bf16[512,1280]{1,0:T(8,128)(2,1)S(1)} %get-tuple-element.21.refs_1_.refs_3_), custom_call_target="tpu_custom_call" | custom-call | tf_op jit(solution)/shard_map/own_columns/pallas_call | solution.py:221
  28.5 0.0 collective-permute-done.13.refs_0_
  28.5 0.0 collective-permute-done.6.refs_1_.refs_4_
  28.5 0.5 %other_columns.1.refs_5_ = f32[256,256]{1,0:T(8,128)S(1)} custom-call(bf16[8,128,256]{2,1,0:T(8,128)(2,1)S(1)} %collective-permute-done.13.refs_0_, bf16[512,1280]{1,0:T(8,128)(2,1)S(1)} %collective-permute-done.6.refs_1_.refs_4_, f32[256,256]{1,0:T(8,128)S(1)} %own_columns.1.refs_2_), custom_call_target="tpu_custom_call" | custom-call | tf_op jit(solution)/shard_map/other_columns/pallas_call | solution.py:221
  29.0 0.1 collective-permute-done.5.refs_2_
  29.1 0.3 hub_columns.1
  29.4 10.8 %all_to_all.5.refs_2_ = f32[8,16,256]{2,1,0:T(8,128)S(1)} all-to-all(f32[8,16,256]{2,1,0:T(8,128)S(1)} %get-tuple-element.25), channel_id=1, replica_groups=mesh['groups'=2,'row'=8,'col'=2] {'row'}, dimensions={0} | all-to-all | bytes 262144 | tf_op jit(solution)/shard_map/all_to_all | solution.py:278
  40.2 0.7 %last_hubs.1 = (f32[128,256]{1,0:T(8,128)}, f32[16,256]{1,0:T(8,128)}) custom-call(s32[1,256]{1,0:T(1,128)S(1)} %bitcast.11, f32[128,256]{1,0:T(8,128)S(1)} %get-tuple-element.24.refs_1_, f32[8,16,256]{2,1,0:T(8,128)S(1)} %all_to_all.5.refs_2_), custom_call_target="tpu_custom_call" | custom-call | tf_op jit(solution)/shard_map/last_hubs/pallas_call | solution.py:221
  (8 shorter events, 0.2 us)
Async XLA Ops:
  4.2 1.5 %collective-permute-start = (f32[128,256]{1,0:T(8,128)S(1)}, f32[128,256]{1,0:T(8,128)S(1)}, u32[]{:S(2)}, u32[]{:S(2)}) collective-permute-start(f32[128,256]{1,0:T(8,128)S(1)} %get-tuple-element.18), channel_id=1, source_target_pairs={{0,1},{1,0},{2,3},{3,2},{4,5},{5,4},{6,7},{7,6},{8,9},{9,8},{10,11... | collective-permute-start | bytes 393224 | tf_op jit(solution)/shard_map/ppermute | solution.py:205
  4.7 3.9 %collective-permute-start.7 = (f32[128,256]{1,0:T(8,128)S(1)}, f32[128,256]{1,0:T(8,128)S(1)}, u32[]{:S(2)}, u32[]{:S(2)}) collective-permute-start(f32[128,256]{1,0:T(8,128)S(1)} %get-tuple-element.23), channel_id=1, source_target_pairs={{0,1},{1,0},{2,3},{3,2},{4,5},{5,4},{6,7},{7,6},{8,9},{9,8},{10,11... | collective-permute-start | bytes 393224 | tf_op jit(solution)/shard_map/ppermute | solution.py:205
  5.7 2.9 %copy-start = (s32[256]{0:T(256)S(1)}, s32[256]{0:T(256)}, u32[]{:S(2)}) copy-start(s32[256]{0:T(256)} %param.9) | copy-start | bytes 3076
  5.7 7.2 %collective-permute-start.1 = (f32[64,256]{1,0:T(8,128)S(1)}, f32[64,256]{1,0:T(8,128)S(1)}, u32[]{:S(2)}, u32[]{:S(2)}) collective-permute-start(f32[64,256]{1,0:T(8,128)S(1)} %get-tuple-element.20), channel_id=1, source_target_pairs={{0,2},{2,0},{4,6},{6,4},{8,10},{10,8},{12,14},{14,12},{1,3},{3,1},... | collective-permute-start | bytes 196616 | tf_op jit(solution)/shard_map/ppermute | solution.py:208
  8.7 6.2 %collective-permute-start.9 = (bf16[1,128,256]{2,1,0:T(8,128)(2,1)S(1)}, bf16[1,128,256]{2,1,0:T(8,128)(2,1)S(1)}, u32[]{:S(2)}, u32[]{:S(2)}) collective-permute-start(bf16[1,128,256]{2,1,0:T(8,128)(2,1)S(1)} %scores.1.refs_0_), channel_id=1, source_target_pairs={{0,8},{2,10},{4,12},{6,14},{8,0},{10,2},{12,4},{14,6},{1,9},{3,11}... | collective-permute-start | bytes 196616 | tf_op jit(solution)/shard_map/ppermute | solution.py:208
  11.3 5.0 %collective-permute-start.8 = (bf16[1,128,256]{2,1,0:T(8,128)(2,1)S(1)}, bf16[1,128,256]{2,1,0:T(8,128)(2,1)S(1)}, u32[]{:S(2)}, u32[]{:S(2)}) collective-permute-start(bf16[1,128,256]{2,1,0:T(8,128)(2,1)S(1)} %scores.1.refs_0_), channel_id=1, source_target_pairs={{0,4},{2,6},{4,0},{6,2},{8,12},{10,14},{12,8},{14,10},{1,5},{3,7},... | collective-permute-start | bytes 196616 | tf_op jit(solution)/shard_map/ppermute | solution.py:208
  12.9 5.4 %collective-permute-start.2 = (f32[64,256]{1,0:T(8,128)S(1)}, f32[64,256]{1,0:T(8,128)S(1)}, u32[]{:S(2)}, u32[]{:S(2)}) collective-permute-start(f32[64,256]{1,0:T(8,128)S(1)} %plane_sum.1.refs_0_), channel_id=1, source_target_pairs={{0,4},{2,6},{4,0},{6,2},{8,12},{10,14},{12,8},{14,10},{1,5},{3,7},... | collective-permute-start | bytes 196616 | tf_op jit(solution)/shard_map/ppermute | solution.py:208
  16.3 9.7 %collective-permute-start.11 = (bf16[3,128,256]{2,1,0:T(8,128)(2,1)S(1)}, bf16[3,128,256]{2,1,0:T(8,128)(2,1)S(1)}, u32[]{:S(2)}, u32[]{:S(2)}) collective-permute-start(bf16[3,128,256]{2,1,0:T(8,128)(2,1)S(1)} %join_first.1.refs_0_), channel_id=1, source_target_pairs={{0,2},{2,0},{4,6},{6,4},{8,10},{10,8},{12,14},{14,12},{1,3},{3,1},... | collective-permute-start | bytes 589832 | tf_op jit(solution)/shard_map/ppermute | solution.py:208
  16.8 4.9 %collective-permute-start.10 = (bf16[1,128,256]{2,1,0:T(8,128)(2,1)S(1)}, bf16[1,128,256]{2,1,0:T(8,128)(2,1)S(1)}, u32[]{:S(2)}, u32[]{:S(2)}) collective-permute-start(bf16[1,128,256]{2,1,0:T(8,128)(2,1)S(1)} %collective-permute-done.9.refs_2_), channel_id=1, source_target_pairs={{0,4},{2,6},{4,0},{6,2},{8,12},{10,14},{12,8},{14,10},{1,5},{3,7},... | collective-permute-start | bytes 196616 | tf_op jit(solution)/shard_map/ppermute | solution.py:208
  18.4 5.8 %collective-permute-start.3 = (f32[64,256]{1,0:T(8,128)S(1)}, f32[64,256]{1,0:T(8,128)S(1)}, u32[]{:S(2)}, u32[]{:S(2)}) collective-permute-start(f32[64,256]{1,0:T(8,128)S(1)} %pair_sum.1.refs_1_), channel_id=1, source_target_pairs={{0,8},{2,10},{4,12},{6,14},{8,0},{10,2},{12,4},{14,6},{1,9},{3,11}... | collective-permute-start | bytes 196616 | tf_op jit(solution)/shard_map/ppermute | solution.py:208
  21.7 4.3 %collective-permute-start.12 = (bf16[1,128,256]{2,1,0:T(8,128)(2,1)S(1)}, bf16[1,128,256]{2,1,0:T(8,128)(2,1)S(1)}, u32[]{:S(2)}, u32[]{:S(2)}) collective-permute-start(bf16[1,128,256]{2,1,0:T(8,128)(2,1)S(1)} %collective-permute-done.10.refs_1_), channel_id=1, source_target_pairs={{0,2},{2,0},{4,6},{6,4},{8,10},{10,8},{12,14},{14,12},{1,3},{3,1},... | collective-permute-start | bytes 196616 | tf_op jit(solution)/shard_map/ppermute | solution.py:208
  23.1 5.4 %collective-permute-start.6 = (bf16[512,1280]{1,0:T(8,128)(2,1)S(1)}, bf16[512,1280]{1,0:T(8,128)(2,1)S(1)}, u32[]{:S(2)}, u32[]{:S(2)}) collective-permute-start(bf16[512,1280]{1,0:T(8,128)(2,1)S(1)} %pass_dense.1), channel_id=1, source_target_pairs={{0,1},{1,0},{2,3},{3,2},{4,5},{5,4},{6,7},{7,6},{8,9},{9,8},{10,11... | collective-permute-start | bytes 3932168 | tf_op jit(solution)/shard_map/ppermute | solution.py:205
  24.2 3.6 %collective-permute-start.4 = (bf16[64,256]{1,0:T(8,128)(2,1)S(1)}, bf16[64,256]{1,0:T(8,128)(2,1)S(1)}, u32[]{:S(2)}, u32[]{:S(2)}) collective-permute-start(bf16[64,256]{1,0:T(8,128)(2,1)S(1)} %hub_sums.1.refs_0_.refs_4_), channel_id=1, source_target_pairs={{0,3},{1,2},{2,1},{3,0},{4,7},{5,6},{6,5},{7,4},{8,11},{9,10},{10,... | collective-permute-start | bytes 98312 | tf_op jit(solution)/shard_map/ppermute | solution.py:215
  26.0 2.5 %collective-permute-start.13 = (bf16[8,128,256]{2,1,0:T(8,128)(2,1)S(1)}, bf16[8,128,256]{2,1,0:T(8,128)(2,1)S(1)}, u32[]{:S(2)}, u32[]{:S(2)}) collective-permute-start(bf16[8,128,256]{2,1,0:T(8,128)(2,1)S(1)} %join_blocks.1.refs_0_), channel_id=1, source_target_pairs={{0,1},{1,0},{2,3},{3,2},{4,5},{5,4},{6,7},{7,6},{8,9},{9,8},{10,11... | collective-permute-start | bytes 1572872 | tf_op jit(solution)/shard_map/ppermute | solution.py:205
  27.9 1.3 %collective-permute-start.5 = (bf16[2,64,256]{2,1,0:T(8,128)(2,1)S(1)}, bf16[2,64,256]{2,1,0:T(8,128)(2,1)S(1)}, u32[]{:S(2)}, u32[]{:S(2)}) collective-permute-start(bf16[2,64,256]{2,1,0:T(8,128)(2,1)S(1)} %join_sides.1.refs_1_), channel_id=1, source_target_pairs={{0,1},{1,0},{2,3},{3,2},{4,5},{5,4},{6,7},{7,6},{8,9},{9,8},{10,11... | collective-permute-start | bytes 196616 | tf_op jit(solution)/shard_map/ppermute | solution.py:205

commit v36 on v34

--- a/solution.py
+++ b/solution.py
@@ -12,7 +12,7 @@
 H = 256
 ITERS = 2
 DAMP = 0.85
-CHUNK = 8
+CHUNK = 4
 X = 2
 MICRO = 10 ** 9
 VMEM_LIMIT = 32 * 1024 * 1024

time: 41.1 us -> 41.4 us (level)
  no operation moved by 1% of the time
where the time goes in v36:
time: 41.4 us; the launch traced here: 41.2 us
  starting transfers between devices  13.7 us (33%)
  blocking collectives  10.6 us (26%)
  waiting for transfers between devices  9.55 us (23%)
  Pallas kernels  6.03 us (15%)
  between operations  1.4 us (3%)
    ppermute x8, starting transfers between devices, to_partner(): return lax.ppermute(x, 'row', [(r, r ^ flip) for r in range(n_row)])  12.7 us
    all_to_all x1, blocking collectives, fast_body(): parts = lax.all_to_all(parts, 'row', 0, 0)  10.6 us
    ppermute x8, waiting for transfers between devices, to_partner(): return lax.ppermute(x, 'row', [(r, r ^ flip) for r in range(n_row)])  7.16 us
    pallas_call x1, Pallas kernels, fast_body(): pl.pallas_call(bind(first_kernel, dims), out_shape=(f32((VB, width)), f32...  3.32 us
    pallas_call x14, Pallas kernels, call(): pl.pallas_call(body, out_shape=out_shape, in_specs=[VMEM] * len(args) + [...  2.72 us
    ppermute x1, waiting for transfers between devices, cross(): lax.ppermute(x, ('row', 'col'), [(r * n_col + c, (r ^ 1) * n_col + 1 - c)...  1.85 us
    ppermute x5, starting transfers between devices, other_core(): return lax.ppermute(x, 'col', [(0, 1), (1, 0)])  0.87 us
  transfers between devices with their start and end apart: 14, of which 8 were waited for; matrix products, arithmetic and copies ran while one was open for 0% of the time, Pallas kernels for 4%

profile of v36, /device:TPU:0, one launch (start us, length us, event | category | flops | bytes accessed | tf_op | source)
XLA Modules:
  0.0 41.2 jit_solution(3549501819590129842)
XLA Ops:
  1.3 3.3 %first_terms.1 = (f32[128,256]{1,0:T(8,128)S(1)}, f32[128,256]{1,0:T(8,128)S(1)}, bf16[512,1280]{1,0:T(8,128)(2,1)S(1)}, f32[640,1280]{1,0:T(8,128)S(1)}, bf16[1280,256]{1,0:T(8,128)(2,1)S(1)}) custom-call(bf16[96,128,128]{2,1,0:T(8,128)(2,1)} %bitcast.12, s32[96]{0:T(128)} %bitcast.13, s32[96]{0:T(128)} %bitcast.14, s32[1]{0:T(128)} %bitcast.6.count_hbm, ...), custom_call_target="tpu_custom_call" | custom-call | tf_op jit(solution)/shard_map/first_terms/pallas_call | solution.py:237
  4.6 0.5 %collective-permute-start = (f32[128,256]{1,0:T(8,128)S(1)}, f32[128,256]{1,0:T(8,128)S(1)}, u32[]{:S(2)}, u32[]{:S(2)}) collective-permute-start(f32[128,256]{1,0:T(8,128)S(1)} %get-tuple-element.18), channel_id=1, source_target_pairs={{0,1},{1,0},{2,3},{3,2},{4,5},{5,4},{6,7},{7,6},{8,9},{9,8},{10,11... | collective-permute-start | bytes 393224 | tf_op jit(solution)/shard_map/ppermute | solution.py:205
  5.1 0.1 collective-permute-start.7
  5.2 0.5 %keep_terms.1 = (f32[256,256]{1,0:T(8,128)S(1)}, bf16[512,1280]{1,0:T(8,128)(2,1)S(1)}) custom-call(f32[640,1280]{1,0:T(8,128)S(1)} %get-tuple-element.15.refs_0_, bf16[1280,256]{1,0:T(8,128)(2,1)S(1)} %get-tuple-element.16.refs_1_), custom_call_target="tpu_custom_call" | custom-call | flops 1000000000 | tf_op jit(solution)/shard_map/keep_terms/pallas_call | solution.py:221
  5.7 0.4 collective-permute-done.refs_1_
  6.1 0.0 copy-start
  6.1 2.9 %collective-permute-start.1 = (f32[64,256]{1,0:T(8,128)S(1)}, f32[64,256]{1,0:T(8,128)S(1)}, u32[]{:S(2)}, u32[]{:S(2)}) collective-permute-start(f32[64,256]{1,0:T(8,128)S(1)} %get-tuple-element.20), channel_id=1, source_target_pairs={{0,2},{2,0},{4,6},{6,4},{8,10},{10,8},{12,14},{14,12},{1,3},{3,1},... | collective-permute-start | bytes 196616 | tf_op jit(solution)/shard_map/ppermute | solution.py:208
  9.0 0.0 collective-permute-done.7.refs_2_
  9.0 0.0 copy-done
  9.1 2.7 %collective-permute-start.9 = (bf16[1,128,256]{2,1,0:T(8,128)(2,1)S(1)}, bf16[1,128,256]{2,1,0:T(8,128)(2,1)S(1)}, u32[]{:S(2)}, u32[]{:S(2)}) collective-permute-start(bf16[1,128,256]{2,1,0:T(8,128)(2,1)S(1)} %scores.1.refs_0_), channel_id=1, source_target_pairs={{0,8},{2,10},{4,12},{6,14},{8,0},{10,2},{12,4},{14,6},{1,9},{3,11}... | collective-permute-start | bytes 196616 | tf_op jit(solution)/shard_map/ppermute | solution.py:208
  11.8 1.6 %collective-permute-start.8 = (bf16[1,128,256]{2,1,0:T(8,128)(2,1)S(1)}, bf16[1,128,256]{2,1,0:T(8,128)(2,1)S(1)}, u32[]{:S(2)}, u32[]{:S(2)}) collective-permute-start(bf16[1,128,256]{2,1,0:T(8,128)(2,1)S(1)} %scores.1.refs_0_), channel_id=1, source_target_pairs={{0,4},{2,6},{4,0},{6,2},{8,12},{10,14},{12,8},{14,10},{1,5},{3,7},... | collective-permute-start | bytes 196616 | tf_op jit(solution)/shard_map/ppermute | solution.py:208
  13.3 0.0 collective-permute-done.1.refs_1_
  13.4 0.5 %collective-permute-start.2 = (f32[64,256]{1,0:T(8,128)S(1)}, f32[64,256]{1,0:T(8,128)S(1)}, u32[]{:S(2)}, u32[]{:S(2)}) collective-permute-start(f32[64,256]{1,0:T(8,128)S(1)} %plane_sum.1.refs_0_), channel_id=1, source_target_pairs={{0,4},{2,6},{4,0},{6,2},{8,12},{10,14},{12,8},{14,10},{1,5},{3,7},... | collective-permute-start | bytes 196616 | tf_op jit(solution)/shard_map/ppermute | solution.py:208
  13.9 1.4 %collective-permute-done.9.refs_2_ = bf16[1,128,256]{2,1,0:T(8,128)(2,1)S(1)} collective-permute-done((bf16[1,128,256]{2,1,0:T(8,128)(2,1)S(1)}, bf16[1,128,256]{2,1,0:T(8,128)(2,1)S(1)}, u32[]{:S(2)}, u32[]{:S(2)}) %collective-permute-start.9) | collective-permute-done | bytes 65568 | tf_op jit(solution)/shard_map/ppermute | solution.py:208
  15.2 1.5 %collective-permute-done.8.refs_1_ = bf16[1,128,256]{2,1,0:T(8,128)(2,1)S(1)} collective-permute-done((bf16[1,128,256]{2,1,0:T(8,128)(2,1)S(1)}, bf16[1,128,256]{2,1,0:T(8,128)(2,1)S(1)}, u32[]{:S(2)}, u32[]{:S(2)}) %collective-permute-start.8) | collective-permute-done | bytes 65568 | tf_op jit(solution)/shard_map/ppermute | solution.py:208
  16.7 0.5 %collective-permute-start.11 = (bf16[3,128,256]{2,1,0:T(8,128)(2,1)S(1)}, bf16[3,128,256]{2,1,0:T(8,128)(2,1)S(1)}, u32[]{:S(2)}, u32[]{:S(2)}) collective-permute-start(bf16[3,128,256]{2,1,0:T(8,128)(2,1)S(1)} %join_first.1.refs_0_), channel_id=1, source_target_pairs={{0,2},{2,0},{4,6},{6,4},{8,10},{10,8},{12,14},{14,12},{1,3},{3,1},... | collective-permute-start | bytes 589832 | tf_op jit(solution)/shard_map/ppermute | solution.py:208
  17.3 1.5 %collective-permute-start.10 = (bf16[1,128,256]{2,1,0:T(8,128)(2,1)S(1)}, bf16[1,128,256]{2,1,0:T(8,128)(2,1)S(1)}, u32[]{:S(2)}, u32[]{:S(2)}) collective-permute-start(bf16[1,128,256]{2,1,0:T(8,128)(2,1)S(1)} %collective-permute-done.9.refs_2_), channel_id=1, source_target_pairs={{0,4},{2,6},{4,0},{6,2},{8,12},{10,14},{12,8},{14,10},{1,5},{3,7},... | collective-permute-start | bytes 196616 | tf_op jit(solution)/shard_map/ppermute | solution.py:208
  18.8 0.0 collective-permute-done.2.refs_1_
  18.8 1.7 %collective-permute-start.3 = (f32[64,256]{1,0:T(8,128)S(1)}, f32[64,256]{1,0:T(8,128)S(1)}, u32[]{:S(2)}, u32[]{:S(2)}) collective-permute-start(f32[64,256]{1,0:T(8,128)S(1)} %pair_sum.1.refs_1_), channel_id=1, source_target_pairs={{0,8},{2,10},{4,12},{6,14},{8,0},{10,2},{12,4},{14,6},{1,9},{3,11}... | collective-permute-start | bytes 196616 | tf_op jit(solution)/shard_map/ppermute | solution.py:208
  20.5 1.6 %collective-permute-done.10.refs_1_ = bf16[1,128,256]{2,1,0:T(8,128)(2,1)S(1)} collective-permute-done((bf16[1,128,256]{2,1,0:T(8,128)(2,1)S(1)}, bf16[1,128,256]{2,1,0:T(8,128)(2,1)S(1)}, u32[]{:S(2)}, u32[]{:S(2)}) %collective-permute-start.10) | collective-permute-done | bytes 65568 | tf_op jit(solution)/shard_map/ppermute | solution.py:208
  22.1 1.3 %collective-permute-start.12 = (bf16[1,128,256]{2,1,0:T(8,128)(2,1)S(1)}, bf16[1,128,256]{2,1,0:T(8,128)(2,1)S(1)}, u32[]{:S(2)}, u32[]{:S(2)}) collective-permute-start(bf16[1,128,256]{2,1,0:T(8,128)(2,1)S(1)} %collective-permute-done.10.refs_1_), channel_id=1, source_target_pairs={{0,2},{2,0},{4,6},{6,4},{8,10},{10,8},{12,14},{14,12},{1,3},{3,1},... | collective-permute-start | bytes 196616 | tf_op jit(solution)/shard_map/ppermute | solution.py:208
  23.4 0.1 pass_dense.1
  23.5 0.1 collective-permute-start.6
  23.6 1.1 %collective-permute-done.3.refs_2_ = f32[64,256]{1,0:T(8,128)S(1)} collective-permute-done((f32[64,256]{1,0:T(8,128)S(1)}, f32[64,256]{1,0:T(8,128)S(1)}, u32[]{:S(2)}, u32[]{:S(2)}) %collective-permute-start.3) | collective-permute-done | bytes 65568 | tf_op jit(solution)/shard_map/ppermute | solution.py:208
  24.7 0.1 collective-permute-start.4
  24.8 1.6 %collective-permute-done.12.refs_3_ = bf16[1,128,256]{2,1,0:T(8,128)(2,1)S(1)} collective-permute-done((bf16[1,128,256]{2,1,0:T(8,128)(2,1)S(1)}, bf16[1,128,256]{2,1,0:T(8,128)(2,1)S(1)}, u32[]{:S(2)}, u32[]{:S(2)}) %collective-permute-start.12) | collective-permute-done | bytes 65568 | tf_op jit(solution)/shard_map/ppermute | solution.py:208
  26.4 0.0 collective-permute-done.11.refs_2_
  26.4 0.1 collective-permute-start.13
  26.5 1.9 %collective-permute-done.4.refs_1_ = bf16[64,256]{1,0:T(8,128)(2,1)S(1)} collective-permute-done((bf16[64,256]{1,0:T(8,128)(2,1)S(1)}, bf16[64,256]{1,0:T(8,128)(2,1)S(1)}, u32[]{:S(2)}, u32[]{:S(2)}) %collective-permute-start.4) | collective-permute-done | bytes 32800 | tf_op jit(solution)/shard_map/ppermute | solution.py:215
  28.4 0.1 collective-permute-start.5
  28.5 0.5 %own_columns.1.refs_2_ = f32[256,256]{1,0:T(8,128)S(1)} custom-call(bf16[8,128,256]{2,1,0:T(8,128)(2,1)S(1)} %join_blocks.1.refs_0_, bf16[512,1280]{1,0:T(8,128)(2,1)S(1)} %get-tuple-element.21.refs_1_.refs_3_), custom_call_target="tpu_custom_call" | custom-call | tf_op jit(solution)/shard_map/own_columns/pallas_call | solution.py:221
  29.0 0.0 collective-permute-done.13.refs_0_
  29.0 0.0 collective-permute-done.6.refs_1_.refs_4_
  29.0 0.5 %other_columns.1.refs_5_ = f32[256,256]{1,0:T(8,128)S(1)} custom-call(bf16[8,128,256]{2,1,0:T(8,128)(2,1)S(1)} %collective-permute-done.13.refs_0_, bf16[512,1280]{1,0:T(8,128)(2,1)S(1)} %collective-permute-done.6.refs_1_.refs_4_, f32[256,256]{1,0:T(8,128)S(1)} %own_columns.1.refs_2_), custom_call_target="tpu_custom_call" | custom-call | tf_op jit(solution)/shard_map/other_columns/pallas_call | solution.py:221
  29.5 0.1 collective-permute-done.5.refs_2_
  29.6 0.3 hub_columns.1
  30.0 10.6 %all_to_all.5.refs_2_ = f32[8,16,256]{2,1,0:T(8,128)S(1)} all-to-all(f32[8,16,256]{2,1,0:T(8,128)S(1)} %get-tuple-element.25), channel_id=1, replica_groups=mesh['groups'=2,'row'=8,'col'=2] {'row'}, dimensions={0} | all-to-all | bytes 262144 | tf_op jit(solution)/shard_map/all_to_all | solution.py:278
  40.6 0.7 %last_hubs.1 = (f32[128,256]{1,0:T(8,128)}, f32[16,256]{1,0:T(8,128)}) custom-call(s32[1,256]{1,0:T(1,128)S(1)} %bitcast.11, f32[128,256]{1,0:T(8,128)S(1)} %get-tuple-element.24.refs_1_, f32[8,16,256]{2,1,0:T(8,128)S(1)} %all_to_all.5.refs_2_), custom_call_target="tpu_custom_call" | custom-call | tf_op jit(solution)/shard_map/last_hubs/pallas_call | solution.py:221
  (8 shorter events, 0.2 us)
Async XLA Ops:
  4.6 1.5 %collective-permute-start = (f32[128,256]{1,0:T(8,128)S(1)}, f32[128,256]{1,0:T(8,128)S(1)}, u32[]{:S(2)}, u32[]{:S(2)}) collective-permute-start(f32[128,256]{1,0:T(8,128)S(1)} %get-tuple-element.18), channel_id=1, source_target_pairs={{0,1},{1,0},{2,3},{3,2},{4,5},{5,4},{6,7},{7,6},{8,9},{9,8},{10,11... | collective-permute-start | bytes 393224 | tf_op jit(solution)/shard_map/ppermute | solution.py:205
  5.1 3.9 %collective-permute-start.7 = (f32[128,256]{1,0:T(8,128)S(1)}, f32[128,256]{1,0:T(8,128)S(1)}, u32[]{:S(2)}, u32[]{:S(2)}) collective-permute-start(f32[128,256]{1,0:T(8,128)S(1)} %get-tuple-element.23), channel_id=1, source_target_pairs={{0,1},{1,0},{2,3},{3,2},{4,5},{5,4},{6,7},{7,6},{8,9},{9,8},{10,11... | collective-permute-start | bytes 393224 | tf_op jit(solution)/shard_map/ppermute | solution.py:205
  6.1 2.9 %copy-start = (s32[256]{0:T(256)S(1)}, s32[256]{0:T(256)}, u32[]{:S(2)}) copy-start(s32[256]{0:T(256)} %param.9) | copy-start | bytes 3076
  6.1 7.2 %collective-permute-start.1 = (f32[64,256]{1,0:T(8,128)S(1)}, f32[64,256]{1,0:T(8,128)S(1)}, u32[]{:S(2)}, u32[]{:S(2)}) collective-permute-start(f32[64,256]{1,0:T(8,128)S(1)} %get-tuple-element.20), channel_id=1, source_target_pairs={{0,2},{2,0},{4,6},{6,4},{8,10},{10,8},{12,14},{14,12},{1,3},{3,1},... | collective-permute-start | bytes 196616 | tf_op jit(solution)/shard_map/ppermute | solution.py:208
  9.1 6.1 %collective-permute-start.9 = (bf16[1,128,256]{2,1,0:T(8,128)(2,1)S(1)}, bf16[1,128,256]{2,1,0:T(8,128)(2,1)S(1)}, u32[]{:S(2)}, u32[]{:S(2)}) collective-permute-start(bf16[1,128,256]{2,1,0:T(8,128)(2,1)S(1)} %scores.1.refs_0_), channel_id=1, source_target_pairs={{0,8},{2,10},{4,12},{6,14},{8,0},{10,2},{12,4},{14,6},{1,9},{3,11}... | collective-permute-start | bytes 196616 | tf_op jit(solution)/shard_map/ppermute | solution.py:208
  11.8 5.0 %collective-permute-start.8 = (bf16[1,128,256]{2,1,0:T(8,128)(2,1)S(1)}, bf16[1,128,256]{2,1,0:T(8,128)(2,1)S(1)}, u32[]{:S(2)}, u32[]{:S(2)}) collective-permute-start(bf16[1,128,256]{2,1,0:T(8,128)(2,1)S(1)} %scores.1.refs_0_), channel_id=1, source_target_pairs={{0,4},{2,6},{4,0},{6,2},{8,12},{10,14},{12,8},{14,10},{1,5},{3,7},... | collective-permute-start | bytes 196616 | tf_op jit(solution)/shard_map/ppermute | solution.py:208
  13.4 5.5 %collective-permute-start.2 = (f32[64,256]{1,0:T(8,128)S(1)}, f32[64,256]{1,0:T(8,128)S(1)}, u32[]{:S(2)}, u32[]{:S(2)}) collective-permute-start(f32[64,256]{1,0:T(8,128)S(1)} %plane_sum.1.refs_0_), channel_id=1, source_target_pairs={{0,4},{2,6},{4,0},{6,2},{8,12},{10,14},{12,8},{14,10},{1,5},{3,7},... | collective-permute-start | bytes 196616 | tf_op jit(solution)/shard_map/ppermute | solution.py:208
  16.7 9.6 %collective-permute-start.11 = (bf16[3,128,256]{2,1,0:T(8,128)(2,1)S(1)}, bf16[3,128,256]{2,1,0:T(8,128)(2,1)S(1)}, u32[]{:S(2)}, u32[]{:S(2)}) collective-permute-start(bf16[3,128,256]{2,1,0:T(8,128)(2,1)S(1)} %join_first.1.refs_0_), channel_id=1, source_target_pairs={{0,2},{2,0},{4,6},{6,4},{8,10},{10,8},{12,14},{14,12},{1,3},{3,1},... | collective-permute-start | bytes 589832 | tf_op jit(solution)/shard_map/ppermute | solution.py:208
  17.3 4.9 %collective-permute-start.10 = (bf16[1,128,256]{2,1,0:T(8,128)(2,1)S(1)}, bf16[1,128,256]{2,1,0:T(8,128)(2,1)S(1)}, u32[]{:S(2)}, u32[]{:S(2)}) collective-permute-start(bf16[1,128,256]{2,1,0:T(8,128)(2,1)S(1)} %collective-permute-done.9.refs_2_), channel_id=1, source_target_pairs={{0,4},{2,6},{4,0},{6,2},{8,12},{10,14},{12,8},{14,10},{1,5},{3,7},... | collective-permute-start | bytes 196616 | tf_op jit(solution)/shard_map/ppermute | solution.py:208
  18.8 5.8 %collective-permute-start.3 = (f32[64,256]{1,0:T(8,128)S(1)}, f32[64,256]{1,0:T(8,128)S(1)}, u32[]{:S(2)}, u32[]{:S(2)}) collective-permute-start(f32[64,256]{1,0:T(8,128)S(1)} %pair_sum.1.refs_1_), channel_id=1, source_target_pairs={{0,8},{2,10},{4,12},{6,14},{8,0},{10,2},{12,4},{14,6},{1,9},{3,11}... | collective-permute-start | bytes 196616 | tf_op jit(solution)/shard_map/ppermute | solution.py:208
  22.1 4.3 %collective-permute-start.12 = (bf16[1,128,256]{2,1,0:T(8,128)(2,1)S(1)}, bf16[1,128,256]{2,1,0:T(8,128)(2,1)S(1)}, u32[]{:S(2)}, u32[]{:S(2)}) collective-permute-start(bf16[1,128,256]{2,1,0:T(8,128)(2,1)S(1)} %collective-permute-done.10.refs_1_), channel_id=1, source_target_pairs={{0,2},{2,0},{4,6},{6,4},{8,10},{10,8},{12,14},{14,12},{1,3},{3,1},... | collective-permute-start | bytes 196616 | tf_op jit(solution)/shard_map/ppermute | solution.py:208
  23.5 5.5 %collective-permute-start.6 = (bf16[512,1280]{1,0:T(8,128)(2,1)S(1)}, bf16[512,1280]{1,0:T(8,128)(2,1)S(1)}, u32[]{:S(2)}, u32[]{:S(2)}) collective-permute-start(bf16[512,1280]{1,0:T(8,128)(2,1)S(1)} %pass_dense.1), channel_id=1, source_target_pairs={{0,1},{1,0},{2,3},{3,2},{4,5},{5,4},{6,7},{7,6},{8,9},{9,8},{10,11... | collective-permute-start | bytes 3932168 | tf_op jit(solution)/shard_map/ppermute | solution.py:205
  24.7 3.7 %collective-permute-start.4 = (bf16[64,256]{1,0:T(8,128)(2,1)S(1)}, bf16[64,256]{1,0:T(8,128)(2,1)S(1)}, u32[]{:S(2)}, u32[]{:S(2)}) collective-permute-start(bf16[64,256]{1,0:T(8,128)(2,1)S(1)} %hub_sums.1.refs_0_.refs_4_), channel_id=1, source_target_pairs={{0,3},{1,2},{2,1},{3,0},{4,7},{5,6},{6,5},{7,4},{8,11},{9,10},{10,... | collective-permute-start | bytes 98312 | tf_op jit(solution)/shard_map/ppermute | solution.py:215
  26.4 2.6 %collective-permute-start.13 = (bf16[8,128,256]{2,1,0:T(8,128)(2,1)S(1)}, bf16[8,128,256]{2,1,0:T(8,128)(2,1)S(1)}, u32[]{:S(2)}, u32[]{:S(2)}) collective-permute-start(bf16[8,128,256]{2,1,0:T(8,128)(2,1)S(1)} %join_blocks.1.refs_0_), channel_id=1, source_target_pairs={{0,1},{1,0},{2,3},{3,2},{4,5},{5,4},{6,7},{7,6},{8,9},{9,8},{10,11... | collective-permute-start | bytes 1572872 | tf_op jit(solution)/shard_map/ppermute | solution.py:205
  28.4 1.3 %collective-permute-start.5 = (bf16[2,64,256]{2,1,0:T(8,128)(2,1)S(1)}, bf16[2,64,256]{2,1,0:T(8,128)(2,1)S(1)}, u32[]{:S(2)}, u32[]{:S(2)}) collective-permute-start(bf16[2,64,256]{2,1,0:T(8,128)(2,1)S(1)} %join_sides.1.refs_1_), channel_id=1, source_target_pairs={{0,1},{1,0},{2,3},{3,2},{4,5},{5,4},{6,7},{7,6},{8,9},{9,8},{10,11... | collective-permute-start | bytes 196616 | tf_op jit(solution)/shard_map/ppermute | solution.py:205
